TPU v7x, 32 devices: a whole 2x2x4 slice. The times are simulated.
32 devices in a mesh: patch: 8 (over z, core), head: 4 (over y, x).
Axes of the slice: x: 2, y: 2, z: 4, core: 2. Of those that a mesh axis runs over, the one named last changes fastest.
Arguments:
- img_qkv: bfloat16 [2048, 9216], P(('patch', 'head')), may hold values from -8 to 8
- txt_qkv: bfloat16 [512, 9216], P('head'), may hold values from -8 to 8
- stale_kv: bfloat16 [2, 2048, 3072], P(None, 'patch', 'head'), may hold values from -8 to 8
- residual: bfloat16 [2048, 3072], P(('patch', 'head')), may hold values from -4 to 4
- gate_scale: float32 [3072], replicated, may hold values from 0.5 to 3
- proj_weight: bfloat16 [3072, 3072], replicated, may hold values from -0.109375 to 0.109375
Outputs:
- image_out: bfloat16 [2048, 3072], P(('patch', 'head'))
- text_attn: bfloat16 [512, 3072], P('head')
All inputs are finite; a program needn't handle non-finite values.
Results may differ from a plain program's by a relative error of at most 0.0075.
Values may be sent and summed in bfloat16 or wider, within the bound.
No kernel may reach another device: no remote copies, remote signals or barrier semaphores. Data moves between devices by JAX's collectives and lax.ppermute only.
A program may use at most 192 MiB of HBM per device.

v0:
```python
import math

import jax
import jax.numpy as jnp
from jax import lax
from jax.sharding import PartitionSpec as P

HD = 128


def block_stats(queries, key_rows, values):
    scores = jnp.einsum("rhd,khd->rhk", queries, key_rows, preferred_element_type=jnp.float32) * (
        1.0 / math.sqrt(HD)
    )
    row_max = jnp.max(scores, axis=2)
    shifted = jnp.exp(scores - row_max[:, :, None])
    row_sum = jnp.sum(shifted, axis=2)
    weighted = jnp.einsum(
        "rhk,khd->rhd", shifted.astype(jnp.bfloat16), values, preferred_element_type=jnp.float32
    )
    return (row_max, row_sum, weighted)


def combine(first, second):
    joint_max = jnp.maximum(first[0], second[0])
    first_scale = jnp.exp(first[0] - joint_max)
    second_scale = jnp.exp(second[0] - joint_max)
    return (
        joint_max,
        first[1] * first_scale + second[1] * second_scale,
        first[2] * first_scale[:, :, None] + second[2] * second_scale[:, :, None],
    )


def finish(totals):
    return (totals[2] / totals[1][:, :, None]).astype(jnp.bfloat16)


def per_device(img_qkv, txt_qkv, stale_kv, residual, gate_scale, proj_weight):
    patch_count = lax.axis_size("patch")
    my_group = lax.axis_index("patch")
    img_rows = img_qkv.shape[0]
    model_width = img_qkv.shape[1] // 3
    head_count = model_width // HD
    img_split = img_qkv.reshape(img_rows, 3, head_count, HD)
    txt_split = txt_qkv.reshape(txt_qkv.shape[0], 3, head_count, HD)
    img_heads, txt_heads = (
        lax.all_to_all(img_split, "head", split_axis=2, concat_axis=0, tiled=True),
        lax.all_to_all(txt_split, "head", split_axis=2, concat_axis=0, tiled=True),
    )
    query_img = img_heads[:, 0]
    keys_img = img_heads[:, 1]
    values_img = img_heads[:, 2]
    query_txt = txt_heads[:, 0]
    keys_txt = txt_heads[:, 1]
    values_txt = txt_heads[:, 2]
    group_rows = query_img.shape[0]
    local_heads = query_img.shape[1]
    text_total_rows = query_txt.shape[0]
    slice_rows = text_total_rows // patch_count
    text_queries = lax.dynamic_slice_in_dim(query_txt, my_group * slice_rows, slice_rows, 0)
    image_init = block_stats(query_img, keys_txt, values_txt)
    text_init = block_stats(text_queries, keys_txt, values_txt)
    own_first = my_group * group_rows
    shard_rows = lax.all_gather(stale_kv, "patch", axis=1, tiled=True)
    shard_count = shard_rows.shape[1] // group_rows
    key_blocks = jnp.moveaxis(shard_rows.reshape(2, shard_count, group_rows, local_heads, HD), 1, 0)
    starts = group_rows * jnp.arange(shard_count, dtype=jnp.int32)

    def one_block(running_pair, inputs):
        key_block, block_first = inputs
        is_fresh = block_first == own_first
        key_rows = jnp.where(is_fresh, keys_img, key_block[0])
        values = jnp.where(is_fresh, values_img, key_block[1])
        image_next = combine(running_pair[0], block_stats(query_img, key_rows, values))
        text_next = combine(running_pair[1], block_stats(text_queries, key_block[0], key_block[1]))
        return ((image_next, text_next), None)

    result, _ = lax.scan(one_block, (image_init, text_init), (key_blocks, starts))
    image_total, text_total = result
    image_attn = finish(image_total)
    text_attn = finish(text_total)
    text_attn = lax.all_gather(text_attn, "patch", axis=0, tiled=True)
    image_back, text_back = (
        lax.all_to_all(image_attn, "head", split_axis=0, concat_axis=1, tiled=True),
        lax.all_to_all(text_attn, "head", split_axis=0, concat_axis=1, tiled=True),
    )
    image_flat = image_back.reshape(img_rows, model_width)
    projected = jnp.dot(image_flat, proj_weight, preferred_element_type=jnp.float32)
    image_out = (residual.astype(jnp.float32) + gate_scale * projected).astype(jnp.bfloat16)
    return (image_out, text_back.reshape(text_back.shape[0], model_width))


def solution(mesh):
    return jax.shard_map(
        per_device,
        mesh=mesh,
        in_specs=(
            P(("patch", "head"), None),
            P("head", None),
            P(None, "patch", "head"),
            P(("patch", "head"), None),
            P(),
            P(),
        ),
        out_specs=(P(("patch", "head"), None), P("head", None)),
        check_vma=False,
    )
```

profile of v0, /device:TPU:0, one launch (start us, length us, event | category | flops | bytes accessed | tf_op | source)
XLA Modules:
  0.0 216.0 jit_solution(15585166651167606172)
XLA Ops:
  7.9 1.5 copy.89
  10.8 5.2 %all-to-all-start.1 = ((bf16[64,3,24,128]{3,0,1,2:T(8,128)(2,1)}), bf16[64,3,24,128]{3,0,1,2:T(8,128)(2,1)S(1)}, u32[]{:S(2)}, u32[]{:S(2)}) async-start(bf16[64,3,24,128]{3,0,1,2:T(8,128)(2,1)} %copy.67), calls=%async_computation.1 | async-start | bytes 2359296 | tf_op jit(solution)/shard_map/all_to_all | solution.py:48
  15.9 3.0 %copy.63 = bf16[128,9216]{0,1:T(8,128)(2,1)S(1)} copy(bf16[128,9216]{1,0:T(8,128)(2,1)} %param.9) | data formatting | bytes 4718592 | tf_op args[1]
  19.0 1.6 copy.64
  20.6 10.4 %all-to-all-done.1 = bf16[64,3,24,128]{3,0,1,2:T(8,128)(2,1)S(1)} async-done(((bf16[64,3,24,128]{3,0,1,2:T(8,128)(2,1)}), bf16[64,3,24,128]{3,0,1,2:T(8,128)(2,1)S(1)}, u32[]{:S(2)}, u32[]{:S(2)}) %all-to-all-start.1) | async-done | bytes 1179680 | tf_op jit(solution)/shard_map/all_to_all | solution.py:48
  31.0 3.6 %all-to-all-start = ((bf16[128,3,24,128]{0,3,1,2:T(8,128)(2,1)}), bf16[128,3,24,128]{0,3,1,2:T(8,128)(2,1)S(1)}, u32[]{:S(2)}, u32[]{:S(2)}) async-start(bf16[128,3,24,128]{0,3,1,2:T(8,128)(2,1)} %copy.64), calls=%async_computation | async-start | bytes 4718592 | tf_op jit(solution)/shard_map/all_to_all | solution.py:49
  37.4 24.4 %all-to-all-done = bf16[128,3,24,128]{0,3,1,2:T(8,128)(2,1)S(1)} async-done(((bf16[128,3,24,128]{0,3,1,2:T(8,128)(2,1)}), bf16[128,3,24,128]{0,3,1,2:T(8,128)(2,1)S(1)}, u32[]{:S(2)}, u32[]{:S(2)}) %all-to-all-start) | async-done | bytes 2359328 | tf_op jit(solution)/shard_map/all_to_all | solution.py:49
  61.8 1.5 copy-done.4
  63.3 3.1 %copy.66 = bf16[4,128,3,6,128]{4,1,0,3,2:T(8,128)(2,1)S(1)} copy(bf16[4,128,3,6,128]{1,4,2,3,0:T(8,128)(2,1)} %bitcast.145) | data formatting | bytes 4718592 | tf_op jit(solution)/shard_map/all_to_all | solution.py:49
  67.3 1.6 bitcast_reduce_fusion.1
  68.9 1.7 copy-done
  70.6 1.7 fusion.32
  72.3 1.4 copy.72
  76.6 2.4 %fusion.26 = f32[256,6]{0,1:T(8,128)S(1)} fusion(f32[6,512,256]{2,1,0:T(8,128)} %copy-done, f32[256,6]{0,1:T(8,128)S(1)} %get-tuple-element.316), kind=kLoop, calls=%fused_computation.42 | loop fusion | flops 2357760 | bytes 3158016 | tf_op jit(solution)/shard_map/reduce_sum | solution.py:17
  80.1 8.7 %copy.71 = bf16[2,2048,768]{1,2,0:T(8,128)(2,1)} copy(bf16[2,2048,768]{2,1,0:T(8,128)(2,1)} %all-gather.2.cloned.1.call-done) | data formatting | bytes 12582912 | tf_op jit(solution)/shard_map/all_gather | solution.py:65
  88.7 8.1 %copy.90 = bf16[192,8,8,256]{3,2,1,0:T(8,128)(2,1)} copy(bf16[192,8,8,256]{3,1,2,0:T(8,128)(2,1)} %bitcast.138) | data formatting | bytes 12582912
  96.9 9.1 %copy.73 = bf16[8,2,256,6,128]{4,2,3,1,0:T(8,128)(2,1)} copy(bf16[8,2,256,6,128]{2,0,4,3,1:T(8,128)(2,1)} %bitcast.139) | data formatting | bytes 12582912 | tf_op jit(solution)/shard_map/while | solution.py:79
  106.1 59.8 %while.20 = (s32[]{:T(128)}, f32[256,6]{0,1:T(8,128)S(1)}, f32[256,6]{0,1:T(8,128)S(1)}, f32[256,6,128]{0,2,1:T(8,128)S(1)}, f32[64,6]{0,1:T(8,128)S(1)}, /*inde...) while((s32[]{:T(128)}, f32[256,6]{0,1:T(8,128)S(1)}, ...), condition=%wide.region_9.10_spmd, body=%wide.region_4.9_spmd.sunk | while | flops 255745536 | bytes 10822880 | solution.py:79
  111.9 1.6 fusion.64
  119.4 1.6 fusion.64
  126.8 1.6 fusion.64
  134.3 1.6 fusion.64
  141.8 1.6 fusion.64
  149.3 1.6 fusion.64
  156.7 1.6 fusion.64
  164.2 1.6 fusion.64
  167.5 3.5 %all-to-all-start.2 = ((bf16[256,6,128]{2,1,0:T(8,128)(2,1)}), bf16[256,6,128]{2,1,0:T(8,128)(2,1)S(1)}, u32[]{:S(2)}, u32[]{:S(2)}) async-start(bf16[256,6,128]{2,1,0:T(8,128)(2,1)} %divide_convert_fusion), calls=%async_computation.2 | async-start | bytes 1048576 | tf_op jit(solution)/shard_map/all_to_all | solution.py:85
  171.2 16.0 %all_gather.7 = bf16[512,6,128]{2,0,1:T(8,128)(2,1)S(1)} all-gather(bf16[64,6,128]{2,0,1:T(8,128)(2,1)S(1)} %divide_convert_fusion.1), channel_id=1, replica_groups=mesh['patch'=8,'head'=4] {'patch'}, dimensions={0}, use_global_device_ids=true | all-gather | bytes 884736 | tf_op jit(solution)/shard_map/all_gather | solution.py:83
  187.1 1.5 copy.78
  188.6 4.5 %all-to-all-start.3 = ((bf16[512,6,128]{2,1,0:T(8,128)(2,1)}), bf16[512,6,128]{2,1,0:T(8,128)(2,1)S(1)}, u32[]{:S(2)}, u32[]{:S(2)}) async-start(bf16[512,6,128]{2,1,0:T(8,128)(2,1)} %copy.78), calls=%async_computation.3 | async-start | bytes 2097152 | tf_op jit(solution)/shard_map/all_to_all | solution.py:86
  193.7 10.5 %fusion.23 = bf16[64,3072]{1,0:T(8,128)(2,1)} fusion(bf16[64,3072]{1,0:T(8,128)(2,1)S(1)} %reshape.40, bf16[3072,3072]{1,0:T(8,128)(2,1)} %param.13, bf16[64,3072]{1,0:T(8,128)(2,1)S(1)} %copy-done.8, f32[3072]{0:T(1024)S(1)} %copy-done.12), kind=kOutput, calls=%fused_computation.37 | convolution fusion | flops 1208745984 | bytes 20066304 | tf_op jit(solution)/shard_map/dot_general | solution.py:89
  204.2 3.1 %all-to-all-done.3 = bf16[512,6,128]{2,1,0:T(8,128)(2,1)S(1)} async-done(((bf16[512,6,128]{2,1,0:T(8,128)(2,1)}), bf16[512,6,128]{2,1,0:T(8,128)(2,1)S(1)}, u32[]{:S(2)}, u32[]{:S(2)}) %all-to-all-start.3) | async-done | bytes 786464 | tf_op jit(solution)/shard_map/all_to_all | solution.py:86
  (111 shorter events, 54.8 us)
Async XLA Ops:
  7.2 72.9 %all-gather.2.cloned.1.call-start = ((), (), s32[]{:S(2)}) async-start(), calls=%async_computation.4 | async-start | bytes 7077888 | tf_op jit(solution)/shard_map/all_gather | solution.py:65
  10.8 20.2 %all-to-all-start.1 = ((bf16[64,3,24,128]{3,0,1,2:T(8,128)(2,1)}), bf16[64,3,24,128]{3,0,1,2:T(8,128)(2,1)S(1)}, u32[]{:S(2)}, u32[]{:S(2)}) async-start(bf16[64,3,24,128]{3,0,1,2:T(8,128)(2,1)} %copy.67), calls=%async_computation.1 | async-start | bytes 2359296 | tf_op jit(solution)/shard_map/all_to_all | solution.py:48
  31.0 30.9 %all-to-all-start = ((bf16[128,3,24,128]{0,3,1,2:T(8,128)(2,1)}), bf16[128,3,24,128]{0,3,1,2:T(8,128)(2,1)S(1)}, u32[]{:S(2)}, u32[]{:S(2)}) async-start(bf16[128,3,24,128]{0,3,1,2:T(8,128)(2,1)} %copy.64), calls=%async_computation | async-start | bytes 4718592 | tf_op jit(solution)/shard_map/all_to_all | solution.py:49
  35.3 1.1 copy-start.5
  61.8 1.5 copy-start.4
  68.9 1.7 copy-start
  74.7 0.6 copy-start.6
  75.8 3.3 %copy-start.9 = (f32[64,6]{0,1:T(8,128)}, f32[64,6]{0,1:T(8,128)S(1)}, u32[]{:S(2)}) copy-start(f32[64,6]{0,1:T(8,128)S(1)} %get-tuple-element.319) | copy-start | bytes 4612
  96.9 9.2 %copy-start.1 = (bf16[256,6,128]{2,0,1:T(8,128)(2,1)S(1)}, bf16[256,6,128]{2,0,1:T(8,128)(2,1)}, u32[]{:S(2)}) copy-start(bf16[256,6,128]{2,0,1:T(8,128)(2,1)} %get-tuple-element.325) | copy-start | bytes 1179652
  96.9 9.2 %copy-start.2 = (bf16[256,6,128]{2,0,1:T(8,128)(2,1)S(1)}, bf16[256,6,128]{2,0,1:T(8,128)(2,1)}, u32[]{:S(2)}) copy-start(bf16[256,6,128]{2,0,1:T(8,128)(2,1)} %get-tuple-element.326) | copy-start | bytes 1179652
  96.9 9.2 %copy-start.3 = (f32[64,6,128]{2,0,1:T(8,128)S(1)}, f32[64,6,128]{2,0,1:T(8,128)}, u32[]{:S(2)}) copy-start(f32[64,6,128]{2,0,1:T(8,128)} %convolution_bitcast_fusion.2) | copy-start | bytes 589828
  96.9 9.2 %copy-start.7 = (bf16[64,6,128]{2,0,1:T(8,128)(2,1)S(1)}, bf16[64,6,128]{2,0,1:T(8,128)(2,1)}, u32[]{:S(2)}) copy-start(bf16[64,6,128]{2,0,1:T(8,128)(2,1)} %copy-done.6) | copy-start | bytes 294916
  96.9 9.2 %copy-start.10 = (f32[64,6]{0,1:T(8,128)S(1)}, f32[64,6]{0,1:T(8,128)}, u32[]{:S(2)}) copy-start(f32[64,6]{0,1:T(8,128)} %copy-done.9) | copy-start | bytes 4612
  96.9 9.2 %copy-start.11 = (f32[64,6]{0,1:T(8,128)S(1)}, f32[64,6]{0,1:T(8,128)}, u32[]{:S(2)}) copy-start(f32[64,6]{0,1:T(8,128)} %fusion.36) | copy-start | bytes 4612
  96.9 9.2 %copy-start.13 = (s32[8]{0:T(128)S(1)}, s32[8]{0:T(128)}, u32[]{:S(2)}) copy-start(s32[8]{0:T(128)} %iota_multiply_fusion) | copy-start | bytes 100
  167.5 21.1 %all-to-all-start.2 = ((bf16[256,6,128]{2,1,0:T(8,128)(2,1)}), bf16[256,6,128]{2,1,0:T(8,128)(2,1)S(1)}, u32[]{:S(2)}, u32[]{:S(2)}) async-start(bf16[256,6,128]{2,1,0:T(8,128)(2,1)} %divide_convert_fusion), calls=%async_computation.2 | async-start | bytes 1048576 | tf_op jit(solution)/shard_map/all_to_all | solution.py:85
  188.6 5.0 %copy-start.8 = (bf16[64,3072]{1,0:T(8,128)(2,1)S(1)}, bf16[64,3072]{1,0:T(8,128)(2,1)}, u32[]{:S(2)}) copy-start(bf16[64,3072]{1,0:T(8,128)(2,1)} %param.11) | copy-start | bytes 1179652
  188.6 5.0 %copy-start.12 = (f32[3072]{0:T(1024)S(1)}, f32[3072]{0:T(1024)}, u32[]{:S(2)}) copy-start(f32[3072]{0:T(1024)} %param.12) | copy-start | bytes 36868
  188.6 18.6 %all-to-all-start.3 = ((bf16[512,6,128]{2,1,0:T(8,128)(2,1)}), bf16[512,6,128]{2,1,0:T(8,128)(2,1)S(1)}, u32[]{:S(2)}, u32[]{:S(2)}) async-start(bf16[512,6,128]{2,1,0:T(8,128)(2,1)} %copy.78), calls=%async_computation.3 | async-start | bytes 2097152 | tf_op jit(solution)/shard_map/all_to_all | solution.py:86
Sparse Core Ops, SparseCore 0:
  9.6 67.4 all-gather.1
where the time goes:
time: 218 us; the launch traced here: 216 us
  matrix products  60.7 us (28%)
  local copies, waits for them, and re-layouts  54.9 us (25%)
  waiting for transfers between devices  38.6 us (18%)
  starting transfers between devices  16.8 us (8%)
  blocking collectives  16 us (7%)
  between operations  14.3 us (7%)
  other arithmetic  9.04 us (4%)
  loops' own time  5.73 us (3%)
    dot_general x18, matrix products, block_stats(): jnp.einsum('rhk,khd->rhd', shifted.astype(jnp.bfloat16), values, preferre...  26.4 us
    all_to_all x1, waiting for transfers between devices, per_device(): lax.all_to_all(txt_split, 'head', split_axis=2, concat_axis=0, tiled=True)  24.4 us
    dot_general x18, matrix products, block_stats(): jnp.einsum('rhd,khd->rhk', queries, key_rows, preferred_element_type=jnp....  23.7 us
    unnamed x32, local copies, waits for them, and re-layouts  18.7 us
    all_gather x1, blocking collectives, per_device(): text_attn = lax.all_gather(text_attn, 'patch', axis=0, tiled=True)  16 us
    while x4, local copies, waits for them, and re-layouts, per_device(): lax.scan(one_block, (image_init, text_init), (key_blocks, starts))  11.1 us
    dot_general x1, matrix products, per_device(): jnp.dot(image_flat, proj_weight, preferred_element_type=jnp.float32)  10.5 us
    all_to_all x1, waiting for transfers between devices, per_device(): lax.all_to_all(img_split, 'head', split_axis=2, concat_axis=0, tiled=True)  10.4 us
  transfers between devices with their start and end apart: 5, of which 3 were waited for; matrix products, arithmetic and copies ran while one was open for 17% of the time, Pallas kernels for 0%

commit v1 on v0

v1 whole, which is shorter than its diff:
```python
import functools
import math

import jax
import jax.numpy as jnp
from jax import lax
from jax.experimental import pallas as pl
from jax.experimental.pallas import tpu as pltpu
from jax.sharding import PartitionSpec as P

HD = 128
SCALE = math.log2(math.e) / math.sqrt(HD)
VMEM_LIMIT = 40 * 1024 * 1024
TILE = 256


def params(steps=1):
    return pltpu.CompilerParams(
        vmem_limit_bytes=VMEM_LIMIT, dimension_semantics=("arbitrary",) * steps
    )


def dot(first, second, contract):
    return lax.dot_general(
        first, second, ((contract[:1], contract[1:]), ((), ())), preferred_element_type=jnp.float32
    )


def scaled_scores(key_rows, queries):
    return dot(key_rows, queries, (1, 1)) * SCALE


def weigh(scores, values, row_max):
    weights = jnp.exp2(scores - row_max)
    row_sum = jnp.sum(weights, axis=0, keepdims=True)
    return row_sum, dot(values, weights.astype(jnp.bfloat16), (0, 0))


def tiles_of(rows):
    tile = min(TILE, rows)
    return [(first, min(tile, rows - first)) for first in range(0, rows, tile)]


def pack_body(_, *refs):
    sources, packed = refs[:-1], refs[-1]
    for part, source in enumerate(sources):
        width = source.shape[1]
        packed[0, :, part * width : (part + 1) * width] = source[...]


def pack(rows_array, row_block, rows, destinations, column_block, width):
    blocks = rows_array.shape[1] // 3 // width

    def source(part):
        return pl.BlockSpec(
            (rows, width), lambda d, info: (info[0], part * blocks + column_block(d))
        )

    return pl.pallas_call(
        pack_body,
        grid_spec=pltpu.PrefetchScalarGridSpec(
            num_scalar_prefetch=1,
            grid=(destinations,),
            in_specs=[source(0), source(1), source(2)],
            out_specs=pl.BlockSpec((1, rows, 3 * width), lambda d, info: (d, 0, 0)),
        ),
        out_shape=jax.ShapeDtypeStruct((destinations, rows, 3 * width), rows_array.dtype),
        compiler_params=params(),
        name="pack_heads",
    )(row_block, rows_array, rows_array, rows_array)


def first_body(pair, info, *refs):
    q_img, k_img, v_img, q_txt, k_txt, v_txt = refs[:6]
    stale = refs[6 : 6 + pair]
    acc_img, stat_img, acc_txt, stat_txt = refs[6 + pair :]
    core = info[0]
    group_rows = q_img.shape[0] // pair
    text_keys, text_values = k_txt[...], v_txt[...]

    def store(queries, key_rows, values, acc, stat, first, count):
        scores = scaled_scores(key_rows, queries)
        row_max = jnp.max(scores, axis=0, keepdims=True)
        row_sum, mixed = weigh(scores, values, row_max)
        acc[0, :, first : first + count] = mixed
        stat[0, 0:1, first : first + count] = row_max
        stat[0, 1:2, first : first + count] = row_sum

    for group in range(pair):
        key_rows = [text_keys, k_img[group * group_rows : (group + 1) * group_rows, :]]
        values = [text_values, v_img[group * group_rows : (group + 1) * group_rows, :]]
        if pair == 2:
            mine = core == group
            key_rows.append(jnp.where(mine, stale[1][0], stale[0][0]))
            values.append(jnp.where(mine, stale[1][1], stale[0][1]))
        key_rows, values = jnp.concatenate(key_rows, 0), jnp.concatenate(values, 0)
        for first, count in tiles_of(group_rows):
            first = first + group * group_rows
            store(q_img[first : first + count, :], key_rows, values, acc_img, stat_img, first, count)
    key_rows = jnp.concatenate([text_keys] + [block[0] for block in stale], 0)
    values = jnp.concatenate([text_values] + [block[1] for block in stale], 0)
    for first, count in tiles_of(q_txt.shape[0]):
        store(q_txt[first : first + count, :], key_rows, values, acc_txt, stat_txt, first, count)


def column_spec(rows, offset):
    return pl.BlockSpec((rows, HD), lambda h, info: (0, offset + h))


def block_spec(block):
    return pl.BlockSpec((2, block.shape[1], HD), lambda h, info: (0, 0, h))


def state_shapes(heads, rows):
    return [
        jax.ShapeDtypeStruct((heads, HD, rows), jnp.float32),
        jax.ShapeDtypeStruct((heads, 8, rows), jnp.float32),
    ]


def state_specs(rows):
    return [
        pl.BlockSpec((1, HD, rows), lambda h, info: (h, 0, 0)),
        pl.BlockSpec((1, 8, rows), lambda h, info: (h, 0, 0)),
    ]


def attend_cost(queries, keys, heads):
    return pl.CostEstimate(
        flops=4 * queries * keys * heads * HD,
        bytes_accessed=4 * queries * heads * HD + 4 * keys * heads * HD,
        transcendentals=queries * keys * heads,
    )


def attend_first(info, img, txt, stale):
    heads = img.shape[1] // (3 * HD)
    rows, text_rows = img.shape[0], txt.shape[0]
    return pl.pallas_call(
        functools.partial(first_body, len(stale)),
        grid_spec=pltpu.PrefetchScalarGridSpec(
            num_scalar_prefetch=1,
            grid=(heads,),
            in_specs=[column_spec(rows, part * heads) for part in range(3)]
            + [column_spec(text_rows, part * heads) for part in range(3)]
            + [block_spec(block) for block in stale],
            out_specs=state_specs(rows) + state_specs(text_rows),
        ),
        out_shape=state_shapes(heads, rows) + state_shapes(heads, text_rows),
        compiler_params=params(),
        cost_estimate=attend_cost(rows + text_rows, 1024, heads),
        name="attend_own",
    )(info, img, img, img, txt, txt, txt, *stale)


def step_body(sets, per_side, final, info, *refs):
    refs = list(refs)
    sources = [refs[3 * i : 3 * i + 3] for i in range(sets)]
    blocks = refs[3 * sets : 3 * sets + 2 * per_side]
    rest = refs[3 * sets + 2 * per_side :]
    if final:
        outputs, scratch = rest[:sets], rest[sets:]
        states = [scratch[2 * i : 2 * i + 2] for i in range(sets)]
    else:
        states = [rest[2 * i : 2 * i + 2] for i in range(sets)]
    for (_, acc_in, stat_in), (acc, stat) in zip(sources, states):
        acc[...] = acc_in[...]
        stat[...] = stat_in[...]
    for side in range(2):
        mine = blocks[side * per_side : (side + 1) * per_side]

        @pl.when(info[1 + side] == 1)
        def _():
            key_rows = jnp.concatenate([block[0] for block in mine], 0)
            values = jnp.concatenate([block[1] for block in mine], 0)
            for (queries, _, _), (acc, stat) in zip(sources, states):
                for first, count in tiles_of(queries.shape[0]):
                    span = slice(first, first + count)
                    scores = scaled_scores(key_rows, queries[span, :])
                    old_max = stat[0, 0:1, span]
                    row_max = jnp.maximum(old_max, jnp.max(scores, axis=0, keepdims=True))
                    row_sum, mixed = weigh(scores, values, row_max)
                    keep = jnp.exp2(old_max - row_max)
                    acc[0, :, span] = acc[0, :, span] * keep + mixed
                    stat[0, 1:2, span] = stat[0, 1:2, span] * keep + row_sum
                    stat[0, 0:1, span] = row_max

    if final:
        for output, (acc, stat) in zip(outputs, states):
            for first, count in tiles_of(output.shape[0]):
                span = slice(first, first + count)
                output[span, :] = (acc[0, :, span] / stat[0, 1:2, span]).T.astype(output.dtype)


def attend_step(info, sources, left, right, final):
    heads = sources[0][0].shape[1] // (3 * HD)
    operands, in_specs, out_specs, out_shape, scratch = [], [], [], [], []
    for qkv, acc, stat in sources:
        rows = qkv.shape[0]
        operands += [qkv, acc, stat]
        in_specs += [column_spec(rows, 0)] + state_specs(rows)
        if final:
            out_specs.append(column_spec(rows, 0))
            out_shape.append(jax.ShapeDtypeStruct((rows, heads * HD), jnp.bfloat16))
            scratch += [pltpu.VMEM((1, HD, rows), jnp.float32), pltpu.VMEM((1, 8, rows), jnp.float32)]
        else:
            out_specs += state_specs(rows)
            out_shape += state_shapes(heads, rows)
    blocks = list(left) + list(right)
    total = sum(qkv.shape[0] for qkv, _, _ in sources)
    keys = sum(block.shape[1] for block in left)
    return pl.pallas_call(
        functools.partial(step_body, len(sources), len(left), final),
        grid_spec=pltpu.PrefetchScalarGridSpec(
            num_scalar_prefetch=1,
            grid=(heads,),
            in_specs=in_specs + [block_spec(block) for block in blocks],
            out_specs=out_specs,
            scratch_shapes=scratch,
        ),
        out_shape=out_shape,
        compiler_params=params(),
        cost_estimate=attend_cost(total, keys, heads),
        name="attend_last" if final else "attend_arrived",
    )(info, *operands, *blocks)


def project_body(order, x_ref, weight, residual, gate, out, flat):
    @pl.when(pl.program_id(0) == 0)
    def _():
        width = x_ref.shape[2]
        for source, place in enumerate(order):
            flat[:, place * width : (place + 1) * width] = x_ref[source]

    projected = jnp.dot(flat[...], weight[...], preferred_element_type=jnp.float32)
    out[...] = (residual[...].astype(jnp.float32) + gate[...] * projected).astype(out.dtype)


def project(x, order, weight, residual, gate):
    rows, model = residual.shape
    columns = 512 if model % 512 == 0 else HD
    return pl.pallas_call(
        functools.partial(project_body, order),
        grid=(model // columns,),
        in_specs=[
            pl.BlockSpec(x.shape, lambda n: (0, 0, 0)),
            pl.BlockSpec((weight.shape[0], columns), lambda n: (0, n)),
            pl.BlockSpec((rows, columns), lambda n: (0, n)),
            pl.BlockSpec((1, columns), lambda n: (0, n)),
        ],
        out_specs=pl.BlockSpec((rows, columns), lambda n: (0, n)),
        out_shape=jax.ShapeDtypeStruct((rows, model), residual.dtype),
        scratch_shapes=[pltpu.VMEM((rows, weight.shape[0]), x.dtype)],
        compiler_params=params(),
        cost_estimate=pl.CostEstimate(
            flops=2 * rows * model * model, bytes_accessed=2 * model * model, transcendentals=0
        ),
        name="project",
    )(x, weight, residual, gate.reshape(1, model))


def per_device(img_qkv, txt_qkv, stale_kv, residual, gate_scale, proj_weight):
    patches, head_owners = lax.axis_size("patch"), lax.axis_size("head")
    patch, owner = lax.axis_index("patch"), lax.axis_index("head")
    model = img_qkv.shape[1] // 3
    owned_heads = stale_kv.shape[2] // HD
    pair = 2 if patches % 2 == 0 and owned_heads % 2 == 0 else 1
    planes = patches // pair
    plane, core = patch // pair, patch % pair
    width = stale_kv.shape[2] // pair
    img_rows = img_qkv.shape[0]
    text_rows = txt_qkv.shape[0] // pair
    destinations = pair * head_owners
    order = [(d % head_owners) * pair + d // head_owners for d in range(destinations)]

    def column_block(d):
        return (d % head_owners) * pair + d // head_owners

    groups = [[g * destinations + d for d in range(destinations)] for g in range(planes)]

    def exchange(x):
        return lax.all_to_all(
            x, ("patch", "head"), split_axis=0, concat_axis=0, axis_index_groups=groups, tiled=True
        )

    swap_pairs = [(p, p + 1 - 2 * (p % 2)) for p in range(patches)]
    mine = lax.dynamic_slice_in_dim(stale_kv, core * width, width, 2)
    stale = [mine]
    if pair == 2:
        theirs = lax.dynamic_slice_in_dim(stale_kv, (1 - core) * width, width, 2)
        stale.append(lax.ppermute(theirs, "patch", swap_pairs))

    zero = jnp.zeros((), jnp.int32)
    img = exchange(
        pack(img_qkv, zero.reshape(1), img_rows, destinations, column_block, width)
    ).reshape(destinations * img_rows, 3 * width)
    txt = exchange(
        pack(txt_qkv, core.astype(jnp.int32).reshape(1), text_rows, destinations, column_block, width)
    ).reshape(destinations * text_rows, 3 * width)

    info = jnp.stack([core, zero, zero]).astype(jnp.int32)
    state = attend_first(info, img, txt, stale)
    from_left, from_right = stale, stale
    for step in range(1, planes):
        right_pairs = [(p, p + pair) for p in range((step - 1) * pair, patches - pair)]
        left_pairs = [(q, p) for p, q in right_pairs]
        left_pairs = [(p + pair, p) for p in range(0, patches - step * pair)]
        from_left = [lax.ppermute(block, "patch", right_pairs) for block in from_left]
        from_right = [lax.ppermute(block, "patch", left_pairs) for block in from_right]
        info = jnp.stack([core, plane >= step, plane + step < planes]).astype(jnp.int32)
        img_source = (img, state[0], state[1])
        txt_source = (txt, state[2], state[3])
        if step < planes - 1:
            state = attend_step(info, [img_source, txt_source], from_left, from_right, False)
        else:
            (image_attn,) = attend_step(info, [img_source], from_left, from_right, True)
            (text_attn,) = attend_step(info, [txt_source], from_left, from_right, True)

    image_back = exchange(image_attn.reshape(destinations, img_rows, width))
    image_out = project(image_back, order, proj_weight, residual, gate_scale)

    text_back = exchange(text_attn.reshape(destinations, text_rows, width))
    text_out = (
        text_back.reshape(pair, head_owners, text_rows, width)
        .transpose(2, 1, 0, 3)
        .reshape(text_rows, model)
    )
    if pair == 2:
        other = lax.ppermute(text_out, "patch", swap_pairs)
        lower = core == 0
        text_out = jnp.concatenate(
            [jnp.where(lower, text_out, other), jnp.where(lower, other, text_out)], 0
        )
    return (image_out, text_out)


def solution(mesh):
    return jax.shard_map(
        per_device,
        mesh=mesh,
        in_specs=(
            P(("patch", "head"), None),
            P("head", None),
            P(None, "patch", "head"),
            P(("patch", "head"), None),
            P(),
            P(),
        ),
        out_specs=(P(("patch", "head"), None), P("head", None)),
        check_vma=False,
    )
```

time: 218 us -> 145 us (0.67)
  the two profiles are of different devices: /device:TPU:0 before, /device:TPU:17 now
where the time goes in v1:
time: 145 us; the launch traced here: 144 us
  Pallas kernels  51.4 us (35%)
  starting transfers between devices  49.8 us (34%)
  waiting for transfers between devices  33.2 us (23%)
  local copies, waits for them, and re-layouts  7.82 us (5%)
    pallas_call x4, Pallas kernels, attend_step(): pl.pallas_call(functools.partial(step_body, len(sources), len(left), fina...  26.3 us
    all_to_all x4, waiting for transfers between devices, exchange(): lax.all_to_all(x, ('patch', 'head'), split_axis=0, concat_axis=0, axis_in...  21.2 us
    all_to_all x4, starting transfers between devices, exchange(): lax.all_to_all(x, ('patch', 'head'), split_axis=0, concat_axis=0, axis_in...  18.2 us
    ppermute x6, starting transfers between devices, per_device(): lax.ppermute(block, 'patch', right_pairs)  17.5 us
    ppermute x6, starting transfers between devices, per_device(): lax.ppermute(block, 'patch', left_pairs)  13.9 us
    ppermute x6, waiting for transfers between devices, per_device(): lax.ppermute(block, 'patch', right_pairs)  10.7 us
    pallas_call x1, Pallas kernels, project(): pl.pallas_call(functools.partial(project_body, order), grid=(model // col...  9.76 us
    pallas_call x1, Pallas kernels, attend_first(): pl.pallas_call(functools.partial(first_body, len(stale)), grid_spec=pltpu...  9.56 us
  transfers between devices with their start and end apart: 18, of which 7 were waited for; matrix products, arithmetic and copies ran while one was open for 2% of the time, Pallas kernels for 31%

profile of v1, /device:TPU:17, one launch (start us, length us, event | category | flops | bytes accessed | tf_op | source)
XLA Modules:
  0.0 144.2 jit_solution(2054135545647718454)
XLA Ops:
  0.7 1.7 %copy-done = bf16[128,9216]{1,0:T(8,128)(2,1)S(1)} copy-done((bf16[128,9216]{1,0:T(8,128)(2,1)S(1)}, bf16[128,9216]{1,0:T(8,128)(2,1)}, u32[]{:S(2)}) %copy-start) | copy-done | bytes 2359320
  2.3 2.9 %pack_heads.3 = bf16[8,64,1152]{2,1,0:T(8,128)(2,1)} custom-call(s32[1]{0:T(128)} %bitcast._, bf16[128,9216]{1,0:T(8,128)(2,1)S(1)} %copy-done, bf16[128,9216]{1,0:T(8,128)(2,1)S(1)} %copy-done, bf16[128,9216]{1,0:T(8,128)(2,1)S(1)} %copy-done), custom_call_target="tpu_custom_call" | custom-call | tf_op jit(solution)/shard_map/pack_heads/pallas_call | solution.py:59
  5.2 4.5 %all-to-all-start.1 = ((bf16[8,64,1152]{2,1,0:T(8,128)(2,1)}), bf16[8,64,1152]{2,1,0:T(8,128)(2,1)S(1)}, u32[]{:S(2)}, u32[]{:S(2)}) async-start(bf16[8,64,1152]{2,1,0:T(8,128)(2,1)} %pack_heads.3), calls=%async_computation.1 | async-start | bytes 2359296 | tf_op jit(solution)/shard_map/all_to_all | solution.py:282
  10.6 2.9 %pack_heads.2 = bf16[8,64,1152]{2,1,0:T(8,128)(2,1)} custom-call(s32[1]{0:T(128)} %constant.40.clone.1._, bf16[64,9216]{1,0:T(8,128)(2,1)S(1)} %copy-done.1, bf16[64,9216]{1,0:T(8,128)(2,1)S(1)} %copy-done.1, bf16[64,9216]{1,0:T(8,128)(2,1)S(1)} %copy-done.1), custom_call_target="tpu_custom_call" | custom-call | tf_op jit(solution)/shard_map/pack_heads/pallas_call | solution.py:59
  13.5 12.3 %all-to-all-done.1 = bf16[8,64,1152]{2,1,0:T(8,128)(2,1)S(1)} async-done(((bf16[8,64,1152]{2,1,0:T(8,128)(2,1)}), bf16[8,64,1152]{2,1,0:T(8,128)(2,1)S(1)}, u32[]{:S(2)}, u32[]{:S(2)}) %all-to-all-start.1) | async-done | bytes 1179680 | tf_op jit(solution)/shard_map/all_to_all | solution.py:282
  25.8 3.7 %all-to-all-start = ((bf16[8,64,1152]{2,1,0:T(8,128)(2,1)}), bf16[8,64,1152]{2,1,0:T(8,128)(2,1)S(1)}, u32[]{:S(2)}, u32[]{:S(2)}) async-start(bf16[8,64,1152]{2,1,0:T(8,128)(2,1)} %pack_heads.2), calls=%async_computation | async-start | bytes 2359296 | tf_op jit(solution)/shard_map/all_to_all | solution.py:282
  29.5 2.1 %collective-permute-start.3 = (bf16[2,256,384]{2,1,0:T(8,128)(2,1)S(1)}, bf16[2,256,384]{2,1,0:T(8,128)(2,1)S(1)}, u32[]{:S(2)}, u32[]{:S(2)}) collective-permute-start(bf16[2,256,384]{2,1,0:T(8,128)(2,1)S(1)} %get-tuple-element.29.refs_6_), channel_id=1, source_target_pairs={{8,0},{12,4},{16,8},{20,12},{24,16},{28,20},{9,1},{13,5},{17,9},{2... | collective-permute-start | bytes 1179656 | tf_op jit(solution)/shard_map/ppermute | solution.py:309
  31.6 3.2 %collective-permute-start.1 = (bf16[2,256,384]{2,1,0:T(8,128)(2,1)S(1)}, bf16[2,256,384]{2,1,0:T(8,128)(2,1)}, u32[]{:S(2)}, u32[]{:S(2)}) collective-permute-start(bf16[2,256,384]{2,1,0:T(8,128)(2,1)S(1)} %get-tuple-element.29.refs_6_), channel_id=1, source_target_pairs={{0,8},{4,12},{8,16},{12,20},{16,24},{20,28},{1,9},{5,13},{9,17},{1... | collective-permute-start | bytes 1179656 | tf_op jit(solution)/shard_map/ppermute | solution.py:308
  34.9 1.9 %collective-permute-start.2 = (bf16[2,256,384]{2,1,0:T(8,128)(2,1)S(1)}, bf16[2,256,384]{2,1,0:T(8,128)(2,1)}, u32[]{:S(2)}, u32[]{:S(2)}) collective-permute-start(bf16[2,256,384]{2,1,0:T(8,128)(2,1)S(1)} %collective-permute-done.refs_7_), channel_id=1, source_target_pairs={{0,8},{4,12},{8,16},{12,20},{16,24},{20,28},{1,9},{5,13},{9,17},{1... | collective-permute-start | bytes 1179656 | tf_op jit(solution)/shard_map/ppermute | solution.py:308
  36.8 3.4 %collective-permute-start.4 = (bf16[2,256,384]{2,1,0:T(8,128)(2,1)S(1)}, bf16[2,256,384]{2,1,0:T(8,128)(2,1)}, u32[]{:S(2)}, u32[]{:S(2)}) collective-permute-start(bf16[2,256,384]{2,1,0:T(8,128)(2,1)S(1)} %collective-permute-done.refs_7_), channel_id=1, source_target_pairs={{8,0},{12,4},{16,8},{20,12},{24,16},{28,20},{9,1},{13,5},{17,9},{2... | collective-permute-start | bytes 1179656 | tf_op jit(solution)/shard_map/ppermute | solution.py:309
  40.9 1.3 collective-permute-done.3.refs_8_
  42.2 2.8 %collective-permute-start.7 = (bf16[2,256,384]{2,1,0:T(8,128)(2,1)S(1)}, bf16[2,256,384]{2,1,0:T(8,128)(2,1)}, u32[]{:S(2)}, u32[]{:S(2)}) collective-permute-start(bf16[2,256,384]{2,1,0:T(8,128)(2,1)S(1)} %collective-permute-done.3.refs_8_), channel_id=1, source_target_pairs={{8,0},{12,4},{16,8},{20,12},{9,1},{13,5},{17,9},{21,13},{10,2},{14... | collective-permute-start | bytes 1179656 | tf_op jit(solution)/shard_map/ppermute | solution.py:309
  45.8 1.9 %collective-permute-start.5 = (bf16[2,256,384]{2,1,0:T(8,128)(2,1)}, bf16[2,256,384]{2,1,0:T(8,128)(2,1)}, u32[]{:S(2)}, u32[]{:S(2)}) collective-permute-start(bf16[2,256,384]{2,1,0:T(8,128)(2,1)} %collective-permute-done.1.refs_6_), channel_id=1, source_target_pairs={{8,16},{12,20},{16,24},{20,28},{9,17},{13,21},{17,25},{21,29},{10,... | collective-permute-start | bytes 1179656 | tf_op jit(solution)/shard_map/ppermute | solution.py:308
  47.7 4.7 %collective-permute-done.2.refs_7_ = bf16[2,256,384]{2,1,0:T(8,128)(2,1)} collective-permute-done((bf16[2,256,384]{2,1,0:T(8,128)(2,1)S(1)}, bf16[2,256,384]{2,1,0:T(8,128)(2,1)}, u32[]{:S(2)}, u32[]{:S(2)}) %collective-permute-start.2) | collective-permute-done | bytes 393248 | tf_op jit(solution)/shard_map/ppermute | solution.py:308
  52.4 3.2 %collective-permute-start.6 = (bf16[2,256,384]{2,1,0:T(8,128)(2,1)}, bf16[2,256,384]{2,1,0:T(8,128)(2,1)}, u32[]{:S(2)}, u32[]{:S(2)}) collective-permute-start(bf16[2,256,384]{2,1,0:T(8,128)(2,1)} %collective-permute-done.2.refs_7_), channel_id=1, source_target_pairs={{8,16},{12,20},{16,24},{20,28},{9,17},{13,21},{17,25},{21,29},{10,... | collective-permute-start | bytes 1179656 | tf_op jit(solution)/shard_map/ppermute | solution.py:308
  55.6 3.5 %collective-permute-start.8 = (bf16[2,256,384]{2,1,0:T(8,128)(2,1)}, bf16[2,256,384]{2,1,0:T(8,128)(2,1)}, u32[]{:S(2)}, u32[]{:S(2)}) collective-permute-start(bf16[2,256,384]{2,1,0:T(8,128)(2,1)} %collective-permute-done.4.refs_9_), channel_id=1, source_target_pairs={{8,0},{12,4},{16,8},{20,12},{9,1},{13,5},{17,9},{21,13},{10,2},{14... | collective-permute-start | bytes 1179656 | tf_op jit(solution)/shard_map/ppermute | solution.py:309
  60.8 3.2 %collective-permute-start.9 = (bf16[2,256,384]{2,1,0:T(8,128)(2,1)}, bf16[2,256,384]{2,1,0:T(8,128)(2,1)S(1)}, u32[]{:S(2)}, u32[]{:S(2)}) collective-permute-start(bf16[2,256,384]{2,1,0:T(8,128)(2,1)} %collective-permute-done.5.refs_6_), channel_id=1, source_target_pairs={{16,24},{20,28},{17,25},{21,29},{18,26},{22,30},{19,27},{23,31}} | collective-permute-start | bytes 1179656 | tf_op jit(solution)/shard_map/ppermute | solution.py:308
  64.0 5.2 %collective-permute-done.6.refs_7_ = bf16[2,256,384]{2,1,0:T(8,128)(2,1)} collective-permute-done((bf16[2,256,384]{2,1,0:T(8,128)(2,1)}, bf16[2,256,384]{2,1,0:T(8,128)(2,1)}, u32[]{:S(2)}, u32[]{:S(2)}) %collective-permute-start.6) | collective-permute-done | bytes 393248 | tf_op jit(solution)/shard_map/ppermute | solution.py:308
  69.2 4.0 %collective-permute-start.10 = (bf16[2,256,384]{2,1,0:T(8,128)(2,1)}, bf16[2,256,384]{2,1,0:T(8,128)(2,1)}, u32[]{:S(2)}, u32[]{:S(2)}) collective-permute-start(bf16[2,256,384]{2,1,0:T(8,128)(2,1)} %collective-permute-done.6.refs_7_), channel_id=1, source_target_pairs={{16,24},{20,28},{17,25},{21,29},{18,26},{22,30},{19,27},{23,31}} | collective-permute-start | bytes 1179656 | tf_op jit(solution)/shard_map/ppermute | solution.py:308
  73.2 1.4 collective-permute-start.12
  75.7 9.6 %attend_own.1 = (f32[3,128,512]{2,1,0:T(8,128)S(1)}, f32[3,8,512]{2,1,0:T(8,128)S(1)}, f32[3,128,512]{2,1,0:T(8,128)S(1)}, f32[3,8,512]{2,1,0:T(8,128)S(1)}) custom-call(s32[3]{0:T(128)S(1)} %pad.9.info, bf16[512,1152]{1,0:T(8,128)(2,1)S(1)} %bitcast.22, bf16[512,1152]{1,0:T(8,128)(2,1)S(1)} %bitcast.23, bf16[512,1152]{1,0:T(8,128)(2,1)S(1)} %bitcast.24, ...), custom_call_target="tpu_custom_call" | custom-call | flops 1610612736 | bytes 3145728 | tf_op jit(solution)/shard_map/attend_own/pallas_call | solution.py:139
  85.3 12.1 %attend_arrived.2 = (f32[3,128,512]{2,1,0:T(8,128)S(1)}, f32[3,8,512]{2,1,0:T(8,128)S(1)}, f32[3,128,512]{2,1,0:T(8,128)S(1)}, f32[3,8,512]{2,1,0:T(8,128)S(1)}) custom-call(s32[3]{0:T(128)S(1)} %pad_add_fusion.2.info, bf16[512,1152]{1,0:T(8,128)(2,1)S(1)} %bitcast.25, f32[3,128,512]{2,1,0:T(8,128)S(1)} %get-tuple-element.14.refs_1_, ...), custom_call_target="tpu_custom_call" | custom-call | flops 805306368 | bytes 2359296 | tf_op jit(solution)/shard_map/attend_arrived/pallas_call | solution.py:212
  97.4 7.1 %attend_arrived.3 = (f32[3,128,512]{2,1,0:T(8,128)S(1)}, f32[3,8,512]{2,1,0:T(8,128)S(1)}, f32[3,128,512]{2,1,0:T(8,128)S(1)}, f32[3,8,512]{2,1,0:T(8,128)S(1)}) custom-call(s32[3]{0:T(128)S(1)} %pad_add_fusion.1.info, bf16[512,1152]{1,0:T(8,128)(2,1)S(1)} %bitcast.26, f32[3,128,512]{2,1,0:T(8,128)S(1)} %get-tuple-element.18.refs_1_, ...), custom_call_target="tpu_custom_call" | custom-call | flops 805306368 | bytes 2359296 | tf_op jit(solution)/shard_map/attend_arrived/pallas_call | solution.py:212
  104.5 3.5 %attend_last.3 = bf16[512,384]{1,0:T(8,128)(2,1)} custom-call(s32[3]{0:T(128)S(1)} %pad_add_fusion.info, bf16[512,1152]{1,0:T(8,128)(2,1)S(1)} %bitcast.21, f32[3,128,512]{2,1,0:T(8,128)S(1)} %get-tuple-element.24.refs_1_, f32[3,8,512]{2,1,0:T(8,128)S(1)} %get-tuple-element.25.refs_2_, bf16[2,256,384]{2,1,0:T(8,128)(2,1)S(1)} %collective-permute-done.9.refs_3_, ...), custom_call_target="tpu_custom_call" | custom-call | flops 402653184 | bytes 1572864 | tf_op jit(solution)/shard_map/attend_last/pallas_call | solution.py:212
  108.1 6.4 %all-to-all-start.3 = ((bf16[8,64,384]{2,1,0:T(8,128)(2,1)}), bf16[8,64,384]{2,1,0:T(8,128)(2,1)}, u32[]{:S(2)}, u32[]{:S(2)}) async-start(bf16[8,64,384]{2,1,0:T(8,128)(2,1)} %bitcast.11), calls=%async_computation.3 | async-start | bytes 786432 | tf_op jit(solution)/shard_map/all_to_all | solution.py:282
  114.5 1.1 copy-done.3
  115.6 3.5 %attend_last.2 = bf16[512,384]{1,0:T(8,128)(2,1)} custom-call(s32[3]{0:T(128)S(1)} %pad_add_fusion.info, bf16[512,1152]{1,0:T(8,128)(2,1)S(1)} %bitcast.27, f32[3,128,512]{2,1,0:T(8,128)S(1)} %copy-done.3, f32[3,8,512]{2,1,0:T(8,128)S(1)} %get-tuple-element.23.refs_2_, bf16[2,256,384]{2,1,0:T(8,128)(2,1)S(1)} %collective-permute-done.9.refs_3_, ...), custom_call_target="tpu_custom_call" | custom-call | flops 402653184 | bytes 1572864 | tf_op jit(solution)/shard_map/attend_last/pallas_call | solution.py:212
  119.2 3.1 %all-to-all-done.3 = bf16[8,64,384]{2,1,0:T(8,128)(2,1)} async-done(((bf16[8,64,384]{2,1,0:T(8,128)(2,1)}), bf16[8,64,384]{2,1,0:T(8,128)(2,1)}, u32[]{:S(2)}, u32[]{:S(2)}) %all-to-all-start.3) | async-done | bytes 393248 | tf_op jit(solution)/shard_map/all_to_all | solution.py:282
  122.2 3.6 %all-to-all-start.2 = ((bf16[8,64,384]{2,1,0:T(8,128)(2,1)}), bf16[8,64,384]{2,1,0:T(8,128)(2,1)S(1)}, u32[]{:S(2)}, u32[]{:S(2)}) async-start(bf16[8,64,384]{2,1,0:T(8,128)(2,1)} %bitcast.9), calls=%async_computation.2 | async-start | bytes 786432 | tf_op jit(solution)/shard_map/all_to_all | solution.py:282
  125.8 1.4 copy.10
  127.7 5.8 %all-to-all-done.2.x_ref = bf16[8,64,384]{2,1,0:T(8,128)(2,1)S(1)} async-done(((bf16[8,64,384]{2,1,0:T(8,128)(2,1)}), bf16[8,64,384]{2,1,0:T(8,128)(2,1)S(1)}, u32[]{:S(2)}, u32[]{:S(2)}) %all-to-all-start.2) | async-done | bytes 393248 | tf_op jit(solution)/shard_map/all_to_all | solution.py:282
  133.5 9.8 %project.1 = bf16[64,3072]{1,0:T(8,128)(2,1)} custom-call(bf16[8,64,384]{2,1,0:T(8,128)(2,1)S(1)} %all-to-all-done.2.x_ref, bf16[3072,3072]{1,0:T(8,128)(2,1)} %weight.1, bf16[64,3072]{1,0:T(8,128)(2,1)S(1)} %copy-done.8, f32[1,3072]{1,0:T(1,128)S(1)} %bitcast.28), custom_call_target="tpu_custom_call" | custom-call | flops 1207959552 | bytes 18874368 | tf_op jit(solution)/shard_map/project/pallas_call | solution.py:242
  (43 shorter events, 6.5 us)
Async XLA Ops:
  0.6 1.7 %copy-start = (bf16[128,9216]{1,0:T(8,128)(2,1)S(1)}, bf16[128,9216]{1,0:T(8,128)(2,1)}, u32[]{:S(2)}) copy-start(bf16[128,9216]{1,0:T(8,128)(2,1)} %refs_2_.3) | copy-start | bytes 7077892
  5.2 4.5 %copy-start.10 = (bf16[2,256,768]{2,1,0:T(8,128)(2,1)S(1)}, bf16[2,256,768]{2,1,0:T(8,128)(2,1)}, u32[]{:S(2)}) copy-start(bf16[2,256,768]{2,1,0:T(8,128)(2,1)} %param.8) | copy-start | bytes 2359300
  5.2 5.4 %copy-start.1 = (bf16[64,9216]{1,0:T(8,128)(2,1)S(1)}, bf16[64,9216]{1,0:T(8,128)(2,1)}, u32[]{:S(2)}) copy-start(bf16[64,9216]{1,0:T(8,128)(2,1)} %refs_2_.2) | copy-start | bytes 3538948
  5.2 20.6 %all-to-all-start.1 = ((bf16[8,64,1152]{2,1,0:T(8,128)(2,1)}), bf16[8,64,1152]{2,1,0:T(8,128)(2,1)S(1)}, u32[]{:S(2)}, u32[]{:S(2)}) async-start(bf16[8,64,1152]{2,1,0:T(8,128)(2,1)} %pack_heads.3), calls=%async_computation.1 | async-start | bytes 2359296 | tf_op jit(solution)/shard_map/all_to_all | solution.py:282
  10.6 24.3 %collective-permute-start = (bf16[2,256,384]{2,1,0:T(8,128)(2,1)}, bf16[2,256,384]{2,1,0:T(8,128)(2,1)S(1)}, u32[]{:S(2)}, u32[]{:S(2)}) collective-permute-start(bf16[2,256,384]{2,1,0:T(8,128)(2,1)} %get-tuple-element.28), channel_id=1, source_target_pairs={{0,4},{4,0},{8,12},{12,8},{16,20},{20,16},{24,28},{28,24},{1,5},{5... | collective-permute-start | bytes 1179656 | tf_op jit(solution)/shard_map/ppermute | solution.py:291
  25.8 48.9 %all-to-all-start = ((bf16[8,64,1152]{2,1,0:T(8,128)(2,1)}), bf16[8,64,1152]{2,1,0:T(8,128)(2,1)S(1)}, u32[]{:S(2)}, u32[]{:S(2)}) async-start(bf16[8,64,1152]{2,1,0:T(8,128)(2,1)} %pack_heads.2), calls=%async_computation | async-start | bytes 2359296 | tf_op jit(solution)/shard_map/all_to_all | solution.py:282
  29.5 12.7 %collective-permute-start.3 = (bf16[2,256,384]{2,1,0:T(8,128)(2,1)S(1)}, bf16[2,256,384]{2,1,0:T(8,128)(2,1)S(1)}, u32[]{:S(2)}, u32[]{:S(2)}) collective-permute-start(bf16[2,256,384]{2,1,0:T(8,128)(2,1)S(1)} %get-tuple-element.29.refs_6_), channel_id=1, source_target_pairs={{8,0},{12,4},{16,8},{20,12},{24,16},{28,20},{9,1},{13,5},{17,9},{2... | collective-permute-start | bytes 1179656 | tf_op jit(solution)/shard_map/ppermute | solution.py:309
  31.6 14.2 %collective-permute-start.1 = (bf16[2,256,384]{2,1,0:T(8,128)(2,1)S(1)}, bf16[2,256,384]{2,1,0:T(8,128)(2,1)}, u32[]{:S(2)}, u32[]{:S(2)}) collective-permute-start(bf16[2,256,384]{2,1,0:T(8,128)(2,1)S(1)} %get-tuple-element.29.refs_6_), channel_id=1, source_target_pairs={{0,8},{4,12},{8,16},{12,20},{16,24},{20,28},{1,9},{5,13},{9,17},{1... | collective-permute-start | bytes 1179656 | tf_op jit(solution)/shard_map/ppermute | solution.py:308
  34.9 17.5 %collective-permute-start.2 = (bf16[2,256,384]{2,1,0:T(8,128)(2,1)S(1)}, bf16[2,256,384]{2,1,0:T(8,128)(2,1)}, u32[]{:S(2)}, u32[]{:S(2)}) collective-permute-start(bf16[2,256,384]{2,1,0:T(8,128)(2,1)S(1)} %collective-permute-done.refs_7_), channel_id=1, source_target_pairs={{0,8},{4,12},{8,16},{12,20},{16,24},{20,28},{1,9},{5,13},{9,17},{1... | collective-permute-start | bytes 1179656 | tf_op jit(solution)/shard_map/ppermute | solution.py:308
  36.8 18.8 %collective-permute-start.4 = (bf16[2,256,384]{2,1,0:T(8,128)(2,1)S(1)}, bf16[2,256,384]{2,1,0:T(8,128)(2,1)}, u32[]{:S(2)}, u32[]{:S(2)}) collective-permute-start(bf16[2,256,384]{2,1,0:T(8,128)(2,1)S(1)} %collective-permute-done.refs_7_), channel_id=1, source_target_pairs={{8,0},{12,4},{16,8},{20,12},{24,16},{28,20},{9,1},{13,5},{17,9},{2... | collective-permute-start | bytes 1179656 | tf_op jit(solution)/shard_map/ppermute | solution.py:309
  40.2 0.7 copy-start.4
  42.2 17.1 %collective-permute-start.7 = (bf16[2,256,384]{2,1,0:T(8,128)(2,1)S(1)}, bf16[2,256,384]{2,1,0:T(8,128)(2,1)}, u32[]{:S(2)}, u32[]{:S(2)}) collective-permute-start(bf16[2,256,384]{2,1,0:T(8,128)(2,1)S(1)} %collective-permute-done.3.refs_8_), channel_id=1, source_target_pairs={{8,0},{12,4},{16,8},{20,12},{9,1},{13,5},{17,9},{21,13},{10,2},{14... | collective-permute-start | bytes 1179656 | tf_op jit(solution)/shard_map/ppermute | solution.py:309
  45.0 0.7 copy-start.6
  45.8 15.0 %collective-permute-start.5 = (bf16[2,256,384]{2,1,0:T(8,128)(2,1)}, bf16[2,256,384]{2,1,0:T(8,128)(2,1)}, u32[]{:S(2)}, u32[]{:S(2)}) collective-permute-start(bf16[2,256,384]{2,1,0:T(8,128)(2,1)} %collective-permute-done.1.refs_6_), channel_id=1, source_target_pairs={{8,16},{12,20},{16,24},{20,28},{9,17},{13,21},{17,25},{21,29},{10,... | collective-permute-start | bytes 1179656 | tf_op jit(solution)/shard_map/ppermute | solution.py:308
  52.4 16.9 %collective-permute-start.6 = (bf16[2,256,384]{2,1,0:T(8,128)(2,1)}, bf16[2,256,384]{2,1,0:T(8,128)(2,1)}, u32[]{:S(2)}, u32[]{:S(2)}) collective-permute-start(bf16[2,256,384]{2,1,0:T(8,128)(2,1)} %collective-permute-done.2.refs_7_), channel_id=1, source_target_pairs={{8,16},{12,20},{16,24},{20,28},{9,17},{13,21},{17,25},{21,29},{10,... | collective-permute-start | bytes 1179656 | tf_op jit(solution)/shard_map/ppermute | solution.py:308
  55.6 17.6 %collective-permute-start.8 = (bf16[2,256,384]{2,1,0:T(8,128)(2,1)}, bf16[2,256,384]{2,1,0:T(8,128)(2,1)}, u32[]{:S(2)}, u32[]{:S(2)}) collective-permute-start(bf16[2,256,384]{2,1,0:T(8,128)(2,1)} %collective-permute-done.4.refs_9_), channel_id=1, source_target_pairs={{8,0},{12,4},{16,8},{20,12},{9,1},{13,5},{17,9},{21,13},{10,2},{14... | collective-permute-start | bytes 1179656 | tf_op jit(solution)/shard_map/ppermute | solution.py:309
  59.3 45.2 %collective-permute-start.11 = (bf16[2,256,384]{2,1,0:T(8,128)(2,1)}, bf16[2,256,384]{2,1,0:T(8,128)(2,1)S(1)}, u32[]{:S(2)}, u32[]{:S(2)}) collective-permute-start(bf16[2,256,384]{2,1,0:T(8,128)(2,1)} %collective-permute-done.7.refs_8_), channel_id=1, source_target_pairs={{8,0},{12,4},{9,1},{13,5},{10,2},{14,6},{11,3},{15,7}} | collective-permute-start | bytes 1179656 | tf_op jit(solution)/shard_map/ppermute | solution.py:309
  60.8 43.7 %collective-permute-start.9 = (bf16[2,256,384]{2,1,0:T(8,128)(2,1)}, bf16[2,256,384]{2,1,0:T(8,128)(2,1)S(1)}, u32[]{:S(2)}, u32[]{:S(2)}) collective-permute-start(bf16[2,256,384]{2,1,0:T(8,128)(2,1)} %collective-permute-done.5.refs_6_), channel_id=1, source_target_pairs={{16,24},{20,28},{17,25},{21,29},{18,26},{22,30},{19,27},{23,31}} | collective-permute-start | bytes 1179656 | tf_op jit(solution)/shard_map/ppermute | solution.py:308
  69.2 35.3 %collective-permute-start.10 = (bf16[2,256,384]{2,1,0:T(8,128)(2,1)}, bf16[2,256,384]{2,1,0:T(8,128)(2,1)}, u32[]{:S(2)}, u32[]{:S(2)}) collective-permute-start(bf16[2,256,384]{2,1,0:T(8,128)(2,1)} %collective-permute-done.6.refs_7_), channel_id=1, source_target_pairs={{16,24},{20,28},{17,25},{21,29},{18,26},{22,30},{19,27},{23,31}} | collective-permute-start | bytes 1179656 | tf_op jit(solution)/shard_map/ppermute | solution.py:308
  73.2 31.3 %collective-permute-start.12 = (bf16[2,256,384]{2,1,0:T(8,128)(2,1)}, bf16[2,256,384]{2,1,0:T(8,128)(2,1)}, u32[]{:S(2)}, u32[]{:S(2)}) collective-permute-start(bf16[2,256,384]{2,1,0:T(8,128)(2,1)} %collective-permute-done.8.refs_9_), channel_id=1, source_target_pairs={{8,0},{12,4},{9,1},{13,5},{10,2},{14,6},{11,3},{15,7}} | collective-permute-start | bytes 1179656 | tf_op jit(solution)/shard_map/ppermute | solution.py:309
  74.7 1.0 copy-start.5
  75.7 9.6 %copy-start.7 = (bf16[2,256,384]{2,1,0:T(8,128)(2,1)S(1)}, bf16[2,256,384]{2,1,0:T(8,128)(2,1)}, u32[]{:S(2)}) copy-start(bf16[2,256,384]{2,1,0:T(8,128)(2,1)} %copy-done.6) | copy-start | bytes 1179652
  104.5 3.6 %copy-start.2 = (f32[3,128,512]{2,1,0:T(8,128)}, f32[3,128,512]{2,1,0:T(8,128)S(1)}, u32[]{:S(2)}) copy-start(f32[3,128,512]{2,1,0:T(8,128)S(1)} %get-tuple-element.22.refs_1_) | copy-start | bytes 2359300
  108.1 14.2 %all-to-all-start.3 = ((bf16[8,64,384]{2,1,0:T(8,128)(2,1)}), bf16[8,64,384]{2,1,0:T(8,128)(2,1)}, u32[]{:S(2)}, u32[]{:S(2)}) async-start(bf16[8,64,384]{2,1,0:T(8,128)(2,1)} %bitcast.11), calls=%async_computation.3 | async-start | bytes 786432 | tf_op jit(solution)/shard_map/all_to_all | solution.py:282
  114.5 1.1 copy-start.3
  119.2 14.3 %copy-start.8 = (bf16[64,3072]{1,0:T(8,128)(2,1)S(1)}, bf16[64,3072]{1,0:T(8,128)(2,1)}, u32[]{:S(2)}) copy-start(bf16[64,3072]{1,0:T(8,128)(2,1)} %residual.1) | copy-start | bytes 1179652
  119.2 14.3 %copy-start.9 = (f32[3072]{0:T(1024)S(1)}, f32[3072]{0:T(1024)}, u32[]{:S(2)}) copy-start(f32[3072]{0:T(1024)} %param.10) | copy-start | bytes 36868
  122.2 11.2 %all-to-all-start.2 = ((bf16[8,64,384]{2,1,0:T(8,128)(2,1)}), bf16[8,64,384]{2,1,0:T(8,128)(2,1)S(1)}, u32[]{:S(2)}, u32[]{:S(2)}) async-start(bf16[8,64,384]{2,1,0:T(8,128)(2,1)} %bitcast.9), calls=%async_computation.2 | async-start | bytes 786432 | tf_op jit(solution)/shard_map/all_to_all | solution.py:282
  127.5 15.7 %collective-permute-start.13 = (bf16[64,3072]{1,0:T(8,128)(2,1)S(1)}, bf16[64,3072]{1,0:T(8,128)(2,1)S(1)}, u32[]{:S(2)}, u32[]{:S(2)}) collective-permute-start(bf16[64,3072]{1,0:T(8,128)(2,1)S(1)} %reshape.32), channel_id=1, source_target_pairs={{0,4},{4,0},{8,12},{12,8},{16,20},{20,16},{24,28},{28,24},{1,5},{5... | collective-permute-start | bytes 1179656 | tf_op jit(solution)/shard_map/ppermute | solution.py:329

commit v2 on v0

v2 whole, which is shorter than its diff:
```python
import functools
import math

import jax
import jax.numpy as jnp
from jax import lax
from jax.experimental import pallas as pl
from jax.experimental.pallas import tpu as pltpu
from jax.sharding import PartitionSpec as P

HD = 128
SCALE = math.log2(math.e) / math.sqrt(HD)
VMEM_LIMIT = 24 * 1024 * 1024
TILE = 256
LARGE = 2.0**60


def params():
    return pltpu.CompilerParams(
        vmem_limit_bytes=VMEM_LIMIT, dimension_semantics=("arbitrary",)
    )


def pack_body(info, *refs):
    sources, packed = refs[:6], refs[-1]
    first = 0
    for group in (sources[:3], sources[3:]):
        rows, width = group[0].shape
        for part, source in enumerate(group):
            packed[0, first : first + rows, part * width : (part + 1) * width] = source[...]
        first += rows


def pack(core, img_qkv, txt_qkv, text_rows, destinations, column_block, width, after):
    img_rows = img_qkv.shape[0]
    blocks = img_qkv.shape[1] // 3 // width

    def source(rows, part, by_core):
        def place(d, info):
            return (info[0] if by_core else 0, part * blocks + column_block(d))

        return pl.BlockSpec((rows, width), place)

    return pl.pallas_call(
        pack_body,
        grid_spec=pltpu.PrefetchScalarGridSpec(
            num_scalar_prefetch=1,
            grid=(destinations,),
            in_specs=[source(img_rows, part, False) for part in range(3)]
            + [source(text_rows, part, True) for part in range(3)]
            + [pl.BlockSpec(memory_space=pl.ANY)] * len(after),
            out_specs=pl.BlockSpec(
                (1, img_rows + text_rows, 3 * width), lambda d, info: (d, 0, 0)
            ),
        ),
        out_shape=jax.ShapeDtypeStruct(
            (destinations, img_rows + text_rows, 3 * width), img_qkv.dtype
        ),
        compiler_params=params(),
        name="pack_heads",
    )(core, img_qkv, img_qkv, img_qkv, txt_qkv, txt_qkv, txt_qkv, *after)


def dot(first, second, contract):
    return lax.dot_general(
        first, second, ((contract[:1], contract[1:]), ((), ())), preferred_element_type=jnp.float32
    )


def with_ones(block):
    return jnp.concatenate([block, jnp.ones_like(block)], axis=1)


def reference_columns(row_max):
    reference = row_max.astype(jnp.bfloat16).astype(jnp.float32)
    return jnp.broadcast_to(reference * (-1.0 / HD), (row_max.shape[0], HD)).astype(jnp.bfloat16)


def weighted(queries, key_rows, values):
    weights = jnp.exp2(dot(queries, key_rows, (1, 1)) * SCALE).astype(jnp.bfloat16)
    return dot(weights, values, (1, 0))


def tiles_of(rows):
    tile = min(TILE, rows)
    return [slice(first, min(first + tile, rows)) for first in range(0, rows, tile)]


def split_rows(block, img_rows):
    return (
        block[:, :img_rows, :].reshape(-1, HD),
        block[:, img_rows:, :].reshape(-1, HD),
    )


def until_small(flag, total, attempt):
    flag[0] = 1

    @pl.loop(0, 2)
    def _(turn):
        @pl.when(flag[0] == 1)
        def _():
            attempt(turn)
            flag[0] = jnp.where(jnp.max(total[0, :, HD:]) > LARGE, 1, 0).astype(jnp.int32)


def most_body(pair, img_rows, sides, info, *refs):
    q_ref, k_ref, v_ref = refs[:3]
    stale = refs[3 : 3 + pair]
    arrived = refs[3 + pair : 3 + pair + sides * pair]
    aug, total, flag = refs[3 + pair + sides * pair :]
    core = info[0]
    k_img, k_txt = split_rows(k_ref[...], img_rows)
    v_img, v_txt = split_rows(v_ref[...], img_rows)
    q_img, q_txt = split_rows(q_ref[...], img_rows)
    fresh_rows = q_img.shape[0]
    group_rows = fresh_rows // pair
    rows = fresh_rows + q_txt.shape[0]

    def queries_at(span):
        if span.stop <= fresh_rows:
            return q_img[span, :]
        return q_txt[span.start - fresh_rows : span.stop - fresh_rows, :]

    def own_sets():
        sets = []
        for group in range(pair):
            span = slice(group * group_rows, (group + 1) * group_rows)
            key_rows, values = [k_txt, k_img[span, :]], [v_txt, v_img[span, :]]
            if pair == 2:
                mine = core == group
                key_rows.append(jnp.where(mine, stale[1][0], stale[0][0]))
                values.append(jnp.where(mine, stale[1][1], stale[0][1]))
            sets.append((span, key_rows, values))
        sets.append(
            (
                slice(fresh_rows, rows),
                [k_txt] + [block[0] for block in stale],
                [v_txt] + [block[1] for block in stale],
            )
        )
        for span, key_rows, values in sets:
            key_rows, values = jnp.concatenate(key_rows, 0), jnp.concatenate(values, 0)
            spans = [
                slice(span.start + t.start, span.start + t.stop)
                for t in tiles_of(span.stop - span.start)
            ]
            yield spans, key_rows, values

    def each_arrived(act):
        for side in range(sides):
            blocks = arrived[side * pair : (side + 1) * pair]

            @pl.when(info[1 + side] == 1)
            def _():
                key_rows = jnp.concatenate([block[0] for block in blocks], 0)
                values = jnp.concatenate([block[1] for block in blocks], 0)
                for first in range(0, rows, fresh_rows):
                    for tile in tiles_of(min(fresh_rows, rows - first)):
                        act(slice(first + tile.start, first + tile.stop), key_rows, values)

    def largest(span, key_rows):
        return jnp.max(dot(queries_at(span), key_rows, (1, 1)), axis=1, keepdims=True)

    def attempt(turn):
        @pl.when(turn == 0)
        def _():
            for spans, key_rows, _ in own_sets():
                for span in spans:
                    aug[0, span, :] = reference_columns(
                        largest(span, key_rows[: min(256, key_rows.shape[0]), :])
                    )

        @pl.when(turn == 1)
        def _():
            def raise_to(span, key_rows, _):
                total[0, span, :] = jnp.maximum(
                    total[0, span, :], jnp.broadcast_to(largest(span, key_rows), total[0, span, :].shape)
                )

            for spans, key_rows, _ in own_sets():
                for span in spans:
                    total[0, span, :] = jnp.broadcast_to(
                        largest(span, key_rows), total[0, span, :].shape
                    )
            each_arrived(raise_to)
            for spans, _, _ in own_sets():
                for span in spans:
                    aug[0, span, :] = reference_columns(total[0, span, :1])

        def queries_of(span):
            return jnp.concatenate([queries_at(span), aug[0, span, :]], axis=1)

        def add(span, key_rows, values):
            total[0, span, :] += weighted(queries_of(span), with_ones(key_rows), with_ones(values))

        for spans, key_rows, values in own_sets():
            key_rows, values = with_ones(key_rows), with_ones(values)
            for span in spans:
                total[0, span, :] = weighted(queries_of(span), key_rows, values)
        each_arrived(add)

    until_small(flag, total, attempt)


def column_spec(array, offset):
    return pl.BlockSpec(array.shape[:2] + (HD,), lambda h, info: (0, 0, offset + h))


def head_spec(shape):
    return pl.BlockSpec((1,) + shape[1:], lambda h, info: (h, 0, 0))


def attend_cost(queries, keys, heads):
    return pl.CostEstimate(
        flops=4 * queries * keys * heads * HD,
        bytes_accessed=4 * queries * heads * HD + 4 * keys * heads * HD,
        transcendentals=queries * keys * heads,
    )


def attend_most(info, qkv, img_rows, stale, arrived):
    heads = qkv.shape[2] // (3 * HD)
    rows = qkv.shape[0] * qkv.shape[1]
    blocks = list(stale) + [block for side in arrived for block in side]
    shapes = [
        jax.ShapeDtypeStruct((heads, rows, HD), jnp.bfloat16),
        jax.ShapeDtypeStruct((heads, rows, 2 * HD), jnp.float32),
    ]
    keys = sum(block.shape[1] for block in blocks) // 2 + rows // 2
    return pl.pallas_call(
        functools.partial(most_body, len(stale), img_rows, len(arrived)),
        grid_spec=pltpu.PrefetchScalarGridSpec(
            num_scalar_prefetch=1,
            grid=(heads,),
            in_specs=[column_spec(qkv, part * heads) for part in range(3)]
            + [column_spec(block, 0) for block in blocks],
            out_specs=[head_spec(shape.shape) for shape in shapes],
            scratch_shapes=[pltpu.SMEM((1,), jnp.int32)],
        ),
        out_shape=shapes,
        compiler_params=params(),
        cost_estimate=attend_cost(rows, keys, heads),
        name="attend_most",
    )(info, qkv, qkv, qkv, *blocks)


def last_body(pair, img_rows, sides, info, *refs):
    q_ref, aug_ref, total_ref = refs[:3]
    arrived = refs[3 : 3 + sides * pair]
    out, total, shift, flag = refs[3 + sides * pair :]
    q_img, q_txt = split_rows(q_ref[...], img_rows)
    fresh_rows = q_img.shape[0]
    rows = total.shape[1]

    def queries_at(span):
        if span.stop <= fresh_rows:
            queries = q_img[span, :]
        else:
            queries = q_txt[span.start - fresh_rows : span.stop - fresh_rows, :]
        return jnp.concatenate([queries, aug_ref[0, span, :]], axis=1)

    def each_arrived(act):
        for side in range(sides):
            blocks = arrived[side * pair : (side + 1) * pair]

            @pl.when(info[1 + side] == 1)
            def _():
                key_rows = with_ones(jnp.concatenate([block[0] for block in blocks], 0))
                values = with_ones(jnp.concatenate([block[1] for block in blocks], 0))
                for first, last in ((0, fresh_rows), (fresh_rows, rows)):
                    for tile in tiles_of(last - first):
                        act(slice(first + tile.start, first + tile.stop), key_rows, values)

    def add(span, key_rows, values):
        total[0, span, :] += weighted(queries_at(span), key_rows, values)

    def raise_to(span, key_rows, _):
        above = jnp.max(dot(queries_at(span), key_rows, (1, 1)), axis=1, keepdims=True)
        shift[span, :] = jnp.maximum(shift[span, :], jnp.broadcast_to(above, shift[span, :].shape))

    def add_shifted(span, key_rows, values):
        scores = dot(queries_at(span), key_rows, (1, 1)) - shift[span, :1]
        total[0, span, :] += dot(jnp.exp2(scores * SCALE).astype(jnp.bfloat16), values, (1, 0))

    def attempt(turn):
        @pl.when(turn == 0)
        def _():
            total[...] = total_ref[...]
            each_arrived(add)

        @pl.when(turn == 1)
        def _():
            shift[...] = jnp.zeros_like(shift)
            each_arrived(raise_to)
            keep = jnp.exp2(shift[...] * -SCALE)
            total[0] = total_ref[0] * jnp.concatenate([keep, keep], axis=1)
            each_arrived(add_shifted)

    until_small(flag, total, attempt)
    attended = (total[0, :, :HD] / total[0, :, HD:]).astype(out.dtype)
    destinations = out.shape[0]
    out[:, :img_rows, :] = attended[:fresh_rows].reshape(destinations, img_rows, HD)
    out[:, img_rows:, :] = attended[fresh_rows:].reshape(destinations, -1, HD)


def attend_last(info, qkv, img_rows, state, arrived):
    heads = qkv.shape[2] // (3 * HD)
    rows = qkv.shape[0] * qkv.shape[1]
    blocks = [block for side in arrived for block in side]
    return pl.pallas_call(
        functools.partial(last_body, len(arrived[0]), img_rows, len(arrived)),
        grid_spec=pltpu.PrefetchScalarGridSpec(
            num_scalar_prefetch=1,
            grid=(heads,),
            in_specs=[column_spec(qkv, 0)]
            + [head_spec(part.shape) for part in state]
            + [column_spec(block, 0) for block in blocks],
            out_specs=pl.BlockSpec(qkv.shape[:2] + (HD,), lambda h, info: (0, 0, h)),
            scratch_shapes=[
                pltpu.VMEM((1, rows, 2 * HD), jnp.float32),
                pltpu.VMEM((rows, HD), jnp.float32),
                pltpu.SMEM((1,), jnp.int32),
            ],
        ),
        out_shape=jax.ShapeDtypeStruct(qkv.shape[:2] + (heads * HD,), qkv.dtype),
        compiler_params=params(),
        cost_estimate=attend_cost(rows, blocks[0].shape[1] * len(arrived[0]), heads),
        name="attend_last",
    )(info, qkv, *state, *blocks)


def project_body(order, x_ref, weight, residual, gate, out, flat):
    @pl.when(pl.program_id(0) == 0)
    def _():
        rows, width = flat.shape[0], x_ref.shape[2]
        for source, place in enumerate(order):
            flat[:, place * width : (place + 1) * width] = x_ref[source, :rows, :]

    projected = jnp.dot(flat[...], weight[...], preferred_element_type=jnp.float32)
    out[...] = (residual[...].astype(jnp.float32) + gate[...] * projected).astype(out.dtype)


def project(x, order, weight, residual, gate):
    rows, model = residual.shape
    columns = 512 if model % 512 == 0 else HD
    return pl.pallas_call(
        functools.partial(project_body, order),
        grid=(model // columns,),
        in_specs=[
            pl.BlockSpec(x.shape, lambda n: (0, 0, 0)),
            pl.BlockSpec((weight.shape[0], columns), lambda n: (0, n)),
            pl.BlockSpec((rows, columns), lambda n: (0, n)),
            pl.BlockSpec((1, columns), lambda n: (0, n)),
        ],
        out_specs=pl.BlockSpec((rows, columns), lambda n: (0, n)),
        out_shape=jax.ShapeDtypeStruct((rows, model), residual.dtype),
        scratch_shapes=[pltpu.VMEM((rows, weight.shape[0]), x.dtype)],
        compiler_params=params(),
        cost_estimate=pl.CostEstimate(
            flops=2 * rows * model * model, bytes_accessed=2 * model * model, transcendentals=0
        ),
        name="project",
    )(x, weight, residual, gate.reshape(1, model))


def unpack_body(order, first, x_ref, out):
    width = x_ref.shape[2]
    for source, place in enumerate(order):
        out[:, place * width : (place + 1) * width] = x_ref[source, first:, :]


def unpack_text(x, order, first):
    model = x.shape[0] * x.shape[2]
    return pl.pallas_call(
        functools.partial(unpack_body, order, first),
        grid=(1,),
        in_specs=[pl.BlockSpec(x.shape, lambda n: (0, 0, 0))],
        out_specs=pl.BlockSpec((x.shape[1] - first, model), lambda n: (0, 0)),
        out_shape=jax.ShapeDtypeStruct((x.shape[1] - first, model), x.dtype),
        compiler_params=params(),
        name="unpack_text",
    )(x)


def per_device(img_qkv, txt_qkv, stale_kv, residual, gate_scale, proj_weight):
    patches, head_owners = lax.axis_size("patch"), lax.axis_size("head")
    patch = lax.axis_index("patch")
    owned_heads = stale_kv.shape[2] // HD
    pair = 2 if patches % 2 == 0 and owned_heads % 2 == 0 else 1
    planes = patches // pair
    plane, core = patch // pair, patch % pair
    width = stale_kv.shape[2] // pair
    img_rows = img_qkv.shape[0]
    text_rows = txt_qkv.shape[0] // pair
    destinations = pair * head_owners

    def column_block(d):
        return (d % head_owners) * pair + d // head_owners

    order = [column_block(d) for d in range(destinations)]
    groups = [[g * destinations + d for d in range(destinations)] for g in range(planes)]

    def exchange(x):
        return lax.all_to_all(
            x, ("patch", "head"), split_axis=0, concat_axis=0, axis_index_groups=groups, tiled=True
        )

    swap_pairs = [(p, p + 1 - 2 * (p % 2)) for p in range(patches)]
    stale = [lax.dynamic_slice_in_dim(stale_kv, core * width, width, 2)]
    if pair == 2:
        theirs = lax.dynamic_slice_in_dim(stale_kv, (1 - core) * width, width, 2)
        stale.append(lax.ppermute(theirs, "patch", swap_pairs))

    core_only = core.astype(jnp.int32).reshape(1)
    qkv = exchange(
        pack(core_only, img_qkv, txt_qkv, text_rows, destinations, column_block, width, stale[1:])
    )

    arrived, valid = [], []
    from_left, from_right = stale, stale
    for step in range(1, planes):
        right_pairs = [(p, p + pair) for p in range((step - 1) * pair, patches - pair)]
        left_pairs = [(p + pair, p) for p in range(0, patches - step * pair)]
        from_left = [lax.ppermute(block, "patch", right_pairs) for block in from_left]
        from_right = [lax.ppermute(block, "patch", left_pairs) for block in from_right]
        arrived += [from_left, from_right]
        valid += [plane >= step, plane + step < planes]
    early = max(0, len(arrived) - 2)
    info = jnp.stack([core] + valid[:early]).astype(jnp.int32)
    last_info = jnp.stack([core] + valid[early:]).astype(jnp.int32)
    state = attend_most(info, qkv, img_rows, stale, arrived[:early])
    attended = attend_last(last_info, qkv, img_rows, state, arrived[early:])

    back = exchange(attended)
    text_out = unpack_text(back, order, img_rows)
    if pair == 2:
        other = lax.ppermute(text_out, "patch", swap_pairs)
        lower = core == 0
        text_out = jnp.concatenate(
            [jnp.where(lower, text_out, other), jnp.where(lower, other, text_out)], 0
        )
    image_out = project(back, order, proj_weight, residual, gate_scale)
    return (image_out, text_out)


def solution(mesh):
    return jax.shard_map(
        per_device,
        mesh=mesh,
        in_specs=(
            P(("patch", "head"), None),
            P("head", None),
            P(None, "patch", "head"),
            P(("patch", "head"), None),
            P(),
            P(),
        ),
        out_specs=(P(("patch", "head"), None), P("head", None)),
        check_vma=False,
    )
```

time: 218 us -> 114 us (0.52)
  the two profiles are of different devices: /device:TPU:0 before, /device:TPU:17 now
where the time goes in v2:
time: 114 us; the launch traced here: 113 us
  starting transfers between devices  37.2 us (33%)
  Pallas kernels  27.3 us (24%)
  blocking collectives  18.1 us (16%)
  local copies, waits for them, and re-layouts  16.1 us (14%)
  waiting for transfers between devices  12.3 us (11%)
    all_to_all x1, blocking collectives, exchange(): lax.all_to_all(x, ('patch', 'head'), split_axis=0, concat_axis=0, axis_in...  18.1 us
    ppermute x6, starting transfers between devices, per_device(): lax.ppermute(block, 'patch', right_pairs)  17.4 us
    pallas_call x1, Pallas kernels, attend_most(): pl.pallas_call(functools.partial(most_body, len(stale), img_rows, len(arr...  16.4 us
    unnamed x24, local copies, waits for them, and re-layouts  14.7 us
    ppermute x6, starting transfers between devices, per_device(): lax.ppermute(block, 'patch', left_pairs)  14.6 us
    ppermute x6, waiting for transfers between devices, per_device(): lax.ppermute(block, 'patch', right_pairs)  8.91 us
    pallas_call x1, Pallas kernels, project(): pl.pallas_call(functools.partial(project_body, order), grid=(model // col...  5.98 us
    all_to_all x1, starting transfers between devices, exchange(): lax.all_to_all(x, ('patch', 'head'), split_axis=0, concat_axis=0, axis_in...  4.09 us
  transfers between devices with their start and end apart: 15, of which 4 were waited for; matrix products, arithmetic and copies ran while one was open for 0% of the time, Pallas kernels for 20%

profile of v2, /device:TPU:17, one launch (start us, length us, event | category | flops | bytes accessed | tf_op | source)
XLA Modules:
  0.0 112.9 jit_solution(10512585088342124049)
XLA Ops:
  0.7 1.3 %constant_dynamic-slice_fusion = (bf16[2,256,384]{2,1,0:T(8,128)(2,1)S(1)}, bf16[2,256,384]{2,1,0:T(8,128)(2,1)S(1)}) fusion(bf16[2,256,768]{2,1,0:T(8,128)(2,1)} %param.8, s32[]{:T(128)S(6)} %select_n.32, s32[]{:T(128)S(6)} %select_n.31), kind=kLoop, calls=%fused_computation.4 | loop fusion | bytes 1572872 | tf_op jit(solution)/shard_map/dynamic_slice | solution.py:410
  2.0 0.7 collective-permute-start
  2.7 1.3 %collective-permute-done.refs_6_.refs_4_ = bf16[2,256,384]{2,1,0:T(8,128)(2,1)S(1)} collective-permute-done((bf16[2,256,384]{2,1,0:T(8,128)(2,1)S(1)}, bf16[2,256,384]{2,1,0:T(8,128)(2,1)S(1)}, u32[]{:S(2)}, u32[]{:S(2)}) %collective-permute-start) | collective-permute-done | bytes 393248 | tf_op jit(solution)/shard_map/ppermute | solution.py:413
  4.1 1.7 %copy-done = bf16[128,9216]{1,0:T(8,128)(2,1)S(1)} copy-done((bf16[128,9216]{1,0:T(8,128)(2,1)S(1)}, bf16[128,9216]{1,0:T(8,128)(2,1)}, u32[]{:S(2)}) %copy-start) | copy-done | bytes 2359320
  5.7 1.0 pack_heads.1
  6.8 1.4 %copy-done.3 = bf16[8,128,1152]{2,1,0:T(8,128)(2,1)} copy-done((bf16[8,128,1152]{2,1,0:T(8,128)(2,1)}, bf16[8,128,1152]{2,1,0:T(8,128)(2,1)S(1)}, u32[]{:S(2)}) %copy-start.3) | copy-done | bytes 2359320
  8.2 4.1 %all-to-all-start = ((bf16[8,128,1152]{2,1,0:T(8,128)(2,1)}), bf16[8,128,1152]{2,1,0:T(8,128)(2,1)S(1)}, u32[]{:S(2)}, u32[]{:S(2)}) async-start(bf16[8,128,1152]{2,1,0:T(8,128)(2,1)} %copy-done.3), calls=%async_computation | async-start | bytes 4718592 | tf_op jit(solution)/shard_map/all_to_all | solution.py:405
  12.3 2.1 %collective-permute-start.3 = (bf16[2,256,384]{2,1,0:T(8,128)(2,1)S(1)}, bf16[2,256,384]{2,1,0:T(8,128)(2,1)S(1)}, u32[]{:S(2)}, u32[]{:S(2)}) collective-permute-start(bf16[2,256,384]{2,1,0:T(8,128)(2,1)S(1)} %get-tuple-element.8.refs_3_), channel_id=1, source_target_pairs={{8,0},{12,4},{16,8},{20,12},{24,16},{28,20},{9,1},{13,5},{17,9},{2... | collective-permute-start | bytes 1179656 | tf_op jit(solution)/shard_map/ppermute | solution.py:426
  14.3 3.2 %collective-permute-start.1 = (bf16[2,256,384]{2,1,0:T(8,128)(2,1)S(1)}, bf16[2,256,384]{2,1,0:T(8,128)(2,1)S(1)}, u32[]{:S(2)}, u32[]{:S(2)}) collective-permute-start(bf16[2,256,384]{2,1,0:T(8,128)(2,1)S(1)} %get-tuple-element.8.refs_3_), channel_id=1, source_target_pairs={{0,8},{4,12},{8,16},{12,20},{16,24},{20,28},{1,9},{5,13},{9,17},{1... | collective-permute-start | bytes 1179656 | tf_op jit(solution)/shard_map/ppermute | solution.py:425
  17.6 1.9 %collective-permute-start.2 = (bf16[2,256,384]{2,1,0:T(8,128)(2,1)S(1)}, bf16[2,256,384]{2,1,0:T(8,128)(2,1)S(1)}, u32[]{:S(2)}, u32[]{:S(2)}) collective-permute-start(bf16[2,256,384]{2,1,0:T(8,128)(2,1)S(1)} %collective-permute-done.refs_6_.refs_4_), channel_id=1, source_target_pairs={{0,8},{4,12},{8,16},{12,20},{16,24},{20,28},{1,9},{5,13},{9,17},{1... | collective-permute-start | bytes 1179656 | tf_op jit(solution)/shard_map/ppermute | solution.py:425
  19.5 3.4 %collective-permute-start.4 = (bf16[2,256,384]{2,1,0:T(8,128)(2,1)S(1)}, bf16[2,256,384]{2,1,0:T(8,128)(2,1)S(1)}, u32[]{:S(2)}, u32[]{:S(2)}) collective-permute-start(bf16[2,256,384]{2,1,0:T(8,128)(2,1)S(1)} %collective-permute-done.refs_6_.refs_4_), channel_id=1, source_target_pairs={{8,0},{12,4},{16,8},{20,12},{24,16},{28,20},{9,1},{13,5},{17,9},{2... | collective-permute-start | bytes 1179656 | tf_op jit(solution)/shard_map/ppermute | solution.py:426
  22.9 2.0 %collective-permute-done.3.refs_7_ = bf16[2,256,384]{2,1,0:T(8,128)(2,1)S(1)} collective-permute-done((bf16[2,256,384]{2,1,0:T(8,128)(2,1)S(1)}, bf16[2,256,384]{2,1,0:T(8,128)(2,1)S(1)}, u32[]{:S(2)}, u32[]{:S(2)}) %collective-permute-start.3) | collective-permute-done | bytes 393248 | tf_op jit(solution)/shard_map/ppermute | solution.py:426
  24.9 2.8 %collective-permute-start.7 = (bf16[2,256,384]{2,1,0:T(8,128)(2,1)S(1)}, bf16[2,256,384]{2,1,0:T(8,128)(2,1)}, u32[]{:S(2)}, u32[]{:S(2)}) collective-permute-start(bf16[2,256,384]{2,1,0:T(8,128)(2,1)S(1)} %collective-permute-done.3.refs_7_), channel_id=1, source_target_pairs={{8,0},{12,4},{16,8},{20,12},{9,1},{13,5},{17,9},{21,13},{10,2},{14... | collective-permute-start | bytes 1179656 | tf_op jit(solution)/shard_map/ppermute | solution.py:426
  27.7 2.1 %collective-permute-start.5 = (bf16[2,256,384]{2,1,0:T(8,128)(2,1)S(1)}, bf16[2,256,384]{2,1,0:T(8,128)(2,1)}, u32[]{:S(2)}, u32[]{:S(2)}) collective-permute-start(bf16[2,256,384]{2,1,0:T(8,128)(2,1)S(1)} %collective-permute-done.1.refs_5_), channel_id=1, source_target_pairs={{8,16},{12,20},{16,24},{20,28},{9,17},{13,21},{17,25},{21,29},{10,... | collective-permute-start | bytes 1179656 | tf_op jit(solution)/shard_map/ppermute | solution.py:425
  30.6 4.5 %collective-permute-done.2.refs_6_ = bf16[2,256,384]{2,1,0:T(8,128)(2,1)S(1)} collective-permute-done((bf16[2,256,384]{2,1,0:T(8,128)(2,1)S(1)}, bf16[2,256,384]{2,1,0:T(8,128)(2,1)S(1)}, u32[]{:S(2)}, u32[]{:S(2)}) %collective-permute-start.2) | collective-permute-done | bytes 393248 | tf_op jit(solution)/shard_map/ppermute | solution.py:425
  35.1 3.2 %collective-permute-start.6 = (bf16[2,256,384]{2,1,0:T(8,128)(2,1)S(1)}, bf16[2,256,384]{2,1,0:T(8,128)(2,1)}, u32[]{:S(2)}, u32[]{:S(2)}) collective-permute-start(bf16[2,256,384]{2,1,0:T(8,128)(2,1)S(1)} %collective-permute-done.2.refs_6_), channel_id=1, source_target_pairs={{8,16},{12,20},{16,24},{20,28},{9,17},{13,21},{17,25},{21,29},{10,... | collective-permute-start | bytes 1179656 | tf_op jit(solution)/shard_map/ppermute | solution.py:425
  39.1 3.5 %collective-permute-start.8 = (bf16[2,256,384]{2,1,0:T(8,128)(2,1)S(1)}, bf16[2,256,384]{2,1,0:T(8,128)(2,1)}, u32[]{:S(2)}, u32[]{:S(2)}) collective-permute-start(bf16[2,256,384]{2,1,0:T(8,128)(2,1)S(1)} %collective-permute-done.4.refs_8_), channel_id=1, source_target_pairs={{8,0},{12,4},{16,8},{20,12},{9,1},{13,5},{17,9},{21,13},{10,2},{14... | collective-permute-start | bytes 1179656 | tf_op jit(solution)/shard_map/ppermute | solution.py:426
  42.6 0.7 copy-done.8
  43.3 1.4 %collective-permute-start.11 = (bf16[2,256,384]{2,1,0:T(8,128)(2,1)}, bf16[2,256,384]{2,1,0:T(8,128)(2,1)}, u32[]{:S(2)}, u32[]{:S(2)}) collective-permute-start(bf16[2,256,384]{2,1,0:T(8,128)(2,1)} %collective-permute-done.7.refs_11_), channel_id=1, source_target_pairs={{8,0},{12,4},{9,1},{13,5},{10,2},{14,6},{11,3},{15,7}} | collective-permute-start | bytes 1179656 | tf_op jit(solution)/shard_map/ppermute | solution.py:426
  44.7 2.9 %collective-permute-start.9 = (bf16[2,256,384]{2,1,0:T(8,128)(2,1)}, bf16[2,256,384]{2,1,0:T(8,128)(2,1)}, u32[]{:S(2)}, u32[]{:S(2)}) collective-permute-start(bf16[2,256,384]{2,1,0:T(8,128)(2,1)} %collective-permute-done.5.refs_9_), channel_id=1, source_target_pairs={{16,24},{20,28},{17,25},{21,29},{18,26},{22,30},{19,27},{23,31}} | collective-permute-start | bytes 1179656 | tf_op jit(solution)/shard_map/ppermute | solution.py:425
  47.6 4.4 %collective-permute-done.6.refs_10_ = bf16[2,256,384]{2,1,0:T(8,128)(2,1)} collective-permute-done((bf16[2,256,384]{2,1,0:T(8,128)(2,1)S(1)}, bf16[2,256,384]{2,1,0:T(8,128)(2,1)}, u32[]{:S(2)}, u32[]{:S(2)}) %collective-permute-start.6) | collective-permute-done | bytes 393248 | tf_op jit(solution)/shard_map/ppermute | solution.py:425
  52.0 4.0 %collective-permute-start.10 = (bf16[2,256,384]{2,1,0:T(8,128)(2,1)}, bf16[2,256,384]{2,1,0:T(8,128)(2,1)}, u32[]{:S(2)}, u32[]{:S(2)}) collective-permute-start(bf16[2,256,384]{2,1,0:T(8,128)(2,1)} %collective-permute-done.6.refs_10_), channel_id=1, source_target_pairs={{16,24},{20,28},{17,25},{21,29},{18,26},{22,30},{19,27},{23,31}} | collective-permute-start | bytes 1179656 | tf_op jit(solution)/shard_map/ppermute | solution.py:425
  56.0 1.4 %collective-permute-start.12 = (bf16[2,256,384]{2,1,0:T(8,128)(2,1)}, bf16[2,256,384]{2,1,0:T(8,128)(2,1)}, u32[]{:S(2)}, u32[]{:S(2)}) collective-permute-start(bf16[2,256,384]{2,1,0:T(8,128)(2,1)} %collective-permute-done.8.refs_12_), channel_id=1, source_target_pairs={{8,0},{12,4},{9,1},{13,5},{10,2},{14,6},{11,3},{15,7}} | collective-permute-start | bytes 1179656 | tf_op jit(solution)/shard_map/ppermute | solution.py:426
  57.6 1.0 copy-done.5
  58.6 1.0 copy-done.7
  59.6 1.0 copy-done.9
  60.6 16.4 %attend_most.1 = (bf16[3,1024,128]{2,1,0:T(8,128)(2,1)S(1)}, f32[3,1024,256]{2,1,0:T(8,128)S(1)}) custom-call(s32[5]{0:T(128)S(1)} %stack.60.info, bf16[8,128,1152]{2,1,0:T(8,128)(2,1)S(1)} %all-to-all-done.refs_0_.refs_1_.refs_2_, bf16[8,128,1152]{2,1,0:T(8,128)(2,1)S(1)} %all-to-all-done.refs_0_.refs_1_.refs_2_, ...), custom_call_target="tpu_custom_call" | custom-call | flops 2818572288 | bytes 4325376 | tf_op jit(solution)/shard_map/attend_most/pallas_call | solution.py:231
  77.1 3.9 %attend_last.1 = bf16[8,128,384]{2,1,0:T(8,128)(2,1)S(1)} custom-call(s32[3]{0:T(128)S(1)} %pad_add_fusion.info, bf16[8,128,1152]{2,1,0:T(8,128)(2,1)S(1)} %all-to-all-done.refs_0_.refs_1_.refs_2_, bf16[3,1024,128]{2,1,0:T(8,128)(2,1)S(1)} %get-tuple-element.4.refs_1_, f32[3,1024,256]{2,1,0:T(8,128)S(1)} %get-tuple-element.5.refs_2_, ...), custom_call_target="tpu_custom_call" | custom-call | flops 805306368 | bytes 2359296 | tf_op jit(solution)/shard_map/attend_last/pallas_call | solution.py:311
  81.0 18.1 %all_to_all.10.x_ref = bf16[8,128,384]{2,1,0:T(8,128)(2,1)S(1)} all-to-all(bf16[8,128,384]{2,1,0:T(8,128)(2,1)S(1)} %attend_last.1), channel_id=1, replica_groups={{0,1,2,3,4,5,6,7},{8,9,10,11,12,13,14,15},{16,17,18,19,20,21,22,23},{24..., dimensions={0} | all-to-all | bytes 1572864 | tf_op jit(solution)/shard_map/all_to_all | solution.py:405
  99.5 6.4 %copy-done.1 = bf16[3072,3072]{1,0:T(8,128)(2,1)S(1)} copy-done((bf16[3072,3072]{1,0:T(8,128)(2,1)S(1)}, bf16[3072,3072]{1,0:T(8,128)(2,1)}, u32[]{:S(2)}) %copy-start.1) | copy-done | bytes 18874392
  105.9 6.0 %project.1 = bf16[64,3072]{1,0:T(8,128)(2,1)} custom-call(bf16[8,128,384]{2,1,0:T(8,128)(2,1)S(1)} %all_to_all.10.x_ref, bf16[3072,3072]{1,0:T(8,128)(2,1)S(1)} %copy-done.1, bf16[64,3072]{1,0:T(8,128)(2,1)S(1)} %copy-done.10, f32[1,3072]{1,0:T(1,128)S(1)} %bitcast.8), custom_call_target="tpu_custom_call" | custom-call | flops 1207959552 | bytes 18874368 | tf_op jit(solution)/shard_map/project/pallas_call | solution.py:347
  111.9 0.9 pad_maximum_fusion
  (33 shorter events, 2.2 us)
Async XLA Ops:
  0.6 3.4 %copy-start.2 = (bf16[64,9216]{1,0:T(8,128)(2,1)S(1)}, bf16[64,9216]{1,0:T(8,128)(2,1)}, u32[]{:S(2)}) copy-start(bf16[64,9216]{1,0:T(8,128)(2,1)} %refs_2_.1) | copy-start | bytes 3538948
  2.0 2.1 %collective-permute-start = (bf16[2,256,384]{2,1,0:T(8,128)(2,1)S(1)}, bf16[2,256,384]{2,1,0:T(8,128)(2,1)S(1)}, u32[]{:S(2)}, u32[]{:S(2)}) collective-permute-start(bf16[2,256,384]{2,1,0:T(8,128)(2,1)S(1)} %get-tuple-element.9), channel_id=1, source_target_pairs={{0,4},{4,0},{8,12},{12,8},{16,20},{20,16},{24,28},{28,24},{1,5},{5... | collective-permute-start | bytes 1179656 | tf_op jit(solution)/shard_map/ppermute | solution.py:413
  4.0 1.7 %copy-start = (bf16[128,9216]{1,0:T(8,128)(2,1)S(1)}, bf16[128,9216]{1,0:T(8,128)(2,1)}, u32[]{:S(2)}) copy-start(bf16[128,9216]{1,0:T(8,128)(2,1)} %refs_5_.1) | copy-start | bytes 7077892
  6.7 1.4 %copy-start.3 = (bf16[8,128,1152]{2,1,0:T(8,128)(2,1)}, bf16[8,128,1152]{2,1,0:T(8,128)(2,1)S(1)}, u32[]{:S(2)}) copy-start(bf16[8,128,1152]{2,1,0:T(8,128)(2,1)S(1)} %pack_heads.1) | copy-start | bytes 7077892
  8.2 49.5 %all-to-all-start = ((bf16[8,128,1152]{2,1,0:T(8,128)(2,1)}), bf16[8,128,1152]{2,1,0:T(8,128)(2,1)S(1)}, u32[]{:S(2)}, u32[]{:S(2)}) async-start(bf16[8,128,1152]{2,1,0:T(8,128)(2,1)} %copy-done.3), calls=%async_computation | async-start | bytes 4718592 | tf_op jit(solution)/shard_map/all_to_all | solution.py:405
  12.3 12.6 %collective-permute-start.3 = (bf16[2,256,384]{2,1,0:T(8,128)(2,1)S(1)}, bf16[2,256,384]{2,1,0:T(8,128)(2,1)S(1)}, u32[]{:S(2)}, u32[]{:S(2)}) collective-permute-start(bf16[2,256,384]{2,1,0:T(8,128)(2,1)S(1)} %get-tuple-element.8.refs_3_), channel_id=1, source_target_pairs={{8,0},{12,4},{16,8},{20,12},{24,16},{28,20},{9,1},{13,5},{17,9},{2... | collective-permute-start | bytes 1179656 | tf_op jit(solution)/shard_map/ppermute | solution.py:426
  14.3 13.4 %collective-permute-start.1 = (bf16[2,256,384]{2,1,0:T(8,128)(2,1)S(1)}, bf16[2,256,384]{2,1,0:T(8,128)(2,1)S(1)}, u32[]{:S(2)}, u32[]{:S(2)}) collective-permute-start(bf16[2,256,384]{2,1,0:T(8,128)(2,1)S(1)} %get-tuple-element.8.refs_3_), channel_id=1, source_target_pairs={{0,8},{4,12},{8,16},{12,20},{16,24},{20,28},{1,9},{5,13},{9,17},{1... | collective-permute-start | bytes 1179656 | tf_op jit(solution)/shard_map/ppermute | solution.py:425
  17.6 17.5 %collective-permute-start.2 = (bf16[2,256,384]{2,1,0:T(8,128)(2,1)S(1)}, bf16[2,256,384]{2,1,0:T(8,128)(2,1)S(1)}, u32[]{:S(2)}, u32[]{:S(2)}) collective-permute-start(bf16[2,256,384]{2,1,0:T(8,128)(2,1)S(1)} %collective-permute-done.refs_6_.refs_4_), channel_id=1, source_target_pairs={{0,8},{4,12},{8,16},{12,20},{16,24},{20,28},{1,9},{5,13},{9,17},{1... | collective-permute-start | bytes 1179656 | tf_op jit(solution)/shard_map/ppermute | solution.py:425
  19.5 19.6 %collective-permute-start.4 = (bf16[2,256,384]{2,1,0:T(8,128)(2,1)S(1)}, bf16[2,256,384]{2,1,0:T(8,128)(2,1)S(1)}, u32[]{:S(2)}, u32[]{:S(2)}) collective-permute-start(bf16[2,256,384]{2,1,0:T(8,128)(2,1)S(1)} %collective-permute-done.refs_6_.refs_4_), channel_id=1, source_target_pairs={{8,0},{12,4},{16,8},{20,12},{24,16},{28,20},{9,1},{13,5},{17,9},{2... | collective-permute-start | bytes 1179656 | tf_op jit(solution)/shard_map/ppermute | solution.py:426
  24.9 18.4 %collective-permute-start.7 = (bf16[2,256,384]{2,1,0:T(8,128)(2,1)S(1)}, bf16[2,256,384]{2,1,0:T(8,128)(2,1)}, u32[]{:S(2)}, u32[]{:S(2)}) collective-permute-start(bf16[2,256,384]{2,1,0:T(8,128)(2,1)S(1)} %collective-permute-done.3.refs_7_), channel_id=1, source_target_pairs={{8,0},{12,4},{16,8},{20,12},{9,1},{13,5},{17,9},{21,13},{10,2},{14... | collective-permute-start | bytes 1179656 | tf_op jit(solution)/shard_map/ppermute | solution.py:426
  27.7 17.0 %collective-permute-start.5 = (bf16[2,256,384]{2,1,0:T(8,128)(2,1)S(1)}, bf16[2,256,384]{2,1,0:T(8,128)(2,1)}, u32[]{:S(2)}, u32[]{:S(2)}) collective-permute-start(bf16[2,256,384]{2,1,0:T(8,128)(2,1)S(1)} %collective-permute-done.1.refs_5_), channel_id=1, source_target_pairs={{8,16},{12,20},{16,24},{20,28},{9,17},{13,21},{17,25},{21,29},{10,... | collective-permute-start | bytes 1179656 | tf_op jit(solution)/shard_map/ppermute | solution.py:425
  29.9 0.7 copy-start.4
  35.1 17.0 %collective-permute-start.6 = (bf16[2,256,384]{2,1,0:T(8,128)(2,1)S(1)}, bf16[2,256,384]{2,1,0:T(8,128)(2,1)}, u32[]{:S(2)}, u32[]{:S(2)}) collective-permute-start(bf16[2,256,384]{2,1,0:T(8,128)(2,1)S(1)} %collective-permute-done.2.refs_6_), channel_id=1, source_target_pairs={{8,16},{12,20},{16,24},{20,28},{9,17},{13,21},{17,25},{21,29},{10,... | collective-permute-start | bytes 1179656 | tf_op jit(solution)/shard_map/ppermute | solution.py:425
  38.3 0.7 copy-start.6
  39.1 17.0 %collective-permute-start.8 = (bf16[2,256,384]{2,1,0:T(8,128)(2,1)S(1)}, bf16[2,256,384]{2,1,0:T(8,128)(2,1)}, u32[]{:S(2)}, u32[]{:S(2)}) collective-permute-start(bf16[2,256,384]{2,1,0:T(8,128)(2,1)S(1)} %collective-permute-done.4.refs_8_), channel_id=1, source_target_pairs={{8,0},{12,4},{16,8},{20,12},{9,1},{13,5},{17,9},{21,13},{10,2},{14... | collective-permute-start | bytes 1179656 | tf_op jit(solution)/shard_map/ppermute | solution.py:426
  42.6 0.7 copy-start.8
  43.3 33.7 %collective-permute-start.11 = (bf16[2,256,384]{2,1,0:T(8,128)(2,1)}, bf16[2,256,384]{2,1,0:T(8,128)(2,1)}, u32[]{:S(2)}, u32[]{:S(2)}) collective-permute-start(bf16[2,256,384]{2,1,0:T(8,128)(2,1)} %collective-permute-done.7.refs_11_), channel_id=1, source_target_pairs={{8,0},{12,4},{9,1},{13,5},{10,2},{14,6},{11,3},{15,7}} | collective-permute-start | bytes 1179656 | tf_op jit(solution)/shard_map/ppermute | solution.py:426
  44.7 32.3 %collective-permute-start.9 = (bf16[2,256,384]{2,1,0:T(8,128)(2,1)}, bf16[2,256,384]{2,1,0:T(8,128)(2,1)}, u32[]{:S(2)}, u32[]{:S(2)}) collective-permute-start(bf16[2,256,384]{2,1,0:T(8,128)(2,1)} %collective-permute-done.5.refs_9_), channel_id=1, source_target_pairs={{16,24},{20,28},{17,25},{21,29},{18,26},{22,30},{19,27},{23,31}} | collective-permute-start | bytes 1179656 | tf_op jit(solution)/shard_map/ppermute | solution.py:425
  52.0 25.0 %collective-permute-start.10 = (bf16[2,256,384]{2,1,0:T(8,128)(2,1)}, bf16[2,256,384]{2,1,0:T(8,128)(2,1)}, u32[]{:S(2)}, u32[]{:S(2)}) collective-permute-start(bf16[2,256,384]{2,1,0:T(8,128)(2,1)} %collective-permute-done.6.refs_10_), channel_id=1, source_target_pairs={{16,24},{20,28},{17,25},{21,29},{18,26},{22,30},{19,27},{23,31}} | collective-permute-start | bytes 1179656 | tf_op jit(solution)/shard_map/ppermute | solution.py:425
  56.0 21.0 %collective-permute-start.12 = (bf16[2,256,384]{2,1,0:T(8,128)(2,1)}, bf16[2,256,384]{2,1,0:T(8,128)(2,1)}, u32[]{:S(2)}, u32[]{:S(2)}) collective-permute-start(bf16[2,256,384]{2,1,0:T(8,128)(2,1)} %collective-permute-done.8.refs_12_), channel_id=1, source_target_pairs={{8,0},{12,4},{9,1},{13,5},{10,2},{14,6},{11,3},{15,7}} | collective-permute-start | bytes 1179656 | tf_op jit(solution)/shard_map/ppermute | solution.py:426
  57.6 1.0 copy-start.5
  58.6 1.0 copy-start.7
  59.6 1.0 copy-start.9
  80.9 18.6 %copy-start.10 = (bf16[64,3072]{1,0:T(8,128)(2,1)S(1)}, bf16[64,3072]{1,0:T(8,128)(2,1)}, u32[]{:S(2)}) copy-start(bf16[64,3072]{1,0:T(8,128)(2,1)} %residual.1) | copy-start | bytes 1179652
  81.0 18.6 %copy-start.11 = (f32[3072]{0:T(1024)S(1)}, f32[3072]{0:T(1024)}, u32[]{:S(2)}) copy-start(f32[3072]{0:T(1024)} %param.10) | copy-start | bytes 36868
  99.1 12.8 %collective-permute-start.13 = (bf16[64,3072]{1,0:T(8,128)(2,1)S(1)}, bf16[64,3072]{1,0:T(8,128)(2,1)S(1)}, u32[]{:S(2)}, u32[]{:S(2)}) collective-permute-start(bf16[64,3072]{1,0:T(8,128)(2,1)S(1)} %unpack_text.1), channel_id=1, source_target_pairs={{0,4},{4,0},{8,12},{12,8},{16,20},{20,16},{24,28},{28,24},{1,5},{5... | collective-permute-start | bytes 1179656 | tf_op jit(solution)/shard_map/ppermute | solution.py:438
  99.5 6.4 %copy-start.1 = (bf16[3072,3072]{1,0:T(8,128)(2,1)S(1)}, bf16[3072,3072]{1,0:T(8,128)(2,1)}, u32[]{:S(2)}) copy-start(bf16[3072,3072]{1,0:T(8,128)(2,1)} %weight.1) | copy-start | bytes 56623108

commit v3 on v2

v3 whole, which is shorter than its diff:
```python
import functools
import math

import jax
import jax.numpy as jnp
from jax import lax
from jax.experimental import pallas as pl
from jax.experimental.pallas import tpu as pltpu
from jax.sharding import PartitionSpec as P

HD = 128
SCALE = math.log2(math.e) / math.sqrt(HD)
VMEM_LIMIT = 24 * 1024 * 1024
TILE = 256
LARGE = 2.0**60


def params():
    return pltpu.CompilerParams(
        vmem_limit_bytes=VMEM_LIMIT, dimension_semantics=("arbitrary",)
    )


def pack_body(info, *refs):
    sources, packed = refs[:6], refs[-1]
    first = 0
    for group in (sources[:3], sources[3:]):
        rows, width = group[0].shape
        for part, source in enumerate(group):
            packed[0, first : first + rows, part * width : (part + 1) * width] = source[...]
        first += rows


def pack(core, img_qkv, txt_qkv, text_rows, destinations, column_block, width, after):
    img_rows = img_qkv.shape[0]
    blocks = img_qkv.shape[1] // 3 // width

    def source(rows, part, by_core):
        def place(d, info):
            return (info[0] if by_core else 0, part * blocks + column_block(d))

        return pl.BlockSpec((rows, width), place)

    return pl.pallas_call(
        pack_body,
        grid_spec=pltpu.PrefetchScalarGridSpec(
            num_scalar_prefetch=1,
            grid=(destinations,),
            in_specs=[source(img_rows, part, False) for part in range(3)]
            + [source(text_rows, part, True) for part in range(3)]
            + [pl.BlockSpec(memory_space=pl.ANY)] * len(after),
            out_specs=pl.BlockSpec(
                (1, img_rows + text_rows, 3 * width), lambda d, info: (d, 0, 0)
            ),
        ),
        out_shape=jax.ShapeDtypeStruct(
            (destinations, img_rows + text_rows, 3 * width), img_qkv.dtype
        ),
        compiler_params=params(),
        name="pack_heads",
    )(core, img_qkv, img_qkv, img_qkv, txt_qkv, txt_qkv, txt_qkv, *after)


def dot(first, second, contract):
    return lax.dot_general(
        first, second, ((contract[:1], contract[1:]), ((), ())), preferred_element_type=jnp.float32
    )


def with_ones(block):
    return jnp.concatenate([block, jnp.ones_like(block)], axis=1)


def reference_columns(row_max):
    reference = row_max.astype(jnp.bfloat16).astype(jnp.float32)
    return jnp.broadcast_to(reference * (-1.0 / HD), (row_max.shape[0], HD)).astype(jnp.bfloat16)


def weighted(queries, key_rows, values):
    weights = jnp.exp2(dot(queries, key_rows, (1, 1)) * SCALE).astype(jnp.bfloat16)
    return dot(weights, values, (1, 0))


def tiles_of(rows):
    tile = min(TILE, rows)
    return [slice(first, min(first + tile, rows)) for first in range(0, rows, tile)]


def split_rows(block, img_rows):
    return (
        block[:, :img_rows, :].reshape(-1, HD),
        block[:, img_rows:, :].reshape(-1, HD),
    )


def until_small(flag, total, attempt):
    flag[0] = 1

    @pl.loop(0, 2)
    def _(turn):
        @pl.when(flag[0] == 1)
        def _():
            attempt(turn)
            flag[0] = jnp.where(jnp.max(total[:, HD:]) > LARGE, 1, 0).astype(jnp.int32)


def head_body(pair, img_rows, others, has_earlier, info, *refs):
    q_ref, k_ref, v_ref = refs[:3]
    stale = refs[3 : 3 + pair]
    arrived = refs[3 + pair : 3 + pair + others]
    out, aug, total, flag = refs[3 + pair + others + has_earlier :]
    core = info[0]
    k_img, k_txt = split_rows(k_ref[...], img_rows)
    v_img, v_txt = split_rows(v_ref[...], img_rows)
    q_img, q_txt = split_rows(q_ref[...], img_rows)
    fresh_rows = q_img.shape[0]
    group_rows = fresh_rows // pair
    rows = fresh_rows + q_txt.shape[0]

    def queries_at(span):
        if span.stop <= fresh_rows:
            return q_img[span, :]
        return q_txt[span.start - fresh_rows : span.stop - fresh_rows, :]

    def key_sets():
        shared = [(k_txt, v_txt)] + [(block[0, 0], block[0, 1]) for block in arrived]
        for group in range(pair):
            span = slice(group * group_rows, (group + 1) * group_rows)
            own = [(k_img[span, :], v_img[span, :])]
            if pair == 2:
                mine = core == group
                own.append(
                    (
                        jnp.where(mine, stale[1][0], stale[0][0]),
                        jnp.where(mine, stale[1][1], stale[0][1]),
                    )
                )
            yield span, own, shared
        yield slice(fresh_rows, rows), [(block[0], block[1]) for block in stale], shared

    def pieces_of(own, shared):
        joined = (
            jnp.concatenate([key_rows for key_rows, _ in own], 0),
            jnp.concatenate([values for _, values in own], 0),
        )
        return shared[:1] + [joined] + shared[1:]

    def spans_of(span):
        return [
            slice(span.start + tile.start, span.start + tile.stop)
            for tile in tiles_of(span.stop - span.start)
        ]

    def largest(span, key_rows):
        return jnp.max(dot(queries_at(span), key_rows, (1, 1)), axis=1, keepdims=True)

    def attempt(turn):
        @pl.when(turn == 0)
        def _():
            for span, _, shared in key_sets():
                for tile in spans_of(span):
                    key_rows = shared[0][0]
                    aug[tile, :] = reference_columns(
                        largest(tile, key_rows[: min(256, key_rows.shape[0]), :])
                    )

        @pl.when(turn == 1)
        def _():
            for span, own, shared in key_sets():
                for tile in spans_of(span):
                    row_max = None
                    for key_rows, _ in pieces_of(own, shared):
                        piece_max = largest(tile, key_rows)
                        row_max = piece_max if row_max is None else jnp.maximum(row_max, piece_max)
                    aug[tile, :] = reference_columns(row_max)

        for span, own, shared in key_sets():
            pieces = [(with_ones(k), with_ones(v)) for k, v in pieces_of(own, shared)]
            for tile in spans_of(span):
                queries = jnp.concatenate([queries_at(tile), aug[tile, :]], axis=1)
                summed = None
                for key_rows, values in pieces:
                    piece = weighted(queries, key_rows, values)
                    summed = piece if summed is None else summed + piece
                total[tile, :] = summed

    until_small(flag, total, attempt)
    attended = (total[:, :HD] / total[:, HD:]).astype(out.dtype)
    destinations = out.shape[0]
    out[:, :img_rows, :] = attended[:fresh_rows].reshape(destinations, img_rows, HD)
    out[:, img_rows:, :] = attended[fresh_rows:].reshape(destinations, -1, HD)


def attend_cost(queries, keys, heads):
    return pl.CostEstimate(
        flops=4 * queries * keys * heads * HD,
        bytes_accessed=4 * queries * heads * HD + 4 * keys * heads * HD,
        transcendentals=queries * keys * heads,
    )


def attend_head(info, qkv, img_rows, stale, gathered, head, place, places, earlier=None):
    heads = qkv.shape[2] // (3 * HD)
    others = gathered.shape[0] - 1
    rows = qkv.shape[0] * qkv.shape[1]

    def columns(array, block):
        return pl.BlockSpec(array.shape[:2] + (HD,), lambda n, info: (0, 0, block))

    def other(index):
        return pl.BlockSpec(
            (1,) + gathered.shape[1:], lambda n, info: (info[1 + index], 0, 0, 0)
        )

    operands = [qkv] * 3 + list(stale) + [gathered] * others
    in_specs = [columns(qkv, part * heads + head) for part in range(3)]
    in_specs += [columns(block, head) for block in stale]
    in_specs += [other(index) for index in range(others)]
    aliases = {}
    if earlier is not None:
        aliases = {1 + len(operands): 0}
        operands.append(earlier)
        in_specs.append(pl.BlockSpec(memory_space=pl.ANY))
    keys = others * gathered.shape[2] + 2 * rows // 2
    return pl.pallas_call(
        functools.partial(head_body, len(stale), img_rows, others, int(earlier is not None)),
        grid_spec=pltpu.PrefetchScalarGridSpec(
            num_scalar_prefetch=1,
            grid=(1,),
            in_specs=in_specs,
            out_specs=pl.BlockSpec(qkv.shape[:2] + (HD,), lambda n, info: (0, 0, place)),
            scratch_shapes=[
                pltpu.VMEM((rows, HD), jnp.bfloat16),
                pltpu.VMEM((rows, 2 * HD), jnp.float32),
                pltpu.SMEM((1,), jnp.int32),
            ],
        ),
        out_shape=jax.ShapeDtypeStruct(qkv.shape[:2] + (places * HD,), qkv.dtype),
        input_output_aliases=aliases,
        compiler_params=params(),
        cost_estimate=attend_cost(rows, keys, 1),
        name="attend_head",
    )(info, *operands)


def project_body(order, last, x_ref, weight, *refs):
    if last:
        residual, gate, earlier, out, flat = refs
    else:
        out, flat = refs

    @pl.when(pl.program_id(0) == 0)
    def _():
        rows, width = flat.shape[0], x_ref.shape[2]
        for source, place in enumerate(order):
            flat[:, place * width : (place + 1) * width] = x_ref[source, :rows, :]

    columns = weight.shape[3]
    block = weight[...].reshape(flat.shape[1], columns)
    projected = jnp.dot(flat[...], block, preferred_element_type=jnp.float32)
    if last:
        projected = earlier[...] + projected
        projected = residual[...].astype(jnp.float32) + gate[...] * projected
    out[...] = projected.astype(out.dtype)


def project(x, order, weight, first_head, rows, final=None):
    model = weight.shape[3]
    heads = x.shape[2] // HD
    columns = 512 if model % 512 == 0 else HD
    row_spec = pl.BlockSpec((rows, columns), lambda n: (0, n))
    operands, in_specs = [x, weight], [
        pl.BlockSpec(x.shape, lambda n: (0, 0, 0)),
        pl.BlockSpec(
            (weight.shape[0], heads, HD, columns), lambda n: (0, first_head // heads, 0, n)
        ),
    ]
    if final is not None:
        residual, gate, earlier = final
        operands += [residual, gate.reshape(1, model), earlier]
        in_specs += [row_spec, pl.BlockSpec((1, columns), lambda n: (0, n)), row_spec]
    depth = x.shape[0] * x.shape[2]
    return pl.pallas_call(
        functools.partial(project_body, order, final is not None),
        grid=(model // columns,),
        in_specs=in_specs,
        out_specs=row_spec,
        out_shape=jax.ShapeDtypeStruct(
            (rows, model), jnp.float32 if final is None else residual.dtype
        ),
        scratch_shapes=[pltpu.VMEM((rows, depth), x.dtype)],
        compiler_params=params(),
        cost_estimate=pl.CostEstimate(
            flops=2 * rows * model * depth, bytes_accessed=2 * model * depth, transcendentals=0
        ),
        name="project_last" if final is not None else "project_early",
    )(*operands)


def unpack_body(order, first, heads, *refs):
    sources, out = refs[:-1], refs[-1]
    for source, place in enumerate(order):
        at = place * heads * HD
        for x_ref in sources:
            width = x_ref.shape[2]
            out[:, at : at + width] = x_ref[source, first:, :]
            at += width


def unpack_text(parts, order, first):
    heads = sum(x.shape[2] for x in parts) // HD
    rows, model = parts[0].shape[1] - first, parts[0].shape[0] * heads * HD
    return pl.pallas_call(
        functools.partial(unpack_body, order, first, heads),
        grid=(1,),
        in_specs=[pl.BlockSpec(x.shape, lambda n: (0, 0, 0)) for x in parts],
        out_specs=pl.BlockSpec((rows, model), lambda n: (0, 0)),
        out_shape=jax.ShapeDtypeStruct((rows, model), parts[0].dtype),
        compiler_params=params(),
        name="unpack_text",
    )(*parts)


def per_device(img_qkv, txt_qkv, stale_kv, residual, gate_scale, proj_weight):
    patches, head_owners = lax.axis_size("patch"), lax.axis_size("head")
    patch = lax.axis_index("patch")
    owned_heads = stale_kv.shape[2] // HD
    pair = 2 if patches % 2 == 0 and owned_heads % 2 == 0 else 1
    planes = patches // pair
    plane, core = patch // pair, patch % pair
    width = stale_kv.shape[2] // pair
    heads = width // HD
    img_rows, model = residual.shape
    text_rows = txt_qkv.shape[0] // pair
    destinations = pair * head_owners

    def column_block(d):
        return (d % head_owners) * pair + d // head_owners

    order = [column_block(d) for d in range(destinations)]
    groups = [[g * destinations + d for d in range(destinations)] for g in range(planes)]
    columns = [[z * pair + c for z in range(planes)] for c in range(pair)]

    def exchange(x):
        return lax.all_to_all(
            x, ("patch", "head"), split_axis=0, concat_axis=0, axis_index_groups=groups, tiled=True
        )

    swap_pairs = [(p, p + 1 - 2 * (p % 2)) for p in range(patches)]
    stale = [lax.dynamic_slice_in_dim(stale_kv, core * width, width, 2)]
    if pair == 2:
        theirs = lax.dynamic_slice_in_dim(stale_kv, (1 - core) * width, width, 2)
        stale.append(lax.ppermute(theirs, "patch", swap_pairs))

    gathered = []
    for head in range(heads):
        columns_of = [block[:, :, head * HD : (head + 1) * HD] for block in stale]
        gathered.append(
            lax.all_gather(
                jnp.concatenate(columns_of, axis=1), "patch", axis=0, axis_index_groups=columns
            )
        )

    core_only = core.astype(jnp.int32).reshape(1)
    qkv = exchange(
        pack(core_only, img_qkv, txt_qkv, text_rows, destinations, column_block, width, stale[1:])
    )

    info = jnp.stack([core] + [(plane + step) % planes for step in range(1, planes)])
    info = info.astype(jnp.int32)
    early = None
    for head in range(heads - 1):
        early = attend_head(
            info, qkv, img_rows, stale, gathered[head], head, head, heads - 1, early
        )
    weight = proj_weight.reshape(destinations, heads, HD, model)
    early = exchange(early)
    late = exchange(attend_head(info, qkv, img_rows, stale, gathered[-1], heads - 1, 0, 1))

    text_out = unpack_text([early, late], order, img_rows)
    if pair == 2:
        other = lax.ppermute(text_out, "patch", swap_pairs)
        lower = core == 0
        text_out = jnp.concatenate(
            [jnp.where(lower, text_out, other), jnp.where(lower, other, text_out)], 0
        )
    partial = project(early, order, weight, 0, img_rows)
    image_out = project(
        late, order, weight, heads - 1, img_rows, (residual, gate_scale, partial)
    )
    return (image_out, text_out)


def solution(mesh):
    return jax.shard_map(
        per_device,
        mesh=mesh,
        in_specs=(
            P(("patch", "head"), None),
            P("head", None),
            P(None, "patch", "head"),
            P(("patch", "head"), None),
            P(),
            P(),
        ),
        out_specs=(P(("patch", "head"), None), P("head", None)),
        check_vma=False,
    )
```

time: 114 us -> 151 us (1.32)
  waiting for transfers between devices: 12.3 us -> 59.4 us
  starting transfers between devices: 37.2 us -> 8.86 us
  between operations: 0.84 us -> 14 us
  local copies, waits for them, and re-layouts: 16.1 us -> 23.6 us
  blocking collectives: 18.1 us -> 13.2 us
  other arithmetic: 1.07 us -> 4.19 us
  Pallas kernels: 27.3 us -> 25.6 us
    all_gather x0 -> x3, waiting for transfers between devices: none -> 50.4 us  [per_device(): lax.all_gather(jnp.concatenate(columns_of, axis=1), 'patch', axis=0, axis...]
    ppermute x12 -> x0, starting transfers between devices: 32 us -> none  [the longest x6 17.4 us: per_device(): lax.ppermute(block, 'patch', right_pairs)]
    ppermute x12 -> x0, waiting for transfers between devices: 10.9 us -> none  [the longest x6 8.91 us: per_device(): lax.ppermute(block, 'patch', right_pairs)]
    all_to_all x1 -> x2, waiting for transfers between devices: 0.01 us -> 8.86 us  [exchange(): lax.all_to_all(x, ('patch', 'head'), split_axis=0, concat_axis=0, axis_in...]
    all_to_all x1, blocking collectives: 18.1 us -> 13.2 us  [exchange(): lax.all_to_all(x, ('patch', 'head'), split_axis=0, concat_axis=0, axis_in...]
    all_to_all x1 -> x2, starting transfers between devices: 4.09 us -> 7.7 us  [exchange(): lax.all_to_all(x, ('patch', 'head'), split_axis=0, concat_axis=0, axis_in...]
    slice x0 -> x2, local copies, waits for them, and re-layouts: none -> 3.53 us  [per_device(): columns_of = [block[:, :, head * HD:(head + 1) * HD] for block in stale]]
    unnamed x24 -> x26, local copies, waits for them, and re-layouts: 14.7 us -> 17.9 us
  transfers between devices with their start and end apart: 15 -> 7, of which waited for: 4 -> 4; matrix products, arithmetic and copies ran while one was open for 0% -> 3% of each run, Pallas kernels for 20% -> 17%
where the time goes in v3:
time: 151 us; the launch traced here: 149 us
  waiting for transfers between devices  59.4 us (39%)
  Pallas kernels  25.6 us (17%)
  local copies, waits for them, and re-layouts  23.6 us (16%)
  between operations  14 us (9%)
  blocking collectives  13.2 us (9%)
  starting transfers between devices  8.86 us (6%)
  other arithmetic  4.19 us (3%)
    all_gather x3, waiting for transfers between devices, per_device(): lax.all_gather(jnp.concatenate(columns_of, axis=1), 'patch', axis=0, axis...  50.4 us
    unnamed x26, local copies, waits for them, and re-layouts  17.9 us
    pallas_call x3, Pallas kernels, attend_head(): pl.pallas_call(functools.partial(head_body, len(stale), img_rows, others,...  17.2 us
    all_to_all x1, blocking collectives, exchange(): lax.all_to_all(x, ('patch', 'head'), split_axis=0, concat_axis=0, axis_in...  13.2 us
    all_to_all x2, waiting for transfers between devices, exchange(): lax.all_to_all(x, ('patch', 'head'), split_axis=0, concat_axis=0, axis_in...  8.86 us
    all_to_all x2, starting transfers between devices, exchange(): lax.all_to_all(x, ('patch', 'head'), split_axis=0, concat_axis=0, axis_in...  7.7 us
    pallas_call x2, Pallas kernels, project(): pl.pallas_call(functools.partial(project_body, order, final is not None),...  7.35 us
    slice x2, local copies, waits for them, and re-layouts, per_device(): columns_of = [block[:, :, head * HD:(head + 1) * HD] for block in stale]  3.53 us
  transfers between devices with their start and end apart: 7, of which 4 were waited for; matrix products, arithmetic and copies ran while one was open for 3% of the time, Pallas kernels for 17%

profile of v3, /device:TPU:17, one launch (start us, length us, event | category | flops | bytes accessed | tf_op | source)
XLA Modules:
  0.0 148.8 jit_solution(5962785221130799411)
XLA Ops:
  7.2 0.0 all-gather.7.cloned.1.call-start
  7.3 2.2 %constant_dynamic-slice_fusion.3 = (bf16[2,256,384]{2,1,0:T(8,128)(2,1)}, bf16[2,256,384]{2,1,0:T(8,128)(2,1)}) fusion(bf16[2,256,768]{2,1,0:T(8,128)(2,1)} %param.8, s32[]{:T(128)S(6)} %select_n.47, s32[]{:T(128)S(6)} %select_n.46), kind=kLoop, calls=%fused_computation.9 | loop fusion | bytes 1572872 | tf_op jit(solution)/shard_map/dynamic_slice | solution.py:350
  9.5 0.7 collective-permute-start
  10.2 1.8 %constant_dynamic-slice_fusion = (bf16[2,256,128]{2,1,0:T(8,128)(2,1)}, bf16[2,256,128]{2,1,0:T(8,128)(2,1)}, bf16[2,256,128]{2,1,0:T(8,128)(2,1)S(1)}) fusion(bf16[2,256,768]{2,1,0:T(8,128)(2,1)} %param.8, s32[]{:T(128)S(6)} %select_n.47, s32[]{:T(128)S(6)} %add.42, s32[]{:T(128)S(6)} %add.41), kind=kLoop, calls=%fused_computation.6 | loop fusion | bytes 786444 | tf_op jit(solution)/shard_map/slice | solution.py:357
  11.9 1.8 %fusion = (bf16[2,256,128]{2,1,0:T(8,128)(2,1)}, bf16[2,256,128]{2,1,0:T(8,128)(2,1)}, bf16[2,256,128]{2,1,0:T(8,128)(2,1)S(1)}) fusion(bf16[2,256,384]{2,1,0:T(8,128)(2,1)} %collective-permute-done.refs_6_.refs_4_), kind=kLoop, calls=%fused_computation.12 | loop fusion | bytes 786432 | tf_op jit(solution)/shard_map/slice | solution.py:357
  13.7 0.7 pad_maximum_fusion.1
  14.4 0.0 all-gather.11.cloned.1.call-start
  14.5 1.7 %pad_maximum_fusion.3 = bf16[2,512,128]{2,1,0:T(8,128)(2,1)} fusion(bf16[2,256,128]{2,1,0:T(8,128)(2,1)} %get-tuple-element.9, bf16[2,256,128]{2,1,0:T(8,128)(2,1)} %get-tuple-element.4), kind=kLoop, calls=%fused_computation.5 | loop fusion | flops 524288 | bytes 524288 | tf_op jit(solution)/shard_map/concatenate | solution.py:360
  16.2 1.1 pack_heads.1
  17.3 1.4 copy-done.6
  18.7 4.2 %all-to-all-start = ((bf16[8,128,1152]{2,1,0:T(8,128)(2,1)}), bf16[8,128,1152]{2,1,0:T(8,128)(2,1)S(1)}, u32[]{:S(2)}, u32[]{:S(2)}) async-start(bf16[8,128,1152]{2,1,0:T(8,128)(2,1)} %copy-done.6), calls=%async_computation | async-start | bytes 4718592 | tf_op jit(solution)/shard_map/all_to_all | solution.py:345
  22.9 0.7 pad_maximum_fusion.2
  23.7 0.1 pad_add_fusion.info
  23.8 19.0 %all-gather.7.cloned.1.call-done = bf16[8,512,128]{2,1,0:T(8,128)(2,1)} async-done(((bf16[2,512,128]{2,1,0:T(8,128)(2,1)}), bf16[8,512,128]{2,1,0:T(8,128)(2,1)}) %all-gather.7.cloned.1.call-update) | async-done | bytes 1048592 | tf_op jit(solution)/shard_map/all_gather | solution.py:359
  42.7 8.9 %all-to-all-done.refs_0_.refs_1_.refs_2_ = bf16[8,128,1152]{2,1,0:T(8,128)(2,1)S(1)} async-done(((bf16[8,128,1152]{2,1,0:T(8,128)(2,1)}), bf16[8,128,1152]{2,1,0:T(8,128)(2,1)S(1)}, u32[]{:S(2)}, u32[]{:S(2)}) %all-to-all-start) | async-done | bytes 2359328 | tf_op jit(solution)/shard_map/all_to_all | solution.py:345
  51.6 1.3 copy-done.7
  52.9 6.2 %attend_head.3 = bf16[8,128,128]{2,1,0:T(8,128)(2,1)} custom-call(s32[4]{0:T(128)S(1)} %pad_add_fusion.info, bf16[8,128,1152]{2,1,0:T(8,128)(2,1)S(1)} %all-to-all-done.refs_0_.refs_1_.refs_2_, bf16[8,128,1152]{2,1,0:T(8,128)(2,1)S(1)} %all-to-all-done.refs_0_.refs_1_.refs_2_, bf16[8,128,1152]{2,1,0:T(8,128)(2,1)S(1)} %all-to-all-done.refs_0_.refs_1_.refs_2_, ...), custom_call_target="tpu_custom_call" | custom-call | flops 1342177280 | bytes 1835008 | tf_op jit(solution)/shard_map/attend_head/pallas_call | solution.py:225
  59.0 3.5 %all-to-all-start.1 = ((bf16[8,128,128]{2,1,0:T(8,128)(2,1)}), bf16[8,128,128]{2,1,0:T(8,128)(2,1)S(1)}, u32[]{:S(2)}, u32[]{:S(2)}) async-start(bf16[8,128,128]{2,1,0:T(8,128)(2,1)} %attend_head.3), calls=%async_computation.1 | async-start | bytes 524288 | tf_op jit(solution)/shard_map/all_to_all | solution.py:345
  62.6 9.2 %all-gather.11.cloned.1.call-done = bf16[8,512,128]{2,1,0:T(8,128)(2,1)} async-done(((bf16[2,512,128]{2,1,0:T(8,128)(2,1)}), bf16[8,512,128]{2,1,0:T(8,128)(2,1)}) %all-gather.11.cloned.1.call-update) | async-done | bytes 1048592 | tf_op jit(solution)/shard_map/all_gather | solution.py:359
  71.8 1.2 copy-done.4
  73.0 5.5 %attend_head.4.refs_8_ = bf16[8,128,256]{2,1,0:T(8,128)(2,1)S(1)} custom-call(s32[4]{0:T(128)S(1)} %pad_add_fusion.info, bf16[8,128,1152]{2,1,0:T(8,128)(2,1)S(1)} %all-to-all-done.refs_0_.refs_1_.refs_2_, bf16[8,128,1152]{2,1,0:T(8,128)(2,1)S(1)} %all-to-all-done.refs_0_.refs_1_.refs_2_, bf16[8,128,1152]{2,1,0:T(8,128)(2,1)S(1)} %all-to-all-done.refs_0_.refs_1_.refs_2_, ...), custom_call_target="tpu_custom_call" | custom-call | flops 1342177280 | bytes 1835008 | tf_op jit(solution)/shard_map/attend_head/pallas_call | solution.py:225
  78.5 22.3 %all-gather.9.cloned.1.call-done = bf16[8,512,128]{2,1,0:T(8,128)(2,1)} async-done(((bf16[2,512,128]{2,1,0:T(8,128)(2,1)}), bf16[8,512,128]{2,1,0:T(8,128)(2,1)}) %all-gather.9.cloned.1.call-update) | async-done | bytes 1048592 | tf_op jit(solution)/shard_map/all_gather | solution.py:359
  100.8 1.2 copy-done.5
  102.0 5.5 %attend_head.5 = bf16[8,128,256]{2,1,0:T(8,128)(2,1)S(1)} custom-call(s32[4]{0:T(128)S(1)} %pad_add_fusion.info, bf16[8,128,1152]{2,1,0:T(8,128)(2,1)S(1)} %all-to-all-done.refs_0_.refs_1_.refs_2_, bf16[8,128,1152]{2,1,0:T(8,128)(2,1)S(1)} %all-to-all-done.refs_0_.refs_1_.refs_2_, ...), custom_call_target="tpu_custom_call", output_to_operand_aliasing={{}: (9, {})} | custom-call | flops 1342177280 | bytes 1835008 | tf_op jit(solution)/shard_map/attend_head/pallas_call | solution.py:225
  107.5 13.2 %all_to_all.15.x_ref.refs_0_ = bf16[8,128,256]{2,1,0:T(8,128)(2,1)S(1)} all-to-all(bf16[8,128,256]{2,1,0:T(8,128)(2,1)S(1)} %attend_head.5), channel_id=1, replica_groups={{0,1,2,3,4,5,6,7},{8,9,10,11,12,13,14,15},{16,17,18,19,20,21,22,23},{24..., dimensions={0} | all-to-all | bytes 1048576 | tf_op jit(solution)/shard_map/all_to_all | solution.py:345
  120.8 0.4 collective-permute-start.1
  121.2 6.4 %copy-done = bf16[3072,3072]{1,0:T(8,128)(2,1)S(1)} copy-done((bf16[3072,3072]{1,0:T(8,128)(2,1)S(1)}, bf16[3072,3072]{1,0:T(8,128)(2,1)}, u32[]{:S(2)}) %copy-start) | copy-done | bytes 18874392
  127.6 3.8 %project_early.1.refs_2_ = f32[64,3072]{1,0:T(8,128)S(1)} custom-call(bf16[8,128,256]{2,1,0:T(8,128)(2,1)S(1)} %all_to_all.15.x_ref.refs_0_, bf16[8,3,128,3072]{3,2,1,0:T(8,128)(2,1)S(1)} %bitcast.9), custom_call_target="tpu_custom_call" | custom-call | flops 805306368 | bytes 12582912 | tf_op jit(solution)/shard_map/project_early/pallas_call | solution.py:283
  131.4 6.4 %copy-done.1 = bf16[3072,3072]{1,0:T(8,128)(2,1)S(1)} copy-done((bf16[3072,3072]{1,0:T(8,128)(2,1)S(1)}, bf16[3072,3072]{1,0:T(8,128)(2,1)}, u32[]{:S(2)}) %copy-start.1) | copy-done | bytes 18874392
  137.8 3.5 %project_last.1 = bf16[64,3072]{1,0:T(8,128)(2,1)} custom-call(bf16[8,128,128]{2,1,0:T(8,128)(2,1)S(1)} %all-to-all-done.1.x_ref.refs_1_, bf16[8,3,128,3072]{3,2,1,0:T(8,128)(2,1)S(1)} %bitcast.10, bf16[64,3072]{1,0:T(8,128)(2,1)S(1)} %copy-done.9, f32[1,3072]{1,0:T(1,128)S(1)} %bitcast.20, f32[64,3072]{1,0:T(8,128)S(1)} %project_early.1.refs_2_), custom_call_target="tpu_custom_call" | custom-call | flops 402653184 | bytes 6291456 | tf_op jit(solution)/shard_map/project_last/pallas_call | solution.py:283
  141.3 0.1 broadcast_select_fusion.1
  141.4 0.9 pad_maximum_fusion
  (28 shorter events, 0.1 us)
Async XLA Ops:
  7.2 35.6 %all-gather.7.cloned.1.call-start = ((), (), s32[]{:S(2)}) async-start(), calls=%async_computation.3 | async-start | bytes 1310720 | tf_op jit(solution)/shard_map/all_gather | solution.py:359
  7.2 9.0 %copy-start.2 = (bf16[128,9216]{1,0:T(8,128)(2,1)S(1)}, bf16[128,9216]{1,0:T(8,128)(2,1)}, u32[]{:S(2)}) copy-start(bf16[128,9216]{1,0:T(8,128)(2,1)} %refs_5_.1) | copy-start | bytes 7077892
  7.2 9.0 %copy-start.3 = (bf16[64,9216]{1,0:T(8,128)(2,1)S(1)}, bf16[64,9216]{1,0:T(8,128)(2,1)}, u32[]{:S(2)}) copy-start(bf16[64,9216]{1,0:T(8,128)(2,1)} %refs_2_.1) | copy-start | bytes 3538948
  9.5 2.4 %collective-permute-start = (bf16[2,256,384]{2,1,0:T(8,128)(2,1)}, bf16[2,256,384]{2,1,0:T(8,128)(2,1)}, u32[]{:S(2)}, u32[]{:S(2)}) collective-permute-start(bf16[2,256,384]{2,1,0:T(8,128)(2,1)} %get-tuple-element.8), channel_id=1, source_target_pairs={{0,4},{4,0},{8,12},{12,8},{16,20},{20,16},{24,28},{28,24},{1,5},{5... | collective-permute-start | bytes 1179656 | tf_op jit(solution)/shard_map/ppermute | solution.py:353
  14.4 57.3 %all-gather.11.cloned.1.call-start = ((), (), s32[]{:S(2)}) async-start(), calls=%async_computation.5 | async-start | bytes 1310720 | tf_op jit(solution)/shard_map/all_gather | solution.py:359
  17.3 1.4 copy-start.6
  18.7 4.2 %copy-start.11 = (bf16[2,256,128]{2,1,0:T(8,128)(2,1)S(1)}, bf16[2,256,128]{2,1,0:T(8,128)(2,1)}, u32[]{:S(2)}) copy-start(bf16[2,256,128]{2,1,0:T(8,128)(2,1)} %get-tuple-element.5) | copy-start | bytes 393220
  18.7 4.2 %copy-start.12 = (bf16[2,256,128]{2,1,0:T(8,128)(2,1)S(1)}, bf16[2,256,128]{2,1,0:T(8,128)(2,1)}, u32[]{:S(2)}) copy-start(bf16[2,256,128]{2,1,0:T(8,128)(2,1)} %get-tuple-element.10) | copy-start | bytes 393220
  18.7 32.9 %copy-start.8 = (bf16[2,256,384]{2,1,0:T(8,128)(2,1)S(1)}, bf16[2,256,384]{2,1,0:T(8,128)(2,1)}, u32[]{:S(2)}) copy-start(bf16[2,256,384]{2,1,0:T(8,128)(2,1)} %get-tuple-element.7.refs_3_) | copy-start | bytes 1179652
  18.7 32.9 %all-to-all-start = ((bf16[8,128,1152]{2,1,0:T(8,128)(2,1)}), bf16[8,128,1152]{2,1,0:T(8,128)(2,1)S(1)}, u32[]{:S(2)}, u32[]{:S(2)}) async-start(bf16[8,128,1152]{2,1,0:T(8,128)(2,1)} %copy-done.6), calls=%async_computation | async-start | bytes 4718592 | tf_op jit(solution)/shard_map/all_to_all | solution.py:345
  22.9 77.9 %all-gather.9.cloned.1.call-start = ((), (), s32[]{:S(2)}) async-start(), calls=%async_computation.4 | async-start | bytes 1310720 | tf_op jit(solution)/shard_map/all_gather | solution.py:359
  51.6 1.3 copy-start.7
  59.0 48.5 %all-to-all-start.1 = ((bf16[8,128,128]{2,1,0:T(8,128)(2,1)}), bf16[8,128,128]{2,1,0:T(8,128)(2,1)S(1)}, u32[]{:S(2)}, u32[]{:S(2)}) async-start(bf16[8,128,128]{2,1,0:T(8,128)(2,1)} %attend_head.3), calls=%async_computation.1 | async-start | bytes 524288 | tf_op jit(solution)/shard_map/all_to_all | solution.py:345
  71.7 1.2 copy-start.4
  100.8 1.2 copy-start.5
  120.8 20.5 %collective-permute-start.1 = (bf16[64,3072]{1,0:T(8,128)(2,1)S(1)}, bf16[64,3072]{1,0:T(8,128)(2,1)S(1)}, u32[]{:S(2)}, u32[]{:S(2)}) collective-permute-start(bf16[64,3072]{1,0:T(8,128)(2,1)S(1)} %unpack_text.1), channel_id=1, source_target_pairs={{0,4},{4,0},{8,12},{12,8},{16,20},{20,16},{24,28},{28,24},{1,5},{5... | collective-permute-start | bytes 1179656 | tf_op jit(solution)/shard_map/ppermute | solution.py:382
  121.2 6.4 %copy-start = (bf16[3072,3072]{1,0:T(8,128)(2,1)S(1)}, bf16[3072,3072]{1,0:T(8,128)(2,1)}, u32[]{:S(2)}) copy-start(bf16[3072,3072]{1,0:T(8,128)(2,1)} %param.11) | copy-start | bytes 56623108
  127.6 3.9 %copy-start.9 = (bf16[64,3072]{1,0:T(8,128)(2,1)S(1)}, bf16[64,3072]{1,0:T(8,128)(2,1)}, u32[]{:S(2)}) copy-start(bf16[64,3072]{1,0:T(8,128)(2,1)} %refs_0_.3) | copy-start | bytes 1179652
  127.6 3.9 %copy-start.10 = (f32[3072]{0:T(1024)S(1)}, f32[3072]{0:T(1024)}, u32[]{:S(2)}) copy-start(f32[3072]{0:T(1024)} %param.10) | copy-start | bytes 36868
  131.4 6.4 %copy-start.1 = (bf16[3072,3072]{1,0:T(8,128)(2,1)S(1)}, bf16[3072,3072]{1,0:T(8,128)(2,1)}, u32[]{:S(2)}) copy-start(bf16[3072,3072]{1,0:T(8,128)(2,1)} %param.11) | copy-start | bytes 56623108
Sparse Core Ops, SparseCore 0:
  14.6 28.1 all-gather.6
  44.3 27.4 all-gather.10
  73.3 27.4 all-gather.8

commit v4 on v3

--- a/solution.py
+++ b/solution.py
@@ -11,6 +11,7 @@
 HD = 128
 SCALE = math.log2(math.e) / math.sqrt(HD)
 VMEM_LIMIT = 24 * 1024 * 1024
+WIDE_LIMIT = 48 * 1024 * 1024
 TILE = 256
 LARGE = 2.0**60
 
@@ -107,8 +108,13 @@
 def head_body(pair, img_rows, others, has_earlier, info, *refs):
     q_ref, k_ref, v_ref = refs[:3]
     stale = refs[3 : 3 + pair]
-    arrived = refs[3 + pair : 3 + pair + others]
-    out, aug, total, flag = refs[3 + pair + others + has_earlier :]
+    candidates = refs[3 + pair : 3 + pair + 2 * others]
+    out, arrived, aug, total, flag = refs[3 + pair + 2 * others + has_earlier :]
+    for index in range(others):
+        from_left = info[1 + index] == 1
+        arrived[index] = jnp.where(
+            from_left, candidates[2 * index][...], candidates[2 * index + 1][...]
+        )
     core = info[0]
     k_img, k_txt = split_rows(k_ref[...], img_rows)
     v_img, v_txt = split_rows(v_ref[...], img_rows)
@@ -123,7 +129,7 @@
         return q_txt[span.start - fresh_rows : span.stop - fresh_rows, :]
 
     def key_sets():
-        shared = [(k_txt, v_txt)] + [(block[0, 0], block[0, 1]) for block in arrived]
+        shared = [(k_txt, v_txt)] + [(arrived[i, 0], arrived[i, 1]) for i in range(others)]
         for group in range(pair):
             span = slice(group * group_rows, (group + 1) * group_rows)
             own = [(k_img[span, :], v_img[span, :])]
@@ -199,29 +205,30 @@
     )
 
 
-def attend_head(info, qkv, img_rows, stale, gathered, head, place, places, earlier=None):
+def attend_head(info, qkv, img_rows, stale, arrived, head, place, places, earlier=None):
     heads = qkv.shape[2] // (3 * HD)
-    others = gathered.shape[0] - 1
+    others = len(arrived)
+    block_shape = arrived[0][0].shape
     rows = qkv.shape[0] * qkv.shape[1]
 
+    def spec(shape, block):
+        return pl.BlockSpec(
+            shape, lambda n, info: (0, 0, block), pipeline_mode=pl.Buffered(buffer_count=1)
+        )
+
     def columns(array, block):
-        return pl.BlockSpec(array.shape[:2] + (HD,), lambda n, info: (0, 0, block))
-
-    def other(index):
-        return pl.BlockSpec(
-            (1,) + gathered.shape[1:], lambda n, info: (info[1 + index], 0, 0, 0)
-        )
-
-    operands = [qkv] * 3 + list(stale) + [gathered] * others
+        return spec(array.shape[:2] + (HD,), block)
+
+    operands = [qkv] * 3 + list(stale) + [block for either in arrived for block in either]
     in_specs = [columns(qkv, part * heads + head) for part in range(3)]
     in_specs += [columns(block, head) for block in stale]
-    in_specs += [other(index) for index in range(others)]
+    in_specs += [spec(block_shape, 0)] * (2 * others)
     aliases = {}
     if earlier is not None:
         aliases = {1 + len(operands): 0}
         operands.append(earlier)
         in_specs.append(pl.BlockSpec(memory_space=pl.ANY))
-    keys = others * gathered.shape[2] + 2 * rows // 2
+    keys = others * block_shape[1] + rows
     return pl.pallas_call(
         functools.partial(head_body, len(stale), img_rows, others, int(earlier is not None)),
         grid_spec=pltpu.PrefetchScalarGridSpec(
@@ -230,6 +237,7 @@
             in_specs=in_specs,
             out_specs=pl.BlockSpec(qkv.shape[:2] + (HD,), lambda n, info: (0, 0, place)),
             scratch_shapes=[
+                pltpu.VMEM((others,) + block_shape, qkv.dtype),
                 pltpu.VMEM((rows, HD), jnp.bfloat16),
                 pltpu.VMEM((rows, 2 * HD), jnp.float32),
                 pltpu.SMEM((1,), jnp.int32),
@@ -243,53 +251,68 @@
     )(info, *operands)
 
 
-def project_body(order, last, x_ref, weight, *refs):
+def project_body(order, first_head, heads, group, last, *refs):
     if last:
-        residual, gate, earlier, out, flat = refs
+        x_ref, weight, residual, gate, earlier, out, flat, held, total, sems = refs
     else:
-        out, flat = refs
-
-    @pl.when(pl.program_id(0) == 0)
-    def _():
-        rows, width = flat.shape[0], x_ref.shape[2]
-        for source, place in enumerate(order):
-            flat[:, place * width : (place + 1) * width] = x_ref[source, :rows, :]
-
-    columns = weight.shape[3]
-    block = weight[...].reshape(flat.shape[1], columns)
-    projected = jnp.dot(flat[...], block, preferred_element_type=jnp.float32)
+        x_ref, weight, out, flat, held, total, sems = refs
+    chunks = weight.shape[0] // group
+    copies = [
+        pltpu.make_async_copy(
+            weight.at[pl.ds(chunk * group, group), pl.ds(first_head, heads)],
+            held.at[pl.ds(chunk * group, group)],
+            sems.at[chunk],
+        )
+        for chunk in range(chunks)
+    ]
+    for copy in copies:
+        copy.start()
+    rows, width = flat.shape[0], x_ref.shape[2]
+    for source, place in enumerate(order):
+        flat[:, place * width : (place + 1) * width] = x_ref[source, :rows, :]
+    depth = group * width
+    for chunk, copy in enumerate(copies):
+        copy.wait()
+        block = held[chunk * group : (chunk + 1) * group].reshape(depth, held.shape[3])
+        part = jnp.dot(
+            flat[:, chunk * depth : (chunk + 1) * depth], block, preferred_element_type=jnp.float32
+        )
+        if chunk == 0:
+            total[...] = part
+        else:
+            total[...] += part
     if last:
-        projected = earlier[...] + projected
-        projected = residual[...].astype(jnp.float32) + gate[...] * projected
-    out[...] = projected.astype(out.dtype)
+        projected = earlier[...] + total[...]
+        out[...] = (residual[...].astype(jnp.float32) + gate[...] * projected).astype(out.dtype)
+    else:
+        out[...] = total[...]
 
 
 def project(x, order, weight, first_head, rows, final=None):
-    model = weight.shape[3]
+    destinations, model = weight.shape[0], weight.shape[3]
     heads = x.shape[2] // HD
-    columns = 512 if model % 512 == 0 else HD
-    row_spec = pl.BlockSpec((rows, columns), lambda n: (0, n))
-    operands, in_specs = [x, weight], [
-        pl.BlockSpec(x.shape, lambda n: (0, 0, 0)),
-        pl.BlockSpec(
-            (weight.shape[0], heads, HD, columns), lambda n: (0, first_head // heads, 0, n)
-        ),
-    ]
+    group = 2 if heads % 2 and destinations % 2 == 0 else 1
+    operands = [x, weight]
+    in_specs = [pl.BlockSpec(memory_space=pltpu.VMEM), pl.BlockSpec(memory_space=pl.ANY)]
     if final is not None:
         residual, gate, earlier = final
         operands += [residual, gate.reshape(1, model), earlier]
-        in_specs += [row_spec, pl.BlockSpec((1, columns), lambda n: (0, n)), row_spec]
+        in_specs += [pl.BlockSpec(memory_space=pltpu.VMEM)] * 3
     depth = x.shape[0] * x.shape[2]
     return pl.pallas_call(
-        functools.partial(project_body, order, final is not None),
-        grid=(model // columns,),
+        functools.partial(project_body, order, first_head, heads, group, final is not None),
         in_specs=in_specs,
-        out_specs=row_spec,
+        out_specs=pl.BlockSpec(memory_space=pltpu.VMEM),
         out_shape=jax.ShapeDtypeStruct(
             (rows, model), jnp.float32 if final is None else residual.dtype
         ),
-        scratch_shapes=[pltpu.VMEM((rows, depth), x.dtype)],
-        compiler_params=params(),
+        scratch_shapes=[
+            pltpu.VMEM((rows, depth), x.dtype),
+            pltpu.VMEM((destinations, heads, HD, model), weight.dtype),
+            pltpu.VMEM((rows, model), jnp.float32),
+            pltpu.SemaphoreType.DMA((destinations // group,)),
+        ],
+        compiler_params=pltpu.CompilerParams(vmem_limit_bytes=WIDE_LIMIT),
         cost_estimate=pl.CostEstimate(
             flops=2 * rows * model * depth, bytes_accessed=2 * model * depth, transcendentals=0
         ),
@@ -339,8 +362,6 @@
 
     order = [column_block(d) for d in range(destinations)]
     groups = [[g * destinations + d for d in range(destinations)] for g in range(planes)]
-    columns = [[z * pair + c for z in range(planes)] for c in range(pair)]
-
     def exchange(x):
         return lax.all_to_all(
             x, ("patch", "head"), split_axis=0, concat_axis=0, axis_index_groups=groups, tiled=True
@@ -352,30 +373,35 @@
         theirs = lax.dynamic_slice_in_dim(stale_kv, (1 - core) * width, width, 2)
         stale.append(lax.ppermute(theirs, "patch", swap_pairs))
 
-    gathered = []
+    arrived = []
     for head in range(heads):
         columns_of = [block[:, :, head * HD : (head + 1) * HD] for block in stale]
-        gathered.append(
-            lax.all_gather(
-                jnp.concatenate(columns_of, axis=1), "patch", axis=0, axis_index_groups=columns
-            )
-        )
+        from_left = from_right = jnp.concatenate(columns_of, axis=1)
+        left, right = [], []
+        for step in range(1, planes):
+            right_pairs = [(p, p + pair) for p in range((step - 1) * pair, patches - pair)]
+            left_pairs = [(p + pair, p) for p in range(0, patches - step * pair)]
+            from_left = lax.ppermute(from_left, "patch", right_pairs)
+            from_right = lax.ppermute(from_right, "patch", left_pairs)
+            left.append(from_left)
+            right.append(from_right)
+        arrived.append(list(zip(left, reversed(right))))
 
     core_only = core.astype(jnp.int32).reshape(1)
     qkv = exchange(
         pack(core_only, img_qkv, txt_qkv, text_rows, destinations, column_block, width, stale[1:])
     )
 
-    info = jnp.stack([core] + [(plane + step) % planes for step in range(1, planes)])
+    info = jnp.stack([core] + [plane >= step for step in range(1, planes)])
     info = info.astype(jnp.int32)
     early = None
     for head in range(heads - 1):
         early = attend_head(
-            info, qkv, img_rows, stale, gathered[head], head, head, heads - 1, early
+            info, qkv, img_rows, stale, arrived[head], head, head, heads - 1, early
         )
     weight = proj_weight.reshape(destinations, heads, HD, model)
     early = exchange(early)
-    late = exchange(attend_head(info, qkv, img_rows, stale, gathered[-1], heads - 1, 0, 1))
+    late = exchange(attend_head(info, qkv, img_rows, stale, arrived[-1], heads - 1, 0, 1))
 
     text_out = unpack_text([early, late], order, img_rows)
     if pair == 2:

time: 151 us -> 117 us (0.77)
  waiting for transfers between devices: 59.4 us -> 1.4 us
  starting transfers between devices: 8.86 us -> 56.4 us
  between operations: 14 us -> 0.99 us
  local copies, waits for them, and re-layouts: 23.6 us -> 13.4 us
  other arithmetic: 4.19 us -> 1.13 us
  Pallas kernels: 25.6 us -> 28 us
    all_gather x3 -> x0, waiting for transfers between devices: 50.4 us -> none  [per_device(): lax.all_gather(jnp.concatenate(columns_of, axis=1), 'patch', axis=0, axis...]
    ppermute x0 -> x18, starting transfers between devices: none -> 42 us  [the longest x9 22 us: per_device(): from_left = lax.ppermute(from_left, 'patch', right_pairs)]
    all_to_all x2, waiting for transfers between devices: 8.86 us -> 0.01 us  [exchange(): lax.all_to_all(x, ('patch', 'head'), split_axis=0, concat_axis=0, axis_in...]
    unnamed x26 -> x34, local copies, waits for them, and re-layouts: 17.9 us -> 10.9 us
    all_to_all x2, starting transfers between devices: 7.7 us -> 13.2 us  [exchange(): lax.all_to_all(x, ('patch', 'head'), split_axis=0, concat_axis=0, axis_in...]
    concatenate x3, other arithmetic: 3.13 us -> 0.06 us  [per_device(): from_left = from_right = jnp.concatenate(columns_of, axis=1)]
    slice x2, local copies, waits for them, and re-layouts: 3.53 us -> 1.13 us  [per_device(): columns_of = [block[:, :, head * HD:(head + 1) * HD] for block in stale]]
    pallas_call x2, Pallas kernels: 7.35 us -> 9.15 us  [project(): pl.pallas_call(functools.partial(project_body, order, first_head, heads,...]
  transfers between devices with their start and end apart: 7 -> 22, of which waited for: 4 -> 1; matrix products, arithmetic and copies ran while one was open for 3% -> 1% of each run, Pallas kernels for 17% -> 24%
where the time goes in v4:
time: 117 us; the launch traced here: 115 us
  starting transfers between devices  56.4 us (48%)
  Pallas kernels  28 us (24%)
  local copies, waits for them, and re-layouts  13.4 us (11%)
  blocking collectives  13.3 us (11%)
  waiting for transfers between devices  1.4 us (1%)
    ppermute x9, starting transfers between devices, per_device(): from_left = lax.ppermute(from_left, 'patch', right_pairs)  22 us
    ppermute x9, starting transfers between devices, per_device(): from_right = lax.ppermute(from_right, 'patch', left_pairs)  20 us
    pallas_call x3, Pallas kernels, attend_head(): pl.pallas_call(functools.partial(head_body, len(stale), img_rows, others,...  17.8 us
    all_to_all x1, blocking collectives, exchange(): lax.all_to_all(x, ('patch', 'head'), split_axis=0, concat_axis=0, axis_in...  13.3 us
    all_to_all x2, starting transfers between devices, exchange(): lax.all_to_all(x, ('patch', 'head'), split_axis=0, concat_axis=0, axis_in...  13.2 us
    unnamed x34, local copies, waits for them, and re-layouts  10.9 us
    pallas_call x2, Pallas kernels, project(): pl.pallas_call(functools.partial(project_body, order, first_head, heads,...  9.15 us
  transfers between devices with their start and end apart: 22, of which 1 were waited for; matrix products, arithmetic and copies ran while one was open for 1% of the time, Pallas kernels for 24%

profile of v4, /device:TPU:17, one launch (start us, length us, event | category | flops | bytes accessed | tf_op | source)
XLA Modules:
  0.0 114.5 jit_solution(15262299178338458)
XLA Ops:
  0.7 1.3 %constant_dynamic-slice_fusion.3 = (bf16[2,256,384]{2,1,0:T(8,128)(2,1)S(1)}, bf16[2,256,384]{2,1,0:T(8,128)(2,1)S(1)}) fusion(bf16[2,256,768]{2,1,0:T(8,128)(2,1)} %param.8, s32[]{:T(128)S(6)} %select_n.32, s32[]{:T(128)S(6)} %select_n.31), kind=kLoop, calls=%fused_computation.9 | loop fusion | bytes 1572872 | tf_op jit(solution)/shard_map/dynamic_slice | solution.py:371
  2.7 1.3 %collective-permute-done.refs_6_.refs_4_ = bf16[2,256,384]{2,1,0:T(8,128)(2,1)S(1)} collective-permute-done((bf16[2,256,384]{2,1,0:T(8,128)(2,1)S(1)}, bf16[2,256,384]{2,1,0:T(8,128)(2,1)S(1)}, u32[]{:S(2)}, u32[]{:S(2)}) %collective-permute-start) | collective-permute-done | bytes 393248 | tf_op jit(solution)/shard_map/ppermute | solution.py:374
  4.1 1.7 %copy-done = bf16[128,9216]{1,0:T(8,128)(2,1)S(1)} copy-done((bf16[128,9216]{1,0:T(8,128)(2,1)S(1)}, bf16[128,9216]{1,0:T(8,128)(2,1)}, u32[]{:S(2)}) %copy-start) | copy-done | bytes 2359320
  5.7 1.0 pack_heads.1
  6.8 1.4 %copy-done.2 = bf16[8,128,1152]{2,1,0:T(8,128)(2,1)} copy-done((bf16[8,128,1152]{2,1,0:T(8,128)(2,1)}, bf16[8,128,1152]{2,1,0:T(8,128)(2,1)S(1)}, u32[]{:S(2)}) %copy-start.2) | copy-done | bytes 2359320
  8.2 4.1 %all-to-all-start = ((bf16[8,128,1152]{2,1,0:T(8,128)(2,1)}), bf16[8,128,1152]{2,1,0:T(8,128)(2,1)S(1)}, u32[]{:S(2)}, u32[]{:S(2)}) async-start(bf16[8,128,1152]{2,1,0:T(8,128)(2,1)} %copy-done.2), calls=%async_computation | async-start | bytes 4718592 | tf_op jit(solution)/shard_map/all_to_all | solution.py:366
  12.3 1.1 constant_dynamic-slice_fusion
  13.4 2.1 %collective-permute-start.14 = (bf16[2,512,128]{2,1,0:T(8,128)(2,1)S(1)}, bf16[2,512,128]{2,1,0:T(8,128)(2,1)S(1)}, u32[]{:S(2)}, u32[]{:S(2)}) collective-permute-start(bf16[2,512,128]{2,1,0:T(8,128)(2,1)S(1)} %pad_maximum_fusion.3), channel_id=1, source_target_pairs={{8,0},{12,4},{16,8},{20,12},{24,16},{28,20},{9,1},{13,5},{17,9},{2... | collective-permute-start | bytes 786440 | tf_op jit(solution)/shard_map/ppermute | solution.py:385
  15.5 3.2 %collective-permute-start.13 = (bf16[2,512,128]{2,1,0:T(8,128)(2,1)S(1)}, bf16[2,512,128]{2,1,0:T(8,128)(2,1)S(1)}, u32[]{:S(2)}, u32[]{:S(2)}) collective-permute-start(bf16[2,512,128]{2,1,0:T(8,128)(2,1)S(1)} %pad_maximum_fusion.3), channel_id=1, source_target_pairs={{0,8},{4,12},{8,16},{12,20},{16,24},{20,28},{1,9},{5,13},{9,17},{1... | collective-permute-start | bytes 786440 | tf_op jit(solution)/shard_map/ppermute | solution.py:384
  18.8 2.1 %collective-permute-start.2 = (bf16[2,512,128]{2,1,0:T(8,128)(2,1)S(1)}, bf16[2,512,128]{2,1,0:T(8,128)(2,1)S(1)}, u32[]{:S(2)}, u32[]{:S(2)}) collective-permute-start(bf16[2,512,128]{2,1,0:T(8,128)(2,1)S(1)} %pad_maximum_fusion.1), channel_id=1, source_target_pairs={{8,0},{12,4},{16,8},{20,12},{24,16},{28,20},{9,1},{13,5},{17,9},{2... | collective-permute-start | bytes 786440 | tf_op jit(solution)/shard_map/ppermute | solution.py:385
  20.8 3.2 %collective-permute-start.1 = (bf16[2,512,128]{2,1,0:T(8,128)(2,1)S(1)}, bf16[2,512,128]{2,1,0:T(8,128)(2,1)S(1)}, u32[]{:S(2)}, u32[]{:S(2)}) collective-permute-start(bf16[2,512,128]{2,1,0:T(8,128)(2,1)S(1)} %pad_maximum_fusion.1), channel_id=1, source_target_pairs={{0,8},{4,12},{8,16},{12,20},{16,24},{20,28},{1,9},{5,13},{9,17},{1... | collective-permute-start | bytes 786440 | tf_op jit(solution)/shard_map/ppermute | solution.py:384
  24.1 2.1 %collective-permute-start.8 = (bf16[2,512,128]{2,1,0:T(8,128)(2,1)S(1)}, bf16[2,512,128]{2,1,0:T(8,128)(2,1)S(1)}, u32[]{:S(2)}, u32[]{:S(2)}) collective-permute-start(bf16[2,512,128]{2,1,0:T(8,128)(2,1)S(1)} %pad_maximum_fusion.2), channel_id=1, source_target_pairs={{8,0},{12,4},{16,8},{20,12},{24,16},{28,20},{9,1},{13,5},{17,9},{2... | collective-permute-start | bytes 786440 | tf_op jit(solution)/shard_map/ppermute | solution.py:385
  26.2 3.2 %collective-permute-start.7 = (bf16[2,512,128]{2,1,0:T(8,128)(2,1)S(1)}, bf16[2,512,128]{2,1,0:T(8,128)(2,1)}, u32[]{:S(2)}, u32[]{:S(2)}) collective-permute-start(bf16[2,512,128]{2,1,0:T(8,128)(2,1)S(1)} %pad_maximum_fusion.2), channel_id=1, source_target_pairs={{0,8},{4,12},{8,16},{12,20},{16,24},{20,28},{1,9},{5,13},{9,17},{1... | collective-permute-start | bytes 786440 | tf_op jit(solution)/shard_map/ppermute | solution.py:384
  29.4 2.8 %collective-permute-start.15 = (bf16[2,512,128]{2,1,0:T(8,128)(2,1)S(1)}, bf16[2,512,128]{2,1,0:T(8,128)(2,1)}, u32[]{:S(2)}, u32[]{:S(2)}) collective-permute-start(bf16[2,512,128]{2,1,0:T(8,128)(2,1)S(1)} %collective-permute-done.14.refs_10_), channel_id=1, source_target_pairs={{8,0},{12,4},{16,8},{20,12},{9,1},{13,5},{17,9},{21,13},{10,2},{14... | collective-permute-start | bytes 786440 | tf_op jit(solution)/shard_map/ppermute | solution.py:385
  32.9 2.8 %collective-permute-start.3 = (bf16[2,512,128]{2,1,0:T(8,128)(2,1)S(1)}, bf16[2,512,128]{2,1,0:T(8,128)(2,1)}, u32[]{:S(2)}, u32[]{:S(2)}) collective-permute-start(bf16[2,512,128]{2,1,0:T(8,128)(2,1)S(1)} %collective-permute-done.2.refs_10_), channel_id=1, source_target_pairs={{8,0},{12,4},{16,8},{20,12},{9,1},{13,5},{17,9},{21,13},{10,2},{14... | collective-permute-start | bytes 786440 | tf_op jit(solution)/shard_map/ppermute | solution.py:385
  35.7 1.9 %collective-permute-start.5 = (bf16[2,512,128]{2,1,0:T(8,128)(2,1)S(1)}, bf16[2,512,128]{2,1,0:T(8,128)(2,1)}, u32[]{:S(2)}, u32[]{:S(2)}) collective-permute-start(bf16[2,512,128]{2,1,0:T(8,128)(2,1)S(1)} %collective-permute-done.1.refs_5_), channel_id=1, source_target_pairs={{8,16},{12,20},{16,24},{20,28},{9,17},{13,21},{17,25},{21,29},{10,... | collective-permute-start | bytes 786440 | tf_op jit(solution)/shard_map/ppermute | solution.py:384
  38.4 1.9 %collective-permute-start.17 = (bf16[2,512,128]{2,1,0:T(8,128)(2,1)S(1)}, bf16[2,512,128]{2,1,0:T(8,128)(2,1)}, u32[]{:S(2)}, u32[]{:S(2)}) collective-permute-start(bf16[2,512,128]{2,1,0:T(8,128)(2,1)S(1)} %collective-permute-done.13.refs_5_), channel_id=1, source_target_pairs={{8,16},{12,20},{16,24},{20,28},{9,17},{13,21},{17,25},{21,29},{10,... | collective-permute-start | bytes 786440 | tf_op jit(solution)/shard_map/ppermute | solution.py:384
  41.0 4.1 %collective-permute-start.9 = (bf16[2,512,128]{2,1,0:T(8,128)(2,1)S(1)}, bf16[2,512,128]{2,1,0:T(8,128)(2,1)S(1)}, u32[]{:S(2)}, u32[]{:S(2)}) collective-permute-start(bf16[2,512,128]{2,1,0:T(8,128)(2,1)S(1)} %collective-permute-done.8.refs_10_), channel_id=1, source_target_pairs={{8,0},{12,4},{16,8},{20,12},{9,1},{13,5},{17,9},{21,13},{10,2},{14... | collective-permute-start | bytes 786440 | tf_op jit(solution)/shard_map/ppermute | solution.py:385
  45.8 1.9 %collective-permute-start.11 = (bf16[2,512,128]{2,1,0:T(8,128)(2,1)}, bf16[2,512,128]{2,1,0:T(8,128)(2,1)}, u32[]{:S(2)}, u32[]{:S(2)}) collective-permute-start(bf16[2,512,128]{2,1,0:T(8,128)(2,1)} %collective-permute-done.7.refs_5_), channel_id=1, source_target_pairs={{8,16},{12,20},{16,24},{20,28},{9,17},{13,21},{17,25},{21,29},{10,... | collective-permute-start | bytes 786440 | tf_op jit(solution)/shard_map/ppermute | solution.py:384
  47.8 1.4 %collective-permute-start.4 = (bf16[2,512,128]{2,1,0:T(8,128)(2,1)}, bf16[2,512,128]{2,1,0:T(8,128)(2,1)}, u32[]{:S(2)}, u32[]{:S(2)}) collective-permute-start(bf16[2,512,128]{2,1,0:T(8,128)(2,1)} %collective-permute-done.3.refs_8_), channel_id=1, source_target_pairs={{8,0},{12,4},{9,1},{13,5},{10,2},{14,6},{11,3},{15,7}} | collective-permute-start | bytes 786440 | tf_op jit(solution)/shard_map/ppermute | solution.py:385
  49.1 2.0 %collective-permute-start.6 = (bf16[2,512,128]{2,1,0:T(8,128)(2,1)}, bf16[2,512,128]{2,1,0:T(8,128)(2,1)}, u32[]{:S(2)}, u32[]{:S(2)}) collective-permute-start(bf16[2,512,128]{2,1,0:T(8,128)(2,1)} %collective-permute-done.5.refs_7_), channel_id=1, source_target_pairs={{16,24},{20,28},{17,25},{21,29},{18,26},{22,30},{19,27},{23,31}} | collective-permute-start | bytes 786440 | tf_op jit(solution)/shard_map/ppermute | solution.py:384
  51.1 1.4 %collective-permute-start.16 = (bf16[2,512,128]{2,1,0:T(8,128)(2,1)}, bf16[2,512,128]{2,1,0:T(8,128)(2,1)}, u32[]{:S(2)}, u32[]{:S(2)}) collective-permute-start(bf16[2,512,128]{2,1,0:T(8,128)(2,1)} %collective-permute-done.15.refs_8_), channel_id=1, source_target_pairs={{8,0},{12,4},{9,1},{13,5},{10,2},{14,6},{11,3},{15,7}} | collective-permute-start | bytes 786440 | tf_op jit(solution)/shard_map/ppermute | solution.py:385
  53.2 2.0 %collective-permute-start.18 = (bf16[2,512,128]{2,1,0:T(8,128)(2,1)}, bf16[2,512,128]{2,1,0:T(8,128)(2,1)}, u32[]{:S(2)}, u32[]{:S(2)}) collective-permute-start(bf16[2,512,128]{2,1,0:T(8,128)(2,1)} %collective-permute-done.17.refs_7_), channel_id=1, source_target_pairs={{16,24},{20,28},{17,25},{21,29},{18,26},{22,30},{19,27},{23,31}} | collective-permute-start | bytes 786440 | tf_op jit(solution)/shard_map/ppermute | solution.py:384
  55.2 1.4 %collective-permute-start.10 = (bf16[2,512,128]{2,1,0:T(8,128)(2,1)}, bf16[2,512,128]{2,1,0:T(8,128)(2,1)}, u32[]{:S(2)}, u32[]{:S(2)}) collective-permute-start(bf16[2,512,128]{2,1,0:T(8,128)(2,1)} %copy-done.14), channel_id=1, source_target_pairs={{8,0},{12,4},{9,1},{13,5},{10,2},{14,6},{11,3},{15,7}} | collective-permute-start | bytes 786440 | tf_op jit(solution)/shard_map/ppermute | solution.py:385
  56.6 2.6 %collective-permute-start.12 = (bf16[2,512,128]{2,1,0:T(8,128)(2,1)}, bf16[2,512,128]{2,1,0:T(8,128)(2,1)}, u32[]{:S(2)}, u32[]{:S(2)}) collective-permute-start(bf16[2,512,128]{2,1,0:T(8,128)(2,1)} %collective-permute-done.11.refs_7_), channel_id=1, source_target_pairs={{16,24},{20,28},{17,25},{21,29},{18,26},{22,30},{19,27},{23,31}} | collective-permute-start | bytes 786440 | tf_op jit(solution)/shard_map/ppermute | solution.py:384
  60.2 5.9 %attend_head.3 = bf16[8,128,128]{2,1,0:T(8,128)(2,1)S(1)} custom-call(s32[4]{0:T(128)S(1)} %pad_add_fusion.info, bf16[8,128,1152]{2,1,0:T(8,128)(2,1)S(1)} %all-to-all-done.refs_0_.refs_1_.refs_2_, bf16[8,128,1152]{2,1,0:T(8,128)(2,1)S(1)} %all-to-all-done.refs_0_.refs_1_.refs_2_, bf16[8,128,1152]{2,1,0:T(8,128)(2,1)S(1)} %all-to-all-done.refs_0_.refs_1_.refs_2_, ...), custom_call_target="tpu_custom_call" | custom-call | flops 1342177280 | bytes 1835008 | tf_op jit(solution)/shard_map/attend_head/pallas_call | solution.py:232
  66.8 9.1 %all-to-all-start.1 = ((bf16[8,128,128]{2,1,0:T(8,128)(2,1)}), bf16[8,128,128]{2,1,0:T(8,128)(2,1)S(1)}, u32[]{:S(2)}, u32[]{:S(2)}) async-start(bf16[8,128,128]{2,1,0:T(8,128)(2,1)} %copy-done.4), calls=%async_computation.1 | async-start | bytes 524288 | tf_op jit(solution)/shard_map/all_to_all | solution.py:366
  77.9 5.9 %attend_head.4.refs_11_ = bf16[8,128,256]{2,1,0:T(8,128)(2,1)S(1)} custom-call(s32[4]{0:T(128)S(1)} %pad_add_fusion.info, bf16[8,128,1152]{2,1,0:T(8,128)(2,1)S(1)} %all-to-all-done.refs_0_.refs_1_.refs_2_, bf16[8,128,1152]{2,1,0:T(8,128)(2,1)S(1)} %all-to-all-done.refs_0_.refs_1_.refs_2_, bf16[8,128,1152]{2,1,0:T(8,128)(2,1)S(1)} %all-to-all-done.refs_0_.refs_1_.refs_2_, ...), custom_call_target="tpu_custom_call" | custom-call | flops 1342177280 | bytes 1835008 | tf_op jit(solution)/shard_map/attend_head/pallas_call | solution.py:232
  83.9 6.0 %attend_head.5 = bf16[8,128,256]{2,1,0:T(8,128)(2,1)S(1)} custom-call(s32[4]{0:T(128)S(1)} %pad_add_fusion.info, bf16[8,128,1152]{2,1,0:T(8,128)(2,1)S(1)} %all-to-all-done.refs_0_.refs_1_.refs_2_, bf16[8,128,1152]{2,1,0:T(8,128)(2,1)S(1)} %all-to-all-done.refs_0_.refs_1_.refs_2_, ...), custom_call_target="tpu_custom_call", output_to_operand_aliasing={{}: (12, {})} | custom-call | flops 1342177280 | bytes 1835008 | tf_op jit(solution)/shard_map/attend_head/pallas_call | solution.py:232
  90.6 13.3 %all_to_all.15.refs_0_ = bf16[8,128,256]{2,1,0:T(8,128)(2,1)S(1)} all-to-all(bf16[8,128,256]{2,1,0:T(8,128)(2,1)} %copy-done.3), channel_id=1, replica_groups={{0,1,2,3,4,5,6,7},{8,9,10,11,12,13,14,15},{16,17,18,19,20,21,22,23},{24..., dimensions={0} | all-to-all | bytes 1048576 | tf_op jit(solution)/shard_map/all_to_all | solution.py:366
  104.3 5.1 %project_early.1.refs_4_ = f32[64,3072]{1,0:T(8,128)S(1)} custom-call(bf16[8,128,256]{2,1,0:T(8,128)(2,1)S(1)} %all_to_all.15.refs_0_, bf16[8,3,128,3072]{3,2,1,0:T(8,128)(2,1)} %bitcast.7), custom_call_target="tpu_custom_call" | custom-call | flops 805306368 | bytes 12582912 | tf_op jit(solution)/shard_map/project_early/pallas_call | solution.py:302
  109.5 4.0 %project_last.1 = bf16[64,3072]{1,0:T(8,128)(2,1)} custom-call(bf16[8,128,128]{2,1,0:T(8,128)(2,1)S(1)} %all-to-all-done.1.refs_0_.refs_1_, bf16[8,3,128,3072]{3,2,1,0:T(8,128)(2,1)} %bitcast.8, bf16[64,3072]{1,0:T(8,128)(2,1)S(1)} %copy-done.5, f32[1,3072]{1,0:T(1,128)S(1)} %bitcast.6, f32[64,3072]{1,0:T(8,128)S(1)} %project_early.1.refs_4_), custom_call_target="tpu_custom_call" | custom-call | flops 402653184 | bytes 6291456 | tf_op jit(solution)/shard_map/project_last/pallas_call | solution.py:302
  (63 shorter events, 10.3 us)
Async XLA Ops:
  0.6 3.4 %copy-start.1 = (bf16[64,9216]{1,0:T(8,128)(2,1)S(1)}, bf16[64,9216]{1,0:T(8,128)(2,1)}, u32[]{:S(2)}) copy-start(bf16[64,9216]{1,0:T(8,128)(2,1)} %refs_2_.2) | copy-start | bytes 3538948
  2.0 2.1 %collective-permute-start = (bf16[2,256,384]{2,1,0:T(8,128)(2,1)S(1)}, bf16[2,256,384]{2,1,0:T(8,128)(2,1)S(1)}, u32[]{:S(2)}, u32[]{:S(2)}) collective-permute-start(bf16[2,256,384]{2,1,0:T(8,128)(2,1)S(1)} %get-tuple-element.8), channel_id=1, source_target_pairs={{0,4},{4,0},{8,12},{12,8},{16,20},{20,16},{24,28},{28,24},{1,5},{5... | collective-permute-start | bytes 1179656 | tf_op jit(solution)/shard_map/ppermute | solution.py:374
  4.0 1.7 %copy-start = (bf16[128,9216]{1,0:T(8,128)(2,1)S(1)}, bf16[128,9216]{1,0:T(8,128)(2,1)}, u32[]{:S(2)}) copy-start(bf16[128,9216]{1,0:T(8,128)(2,1)} %refs_5_.1) | copy-start | bytes 7077892
  6.7 1.4 %copy-start.2 = (bf16[8,128,1152]{2,1,0:T(8,128)(2,1)}, bf16[8,128,1152]{2,1,0:T(8,128)(2,1)S(1)}, u32[]{:S(2)}) copy-start(bf16[8,128,1152]{2,1,0:T(8,128)(2,1)S(1)} %pack_heads.1) | copy-start | bytes 7077892
  8.2 51.1 %all-to-all-start = ((bf16[8,128,1152]{2,1,0:T(8,128)(2,1)}), bf16[8,128,1152]{2,1,0:T(8,128)(2,1)S(1)}, u32[]{:S(2)}, u32[]{:S(2)}) async-start(bf16[8,128,1152]{2,1,0:T(8,128)(2,1)} %copy-done.2), calls=%async_computation | async-start | bytes 4718592 | tf_op jit(solution)/shard_map/all_to_all | solution.py:366
  13.4 12.7 %collective-permute-start.14 = (bf16[2,512,128]{2,1,0:T(8,128)(2,1)S(1)}, bf16[2,512,128]{2,1,0:T(8,128)(2,1)S(1)}, u32[]{:S(2)}, u32[]{:S(2)}) collective-permute-start(bf16[2,512,128]{2,1,0:T(8,128)(2,1)S(1)} %pad_maximum_fusion.3), channel_id=1, source_target_pairs={{8,0},{12,4},{16,8},{20,12},{24,16},{28,20},{9,1},{13,5},{17,9},{2... | collective-permute-start | bytes 786440 | tf_op jit(solution)/shard_map/ppermute | solution.py:385
  15.5 13.9 %collective-permute-start.13 = (bf16[2,512,128]{2,1,0:T(8,128)(2,1)S(1)}, bf16[2,512,128]{2,1,0:T(8,128)(2,1)S(1)}, u32[]{:S(2)}, u32[]{:S(2)}) collective-permute-start(bf16[2,512,128]{2,1,0:T(8,128)(2,1)S(1)} %pad_maximum_fusion.3), channel_id=1, source_target_pairs={{0,8},{4,12},{8,16},{12,20},{16,24},{20,28},{1,9},{5,13},{9,17},{1... | collective-permute-start | bytes 786440 | tf_op jit(solution)/shard_map/ppermute | solution.py:384
  18.8 14.1 %collective-permute-start.2 = (bf16[2,512,128]{2,1,0:T(8,128)(2,1)S(1)}, bf16[2,512,128]{2,1,0:T(8,128)(2,1)S(1)}, u32[]{:S(2)}, u32[]{:S(2)}) collective-permute-start(bf16[2,512,128]{2,1,0:T(8,128)(2,1)S(1)} %pad_maximum_fusion.1), channel_id=1, source_target_pairs={{8,0},{12,4},{16,8},{20,12},{24,16},{28,20},{9,1},{13,5},{17,9},{2... | collective-permute-start | bytes 786440 | tf_op jit(solution)/shard_map/ppermute | solution.py:385
  20.8 14.9 %collective-permute-start.1 = (bf16[2,512,128]{2,1,0:T(8,128)(2,1)S(1)}, bf16[2,512,128]{2,1,0:T(8,128)(2,1)S(1)}, u32[]{:S(2)}, u32[]{:S(2)}) collective-permute-start(bf16[2,512,128]{2,1,0:T(8,128)(2,1)S(1)} %pad_maximum_fusion.1), channel_id=1, source_target_pairs={{0,8},{4,12},{8,16},{12,20},{16,24},{20,28},{1,9},{5,13},{9,17},{1... | collective-permute-start | bytes 786440 | tf_op jit(solution)/shard_map/ppermute | solution.py:384
  24.1 14.2 %collective-permute-start.8 = (bf16[2,512,128]{2,1,0:T(8,128)(2,1)S(1)}, bf16[2,512,128]{2,1,0:T(8,128)(2,1)S(1)}, u32[]{:S(2)}, u32[]{:S(2)}) collective-permute-start(bf16[2,512,128]{2,1,0:T(8,128)(2,1)S(1)} %pad_maximum_fusion.2), channel_id=1, source_target_pairs={{8,0},{12,4},{16,8},{20,12},{24,16},{28,20},{9,1},{13,5},{17,9},{2... | collective-permute-start | bytes 786440 | tf_op jit(solution)/shard_map/ppermute | solution.py:385
  26.2 14.8 %collective-permute-start.7 = (bf16[2,512,128]{2,1,0:T(8,128)(2,1)S(1)}, bf16[2,512,128]{2,1,0:T(8,128)(2,1)}, u32[]{:S(2)}, u32[]{:S(2)}) collective-permute-start(bf16[2,512,128]{2,1,0:T(8,128)(2,1)S(1)} %pad_maximum_fusion.2), channel_id=1, source_target_pairs={{0,8},{4,12},{8,16},{12,20},{16,24},{20,28},{1,9},{5,13},{9,17},{1... | collective-permute-start | bytes 786440 | tf_op jit(solution)/shard_map/ppermute | solution.py:384
  29.4 16.4 %collective-permute-start.15 = (bf16[2,512,128]{2,1,0:T(8,128)(2,1)S(1)}, bf16[2,512,128]{2,1,0:T(8,128)(2,1)}, u32[]{:S(2)}, u32[]{:S(2)}) collective-permute-start(bf16[2,512,128]{2,1,0:T(8,128)(2,1)S(1)} %collective-permute-done.14.refs_10_), channel_id=1, source_target_pairs={{8,0},{12,4},{16,8},{20,12},{9,1},{13,5},{17,9},{21,13},{10,2},{14... | collective-permute-start | bytes 786440 | tf_op jit(solution)/shard_map/ppermute | solution.py:385
  32.9 14.9 %collective-permute-start.3 = (bf16[2,512,128]{2,1,0:T(8,128)(2,1)S(1)}, bf16[2,512,128]{2,1,0:T(8,128)(2,1)}, u32[]{:S(2)}, u32[]{:S(2)}) collective-permute-start(bf16[2,512,128]{2,1,0:T(8,128)(2,1)S(1)} %collective-permute-done.2.refs_10_), channel_id=1, source_target_pairs={{8,0},{12,4},{16,8},{20,12},{9,1},{13,5},{17,9},{21,13},{10,2},{14... | collective-permute-start | bytes 786440 | tf_op jit(solution)/shard_map/ppermute | solution.py:385
  35.7 13.4 %collective-permute-start.5 = (bf16[2,512,128]{2,1,0:T(8,128)(2,1)S(1)}, bf16[2,512,128]{2,1,0:T(8,128)(2,1)}, u32[]{:S(2)}, u32[]{:S(2)}) collective-permute-start(bf16[2,512,128]{2,1,0:T(8,128)(2,1)S(1)} %collective-permute-done.1.refs_5_), channel_id=1, source_target_pairs={{8,16},{12,20},{16,24},{20,28},{9,17},{13,21},{17,25},{21,29},{10,... | collective-permute-start | bytes 786440 | tf_op jit(solution)/shard_map/ppermute | solution.py:384
  38.4 12.8 %collective-permute-start.17 = (bf16[2,512,128]{2,1,0:T(8,128)(2,1)S(1)}, bf16[2,512,128]{2,1,0:T(8,128)(2,1)}, u32[]{:S(2)}, u32[]{:S(2)}) collective-permute-start(bf16[2,512,128]{2,1,0:T(8,128)(2,1)S(1)} %collective-permute-done.13.refs_5_), channel_id=1, source_target_pairs={{8,16},{12,20},{16,24},{20,28},{9,17},{13,21},{17,25},{21,29},{10,... | collective-permute-start | bytes 786440 | tf_op jit(solution)/shard_map/ppermute | solution.py:384
  41.0 11.5 %collective-permute-start.9 = (bf16[2,512,128]{2,1,0:T(8,128)(2,1)S(1)}, bf16[2,512,128]{2,1,0:T(8,128)(2,1)S(1)}, u32[]{:S(2)}, u32[]{:S(2)}) collective-permute-start(bf16[2,512,128]{2,1,0:T(8,128)(2,1)S(1)} %collective-permute-done.8.refs_10_), channel_id=1, source_target_pairs={{8,0},{12,4},{16,8},{20,12},{9,1},{13,5},{17,9},{21,13},{10,2},{14... | collective-permute-start | bytes 786440 | tf_op jit(solution)/shard_map/ppermute | solution.py:385
  45.8 9.4 %collective-permute-start.11 = (bf16[2,512,128]{2,1,0:T(8,128)(2,1)}, bf16[2,512,128]{2,1,0:T(8,128)(2,1)}, u32[]{:S(2)}, u32[]{:S(2)}) collective-permute-start(bf16[2,512,128]{2,1,0:T(8,128)(2,1)} %collective-permute-done.7.refs_5_), channel_id=1, source_target_pairs={{8,16},{12,20},{16,24},{20,28},{9,17},{13,21},{17,25},{21,29},{10,... | collective-permute-start | bytes 786440 | tf_op jit(solution)/shard_map/ppermute | solution.py:384
  47.8 8.8 %collective-permute-start.4 = (bf16[2,512,128]{2,1,0:T(8,128)(2,1)}, bf16[2,512,128]{2,1,0:T(8,128)(2,1)}, u32[]{:S(2)}, u32[]{:S(2)}) collective-permute-start(bf16[2,512,128]{2,1,0:T(8,128)(2,1)} %collective-permute-done.3.refs_8_), channel_id=1, source_target_pairs={{8,0},{12,4},{9,1},{13,5},{10,2},{14,6},{11,3},{15,7}} | collective-permute-start | bytes 786440 | tf_op jit(solution)/shard_map/ppermute | solution.py:385
  49.1 10.1 %collective-permute-start.6 = (bf16[2,512,128]{2,1,0:T(8,128)(2,1)}, bf16[2,512,128]{2,1,0:T(8,128)(2,1)}, u32[]{:S(2)}, u32[]{:S(2)}) collective-permute-start(bf16[2,512,128]{2,1,0:T(8,128)(2,1)} %collective-permute-done.5.refs_7_), channel_id=1, source_target_pairs={{16,24},{20,28},{17,25},{21,29},{18,26},{22,30},{19,27},{23,31}} | collective-permute-start | bytes 786440 | tf_op jit(solution)/shard_map/ppermute | solution.py:384
  51.1 24.8 %collective-permute-start.16 = (bf16[2,512,128]{2,1,0:T(8,128)(2,1)}, bf16[2,512,128]{2,1,0:T(8,128)(2,1)}, u32[]{:S(2)}, u32[]{:S(2)}) collective-permute-start(bf16[2,512,128]{2,1,0:T(8,128)(2,1)} %collective-permute-done.15.refs_8_), channel_id=1, source_target_pairs={{8,0},{12,4},{9,1},{13,5},{10,2},{14,6},{11,3},{15,7}} | collective-permute-start | bytes 786440 | tf_op jit(solution)/shard_map/ppermute | solution.py:385
  53.2 22.8 %collective-permute-start.18 = (bf16[2,512,128]{2,1,0:T(8,128)(2,1)}, bf16[2,512,128]{2,1,0:T(8,128)(2,1)}, u32[]{:S(2)}, u32[]{:S(2)}) collective-permute-start(bf16[2,512,128]{2,1,0:T(8,128)(2,1)} %collective-permute-done.17.refs_7_), channel_id=1, source_target_pairs={{16,24},{20,28},{17,25},{21,29},{18,26},{22,30},{19,27},{23,31}} | collective-permute-start | bytes 786440 | tf_op jit(solution)/shard_map/ppermute | solution.py:384
  55.2 28.6 %collective-permute-start.10 = (bf16[2,512,128]{2,1,0:T(8,128)(2,1)}, bf16[2,512,128]{2,1,0:T(8,128)(2,1)}, u32[]{:S(2)}, u32[]{:S(2)}) collective-permute-start(bf16[2,512,128]{2,1,0:T(8,128)(2,1)} %copy-done.14), channel_id=1, source_target_pairs={{8,0},{12,4},{9,1},{13,5},{10,2},{14,6},{11,3},{15,7}} | collective-permute-start | bytes 786440 | tf_op jit(solution)/shard_map/ppermute | solution.py:385
  56.6 27.3 %collective-permute-start.12 = (bf16[2,512,128]{2,1,0:T(8,128)(2,1)}, bf16[2,512,128]{2,1,0:T(8,128)(2,1)}, u32[]{:S(2)}, u32[]{:S(2)}) collective-permute-start(bf16[2,512,128]{2,1,0:T(8,128)(2,1)} %collective-permute-done.11.refs_7_), channel_id=1, source_target_pairs={{16,24},{20,28},{17,25},{21,29},{18,26},{22,30},{19,27},{23,31}} | collective-permute-start | bytes 786440 | tf_op jit(solution)/shard_map/ppermute | solution.py:384
  59.3 1.0 copy-start.11
  66.8 23.8 %all-to-all-start.1 = ((bf16[8,128,128]{2,1,0:T(8,128)(2,1)}), bf16[8,128,128]{2,1,0:T(8,128)(2,1)S(1)}, u32[]{:S(2)}, u32[]{:S(2)}) async-start(bf16[8,128,128]{2,1,0:T(8,128)(2,1)} %copy-done.4), calls=%async_computation.1 | async-start | bytes 524288 | tf_op jit(solution)/shard_map/all_to_all | solution.py:366
  76.0 1.0 copy-start.7
  76.9 0.9 copy-start.9
  77.9 6.0 %copy-start.13 = (bf16[2,512,128]{2,1,0:T(8,128)(2,1)S(1)}, bf16[2,512,128]{2,1,0:T(8,128)(2,1)}, u32[]{:S(2)}) copy-start(bf16[2,512,128]{2,1,0:T(8,128)(2,1)} %copy-done.12) | copy-start | bytes 786436
  77.9 6.0 %copy-start.15 = (bf16[2,512,128]{2,1,0:T(8,128)(2,1)S(1)}, bf16[2,512,128]{2,1,0:T(8,128)(2,1)}, u32[]{:S(2)}) copy-start(bf16[2,512,128]{2,1,0:T(8,128)(2,1)} %copy-done.14) | copy-start | bytes 786436
  103.9 9.6 %collective-permute-start.19 = (bf16[64,3072]{1,0:T(8,128)(2,1)S(1)}, bf16[64,3072]{1,0:T(8,128)(2,1)S(1)}, u32[]{:S(2)}, u32[]{:S(2)}) collective-permute-start(bf16[64,3072]{1,0:T(8,128)(2,1)S(1)} %unpack_text.1), channel_id=1, source_target_pairs={{0,4},{4,0},{8,12},{12,8},{16,20},{20,16},{24,28},{28,24},{1,5},{5... | collective-permute-start | bytes 1179656 | tf_op jit(solution)/shard_map/ppermute | solution.py:408
  104.3 5.1 %copy-start.5 = (bf16[64,3072]{1,0:T(8,128)(2,1)S(1)}, bf16[64,3072]{1,0:T(8,128)(2,1)}, u32[]{:S(2)}) copy-start(bf16[64,3072]{1,0:T(8,128)(2,1)} %refs_2_.3) | copy-start | bytes 1179652
  104.3 5.2 %copy-start.16 = (f32[3072]{0:T(1024)S(1)}, f32[3072]{0:T(1024)}, u32[]{:S(2)}) copy-start(f32[3072]{0:T(1024)} %param.10) | copy-start | bytes 36868
  (7 other events, 5.0 us)

commit v5 on v4

--- a/solution.py
+++ b/solution.py
@@ -10,7 +10,7 @@
 
 HD = 128
 SCALE = math.log2(math.e) / math.sqrt(HD)
-VMEM_LIMIT = 24 * 1024 * 1024
+VMEM_LIMIT = 16 * 1024 * 1024
 WIDE_LIMIT = 48 * 1024 * 1024
 TILE = 256
 LARGE = 2.0**60
@@ -22,44 +22,43 @@
     )
 
 
-def pack_body(info, *refs):
-    sources, packed = refs[:6], refs[-1]
-    first = 0
-    for group in (sources[:3], sources[3:]):
-        rows, width = group[0].shape
-        for part, source in enumerate(group):
-            packed[0, first : first + rows, part * width : (part + 1) * width] = source[...]
-        first += rows
-
-
-def pack(core, img_qkv, txt_qkv, text_rows, destinations, column_block, width, after):
-    img_rows = img_qkv.shape[0]
-    blocks = img_qkv.shape[1] // 3 // width
-
-    def source(rows, part, by_core):
-        def place(d, info):
-            return (info[0] if by_core else 0, part * blocks + column_block(d))
-
-        return pl.BlockSpec((rows, width), place)
-
+def pack_body(text_rows, places, width, core, img, txt, packed, sem):
+    img_rows, model = img.shape[0], img.shape[1] // 3
+    first = pl.multiple_of(core[0] * text_rows, text_rows)
+    copies = []
+    for destination, place in enumerate(places):
+        for part in range(3):
+            source = pl.ds(part * model + place * width, width)
+            target = pl.ds(part * width, width)
+            copies.append((img.at[:, source], packed.at[destination, pl.ds(0, img_rows), target]))
+            copies.append(
+                (
+                    txt.at[pl.ds(first, text_rows), source],
+                    packed.at[destination, pl.ds(img_rows, text_rows), target],
+                )
+            )
+    copies = [
+        pltpu.make_async_copy(source, target, sem.at[index])
+        for index, (source, target) in enumerate(copies)
+    ]
+    for copy in copies:
+        copy.start()
+    for copy in copies:
+        copy.wait()
+
+
+def pack(core, img_qkv, txt_qkv, text_rows, places, width):
+    rows = img_qkv.shape[0] + text_rows
+    anywhere = pl.BlockSpec(memory_space=pl.ANY)
     return pl.pallas_call(
-        pack_body,
-        grid_spec=pltpu.PrefetchScalarGridSpec(
-            num_scalar_prefetch=1,
-            grid=(destinations,),
-            in_specs=[source(img_rows, part, False) for part in range(3)]
-            + [source(text_rows, part, True) for part in range(3)]
-            + [pl.BlockSpec(memory_space=pl.ANY)] * len(after),
-            out_specs=pl.BlockSpec(
-                (1, img_rows + text_rows, 3 * width), lambda d, info: (d, 0, 0)
-            ),
-        ),
-        out_shape=jax.ShapeDtypeStruct(
-            (destinations, img_rows + text_rows, 3 * width), img_qkv.dtype
-        ),
-        compiler_params=params(),
+        functools.partial(pack_body, text_rows, places, width),
+        in_specs=[pl.BlockSpec(memory_space=pltpu.SMEM), anywhere, anywhere],
+        out_specs=anywhere,
+        out_shape=jax.ShapeDtypeStruct((len(places), rows, 3 * width), img_qkv.dtype),
+        scratch_shapes=[pltpu.SemaphoreType.DMA((6 * len(places),))],
+        compiler_params=pltpu.CompilerParams(vmem_limit_bytes=WIDE_LIMIT),
         name="pack_heads",
-    )(core, img_qkv, img_qkv, img_qkv, txt_qkv, txt_qkv, txt_qkv, *after)
+    )(core, img_qkv, txt_qkv)
 
 
 def dot(first, second, contract):
@@ -105,11 +104,12 @@
             flag[0] = jnp.where(jnp.max(total[:, HD:]) > LARGE, 1, 0).astype(jnp.int32)
 
 
-def head_body(pair, img_rows, others, has_earlier, info, *refs):
+def head_body(pair, img_rows, others, untouched, info, *refs):
     q_ref, k_ref, v_ref = refs[:3]
     stale = refs[3 : 3 + pair]
     candidates = refs[3 + pair : 3 + pair + 2 * others]
-    out, arrived, aug, total, flag = refs[3 + pair + 2 * others + has_earlier :]
+    out = refs[3 + pair + 2 * others + untouched]
+    arrived, aug, total, flag = refs[-4:]
     for index in range(others):
         from_left = info[1 + index] == 1
         arrived[index] = jnp.where(
@@ -205,7 +205,7 @@
     )
 
 
-def attend_head(info, qkv, img_rows, stale, arrived, head, place, places, earlier=None):
+def attend_head(info, qkv, img_rows, stale, arrived, head, place, places, earlier=None, passing=()):
     heads = qkv.shape[2] // (3 * HD)
     others = len(arrived)
     block_shape = arrived[0][0].shape
@@ -227,15 +227,21 @@
     if earlier is not None:
         aliases = {1 + len(operands): 0}
         operands.append(earlier)
-        in_specs.append(pl.BlockSpec(memory_space=pl.ANY))
+    for index, array in enumerate(passing):
+        aliases[1 + len(operands)] = 1 + index
+        operands.append(array)
+    untouched = len(operands) - len(in_specs)
+    anywhere = pl.BlockSpec(memory_space=pl.ANY)
+    in_specs += [anywhere] * untouched
     keys = others * block_shape[1] + rows
     return pl.pallas_call(
-        functools.partial(head_body, len(stale), img_rows, others, int(earlier is not None)),
+        functools.partial(head_body, len(stale), img_rows, others, untouched),
         grid_spec=pltpu.PrefetchScalarGridSpec(
             num_scalar_prefetch=1,
             grid=(1,),
             in_specs=in_specs,
-            out_specs=pl.BlockSpec(qkv.shape[:2] + (HD,), lambda n, info: (0, 0, place)),
+            out_specs=[pl.BlockSpec(qkv.shape[:2] + (HD,), lambda n, info: (0, 0, place))]
+            + [anywhere] * len(passing),
             scratch_shapes=[
                 pltpu.VMEM((others,) + block_shape, qkv.dtype),
                 pltpu.VMEM((rows, HD), jnp.bfloat16),
@@ -243,12 +249,228 @@
                 pltpu.SMEM((1,), jnp.int32),
             ],
         ),
-        out_shape=jax.ShapeDtypeStruct(qkv.shape[:2] + (places * HD,), qkv.dtype),
+        out_shape=[jax.ShapeDtypeStruct(qkv.shape[:2] + (places * HD,), qkv.dtype)]
+        + [jax.ShapeDtypeStruct(array.shape, array.dtype) for array in passing],
         input_output_aliases=aliases,
         compiler_params=params(),
         cost_estimate=attend_cost(rows, keys, 1),
         name="attend_head",
     )(info, *operands)
+
+
+def most_body(pair, img_rows, sides, info, *refs):
+    q_ref, k_ref, v_ref = refs[:3]
+    stale = refs[3 : 3 + pair]
+    arrived = refs[3 + pair : 3 + pair + sides]
+    aug_out, total_out, flag = refs[4 + pair + sides :]
+    aug, total = aug_out.at[0], total_out.at[0]
+    core = info[0]
+    k_img, k_txt = split_rows(k_ref[...], img_rows)
+    v_img, v_txt = split_rows(v_ref[...], img_rows)
+    q_img, q_txt = split_rows(q_ref[...], img_rows)
+    fresh_rows = q_img.shape[0]
+    group_rows = fresh_rows // pair
+    rows = fresh_rows + q_txt.shape[0]
+
+    def queries_at(span):
+        if span.stop <= fresh_rows:
+            return q_img[span, :]
+        return q_txt[span.start - fresh_rows : span.stop - fresh_rows, :]
+
+    def own_sets():
+        sets = []
+        for group in range(pair):
+            span = slice(group * group_rows, (group + 1) * group_rows)
+            key_rows, values = [k_txt, k_img[span, :]], [v_txt, v_img[span, :]]
+            if pair == 2:
+                mine = core == group
+                key_rows.append(jnp.where(mine, stale[1][0], stale[0][0]))
+                values.append(jnp.where(mine, stale[1][1], stale[0][1]))
+            sets.append((span, key_rows, values))
+        sets.append(
+            (
+                slice(fresh_rows, rows),
+                [k_txt] + [block[0] for block in stale],
+                [v_txt] + [block[1] for block in stale],
+            )
+        )
+        for span, key_rows, values in sets:
+            key_rows, values = jnp.concatenate(key_rows, 0), jnp.concatenate(values, 0)
+            spans = [
+                slice(span.start + t.start, span.start + t.stop)
+                for t in tiles_of(span.stop - span.start)
+            ]
+            yield spans, key_rows, values
+
+    def each_arrived(act):
+        for side in range(sides):
+            block = arrived[side]
+
+            @pl.when(info[1 + side] == 1)
+            def _():
+                key_rows, values = block[0], block[1]
+                for first in range(0, rows, fresh_rows):
+                    for tile in tiles_of(min(fresh_rows, rows - first)):
+                        act(slice(first + tile.start, first + tile.stop), key_rows, values)
+
+    def largest(span, key_rows):
+        return jnp.max(dot(queries_at(span), key_rows, (1, 1)), axis=1, keepdims=True)
+
+    def attempt(turn):
+        @pl.when(turn == 0)
+        def _():
+            for spans, key_rows, _ in own_sets():
+                for span in spans:
+                    aug[span, :] = reference_columns(
+                        largest(span, key_rows[: min(256, key_rows.shape[0]), :])
+                    )
+
+        @pl.when(turn == 1)
+        def _():
+            def raise_to(span, key_rows, _):
+                total[span, :] = jnp.maximum(
+                    total[span, :], jnp.broadcast_to(largest(span, key_rows), total[span, :].shape)
+                )
+
+            for spans, key_rows, _ in own_sets():
+                for span in spans:
+                    total[span, :] = jnp.broadcast_to(
+                        largest(span, key_rows), total[span, :].shape
+                    )
+            each_arrived(raise_to)
+            for spans, _, _ in own_sets():
+                for span in spans:
+                    aug[span, :] = reference_columns(total[span, :1])
+
+        def queries_of(span):
+            return jnp.concatenate([queries_at(span), aug[span, :]], axis=1)
+
+        def add(span, key_rows, values):
+            total[span, :] += weighted(queries_of(span), with_ones(key_rows), with_ones(values))
+
+        for spans, key_rows, values in own_sets():
+            key_rows, values = with_ones(key_rows), with_ones(values)
+            for span in spans:
+                total[span, :] = weighted(queries_of(span), key_rows, values)
+        each_arrived(add)
+
+    until_small(flag, total, attempt)
+
+
+def one_spec(shape, block=0):
+    return pl.BlockSpec(
+        shape, lambda n, info: (0, 0, block), pipeline_mode=pl.Buffered(buffer_count=1)
+    )
+
+
+def attend_most(info, qkv, img_rows, stale, arrived, head, after):
+    heads = qkv.shape[2] // (3 * HD)
+    rows = qkv.shape[0] * qkv.shape[1]
+    shapes = [
+        jax.ShapeDtypeStruct((1, rows, HD), jnp.bfloat16),
+        jax.ShapeDtypeStruct((1, rows, 2 * HD), jnp.float32),
+    ]
+    in_specs = [one_spec(qkv.shape[:2] + (HD,), part * heads + head) for part in range(3)]
+    in_specs += [one_spec(block.shape[:2] + (HD,), head) for block in stale]
+    in_specs += [one_spec(block.shape) for block in arrived]
+    in_specs += [pl.BlockSpec(memory_space=pl.ANY)]
+    keys = sum(block.shape[1] for block in arrived) // 2 + rows
+    return pl.pallas_call(
+        functools.partial(most_body, len(stale), img_rows, len(arrived)),
+        grid_spec=pltpu.PrefetchScalarGridSpec(
+            num_scalar_prefetch=1,
+            grid=(1,),
+            in_specs=in_specs,
+            out_specs=[one_spec(shape.shape) for shape in shapes],
+            scratch_shapes=[pltpu.SMEM((1,), jnp.int32)],
+        ),
+        out_shape=shapes,
+        compiler_params=params(),
+        cost_estimate=attend_cost(rows, keys, 1),
+        name="attend_most",
+    )(info, *[qkv] * 3, *stale, *arrived, after)
+
+
+def last_body(img_rows, sides, info, *refs):
+    q_ref, aug_ref, total_ref = refs[:3]
+    arrived = refs[3 : 3 + sides]
+    out, total, shift, flag = refs[3 + sides :]
+    q_img, q_txt = split_rows(q_ref[...], img_rows)
+    fresh_rows = q_img.shape[0]
+    rows = total.shape[0]
+
+    def queries_at(span):
+        if span.stop <= fresh_rows:
+            queries = q_img[span, :]
+        else:
+            queries = q_txt[span.start - fresh_rows : span.stop - fresh_rows, :]
+        return jnp.concatenate([queries, aug_ref[0, span, :]], axis=1)
+
+    def each_arrived(act):
+        for side in range(sides):
+            block = arrived[side]
+
+            @pl.when(info[1 + side] == 1)
+            def _():
+                key_rows, values = with_ones(block[0]), with_ones(block[1])
+                for first, last in ((0, fresh_rows), (fresh_rows, rows)):
+                    for tile in tiles_of(last - first):
+                        act(slice(first + tile.start, first + tile.stop), key_rows, values)
+
+    def add(span, key_rows, values):
+        total[span, :] += weighted(queries_at(span), key_rows, values)
+
+    def raise_to(span, key_rows, _):
+        above = jnp.max(dot(queries_at(span), key_rows, (1, 1)), axis=1, keepdims=True)
+        shift[span, :] = jnp.maximum(shift[span, :], jnp.broadcast_to(above, shift[span, :].shape))
+
+    def add_shifted(span, key_rows, values):
+        scores = dot(queries_at(span), key_rows, (1, 1)) - shift[span, :1]
+        total[span, :] += dot(jnp.exp2(scores * SCALE).astype(jnp.bfloat16), values, (1, 0))
+
+    def attempt(turn):
+        @pl.when(turn == 0)
+        def _():
+            total[...] = total_ref[0]
+            each_arrived(add)
+
+        @pl.when(turn == 1)
+        def _():
+            shift[...] = jnp.zeros_like(shift)
+            each_arrived(raise_to)
+            keep = jnp.exp2(shift[...] * -SCALE)
+            total[...] = total_ref[0] * jnp.concatenate([keep, keep], axis=1)
+            each_arrived(add_shifted)
+
+    until_small(flag, total, attempt)
+    attended = (total[:, :HD] / total[:, HD:]).astype(out.dtype)
+    destinations = out.shape[0]
+    out[:, :img_rows, :] = attended[:fresh_rows].reshape(destinations, img_rows, HD)
+    out[:, img_rows:, :] = attended[fresh_rows:].reshape(destinations, -1, HD)
+
+
+def attend_last(info, qkv, img_rows, state, arrived, head):
+    rows = qkv.shape[0] * qkv.shape[1]
+    return pl.pallas_call(
+        functools.partial(last_body, img_rows, len(arrived)),
+        grid_spec=pltpu.PrefetchScalarGridSpec(
+            num_scalar_prefetch=1,
+            grid=(1,),
+            in_specs=[one_spec(qkv.shape[:2] + (HD,), head)]
+            + [one_spec(part.shape) for part in state]
+            + [one_spec(block.shape) for block in arrived],
+            out_specs=one_spec(qkv.shape[:2] + (HD,)),
+            scratch_shapes=[
+                pltpu.VMEM((rows, 2 * HD), jnp.float32),
+                pltpu.VMEM((rows, HD), jnp.float32),
+                pltpu.SMEM((1,), jnp.int32),
+            ],
+        ),
+        out_shape=jax.ShapeDtypeStruct(qkv.shape[:2] + (HD,), qkv.dtype),
+        compiler_params=params(),
+        cost_estimate=attend_cost(rows, arrived[0].shape[1], 1),
+        name="attend_last",
+    )(info, qkv, *state, *arrived)
 
 
 def project_body(order, first_head, heads, group, last, *refs):
@@ -362,6 +584,7 @@
 
     order = [column_block(d) for d in range(destinations)]
     groups = [[g * destinations + d for d in range(destinations)] for g in range(planes)]
+
     def exchange(x):
         return lax.all_to_all(
             x, ("patch", "head"), split_axis=0, concat_axis=0, axis_index_groups=groups, tiled=True
@@ -373,35 +596,44 @@
         theirs = lax.dynamic_slice_in_dim(stale_kv, (1 - core) * width, width, 2)
         stale.append(lax.ppermute(theirs, "patch", swap_pairs))
 
-    arrived = []
+    core_only = core.astype(jnp.int32).reshape(1)
+    qkv = exchange(pack(core_only, img_qkv, txt_qkv, text_rows, order, width))
+
+    def relay(left, right, step):
+        right_pairs = [(p, p + pair) for p in range((step - 1) * pair, patches - pair)]
+        left_pairs = [(p + pair, p) for p in range(0, patches - step * pair)]
+        return lax.ppermute(left, "patch", right_pairs), lax.ppermute(right, "patch", left_pairs)
+
+    came = []
     for head in range(heads):
-        columns_of = [block[:, :, head * HD : (head + 1) * HD] for block in stale]
-        from_left = from_right = jnp.concatenate(columns_of, axis=1)
-        left, right = [], []
-        for step in range(1, planes):
-            right_pairs = [(p, p + pair) for p in range((step - 1) * pair, patches - pair)]
-            left_pairs = [(p + pair, p) for p in range(0, patches - step * pair)]
-            from_left = lax.ppermute(from_left, "patch", right_pairs)
-            from_right = lax.ppermute(from_right, "patch", left_pairs)
-            left.append(from_left)
-            right.append(from_right)
-        arrived.append(list(zip(left, reversed(right))))
-
-    core_only = core.astype(jnp.int32).reshape(1)
-    qkv = exchange(
-        pack(core_only, img_qkv, txt_qkv, text_rows, destinations, column_block, width, stale[1:])
-    )
-
-    info = jnp.stack([core] + [plane >= step for step in range(1, planes)])
-    info = info.astype(jnp.int32)
+        own = jnp.concatenate([block[:, :, head * HD : (head + 1) * HD] for block in stale], axis=1)
+        steps, held = [], (own, own)
+        for step in range(1, planes - (head == heads - 1)):
+            held = relay(*held, step)
+            steps.append(held)
+        came.append(steps)
+
+    info = jnp.stack([core] + [plane >= step for step in range(1, planes)]).astype(jnp.int32)
     early = None
     for head in range(heads - 1):
-        early = attend_head(
-            info, qkv, img_rows, stale, arrived[head], head, head, heads - 1, early
-        )
+        left, right = zip(*came[head])
+        arrived = list(zip(left, reversed(right)))
+        passing = came[-1][-1] if head == 0 else ()
+        early, *passed = attend_head(
+            info, qkv, img_rows, stale, arrived, head, head, heads - 1, early, passing
+        )
+        if passing:
+            came[-1][-1] = tuple(passed)
+    last = relay(*came[-1][-1], planes - 1)
+    there = [(plane >= step, plane + step < planes) for step in range(1, planes)]
+    info = jnp.stack([core] + [flag for both in there[:-1] for flag in both]).astype(jnp.int32)
+    state = attend_most(
+        info, qkv, img_rows, stale, [block for both in came[-1] for block in both], heads - 1, early
+    )
+    info = jnp.stack([core, *there[-1]]).astype(jnp.int32)
+    late = exchange(attend_last(info, qkv, img_rows, state, last, heads - 1))
+    early = exchange(early)
     weight = proj_weight.reshape(destinations, heads, HD, model)
-    early = exchange(early)
-    late = exchange(attend_head(info, qkv, img_rows, stale, arrived[-1], heads - 1, 0, 1))
 
     text_out = unpack_text([early, late], order, img_rows)
     if pair == 2:

time: 117 us -> 125 us (1.068)
  the two profiles are of different devices: /device:TPU:17 before, /device:TPU:0 now
where the time goes in v5:
time: 125 us; the launch traced here: 124 us
  starting transfers between devices  42.7 us (34%)
  Pallas kernels  32.6 us (26%)
  waiting for transfers between devices  21.5 us (17%)
  local copies, waits for them, and re-layouts  15 us (12%)
  blocking collectives  10.2 us (8%)
    ppermute x9, waiting for transfers between devices, relay(): lax.ppermute(right, 'patch', left_pairs)  21.2 us
    ppermute x9, starting transfers between devices, relay(): lax.ppermute(left, 'patch', right_pairs)  20.8 us
    unnamed x34, local copies, waits for them, and re-layouts  12.6 us
    pallas_call x2, Pallas kernels, attend_head(): pl.pallas_call(functools.partial(head_body, len(stale), img_rows, others,...  11.9 us
    ppermute x9, starting transfers between devices, relay(): lax.ppermute(right, 'patch', left_pairs)  11.8 us
    all_to_all x1, blocking collectives, exchange(): lax.all_to_all(x, ('patch', 'head'), split_axis=0, concat_axis=0, axis_in...  10.2 us
    pallas_call x2, Pallas kernels, project(): pl.pallas_call(functools.partial(project_body, order, first_head, heads,...  10.2 us
    all_to_all x2, starting transfers between devices, exchange(): lax.all_to_all(x, ('patch', 'head'), split_axis=0, concat_axis=0, axis_in...  9.31 us
  transfers between devices with their start and end apart: 22, of which 7 were waited for; matrix products, arithmetic and copies ran while one was open for 2% of the time, Pallas kernels for 20%

profile of v5, /device:TPU:0, one launch (start us, length us, event | category | flops | bytes accessed | tf_op | source)
XLA Modules:
  0.0 124.3 jit_solution(3334161579266796526)
XLA Ops:
  0.7 1.7 %copy-done.3 = bf16[128,9216]{1,0:T(8,128)(2,1)S(1)} copy-done((bf16[128,9216]{1,0:T(8,128)(2,1)S(1)}, bf16[128,9216]{1,0:T(8,128)(2,1)}, u32[]{:S(2)}) %copy-start.3) | copy-done | bytes 2359320
  4.5 1.4 %copy-done = bf16[8,128,1152]{2,1,0:T(8,128)(2,1)} copy-done((bf16[8,128,1152]{2,1,0:T(8,128)(2,1)}, bf16[8,128,1152]{2,1,0:T(8,128)(2,1)S(1)}, u32[]{:S(2)}) %copy-start) | copy-done | bytes 2359320
  5.9 5.2 %all-to-all-start = ((bf16[8,128,1152]{2,1,0:T(8,128)(2,1)}), bf16[8,128,1152]{2,1,0:T(8,128)(2,1)S(1)}, u32[]{:S(2)}, u32[]{:S(2)}) async-start(bf16[8,128,1152]{2,1,0:T(8,128)(2,1)} %copy-done), calls=%async_computation | async-start | bytes 4718592 | tf_op jit(solution)/shard_map/all_to_all | solution.py:589
  14.3 3.5 %collective-permute-start.1 = (bf16[2,512,128]{2,1,0:T(8,128)(2,1)S(1)}, bf16[2,512,128]{2,1,0:T(8,128)(2,1)S(1)}, u32[]{:S(2)}, u32[]{:S(2)}) collective-permute-start(bf16[2,512,128]{2,1,0:T(8,128)(2,1)S(1)} %pad_maximum_fusion.1), channel_id=1, source_target_pairs={{0,8},{4,12},{8,16},{12,20},{16,24},{20,28},{1,9},{5,13},{9,17},{1... | collective-permute-start | bytes 786440 | tf_op jit(solution)/shard_map/ppermute | solution.py:605
  17.9 1.3 %collective-permute-start.4 = (bf16[2,512,128]{2,1,0:T(8,128)(2,1)S(1)}, bf16[2,512,128]{2,1,0:T(8,128)(2,1)S(1)}, u32[]{:S(2)}, u32[]{:S(2)}) collective-permute-start(bf16[2,512,128]{2,1,0:T(8,128)(2,1)S(1)} %pad_maximum_fusion.2), channel_id=1, source_target_pairs={{8,0},{12,4},{16,8},{20,12},{24,16},{28,20},{9,1},{13,5},{17,9},{2... | collective-permute-start | bytes 786440 | tf_op jit(solution)/shard_map/ppermute | solution.py:605
  19.2 4.6 %collective-permute-start.3 = (bf16[2,512,128]{2,1,0:T(8,128)(2,1)S(1)}, bf16[2,512,128]{2,1,0:T(8,128)(2,1)S(1)}, u32[]{:S(2)}, u32[]{:S(2)}) collective-permute-start(bf16[2,512,128]{2,1,0:T(8,128)(2,1)S(1)} %pad_maximum_fusion.2), channel_id=1, source_target_pairs={{0,8},{4,12},{8,16},{12,20},{16,24},{20,28},{1,9},{5,13},{9,17},{1... | collective-permute-start | bytes 786440 | tf_op jit(solution)/shard_map/ppermute | solution.py:605
  23.7 1.3 %collective-permute-start.2 = (bf16[2,512,128]{2,1,0:T(8,128)(2,1)S(1)}, bf16[2,512,128]{2,1,0:T(8,128)(2,1)}, u32[]{:S(2)}, u32[]{:S(2)}) collective-permute-start(bf16[2,512,128]{2,1,0:T(8,128)(2,1)S(1)} %pad_maximum_fusion.1), channel_id=1, source_target_pairs={{8,0},{12,4},{16,8},{20,12},{24,16},{28,20},{9,1},{13,5},{17,9},{2... | collective-permute-start | bytes 786440 | tf_op jit(solution)/shard_map/ppermute | solution.py:605
  25.1 1.3 %collective-permute-start.12 = (bf16[2,512,128]{2,1,0:T(8,128)(2,1)S(1)}, bf16[2,512,128]{2,1,0:T(8,128)(2,1)S(1)}, u32[]{:S(2)}, u32[]{:S(2)}) collective-permute-start(bf16[2,512,128]{2,1,0:T(8,128)(2,1)S(1)} %pad_maximum_fusion.3), channel_id=1, source_target_pairs={{8,0},{12,4},{16,8},{20,12},{24,16},{28,20},{9,1},{13,5},{17,9},{2... | collective-permute-start | bytes 786440 | tf_op jit(solution)/shard_map/ppermute | solution.py:605
  26.4 5.2 %collective-permute-start.11 = (bf16[2,512,128]{2,1,0:T(8,128)(2,1)S(1)}, bf16[2,512,128]{2,1,0:T(8,128)(2,1)S(1)}, u32[]{:S(2)}, u32[]{:S(2)}) collective-permute-start(bf16[2,512,128]{2,1,0:T(8,128)(2,1)S(1)} %pad_maximum_fusion.3), channel_id=1, source_target_pairs={{0,8},{4,12},{8,16},{12,20},{16,24},{20,28},{1,9},{5,13},{9,17},{1... | collective-permute-start | bytes 786440 | tf_op jit(solution)/shard_map/ppermute | solution.py:605
  31.6 1.3 %collective-permute-start.5 = (bf16[2,512,128]{2,1,0:T(8,128)(2,1)S(1)}, bf16[2,512,128]{2,1,0:T(8,128)(2,1)}, u32[]{:S(2)}, u32[]{:S(2)}) collective-permute-start(bf16[2,512,128]{2,1,0:T(8,128)(2,1)S(1)} %collective-permute-done.4.refs_10_), channel_id=1, source_target_pairs={{8,0},{12,4},{16,8},{20,12},{9,1},{13,5},{17,9},{21,13},{10,2},{14... | collective-permute-start | bytes 786440 | tf_op jit(solution)/shard_map/ppermute | solution.py:605
  33.6 1.4 %collective-permute-start.7 = (bf16[2,512,128]{2,1,0:T(8,128)(2,1)S(1)}, bf16[2,512,128]{2,1,0:T(8,128)(2,1)}, u32[]{:S(2)}, u32[]{:S(2)}) collective-permute-start(bf16[2,512,128]{2,1,0:T(8,128)(2,1)S(1)} %collective-permute-done.3.refs_5_), channel_id=1, source_target_pairs={{8,16},{12,20},{16,24},{20,28},{9,17},{13,21},{17,25},{21,29},{10,... | collective-permute-start | bytes 786440 | tf_op jit(solution)/shard_map/ppermute | solution.py:605
  37.1 3.4 %collective-permute-done.12.refs_10_ = bf16[2,512,128]{2,1,0:T(8,128)(2,1)S(1)} collective-permute-done((bf16[2,512,128]{2,1,0:T(8,128)(2,1)S(1)}, bf16[2,512,128]{2,1,0:T(8,128)(2,1)S(1)}, u32[]{:S(2)}, u32[]{:S(2)}) %collective-permute-start.12) | collective-permute-done | bytes 262176 | tf_op jit(solution)/shard_map/ppermute | solution.py:605
  40.5 1.3 %collective-permute-start.13 = (bf16[2,512,128]{2,1,0:T(8,128)(2,1)S(1)}, bf16[2,512,128]{2,1,0:T(8,128)(2,1)}, u32[]{:S(2)}, u32[]{:S(2)}) collective-permute-start(bf16[2,512,128]{2,1,0:T(8,128)(2,1)S(1)} %collective-permute-done.12.refs_10_), channel_id=1, source_target_pairs={{8,0},{12,4},{16,8},{20,12},{9,1},{13,5},{17,9},{21,13},{10,2},{14... | collective-permute-start | bytes 786440 | tf_op jit(solution)/shard_map/ppermute | solution.py:605
  42.5 1.4 %collective-permute-start.15 = (bf16[2,512,128]{2,1,0:T(8,128)(2,1)S(1)}, bf16[2,512,128]{2,1,0:T(8,128)(2,1)}, u32[]{:S(2)}, u32[]{:S(2)}) collective-permute-start(bf16[2,512,128]{2,1,0:T(8,128)(2,1)S(1)} %collective-permute-done.11.refs_5_), channel_id=1, source_target_pairs={{8,16},{12,20},{16,24},{20,28},{9,17},{13,21},{17,25},{21,29},{10,... | collective-permute-start | bytes 786440 | tf_op jit(solution)/shard_map/ppermute | solution.py:605
  46.3 1.3 %collective-permute-start.6 = (bf16[2,512,128]{2,1,0:T(8,128)(2,1)}, bf16[2,512,128]{2,1,0:T(8,128)(2,1)}, u32[]{:S(2)}, u32[]{:S(2)}) collective-permute-start(bf16[2,512,128]{2,1,0:T(8,128)(2,1)} %collective-permute-done.5.refs_8_), channel_id=1, source_target_pairs={{8,0},{12,4},{9,1},{13,5},{10,2},{14,6},{11,3},{15,7}} | collective-permute-start | bytes 786440 | tf_op jit(solution)/shard_map/ppermute | solution.py:605
  47.6 1.4 %collective-permute-start.8 = (bf16[2,512,128]{2,1,0:T(8,128)(2,1)}, bf16[2,512,128]{2,1,0:T(8,128)(2,1)}, u32[]{:S(2)}, u32[]{:S(2)}) collective-permute-start(bf16[2,512,128]{2,1,0:T(8,128)(2,1)} %collective-permute-done.7.refs_7_), channel_id=1, source_target_pairs={{16,24},{20,28},{17,25},{21,29},{18,26},{22,30},{19,27},{23,31}} | collective-permute-start | bytes 786440 | tf_op jit(solution)/shard_map/ppermute | solution.py:605
  49.0 1.9 %collective-permute-done.13.refs_8_ = bf16[2,512,128]{2,1,0:T(8,128)(2,1)} collective-permute-done((bf16[2,512,128]{2,1,0:T(8,128)(2,1)S(1)}, bf16[2,512,128]{2,1,0:T(8,128)(2,1)}, u32[]{:S(2)}, u32[]{:S(2)}) %collective-permute-start.13) | collective-permute-done | bytes 262176 | tf_op jit(solution)/shard_map/ppermute | solution.py:605
  50.9 1.3 %collective-permute-start.14 = (bf16[2,512,128]{2,1,0:T(8,128)(2,1)}, bf16[2,512,128]{2,1,0:T(8,128)(2,1)}, u32[]{:S(2)}, u32[]{:S(2)}) collective-permute-start(bf16[2,512,128]{2,1,0:T(8,128)(2,1)} %collective-permute-done.13.refs_8_), channel_id=1, source_target_pairs={{8,0},{12,4},{9,1},{13,5},{10,2},{14,6},{11,3},{15,7}} | collective-permute-start | bytes 786440 | tf_op jit(solution)/shard_map/ppermute | solution.py:605
  52.2 1.4 %collective-permute-start.16 = (bf16[2,512,128]{2,1,0:T(8,128)(2,1)}, bf16[2,512,128]{2,1,0:T(8,128)(2,1)}, u32[]{:S(2)}, u32[]{:S(2)}) collective-permute-start(bf16[2,512,128]{2,1,0:T(8,128)(2,1)} %collective-permute-done.15.refs_7_), channel_id=1, source_target_pairs={{16,24},{20,28},{17,25},{21,29},{18,26},{22,30},{19,27},{23,31}} | collective-permute-start | bytes 786440 | tf_op jit(solution)/shard_map/ppermute | solution.py:605
  53.6 8.8 %collective-permute-done.10.refs_12_ = bf16[2,512,128]{2,1,0:T(8,128)(2,1)} collective-permute-done((bf16[2,512,128]{2,1,0:T(8,128)(2,1)}, bf16[2,512,128]{2,1,0:T(8,128)(2,1)}, u32[]{:S(2)}, u32[]{:S(2)}) %collective-permute-start.10) | collective-permute-done | bytes 262176 | tf_op jit(solution)/shard_map/ppermute | solution.py:605
  62.4 5.2 %collective-permute-done.6.refs_6_ = bf16[2,512,128]{2,1,0:T(8,128)(2,1)} collective-permute-done((bf16[2,512,128]{2,1,0:T(8,128)(2,1)}, bf16[2,512,128]{2,1,0:T(8,128)(2,1)}, u32[]{:S(2)}, u32[]{:S(2)}) %collective-permute-start.6) | collective-permute-done | bytes 262176 | tf_op jit(solution)/shard_map/ppermute | solution.py:605
  69.5 6.0 %attend_head.2 = (bf16[8,128,256]{2,1,0:T(8,128)(2,1)S(1)}, bf16[2,512,128]{2,1,0:T(8,128)(2,1)S(1)}, bf16[2,512,128]{2,1,0:T(8,128)(2,1)}) custom-call(s32[4]{0:T(128)S(1)} %pad_add_fusion.1.info, bf16[8,128,1152]{2,1,0:T(8,128)(2,1)S(1)} %all-to-all-done.refs_0_.refs_1_.refs_2_, ...), custom_call_target="tpu_custom_call", output_to_operand_aliasing={{1}: (12, {}), {2}: (13, {})} | custom-call | flops 1342177280 | bytes 1835008 | tf_op jit(solution)/shard_map/attend_head/pallas_call | solution.py:237
  75.5 5.9 %attend_head.3.refs_9_ = bf16[8,128,256]{2,1,0:T(8,128)(2,1)S(1)} custom-call(s32[4]{0:T(128)S(1)} %pad_add_fusion.1.info, bf16[8,128,1152]{2,1,0:T(8,128)(2,1)S(1)} %all-to-all-done.refs_0_.refs_1_.refs_2_, bf16[8,128,1152]{2,1,0:T(8,128)(2,1)S(1)} %all-to-all-done.refs_0_.refs_1_.refs_2_, ...), custom_call_target="tpu_custom_call", output_to_operand_aliasing={{}: (12, {})} | custom-call | flops 1342177280 | bytes 1835008 | tf_op jit(solution)/shard_map/attend_head/pallas_call | solution.py:237
  82.3 4.1 %all-to-all-start.2 = ((bf16[8,128,256]{2,1,0:T(8,128)(2,1)}), bf16[8,128,256]{2,1,0:T(8,128)(2,1)}, u32[]{:S(2)}, u32[]{:S(2)}) async-start(bf16[8,128,256]{2,1,0:T(8,128)(2,1)} %copy-done.1), calls=%async_computation.2 | async-start | bytes 1048576 | tf_op jit(solution)/shard_map/all_to_all | solution.py:589
  86.4 1.4 %collective-permute-start.17 = (bf16[2,512,128]{2,1,0:T(8,128)(2,1)S(1)}, bf16[2,512,128]{2,1,0:T(8,128)(2,1)}, u32[]{:S(2)}, u32[]{:S(2)}) collective-permute-start(bf16[2,512,128]{2,1,0:T(8,128)(2,1)S(1)} %get-tuple-element.7.refs_7_), channel_id=1, source_target_pairs={{16,24},{20,28},{17,25},{21,29},{18,26},{22,30},{19,27},{23,31}} | collective-permute-start | bytes 786440 | tf_op jit(solution)/shard_map/ppermute | solution.py:605
  87.8 1.5 %collective-permute-start.18 = (bf16[2,512,128]{2,1,0:T(8,128)(2,1)}, bf16[2,512,128]{2,1,0:T(8,128)(2,1)}, u32[]{:S(2)}, u32[]{:S(2)}) collective-permute-start(bf16[2,512,128]{2,1,0:T(8,128)(2,1)} %get-tuple-element.8.refs_8_), channel_id=1, source_target_pairs={{8,0},{12,4},{9,1},{13,5},{10,2},{14,6},{11,3},{15,7}} | collective-permute-start | bytes 786440 | tf_op jit(solution)/shard_map/ppermute | solution.py:605
  91.5 5.6 %attend_most.1 = (bf16[1,1024,128]{2,1,0:T(8,128)(2,1)S(1)}, f32[1,1024,256]{2,1,0:T(8,128)S(1)}) custom-call(s32[5]{0:T(128)S(1)} %stack.67.info, bf16[8,128,1152]{2,1,0:T(8,128)(2,1)S(1)} %all-to-all-done.refs_0_.refs_1_.refs_2_, bf16[8,128,1152]{2,1,0:T(8,128)(2,1)S(1)} %all-to-all-done.refs_0_.refs_1_.refs_2_, ...), custom_call_target="tpu_custom_call" | custom-call | flops 1073741824 | bytes 1572864 | tf_op jit(solution)/shard_map/attend_most/pallas_call | solution.py:378
  97.1 1.5 %collective-permute-done.18.refs_4_ = bf16[2,512,128]{2,1,0:T(8,128)(2,1)} collective-permute-done((bf16[2,512,128]{2,1,0:T(8,128)(2,1)}, bf16[2,512,128]{2,1,0:T(8,128)(2,1)}, u32[]{:S(2)}, u32[]{:S(2)}) %collective-permute-start.18) | collective-permute-done | bytes 262176 | tf_op jit(solution)/shard_map/ppermute | solution.py:605
  98.6 2.9 %attend_last.1 = bf16[8,128,128]{2,1,0:T(8,128)(2,1)S(1)} custom-call(s32[3]{0:T(128)S(1)} %pad_add_fusion.info, bf16[8,128,1152]{2,1,0:T(8,128)(2,1)S(1)} %all-to-all-done.refs_0_.refs_1_.refs_2_, bf16[1,1024,128]{2,1,0:T(8,128)(2,1)S(1)} %get-tuple-element.10.refs_1_, f32[1,1024,256]{2,1,0:T(8,128)S(1)} %get-tuple-element.11.refs_2_, ...), custom_call_target="tpu_custom_call" | custom-call | flops 268435456 | bytes 786432 | tf_op jit(solution)/shard_map/attend_last/pallas_call | solution.py:454
  101.5 10.2 %all_to_all.15.refs_0_.refs_1_ = bf16[8,128,128]{2,1,0:T(8,128)(2,1)S(1)} all-to-all(bf16[8,128,128]{2,1,0:T(8,128)(2,1)S(1)} %attend_last.1), channel_id=1, replica_groups={{0,1,2,3,4,5,6,7},{8,9,10,11,12,13,14,15},{16,17,18,19,20,21,22,23},{24..., dimensions={0} | all-to-all | bytes 524288 | tf_op jit(solution)/shard_map/all_to_all | solution.py:589
  113.1 6.2 %project_early.1.refs_4_ = f32[64,3072]{1,0:T(8,128)S(1)} custom-call(bf16[8,128,256]{2,1,0:T(8,128)(2,1)} %all-to-all-done.2.refs_0_, bf16[8,3,128,3072]{3,2,1,0:T(8,128)(2,1)} %bitcast.10), custom_call_target="tpu_custom_call" | custom-call | flops 805306368 | bytes 12582912 | tf_op jit(solution)/shard_map/project_early/pallas_call | solution.py:524
  119.3 4.0 %project_last.1 = bf16[64,3072]{1,0:T(8,128)(2,1)} custom-call(bf16[8,128,128]{2,1,0:T(8,128)(2,1)S(1)} %all_to_all.15.refs_0_.refs_1_, bf16[8,3,128,3072]{3,2,1,0:T(8,128)(2,1)} %bitcast.11, bf16[64,3072]{1,0:T(8,128)(2,1)S(1)} %copy-done.5, f32[1,3072]{1,0:T(1,128)S(1)} %bitcast.9, f32[64,3072]{1,0:T(8,128)S(1)} %project_early.1.refs_4_), custom_call_target="tpu_custom_call" | custom-call | flops 402653184 | bytes 6291456 | tf_op jit(solution)/shard_map/project_last/pallas_call | solution.py:524
  (66 shorter events, 18.6 us)
Async XLA Ops:
  0.6 1.7 %copy-start.3 = (bf16[128,9216]{1,0:T(8,128)(2,1)S(1)}, bf16[128,9216]{1,0:T(8,128)(2,1)}, u32[]{:S(2)}) copy-start(bf16[128,9216]{1,0:T(8,128)(2,1)} %txt.1) | copy-start | bytes 7077892
  2.3 1.3 %copy-start.4 = (bf16[64,9216]{1,0:T(8,128)(2,1)S(1)}, bf16[64,9216]{1,0:T(8,128)(2,1)}, u32[]{:S(2)}) copy-start(bf16[64,9216]{1,0:T(8,128)(2,1)} %img.1) | copy-start | bytes 3538948
  4.5 1.4 %copy-start = (bf16[8,128,1152]{2,1,0:T(8,128)(2,1)}, bf16[8,128,1152]{2,1,0:T(8,128)(2,1)S(1)}, u32[]{:S(2)}) copy-start(bf16[8,128,1152]{2,1,0:T(8,128)(2,1)S(1)} %pack_heads.1) | copy-start | bytes 7077892
  5.9 61.7 %all-to-all-start = ((bf16[8,128,1152]{2,1,0:T(8,128)(2,1)}), bf16[8,128,1152]{2,1,0:T(8,128)(2,1)S(1)}, u32[]{:S(2)}, u32[]{:S(2)}) async-start(bf16[8,128,1152]{2,1,0:T(8,128)(2,1)} %copy-done), calls=%async_computation | async-start | bytes 4718592 | tf_op jit(solution)/shard_map/all_to_all | solution.py:589
  12.3 1.9 %collective-permute-start = (bf16[2,256,384]{2,1,0:T(8,128)(2,1)S(1)}, bf16[2,256,384]{2,1,0:T(8,128)(2,1)S(1)}, u32[]{:S(2)}, u32[]{:S(2)}) collective-permute-start(bf16[2,256,384]{2,1,0:T(8,128)(2,1)S(1)} %get-tuple-element.17), channel_id=1, source_target_pairs={{0,4},{4,0},{8,12},{12,8},{16,20},{20,16},{24,28},{28,24},{1,5},{5... | collective-permute-start | bytes 1179656 | tf_op jit(solution)/shard_map/ppermute | solution.py:597
  14.3 12.0 %collective-permute-start.1 = (bf16[2,512,128]{2,1,0:T(8,128)(2,1)S(1)}, bf16[2,512,128]{2,1,0:T(8,128)(2,1)S(1)}, u32[]{:S(2)}, u32[]{:S(2)}) collective-permute-start(bf16[2,512,128]{2,1,0:T(8,128)(2,1)S(1)} %pad_maximum_fusion.1), channel_id=1, source_target_pairs={{0,8},{4,12},{8,16},{12,20},{16,24},{20,28},{1,9},{5,13},{9,17},{1... | collective-permute-start | bytes 786440 | tf_op jit(solution)/shard_map/ppermute | solution.py:605
  17.9 13.7 %collective-permute-start.4 = (bf16[2,512,128]{2,1,0:T(8,128)(2,1)S(1)}, bf16[2,512,128]{2,1,0:T(8,128)(2,1)S(1)}, u32[]{:S(2)}, u32[]{:S(2)}) collective-permute-start(bf16[2,512,128]{2,1,0:T(8,128)(2,1)S(1)} %pad_maximum_fusion.2), channel_id=1, source_target_pairs={{8,0},{12,4},{16,8},{20,12},{24,16},{28,20},{9,1},{13,5},{17,9},{2... | collective-permute-start | bytes 786440 | tf_op jit(solution)/shard_map/ppermute | solution.py:605
  19.2 14.4 %collective-permute-start.3 = (bf16[2,512,128]{2,1,0:T(8,128)(2,1)S(1)}, bf16[2,512,128]{2,1,0:T(8,128)(2,1)S(1)}, u32[]{:S(2)}, u32[]{:S(2)}) collective-permute-start(bf16[2,512,128]{2,1,0:T(8,128)(2,1)S(1)} %pad_maximum_fusion.2), channel_id=1, source_target_pairs={{0,8},{4,12},{8,16},{12,20},{16,24},{20,28},{1,9},{5,13},{9,17},{1... | collective-permute-start | bytes 786440 | tf_op jit(solution)/shard_map/ppermute | solution.py:605
  23.7 12.0 %collective-permute-start.2 = (bf16[2,512,128]{2,1,0:T(8,128)(2,1)S(1)}, bf16[2,512,128]{2,1,0:T(8,128)(2,1)}, u32[]{:S(2)}, u32[]{:S(2)}) collective-permute-start(bf16[2,512,128]{2,1,0:T(8,128)(2,1)S(1)} %pad_maximum_fusion.1), channel_id=1, source_target_pairs={{8,0},{12,4},{16,8},{20,12},{24,16},{28,20},{9,1},{13,5},{17,9},{2... | collective-permute-start | bytes 786440 | tf_op jit(solution)/shard_map/ppermute | solution.py:605
  25.1 15.4 %collective-permute-start.12 = (bf16[2,512,128]{2,1,0:T(8,128)(2,1)S(1)}, bf16[2,512,128]{2,1,0:T(8,128)(2,1)S(1)}, u32[]{:S(2)}, u32[]{:S(2)}) collective-permute-start(bf16[2,512,128]{2,1,0:T(8,128)(2,1)S(1)} %pad_maximum_fusion.3), channel_id=1, source_target_pairs={{8,0},{12,4},{16,8},{20,12},{24,16},{28,20},{9,1},{13,5},{17,9},{2... | collective-permute-start | bytes 786440 | tf_op jit(solution)/shard_map/ppermute | solution.py:605
  26.4 16.1 %collective-permute-start.11 = (bf16[2,512,128]{2,1,0:T(8,128)(2,1)S(1)}, bf16[2,512,128]{2,1,0:T(8,128)(2,1)S(1)}, u32[]{:S(2)}, u32[]{:S(2)}) collective-permute-start(bf16[2,512,128]{2,1,0:T(8,128)(2,1)S(1)} %pad_maximum_fusion.3), channel_id=1, source_target_pairs={{0,8},{4,12},{8,16},{12,20},{16,24},{20,28},{1,9},{5,13},{9,17},{1... | collective-permute-start | bytes 786440 | tf_op jit(solution)/shard_map/ppermute | solution.py:605
  31.6 13.4 %collective-permute-start.5 = (bf16[2,512,128]{2,1,0:T(8,128)(2,1)S(1)}, bf16[2,512,128]{2,1,0:T(8,128)(2,1)}, u32[]{:S(2)}, u32[]{:S(2)}) collective-permute-start(bf16[2,512,128]{2,1,0:T(8,128)(2,1)S(1)} %collective-permute-done.4.refs_10_), channel_id=1, source_target_pairs={{8,0},{12,4},{16,8},{20,12},{9,1},{13,5},{17,9},{21,13},{10,2},{14... | collective-permute-start | bytes 786440 | tf_op jit(solution)/shard_map/ppermute | solution.py:605
  33.6 12.7 %collective-permute-start.7 = (bf16[2,512,128]{2,1,0:T(8,128)(2,1)S(1)}, bf16[2,512,128]{2,1,0:T(8,128)(2,1)}, u32[]{:S(2)}, u32[]{:S(2)}) collective-permute-start(bf16[2,512,128]{2,1,0:T(8,128)(2,1)S(1)} %collective-permute-done.3.refs_5_), channel_id=1, source_target_pairs={{8,16},{12,20},{16,24},{20,28},{9,17},{13,21},{17,25},{21,29},{10,... | collective-permute-start | bytes 786440 | tf_op jit(solution)/shard_map/ppermute | solution.py:605
  35.7 11.9 %collective-permute-start.9 = (bf16[2,512,128]{2,1,0:T(8,128)(2,1)S(1)}, bf16[2,512,128]{2,1,0:T(8,128)(2,1)S(1)}, u32[]{:S(2)}, u32[]{:S(2)}) collective-permute-start(bf16[2,512,128]{2,1,0:T(8,128)(2,1)S(1)} %collective-permute-done.1.refs_5_), channel_id=1, source_target_pairs={{8,16},{12,20},{16,24},{20,28},{9,17},{13,21},{17,25},{21,29},{10,... | collective-permute-start | bytes 786440 | tf_op jit(solution)/shard_map/ppermute | solution.py:605
  40.5 10.4 %collective-permute-start.13 = (bf16[2,512,128]{2,1,0:T(8,128)(2,1)S(1)}, bf16[2,512,128]{2,1,0:T(8,128)(2,1)}, u32[]{:S(2)}, u32[]{:S(2)}) collective-permute-start(bf16[2,512,128]{2,1,0:T(8,128)(2,1)S(1)} %collective-permute-done.12.refs_10_), channel_id=1, source_target_pairs={{8,0},{12,4},{16,8},{20,12},{9,1},{13,5},{17,9},{21,13},{10,2},{14... | collective-permute-start | bytes 786440 | tf_op jit(solution)/shard_map/ppermute | solution.py:605
  42.5 9.6 %collective-permute-start.15 = (bf16[2,512,128]{2,1,0:T(8,128)(2,1)S(1)}, bf16[2,512,128]{2,1,0:T(8,128)(2,1)}, u32[]{:S(2)}, u32[]{:S(2)}) collective-permute-start(bf16[2,512,128]{2,1,0:T(8,128)(2,1)S(1)} %collective-permute-done.11.refs_5_), channel_id=1, source_target_pairs={{8,16},{12,20},{16,24},{20,28},{9,17},{13,21},{17,25},{21,29},{10,... | collective-permute-start | bytes 786440 | tf_op jit(solution)/shard_map/ppermute | solution.py:605
  45.0 17.4 %collective-permute-start.10 = (bf16[2,512,128]{2,1,0:T(8,128)(2,1)}, bf16[2,512,128]{2,1,0:T(8,128)(2,1)}, u32[]{:S(2)}, u32[]{:S(2)}) collective-permute-start(bf16[2,512,128]{2,1,0:T(8,128)(2,1)} %collective-permute-done.2.refs_6_), channel_id=1, source_target_pairs={{8,0},{12,4},{16,8},{20,12},{9,1},{13,5},{17,9},{21,13},{10,2},{14... | collective-permute-start | bytes 786440 | tf_op jit(solution)/shard_map/ppermute | solution.py:605
  46.3 21.3 %collective-permute-start.6 = (bf16[2,512,128]{2,1,0:T(8,128)(2,1)}, bf16[2,512,128]{2,1,0:T(8,128)(2,1)}, u32[]{:S(2)}, u32[]{:S(2)}) collective-permute-start(bf16[2,512,128]{2,1,0:T(8,128)(2,1)} %collective-permute-done.5.refs_8_), channel_id=1, source_target_pairs={{8,0},{12,4},{9,1},{13,5},{10,2},{14,6},{11,3},{15,7}} | collective-permute-start | bytes 786440 | tf_op jit(solution)/shard_map/ppermute | solution.py:605
  47.6 20.0 %collective-permute-start.8 = (bf16[2,512,128]{2,1,0:T(8,128)(2,1)}, bf16[2,512,128]{2,1,0:T(8,128)(2,1)}, u32[]{:S(2)}, u32[]{:S(2)}) collective-permute-start(bf16[2,512,128]{2,1,0:T(8,128)(2,1)} %collective-permute-done.7.refs_7_), channel_id=1, source_target_pairs={{16,24},{20,28},{17,25},{21,29},{18,26},{22,30},{19,27},{23,31}} | collective-permute-start | bytes 786440 | tf_op jit(solution)/shard_map/ppermute | solution.py:605
  50.9 24.6 %collective-permute-start.14 = (bf16[2,512,128]{2,1,0:T(8,128)(2,1)}, bf16[2,512,128]{2,1,0:T(8,128)(2,1)}, u32[]{:S(2)}, u32[]{:S(2)}) collective-permute-start(bf16[2,512,128]{2,1,0:T(8,128)(2,1)} %collective-permute-done.13.refs_8_), channel_id=1, source_target_pairs={{8,0},{12,4},{9,1},{13,5},{10,2},{14,6},{11,3},{15,7}} | collective-permute-start | bytes 786440 | tf_op jit(solution)/shard_map/ppermute | solution.py:605
  52.2 23.3 %collective-permute-start.16 = (bf16[2,512,128]{2,1,0:T(8,128)(2,1)}, bf16[2,512,128]{2,1,0:T(8,128)(2,1)}, u32[]{:S(2)}, u32[]{:S(2)}) collective-permute-start(bf16[2,512,128]{2,1,0:T(8,128)(2,1)} %collective-permute-done.15.refs_7_), channel_id=1, source_target_pairs={{16,24},{20,28},{17,25},{21,29},{18,26},{22,30},{19,27},{23,31}} | collective-permute-start | bytes 786440 | tf_op jit(solution)/shard_map/ppermute | solution.py:605
  67.6 1.0 copy-start.9
  68.6 0.9 copy-start.11
  69.5 6.0 %copy-start.13 = (bf16[2,512,128]{2,1,0:T(8,128)(2,1)S(1)}, bf16[2,512,128]{2,1,0:T(8,128)(2,1)}, u32[]{:S(2)}) copy-start(bf16[2,512,128]{2,1,0:T(8,128)(2,1)} %copy-done.12) | copy-start | bytes 786436
  69.5 6.0 %copy-start.15 = (bf16[2,512,128]{2,1,0:T(8,128)(2,1)S(1)}, bf16[2,512,128]{2,1,0:T(8,128)(2,1)}, u32[]{:S(2)}) copy-start(bf16[2,512,128]{2,1,0:T(8,128)(2,1)} %copy-done.14) | copy-start | bytes 786436
  82.3 19.3 %all-to-all-start.2 = ((bf16[8,128,256]{2,1,0:T(8,128)(2,1)}), bf16[8,128,256]{2,1,0:T(8,128)(2,1)}, u32[]{:S(2)}, u32[]{:S(2)}) async-start(bf16[8,128,256]{2,1,0:T(8,128)(2,1)} %copy-done.1), calls=%async_computation.2 | async-start | bytes 1048576 | tf_op jit(solution)/shard_map/all_to_all | solution.py:589
  86.4 10.7 %collective-permute-start.17 = (bf16[2,512,128]{2,1,0:T(8,128)(2,1)S(1)}, bf16[2,512,128]{2,1,0:T(8,128)(2,1)}, u32[]{:S(2)}, u32[]{:S(2)}) collective-permute-start(bf16[2,512,128]{2,1,0:T(8,128)(2,1)S(1)} %get-tuple-element.7.refs_7_), channel_id=1, source_target_pairs={{16,24},{20,28},{17,25},{21,29},{18,26},{22,30},{19,27},{23,31}} | collective-permute-start | bytes 786440 | tf_op jit(solution)/shard_map/ppermute | solution.py:605
  87.8 10.8 %collective-permute-start.18 = (bf16[2,512,128]{2,1,0:T(8,128)(2,1)}, bf16[2,512,128]{2,1,0:T(8,128)(2,1)}, u32[]{:S(2)}, u32[]{:S(2)}) collective-permute-start(bf16[2,512,128]{2,1,0:T(8,128)(2,1)} %get-tuple-element.8.refs_8_), channel_id=1, source_target_pairs={{8,0},{12,4},{9,1},{13,5},{10,2},{14,6},{11,3},{15,7}} | collective-permute-start | bytes 786440 | tf_op jit(solution)/shard_map/ppermute | solution.py:605
  89.5 1.0 copy-start.2
  112.8 10.5 %collective-permute-start.19 = (bf16[64,3072]{1,0:T(8,128)(2,1)S(1)}, bf16[64,3072]{1,0:T(8,128)(2,1)S(1)}, u32[]{:S(2)}, u32[]{:S(2)}) collective-permute-start(bf16[64,3072]{1,0:T(8,128)(2,1)S(1)} %unpack_text.1), channel_id=1, source_target_pairs={{0,4},{4,0},{8,12},{12,8},{16,20},{20,16},{24,28},{28,24},{1,5},{5... | collective-permute-start | bytes 1179656 | tf_op jit(solution)/shard_map/ppermute | solution.py:640
  113.1 6.2 %copy-start.5 = (bf16[64,3072]{1,0:T(8,128)(2,1)S(1)}, bf16[64,3072]{1,0:T(8,128)(2,1)}, u32[]{:S(2)}) copy-start(bf16[64,3072]{1,0:T(8,128)(2,1)} %refs_2_.1) | copy-start | bytes 1179652
  113.1 6.2 %copy-start.16 = (f32[3072]{0:T(1024)S(1)}, f32[3072]{0:T(1024)}, u32[]{:S(2)}) copy-start(f32[3072]{0:T(1024)} %param.10) | copy-start | bytes 36868
  (7 other events, 5.3 us)

commit v6 on v0

v6 whole, which is shorter than its diff:
```python
import functools
import math

import jax
import jax.numpy as jnp
from jax import lax
from jax.experimental import pallas as pl
from jax.experimental.pallas import tpu as pltpu
from jax.sharding import PartitionSpec as P

HD = 128
SCALE = math.log2(math.e) / math.sqrt(HD)
VMEM_LIMIT = 12 * 1024 * 1024
WIDE_LIMIT = 48 * 1024 * 1024
TILE = 512
FIRST_KEYS = 256
LARGE = 2.0**60


def params(block_elements=0):
    return pltpu.CompilerParams(
        vmem_limit_bytes=VMEM_LIMIT + 4 * block_elements, dimension_semantics=("arbitrary",)
    )


def pack_body(text_rows, places, width, core, img, txt, packed, sem):
    img_rows, model = img.shape[0], img.shape[1] // 3
    first = pl.multiple_of(core[0] * text_rows, text_rows)
    copies = []
    for destination, place in enumerate(places):
        for part in range(3):
            source = pl.ds(part * model + place * width, width)
            target = pl.ds(part * width, width)
            copies.append((img.at[:, source], packed.at[destination, pl.ds(0, img_rows), target]))
            copies.append(
                (
                    txt.at[pl.ds(first, text_rows), source],
                    packed.at[destination, pl.ds(img_rows, text_rows), target],
                )
            )
    copies = [
        pltpu.make_async_copy(source, target, sem.at[index])
        for index, (source, target) in enumerate(copies)
    ]
    for copy in copies:
        copy.start()
    for copy in copies:
        copy.wait()


def pack(core, img_qkv, txt_qkv, text_rows, places, width):
    rows = img_qkv.shape[0] + text_rows
    anywhere = pl.BlockSpec(memory_space=pl.ANY)
    return pl.pallas_call(
        functools.partial(pack_body, text_rows, places, width),
        in_specs=[pl.BlockSpec(memory_space=pltpu.SMEM), anywhere, anywhere],
        out_specs=anywhere,
        out_shape=jax.ShapeDtypeStruct((len(places), rows, 3 * width), img_qkv.dtype),
        scratch_shapes=[pltpu.SemaphoreType.DMA((6 * len(places),))],
        compiler_params=pltpu.CompilerParams(vmem_limit_bytes=WIDE_LIMIT),
        name="pack_heads",
    )(core, img_qkv, txt_qkv)


def dot(first, second, contract):
    return lax.dot_general(
        first, second, ((contract[:1], contract[1:]), ((), ())), preferred_element_type=jnp.float32
    )


def with_ones(block):
    return jnp.concatenate([block, jnp.ones_like(block)], axis=1)


def reference_columns(row_max):
    reference = row_max.astype(jnp.bfloat16).astype(jnp.float32)
    return jnp.broadcast_to(reference * (-1.0 / HD), (row_max.shape[0], HD)).astype(jnp.bfloat16)


def weighted(queries, key_rows, values):
    weights = jnp.exp2(dot(queries, key_rows, (1, 1)) * SCALE).astype(jnp.bfloat16)
    return dot(weights, values, (1, 0))


def tiles_of(rows):
    tile = min(TILE, rows)
    return [slice(first, min(first + tile, rows)) for first in range(0, rows, tile)]


def until_small(flag, total, attempt):
    flag[0] = 1

    @pl.loop(0, 2)
    def _(turn):
        @pl.when(flag[0] == 1)
        def _():
            attempt(turn)
            flag[0] = jnp.where(jnp.max(total[:, HD:]) > LARGE, 1, 0).astype(jnp.int32)


class Sides:
    def __init__(self, sides, heads):
        self.operands, self.specs, self.counts = [], [], []
        for blocks, by_core in sides:
            self.counts.append(len(blocks))
            for block in blocks:
                self.operands.append(block)
                self.specs.append(stale_spec(block, heads, by_core))

    def each(self, info, refs, act):
        for index, count in enumerate(self.counts):
            blocks, refs = refs[:count], refs[count:]

            @pl.when(info[1 + index] == 1)
            def _():
                act(
                    jnp.concatenate([block[0] for block in blocks], 0),
                    jnp.concatenate([block[1] for block in blocks], 0),
                )


def stale_spec(block, heads, by_core):
    shape = (2, block.shape[1], HD)
    if by_core:
        return pl.BlockSpec(shape, lambda h, info: (0, 0, info[0] * heads + h))
    return pl.BlockSpec(shape, lambda h, info: (0, 0, h))


def column_spec(shape, offset=0):
    return pl.BlockSpec(shape[:2] + (HD,), lambda h, info: (0, 0, offset + h))


def head_spec(shape):
    return pl.BlockSpec((1,) + shape[1:], lambda h, info: (h, 0, 0))


def accumulate(flag, total, aug, shift, queries, first_keys, own, each_arrived):
    rows = total.shape[0]

    def scored(span, key_rows):
        return dot(queries[span, :], key_rows, (1, 1))

    def raise_to(span, key_rows):
        row_max = jnp.max(scored(span, key_rows), axis=1, keepdims=True)
        shift[span, :] = jnp.maximum(shift[span, :], jnp.broadcast_to(row_max, shift[span, :].shape))

    def attempt(turn):
        @pl.when(turn == 0)
        def _():
            for tile in tiles_of(rows):
                row_max = jnp.max(scored(tile, first_keys), axis=1, keepdims=True)
                aug[tile, :] = reference_columns(row_max)

        @pl.when(turn == 1)
        def _():
            shift[...] = jnp.full_like(shift, -jnp.inf)
            for span, key_rows, _ in own:
                raise_to(span, key_rows)
            each_arrived(lambda key_rows, _: raise_to(slice(0, rows), key_rows))
            aug[...] = reference_columns(shift[:, :1])

        def add(span, key_rows, values):
            both = jnp.concatenate([queries[span, :], aug[span, :]], axis=1)
            total[span, :] += weighted(both, with_ones(key_rows), with_ones(values))

        total[...] = jnp.zeros_like(total)
        for span, key_rows, values in own:
            add(span, key_rows, values)

        def add_everywhere(key_rows, values):
            for tile in tiles_of(rows):
                add(tile, key_rows, values)

        each_arrived(add_everywhere)

    until_small(flag, total, attempt)


def rows_of(block, first, last):
    return block[:, first:last, :].reshape(-1, HD)


def text_body(pair, img_rows, sides, wanted, info, *refs):
    q_ref, k_ref, v_ref = refs[:3]
    stale, arrived = refs[3 : 3 + pair], refs[3 + pair : 3 + pair + len(sides.operands)]
    out, aug, total, shift, flag = refs[3 + pair + len(sides.operands) :]

    @pl.when(info[wanted] == 1)
    def _():
        rows = total.shape[0]
        last = q_ref.shape[1]
        queries = rows_of(q_ref[...], img_rows, last)
        text_keys = rows_of(k_ref[...], img_rows, last)
        text_values = rows_of(v_ref[...], img_rows, last)
        everywhere = slice(0, rows)
        own = [
            (everywhere, text_keys, text_values),
            (
                everywhere,
                jnp.concatenate([block[0] for block in stale], 0),
                jnp.concatenate([block[1] for block in stale], 0),
            ),
        ]
        accumulate(
            flag, total, aug, shift, queries, text_keys[: min(FIRST_KEYS, rows), :], own,
            functools.partial(sides.each, info, arrived),
        )
        attended = (total[:, :HD] / total[:, HD:]).astype(out.dtype)
        out[...] = attended.reshape(out.shape)


def image_body(pair, img_rows, sides, info, *refs):
    q_ref, k_ref, v_ref = refs[:3]
    stale, arrived = refs[3 : 3 + pair], refs[3 + pair : 3 + pair + len(sides.operands)]
    aug, total, shift, flag = refs[4 + pair + len(sides.operands) :]
    aug, total = aug.at[0], total.at[0]
    rows = total.shape[0]
    last = q_ref.shape[1]
    core = info[0]
    queries = rows_of(q_ref[...], 0, img_rows)
    img_keys, img_values = rows_of(k_ref[...], 0, img_rows), rows_of(v_ref[...], 0, img_rows)
    text_keys = rows_of(k_ref[...], img_rows, last)
    text_values = rows_of(v_ref[...], img_rows, last)
    group_rows = rows // pair
    own = [(slice(0, rows), text_keys, text_values)]
    for group in range(pair):
        span = slice(group * group_rows, (group + 1) * group_rows)
        key_rows, values = [img_keys[span, :]], [img_values[span, :]]
        if pair == 2:
            mine = core == group
            key_rows.append(jnp.where(mine, stale[1][0], stale[0][0]))
            values.append(jnp.where(mine, stale[1][1], stale[0][1]))
        own.append((span, jnp.concatenate(key_rows, 0), jnp.concatenate(values, 0)))
    accumulate(
        flag, total, aug, shift, queries,
        text_keys[: min(FIRST_KEYS, text_keys.shape[0]), :], own,
        functools.partial(sides.each, info, arrived),
    )


def last_body(img_rows, sides, info, *refs):
    q_ref, aug_ref, total_ref = refs[:3]
    arrived = refs[3 : 3 + len(sides.operands)]
    out, total, shift, flag = refs[4 + len(sides.operands) :]
    rows = total.shape[0]
    queries = rows_of(q_ref[...], 0, img_rows)
    each_arrived = functools.partial(sides.each, info, arrived)

    def referred(span, key_rows):
        both = jnp.concatenate([queries[span, :], aug_ref[0, span, :]], axis=1)
        return dot(both, with_ones(key_rows), (1, 1))

    def add(key_rows, values):
        for tile in tiles_of(rows):
            weights = jnp.exp2(referred(tile, key_rows) * SCALE).astype(jnp.bfloat16)
            total[tile, :] += dot(weights, with_ones(values), (1, 0))

    def raise_to(key_rows, _):
        above = jnp.max(referred(slice(0, rows), key_rows), axis=1, keepdims=True)
        shift[...] = jnp.maximum(shift[...], jnp.broadcast_to(above, shift.shape))

    def add_shifted(key_rows, values):
        scores = referred(slice(0, rows), key_rows) - shift[:, :1]
        weights = jnp.exp2(scores * SCALE).astype(jnp.bfloat16)
        total[...] += dot(weights, with_ones(values), (1, 0))

    def attempt(turn):
        @pl.when(turn == 0)
        def _():
            total[...] = total_ref[0]
            each_arrived(add)

        @pl.when(turn == 1)
        def _():
            shift[...] = jnp.zeros_like(shift)
            each_arrived(raise_to)
            keep = jnp.exp2(shift[...] * -SCALE)
            total[...] = total_ref[0] * jnp.concatenate([keep, keep], axis=1)
            each_arrived(add_shifted)

    until_small(flag, total, attempt)
    attended = (total[:, :HD] / total[:, HD:]).astype(out.dtype)
    out[...] = attended.reshape(out.shape)


def attend_cost(queries, keys, heads):
    return pl.CostEstimate(
        flops=4 * queries * keys * heads * HD,
        bytes_accessed=4 * queries * heads * HD + 4 * keys * heads * HD,
        transcendentals=queries * keys * heads,
    )


def call_heads(body, name, heads, info, operands, specs, outs, out_specs, scratch, cost):
    return pl.pallas_call(
        body,
        grid_spec=pltpu.PrefetchScalarGridSpec(
            num_scalar_prefetch=1,
            grid=(heads,),
            in_specs=specs,
            out_specs=out_specs,
            scratch_shapes=scratch,
        ),
        out_shape=outs,
        compiler_params=params(
            sum(math.prod(spec.block_shape) for spec in specs if spec.block_shape is not None)
        ),
        cost_estimate=cost,
        name=name,
    )(info, *operands)


def common(qkv, stale, heads, sides):
    operands = [qkv] * 3 + list(stale) + sides.operands
    specs = [column_spec(qkv.shape, part * heads) for part in range(3)]
    specs += [stale_spec(block, heads, len(stale) > 1) for block in stale] + sides.specs
    return operands, specs


def scratch_of(rows):
    return [pltpu.VMEM((rows, HD), jnp.float32), pltpu.SMEM((1,), jnp.int32)]


def attend_text(info, wanted, qkv, img_rows, stale, sides):
    heads = qkv.shape[2] // (3 * HD)
    sides = Sides(sides, heads)
    operands, specs = common(qkv, stale, heads, sides)
    text_rows = qkv.shape[1] - img_rows
    rows = qkv.shape[0] * text_rows
    out = jax.ShapeDtypeStruct((qkv.shape[0], text_rows, heads * HD), qkv.dtype)
    return call_heads(
        functools.partial(text_body, len(stale), img_rows, sides, wanted),
        "attend_text", heads, info, operands, specs, out, column_spec(out.shape),
        [pltpu.VMEM((rows, HD), jnp.bfloat16), pltpu.VMEM((rows, 2 * HD), jnp.float32)]
        + scratch_of(rows),
        attend_cost(rows, 4 * rows, heads),
    )


def attend_image(info, qkv, img_rows, stale, sides, after):
    heads = qkv.shape[2] // (3 * HD)
    sides = Sides(sides, heads)
    operands, specs = common(qkv, stale, heads, sides)
    rows = qkv.shape[0] * img_rows
    outs = [
        jax.ShapeDtypeStruct((heads, rows, HD), jnp.bfloat16),
        jax.ShapeDtypeStruct((heads, rows, 2 * HD), jnp.float32),
    ]
    return call_heads(
        functools.partial(image_body, len(stale), img_rows, sides),
        "attend_image", heads, info, operands + [after],
        specs + [pl.BlockSpec(memory_space=pl.ANY)], outs,
        [head_spec(out.shape) for out in outs], scratch_of(rows),
        attend_cost(rows, 4 * rows, heads),
    )


def attend_last(info, qkv, img_rows, state, sides, after):
    heads = qkv.shape[2] // (3 * HD)
    sides = Sides(sides, heads)
    rows = qkv.shape[0] * img_rows
    out = jax.ShapeDtypeStruct((qkv.shape[0], img_rows, heads * HD), qkv.dtype)
    specs = [column_spec(qkv.shape)] + [head_spec(part.shape) for part in state] + sides.specs
    return call_heads(
        functools.partial(last_body, img_rows, sides),
        "attend_last", heads, info, [qkv, *state] + sides.operands + [after],
        specs + [pl.BlockSpec(memory_space=pl.ANY)], out, column_spec(out.shape),
        [pltpu.VMEM((rows, 2 * HD), jnp.float32)] + scratch_of(rows),
        attend_cost(rows, rows, heads),
    )


def project_body(order, x_ref, weight, residual, gate, out, held, total, sems):
    copies = [
        pltpu.make_async_copy(weight.at[place], held.at[place], sems.at[place])
        for place in order
    ]
    for copy in copies:
        copy.start()
    for source, (place, copy) in enumerate(zip(order, copies)):
        copy.wait()
        part = jnp.dot(x_ref[source], held[place], preferred_element_type=jnp.float32)
        if source == 0:
            total[...] = part
        else:
            total[...] += part
    out[...] = (residual[...].astype(jnp.float32) + gate[...] * total[...]).astype(out.dtype)


def project(x, order, weight, residual, gate):
    rows, model = residual.shape
    destinations, _, width = x.shape
    vmem = pl.BlockSpec(memory_space=pltpu.VMEM)
    return pl.pallas_call(
        functools.partial(project_body, order),
        in_specs=[vmem, pl.BlockSpec(memory_space=pl.ANY), vmem, vmem],
        out_specs=vmem,
        out_shape=jax.ShapeDtypeStruct((rows, model), residual.dtype),
        scratch_shapes=[
            pltpu.VMEM((destinations, width, model), weight.dtype),
            pltpu.VMEM((rows, model), jnp.float32),
            pltpu.SemaphoreType.DMA((destinations,)),
        ],
        compiler_params=pltpu.CompilerParams(vmem_limit_bytes=WIDE_LIMIT),
        cost_estimate=pl.CostEstimate(
            flops=2 * rows * model * model, bytes_accessed=2 * model * model, transcendentals=0
        ),
        name="project",
    )(x, weight.reshape(destinations, width, model), residual, gate.reshape(1, model))


def unpack_body(order, x_ref, out):
    width = x_ref.shape[2]
    for source, place in enumerate(order):
        out[:, place * width : (place + 1) * width] = x_ref[source]


def unpack(x, order):
    rows, model = x.shape[1], x.shape[0] * x.shape[2]
    return pl.pallas_call(
        functools.partial(unpack_body, order),
        grid=(1,),
        in_specs=[pl.BlockSpec(x.shape, lambda n: (0, 0, 0))],
        out_specs=pl.BlockSpec((rows, model), lambda n: (0, 0)),
        out_shape=jax.ShapeDtypeStruct((rows, model), x.dtype),
        compiler_params=params(),
        name="unpack_text",
    )(x)


def per_device(img_qkv, txt_qkv, stale_kv, residual, gate_scale, proj_weight):
    patches, head_owners = lax.axis_size("patch"), lax.axis_size("head")
    patch = lax.axis_index("patch")
    owned_heads = stale_kv.shape[2] // HD
    pair = 2 if patches % 2 == 0 and owned_heads % 2 == 0 else 1
    planes = patches // pair
    plane, core = patch // pair, patch % pair
    width = stale_kv.shape[2] // pair
    heads = width // HD
    img_rows, model = residual.shape
    text_rows = txt_qkv.shape[0] // pair
    destinations = pair * head_owners

    order = [(d % head_owners) * pair + d // head_owners for d in range(destinations)]
    groups = [[g * destinations + d for d in range(destinations)] for g in range(planes)]
    swap_pairs = [(p, p + 1 - 2 * (p % 2)) for p in range(patches)]

    def exchange(x):
        return lax.all_to_all(
            x, ("patch", "head"), split_axis=0, concat_axis=0, axis_index_groups=groups, tiled=True
        )

    def swap(x):
        return lax.ppermute(x, "patch", swap_pairs)

    def up_pairs(step):
        return [(z, z + 1) for z in range(step - 1, planes - 1)]

    def down_pairs(step):
        return [(z + 1, z) for z in range(0, planes - step)]

    core_only = core.astype(jnp.int32).reshape(1)
    qkv = exchange(pack(core_only, img_qkv, txt_qkv, text_rows, order, width))

    sides, there = [], []
    above = lambda step: plane + step < planes
    below = lambda step: plane >= step
    if pair == 2:
        stale = [stale_kv, swap(stale_kv)]
        held = stale
        for step in range(1, planes):
            pairs = [(2 * a, 2 * b) for a, b in up_pairs(step)]
            pairs += [(2 * a + 1, 2 * b + 1) for a, b in down_pairs(step)]
            held = [lax.ppermute(block, "patch", pairs) for block in held]
            others = [
                swap(lax.dynamic_slice_in_dim(block, (1 - core) * width, width, 2))
                for block in held
            ]
            sides.append([(held, True), (others, False)])
            upward = core == 0
            there.append(
                [
                    jnp.where(upward, below(step), above(step)),
                    jnp.where(upward, above(step), below(step)),
                ]
            )
    else:
        stale = [stale_kv]
        from_below = from_above = stale_kv
        for step in range(1, planes):
            from_below = lax.ppermute(from_below, "patch", up_pairs(step))
            from_above = lax.ppermute(from_above, "patch", down_pairs(step))
            sides.append([([from_below], False), ([from_above], False)])
            there.append([below(step), above(step)])

    early = planes > 2
    inner = (plane > 0) & (plane < planes - 1)
    before = [side for step in sides[:-1] for side in step]
    flags = [flag for step in there[:-1] for flag in step]
    info = jnp.stack([core] + flags + [inner]).astype(jnp.int32)
    last_info = jnp.stack([core] + there[-1]).astype(jnp.int32)

    if early:
        text_attn = attend_text(info, 1 + len(flags), qkv, img_rows, stale, before)
    else:
        all_info = jnp.stack([core] + flags + there[-1] + [core >= 0]).astype(jnp.int32)
        text_attn = attend_text(
            all_info, 3 + len(flags), qkv, img_rows, stale, before + sides[-1]
        )
    state = attend_image(info, qkv, img_rows, stale, before, text_attn)
    text_back = exchange(text_attn)
    image_attn = attend_last(last_info, qkv, img_rows, state, sides[-1], text_back)

    text_out = unpack(text_back, order)
    if early:
        ends = [(1, 0), (planes - 2, planes - 1)]
        ends = [(a * pair + c, b * pair + c) for a, b in ends for c in range(pair)]
        text_out = jnp.where(inner, text_out, lax.ppermute(text_out, "patch", ends))
    if pair == 2:
        other = swap(text_out)
        lower = core == 0
        text_out = jnp.concatenate(
            [jnp.where(lower, text_out, other), jnp.where(lower, other, text_out)], 0
        )

    image_out = project(exchange(image_attn), order, proj_weight, residual, gate_scale)
    return (image_out, text_out)


def solution(mesh):
    return jax.shard_map(
        per_device,
        mesh=mesh,
        in_specs=(
            P(("patch", "head"), None),
            P("head", None),
            P(None, "patch", "head"),
            P(("patch", "head"), None),
            P(),
            P(),
        ),
        out_specs=(P(("patch", "head"), None), P("head", None)),
        check_vma=False,
    )
```

time: 218 us -> 117 us (0.54)
  the two profiles are of different devices: /device:TPU:0 before, /device:TPU:17 now
where the time goes in v6:
time: 117 us; the launch traced here: 116 us
  starting transfers between devices  43.2 us (37%)
  Pallas kernels  38.2 us (33%)
  local copies, waits for them, and re-layouts  16.7 us (14%)
  waiting for transfers between devices  14.6 us (12%)
  other arithmetic  2.11 us (2%)
    pallas_call x3, Pallas kernels, call_heads(): pl.pallas_call(body, grid_spec=pltpu.PrefetchScalarGridSpec(num_scalar_pr...  28.7 us
    ppermute x6, starting transfers between devices, per_device(): held = [lax.ppermute(block, 'patch', pairs) for block in held]  14.1 us
    ppermute x8, starting transfers between devices, swap(): return lax.ppermute(x, 'patch', swap_pairs)  13.8 us
    all_to_all x3, starting transfers between devices, exchange(): lax.all_to_all(x, ('patch', 'head'), split_axis=0, concat_axis=0, axis_in...  13.3 us
    all_to_all x3, waiting for transfers between devices, exchange(): lax.all_to_all(x, ('patch', 'head'), split_axis=0, concat_axis=0, axis_in...  10 us
    dynamic_slice x6, local copies, waits for them, and re-layouts, per_device(): lax.dynamic_slice_in_dim(block, (1 - core) * width, width, 2)  9.02 us
    pallas_call x1, Pallas kernels, project(): pl.pallas_call(functools.partial(project_body, order), in_specs=[vmem, pl...  7.82 us
    unnamed x18, local copies, waits for them, and re-layouts  7.61 us
  transfers between devices with their start and end apart: 18, of which 5 were waited for; matrix products, arithmetic and copies ran while one was open for 9% of the time, Pallas kernels for 33%

profile of v6, /device:TPU:17, one launch (start us, length us, event | category | flops | bytes accessed | tf_op | source)
XLA Modules:
  0.0 115.7 jit_solution(3859398041801932713)
XLA Ops:
  1.4 2.1 %collective-permute-start.1 = (bf16[2,256,768]{2,1,0:T(8,128)(2,1)}, bf16[2,256,768]{2,1,0:T(8,128)(2,1)S(1)}, u32[]{:S(2)}, u32[]{:S(2)}) collective-permute-start(bf16[2,256,768]{2,1,0:T(8,128)(2,1)} %refs_3_.3), channel_id=1, source_target_pairs={{0,8},{8,16},{16,24},{12,4},{20,12},{28,20},{1,9},{9,17},{17,25},{... | collective-permute-start | bytes 2359304 | tf_op jit(solution)/shard_map/ppermute | solution.py:474
  3.6 2.1 %collective-permute-start.2 = (bf16[2,256,768]{2,1,0:T(8,128)(2,1)}, bf16[2,256,768]{2,1,0:T(8,128)(2,1)}, u32[]{:S(2)}, u32[]{:S(2)}) collective-permute-start(bf16[2,256,768]{2,1,0:T(8,128)(2,1)} %collective-permute-done.refs_4_), channel_id=1, source_target_pairs={{0,8},{8,16},{16,24},{12,4},{20,12},{28,20},{1,9},{9,17},{17,25},{... | collective-permute-start | bytes 2359304 | tf_op jit(solution)/shard_map/ppermute | solution.py:474
  5.7 1.7 %copy-done.3 = bf16[128,9216]{1,0:T(8,128)(2,1)S(1)} copy-done((bf16[128,9216]{1,0:T(8,128)(2,1)S(1)}, bf16[128,9216]{1,0:T(8,128)(2,1)}, u32[]{:S(2)}) %copy-start.3) | copy-done | bytes 2359320
  7.4 1.3 %copy-done.6 = bf16[64,9216]{1,0:T(8,128)(2,1)S(1)} copy-done((bf16[64,9216]{1,0:T(8,128)(2,1)S(1)}, bf16[64,9216]{1,0:T(8,128)(2,1)}, u32[]{:S(2)}) %copy-start.6) | copy-done | bytes 1179672
  9.6 1.4 %copy-done = bf16[8,128,1152]{2,1,0:T(8,128)(2,1)} copy-done((bf16[8,128,1152]{2,1,0:T(8,128)(2,1)}, bf16[8,128,1152]{2,1,0:T(8,128)(2,1)S(1)}, u32[]{:S(2)}) %copy-start) | copy-done | bytes 2359320
  11.0 5.5 %all-to-all-start = ((bf16[8,128,1152]{2,1,0:T(8,128)(2,1)}), bf16[8,128,1152]{2,1,0:T(8,128)(2,1)S(1)}, u32[]{:S(2)}, u32[]{:S(2)}) async-start(bf16[8,128,1152]{2,1,0:T(8,128)(2,1)} %copy-done), calls=%async_computation | async-start | bytes 4718592 | tf_op jit(solution)/shard_map/all_to_all | solution.py:449
  16.5 3.9 %collective-permute-start.5 = (bf16[2,256,768]{2,1,0:T(8,128)(2,1)S(1)}, bf16[2,256,768]{2,1,0:T(8,128)(2,1)}, u32[]{:S(2)}, u32[]{:S(2)}) collective-permute-start(bf16[2,256,768]{2,1,0:T(8,128)(2,1)S(1)} %collective-permute-done.1.refs_5_), channel_id=1, source_target_pairs={{8,16},{16,24},{12,4},{20,12},{9,17},{17,25},{13,5},{21,13},{10,18... | collective-permute-start | bytes 2359304 | tf_op jit(solution)/shard_map/ppermute | solution.py:474
  20.4 2.8 %collective-permute-done.2.refs_6_ = bf16[2,256,768]{2,1,0:T(8,128)(2,1)} collective-permute-done((bf16[2,256,768]{2,1,0:T(8,128)(2,1)}, bf16[2,256,768]{2,1,0:T(8,128)(2,1)}, u32[]{:S(2)}, u32[]{:S(2)}) %collective-permute-start.2) | collective-permute-done | bytes 786464 | tf_op jit(solution)/shard_map/ppermute | solution.py:474
  23.1 3.0 %collective-permute-start.6 = (bf16[2,256,768]{2,1,0:T(8,128)(2,1)}, bf16[2,256,768]{2,1,0:T(8,128)(2,1)}, u32[]{:S(2)}, u32[]{:S(2)}) collective-permute-start(bf16[2,256,768]{2,1,0:T(8,128)(2,1)} %collective-permute-done.2.refs_6_), channel_id=1, source_target_pairs={{8,16},{16,24},{12,4},{20,12},{9,17},{17,25},{13,5},{21,13},{10,18... | collective-permute-start | bytes 2359304 | tf_op jit(solution)/shard_map/ppermute | solution.py:474
  26.1 1.5 %collective-permute-start.3 = (bf16[2,256,384]{2,1,0:T(8,128)(2,1)S(1)}, bf16[2,256,384]{2,1,0:T(8,128)(2,1)S(1)}, u32[]{:S(2)}, u32[]{:S(2)}) collective-permute-start(bf16[2,256,384]{2,1,0:T(8,128)(2,1)S(1)} %constant_dynamic-slice_fusion.5), channel_id=1, source_target_pairs={{0,4},{4,0},{8,12},{12,8},{16,20},{20,16},{24,28},{28,24},{1,5},{5... | collective-permute-start | bytes 1179656 | tf_op jit(solution)/shard_map/ppermute | solution.py:454
  27.6 1.8 %constant_dynamic-slice_fusion.4 = bf16[2,256,384]{2,1,0:T(8,128)(2,1)} fusion(bf16[2,256,768]{2,1,0:T(8,128)(2,1)} %collective-permute-done.2.refs_6_, s32[]{:T(128)S(6)} %select_n.64), kind=kLoop, calls=%fused_computation.8 | loop fusion | bytes 786436 | tf_op jit(solution)/shard_map/dynamic_slice | solution.py:476
  29.4 1.5 %collective-permute-start.9 = (bf16[2,256,768]{2,1,0:T(8,128)(2,1)}, bf16[2,256,768]{2,1,0:T(8,128)(2,1)}, u32[]{:S(2)}, u32[]{:S(2)}) collective-permute-start(bf16[2,256,768]{2,1,0:T(8,128)(2,1)} %collective-permute-done.5.refs_9_), channel_id=1, source_target_pairs={{16,24},{12,4},{17,25},{13,5},{18,26},{14,6},{19,27},{15,7}} | collective-permute-start | bytes 2359304 | tf_op jit(solution)/shard_map/ppermute | solution.py:474
  31.0 1.8 %constant_dynamic-slice_fusion.3 = bf16[2,256,384]{2,1,0:T(8,128)(2,1)} fusion(bf16[2,256,768]{2,1,0:T(8,128)(2,1)} %collective-permute-done.5.refs_9_, s32[]{:T(128)S(6)} %select_n.64), kind=kLoop, calls=%fused_computation.7 | loop fusion | bytes 786436 | tf_op jit(solution)/shard_map/dynamic_slice | solution.py:476
  32.8 5.8 %collective-permute-start.7 = (bf16[2,256,384]{2,1,0:T(8,128)(2,1)}, bf16[2,256,384]{2,1,0:T(8,128)(2,1)}, u32[]{:S(2)}, u32[]{:S(2)}) collective-permute-start(bf16[2,256,384]{2,1,0:T(8,128)(2,1)} %constant_dynamic-slice_fusion.3), channel_id=1, source_target_pairs={{0,4},{4,0},{8,12},{12,8},{16,20},{20,16},{24,28},{28,24},{1,5},{5... | collective-permute-start | bytes 1179656 | tf_op jit(solution)/shard_map/ppermute | solution.py:454
  38.6 1.6 %collective-permute-start.10 = (bf16[2,256,768]{2,1,0:T(8,128)(2,1)}, bf16[2,256,768]{2,1,0:T(8,128)(2,1)}, u32[]{:S(2)}, u32[]{:S(2)}) collective-permute-start(bf16[2,256,768]{2,1,0:T(8,128)(2,1)} %collective-permute-done.6.refs_10_), channel_id=1, source_target_pairs={{16,24},{12,4},{17,25},{13,5},{18,26},{14,6},{19,27},{15,7}} | collective-permute-start | bytes 2359304 | tf_op jit(solution)/shard_map/ppermute | solution.py:474
  40.2 1.8 %constant_dynamic-slice_fusion.2 = bf16[2,256,384]{2,1,0:T(8,128)(2,1)} fusion(bf16[2,256,768]{2,1,0:T(8,128)(2,1)} %collective-permute-done.6.refs_10_, s32[]{:T(128)S(6)} %select_n.64), kind=kLoop, calls=%fused_computation.6 | loop fusion | bytes 786436 | tf_op jit(solution)/shard_map/dynamic_slice | solution.py:476
  42.0 5.1 %collective-permute-start.8 = (bf16[2,256,384]{2,1,0:T(8,128)(2,1)}, bf16[2,256,384]{2,1,0:T(8,128)(2,1)}, u32[]{:S(2)}, u32[]{:S(2)}) collective-permute-start(bf16[2,256,384]{2,1,0:T(8,128)(2,1)} %constant_dynamic-slice_fusion.2), channel_id=1, source_target_pairs={{0,4},{4,0},{8,12},{12,8},{16,20},{20,16},{24,28},{28,24},{1,5},{5... | collective-permute-start | bytes 1179656 | tf_op jit(solution)/shard_map/ppermute | solution.py:454
  47.2 1.6 %collective-permute-done.8.refs_12_ = bf16[2,256,384]{2,1,0:T(8,128)(2,1)} collective-permute-done((bf16[2,256,384]{2,1,0:T(8,128)(2,1)}, bf16[2,256,384]{2,1,0:T(8,128)(2,1)}, u32[]{:S(2)}, u32[]{:S(2)}) %collective-permute-start.8) | collective-permute-done | bytes 393248 | tf_op jit(solution)/shard_map/ppermute | solution.py:454
  48.8 1.1 copy-done.1
  49.9 12.6 %attend_text.1.refs_13_ = bf16[8,64,384]{2,1,0:T(8,128)(2,1)} custom-call(s32[6]{0:T(128)S(1)} %stack.68.info, bf16[8,128,1152]{2,1,0:T(8,128)(2,1)S(1)} %all-to-all-done.refs_0_.refs_1_.refs_2_, bf16[8,128,1152]{2,1,0:T(8,128)(2,1)S(1)} %all-to-all-done.refs_0_.refs_1_.refs_2_, bf16[8,128,1152]{2,1,0:T(8,128)(2,1)S(1)} %all-to-all-done.refs_0_.refs_1_.refs_2_, ...), custom_call_target="tpu_custom_call" | custom-call | flops 1610612736 | bytes 3932160 | tf_op jit(solution)/shard_map/attend_text/pallas_call | solution.py:295
  62.5 4.1 %all-to-all-start.1 = ((bf16[8,64,384]{2,1,0:T(8,128)(2,1)}), bf16[8,64,384]{2,1,0:T(8,128)(2,1)S(1)}, u32[]{:S(2)}, u32[]{:S(2)}) async-start(bf16[8,64,384]{2,1,0:T(8,128)(2,1)} %attend_text.1.refs_13_), calls=%async_computation.1 | async-start | bytes 786432 | tf_op jit(solution)/shard_map/all_to_all | solution.py:449
  66.6 1.8 %constant_dynamic-slice_fusion.1 = bf16[2,256,384]{2,1,0:T(8,128)(2,1)} fusion(bf16[2,256,768]{2,1,0:T(8,128)(2,1)} %collective-permute-done.9.refs_3_, s32[]{:T(128)S(6)} %select_n.64), kind=kLoop, calls=%fused_computation.5 | loop fusion | bytes 786436 | tf_op jit(solution)/shard_map/dynamic_slice | solution.py:476
  68.4 1.8 %constant_dynamic-slice_fusion = bf16[2,256,384]{2,1,0:T(8,128)(2,1)} fusion(bf16[2,256,768]{2,1,0:T(8,128)(2,1)} %collective-permute-done.10.refs_4_, s32[]{:T(128)S(6)} %select_n.64), kind=kLoop, calls=%fused_computation.4 | loop fusion | bytes 786436 | tf_op jit(solution)/shard_map/dynamic_slice | solution.py:476
  70.7 3.6 %all-to-all-done.1.refs_7_.x_ref = bf16[8,64,384]{2,1,0:T(8,128)(2,1)S(1)} async-done(((bf16[8,64,384]{2,1,0:T(8,128)(2,1)}), bf16[8,64,384]{2,1,0:T(8,128)(2,1)S(1)}, u32[]{:S(2)}, u32[]{:S(2)}) %all-to-all-start.1) | async-done | bytes 393248 | tf_op jit(solution)/shard_map/all_to_all | solution.py:449
  75.1 2.0 %collective-permute-start.13 = (bf16[64,3072]{1,0:T(8,128)(2,1)}, bf16[64,3072]{1,0:T(8,128)(2,1)}, u32[]{:S(2)}, u32[]{:S(2)}) collective-permute-start(bf16[64,3072]{1,0:T(8,128)(2,1)} %unpack_text.1), channel_id=1, source_target_pairs={{8,0},{12,4},{16,24},{20,28},{9,1},{13,5},{17,25},{21,29},{10,2},{... | collective-permute-start | bytes 1179656 | tf_op jit(solution)/shard_map/ppermute | solution.py:518
  77.2 1.1 copy-done.2
  79.3 12.0 %attend_image.1 = (bf16[3,512,128]{2,1,0:T(8,128)(2,1)S(1)}, f32[3,512,256]{2,1,0:T(8,128)S(1)}) custom-call(s32[6]{0:T(128)S(1)} %stack.68.info, bf16[8,128,1152]{2,1,0:T(8,128)(2,1)S(1)} %all-to-all-done.refs_0_.refs_1_.refs_2_, bf16[8,128,1152]{2,1,0:T(8,128)(2,1)S(1)} %all-to-all-done.refs_0_.refs_1_.refs_2_, ...), custom_call_target="tpu_custom_call" | custom-call | flops 1610612736 | bytes 3932160 | tf_op jit(solution)/shard_map/attend_image/pallas_call | solution.py:295
  91.3 4.1 %attend_last.1 = bf16[8,64,384]{2,1,0:T(8,128)(2,1)} custom-call(s32[3]{0:T(128)S(1)} %pad_add_fusion.info, bf16[8,128,1152]{2,1,0:T(8,128)(2,1)S(1)} %all-to-all-done.refs_0_.refs_1_.refs_2_, bf16[3,512,128]{2,1,0:T(8,128)(2,1)S(1)} %get-tuple-element.4.refs_1_, f32[3,512,256]{2,1,0:T(8,128)S(1)} %get-tuple-element.5.refs_2_, ...), custom_call_target="tpu_custom_call" | custom-call | flops 402653184 | bytes 1572864 | tf_op jit(solution)/shard_map/attend_last/pallas_call | solution.py:295
  95.4 3.7 %all-to-all-start.2 = ((bf16[8,64,384]{2,1,0:T(8,128)(2,1)}), bf16[8,64,384]{2,1,0:T(8,128)(2,1)S(1)}, u32[]{:S(2)}, u32[]{:S(2)}) async-start(bf16[8,64,384]{2,1,0:T(8,128)(2,1)} %attend_last.1), calls=%async_computation.2 | async-start | bytes 786432 | tf_op jit(solution)/shard_map/all_to_all | solution.py:449
  99.2 1.0 broadcast_select_fusion
  100.4 6.4 %all-to-all-done.2.x_ref = bf16[8,64,384]{2,1,0:T(8,128)(2,1)S(1)} async-done(((bf16[8,64,384]{2,1,0:T(8,128)(2,1)}), bf16[8,64,384]{2,1,0:T(8,128)(2,1)S(1)}, u32[]{:S(2)}, u32[]{:S(2)}) %all-to-all-start.2) | async-done | bytes 393248 | tf_op jit(solution)/shard_map/all_to_all | solution.py:449
  106.8 7.8 %project.1 = bf16[64,3072]{1,0:T(8,128)(2,1)} custom-call(bf16[8,64,384]{2,1,0:T(8,128)(2,1)S(1)} %all-to-all-done.2.x_ref, bf16[8,384,3072]{2,1,0:T(8,128)(2,1)} %bitcast.11, bf16[64,3072]{1,0:T(8,128)(2,1)S(1)} %copy-done.7, f32[1,3072]{1,0:T(1,128)S(1)} %bitcast.10), custom_call_target="tpu_custom_call" | custom-call | flops 1207959552 | bytes 18874368 | tf_op jit(solution)/shard_map/project/pallas_call | solution.py:394
  (39 shorter events, 5.6 us)
Async XLA Ops:
  0.6 3.0 %collective-permute-start = (bf16[2,256,768]{2,1,0:T(8,128)(2,1)}, bf16[2,256,768]{2,1,0:T(8,128)(2,1)}, u32[]{:S(2)}, u32[]{:S(2)}) collective-permute-start(bf16[2,256,768]{2,1,0:T(8,128)(2,1)} %refs_3_.3), channel_id=1, source_target_pairs={{0,4},{4,0},{8,12},{12,8},{16,20},{20,16},{24,28},{28,24},{1,5},{5... | collective-permute-start | bytes 2359304 | tf_op jit(solution)/shard_map/ppermute | solution.py:454
  1.4 15.1 %collective-permute-start.1 = (bf16[2,256,768]{2,1,0:T(8,128)(2,1)}, bf16[2,256,768]{2,1,0:T(8,128)(2,1)S(1)}, u32[]{:S(2)}, u32[]{:S(2)}) collective-permute-start(bf16[2,256,768]{2,1,0:T(8,128)(2,1)} %refs_3_.3), channel_id=1, source_target_pairs={{0,8},{8,16},{16,24},{12,4},{20,12},{28,20},{1,9},{9,17},{17,25},{... | collective-permute-start | bytes 2359304 | tf_op jit(solution)/shard_map/ppermute | solution.py:474
  3.6 19.5 %collective-permute-start.2 = (bf16[2,256,768]{2,1,0:T(8,128)(2,1)}, bf16[2,256,768]{2,1,0:T(8,128)(2,1)}, u32[]{:S(2)}, u32[]{:S(2)}) collective-permute-start(bf16[2,256,768]{2,1,0:T(8,128)(2,1)} %collective-permute-done.refs_4_), channel_id=1, source_target_pairs={{0,8},{8,16},{16,24},{12,4},{20,12},{28,20},{1,9},{9,17},{17,25},{... | collective-permute-start | bytes 2359304 | tf_op jit(solution)/shard_map/ppermute | solution.py:474
  5.7 1.7 %copy-start.3 = (bf16[128,9216]{1,0:T(8,128)(2,1)S(1)}, bf16[128,9216]{1,0:T(8,128)(2,1)}, u32[]{:S(2)}) copy-start(bf16[128,9216]{1,0:T(8,128)(2,1)} %txt.1) | copy-start | bytes 7077892
  7.4 1.3 %copy-start.6 = (bf16[64,9216]{1,0:T(8,128)(2,1)S(1)}, bf16[64,9216]{1,0:T(8,128)(2,1)}, u32[]{:S(2)}) copy-start(bf16[64,9216]{1,0:T(8,128)(2,1)} %img.1) | copy-start | bytes 3538948
  9.6 1.4 %copy-start = (bf16[8,128,1152]{2,1,0:T(8,128)(2,1)}, bf16[8,128,1152]{2,1,0:T(8,128)(2,1)S(1)}, u32[]{:S(2)}) copy-start(bf16[8,128,1152]{2,1,0:T(8,128)(2,1)S(1)} %pack_heads.1) | copy-start | bytes 7077892
  11.0 36.2 %all-to-all-start = ((bf16[8,128,1152]{2,1,0:T(8,128)(2,1)}), bf16[8,128,1152]{2,1,0:T(8,128)(2,1)S(1)}, u32[]{:S(2)}, u32[]{:S(2)}) async-start(bf16[8,128,1152]{2,1,0:T(8,128)(2,1)} %copy-done), calls=%async_computation | async-start | bytes 4718592 | tf_op jit(solution)/shard_map/all_to_all | solution.py:449
  16.5 12.9 %collective-permute-start.5 = (bf16[2,256,768]{2,1,0:T(8,128)(2,1)S(1)}, bf16[2,256,768]{2,1,0:T(8,128)(2,1)}, u32[]{:S(2)}, u32[]{:S(2)}) collective-permute-start(bf16[2,256,768]{2,1,0:T(8,128)(2,1)S(1)} %collective-permute-done.1.refs_5_), channel_id=1, source_target_pairs={{8,16},{16,24},{12,4},{20,12},{9,17},{17,25},{13,5},{21,13},{10,18... | collective-permute-start | bytes 2359304 | tf_op jit(solution)/shard_map/ppermute | solution.py:474
  23.1 15.5 %collective-permute-start.6 = (bf16[2,256,768]{2,1,0:T(8,128)(2,1)}, bf16[2,256,768]{2,1,0:T(8,128)(2,1)}, u32[]{:S(2)}, u32[]{:S(2)}) collective-permute-start(bf16[2,256,768]{2,1,0:T(8,128)(2,1)} %collective-permute-done.2.refs_6_), channel_id=1, source_target_pairs={{8,16},{16,24},{12,4},{20,12},{9,17},{17,25},{13,5},{21,13},{10,18... | collective-permute-start | bytes 2359304 | tf_op jit(solution)/shard_map/ppermute | solution.py:474
  26.1 15.9 %collective-permute-start.3 = (bf16[2,256,384]{2,1,0:T(8,128)(2,1)S(1)}, bf16[2,256,384]{2,1,0:T(8,128)(2,1)S(1)}, u32[]{:S(2)}, u32[]{:S(2)}) collective-permute-start(bf16[2,256,384]{2,1,0:T(8,128)(2,1)S(1)} %constant_dynamic-slice_fusion.5), channel_id=1, source_target_pairs={{0,4},{4,0},{8,12},{12,8},{16,20},{20,16},{24,28},{28,24},{1,5},{5... | collective-permute-start | bytes 1179656 | tf_op jit(solution)/shard_map/ppermute | solution.py:454
  29.4 17.8 %collective-permute-start.4 = (bf16[2,256,384]{2,1,0:T(8,128)(2,1)}, bf16[2,256,384]{2,1,0:T(8,128)(2,1)}, u32[]{:S(2)}, u32[]{:S(2)}) collective-permute-start(bf16[2,256,384]{2,1,0:T(8,128)(2,1)} %constant_dynamic-slice_fusion.4), channel_id=1, source_target_pairs={{0,4},{4,0},{8,12},{12,8},{16,20},{20,16},{24,28},{28,24},{1,5},{5... | collective-permute-start | bytes 1179656 | tf_op jit(solution)/shard_map/ppermute | solution.py:454
  29.4 37.2 %collective-permute-start.9 = (bf16[2,256,768]{2,1,0:T(8,128)(2,1)}, bf16[2,256,768]{2,1,0:T(8,128)(2,1)}, u32[]{:S(2)}, u32[]{:S(2)}) collective-permute-start(bf16[2,256,768]{2,1,0:T(8,128)(2,1)} %collective-permute-done.5.refs_9_), channel_id=1, source_target_pairs={{16,24},{12,4},{17,25},{13,5},{18,26},{14,6},{19,27},{15,7}} | collective-permute-start | bytes 2359304 | tf_op jit(solution)/shard_map/ppermute | solution.py:474
  32.8 14.4 %collective-permute-start.7 = (bf16[2,256,384]{2,1,0:T(8,128)(2,1)}, bf16[2,256,384]{2,1,0:T(8,128)(2,1)}, u32[]{:S(2)}, u32[]{:S(2)}) collective-permute-start(bf16[2,256,384]{2,1,0:T(8,128)(2,1)} %constant_dynamic-slice_fusion.3), channel_id=1, source_target_pairs={{0,4},{4,0},{8,12},{12,8},{16,20},{20,16},{24,28},{28,24},{1,5},{5... | collective-permute-start | bytes 1179656 | tf_op jit(solution)/shard_map/ppermute | solution.py:454
  38.6 29.8 %collective-permute-start.10 = (bf16[2,256,768]{2,1,0:T(8,128)(2,1)}, bf16[2,256,768]{2,1,0:T(8,128)(2,1)}, u32[]{:S(2)}, u32[]{:S(2)}) collective-permute-start(bf16[2,256,768]{2,1,0:T(8,128)(2,1)} %collective-permute-done.6.refs_10_), channel_id=1, source_target_pairs={{16,24},{12,4},{17,25},{13,5},{18,26},{14,6},{19,27},{15,7}} | collective-permute-start | bytes 2359304 | tf_op jit(solution)/shard_map/ppermute | solution.py:474
  42.0 20.5 %copy-start.4 = (bf16[2,256,384]{2,1,0:T(8,128)(2,1)}, bf16[2,256,384]{2,1,0:T(8,128)(2,1)S(1)}, u32[]{:S(2)}) copy-start(bf16[2,256,384]{2,1,0:T(8,128)(2,1)S(1)} %collective-permute-done.3.refs_7_) | copy-start | bytes 1179652
  42.0 6.8 %collective-permute-start.8 = (bf16[2,256,384]{2,1,0:T(8,128)(2,1)}, bf16[2,256,384]{2,1,0:T(8,128)(2,1)}, u32[]{:S(2)}, u32[]{:S(2)}) collective-permute-start(bf16[2,256,384]{2,1,0:T(8,128)(2,1)} %constant_dynamic-slice_fusion.2), channel_id=1, source_target_pairs={{0,4},{4,0},{8,12},{12,8},{16,20},{20,16},{24,28},{28,24},{1,5},{5... | collective-permute-start | bytes 1179656 | tf_op jit(solution)/shard_map/ppermute | solution.py:454
  48.8 1.1 copy-start.1
  62.5 11.7 %all-to-all-start.1 = ((bf16[8,64,384]{2,1,0:T(8,128)(2,1)}), bf16[8,64,384]{2,1,0:T(8,128)(2,1)S(1)}, u32[]{:S(2)}, u32[]{:S(2)}) async-start(bf16[8,64,384]{2,1,0:T(8,128)(2,1)} %attend_text.1.refs_13_), calls=%async_computation.1 | async-start | bytes 786432 | tf_op jit(solution)/shard_map/all_to_all | solution.py:449
  68.4 22.9 %collective-permute-start.11 = (bf16[2,256,384]{2,1,0:T(8,128)(2,1)}, bf16[2,256,384]{2,1,0:T(8,128)(2,1)}, u32[]{:S(2)}, u32[]{:S(2)}) collective-permute-start(bf16[2,256,384]{2,1,0:T(8,128)(2,1)} %constant_dynamic-slice_fusion.1), channel_id=1, source_target_pairs={{0,4},{4,0},{8,12},{12,8},{16,20},{20,16},{24,28},{28,24},{1,5},{5... | collective-permute-start | bytes 1179656 | tf_op jit(solution)/shard_map/ppermute | solution.py:454
  70.2 21.1 %collective-permute-start.12 = (bf16[2,256,384]{2,1,0:T(8,128)(2,1)}, bf16[2,256,384]{2,1,0:T(8,128)(2,1)}, u32[]{:S(2)}, u32[]{:S(2)}) collective-permute-start(bf16[2,256,384]{2,1,0:T(8,128)(2,1)} %constant_dynamic-slice_fusion), channel_id=1, source_target_pairs={{0,4},{4,0},{8,12},{12,8},{16,20},{20,16},{24,28},{28,24},{1,5},{5... | collective-permute-start | bytes 1179656 | tf_op jit(solution)/shard_map/ppermute | solution.py:454
  75.1 24.1 %collective-permute-start.13 = (bf16[64,3072]{1,0:T(8,128)(2,1)}, bf16[64,3072]{1,0:T(8,128)(2,1)}, u32[]{:S(2)}, u32[]{:S(2)}) collective-permute-start(bf16[64,3072]{1,0:T(8,128)(2,1)} %unpack_text.1), channel_id=1, source_target_pairs={{8,0},{12,4},{16,24},{20,28},{9,1},{13,5},{17,25},{21,29},{10,2},{... | collective-permute-start | bytes 1179656 | tf_op jit(solution)/shard_map/ppermute | solution.py:518
  77.2 1.1 copy-start.2
  78.3 1.0 copy-start.5
  95.4 11.4 %copy-start.7 = (bf16[64,3072]{1,0:T(8,128)(2,1)S(1)}, bf16[64,3072]{1,0:T(8,128)(2,1)}, u32[]{:S(2)}) copy-start(bf16[64,3072]{1,0:T(8,128)(2,1)} %residual.1) | copy-start | bytes 1179652
  95.4 11.4 %copy-start.8 = (f32[3072]{0:T(1024)S(1)}, f32[3072]{0:T(1024)}, u32[]{:S(2)}) copy-start(f32[3072]{0:T(1024)} %param.10) | copy-start | bytes 36868
  95.4 11.4 %all-to-all-start.2 = ((bf16[8,64,384]{2,1,0:T(8,128)(2,1)}), bf16[8,64,384]{2,1,0:T(8,128)(2,1)S(1)}, u32[]{:S(2)}, u32[]{:S(2)}) async-start(bf16[8,64,384]{2,1,0:T(8,128)(2,1)} %attend_last.1), calls=%async_computation.2 | async-start | bytes 786432 | tf_op jit(solution)/shard_map/all_to_all | solution.py:449
  100.2 14.4 %collective-permute-start.14 = (bf16[64,3072]{1,0:T(8,128)(2,1)S(1)}, bf16[64,3072]{1,0:T(8,128)(2,1)S(1)}, u32[]{:S(2)}, u32[]{:S(2)}) collective-permute-start(bf16[64,3072]{1,0:T(8,128)(2,1)S(1)} %broadcast_select_fusion), channel_id=1, source_target_pairs={{0,4},{4,0},{8,12},{12,8},{16,20},{20,16},{24,28},{28,24},{1,5},{5... | collective-permute-start | bytes 1179656 | tf_op jit(solution)/shard_map/ppermute | solution.py:454

commit v7 on v6

v7 whole, which is shorter than its diff:
```python
import functools
import math

import jax
import jax.numpy as jnp
from jax import lax
from jax.experimental import pallas as pl
from jax.experimental.pallas import tpu as pltpu
from jax.sharding import PartitionSpec as P

HD = 128
SCALE = math.log2(math.e) / math.sqrt(HD)
VMEM_LIMIT = 12 * 1024 * 1024
WIDE_LIMIT = 60 * 1024 * 1024
TILE = 256
FIRST_KEYS = 256
LARGE = 2.0**60


def params(block_elements=0):
    return pltpu.CompilerParams(
        vmem_limit_bytes=VMEM_LIMIT + 4 * block_elements, dimension_semantics=("arbitrary",)
    )


def pack_body(rows, places, width, first_block, array, *refs):
    packed, sem = refs[-2:]
    model = array.shape[1] // 3
    first = pl.multiple_of(first_block[0] * rows, rows)
    copies = []
    for destination, place in enumerate(places):
        for part in range(3):
            copies.append(
                pltpu.make_async_copy(
                    array.at[pl.ds(first, rows), pl.ds(part * model + place * width, width)],
                    packed.at[destination, :, pl.ds(part * width, width)],
                    sem.at[len(copies)],
                )
            )
    for copy in copies:
        copy.start()
    for copy in copies:
        copy.wait()


def pack(first_block, array, rows, places, width, after=()):
    anywhere = pl.BlockSpec(memory_space=pl.ANY)
    return pl.pallas_call(
        functools.partial(pack_body, rows, places, width),
        in_specs=[pl.BlockSpec(memory_space=pltpu.SMEM)] + [anywhere] * (1 + len(after)),
        out_specs=anywhere,
        out_shape=jax.ShapeDtypeStruct((len(places), rows, 3 * width), array.dtype),
        scratch_shapes=[pltpu.SemaphoreType.DMA((3 * len(places),))],
        compiler_params=pltpu.CompilerParams(vmem_limit_bytes=WIDE_LIMIT),
        name="pack_heads",
    )(first_block, array, *after)


def dot(first, second, contract):
    return lax.dot_general(
        first, second, ((contract[:1], contract[1:]), ((), ())), preferred_element_type=jnp.float32
    )


def with_ones(block):
    return jnp.concatenate([block, jnp.ones_like(block)], axis=1)


def reference_columns(row_max):
    reference = row_max.astype(jnp.bfloat16).astype(jnp.float32)
    return jnp.broadcast_to(reference * (-1.0 / HD), (row_max.shape[0], HD)).astype(jnp.bfloat16)


def weighted(queries, key_rows, values):
    weights = jnp.exp2(dot(queries, key_rows, (1, 1)) * SCALE).astype(jnp.bfloat16)
    return dot(weights, values, (1, 0))


def tiles_of(rows):
    tile = min(TILE, rows)
    return [slice(first, min(first + tile, rows)) for first in range(0, rows, tile)]


def until_small(flag, total, attempt):
    flag[0] = 1

    @pl.loop(0, 2)
    def _(turn):
        @pl.when(flag[0] == 1)
        def _():
            attempt(turn)
            flag[0] = jnp.where(jnp.max(total[:, HD:]) > LARGE, 1, 0).astype(jnp.int32)


class Sides:
    def __init__(self, sides, heads):
        self.operands = [block for blocks in sides for block in blocks]
        self.specs = [stale_spec(block, heads) for block in self.operands]
        self.counts = [len(blocks) for blocks in sides]

    def each(self, info, refs, act):
        for index, count in enumerate(self.counts):
            blocks, refs = refs[:count], refs[count:]

            @pl.when(info[1 + index] == 1)
            def _():
                act(
                    jnp.concatenate([block[0] for block in blocks], 0),
                    jnp.concatenate([block[1] for block in blocks], 0),
                )


def stale_spec(block, heads):
    shape = (2, block.shape[1], HD)
    return pl.BlockSpec(shape, lambda h, info: (0, 0, info[0] * heads + h))


def column_spec(shape, offset=0):
    return pl.BlockSpec(shape[:2] + (HD,), lambda h, info: (0, 0, offset + h))


def accumulate(flag, total, aug, shift, queries, first_keys, own, each_arrived):
    rows = total.shape[0]

    def scored(span, key_rows):
        return dot(queries[span, :], key_rows, (1, 1))

    def raise_to(span, key_rows):
        row_max = jnp.max(scored(span, key_rows), axis=1, keepdims=True)
        shift[span, :] = jnp.maximum(shift[span, :], jnp.broadcast_to(row_max, shift[span, :].shape))

    def attempt(turn):
        @pl.when(turn == 0)
        def _():
            for tile in tiles_of(rows):
                row_max = jnp.max(scored(tile, first_keys), axis=1, keepdims=True)
                aug[tile, :] = reference_columns(row_max)

        @pl.when(turn == 1)
        def _():
            shift[...] = jnp.full_like(shift, -jnp.inf)
            for span, key_rows, _ in own:
                raise_to(span, key_rows)
            each_arrived(lambda key_rows, _: raise_to(slice(0, rows), key_rows))
            aug[...] = reference_columns(shift[:, :1])

        def add(span, key_rows, values):
            both = jnp.concatenate([queries[span, :], aug[span, :]], axis=1)
            total[span, :] += weighted(both, with_ones(key_rows), with_ones(values))

        total[...] = jnp.zeros_like(total)
        for span, key_rows, values in own:
            for tile in tiles_of(span.stop - span.start):
                add(slice(span.start + tile.start, span.start + tile.stop), key_rows, values)

        def add_everywhere(key_rows, values):
            for tile in tiles_of(rows):
                add(tile, key_rows, values)

        each_arrived(add_everywhere)

    until_small(flag, total, attempt)


def flat(block):
    return block[...].reshape(-1, HD)


def text_body(pair, sides, wanted, info, *refs):
    q_ref, k_ref, v_ref = refs[:3]
    stale, arrived = refs[3 : 3 + pair], refs[3 + pair : 3 + pair + len(sides.operands)]
    out, aug, total, shift, flag = refs[3 + pair + len(sides.operands) :]

    @pl.when(info[wanted] == 1)
    def _():
        rows = total.shape[0]
        text_keys, text_values = flat(k_ref), flat(v_ref)
        everywhere = slice(0, rows)
        own = [
            (everywhere, text_keys, text_values),
            (
                everywhere,
                jnp.concatenate([block[0] for block in stale], 0),
                jnp.concatenate([block[1] for block in stale], 0),
            ),
        ]
        accumulate(
            flag, total, aug, shift, flat(q_ref), text_keys[: min(FIRST_KEYS, rows), :], own,
            functools.partial(sides.each, info, arrived),
        )
        attended = (total[:, :HD] / total[:, HD:]).astype(out.dtype)
        out[...] = attended.reshape(out.shape)


def image_body(pair, sides, info, *refs):
    q_ref, k_ref, v_ref, text_k_ref, text_v_ref = refs[:5]
    stale, arrived = refs[5 : 5 + pair], refs[5 + pair : 5 + pair + len(sides.operands)]
    out, aug, total, shift, flag = refs[6 + pair + len(sides.operands) :]
    rows = total.shape[0]
    core = info[0]
    img_keys, img_values = flat(k_ref), flat(v_ref)
    text_keys, text_values = flat(text_k_ref), flat(text_v_ref)
    group_rows = rows // pair
    own = [(slice(0, rows), text_keys, text_values)]
    for group in range(pair):
        span = slice(group * group_rows, (group + 1) * group_rows)
        key_rows, values = [img_keys[span, :]], [img_values[span, :]]
        if pair == 2:
            mine = core == group
            key_rows.append(jnp.where(mine, stale[1][0], stale[0][0]))
            values.append(jnp.where(mine, stale[1][1], stale[0][1]))
        own.append((span, jnp.concatenate(key_rows, 0), jnp.concatenate(values, 0)))
    accumulate(
        flag, total, aug, shift, flat(q_ref),
        text_keys[: min(FIRST_KEYS, text_keys.shape[0]), :], own,
        functools.partial(sides.each, info, arrived),
    )
    attended = (total[:, :HD] / total[:, HD:]).astype(out.dtype)
    out[...] = attended.reshape(out.shape)


def attend_cost(queries, keys, heads):
    return pl.CostEstimate(
        flops=4 * queries * keys * heads * HD,
        bytes_accessed=4 * queries * heads * HD + 4 * keys * heads * HD,
        transcendentals=queries * keys * heads,
    )


def call_heads(body, name, heads, info, operands, specs, outs, out_specs, scratch, cost):
    return pl.pallas_call(
        body,
        grid_spec=pltpu.PrefetchScalarGridSpec(
            num_scalar_prefetch=1,
            grid=(heads,),
            in_specs=specs,
            out_specs=out_specs,
            scratch_shapes=scratch,
        ),
        out_shape=outs,
        compiler_params=params(
            sum(math.prod(spec.block_shape) for spec in specs if spec.block_shape is not None)
        ),
        cost_estimate=cost,
        name=name,
    )(info, *operands)


def scratch_of(rows):
    return [
        pltpu.VMEM((rows, HD), jnp.bfloat16),
        pltpu.VMEM((rows, 2 * HD), jnp.float32),
        pltpu.VMEM((rows, HD), jnp.float32),
        pltpu.SMEM((1,), jnp.int32),
    ]


def attend_text(info, wanted, txt, stale, sides):
    heads = txt.shape[2] // (3 * HD)
    sides = Sides(sides, heads)
    rows = txt.shape[0] * txt.shape[1]
    out = jax.ShapeDtypeStruct(txt.shape[:2] + (heads * HD,), txt.dtype)
    return call_heads(
        functools.partial(text_body, len(stale), sides, wanted),
        "attend_text", heads, info, [txt] * 3 + list(stale) + sides.operands,
        [column_spec(txt.shape, part * heads) for part in range(3)]
        + [stale_spec(block, heads) for block in stale]
        + sides.specs,
        out, column_spec(out.shape), scratch_of(rows), attend_cost(rows, 4 * rows, heads),
    )


def attend_image(info, img, txt, stale, sides, after):
    heads = img.shape[2] // (3 * HD)
    sides = Sides(sides, heads)
    rows = img.shape[0] * img.shape[1]
    out = jax.ShapeDtypeStruct(img.shape[:2] + (heads * HD,), img.dtype)
    return call_heads(
        functools.partial(image_body, len(stale), sides),
        "attend_image", heads, info,
        [img] * 3 + [txt] * 2 + list(stale) + sides.operands + [after],
        [column_spec(img.shape, part * heads) for part in range(3)]
        + [column_spec(txt.shape, part * heads) for part in (1, 2)]
        + [stale_spec(block, heads) for block in stale]
        + sides.specs
        + [pl.BlockSpec(memory_space=pl.ANY)],
        out, column_spec(out.shape), scratch_of(rows), attend_cost(rows, 5 * rows, heads),
    )


def project_body(order, x_ref, weight, residual, gate, out, held, total, sems):
    copies = [
        pltpu.make_async_copy(weight.at[place], held.at[place], sems.at[place])
        for place in order
    ]
    for copy in copies:
        copy.start()
    for source, (place, copy) in enumerate(zip(order, copies)):
        copy.wait()
        part = jnp.dot(x_ref[source], held[place], preferred_element_type=jnp.float32)
        if source == 0:
            total[...] = part
        else:
            total[...] += part
    out[...] = (residual[...].astype(jnp.float32) + gate[...] * total[...]).astype(out.dtype)


def project(x, order, weight, residual, gate):
    rows, model = residual.shape
    destinations, _, width = x.shape
    vmem = pl.BlockSpec(memory_space=pltpu.VMEM)
    return pl.pallas_call(
        functools.partial(project_body, order),
        in_specs=[vmem, pl.BlockSpec(memory_space=pl.ANY), vmem, vmem],
        out_specs=vmem,
        out_shape=jax.ShapeDtypeStruct((rows, model), residual.dtype),
        scratch_shapes=[
            pltpu.VMEM((destinations, width, model), weight.dtype),
            pltpu.VMEM((rows, model), jnp.float32),
            pltpu.SemaphoreType.DMA((destinations,)),
        ],
        compiler_params=pltpu.CompilerParams(vmem_limit_bytes=WIDE_LIMIT),
        cost_estimate=pl.CostEstimate(
            flops=2 * rows * model * model, bytes_accessed=2 * model * model, transcendentals=0
        ),
        name="project",
    )(x, weight.reshape(destinations, width, model), residual, gate.reshape(1, model))


def unpack_body(order, x_ref, out):
    width = x_ref.shape[2]
    for source, place in enumerate(order):
        out[:, place * width : (place + 1) * width] = x_ref[source]


def unpack(x, order):
    rows, model = x.shape[1], x.shape[0] * x.shape[2]
    return pl.pallas_call(
        functools.partial(unpack_body, order),
        grid=(1,),
        in_specs=[pl.BlockSpec(x.shape, lambda n: (0, 0, 0))],
        out_specs=pl.BlockSpec((rows, model), lambda n: (0, 0)),
        out_shape=jax.ShapeDtypeStruct((rows, model), x.dtype),
        compiler_params=params(),
        name="unpack_text",
    )(x)


def per_device(img_qkv, txt_qkv, stale_kv, residual, gate_scale, proj_weight):
    patches, head_owners = lax.axis_size("patch"), lax.axis_size("head")
    patch = lax.axis_index("patch")
    owned_heads = stale_kv.shape[2] // HD
    pair = 2 if patches % 2 == 0 and owned_heads % 2 == 0 else 1
    planes = patches // pair
    plane, core = patch // pair, patch % pair
    width = stale_kv.shape[2] // pair
    heads = width // HD
    img_rows, model = residual.shape
    text_rows = txt_qkv.shape[0] // pair
    destinations = pair * head_owners

    order = [(d % head_owners) * pair + d // head_owners for d in range(destinations)]
    groups = [[g * destinations + d for d in range(destinations)] for g in range(planes)]
    swap_pairs = [(p, p + 1 - 2 * (p % 2)) for p in range(patches)]

    def exchange(x):
        return lax.all_to_all(
            x, ("patch", "head"), split_axis=0, concat_axis=0, axis_index_groups=groups, tiled=True
        )

    def swap(x):
        return lax.ppermute(x, "patch", swap_pairs)

    def up_pairs(step):
        return [(z, z + 1) for z in range(step - 1, planes - 1)]

    def down_pairs(step):
        return [(z + 1, z) for z in range(0, planes - step)]

    core_only = core.astype(jnp.int32).reshape(1)
    txt = exchange(pack(core_only, txt_qkv, text_rows, order, width))

    sides, there = [], []
    above = lambda step: plane + step < planes
    below = lambda step: plane >= step
    if pair == 2:
        stale = [stale_kv, swap(stale_kv)]
        held = [stale_kv, stale_kv]
        for step in range(1, planes):
            pairs = [
                [(2 * a + turn, 2 * b) for a, b in up_pairs(step)]
                + [(2 * a + 1 - turn, 2 * b + 1) for a, b in down_pairs(step)]
                for turn in ((0, 1) if step == 1 else (0, 0))
            ]
            held = [lax.ppermute(block, "patch", way) for block, way in zip(held, pairs)]
            sides += [held, [swap(block) for block in held]]
            upward = core == 0
            there += [
                jnp.where(upward, below(step), above(step)),
                jnp.where(upward, above(step), below(step)),
            ]
    else:
        stale = [stale_kv]
        from_below = from_above = stale_kv
        for step in range(1, planes):
            from_below = lax.ppermute(from_below, "patch", up_pairs(step))
            from_above = lax.ppermute(from_above, "patch", down_pairs(step))
            sides += [[from_below], [from_above]]
            there += [below(step), above(step)]
    zero_only = jnp.zeros((1,), jnp.int32)
    img = exchange(pack(zero_only, img_qkv, img_rows, order, width, [txt] + sides[0]))

    early = planes > 2
    inner = (plane > 0) & (plane < planes - 1)
    known = len(sides) - 2 if early else len(sides)
    wanted = inner if early else core >= 0
    info = jnp.stack([core] + there[:known] + [wanted]).astype(jnp.int32)
    text_attn = attend_text(info, 1 + known, txt, stale, sides[:known])
    info = jnp.stack([core] + there).astype(jnp.int32)
    image_attn = attend_image(info, img, txt, stale, sides, text_attn)
    text_back = exchange(text_attn)

    text_out = unpack(text_back, order)
    if early:
        ends = [(1, 0), (planes - 2, planes - 1)]
        ends = [(a * pair + c, b * pair + c) for a, b in ends for c in range(pair)]
        text_out = jnp.where(inner, text_out, lax.ppermute(text_out, "patch", ends))
    if pair == 2:
        other = swap(text_out)
        lower = core == 0
        text_out = jnp.concatenate(
            [jnp.where(lower, text_out, other), jnp.where(lower, other, text_out)], 0
        )

    image_out = project(exchange(image_attn), order, proj_weight, residual, gate_scale)
    return (image_out, text_out)


def solution(mesh):
    return jax.shard_map(
        per_device,
        mesh=mesh,
        in_specs=(
            P(("patch", "head"), None),
            P("head", None),
            P(None, "patch", "head"),
            P(("patch", "head"), None),
            P(),
            P(),
        ),
        out_specs=(P(("patch", "head"), None), P("head", None)),
        check_vma=False,
    )
```

time: 117 us -> 210 us (1.79); the launches traced: 116 us -> 206 us
  Pallas kernels: 38.2 us -> 109 us
  waiting for transfers between devices: 14.6 us -> 45.5 us
  starting transfers between devices: 43.2 us -> 31.6 us
  local copies, waits for them, and re-layouts: 16.7 us -> 5.47 us
  blocking collectives: 0 us -> 10.4 us
    pallas_call x1 -> x2, Pallas kernels: 0.9 us -> 74.1 us  [pack(): pl.pallas_call(functools.partial(pack_body, rows, places, width), in_spec...]
    all_to_all x3, waiting for transfers between devices: 10 us -> 28.1 us  [exchange(): lax.all_to_all(x, ('patch', 'head'), split_axis=0, concat_axis=0, axis_in...]
    ppermute x6, waiting for transfers between devices: 2.78 us -> 14.8 us  [per_device(): lax.ppermute(block, 'patch', way)]
    ppermute x8, starting transfers between devices: 13.8 us -> 1.94 us  [swap(): return lax.ppermute(x, 'patch', swap_pairs)]
    all_to_all x0 -> x1, blocking collectives: none -> 10.4 us  [exchange(): lax.all_to_all(x, ('patch', 'head'), split_axis=0, concat_axis=0, axis_in...]
    dynamic_slice x6 -> x0, local copies, waits for them, and re-layouts: 9.02 us -> none  [per_device(): lax.dynamic_slice_in_dim(block, (1 - core) * width, width, 2)]
    pallas_call x3 -> x2, Pallas kernels: 28.7 us -> 24.8 us  [call_heads(): pl.pallas_call(body, grid_spec=pltpu.PrefetchScalarGridSpec(num_scalar_pr...]
    unnamed x18 -> x20, local copies, waits for them, and re-layouts: 7.61 us -> 5.31 us
  transfers between devices with their start and end apart: 18 -> 18, of which waited for: 5 -> 6; matrix products, arithmetic and copies ran while one was open for 9% -> 2% of each run, Pallas kernels for 33% -> 48%
where the time goes in v7:
time: 210 us; the launch traced here: 206 us
  Pallas kernels  109 us (52%)
  waiting for transfers between devices  45.5 us (22%)
  starting transfers between devices  31.6 us (15%)
  blocking collectives  10.4 us (5%)
  local copies, waits for them, and re-layouts  5.47 us (3%)
  other arithmetic  3.9 us (2%)
    pallas_call x2, Pallas kernels, pack(): pl.pallas_call(functools.partial(pack_body, rows, places, width), in_spec...  74.1 us
    all_to_all x3, waiting for transfers between devices, exchange(): lax.all_to_all(x, ('patch', 'head'), split_axis=0, concat_axis=0, axis_in...  28.1 us
    pallas_call x2, Pallas kernels, call_heads(): pl.pallas_call(body, grid_spec=pltpu.PrefetchScalarGridSpec(num_scalar_pr...  24.8 us
    ppermute x6, waiting for transfers between devices, per_device(): lax.ppermute(block, 'patch', way)  14.8 us
    all_to_all x3, starting transfers between devices, exchange(): lax.all_to_all(x, ('patch', 'head'), split_axis=0, concat_axis=0, axis_in...  14.4 us
    ppermute x6, starting transfers between devices, per_device(): lax.ppermute(block, 'patch', way)  13.3 us
    all_to_all x1, blocking collectives, exchange(): lax.all_to_all(x, ('patch', 'head'), split_axis=0, concat_axis=0, axis_in...  10.4 us
    pallas_call x1, Pallas kernels, project(): pl.pallas_call(functools.partial(project_body, order), in_specs=[vmem, pl...  8.93 us
  transfers between devices with their start and end apart: 18, of which 6 were waited for; matrix products, arithmetic and copies ran while one was open for 2% of the time, Pallas kernels for 48%

profile of v7, /device:TPU:17, one launch (start us, length us, event | category | flops | bytes accessed | tf_op | source)
XLA Modules:
  0.0 206.4 jit_solution(9491535121590063024)
XLA Ops:
  0.6 2.1 %collective-permute-start = (bf16[2,256,768]{2,1,0:T(8,128)(2,1)}, bf16[2,256,768]{2,1,0:T(8,128)(2,1)S(1)}, u32[]{:S(2)}, u32[]{:S(2)}) collective-permute-start(bf16[2,256,768]{2,1,0:T(8,128)(2,1)} %refs_5_.1), channel_id=1, source_target_pairs={{0,8},{8,16},{16,24},{12,4},{20,12},{28,20},{1,9},{9,17},{17,25},{... | collective-permute-start | bytes 2359304 | tf_op jit(solution)/shard_map/ppermute | solution.py:395
  2.7 3.0 %collective-permute-start.1 = (bf16[2,256,768]{2,1,0:T(8,128)(2,1)}, bf16[2,256,768]{2,1,0:T(8,128)(2,1)S(1)}, u32[]{:S(2)}, u32[]{:S(2)}) collective-permute-start(bf16[2,256,768]{2,1,0:T(8,128)(2,1)} %refs_5_.1), channel_id=1, source_target_pairs={{4,8},{12,16},{20,24},{8,4},{16,12},{24,20},{5,9},{13,17},{21,25},... | collective-permute-start | bytes 2359304 | tf_op jit(solution)/shard_map/ppermute | solution.py:395
  5.7 13.9 %collective-permute-done.refs_1_.refs_5_.refs_7_ = bf16[2,256,768]{2,1,0:T(8,128)(2,1)S(1)} collective-permute-done((bf16[2,256,768]{2,1,0:T(8,128)(2,1)}, bf16[2,256,768]{2,1,0:T(8,128)(2,1)S(1)}, u32[]{:S(2)}, u32[]{:S(2)}) %collective-permute-start) | collective-permute-done | bytes 786464 | tf_op jit(solution)/shard_map/ppermute | solution.py:395
  19.6 2.2 %collective-permute-start.5 = (bf16[2,256,768]{2,1,0:T(8,128)(2,1)S(1)}, bf16[2,256,768]{2,1,0:T(8,128)(2,1)}, u32[]{:S(2)}, u32[]{:S(2)}) collective-permute-start(bf16[2,256,768]{2,1,0:T(8,128)(2,1)S(1)} %collective-permute-done.refs_1_.refs_5_.refs_7_), channel_id=1, source_target_pairs={{8,16},{16,24},{12,4},{20,12},{9,17},{17,25},{13,5},{21,13},{10,18... | collective-permute-start | bytes 2359304 | tf_op jit(solution)/shard_map/ppermute | solution.py:395
  21.7 0.9 collective-permute-done.1.refs_2_.refs_6_.refs_8_
  22.6 3.0 %collective-permute-start.6 = (bf16[2,256,768]{2,1,0:T(8,128)(2,1)S(1)}, bf16[2,256,768]{2,1,0:T(8,128)(2,1)}, u32[]{:S(2)}, u32[]{:S(2)}) collective-permute-start(bf16[2,256,768]{2,1,0:T(8,128)(2,1)S(1)} %collective-permute-done.1.refs_2_.refs_6_.refs_8_), channel_id=1, source_target_pairs={{8,16},{16,24},{12,4},{20,12},{9,17},{17,25},{13,5},{21,13},{10,18... | collective-permute-start | bytes 2359304 | tf_op jit(solution)/shard_map/ppermute | solution.py:395
  25.6 37.0 %pack_heads.2 = bf16[8,64,1152]{2,1,0:T(8,128)(2,1)} custom-call(s32[1]{0:T(128)} %bitcast.first_block, bf16[128,9216]{1,0:T(8,128)(2,1)} %array.2), custom_call_target="tpu_custom_call" | custom-call | tf_op jit(solution)/shard_map/pack_heads/pallas_call | solution.py:48
  62.7 6.7 %all-to-all-start = ((bf16[8,64,1152]{2,1,0:T(8,128)(2,1)}), bf16[8,64,1152]{2,1,0:T(8,128)(2,1)S(1)}, u32[]{:S(2)}, u32[]{:S(2)}) async-start(bf16[8,64,1152]{2,1,0:T(8,128)(2,1)} %pack_heads.2), calls=%async_computation | async-start | bytes 2359296 | tf_op jit(solution)/shard_map/all_to_all | solution.py:367
  69.9 0.5 collective-permute-start.7
  70.6 2.5 %collective-permute-done.2.refs_4_.refs_6_ = bf16[2,256,768]{2,1,0:T(8,128)(2,1)} collective-permute-done((bf16[2,256,768]{2,1,0:T(8,128)(2,1)}, bf16[2,256,768]{2,1,0:T(8,128)(2,1)}, u32[]{:S(2)}, u32[]{:S(2)}) %collective-permute-start.2) | collective-permute-done | bytes 786464 | tf_op jit(solution)/shard_map/ppermute | solution.py:372
  73.1 1.5 collective-permute-start.9
  74.6 1.5 collective-permute-start.10
  76.2 9.3 %all-to-all-done.refs_0_.refs_1_.refs_2_.refs_3_.refs_4_ = bf16[8,64,1152]{2,1,0:T(8,128)(2,1)S(1)} async-done(((bf16[8,64,1152]{2,1,0:T(8,128)(2,1)}), bf16[8,64,1152]{2,1,0:T(8,128)(2,1)S(1)}, u32[]{:S(2)}, u32[]{:S(2)}) %all-to-all-start) | async-done | bytes 1179680 | tf_op jit(solution)/shard_map/all_to_all | solution.py:367
  85.5 1.5 copy-done.6
  87.0 12.1 %attend_text.1.refs_19_ = bf16[8,64,384]{2,1,0:T(8,128)(2,1)S(1)} custom-call(s32[6]{0:T(128)S(1)} %stack.72.info, bf16[8,64,1152]{2,1,0:T(8,128)(2,1)S(1)} %all-to-all-done.refs_0_.refs_1_.refs_2_.refs_3_.refs_4_, bf16[8,64,1152]{2,1,0:T(8,128)(2,1)S(1)} %all-to-all-done.refs_0_.refs_1_.refs_2_.refs_3_.refs_4_, ...), custom_call_target="tpu_custom_call" | custom-call | flops 1610612736 | bytes 3932160 | tf_op jit(solution)/shard_map/attend_text/pallas_call | solution.py:231
  99.1 10.4 %all_to_all.20.x_ref = bf16[8,64,384]{2,1,0:T(8,128)(2,1)S(1)} all-to-all(bf16[8,64,384]{2,1,0:T(8,128)(2,1)S(1)} %attend_text.1.refs_19_), channel_id=1, replica_groups={{0,1,2,3,4,5,6,7},{8,9,10,11,12,13,14,15},{16,17,18,19,20,21,22,23},{24..., dimensions={0} | all-to-all | bytes 786432 | tf_op jit(solution)/shard_map/all_to_all | solution.py:367
  109.5 0.8 unpack_text.1
  110.3 2.0 collective-permute-start.13
  112.3 37.0 %pack_heads.3 = bf16[8,64,1152]{2,1,0:T(8,128)(2,1)} custom-call(s32[1]{0:T(128)} %constant.37.clone.1.first_block, bf16[64,9216]{1,0:T(8,128)(2,1)} %array.3, bf16[8,64,1152]{2,1,0:T(8,128)(2,1)} %copy-done, bf16[2,256,768]{2,1,0:T(8,128)(2,1)} %copy-done.2, bf16[2,256,768]{2,1,0:T(8,128)(2,1)} %copy-done.4), custom_call_target="tpu_custom_call" | custom-call | tf_op jit(solution)/shard_map/pack_heads/pallas_call | solution.py:48
  149.4 4.0 %all-to-all-start.1 = ((bf16[8,64,1152]{2,1,0:T(8,128)(2,1)}), bf16[8,64,1152]{2,1,0:T(8,128)(2,1)S(1)}, u32[]{:S(2)}, u32[]{:S(2)}) async-start(bf16[8,64,1152]{2,1,0:T(8,128)(2,1)} %pack_heads.3), calls=%async_computation.1 | async-start | bytes 2359296 | tf_op jit(solution)/shard_map/all_to_all | solution.py:367
  153.9 1.8 broadcast_select_fusion
  156.2 13.3 %all-to-all-done.1.refs_0_.refs_1_.refs_2_ = bf16[8,64,1152]{2,1,0:T(8,128)(2,1)S(1)} async-done(((bf16[8,64,1152]{2,1,0:T(8,128)(2,1)}), bf16[8,64,1152]{2,1,0:T(8,128)(2,1)S(1)}, u32[]{:S(2)}, u32[]{:S(2)}) %all-to-all-start.1) | async-done | bytes 1179680 | tf_op jit(solution)/shard_map/all_to_all | solution.py:367
  169.5 1.1 copy-done.5
  170.7 1.1 copy-done.7
  171.8 12.7 %attend_image.1 = bf16[8,64,384]{2,1,0:T(8,128)(2,1)S(1)} custom-call(s32[7]{0:T(128)S(1)} %stack.69.info, bf16[8,64,1152]{2,1,0:T(8,128)(2,1)S(1)} %all-to-all-done.1.refs_0_.refs_1_.refs_2_, bf16[8,64,1152]{2,1,0:T(8,128)(2,1)S(1)} %all-to-all-done.1.refs_0_.refs_1_.refs_2_, bf16[8,64,1152]{2,1,0:T(8,128)(2,1)S(1)} %all-to-all-done.1.refs_0_.refs_1_.refs_2_, ...), custom_call_target="tpu_custom_call" | custom-call | flops 2013265920 | bytes 4718592 | tf_op jit(solution)/shard_map/attend_image/pallas_call | solution.py:231
  184.5 0.7 copy-done.8
  185.3 3.6 %all-to-all-start.2 = ((bf16[8,64,384]{2,1,0:T(8,128)(2,1)}), bf16[8,64,384]{2,1,0:T(8,128)(2,1)S(1)}, u32[]{:S(2)}, u32[]{:S(2)}) async-start(bf16[8,64,384]{2,1,0:T(8,128)(2,1)} %copy-done.8), calls=%async_computation.2 | async-start | bytes 786432 | tf_op jit(solution)/shard_map/all_to_all | solution.py:367
  188.9 1.2 broadcast_select_fusion.2
  190.1 0.9 pad_maximum_fusion
  191.0 5.5 %all-to-all-done.2.x_ref = bf16[8,64,384]{2,1,0:T(8,128)(2,1)S(1)} async-done(((bf16[8,64,384]{2,1,0:T(8,128)(2,1)}), bf16[8,64,384]{2,1,0:T(8,128)(2,1)S(1)}, u32[]{:S(2)}, u32[]{:S(2)}) %all-to-all-start.2) | async-done | bytes 393248 | tf_op jit(solution)/shard_map/all_to_all | solution.py:367
  196.5 0.8 copy-done.9
  197.3 8.9 %project.1 = bf16[64,3072]{1,0:T(8,128)(2,1)} custom-call(bf16[8,64,384]{2,1,0:T(8,128)(2,1)} %copy-done.9, bf16[8,384,3072]{2,1,0:T(8,128)(2,1)} %bitcast.10, bf16[64,3072]{1,0:T(8,128)(2,1)} %residual.1, f32[1,3072]{1,0:T(1,128)} %bitcast.11), custom_call_target="tpu_custom_call" | custom-call | flops 1207959552 | bytes 18874368 | tf_op jit(solution)/shard_map/project/pallas_call | solution.py:312
  (36 shorter events, 1.7 us)
Async XLA Ops:
  0.6 18.9 %collective-permute-start = (bf16[2,256,768]{2,1,0:T(8,128)(2,1)}, bf16[2,256,768]{2,1,0:T(8,128)(2,1)S(1)}, u32[]{:S(2)}, u32[]{:S(2)}) collective-permute-start(bf16[2,256,768]{2,1,0:T(8,128)(2,1)} %refs_5_.1), channel_id=1, source_target_pairs={{0,8},{8,16},{16,24},{12,4},{20,12},{28,20},{1,9},{9,17},{17,25},{... | collective-permute-start | bytes 2359304 | tf_op jit(solution)/shard_map/ppermute | solution.py:395
  2.7 19.9 %collective-permute-start.1 = (bf16[2,256,768]{2,1,0:T(8,128)(2,1)}, bf16[2,256,768]{2,1,0:T(8,128)(2,1)S(1)}, u32[]{:S(2)}, u32[]{:S(2)}) collective-permute-start(bf16[2,256,768]{2,1,0:T(8,128)(2,1)} %refs_5_.1), channel_id=1, source_target_pairs={{4,8},{12,16},{20,24},{8,4},{16,12},{24,20},{5,9},{13,17},{21,25},... | collective-permute-start | bytes 2359304 | tf_op jit(solution)/shard_map/ppermute | solution.py:395
  19.6 65.9 %copy-start.2 = (bf16[2,256,768]{2,1,0:T(8,128)(2,1)}, bf16[2,256,768]{2,1,0:T(8,128)(2,1)S(1)}, u32[]{:S(2)}) copy-start(bf16[2,256,768]{2,1,0:T(8,128)(2,1)S(1)} %collective-permute-done.refs_1_.refs_5_.refs_7_) | copy-start | bytes 2359300
  19.6 50.3 %collective-permute-start.5 = (bf16[2,256,768]{2,1,0:T(8,128)(2,1)S(1)}, bf16[2,256,768]{2,1,0:T(8,128)(2,1)}, u32[]{:S(2)}, u32[]{:S(2)}) collective-permute-start(bf16[2,256,768]{2,1,0:T(8,128)(2,1)S(1)} %collective-permute-done.refs_1_.refs_5_.refs_7_), channel_id=1, source_target_pairs={{8,16},{16,24},{12,4},{20,12},{9,17},{17,25},{13,5},{21,13},{10,18... | collective-permute-start | bytes 2359304 | tf_op jit(solution)/shard_map/ppermute | solution.py:395
  22.6 62.9 %copy-start.4 = (bf16[2,256,768]{2,1,0:T(8,128)(2,1)}, bf16[2,256,768]{2,1,0:T(8,128)(2,1)S(1)}, u32[]{:S(2)}) copy-start(bf16[2,256,768]{2,1,0:T(8,128)(2,1)S(1)} %collective-permute-done.1.refs_2_.refs_6_.refs_8_) | copy-start | bytes 2359300
  22.6 47.8 %collective-permute-start.6 = (bf16[2,256,768]{2,1,0:T(8,128)(2,1)S(1)}, bf16[2,256,768]{2,1,0:T(8,128)(2,1)}, u32[]{:S(2)}, u32[]{:S(2)}) collective-permute-start(bf16[2,256,768]{2,1,0:T(8,128)(2,1)S(1)} %collective-permute-done.1.refs_2_.refs_6_.refs_8_), channel_id=1, source_target_pairs={{8,16},{16,24},{12,4},{20,12},{9,17},{17,25},{13,5},{21,13},{10,18... | collective-permute-start | bytes 2359304 | tf_op jit(solution)/shard_map/ppermute | solution.py:395
  62.7 22.8 %all-to-all-start = ((bf16[8,64,1152]{2,1,0:T(8,128)(2,1)}), bf16[8,64,1152]{2,1,0:T(8,128)(2,1)S(1)}, u32[]{:S(2)}, u32[]{:S(2)}) async-start(bf16[8,64,1152]{2,1,0:T(8,128)(2,1)} %pack_heads.2), calls=%async_computation | async-start | bytes 2359296 | tf_op jit(solution)/shard_map/all_to_all | solution.py:367
  69.4 3.7 %collective-permute-start.2 = (bf16[2,256,768]{2,1,0:T(8,128)(2,1)}, bf16[2,256,768]{2,1,0:T(8,128)(2,1)}, u32[]{:S(2)}, u32[]{:S(2)}) collective-permute-start(bf16[2,256,768]{2,1,0:T(8,128)(2,1)} %refs_5_.1), channel_id=1, source_target_pairs={{0,4},{4,0},{8,12},{12,8},{16,20},{20,16},{24,28},{28,24},{1,5},{5... | collective-permute-start | bytes 2359304 | tf_op jit(solution)/shard_map/ppermute | solution.py:372
  69.4 5.3 %collective-permute-start.3 = (bf16[2,256,768]{2,1,0:T(8,128)(2,1)S(1)}, bf16[2,256,768]{2,1,0:T(8,128)(2,1)}, u32[]{:S(2)}, u32[]{:S(2)}) collective-permute-start(bf16[2,256,768]{2,1,0:T(8,128)(2,1)S(1)} %collective-permute-done.refs_1_.refs_5_.refs_7_), channel_id=1, source_target_pairs={{0,4},{4,0},{8,12},{12,8},{16,20},{20,16},{24,28},{28,24},{1,5},{5... | collective-permute-start | bytes 2359304 | tf_op jit(solution)/shard_map/ppermute | solution.py:372
  69.9 15.6 %collective-permute-start.4 = (bf16[2,256,768]{2,1,0:T(8,128)(2,1)S(1)}, bf16[2,256,768]{2,1,0:T(8,128)(2,1)}, u32[]{:S(2)}, u32[]{:S(2)}) collective-permute-start(bf16[2,256,768]{2,1,0:T(8,128)(2,1)S(1)} %collective-permute-done.1.refs_2_.refs_6_.refs_8_), channel_id=1, source_target_pairs={{0,4},{4,0},{8,12},{12,8},{16,20},{20,16},{24,28},{28,24},{1,5},{5... | collective-permute-start | bytes 2359304 | tf_op jit(solution)/shard_map/ppermute | solution.py:372
  69.9 15.6 %collective-permute-start.7 = (bf16[2,256,768]{2,1,0:T(8,128)(2,1)}, bf16[2,256,768]{2,1,0:T(8,128)(2,1)}, u32[]{:S(2)}, u32[]{:S(2)}) collective-permute-start(bf16[2,256,768]{2,1,0:T(8,128)(2,1)} %collective-permute-done.5.refs_9_.refs_11_), channel_id=1, source_target_pairs={{0,4},{4,0},{8,12},{12,8},{16,20},{20,16},{24,28},{28,24},{1,5},{5... | collective-permute-start | bytes 2359304 | tf_op jit(solution)/shard_map/ppermute | solution.py:372
  70.4 15.1 %collective-permute-start.8 = (bf16[2,256,768]{2,1,0:T(8,128)(2,1)}, bf16[2,256,768]{2,1,0:T(8,128)(2,1)}, u32[]{:S(2)}, u32[]{:S(2)}) collective-permute-start(bf16[2,256,768]{2,1,0:T(8,128)(2,1)} %collective-permute-done.6.refs_10_.refs_12_), channel_id=1, source_target_pairs={{0,4},{4,0},{8,12},{12,8},{16,20},{20,16},{24,28},{28,24},{1,5},{5... | collective-permute-start | bytes 2359304 | tf_op jit(solution)/shard_map/ppermute | solution.py:372
  73.1 80.3 %collective-permute-start.9 = (bf16[2,256,768]{2,1,0:T(8,128)(2,1)}, bf16[2,256,768]{2,1,0:T(8,128)(2,1)}, u32[]{:S(2)}, u32[]{:S(2)}) collective-permute-start(bf16[2,256,768]{2,1,0:T(8,128)(2,1)} %collective-permute-done.5.refs_9_.refs_11_), channel_id=1, source_target_pairs={{16,24},{12,4},{17,25},{13,5},{18,26},{14,6},{19,27},{15,7}} | collective-permute-start | bytes 2359304 | tf_op jit(solution)/shard_map/ppermute | solution.py:395
  74.6 79.1 %collective-permute-start.10 = (bf16[2,256,768]{2,1,0:T(8,128)(2,1)}, bf16[2,256,768]{2,1,0:T(8,128)(2,1)}, u32[]{:S(2)}, u32[]{:S(2)}) collective-permute-start(bf16[2,256,768]{2,1,0:T(8,128)(2,1)} %collective-permute-done.6.refs_10_.refs_12_), channel_id=1, source_target_pairs={{16,24},{12,4},{17,25},{13,5},{18,26},{14,6},{19,27},{15,7}} | collective-permute-start | bytes 2359304 | tf_op jit(solution)/shard_map/ppermute | solution.py:395
  85.5 13.7 %copy-start = (bf16[8,64,1152]{2,1,0:T(8,128)(2,1)}, bf16[8,64,1152]{2,1,0:T(8,128)(2,1)S(1)}, u32[]{:S(2)}) copy-start(bf16[8,64,1152]{2,1,0:T(8,128)(2,1)S(1)} %all-to-all-done.refs_0_.refs_1_.refs_2_.refs_3_.refs_4_) | copy-start | bytes 3538948
  85.5 1.5 copy-start.6
  110.3 43.7 %collective-permute-start.13 = (bf16[64,3072]{1,0:T(8,128)(2,1)}, bf16[64,3072]{1,0:T(8,128)(2,1)}, u32[]{:S(2)}, u32[]{:S(2)}) collective-permute-start(bf16[64,3072]{1,0:T(8,128)(2,1)} %unpack_text.1), channel_id=1, source_target_pairs={{8,0},{12,4},{16,24},{20,28},{9,1},{13,5},{17,25},{21,29},{10,2},{... | collective-permute-start | bytes 1179656 | tf_op jit(solution)/shard_map/ppermute | solution.py:427
  149.4 20.1 %copy-start.1 = (bf16[8,64,1152]{2,1,0:T(8,128)(2,1)S(1)}, bf16[8,64,1152]{2,1,0:T(8,128)(2,1)}, u32[]{:S(2)}) copy-start(bf16[8,64,1152]{2,1,0:T(8,128)(2,1)} %copy-done) | copy-start | bytes 3538948
  149.4 20.1 %copy-start.3 = (bf16[2,256,768]{2,1,0:T(8,128)(2,1)S(1)}, bf16[2,256,768]{2,1,0:T(8,128)(2,1)}, u32[]{:S(2)}) copy-start(bf16[2,256,768]{2,1,0:T(8,128)(2,1)} %copy-done.2) | copy-start | bytes 2359300
  149.4 20.1 %all-to-all-start.1 = ((bf16[8,64,1152]{2,1,0:T(8,128)(2,1)}), bf16[8,64,1152]{2,1,0:T(8,128)(2,1)S(1)}, u32[]{:S(2)}, u32[]{:S(2)}) async-start(bf16[8,64,1152]{2,1,0:T(8,128)(2,1)} %pack_heads.3), calls=%async_computation.1 | async-start | bytes 2359296 | tf_op jit(solution)/shard_map/all_to_all | solution.py:367
  153.4 16.1 %collective-permute-start.11 = (bf16[2,256,768]{2,1,0:T(8,128)(2,1)}, bf16[2,256,768]{2,1,0:T(8,128)(2,1)}, u32[]{:S(2)}, u32[]{:S(2)}) collective-permute-start(bf16[2,256,768]{2,1,0:T(8,128)(2,1)} %collective-permute-done.9.refs_15_), channel_id=1, source_target_pairs={{0,4},{4,0},{8,12},{12,8},{16,20},{20,16},{24,28},{28,24},{1,5},{5... | collective-permute-start | bytes 2359304 | tf_op jit(solution)/shard_map/ppermute | solution.py:372
  153.8 15.7 %collective-permute-start.12 = (bf16[2,256,768]{2,1,0:T(8,128)(2,1)}, bf16[2,256,768]{2,1,0:T(8,128)(2,1)}, u32[]{:S(2)}, u32[]{:S(2)}) collective-permute-start(bf16[2,256,768]{2,1,0:T(8,128)(2,1)} %collective-permute-done.10.refs_16_), channel_id=1, source_target_pairs={{0,4},{4,0},{8,12},{12,8},{16,20},{20,16},{24,28},{28,24},{1,5},{5... | collective-permute-start | bytes 2359304 | tf_op jit(solution)/shard_map/ppermute | solution.py:372
  155.7 33.1 %collective-permute-start.14 = (bf16[64,3072]{1,0:T(8,128)(2,1)}, bf16[64,3072]{1,0:T(8,128)(2,1)}, u32[]{:S(2)}, u32[]{:S(2)}) collective-permute-start(bf16[64,3072]{1,0:T(8,128)(2,1)} %broadcast_select_fusion), channel_id=1, source_target_pairs={{0,4},{4,0},{8,12},{12,8},{16,20},{20,16},{24,28},{28,24},{1,5},{5... | collective-permute-start | bytes 1179656 | tf_op jit(solution)/shard_map/ppermute | solution.py:372
  169.5 1.1 copy-start.5
  170.7 1.1 copy-start.7
  184.5 0.7 copy-start.8
  185.3 11.3 %all-to-all-start.2 = ((bf16[8,64,384]{2,1,0:T(8,128)(2,1)}), bf16[8,64,384]{2,1,0:T(8,128)(2,1)S(1)}, u32[]{:S(2)}, u32[]{:S(2)}) async-start(bf16[8,64,384]{2,1,0:T(8,128)(2,1)} %copy-done.8), calls=%async_computation.2 | async-start | bytes 786432 | tf_op jit(solution)/shard_map/all_to_all | solution.py:367
  196.5 0.8 copy-start.9

commit v8 on v7

v8 whole, which is shorter than its diff:
```python
import functools
import math

import jax
import jax.numpy as jnp
from jax import lax
from jax.experimental import pallas as pl
from jax.experimental.pallas import tpu as pltpu
from jax.sharding import PartitionSpec as P

HD = 128
SCALE = math.log2(math.e) / math.sqrt(HD)
VMEM_LIMIT = 12 * 1024 * 1024
WIDE_LIMIT = 48 * 1024 * 1024
TILE = 256
FIRST_KEYS = 256
LARGE = 2.0**60


def params(block_elements=0):
    return pltpu.CompilerParams(
        vmem_limit_bytes=VMEM_LIMIT + 4 * block_elements, dimension_semantics=("arbitrary",)
    )


def pack_body(_, *refs):
    sources, packed = refs[:3], refs[-1]
    width = sources[0].shape[1]
    for part, source in enumerate(sources):
        packed[0, :, part * width : (part + 1) * width] = source[...]


def pack(first_block, array, rows, head_owners, pair, width, after=()):
    blocks = array.shape[1] // 3 // width
    destinations = head_owners * pair

    def source(part):
        def place(d, info):
            return (info[0], part * blocks + (d % head_owners) * pair + d // head_owners)

        return pl.BlockSpec((rows, width), place)

    return pl.pallas_call(
        pack_body,
        grid_spec=pltpu.PrefetchScalarGridSpec(
            num_scalar_prefetch=1,
            grid=(destinations,),
            in_specs=[source(0), source(1), source(2)]
            + [pl.BlockSpec(memory_space=pl.ANY)] * len(after),
            out_specs=pl.BlockSpec((1, rows, 3 * width), lambda d, info: (d, 0, 0)),
        ),
        out_shape=jax.ShapeDtypeStruct((destinations, rows, 3 * width), array.dtype),
        compiler_params=params(),
        name="pack_heads",
    )(first_block, array, array, array, *after)


def dot(first, second, contract):
    return lax.dot_general(
        first, second, ((contract[:1], contract[1:]), ((), ())), preferred_element_type=jnp.float32
    )


def with_ones(block):
    return jnp.concatenate([block, jnp.ones_like(block)], axis=1)


def reference_columns(row_max):
    reference = row_max.astype(jnp.bfloat16).astype(jnp.float32)
    return jnp.broadcast_to(reference * (-1.0 / HD), (row_max.shape[0], HD)).astype(jnp.bfloat16)


def weighted(queries, key_rows, values):
    weights = jnp.exp2(dot(queries, key_rows, (1, 1)) * SCALE).astype(jnp.bfloat16)
    return dot(weights, values, (1, 0))


def tiles_of(rows):
    tile = min(TILE, rows)
    return [slice(first, min(first + tile, rows)) for first in range(0, rows, tile)]


def until_small(flag, total, attempt):
    flag[0] = 1

    @pl.loop(0, 2)
    def _(turn):
        @pl.when(flag[0] == 1)
        def _():
            attempt(turn)
            flag[0] = jnp.where(jnp.max(total[:, HD:]) > LARGE, 1, 0).astype(jnp.int32)


class Arrivals:
    def __init__(self, entries, heads):
        self.entries = [[len(blocks) for blocks in candidates] for candidates in entries]
        self.operands = [b for candidates in entries for blocks in candidates for b in blocks]
        self.specs = [stale_spec(block, heads) for block in self.operands]
        rows = sum(block.shape[1] for block in entries[0][0])
        self.scratch = pltpu.VMEM((len(entries), 2, rows, HD), self.operands[0].dtype)

    def settle(self, info, refs, chosen):
        for index, counts in enumerate(self.entries):
            first, refs = refs[: counts[0]], refs[counts[0] :]
            second = None
            if len(counts) > 1:
                second, refs = refs[: counts[1]], refs[counts[1] :]
            at = 0
            for place, block in enumerate(first):
                value = block[...]
                if second is not None:
                    value = jnp.where(info[1 + index] == 1, value, second[place][...])
                chosen[index, :, at : at + block.shape[1], :] = value
                at += block.shape[1]

    def pieces(self, chosen):
        return [(chosen[index, 0], chosen[index, 1]) for index in range(len(self.entries))]


def stale_spec(block, heads):
    shape = (2, block.shape[1], HD)
    return pl.BlockSpec(shape, lambda h, info: (0, 0, info[0] * heads + h))


def column_spec(shape, offset=0):
    return pl.BlockSpec(shape[:2] + (HD,), lambda h, info: (0, 0, offset + h))


def accumulate(flag, total, aug, queries, first_keys, own, pieces):
    def raised(tile, row_max, some):
        for key_rows, _ in some:
            piece_max = jnp.max(dot(queries[tile, :], key_rows, (1, 1)), axis=1, keepdims=True)
            row_max = piece_max if row_max is None else jnp.maximum(row_max, piece_max)
        return row_max

    def tiles():
        for span, some in own:
            for tile in tiles_of(span.stop - span.start):
                yield slice(span.start + tile.start, span.start + tile.stop), some

    def attempt(turn):
        @pl.when(turn == 0)
        def _():
            for tile, _ in tiles():
                aug[tile, :] = reference_columns(raised(tile, None, [(first_keys, None)]))

        @pl.when(turn == 1)
        def _():
            for tile, some in tiles():
                aug[tile, :] = reference_columns(raised(tile, None, some + pieces))

        for tile, some in tiles():
            both = jnp.concatenate([queries[tile, :], aug[tile, :]], axis=1)
            summed = None
            for key_rows, values in some + pieces:
                part = weighted(both, with_ones(key_rows), with_ones(values))
                summed = part if summed is None else summed + part
            total[tile, :] = summed

    until_small(flag, total, attempt)


def flat(block):
    return block[...].reshape(-1, HD)


def joined(blocks):
    return (
        jnp.concatenate([block[0] for block in blocks], 0),
        jnp.concatenate([block[1] for block in blocks], 0),
    )


def text_body(pair, arrivals, wanted, info, *refs):
    q_ref, k_ref, v_ref = refs[:3]
    stale, came = refs[3 : 3 + pair], refs[3 + pair : 3 + pair + len(arrivals.operands)]
    out, chosen, aug, total, flag = refs[3 + pair + len(arrivals.operands) :]

    @pl.when(info[wanted] == 1)
    def _():
        arrivals.settle(info, came, chosen)
        rows = total.shape[0]
        text_keys, text_values = flat(k_ref), flat(v_ref)
        own = [(slice(0, rows), [(text_keys, text_values), joined(stale)])]
        accumulate(
            flag, total, aug, flat(q_ref), text_keys[: min(FIRST_KEYS, rows), :], own,
            arrivals.pieces(chosen),
        )
        attended = (total[:, :HD] / total[:, HD:]).astype(out.dtype)
        out[...] = attended.reshape(out.shape)


def image_body(pair, arrivals, info, *refs):
    q_ref, k_ref, v_ref, text_k_ref, text_v_ref = refs[:5]
    stale, came = refs[5 : 5 + pair], refs[5 + pair : 5 + pair + len(arrivals.operands)]
    out, chosen, aug, total, flag = refs[6 + pair + len(arrivals.operands) :]
    arrivals.settle(info, came, chosen)
    rows = total.shape[0]
    core = info[0]
    img_keys, img_values = flat(k_ref), flat(v_ref)
    text_keys, text_values = flat(text_k_ref), flat(text_v_ref)
    group_rows = rows // pair
    own = []
    for group in range(pair):
        span = slice(group * group_rows, (group + 1) * group_rows)
        key_rows, values = [img_keys[span, :]], [img_values[span, :]]
        if pair == 2:
            mine = core == group
            key_rows.append(jnp.where(mine, stale[1][0], stale[0][0]))
            values.append(jnp.where(mine, stale[1][1], stale[0][1]))
        fresh = (jnp.concatenate(key_rows, 0), jnp.concatenate(values, 0))
        own.append((span, [(text_keys, text_values), fresh]))
    accumulate(
        flag, total, aug, flat(q_ref), text_keys[: min(FIRST_KEYS, text_keys.shape[0]), :], own,
        arrivals.pieces(chosen),
    )
    attended = (total[:, :HD] / total[:, HD:]).astype(out.dtype)
    out[...] = attended.reshape(out.shape)


def attend_cost(queries, keys, heads):
    return pl.CostEstimate(
        flops=4 * queries * keys * heads * HD,
        bytes_accessed=4 * queries * heads * HD + 4 * keys * heads * HD,
        transcendentals=queries * keys * heads,
    )


def call_heads(body, name, heads, info, operands, specs, outs, out_specs, scratch, cost):
    return pl.pallas_call(
        body,
        grid_spec=pltpu.PrefetchScalarGridSpec(
            num_scalar_prefetch=1,
            grid=(heads,),
            in_specs=specs,
            out_specs=out_specs,
            scratch_shapes=scratch,
        ),
        out_shape=outs,
        compiler_params=params(
            sum(math.prod(spec.block_shape) for spec in specs if spec.block_shape is not None)
        ),
        cost_estimate=cost,
        name=name,
    )(info, *operands)


def scratch_of(rows, arrivals):
    return [
        arrivals.scratch,
        pltpu.VMEM((rows, HD), jnp.bfloat16),
        pltpu.VMEM((rows, 2 * HD), jnp.float32),
        pltpu.SMEM((1,), jnp.int32),
    ]


def attend_text(info, wanted, txt, stale, entries):
    heads = txt.shape[2] // (3 * HD)
    arrivals = Arrivals(entries, heads)
    rows = txt.shape[0] * txt.shape[1]
    out = jax.ShapeDtypeStruct(txt.shape[:2] + (heads * HD,), txt.dtype)
    return call_heads(
        functools.partial(text_body, len(stale), arrivals, wanted),
        "attend_text", heads, info, [txt] * 3 + list(stale) + arrivals.operands,
        [column_spec(txt.shape, part * heads) for part in range(3)]
        + [stale_spec(block, heads) for block in stale]
        + arrivals.specs,
        out, column_spec(out.shape), scratch_of(rows, arrivals), attend_cost(rows, 4 * rows, heads),
    )


def attend_image(info, img, txt, stale, entries, after):
    heads = img.shape[2] // (3 * HD)
    arrivals = Arrivals(entries, heads)
    rows = img.shape[0] * img.shape[1]
    out = jax.ShapeDtypeStruct(img.shape[:2] + (heads * HD,), img.dtype)
    return call_heads(
        functools.partial(image_body, len(stale), arrivals),
        "attend_image", heads, info,
        [img] * 3 + [txt] * 2 + list(stale) + arrivals.operands + [after],
        [column_spec(img.shape, part * heads) for part in range(3)]
        + [column_spec(txt.shape, part * heads) for part in (1, 2)]
        + [stale_spec(block, heads) for block in stale]
        + arrivals.specs
        + [pl.BlockSpec(memory_space=pl.ANY)],
        out, column_spec(out.shape), scratch_of(rows, arrivals), attend_cost(rows, 5 * rows, heads),
    )


def project_body(order, x_ref, weight, residual, gate, out, held, total, sems):
    copies = [
        pltpu.make_async_copy(weight.at[place], held.at[place], sems.at[place])
        for place in order
    ]
    for copy in copies:
        copy.start()
    for source, (place, copy) in enumerate(zip(order, copies)):
        copy.wait()
        part = jnp.dot(x_ref[source], held[place], preferred_element_type=jnp.float32)
        if source == 0:
            total[...] = part
        else:
            total[...] += part
    out[...] = (residual[...].astype(jnp.float32) + gate[...] * total[...]).astype(out.dtype)


def project(x, order, weight, residual, gate):
    rows, model = residual.shape
    destinations, _, width = x.shape
    vmem = pl.BlockSpec(memory_space=pltpu.VMEM)
    return pl.pallas_call(
        functools.partial(project_body, order),
        in_specs=[vmem, pl.BlockSpec(memory_space=pl.ANY), vmem, vmem],
        out_specs=vmem,
        out_shape=jax.ShapeDtypeStruct((rows, model), residual.dtype),
        scratch_shapes=[
            pltpu.VMEM((destinations, width, model), weight.dtype),
            pltpu.VMEM((rows, model), jnp.float32),
            pltpu.SemaphoreType.DMA((destinations,)),
        ],
        compiler_params=pltpu.CompilerParams(vmem_limit_bytes=WIDE_LIMIT),
        cost_estimate=pl.CostEstimate(
            flops=2 * rows * model * model, bytes_accessed=2 * model * model, transcendentals=0
        ),
        name="project",
    )(x, weight.reshape(destinations, width, model), residual, gate.reshape(1, model))


def after_body(*refs):
    del refs


def after(x, other):
    anywhere = pl.BlockSpec(memory_space=pl.ANY)
    return pl.pallas_call(
        after_body,
        in_specs=[anywhere, anywhere],
        out_specs=anywhere,
        out_shape=jax.ShapeDtypeStruct(x.shape, x.dtype),
        input_output_aliases={0: 0},
        name="after",
    )(x, other)


def unpack_body(order, x_ref, out):
    width = x_ref.shape[2]
    for source, place in enumerate(order):
        out[:, place * width : (place + 1) * width] = x_ref[source]


def unpack(x, order):
    rows, model = x.shape[1], x.shape[0] * x.shape[2]
    return pl.pallas_call(
        functools.partial(unpack_body, order),
        grid=(1,),
        in_specs=[pl.BlockSpec(x.shape, lambda n: (0, 0, 0))],
        out_specs=pl.BlockSpec((rows, model), lambda n: (0, 0)),
        out_shape=jax.ShapeDtypeStruct((rows, model), x.dtype),
        compiler_params=params(),
        name="unpack_text",
    )(x)


def per_device(img_qkv, txt_qkv, stale_kv, residual, gate_scale, proj_weight):
    patches, head_owners = lax.axis_size("patch"), lax.axis_size("head")
    patch = lax.axis_index("patch")
    owned_heads = stale_kv.shape[2] // HD
    pair = 2 if patches % 2 == 0 and owned_heads % 2 == 0 else 1
    planes = patches // pair
    plane, core = patch // pair, patch % pair
    width = stale_kv.shape[2] // pair
    heads = width // HD
    img_rows, model = residual.shape
    text_rows = txt_qkv.shape[0] // pair
    destinations = pair * head_owners

    order = [(d % head_owners) * pair + d // head_owners for d in range(destinations)]
    groups = [[g * destinations + d for d in range(destinations)] for g in range(planes)]
    swap_pairs = [(p, p + 1 - 2 * (p % 2)) for p in range(patches)]

    def exchange(x):
        return lax.all_to_all(
            x, ("patch", "head"), split_axis=0, concat_axis=0, axis_index_groups=groups, tiled=True
        )

    def swap(x):
        return lax.ppermute(x, "patch", swap_pairs)

    def up_pairs(step):
        return [(z, z + 1) for z in range(step - 1, planes - 1)]

    def down_pairs(step):
        return [(z + 1, z) for z in range(0, planes - step)]

    core_only = core.astype(jnp.int32).reshape(1)
    txt = exchange(pack(core_only, txt_qkv, text_rows, head_owners, pair, width))

    along, against = [], []
    if pair == 2:
        stale = [stale_kv, swap(stale_kv)]
        held = [stale_kv, stale_kv]
        for step in range(1, planes):
            pairs = [
                [(2 * a + turn, 2 * b) for a, b in up_pairs(step)]
                + [(2 * a + 1 - turn, 2 * b + 1) for a, b in down_pairs(step)]
                for turn in ((0, 1) if step == 1 else (0, 0))
            ]
            held = [lax.ppermute(block, "patch", way) for block, way in zip(held, pairs)]
            along.append(held)
            against.append([swap(block) for block in held])
        ahead = jnp.where(core == 0, plane, planes - 1 - plane)
    else:
        stale = [stale_kv]
        from_below = from_above = stale_kv
        for step in range(1, planes):
            from_below = lax.ppermute(from_below, "patch", up_pairs(step))
            from_above = lax.ppermute(from_above, "patch", down_pairs(step))
            along.append([from_below])
            against.append([from_above])
        ahead = plane
    held_first = along[0]
    entries = [[along[i - 1], against[planes - i - 1]] for i in range(1, planes)]
    first_holds = [ahead >= i for i in range(1, planes)]
    zero_only = jnp.zeros((1,), jnp.int32)
    img = exchange(pack(zero_only, img_qkv, img_rows, head_owners, pair, width, [txt] + held_first))

    early = planes > 2
    inner = (plane > 0) & (plane < planes - 1)
    info = jnp.stack([core] + first_holds + [inner if early else core >= 0]).astype(jnp.int32)
    known = entries
    if early:
        known = [[along[0]]] + entries[1:-1] + [[against[0]]]
    text_attn = attend_text(info, planes, txt, stale, known)
    image_attn = attend_image(info, img, txt, stale, entries, text_attn)
    text_back = exchange(after(text_attn, img))

    text_out = unpack(text_back, order)
    if early:
        ends = [(1, 0), (planes - 2, planes - 1)]
        ends = [(a * pair + c, b * pair + c) for a, b in ends for c in range(pair)]
        text_out = jnp.where(inner, text_out, lax.ppermute(text_out, "patch", ends))
    if pair == 2:
        other = swap(text_out)
        lower = core == 0
        text_out = jnp.concatenate(
            [jnp.where(lower, text_out, other), jnp.where(lower, other, text_out)], 0
        )

    image_out = project(exchange(image_attn), order, proj_weight, residual, gate_scale)
    return (image_out, text_out)


def solution(mesh):
    return jax.shard_map(
        per_device,
        mesh=mesh,
        in_specs=(
            P(("patch", "head"), None),
            P("head", None),
            P(None, "patch", "head"),
            P(("patch", "head"), None),
            P(),
            P(),
        ),
        out_specs=(P(("patch", "head"), None), P("head", None)),
        check_vma=False,
    )
```

time: 210 us -> 120 us (0.57)
  Pallas kernels: 109 us -> 30.7 us
  waiting for transfers between devices: 45.5 us -> 27.3 us
  blocking collectives: 10.4 us -> 15.9 us
  starting transfers between devices: 31.6 us -> 35.6 us
  other arithmetic: 3.9 us -> 1.03 us
    pallas_call x2 -> x3, Pallas kernels: 74.1 us -> 1.33 us  [the longest x2 1.33 us: pack(): pl.pallas_call(pack_body, grid_spec=pltpu.PrefetchScalarGridSpec(num_scal...]
    all_to_all x3, waiting for transfers between devices: 28.1 us -> 11.1 us  [exchange(): lax.all_to_all(x, ('patch', 'head'), split_axis=0, concat_axis=0, axis_in...]
    ppermute x1, waiting for transfers between devices: 0.01 us -> 7.79 us  [per_device(): text_out = jnp.where(inner, text_out, lax.ppermute(text_out, 'patch', ends))]
    ppermute x8, starting transfers between devices: 1.94 us -> 8.91 us  [swap(): return lax.ppermute(x, 'patch', swap_pairs)]
    ppermute x6, waiting for transfers between devices: 14.8 us -> 8.46 us  [per_device(): lax.ppermute(block, 'patch', way)]
    all_to_all x1, blocking collectives: 10.4 us -> 15.9 us  [exchange(): lax.all_to_all(x, ('patch', 'head'), split_axis=0, concat_axis=0, axis_in...]
    pallas_call x2, Pallas kernels: 24.8 us -> 21.6 us  [call_heads(): pl.pallas_call(body, grid_spec=pltpu.PrefetchScalarGridSpec(num_scalar_pr...]
    ppermute x8, waiting for transfers between devices: 2.55 us -> 0.02 us  [swap(): return lax.ppermute(x, 'patch', swap_pairs)]
  transfers between devices with their start and end apart: 18 -> 18, of which waited for: 6 -> 6; matrix products, arithmetic and copies ran while one was open for 2% -> 2% of each run, Pallas kernels for 48% -> 19%
where the time goes in v8:
time: 120 us; the launch traced here: 118 us
  starting transfers between devices  35.6 us (30%)
  Pallas kernels  30.7 us (26%)
  waiting for transfers between devices  27.3 us (23%)
  blocking collectives  15.9 us (13%)
  local copies, waits for them, and re-layouts  6.69 us (6%)
    pallas_call x2, Pallas kernels, call_heads(): pl.pallas_call(body, grid_spec=pltpu.PrefetchScalarGridSpec(num_scalar_pr...  21.6 us
    all_to_all x1, blocking collectives, exchange(): lax.all_to_all(x, ('patch', 'head'), split_axis=0, concat_axis=0, axis_in...  15.9 us
    ppermute x6, starting transfers between devices, per_device(): lax.ppermute(block, 'patch', way)  13.4 us
    all_to_all x3, starting transfers between devices, exchange(): lax.all_to_all(x, ('patch', 'head'), split_axis=0, concat_axis=0, axis_in...  12 us
    all_to_all x3, waiting for transfers between devices, exchange(): lax.all_to_all(x, ('patch', 'head'), split_axis=0, concat_axis=0, axis_in...  11.1 us
    ppermute x8, starting transfers between devices, swap(): return lax.ppermute(x, 'patch', swap_pairs)  8.91 us
    ppermute x6, waiting for transfers between devices, per_device(): lax.ppermute(block, 'patch', way)  8.46 us
    pallas_call x1, Pallas kernels, project(): pl.pallas_call(functools.partial(project_body, order), in_specs=[vmem, pl...  7.81 us
  transfers between devices with their start and end apart: 18, of which 6 were waited for; matrix products, arithmetic and copies ran while one was open for 2% of the time, Pallas kernels for 19%

profile of v8, /device:TPU:17, one launch (start us, length us, event | category | flops | bytes accessed | tf_op | source)
XLA Modules:
  0.0 118.2 jit_solution(8572284974269720702)
XLA Ops:
  0.6 2.1 %collective-permute-start = (bf16[2,256,768]{2,1,0:T(8,128)(2,1)}, bf16[2,256,768]{2,1,0:T(8,128)(2,1)S(1)}, u32[]{:S(2)}, u32[]{:S(2)}) collective-permute-start(bf16[2,256,768]{2,1,0:T(8,128)(2,1)} %refs_5_.1), channel_id=1, source_target_pairs={{0,8},{8,16},{16,24},{12,4},{20,12},{28,20},{1,9},{9,17},{17,25},{... | collective-permute-start | bytes 2359304 | tf_op jit(solution)/shard_map/ppermute | solution.py:408
  2.7 3.0 %collective-permute-start.1 = (bf16[2,256,768]{2,1,0:T(8,128)(2,1)}, bf16[2,256,768]{2,1,0:T(8,128)(2,1)}, u32[]{:S(2)}, u32[]{:S(2)}) collective-permute-start(bf16[2,256,768]{2,1,0:T(8,128)(2,1)} %refs_5_.1), channel_id=1, source_target_pairs={{4,8},{12,16},{20,24},{8,4},{16,12},{24,20},{5,9},{13,17},{21,25},... | collective-permute-start | bytes 2359304 | tf_op jit(solution)/shard_map/ppermute | solution.py:408
  5.7 1.7 %copy-done.2 = bf16[128,9216]{1,0:T(8,128)(2,1)S(1)} copy-done((bf16[128,9216]{1,0:T(8,128)(2,1)S(1)}, bf16[128,9216]{1,0:T(8,128)(2,1)}, u32[]{:S(2)}) %copy-start.2) | copy-done | bytes 2359320
  7.4 0.7 pack_heads.2
  8.1 1.0 copy-done.4
  9.1 4.9 %all-to-all-start = ((bf16[8,64,1152]{2,1,0:T(8,128)(2,1)}), bf16[8,64,1152]{2,1,0:T(8,128)(2,1)S(1)}, u32[]{:S(2)}, u32[]{:S(2)}) async-start(bf16[8,64,1152]{2,1,0:T(8,128)(2,1)} %copy-done.4), calls=%async_computation | async-start | bytes 2359296 | tf_op jit(solution)/shard_map/all_to_all | solution.py:382
  14.0 5.7 %collective-permute-done.refs_4_.refs_5_.refs_7_ = bf16[2,256,768]{2,1,0:T(8,128)(2,1)S(1)} collective-permute-done((bf16[2,256,768]{2,1,0:T(8,128)(2,1)}, bf16[2,256,768]{2,1,0:T(8,128)(2,1)S(1)}, u32[]{:S(2)}, u32[]{:S(2)}) %collective-permute-start) | collective-permute-done | bytes 786464 | tf_op jit(solution)/shard_map/ppermute | solution.py:408
  19.7 2.2 %collective-permute-start.3 = (bf16[2,256,768]{2,1,0:T(8,128)(2,1)S(1)}, bf16[2,256,768]{2,1,0:T(8,128)(2,1)}, u32[]{:S(2)}, u32[]{:S(2)}) collective-permute-start(bf16[2,256,768]{2,1,0:T(8,128)(2,1)S(1)} %collective-permute-done.refs_4_.refs_5_.refs_7_), channel_id=1, source_target_pairs={{8,16},{16,24},{12,4},{20,12},{9,17},{17,25},{13,5},{21,13},{10,18... | collective-permute-start | bytes 2359304 | tf_op jit(solution)/shard_map/ppermute | solution.py:408
  21.8 0.8 collective-permute-done.1.refs_5_.refs_6_.refs_8_
  22.6 2.9 %collective-permute-start.6 = (bf16[2,256,768]{2,1,0:T(8,128)(2,1)}, bf16[2,256,768]{2,1,0:T(8,128)(2,1)}, u32[]{:S(2)}, u32[]{:S(2)}) collective-permute-start(bf16[2,256,768]{2,1,0:T(8,128)(2,1)} %collective-permute-done.1.refs_5_.refs_6_.refs_8_), channel_id=1, source_target_pairs={{8,16},{16,24},{12,4},{20,12},{9,17},{17,25},{13,5},{21,13},{10,18... | collective-permute-start | bytes 2359304 | tf_op jit(solution)/shard_map/ppermute | solution.py:408
  25.6 4.5 %all-to-all-done.refs_3_.refs_0_.refs_1_.refs_2_.refs_4_ = bf16[8,64,1152]{2,1,0:T(8,128)(2,1)S(1)} async-done(((bf16[8,64,1152]{2,1,0:T(8,128)(2,1)}), bf16[8,64,1152]{2,1,0:T(8,128)(2,1)S(1)}, u32[]{:S(2)}, u32[]{:S(2)}) %all-to-all-start) | async-done | bytes 1179680 | tf_op jit(solution)/shard_map/all_to_all | solution.py:382
  30.0 0.7 pack_heads.3
  30.7 1.0 copy-done.5
  31.7 3.7 %all-to-all-start.1 = ((bf16[8,64,1152]{2,1,0:T(8,128)(2,1)}), bf16[8,64,1152]{2,1,0:T(8,128)(2,1)S(1)}, u32[]{:S(2)}, u32[]{:S(2)}) async-start(bf16[8,64,1152]{2,1,0:T(8,128)(2,1)} %copy-done.5), calls=%async_computation.1 | async-start | bytes 2359296 | tf_op jit(solution)/shard_map/all_to_all | solution.py:382
  36.5 2.0 %collective-permute-done.6.refs_8_.refs_12_ = bf16[2,256,768]{2,1,0:T(8,128)(2,1)} collective-permute-done((bf16[2,256,768]{2,1,0:T(8,128)(2,1)}, bf16[2,256,768]{2,1,0:T(8,128)(2,1)}, u32[]{:S(2)}, u32[]{:S(2)}) %collective-permute-start.6) | collective-permute-done | bytes 786464 | tf_op jit(solution)/shard_map/ppermute | solution.py:408
  38.4 6.3 %collective-permute-start.10 = (bf16[2,256,768]{2,1,0:T(8,128)(2,1)}, bf16[2,256,768]{2,1,0:T(8,128)(2,1)}, u32[]{:S(2)}, u32[]{:S(2)}) collective-permute-start(bf16[2,256,768]{2,1,0:T(8,128)(2,1)} %collective-permute-done.6.refs_8_.refs_12_), channel_id=1, source_target_pairs={{0,4},{4,0},{8,12},{12,8},{16,20},{20,16},{24,28},{28,24},{1,5},{5... | collective-permute-start | bytes 2359304 | tf_op jit(solution)/shard_map/ppermute | solution.py:387
  44.8 1.6 %collective-permute-start.4 = (bf16[2,256,768]{2,1,0:T(8,128)(2,1)}, bf16[2,256,768]{2,1,0:T(8,128)(2,1)}, u32[]{:S(2)}, u32[]{:S(2)}) collective-permute-start(bf16[2,256,768]{2,1,0:T(8,128)(2,1)} %collective-permute-done.3.refs_7_.refs_11_), channel_id=1, source_target_pairs={{16,24},{12,4},{17,25},{13,5},{18,26},{14,6},{19,27},{15,7}} | collective-permute-start | bytes 2359304 | tf_op jit(solution)/shard_map/ppermute | solution.py:408
  46.5 1.6 %collective-permute-start.7 = (bf16[2,256,768]{2,1,0:T(8,128)(2,1)}, bf16[2,256,768]{2,1,0:T(8,128)(2,1)}, u32[]{:S(2)}, u32[]{:S(2)}) collective-permute-start(bf16[2,256,768]{2,1,0:T(8,128)(2,1)} %collective-permute-done.6.refs_8_.refs_12_), channel_id=1, source_target_pairs={{16,24},{12,4},{17,25},{13,5},{18,26},{14,6},{19,27},{15,7}} | collective-permute-start | bytes 2359304 | tf_op jit(solution)/shard_map/ppermute | solution.py:408
  48.1 1.1 copy-done.6
  49.2 10.1 %attend_text.1.refs_19_ = bf16[8,64,384]{2,1,0:T(8,128)(2,1)S(1)} custom-call(s32[5]{0:T(128)S(1)} %stack.39.info, bf16[8,64,1152]{2,1,0:T(8,128)(2,1)S(1)} %all-to-all-done.refs_3_.refs_0_.refs_1_.refs_2_.refs_4_, bf16[8,64,1152]{2,1,0:T(8,128)(2,1)S(1)} %all-to-all-done.refs_3_.refs_0_.refs_1_.refs_2_.refs_4_, ...), custom_call_target="tpu_custom_call" | custom-call | flops 1610612736 | bytes 3932160 | tf_op jit(solution)/shard_map/attend_text/pallas_call | solution.py:230
  59.3 0.7 copy.9.refs_0_
  60.1 1.0 copy-done
  61.1 15.9 %all_to_all.20.x_ref = bf16[8,64,384]{2,1,0:T(8,128)(2,1)S(1)} all-to-all(bf16[8,64,384]{2,1,0:T(8,128)(2,1)} %after.1), channel_id=1, replica_groups={{0,1,2,3,4,5,6,7},{8,9,10,11,12,13,14,15},{16,17,18,19,20,21,22,23},{24..., dimensions={0} | all-to-all | bytes 786432 | tf_op jit(solution)/shard_map/all_to_all | solution.py:382
  77.0 1.3 %collective-permute-start.13 = (bf16[64,3072]{1,0:T(8,128)(2,1)S(1)}, bf16[64,3072]{1,0:T(8,128)(2,1)S(1)}, u32[]{:S(2)}, u32[]{:S(2)}) collective-permute-start(bf16[64,3072]{1,0:T(8,128)(2,1)S(1)} %unpack_text.1), channel_id=1, source_target_pairs={{8,0},{12,4},{16,24},{20,28},{9,1},{13,5},{17,25},{21,29},{10,2},{... | collective-permute-start | bytes 1179656 | tf_op jit(solution)/shard_map/ppermute | solution.py:441
  78.4 0.5 collective-permute-start.5
  78.9 7.8 %collective-permute-done.13 = bf16[64,3072]{1,0:T(8,128)(2,1)S(1)} collective-permute-done((bf16[64,3072]{1,0:T(8,128)(2,1)S(1)}, bf16[64,3072]{1,0:T(8,128)(2,1)S(1)}, u32[]{:S(2)}, u32[]{:S(2)}) %collective-permute-start.13) | collective-permute-done | bytes 393248 | tf_op jit(solution)/shard_map/ppermute | solution.py:441
  86.8 1.0 collective-permute-start.14
  87.8 11.5 %attend_image.1 = bf16[8,64,384]{2,1,0:T(8,128)(2,1)} custom-call(s32[5]{0:T(128)S(1)} %stack.39.info, bf16[8,64,1152]{2,1,0:T(8,128)(2,1)S(1)} %copy-done.1, bf16[8,64,1152]{2,1,0:T(8,128)(2,1)S(1)} %copy-done.1, bf16[8,64,1152]{2,1,0:T(8,128)(2,1)S(1)} %copy-done.1, bf16[8,64,1152]{2,1,0:T(8,128)(2,1)S(1)} %all-to-all-done.refs_3_.refs_0_.refs_1_.refs_2_.refs_4_, ...), custom_call_target="tpu_custom_call" | custom-call | flops 2013265920 | bytes 4718592 | tf_op jit(solution)/shard_map/attend_image/pallas_call | solution.py:230
  99.3 3.4 %all-to-all-start.2 = ((bf16[8,64,384]{2,1,0:T(8,128)(2,1)}), bf16[8,64,384]{2,1,0:T(8,128)(2,1)S(1)}, u32[]{:S(2)}, u32[]{:S(2)}) async-start(bf16[8,64,384]{2,1,0:T(8,128)(2,1)} %attend_image.1), calls=%async_computation.2 | async-start | bytes 786432 | tf_op jit(solution)/shard_map/all_to_all | solution.py:382
  102.8 0.9 pad_maximum_fusion
  103.7 6.6 %all-to-all-done.2.x_ref = bf16[8,64,384]{2,1,0:T(8,128)(2,1)S(1)} async-done(((bf16[8,64,384]{2,1,0:T(8,128)(2,1)}), bf16[8,64,384]{2,1,0:T(8,128)(2,1)S(1)}, u32[]{:S(2)}, u32[]{:S(2)}) %all-to-all-start.2) | async-done | bytes 393248 | tf_op jit(solution)/shard_map/all_to_all | solution.py:382
  110.3 7.8 %project.1 = bf16[64,3072]{1,0:T(8,128)(2,1)} custom-call(bf16[8,64,384]{2,1,0:T(8,128)(2,1)S(1)} %all-to-all-done.2.x_ref, bf16[8,384,3072]{2,1,0:T(8,128)(2,1)} %bitcast.8, bf16[64,3072]{1,0:T(8,128)(2,1)S(1)} %copy-done.8, f32[1,3072]{1,0:T(1,128)S(1)} %bitcast.7), custom_call_target="tpu_custom_call" | custom-call | flops 1207959552 | bytes 18874368 | tf_op jit(solution)/shard_map/project/pallas_call | solution.py:311
  (37 shorter events, 1.4 us)
Async XLA Ops:
  0.6 19.0 %collective-permute-start = (bf16[2,256,768]{2,1,0:T(8,128)(2,1)}, bf16[2,256,768]{2,1,0:T(8,128)(2,1)S(1)}, u32[]{:S(2)}, u32[]{:S(2)}) collective-permute-start(bf16[2,256,768]{2,1,0:T(8,128)(2,1)} %refs_5_.1), channel_id=1, source_target_pairs={{0,8},{8,16},{16,24},{12,4},{20,12},{28,20},{1,9},{9,17},{17,25},{... | collective-permute-start | bytes 2359304 | tf_op jit(solution)/shard_map/ppermute | solution.py:408
  2.7 19.9 %collective-permute-start.1 = (bf16[2,256,768]{2,1,0:T(8,128)(2,1)}, bf16[2,256,768]{2,1,0:T(8,128)(2,1)}, u32[]{:S(2)}, u32[]{:S(2)}) collective-permute-start(bf16[2,256,768]{2,1,0:T(8,128)(2,1)} %refs_5_.1), channel_id=1, source_target_pairs={{4,8},{12,16},{20,24},{8,4},{16,12},{24,20},{5,9},{13,17},{21,25},... | collective-permute-start | bytes 2359304 | tf_op jit(solution)/shard_map/ppermute | solution.py:408
  5.7 1.7 %copy-start.2 = (bf16[128,9216]{1,0:T(8,128)(2,1)S(1)}, bf16[128,9216]{1,0:T(8,128)(2,1)}, u32[]{:S(2)}) copy-start(bf16[128,9216]{1,0:T(8,128)(2,1)} %refs_2_.2) | copy-start | bytes 7077892
  8.1 1.0 copy-start.4
  9.1 21.0 %copy-start.3 = (bf16[64,9216]{1,0:T(8,128)(2,1)S(1)}, bf16[64,9216]{1,0:T(8,128)(2,1)}, u32[]{:S(2)}) copy-start(bf16[64,9216]{1,0:T(8,128)(2,1)} %refs_2_.3) | copy-start | bytes 3538948
  9.1 21.0 %all-to-all-start = ((bf16[8,64,1152]{2,1,0:T(8,128)(2,1)}), bf16[8,64,1152]{2,1,0:T(8,128)(2,1)S(1)}, u32[]{:S(2)}, u32[]{:S(2)}) async-start(bf16[8,64,1152]{2,1,0:T(8,128)(2,1)} %copy-done.4), calls=%async_computation | async-start | bytes 2359296 | tf_op jit(solution)/shard_map/all_to_all | solution.py:382
  19.7 16.4 %collective-permute-start.3 = (bf16[2,256,768]{2,1,0:T(8,128)(2,1)S(1)}, bf16[2,256,768]{2,1,0:T(8,128)(2,1)}, u32[]{:S(2)}, u32[]{:S(2)}) collective-permute-start(bf16[2,256,768]{2,1,0:T(8,128)(2,1)S(1)} %collective-permute-done.refs_4_.refs_5_.refs_7_), channel_id=1, source_target_pairs={{8,16},{16,24},{12,4},{20,12},{9,17},{17,25},{13,5},{21,13},{10,18... | collective-permute-start | bytes 2359304 | tf_op jit(solution)/shard_map/ppermute | solution.py:408
  22.6 15.8 %collective-permute-start.6 = (bf16[2,256,768]{2,1,0:T(8,128)(2,1)}, bf16[2,256,768]{2,1,0:T(8,128)(2,1)}, u32[]{:S(2)}, u32[]{:S(2)}) collective-permute-start(bf16[2,256,768]{2,1,0:T(8,128)(2,1)} %collective-permute-done.1.refs_5_.refs_6_.refs_8_), channel_id=1, source_target_pairs={{8,16},{16,24},{12,4},{20,12},{9,17},{17,25},{13,5},{21,13},{10,18... | collective-permute-start | bytes 2359304 | tf_op jit(solution)/shard_map/ppermute | solution.py:408
  30.7 1.0 copy-start.5
  31.7 28.3 %all-to-all-start.1 = ((bf16[8,64,1152]{2,1,0:T(8,128)(2,1)}), bf16[8,64,1152]{2,1,0:T(8,128)(2,1)S(1)}, u32[]{:S(2)}, u32[]{:S(2)}) async-start(bf16[8,64,1152]{2,1,0:T(8,128)(2,1)} %copy-done.5), calls=%async_computation.1 | async-start | bytes 2359296 | tf_op jit(solution)/shard_map/all_to_all | solution.py:382
  35.4 9.4 %collective-permute-start.2 = (bf16[2,256,768]{2,1,0:T(8,128)(2,1)}, bf16[2,256,768]{2,1,0:T(8,128)(2,1)}, u32[]{:S(2)}, u32[]{:S(2)}) collective-permute-start(bf16[2,256,768]{2,1,0:T(8,128)(2,1)} %refs_5_.1), channel_id=1, source_target_pairs={{0,4},{4,0},{8,12},{12,8},{16,20},{20,16},{24,28},{28,24},{1,5},{5... | collective-permute-start | bytes 2359304 | tf_op jit(solution)/shard_map/ppermute | solution.py:387
  35.6 10.9 %collective-permute-start.11 = (bf16[2,256,768]{2,1,0:T(8,128)(2,1)S(1)}, bf16[2,256,768]{2,1,0:T(8,128)(2,1)}, u32[]{:S(2)}, u32[]{:S(2)}) collective-permute-start(bf16[2,256,768]{2,1,0:T(8,128)(2,1)S(1)} %collective-permute-done.refs_4_.refs_5_.refs_7_), channel_id=1, source_target_pairs={{0,4},{4,0},{8,12},{12,8},{16,20},{20,16},{24,28},{28,24},{1,5},{5... | collective-permute-start | bytes 2359304 | tf_op jit(solution)/shard_map/ppermute | solution.py:387
  35.9 12.1 %collective-permute-start.12 = (bf16[2,256,768]{2,1,0:T(8,128)(2,1)}, bf16[2,256,768]{2,1,0:T(8,128)(2,1)}, u32[]{:S(2)}, u32[]{:S(2)}) collective-permute-start(bf16[2,256,768]{2,1,0:T(8,128)(2,1)} %collective-permute-done.1.refs_5_.refs_6_.refs_8_), channel_id=1, source_target_pairs={{0,4},{4,0},{8,12},{12,8},{16,20},{20,16},{24,28},{28,24},{1,5},{5... | collective-permute-start | bytes 2359304 | tf_op jit(solution)/shard_map/ppermute | solution.py:387
  36.1 12.0 %collective-permute-start.9 = (bf16[2,256,768]{2,1,0:T(8,128)(2,1)}, bf16[2,256,768]{2,1,0:T(8,128)(2,1)}, u32[]{:S(2)}, u32[]{:S(2)}) collective-permute-start(bf16[2,256,768]{2,1,0:T(8,128)(2,1)} %collective-permute-done.3.refs_7_.refs_11_), channel_id=1, source_target_pairs={{0,4},{4,0},{8,12},{12,8},{16,20},{20,16},{24,28},{28,24},{1,5},{5... | collective-permute-start | bytes 2359304 | tf_op jit(solution)/shard_map/ppermute | solution.py:387
  38.4 9.7 %collective-permute-start.10 = (bf16[2,256,768]{2,1,0:T(8,128)(2,1)}, bf16[2,256,768]{2,1,0:T(8,128)(2,1)}, u32[]{:S(2)}, u32[]{:S(2)}) collective-permute-start(bf16[2,256,768]{2,1,0:T(8,128)(2,1)} %collective-permute-done.6.refs_8_.refs_12_), channel_id=1, source_target_pairs={{0,4},{4,0},{8,12},{12,8},{16,20},{20,16},{24,28},{28,24},{1,5},{5... | collective-permute-start | bytes 2359304 | tf_op jit(solution)/shard_map/ppermute | solution.py:387
  44.8 33.5 %collective-permute-start.4 = (bf16[2,256,768]{2,1,0:T(8,128)(2,1)}, bf16[2,256,768]{2,1,0:T(8,128)(2,1)}, u32[]{:S(2)}, u32[]{:S(2)}) collective-permute-start(bf16[2,256,768]{2,1,0:T(8,128)(2,1)} %collective-permute-done.3.refs_7_.refs_11_), channel_id=1, source_target_pairs={{16,24},{12,4},{17,25},{13,5},{18,26},{14,6},{19,27},{15,7}} | collective-permute-start | bytes 2359304 | tf_op jit(solution)/shard_map/ppermute | solution.py:408
  46.5 32.4 %collective-permute-start.7 = (bf16[2,256,768]{2,1,0:T(8,128)(2,1)}, bf16[2,256,768]{2,1,0:T(8,128)(2,1)}, u32[]{:S(2)}, u32[]{:S(2)}) collective-permute-start(bf16[2,256,768]{2,1,0:T(8,128)(2,1)} %collective-permute-done.6.refs_8_.refs_12_), channel_id=1, source_target_pairs={{16,24},{12,4},{17,25},{13,5},{18,26},{14,6},{19,27},{15,7}} | collective-permute-start | bytes 2359304 | tf_op jit(solution)/shard_map/ppermute | solution.py:408
  48.1 1.1 copy-start.6
  60.1 1.0 copy-start
  61.1 26.7 %copy-start.1 = (bf16[8,64,1152]{2,1,0:T(8,128)(2,1)S(1)}, bf16[8,64,1152]{2,1,0:T(8,128)(2,1)}, u32[]{:S(2)}) copy-start(bf16[8,64,1152]{2,1,0:T(8,128)(2,1)} %copy-done) | copy-start | bytes 3538948
  61.1 26.7 %copy-start.7 = (bf16[2,256,768]{2,1,0:T(8,128)(2,1)S(1)}, bf16[2,256,768]{2,1,0:T(8,128)(2,1)}, u32[]{:S(2)}) copy-start(bf16[2,256,768]{2,1,0:T(8,128)(2,1)} %refs_5_.1) | copy-start | bytes 2359300
  77.0 9.7 %collective-permute-start.13 = (bf16[64,3072]{1,0:T(8,128)(2,1)S(1)}, bf16[64,3072]{1,0:T(8,128)(2,1)S(1)}, u32[]{:S(2)}, u32[]{:S(2)}) collective-permute-start(bf16[64,3072]{1,0:T(8,128)(2,1)S(1)} %unpack_text.1), channel_id=1, source_target_pairs={{8,0},{12,4},{16,24},{20,28},{9,1},{13,5},{17,25},{21,29},{10,2},{... | collective-permute-start | bytes 1179656 | tf_op jit(solution)/shard_map/ppermute | solution.py:441
  78.4 9.4 %collective-permute-start.5 = (bf16[2,256,768]{2,1,0:T(8,128)(2,1)}, bf16[2,256,768]{2,1,0:T(8,128)(2,1)S(1)}, u32[]{:S(2)}, u32[]{:S(2)}) collective-permute-start(bf16[2,256,768]{2,1,0:T(8,128)(2,1)} %collective-permute-done.4.refs_15_), channel_id=1, source_target_pairs={{0,4},{4,0},{8,12},{12,8},{16,20},{20,16},{24,28},{28,24},{1,5},{5... | collective-permute-start | bytes 2359304 | tf_op jit(solution)/shard_map/ppermute | solution.py:387
  78.8 8.9 %collective-permute-start.8 = (bf16[2,256,768]{2,1,0:T(8,128)(2,1)}, bf16[2,256,768]{2,1,0:T(8,128)(2,1)S(1)}, u32[]{:S(2)}, u32[]{:S(2)}) collective-permute-start(bf16[2,256,768]{2,1,0:T(8,128)(2,1)} %collective-permute-done.7.refs_16_), channel_id=1, source_target_pairs={{0,4},{4,0},{8,12},{12,8},{16,20},{20,16},{24,28},{28,24},{1,5},{5... | collective-permute-start | bytes 2359304 | tf_op jit(solution)/shard_map/ppermute | solution.py:387
  86.8 15.9 %collective-permute-start.14 = (bf16[64,3072]{1,0:T(8,128)(2,1)S(1)}, bf16[64,3072]{1,0:T(8,128)(2,1)S(1)}, u32[]{:S(2)}, u32[]{:S(2)}) collective-permute-start(bf16[64,3072]{1,0:T(8,128)(2,1)S(1)} %broadcast_select_fusion), channel_id=1, source_target_pairs={{0,4},{4,0},{8,12},{12,8},{16,20},{20,16},{24,28},{28,24},{1,5},{5... | collective-permute-start | bytes 1179656 | tf_op jit(solution)/shard_map/ppermute | solution.py:387
  99.3 11.1 %all-to-all-start.2 = ((bf16[8,64,384]{2,1,0:T(8,128)(2,1)}), bf16[8,64,384]{2,1,0:T(8,128)(2,1)S(1)}, u32[]{:S(2)}, u32[]{:S(2)}) async-start(bf16[8,64,384]{2,1,0:T(8,128)(2,1)} %attend_image.1), calls=%async_computation.2 | async-start | bytes 786432 | tf_op jit(solution)/shard_map/all_to_all | solution.py:382
  102.7 7.7 %copy-start.8 = (bf16[64,3072]{1,0:T(8,128)(2,1)S(1)}, bf16[64,3072]{1,0:T(8,128)(2,1)}, u32[]{:S(2)}) copy-start(bf16[64,3072]{1,0:T(8,128)(2,1)} %residual.1) | copy-start | bytes 1179652
  102.7 7.6 %copy-start.9 = (f32[3072]{0:T(1024)S(1)}, f32[3072]{0:T(1024)}, u32[]{:S(2)}) copy-start(f32[3072]{0:T(1024)} %param.10) | copy-start | bytes 36868

commit v9 on v8

--- a/solution.py
+++ b/solution.py
@@ -10,9 +10,9 @@
 
 HD = 128
 SCALE = math.log2(math.e) / math.sqrt(HD)
-VMEM_LIMIT = 12 * 1024 * 1024
+VMEM_LIMIT = 20 * 1024 * 1024
 WIDE_LIMIT = 48 * 1024 * 1024
-TILE = 256
+TILE = 512
 FIRST_KEYS = 256
 LARGE = 2.0**60
 
@@ -95,7 +95,12 @@
     def __init__(self, entries, heads):
         self.entries = [[len(blocks) for blocks in candidates] for candidates in entries]
         self.operands = [b for candidates in entries for blocks in candidates for b in blocks]
-        self.specs = [stale_spec(block, heads) for block in self.operands]
+        self.specs = [
+            stale_spec(block, heads, (index, place) if len(candidates) > 1 else None)
+            for index, candidates in enumerate(entries)
+            for place, blocks in enumerate(candidates)
+            for block in blocks
+        ]
         rows = sum(block.shape[1] for block in entries[0][0])
         self.scratch = pltpu.VMEM((len(entries), 2, rows, HD), self.operands[0].dtype)
 
@@ -117,9 +122,15 @@
         return [(chosen[index, 0], chosen[index, 1]) for index in range(len(self.entries))]
 
 
-def stale_spec(block, heads):
-    shape = (2, block.shape[1], HD)
-    return pl.BlockSpec(shape, lambda h, info: (0, 0, info[0] * heads + h))
+def stale_spec(block, heads, candidate=None):
+    def place(h, info):
+        column = info[0] * heads + h
+        if candidate is not None:
+            index, second = candidate
+            column = jnp.where(info[1 + index] == 1 - second, column, 0)
+        return (0, 0, column)
+
+    return pl.BlockSpec((2, block.shape[1], HD), place)
 
 
 def column_spec(shape, offset=0):
@@ -434,7 +445,7 @@
     image_attn = attend_image(info, img, txt, stale, entries, text_attn)
     text_back = exchange(after(text_attn, img))
 
-    text_out = unpack(text_back, order)
+    text_out = unpack(after(text_back, image_attn), order)
     if early:
         ends = [(1, 0), (planes - 2, planes - 1)]
         ends = [(a * pair + c, b * pair + c) for a, b in ends for c in range(pair)]

time: 120 us -> 121 us (level)
  the two profiles are of different devices: /device:TPU:17 before, /device:TPU:1 now
where the time goes in v9:
time: 121 us
  waiting for transfers between devices  51.3 us (42%)
  starting transfers between devices  32.3 us (27%)
  Pallas kernels  24.4 us (20%)
  local copies, waits for them, and re-layouts  10.8 us (9%)
    ppermute x6, waiting for transfers between devices, per_device(): lax.ppermute(block, 'patch', way)  25.6 us
    all_to_all x4, starting transfers between devices, exchange(): lax.all_to_all(x, ('patch', 'head'), split_axis=0, concat_axis=0, axis_in...  15.4 us
    ppermute x1, waiting for transfers between devices, per_device(): text_out = jnp.where(inner, text_out, lax.ppermute(text_out, 'patch', ends))  15.4 us
    pallas_call x2, Pallas kernels, call_heads(): pl.pallas_call(body, grid_spec=pltpu.PrefetchScalarGridSpec(num_scalar_pr...  15.2 us
    ppermute x6, starting transfers between devices, per_device(): lax.ppermute(block, 'patch', way)  13.2 us
    unnamed x25, local copies, waits for them, and re-layouts  10.8 us
    all_to_all x4, waiting for transfers between devices, exchange(): lax.all_to_all(x, ('patch', 'head'), split_axis=0, concat_axis=0, axis_in...  10.3 us
    pallas_call x1, Pallas kernels, project(): pl.pallas_call(functools.partial(project_body, order), in_specs=[vmem, pl...  7.82 us
  transfers between devices with their start and end apart: 19, of which 7 were waited for; matrix products, arithmetic and copies ran while one was open for 1% of the time, Pallas kernels for 20%

profile of v9, /device:TPU:1, one launch (start us, length us, event | category | flops | bytes accessed | tf_op | source)
XLA Modules:
  0.0 120.7 jit_solution(4343419562320547938)
XLA Ops:
  0.6 1.3 %collective-permute-start = (bf16[2,256,768]{2,1,0:T(8,128)(2,1)}, bf16[2,256,768]{2,1,0:T(8,128)(2,1)S(1)}, u32[]{:S(2)}, u32[]{:S(2)}) collective-permute-start(bf16[2,256,768]{2,1,0:T(8,128)(2,1)} %refs_5_.1), channel_id=1, source_target_pairs={{0,8},{8,16},{16,24},{12,4},{20,12},{28,20},{1,9},{9,17},{17,25},{... | collective-permute-start | bytes 2359304 | tf_op jit(solution)/shard_map/ppermute | solution.py:419
  1.9 6.8 %collective-permute-start.1 = (bf16[2,256,768]{2,1,0:T(8,128)(2,1)}, bf16[2,256,768]{2,1,0:T(8,128)(2,1)}, u32[]{:S(2)}, u32[]{:S(2)}) collective-permute-start(bf16[2,256,768]{2,1,0:T(8,128)(2,1)} %refs_5_.1), channel_id=1, source_target_pairs={{4,8},{12,16},{20,24},{8,4},{16,12},{24,20},{5,9},{13,17},{21,25},... | collective-permute-start | bytes 2359304 | tf_op jit(solution)/shard_map/ppermute | solution.py:419
  8.7 9.5 %collective-permute-done.refs_4_.refs_5_.refs_7_ = bf16[2,256,768]{2,1,0:T(8,128)(2,1)S(1)} collective-permute-done((bf16[2,256,768]{2,1,0:T(8,128)(2,1)}, bf16[2,256,768]{2,1,0:T(8,128)(2,1)S(1)}, u32[]{:S(2)}, u32[]{:S(2)}) %collective-permute-start) | collective-permute-done | bytes 786464 | tf_op jit(solution)/shard_map/ppermute | solution.py:419
  18.3 1.3 %collective-permute-start.3 = (bf16[2,256,768]{2,1,0:T(8,128)(2,1)S(1)}, bf16[2,256,768]{2,1,0:T(8,128)(2,1)}, u32[]{:S(2)}, u32[]{:S(2)}) collective-permute-start(bf16[2,256,768]{2,1,0:T(8,128)(2,1)S(1)} %collective-permute-done.refs_4_.refs_5_.refs_7_), channel_id=1, source_target_pairs={{8,16},{16,24},{12,4},{20,12},{9,17},{17,25},{13,5},{21,13},{10,18... | collective-permute-start | bytes 2359304 | tf_op jit(solution)/shard_map/ppermute | solution.py:419
  19.5 3.9 %collective-permute-done.1.refs_5_.refs_6_.refs_8_ = bf16[2,256,768]{2,1,0:T(8,128)(2,1)} collective-permute-done((bf16[2,256,768]{2,1,0:T(8,128)(2,1)}, bf16[2,256,768]{2,1,0:T(8,128)(2,1)}, u32[]{:S(2)}, u32[]{:S(2)}) %collective-permute-start.1) | collective-permute-done | bytes 786464 | tf_op jit(solution)/shard_map/ppermute | solution.py:419
  23.5 1.3 %collective-permute-start.6 = (bf16[2,256,768]{2,1,0:T(8,128)(2,1)}, bf16[2,256,768]{2,1,0:T(8,128)(2,1)}, u32[]{:S(2)}, u32[]{:S(2)}) collective-permute-start(bf16[2,256,768]{2,1,0:T(8,128)(2,1)} %collective-permute-done.1.refs_5_.refs_6_.refs_8_), channel_id=1, source_target_pairs={{8,16},{16,24},{12,4},{20,12},{9,17},{17,25},{13,5},{21,13},{10,18... | collective-permute-start | bytes 2359304 | tf_op jit(solution)/shard_map/ppermute | solution.py:419
  24.8 1.7 %copy-done.2 = bf16[128,9216]{1,0:T(8,128)(2,1)S(1)} copy-done((bf16[128,9216]{1,0:T(8,128)(2,1)S(1)}, bf16[128,9216]{1,0:T(8,128)(2,1)}, u32[]{:S(2)}) %copy-start.2) | copy-done | bytes 2359320
  27.1 1.0 copy-done.4
  28.1 4.0 %all-to-all-start = ((bf16[8,64,1152]{2,1,0:T(8,128)(2,1)}), bf16[8,64,1152]{2,1,0:T(8,128)(2,1)S(1)}, u32[]{:S(2)}, u32[]{:S(2)}) async-start(bf16[8,64,1152]{2,1,0:T(8,128)(2,1)} %copy-done.4), calls=%async_computation | async-start | bytes 2359296 | tf_op jit(solution)/shard_map/all_to_all | solution.py:393
  32.6 1.3 %collective-permute-start.4 = (bf16[2,256,768]{2,1,0:T(8,128)(2,1)}, bf16[2,256,768]{2,1,0:T(8,128)(2,1)}, u32[]{:S(2)}, u32[]{:S(2)}) collective-permute-start(bf16[2,256,768]{2,1,0:T(8,128)(2,1)} %collective-permute-done.3.refs_7_.refs_11_), channel_id=1, source_target_pairs={{16,24},{12,4},{17,25},{13,5},{18,26},{14,6},{19,27},{15,7}} | collective-permute-start | bytes 2359304 | tf_op jit(solution)/shard_map/ppermute | solution.py:419
  33.9 6.4 %collective-permute-done.6.refs_8_.refs_12_ = bf16[2,256,768]{2,1,0:T(8,128)(2,1)} collective-permute-done((bf16[2,256,768]{2,1,0:T(8,128)(2,1)}, bf16[2,256,768]{2,1,0:T(8,128)(2,1)}, u32[]{:S(2)}, u32[]{:S(2)}) %collective-permute-start.6) | collective-permute-done | bytes 786464 | tf_op jit(solution)/shard_map/ppermute | solution.py:419
  40.3 1.3 %collective-permute-start.7 = (bf16[2,256,768]{2,1,0:T(8,128)(2,1)}, bf16[2,256,768]{2,1,0:T(8,128)(2,1)}, u32[]{:S(2)}, u32[]{:S(2)}) collective-permute-start(bf16[2,256,768]{2,1,0:T(8,128)(2,1)} %collective-permute-done.6.refs_8_.refs_12_), channel_id=1, source_target_pairs={{16,24},{12,4},{17,25},{13,5},{18,26},{14,6},{19,27},{15,7}} | collective-permute-start | bytes 2359304 | tf_op jit(solution)/shard_map/ppermute | solution.py:419
  41.5 6.6 %all-to-all-done.refs_3_.refs_0_.refs_1_.refs_2_.refs_4_ = bf16[8,64,1152]{2,1,0:T(8,128)(2,1)S(1)} async-done(((bf16[8,64,1152]{2,1,0:T(8,128)(2,1)}), bf16[8,64,1152]{2,1,0:T(8,128)(2,1)S(1)}, u32[]{:S(2)}, u32[]{:S(2)}) %all-to-all-start) | async-done | bytes 1179680 | tf_op jit(solution)/shard_map/all_to_all | solution.py:393
  48.9 1.0 copy-done.5
  49.9 3.7 %all-to-all-start.1 = ((bf16[8,64,1152]{2,1,0:T(8,128)(2,1)}), bf16[8,64,1152]{2,1,0:T(8,128)(2,1)S(1)}, u32[]{:S(2)}, u32[]{:S(2)}) async-start(bf16[8,64,1152]{2,1,0:T(8,128)(2,1)} %copy-done.5), calls=%async_computation.1 | async-start | bytes 2359296 | tf_op jit(solution)/shard_map/all_to_all | solution.py:393
  54.6 5.8 %collective-permute-done.7.refs_16_ = bf16[2,256,768]{2,1,0:T(8,128)(2,1)} collective-permute-done((bf16[2,256,768]{2,1,0:T(8,128)(2,1)}, bf16[2,256,768]{2,1,0:T(8,128)(2,1)}, u32[]{:S(2)}, u32[]{:S(2)}) %collective-permute-start.7) | collective-permute-done | bytes 786464 | tf_op jit(solution)/shard_map/ppermute | solution.py:419
  60.6 1.1 copy-done.8
  61.7 3.6 %attend_text.1.refs_19_ = bf16[8,64,384]{2,1,0:T(8,128)(2,1)S(1)} custom-call(s32[5]{0:T(128)S(1)} %stack.39.info, bf16[8,64,1152]{2,1,0:T(8,128)(2,1)S(1)} %all-to-all-done.refs_3_.refs_0_.refs_1_.refs_2_.refs_4_, bf16[8,64,1152]{2,1,0:T(8,128)(2,1)S(1)} %all-to-all-done.refs_3_.refs_0_.refs_1_.refs_2_.refs_4_, ...), custom_call_target="tpu_custom_call" | custom-call | flops 1610612736 | bytes 3932160 | tf_op jit(solution)/shard_map/attend_text/pallas_call | solution.py:241
  65.3 0.7 copy.10.refs_0_
  66.0 3.6 %all-to-all-done.1.refs_0_.refs_1_.refs_2_ = bf16[8,64,1152]{2,1,0:T(8,128)(2,1)S(1)} async-done(((bf16[8,64,1152]{2,1,0:T(8,128)(2,1)}), bf16[8,64,1152]{2,1,0:T(8,128)(2,1)S(1)}, u32[]{:S(2)}, u32[]{:S(2)}) %all-to-all-start.1) | async-done | bytes 1179680 | tf_op jit(solution)/shard_map/all_to_all | solution.py:393
  69.7 1.0 copy-done
  70.7 3.6 %all-to-all-start.3 = ((bf16[8,64,384]{2,1,0:T(8,128)(2,1)}), bf16[8,64,384]{2,1,0:T(8,128)(2,1)S(1)}, u32[]{:S(2)}, u32[]{:S(2)}) async-start(bf16[8,64,384]{2,1,0:T(8,128)(2,1)} %after.2), calls=%async_computation.3 | async-start | bytes 786432 | tf_op jit(solution)/shard_map/all_to_all | solution.py:393
  74.3 1.3 %copy-done.1 = bf16[8,64,1152]{2,1,0:T(8,128)(2,1)S(1)} copy-done((bf16[8,64,1152]{2,1,0:T(8,128)(2,1)S(1)}, bf16[8,64,1152]{2,1,0:T(8,128)(2,1)}, u32[]{:S(2)}) %copy-start.1) | copy-done | bytes 1179672
  75.6 1.1 copy-done.9
  76.7 11.6 %attend_image.1.refs_1_ = bf16[8,64,384]{2,1,0:T(8,128)(2,1)} custom-call(s32[5]{0:T(128)S(1)} %stack.39.info, bf16[8,64,1152]{2,1,0:T(8,128)(2,1)S(1)} %copy-done.1, bf16[8,64,1152]{2,1,0:T(8,128)(2,1)S(1)} %copy-done.1, bf16[8,64,1152]{2,1,0:T(8,128)(2,1)S(1)} %copy-done.1, bf16[8,64,1152]{2,1,0:T(8,128)(2,1)S(1)} %all-to-all-done.refs_3_.refs_0_.refs_1_.refs_2_.refs_4_, ...), custom_call_target="tpu_custom_call" | custom-call | flops 2013265920 | bytes 4718592 | tf_op jit(solution)/shard_map/attend_image/pallas_call | solution.py:241
  88.3 0.7 copy-done.6
  89.1 1.0 copy-done.7
  90.1 1.4 %collective-permute-start.13 = (bf16[64,3072]{1,0:T(8,128)(2,1)S(1)}, bf16[64,3072]{1,0:T(8,128)(2,1)S(1)}, u32[]{:S(2)}, u32[]{:S(2)}) collective-permute-start(bf16[64,3072]{1,0:T(8,128)(2,1)S(1)} %unpack_text.1), channel_id=1, source_target_pairs={{8,0},{12,4},{16,24},{20,28},{9,1},{13,5},{17,25},{21,29},{10,2},{... | collective-permute-start | bytes 1179656 | tf_op jit(solution)/shard_map/ppermute | solution.py:452
  91.5 4.2 %all-to-all-start.2 = ((bf16[8,64,384]{2,1,0:T(8,128)(2,1)}), bf16[8,64,384]{2,1,0:T(8,128)(2,1)S(1)}, u32[]{:S(2)}, u32[]{:S(2)}) async-start(bf16[8,64,384]{2,1,0:T(8,128)(2,1)} %attend_image.1.refs_1_), calls=%async_computation.2 | async-start | bytes 786432 | tf_op jit(solution)/shard_map/all_to_all | solution.py:393
  95.7 15.4 %collective-permute-done.13 = bf16[64,3072]{1,0:T(8,128)(2,1)S(1)} collective-permute-done((bf16[64,3072]{1,0:T(8,128)(2,1)S(1)}, bf16[64,3072]{1,0:T(8,128)(2,1)S(1)}, u32[]{:S(2)}, u32[]{:S(2)}) %collective-permute-start.13) | collective-permute-done | bytes 393248 | tf_op jit(solution)/shard_map/ppermute | solution.py:452
  111.8 7.8 %project.1 = bf16[64,3072]{1,0:T(8,128)(2,1)} custom-call(bf16[8,64,384]{2,1,0:T(8,128)(2,1)S(1)} %all-to-all-done.2.x_ref, bf16[8,384,3072]{2,1,0:T(8,128)(2,1)} %bitcast.8, bf16[64,3072]{1,0:T(8,128)(2,1)S(1)} %copy-done.10, f32[1,3072]{1,0:T(1,128)S(1)} %bitcast.7), custom_call_target="tpu_custom_call" | custom-call | flops 1207959552 | bytes 18874368 | tf_op jit(solution)/shard_map/project/pallas_call | solution.py:322
  119.7 0.9 pad_maximum_fusion
  (43 shorter events, 3.8 us)
Async XLA Ops:
  0.6 17.6 %collective-permute-start = (bf16[2,256,768]{2,1,0:T(8,128)(2,1)}, bf16[2,256,768]{2,1,0:T(8,128)(2,1)S(1)}, u32[]{:S(2)}, u32[]{:S(2)}) collective-permute-start(bf16[2,256,768]{2,1,0:T(8,128)(2,1)} %refs_5_.1), channel_id=1, source_target_pairs={{0,8},{8,16},{16,24},{12,4},{20,12},{28,20},{1,9},{9,17},{17,25},{... | collective-permute-start | bytes 2359304 | tf_op jit(solution)/shard_map/ppermute | solution.py:419
  1.9 21.5 %collective-permute-start.1 = (bf16[2,256,768]{2,1,0:T(8,128)(2,1)}, bf16[2,256,768]{2,1,0:T(8,128)(2,1)}, u32[]{:S(2)}, u32[]{:S(2)}) collective-permute-start(bf16[2,256,768]{2,1,0:T(8,128)(2,1)} %refs_5_.1), channel_id=1, source_target_pairs={{4,8},{12,16},{20,24},{8,4},{16,12},{24,20},{5,9},{13,17},{21,25},... | collective-permute-start | bytes 2359304 | tf_op jit(solution)/shard_map/ppermute | solution.py:419
  18.3 14.4 %collective-permute-start.3 = (bf16[2,256,768]{2,1,0:T(8,128)(2,1)S(1)}, bf16[2,256,768]{2,1,0:T(8,128)(2,1)}, u32[]{:S(2)}, u32[]{:S(2)}) collective-permute-start(bf16[2,256,768]{2,1,0:T(8,128)(2,1)S(1)} %collective-permute-done.refs_4_.refs_5_.refs_7_), channel_id=1, source_target_pairs={{8,16},{16,24},{12,4},{20,12},{9,17},{17,25},{13,5},{21,13},{10,18... | collective-permute-start | bytes 2359304 | tf_op jit(solution)/shard_map/ppermute | solution.py:419
  23.5 16.8 %collective-permute-start.6 = (bf16[2,256,768]{2,1,0:T(8,128)(2,1)}, bf16[2,256,768]{2,1,0:T(8,128)(2,1)}, u32[]{:S(2)}, u32[]{:S(2)}) collective-permute-start(bf16[2,256,768]{2,1,0:T(8,128)(2,1)} %collective-permute-done.1.refs_5_.refs_6_.refs_8_), channel_id=1, source_target_pairs={{8,16},{16,24},{12,4},{20,12},{9,17},{17,25},{13,5},{21,13},{10,18... | collective-permute-start | bytes 2359304 | tf_op jit(solution)/shard_map/ppermute | solution.py:419
  24.8 1.7 %copy-start.2 = (bf16[128,9216]{1,0:T(8,128)(2,1)S(1)}, bf16[128,9216]{1,0:T(8,128)(2,1)}, u32[]{:S(2)}) copy-start(bf16[128,9216]{1,0:T(8,128)(2,1)} %refs_2_.2) | copy-start | bytes 7077892
  27.1 1.0 copy-start.4
  28.1 20.0 %copy-start.3 = (bf16[64,9216]{1,0:T(8,128)(2,1)S(1)}, bf16[64,9216]{1,0:T(8,128)(2,1)}, u32[]{:S(2)}) copy-start(bf16[64,9216]{1,0:T(8,128)(2,1)} %refs_2_.3) | copy-start | bytes 3538948
  28.1 20.0 %all-to-all-start = ((bf16[8,64,1152]{2,1,0:T(8,128)(2,1)}), bf16[8,64,1152]{2,1,0:T(8,128)(2,1)S(1)}, u32[]{:S(2)}, u32[]{:S(2)}) async-start(bf16[8,64,1152]{2,1,0:T(8,128)(2,1)} %copy-done.4), calls=%async_computation | async-start | bytes 2359296 | tf_op jit(solution)/shard_map/all_to_all | solution.py:393
  32.1 21.6 %collective-permute-start.2 = (bf16[2,256,768]{2,1,0:T(8,128)(2,1)}, bf16[2,256,768]{2,1,0:T(8,128)(2,1)}, u32[]{:S(2)}, u32[]{:S(2)}) collective-permute-start(bf16[2,256,768]{2,1,0:T(8,128)(2,1)} %refs_5_.1), channel_id=1, source_target_pairs={{0,4},{4,0},{8,12},{12,8},{16,20},{20,16},{24,28},{28,24},{1,5},{5... | collective-permute-start | bytes 2359304 | tf_op jit(solution)/shard_map/ppermute | solution.py:398
  32.1 22.0 %collective-permute-start.11 = (bf16[2,256,768]{2,1,0:T(8,128)(2,1)S(1)}, bf16[2,256,768]{2,1,0:T(8,128)(2,1)}, u32[]{:S(2)}, u32[]{:S(2)}) collective-permute-start(bf16[2,256,768]{2,1,0:T(8,128)(2,1)S(1)} %collective-permute-done.refs_4_.refs_5_.refs_7_), channel_id=1, source_target_pairs={{0,4},{4,0},{8,12},{12,8},{16,20},{20,16},{24,28},{28,24},{1,5},{5... | collective-permute-start | bytes 2359304 | tf_op jit(solution)/shard_map/ppermute | solution.py:398
  32.6 21.6 %collective-permute-start.4 = (bf16[2,256,768]{2,1,0:T(8,128)(2,1)}, bf16[2,256,768]{2,1,0:T(8,128)(2,1)}, u32[]{:S(2)}, u32[]{:S(2)}) collective-permute-start(bf16[2,256,768]{2,1,0:T(8,128)(2,1)} %collective-permute-done.3.refs_7_.refs_11_), channel_id=1, source_target_pairs={{16,24},{12,4},{17,25},{13,5},{18,26},{14,6},{19,27},{15,7}} | collective-permute-start | bytes 2359304 | tf_op jit(solution)/shard_map/ppermute | solution.py:419
  40.3 20.2 %collective-permute-start.7 = (bf16[2,256,768]{2,1,0:T(8,128)(2,1)}, bf16[2,256,768]{2,1,0:T(8,128)(2,1)}, u32[]{:S(2)}, u32[]{:S(2)}) collective-permute-start(bf16[2,256,768]{2,1,0:T(8,128)(2,1)} %collective-permute-done.6.refs_8_.refs_12_), channel_id=1, source_target_pairs={{16,24},{12,4},{17,25},{13,5},{18,26},{14,6},{19,27},{15,7}} | collective-permute-start | bytes 2359304 | tf_op jit(solution)/shard_map/ppermute | solution.py:419
  48.9 1.0 copy-start.5
  49.9 19.8 %all-to-all-start.1 = ((bf16[8,64,1152]{2,1,0:T(8,128)(2,1)}), bf16[8,64,1152]{2,1,0:T(8,128)(2,1)S(1)}, u32[]{:S(2)}, u32[]{:S(2)}) async-start(bf16[8,64,1152]{2,1,0:T(8,128)(2,1)} %copy-done.5), calls=%async_computation.1 | async-start | bytes 2359296 | tf_op jit(solution)/shard_map/all_to_all | solution.py:393
  53.6 7.0 %collective-permute-start.12 = (bf16[2,256,768]{2,1,0:T(8,128)(2,1)}, bf16[2,256,768]{2,1,0:T(8,128)(2,1)}, u32[]{:S(2)}, u32[]{:S(2)}) collective-permute-start(bf16[2,256,768]{2,1,0:T(8,128)(2,1)} %collective-permute-done.1.refs_5_.refs_6_.refs_8_), channel_id=1, source_target_pairs={{0,4},{4,0},{8,12},{12,8},{16,20},{20,16},{24,28},{28,24},{1,5},{5... | collective-permute-start | bytes 2359304 | tf_op jit(solution)/shard_map/ppermute | solution.py:398
  53.7 6.8 %collective-permute-start.9 = (bf16[2,256,768]{2,1,0:T(8,128)(2,1)}, bf16[2,256,768]{2,1,0:T(8,128)(2,1)}, u32[]{:S(2)}, u32[]{:S(2)}) collective-permute-start(bf16[2,256,768]{2,1,0:T(8,128)(2,1)} %collective-permute-done.3.refs_7_.refs_11_), channel_id=1, source_target_pairs={{0,4},{4,0},{8,12},{12,8},{16,20},{20,16},{24,28},{28,24},{1,5},{5... | collective-permute-start | bytes 2359304 | tf_op jit(solution)/shard_map/ppermute | solution.py:398
  54.1 6.4 %collective-permute-start.10 = (bf16[2,256,768]{2,1,0:T(8,128)(2,1)}, bf16[2,256,768]{2,1,0:T(8,128)(2,1)}, u32[]{:S(2)}, u32[]{:S(2)}) collective-permute-start(bf16[2,256,768]{2,1,0:T(8,128)(2,1)} %collective-permute-done.6.refs_8_.refs_12_), channel_id=1, source_target_pairs={{0,4},{4,0},{8,12},{12,8},{16,20},{20,16},{24,28},{28,24},{1,5},{5... | collective-permute-start | bytes 2359304 | tf_op jit(solution)/shard_map/ppermute | solution.py:398
  54.3 20.0 %collective-permute-start.5 = (bf16[2,256,768]{2,1,0:T(8,128)(2,1)}, bf16[2,256,768]{2,1,0:T(8,128)(2,1)}, u32[]{:S(2)}, u32[]{:S(2)}) collective-permute-start(bf16[2,256,768]{2,1,0:T(8,128)(2,1)} %collective-permute-done.4.refs_15_), channel_id=1, source_target_pairs={{0,4},{4,0},{8,12},{12,8},{16,20},{20,16},{24,28},{28,24},{1,5},{5... | collective-permute-start | bytes 2359304 | tf_op jit(solution)/shard_map/ppermute | solution.py:398
  60.4 13.8 %collective-permute-start.8 = (bf16[2,256,768]{2,1,0:T(8,128)(2,1)}, bf16[2,256,768]{2,1,0:T(8,128)(2,1)}, u32[]{:S(2)}, u32[]{:S(2)}) collective-permute-start(bf16[2,256,768]{2,1,0:T(8,128)(2,1)} %collective-permute-done.7.refs_16_), channel_id=1, source_target_pairs={{0,4},{4,0},{8,12},{12,8},{16,20},{20,16},{24,28},{28,24},{1,5},{5... | collective-permute-start | bytes 2359304 | tf_op jit(solution)/shard_map/ppermute | solution.py:398
  60.6 1.1 copy-start.8
  69.7 1.0 copy-start
  70.7 17.6 %all-to-all-start.3 = ((bf16[8,64,384]{2,1,0:T(8,128)(2,1)}), bf16[8,64,384]{2,1,0:T(8,128)(2,1)S(1)}, u32[]{:S(2)}, u32[]{:S(2)}) async-start(bf16[8,64,384]{2,1,0:T(8,128)(2,1)} %after.2), calls=%async_computation.3 | async-start | bytes 786432 | tf_op jit(solution)/shard_map/all_to_all | solution.py:393
  74.3 1.3 %copy-start.1 = (bf16[8,64,1152]{2,1,0:T(8,128)(2,1)S(1)}, bf16[8,64,1152]{2,1,0:T(8,128)(2,1)}, u32[]{:S(2)}) copy-start(bf16[8,64,1152]{2,1,0:T(8,128)(2,1)} %copy-done) | copy-start | bytes 3538948
  75.6 1.1 copy-start.9
  88.3 0.7 copy-start.6
  89.1 1.0 copy-start.7
  90.1 21.8 %copy-start.10 = (bf16[64,3072]{1,0:T(8,128)(2,1)S(1)}, bf16[64,3072]{1,0:T(8,128)(2,1)}, u32[]{:S(2)}) copy-start(bf16[64,3072]{1,0:T(8,128)(2,1)} %residual.1) | copy-start | bytes 1179652
  90.1 21.8 %copy-start.11 = (f32[3072]{0:T(1024)S(1)}, f32[3072]{0:T(1024)}, u32[]{:S(2)}) copy-start(f32[3072]{0:T(1024)} %param.10) | copy-start | bytes 36868
  90.1 21.0 %collective-permute-start.13 = (bf16[64,3072]{1,0:T(8,128)(2,1)S(1)}, bf16[64,3072]{1,0:T(8,128)(2,1)S(1)}, u32[]{:S(2)}, u32[]{:S(2)}) collective-permute-start(bf16[64,3072]{1,0:T(8,128)(2,1)S(1)} %unpack_text.1), channel_id=1, source_target_pairs={{8,0},{12,4},{16,24},{20,28},{9,1},{13,5},{17,25},{21,29},{10,2},{... | collective-permute-start | bytes 1179656 | tf_op jit(solution)/shard_map/ppermute | solution.py:452
  91.5 20.3 %all-to-all-start.2 = ((bf16[8,64,384]{2,1,0:T(8,128)(2,1)}), bf16[8,64,384]{2,1,0:T(8,128)(2,1)S(1)}, u32[]{:S(2)}, u32[]{:S(2)}) async-start(bf16[8,64,384]{2,1,0:T(8,128)(2,1)} %attend_image.1.refs_1_), calls=%async_computation.2 | async-start | bytes 786432 | tf_op jit(solution)/shard_map/all_to_all | solution.py:393
  111.1 8.5 %collective-permute-start.14 = (bf16[64,3072]{1,0:T(8,128)(2,1)S(1)}, bf16[64,3072]{1,0:T(8,128)(2,1)S(1)}, u32[]{:S(2)}, u32[]{:S(2)}) collective-permute-start(bf16[64,3072]{1,0:T(8,128)(2,1)S(1)} %broadcast_select_fusion), channel_id=1, source_target_pairs={{0,4},{4,0},{8,12},{12,8},{16,20},{20,16},{24,28},{28,24},{1,5},{5... | collective-permute-start | bytes 1179656 | tf_op jit(solution)/shard_map/ppermute | solution.py:398

commit v10 on v8

v10 whole, which is shorter than its diff:
```python
import functools
import math

import jax
import jax.numpy as jnp
from jax import lax
from jax.experimental import pallas as pl
from jax.experimental.pallas import tpu as pltpu
from jax.sharding import PartitionSpec as P

HD = 128
SCALE = math.log2(math.e) / math.sqrt(HD)
VMEM_LIMIT = 12 * 1024 * 1024
WIDE_LIMIT = 48 * 1024 * 1024
TILE = 256
FIRST_KEYS = 256
LARGE = 2.0**60


def params(block_elements=0):
    return pltpu.CompilerParams(
        vmem_limit_bytes=VMEM_LIMIT + 4 * block_elements, dimension_semantics=("arbitrary",)
    )


def pack_body(_, *refs):
    sources, packed = refs[:3], refs[-1]
    width = sources[0].shape[1]
    for part, source in enumerate(sources):
        packed[0, :, part * width : (part + 1) * width] = source[...]


def pack(first_block, array, rows, head_owners, pair, width, after=()):
    blocks = array.shape[1] // 3 // width
    destinations = head_owners * pair

    def source(part):
        def place(d, info):
            return (info[0], part * blocks + (d % head_owners) * pair + d // head_owners)

        return pl.BlockSpec((rows, width), place)

    return pl.pallas_call(
        pack_body,
        grid_spec=pltpu.PrefetchScalarGridSpec(
            num_scalar_prefetch=1,
            grid=(destinations,),
            in_specs=[source(0), source(1), source(2)]
            + [pl.BlockSpec(memory_space=pl.ANY)] * len(after),
            out_specs=pl.BlockSpec((1, rows, 3 * width), lambda d, info: (d, 0, 0)),
        ),
        out_shape=jax.ShapeDtypeStruct((destinations, rows, 3 * width), array.dtype),
        compiler_params=params(),
        name="pack_heads",
    )(first_block, array, array, array, *after)


def dot(first, second, contract):
    return lax.dot_general(
        first, second, ((contract[:1], contract[1:]), ((), ())), preferred_element_type=jnp.float32
    )


def with_ones(block):
    return jnp.concatenate([block, jnp.ones_like(block)], axis=1)


def reference_columns(row_max):
    reference = row_max.astype(jnp.bfloat16).astype(jnp.float32)
    return jnp.broadcast_to(reference * (-1.0 / HD), (row_max.shape[0], HD)).astype(jnp.bfloat16)


def weighted(queries, key_rows, values):
    weights = jnp.exp2(dot(queries, key_rows, (1, 1)) * SCALE).astype(jnp.bfloat16)
    return dot(weights, values, (1, 0))


def tiles_of(rows):
    tile = min(TILE, rows)
    return [slice(first, min(first + tile, rows)) for first in range(0, rows, tile)]


def until_small(flag, total, attempt):
    flag[0] = 1

    @pl.loop(0, 2)
    def _(turn):
        @pl.when(flag[0] == 1)
        def _():
            attempt(turn)
            flag[0] = jnp.where(jnp.max(total[:, :, HD:]) > LARGE, 1, 0).astype(jnp.int32)


def copy_columns(target, at, block, core, width):
    columns = pl.ds(pl.multiple_of(core * width, width), width)
    target[:, at : at + block.shape[1], :] = block[:, :, columns]


def settle(info, refs, entries, chosen):
    width = chosen.shape[3]
    for index, candidates in enumerate(entries):
        for place, count in enumerate(candidates):
            blocks, refs = refs[:count], refs[count:]

            def copy():
                at = 0
                for block in blocks:
                    copy_columns(chosen.at[index], at, block, info[0], width)
                    at += block.shape[1]

            if len(candidates) == 1:
                copy()
            else:
                pl.when(info[1 + index] == 1 - place)(copy)


def accumulate(flag, total, aug, heads, queries_of, first_keys_of, own, chosen):
    def columns(head):
        return slice(head * HD, (head + 1) * HD)

    def pieces(head, some):
        return some(head) + [
            (chosen[index, 0, :, columns(head)], chosen[index, 1, :, columns(head)])
            for index in range(chosen.shape[0])
        ]

    def tiles():
        for head in range(heads):
            queries = queries_of(head)
            for span, some in own:
                for tile in tiles_of(span.stop - span.start):
                    tile = slice(span.start + tile.start, span.start + tile.stop)
                    yield head, tile, queries[tile, :], some

    def largest(queries, key_rows):
        return jnp.max(dot(queries, key_rows, (1, 1)), axis=1, keepdims=True)

    def attempt(turn):
        @pl.when(turn == 0)
        def _():
            for head, tile, queries, _ in tiles():
                aug[head, tile, :] = reference_columns(largest(queries, first_keys_of(head)))

        @pl.when(turn == 1)
        def _():
            for head, tile, queries, some in tiles():
                row_max = None
                for key_rows, _ in pieces(head, some):
                    piece_max = largest(queries, key_rows)
                    row_max = piece_max if row_max is None else jnp.maximum(row_max, piece_max)
                aug[head, tile, :] = reference_columns(row_max)

        for head, tile, queries, some in tiles():
            both = jnp.concatenate([queries, aug[head, tile, :]], axis=1)
            summed = None
            for key_rows, values in pieces(head, some):
                part = weighted(both, with_ones(key_rows), with_ones(values))
                summed = part if summed is None else summed + part
            total[head, tile, :] = summed

    until_small(flag, total, attempt)


def finish(out, total):
    for head in range(total.shape[0]):
        attended = (total[head, :, :HD] / total[head, :, HD:]).astype(out.dtype)
        out[:, :, head * HD : (head + 1) * HD] = attended.reshape(out.shape[:2] + (HD,))


def part_of(ref, part, head, width):
    first = part * width + head * HD
    return ref[:, :, first : first + HD].reshape(-1, HD)


def text_body(pair, entries, info, txt, *refs, wanted):
    stale, came = refs[:pair], refs[pair:-6]
    out, chosen, beside, aug, total, flag = refs[-6:]
    width = chosen.shape[3]
    heads = width // HD

    @pl.when(info[wanted] == 1)
    def _():
        settle(info, came, entries, chosen)
        at = 0
        for block in stale:
            copy_columns(beside.at[0], at, block, info[0], width)
            at += block.shape[1]

        def own(head):
            columns = slice(head * HD, (head + 1) * HD)
            return [
                (part_of(txt, 1, head, width), part_of(txt, 2, head, width)),
                (beside[0, 0, :, columns], beside[0, 1, :, columns]),
            ]

        accumulate(
            flag, total, aug, heads,
            lambda head: part_of(txt, 0, head, width),
            lambda head: part_of(txt, 1, head, width)[: min(FIRST_KEYS, total.shape[1]), :],
            [(slice(0, total.shape[1]), own)], chosen,
        )
        finish(out, total)


def image_body(pair, entries, info, img, txt, *refs):
    stale, came = refs[:pair], refs[pair:-6]
    out, chosen, beside, aug, total, flag = refs[-6:]
    width = chosen.shape[3]
    heads = width // HD
    rows = total.shape[1]
    group_rows, sources = rows // pair, img.shape[0] // pair
    settle(info, came, entries, chosen)
    for group in range(pair):
        for part in range(2):
            fresh = img[
                group * sources : (group + 1) * sources, :, (1 + part) * width : (2 + part) * width
            ]
            beside[group, part, :group_rows, :] = fresh.reshape(group_rows, width)
        if pair == 2:
            for place, block in enumerate(stale):

                @pl.when((info[0] == group) == (place == 1))
                def _():
                    copy_columns(beside.at[group], group_rows, block, info[0], width)

    def own(group):
        def some(head):
            columns = slice(head * HD, (head + 1) * HD)
            return [
                (part_of(txt, 1, head, width), part_of(txt, 2, head, width)),
                (beside[group, 0, :, columns], beside[group, 1, :, columns]),
            ]

        return (slice(group * group_rows, (group + 1) * group_rows), some)

    text_keys = txt.shape[0] * txt.shape[1]
    accumulate(
        flag, total, aug, heads,
        lambda head: part_of(img, 0, head, width),
        lambda head: part_of(txt, 1, head, width)[: min(FIRST_KEYS, text_keys), :],
        [own(group) for group in range(pair)], chosen,
    )
    finish(out, total)


def attend(name, body, info, fresh, stale, entries, groups):
    first = fresh[0]
    width = first.shape[2] // 3
    heads, rows = width // HD, first.shape[0] * first.shape[1]
    keys = sum(block.shape[1] for block in stale)
    came = [b for candidates in entries for blocks in candidates for b in blocks]
    counts = [[len(blocks) for blocks in candidates] for candidates in entries]
    vmem = pl.BlockSpec(memory_space=pltpu.VMEM)
    scratch = [
        ((len(entries), 2, keys, width), first.dtype),
        ((groups, 2, keys, width), first.dtype),
        ((heads, rows, HD), jnp.bfloat16),
        ((heads, rows, 2 * HD), jnp.float32),
    ]
    needed = sum(math.prod(shape) * jnp.dtype(kind).itemsize for shape, kind in scratch)
    return pl.pallas_call(
        functools.partial(body, len(stale), counts),
        in_specs=[pl.BlockSpec(memory_space=pltpu.SMEM)]
        + [vmem] * (len(fresh) + len(stale) + len(came)),
        out_specs=vmem,
        out_shape=jax.ShapeDtypeStruct(first.shape[:2] + (width,), first.dtype),
        scratch_shapes=[pltpu.VMEM(*one) for one in scratch] + [pltpu.SMEM((1,), jnp.int32)],
        compiler_params=pltpu.CompilerParams(vmem_limit_bytes=VMEM_LIMIT + needed),
        cost_estimate=pl.CostEstimate(
            flops=4 * rows * keys * (2 + len(entries)) * width,
            bytes_accessed=4 * keys * (2 + len(entries)) * width,
            transcendentals=rows * keys * (2 + len(entries)) * heads,
        ),
        name=name,
    )(info, *fresh, *stale, *came)


def project_body(order, x_ref, weight, residual, gate, out, held, total, sems):
    copies = [
        pltpu.make_async_copy(weight.at[place], held.at[place], sems.at[place])
        for place in order
    ]
    for copy in copies:
        copy.start()
    for source, (place, copy) in enumerate(zip(order, copies)):
        copy.wait()
        part = jnp.dot(x_ref[source], held[place], preferred_element_type=jnp.float32)
        if source == 0:
            total[...] = part
        else:
            total[...] += part
    out[...] = (residual[...].astype(jnp.float32) + gate[...] * total[...]).astype(out.dtype)


def project(x, order, weight, residual, gate):
    rows, model = residual.shape
    destinations, _, width = x.shape
    vmem = pl.BlockSpec(memory_space=pltpu.VMEM)
    return pl.pallas_call(
        functools.partial(project_body, order),
        in_specs=[vmem, pl.BlockSpec(memory_space=pl.ANY), vmem, vmem],
        out_specs=vmem,
        out_shape=jax.ShapeDtypeStruct((rows, model), residual.dtype),
        scratch_shapes=[
            pltpu.VMEM((destinations, width, model), weight.dtype),
            pltpu.VMEM((rows, model), jnp.float32),
            pltpu.SemaphoreType.DMA((destinations,)),
        ],
        compiler_params=pltpu.CompilerParams(vmem_limit_bytes=WIDE_LIMIT),
        cost_estimate=pl.CostEstimate(
            flops=2 * rows * model * model, bytes_accessed=2 * model * model, transcendentals=0
        ),
        name="project",
    )(x, weight.reshape(destinations, width, model), residual, gate.reshape(1, model))


def after_body(*refs):
    del refs


def after(x, other):
    anywhere = pl.BlockSpec(memory_space=pl.ANY)
    return pl.pallas_call(
        after_body,
        in_specs=[anywhere, anywhere],
        out_specs=anywhere,
        out_shape=jax.ShapeDtypeStruct(x.shape, x.dtype),
        input_output_aliases={0: 0},
        name="after",
    )(x, other)


def unpack_body(order, x_ref, out):
    width = x_ref.shape[2]
    for source, place in enumerate(order):
        out[:, place * width : (place + 1) * width] = x_ref[source]


def unpack(x, order):
    rows, model = x.shape[1], x.shape[0] * x.shape[2]
    return pl.pallas_call(
        functools.partial(unpack_body, order),
        grid=(1,),
        in_specs=[pl.BlockSpec(x.shape, lambda n: (0, 0, 0))],
        out_specs=pl.BlockSpec((rows, model), lambda n: (0, 0)),
        out_shape=jax.ShapeDtypeStruct((rows, model), x.dtype),
        compiler_params=params(),
        name="unpack_text",
    )(x)


def per_device(img_qkv, txt_qkv, stale_kv, residual, gate_scale, proj_weight):
    patches, head_owners = lax.axis_size("patch"), lax.axis_size("head")
    patch = lax.axis_index("patch")
    owned_heads = stale_kv.shape[2] // HD
    pair = 2 if patches % 2 == 0 and owned_heads % 2 == 0 else 1
    planes = patches // pair
    plane, core = patch // pair, patch % pair
    width = stale_kv.shape[2] // pair
    heads = width // HD
    img_rows, model = residual.shape
    text_rows = txt_qkv.shape[0] // pair
    destinations = pair * head_owners

    order = [(d % head_owners) * pair + d // head_owners for d in range(destinations)]
    groups = [[g * destinations + d for d in range(destinations)] for g in range(planes)]
    swap_pairs = [(p, p + 1 - 2 * (p % 2)) for p in range(patches)]

    def exchange(x):
        return lax.all_to_all(
            x, ("patch", "head"), split_axis=0, concat_axis=0, axis_index_groups=groups, tiled=True
        )

    def swap(x):
        return lax.ppermute(x, "patch", swap_pairs)

    def up_pairs(step):
        return [(z, z + 1) for z in range(step - 1, planes - 1)]

    def down_pairs(step):
        return [(z + 1, z) for z in range(0, planes - step)]

    def pack_img(earlier):
        first = jnp.zeros((1,), jnp.int32)
        return pack(first, img_qkv, img_rows, head_owners, pair, width, earlier)

    core_only = core.astype(jnp.int32).reshape(1)
    packed = pack(core_only, txt_qkv, text_rows, head_owners, pair, width)
    txt = exchange(packed)

    along, against = [], []
    if pair == 2:
        stale = [stale_kv, swap(stale_kv)]
        held = [stale_kv, stale_kv]
        for step in range(1, planes):
            pairs = [
                [(2 * a + turn, 2 * b) for a, b in up_pairs(step)]
                + [(2 * a + 1 - turn, 2 * b + 1) for a, b in down_pairs(step)]
                for turn in ((0, 1) if step == 1 else (0, 0))
            ]
            held = [lax.ppermute(block, "patch", way) for block, way in zip(held, pairs)]
            if step == 1:
                held = [after(block, packed) for block in held]
            elif step == 2:
                packed = pack_img([txt] + along[0])
                held = [after(block, packed) for block in held]
            along.append(held)
            against.append([swap(block) for block in held])
        ahead = jnp.where(core == 0, plane, planes - 1 - plane)
    else:
        stale = [stale_kv]
        from_below = from_above = stale_kv
        for step in range(1, planes):
            from_below = lax.ppermute(from_below, "patch", up_pairs(step))
            from_above = lax.ppermute(from_above, "patch", down_pairs(step))
            along.append([from_below])
            against.append([from_above])
        ahead = plane
    entries = [[along[i - 1], against[planes - i - 1]] for i in range(1, planes)]
    first_holds = [ahead >= i for i in range(1, planes)]
    if pair == 1 or planes < 3:
        packed = pack_img([txt] + along[0])
    img = exchange(packed)

    early = planes > 2
    inner = (plane > 0) & (plane < planes - 1)
    info = jnp.stack([core] + first_holds + [inner if early else core >= 0]).astype(jnp.int32)
    known = entries
    if early:
        known = [[along[0]]] + entries[1:-1] + [[against[0]]]
    text_attn = attend(
        "attend_text", functools.partial(text_body, wanted=planes), info, [txt], stale, known, 1
    )
    text_attn = after(text_attn, img)
    img = after(img, text_attn)
    image_attn = attend("attend_image", image_body, info, [img, txt], stale, entries, pair)
    image_back = exchange(image_attn)
    text_out = unpack(after(exchange(text_attn), image_attn), order)
    image_out = project(image_back, order, proj_weight, residual, gate_scale)
    if early:
        ends = [(1, 0), (planes - 2, planes - 1)]
        ends = [(a * pair + c, b * pair + c) for a, b in ends for c in range(pair)]
        hopped = after(lax.ppermute(text_out, "patch", ends), image_out)
        text_out = jnp.where(inner, text_out, hopped)
    if pair == 2:
        other = swap(text_out)
        lower = core == 0
        text_out = jnp.concatenate(
            [jnp.where(lower, text_out, other), jnp.where(lower, other, text_out)], 0
        )

    return (image_out, text_out)


def solution(mesh):
    return jax.shard_map(
        per_device,
        mesh=mesh,
        in_specs=(
            P(("patch", "head"), None),
            P("head", None),
            P(None, "patch", "head"),
            P(("patch", "head"), None),
            P(),
            P(),
        ),
        out_specs=(P(("patch", "head"), None), P("head", None)),
        check_vma=False,
    )
```

time: 120 us -> 117 us (0.975)
  blocking collectives: 15.9 us -> 0 us
  local copies, waits for them, and re-layouts: 6.69 us -> 20.4 us
  waiting for transfers between devices: 27.3 us -> 16.3 us
  starting transfers between devices: 35.6 us -> 46.4 us
    all_to_all x1 -> x0, blocking collectives: 15.9 us -> none  [exchange(): lax.all_to_all(x, ('patch', 'head'), split_axis=0, concat_axis=0, axis_in...]
    unnamed x21 -> x48, local copies, waits for them, and re-layouts: 6.6 us -> 20.3 us
    all_to_all x3 -> x4, starting transfers between devices: 12 us -> 22.3 us  [exchange(): lax.all_to_all(x, ('patch', 'head'), split_axis=0, concat_axis=0, axis_in...]
    ppermute x1, waiting for transfers between devices: 7.79 us -> 0.01 us  [per_device(): hopped = after(lax.ppermute(text_out, 'patch', ends), image_out)]
    pallas_call x2, Pallas kernels: 21.6 us -> 16.5 us  [attend(): pl.pallas_call(functools.partial(body, len(stale), counts), in_specs=[pl....]
    pallas_call x2, Pallas kernels: 1.33 us -> 5.81 us  [pack(): pl.pallas_call(pack_body, grid_spec=pltpu.PrefetchScalarGridSpec(num_scal...]
    all_to_all x3 -> x4, waiting for transfers between devices: 11.1 us -> 8.18 us  [exchange(): lax.all_to_all(x, ('patch', 'head'), split_axis=0, concat_axis=0, axis_in...]
    ppermute x6, waiting for transfers between devices: 8.46 us -> 6.61 us  [per_device(): lax.ppermute(block, 'patch', way)]
  transfers between devices with their start and end apart: 18 -> 19, of which waited for: 6 -> 5; matrix products, arithmetic and copies ran while one was open for 2% -> 0% of each run, Pallas kernels for 19% -> 27%
where the time goes in v10:
time: 117 us; the launch traced here: 116 us
  starting transfers between devices  46.4 us (40%)
  Pallas kernels  31.2 us (27%)
  local copies, waits for them, and re-layouts  20.4 us (17%)
  waiting for transfers between devices  16.3 us (14%)
    all_to_all x4, starting transfers between devices, exchange(): lax.all_to_all(x, ('patch', 'head'), split_axis=0, concat_axis=0, axis_in...  22.3 us
    unnamed x48, local copies, waits for them, and re-layouts  20.3 us
    pallas_call x2, Pallas kernels, attend(): pl.pallas_call(functools.partial(body, len(stale), counts), in_specs=[pl....  16.5 us
    ppermute x6, starting transfers between devices, per_device(): lax.ppermute(block, 'patch', way)  13.4 us
    ppermute x8, starting transfers between devices, swap(): return lax.ppermute(x, 'patch', swap_pairs)  9.4 us
    all_to_all x4, waiting for transfers between devices, exchange(): lax.all_to_all(x, ('patch', 'head'), split_axis=0, concat_axis=0, axis_in...  8.18 us
    pallas_call x1, Pallas kernels, project(): pl.pallas_call(functools.partial(project_body, order), in_specs=[vmem, pl...  7.81 us
    ppermute x6, waiting for transfers between devices, per_device(): lax.ppermute(block, 'patch', way)  6.61 us
  transfers between devices with their start and end apart: 19, of which 5 were waited for; matrix products, arithmetic and copies ran while one was open for 0% of the time, Pallas kernels for 27%

profile of v10, /device:TPU:17, one launch (start us, length us, event | category | flops | bytes accessed | tf_op | source)
XLA Modules:
  0.0 116.2 jit_solution(13649596824437707609)
XLA Ops:
  0.6 3.8 %collective-permute-start.1 = (bf16[2,256,768]{2,1,0:T(8,128)(2,1)}, bf16[2,256,768]{2,1,0:T(8,128)(2,1)S(1)}, u32[]{:S(2)}, u32[]{:S(2)}) collective-permute-start(bf16[2,256,768]{2,1,0:T(8,128)(2,1)} %refs_0_.7), channel_id=1, source_target_pairs={{4,8},{12,16},{20,24},{8,4},{16,12},{24,20},{5,9},{13,17},{21,25},... | collective-permute-start | bytes 2359304 | tf_op jit(solution)/shard_map/ppermute | solution.py:401
  4.4 2.1 %collective-permute-start = (bf16[2,256,768]{2,1,0:T(8,128)(2,1)}, bf16[2,256,768]{2,1,0:T(8,128)(2,1)S(1)}, u32[]{:S(2)}, u32[]{:S(2)}) collective-permute-start(bf16[2,256,768]{2,1,0:T(8,128)(2,1)} %refs_0_.7), channel_id=1, source_target_pairs={{0,8},{8,16},{16,24},{12,4},{20,12},{28,20},{1,9},{9,17},{17,25},{... | collective-permute-start | bytes 2359304 | tf_op jit(solution)/shard_map/ppermute | solution.py:401
  6.5 1.7 %copy-done = bf16[128,9216]{1,0:T(8,128)(2,1)S(1)} copy-done((bf16[128,9216]{1,0:T(8,128)(2,1)S(1)}, bf16[128,9216]{1,0:T(8,128)(2,1)}, u32[]{:S(2)}) %copy-start) | copy-done | bytes 2359320
  8.2 2.9 %pack_heads.2.refs_1_ = bf16[8,64,1152]{2,1,0:T(8,128)(2,1)} custom-call(s32[1]{0:T(128)} %bitcast._, bf16[128,9216]{1,0:T(8,128)(2,1)S(1)} %copy-done, bf16[128,9216]{1,0:T(8,128)(2,1)S(1)} %copy-done, bf16[128,9216]{1,0:T(8,128)(2,1)S(1)} %copy-done), custom_call_target="tpu_custom_call" | custom-call | tf_op jit(solution)/shard_map/pack_heads/pallas_call | solution.py:43
  11.1 4.0 %all-to-all-start = ((bf16[8,64,1152]{2,1,0:T(8,128)(2,1)}), bf16[8,64,1152]{2,1,0:T(8,128)(2,1)S(1)}, u32[]{:S(2)}, u32[]{:S(2)}) async-start(bf16[8,64,1152]{2,1,0:T(8,128)(2,1)} %pack_heads.2.refs_1_), calls=%async_computation | async-start | bytes 2359296 | tf_op jit(solution)/shard_map/all_to_all | solution.py:370
  15.0 4.8 %collective-permute-done.1.refs_0_ = bf16[2,256,768]{2,1,0:T(8,128)(2,1)S(1)} collective-permute-done((bf16[2,256,768]{2,1,0:T(8,128)(2,1)}, bf16[2,256,768]{2,1,0:T(8,128)(2,1)S(1)}, u32[]{:S(2)}, u32[]{:S(2)}) %collective-permute-start.1) | collective-permute-done | bytes 786464 | tf_op jit(solution)/shard_map/ppermute | solution.py:401
  20.8 2.2 %collective-permute-start.4 = (bf16[2,256,768]{2,1,0:T(8,128)(2,1)}, bf16[2,256,768]{2,1,0:T(8,128)(2,1)S(1)}, u32[]{:S(2)}, u32[]{:S(2)}) collective-permute-start(bf16[2,256,768]{2,1,0:T(8,128)(2,1)} %after.9.refs_5_.refs_3_), channel_id=1, source_target_pairs={{8,16},{16,24},{12,4},{20,12},{9,17},{17,25},{13,5},{21,13},{10,18... | collective-permute-start | bytes 2359304 | tf_op jit(solution)/shard_map/ppermute | solution.py:401
  23.9 2.1 %collective-permute-start.3 = (bf16[2,256,768]{2,1,0:T(8,128)(2,1)}, bf16[2,256,768]{2,1,0:T(8,128)(2,1)S(1)}, u32[]{:S(2)}, u32[]{:S(2)}) collective-permute-start(bf16[2,256,768]{2,1,0:T(8,128)(2,1)} %after.8.refs_4_.refs_2_), channel_id=1, source_target_pairs={{8,16},{16,24},{12,4},{20,12},{9,17},{17,25},{13,5},{21,13},{10,18... | collective-permute-start | bytes 2359304 | tf_op jit(solution)/shard_map/ppermute | solution.py:401
  26.0 2.1 %collective-permute-start.2 = (bf16[2,256,768]{2,1,0:T(8,128)(2,1)}, bf16[2,256,768]{2,1,0:T(8,128)(2,1)}, u32[]{:S(2)}, u32[]{:S(2)}) collective-permute-start(bf16[2,256,768]{2,1,0:T(8,128)(2,1)} %refs_0_.7), channel_id=1, source_target_pairs={{0,4},{4,0},{8,12},{12,8},{16,20},{20,16},{24,28},{28,24},{1,5},{5... | collective-permute-start | bytes 2359304 | tf_op jit(solution)/shard_map/ppermute | solution.py:375
  28.2 2.9 %all-to-all-done.refs_3_.txt = bf16[8,64,1152]{2,1,0:T(8,128)(2,1)S(1)} async-done(((bf16[8,64,1152]{2,1,0:T(8,128)(2,1)}), bf16[8,64,1152]{2,1,0:T(8,128)(2,1)S(1)}, u32[]{:S(2)}, u32[]{:S(2)}) %all-to-all-start) | async-done | bytes 1179680 | tf_op jit(solution)/shard_map/all_to_all | solution.py:370
  31.1 1.1 copy-done.4
  32.3 1.3 %copy-done.10 = bf16[64,9216]{1,0:T(8,128)(2,1)S(1)} copy-done((bf16[64,9216]{1,0:T(8,128)(2,1)S(1)}, bf16[64,9216]{1,0:T(8,128)(2,1)}, u32[]{:S(2)}) %copy-start.10) | copy-done | bytes 1179672
  33.5 2.9 %pack_heads.3.refs_1_ = bf16[8,64,1152]{2,1,0:T(8,128)(2,1)} custom-call(s32[1]{0:T(128)} %constant.35.clone.1._, bf16[64,9216]{1,0:T(8,128)(2,1)S(1)} %copy-done.10, bf16[64,9216]{1,0:T(8,128)(2,1)S(1)} %copy-done.10, bf16[64,9216]{1,0:T(8,128)(2,1)S(1)} %copy-done.10, bf16[8,64,1152]{2,1,0:T(8,128)(2,1)S(1)} %all-to-all-done.refs_3_.txt, ...), custom_call_target="tpu_custom_call" | custom-call | tf_op jit(solution)/shard_map/pack_heads/pallas_call | solution.py:43
  37.3 1.5 %collective-permute-start.11 = (bf16[2,256,768]{2,1,0:T(8,128)(2,1)}, bf16[2,256,768]{2,1,0:T(8,128)(2,1)}, u32[]{:S(2)}, u32[]{:S(2)}) collective-permute-start(bf16[2,256,768]{2,1,0:T(8,128)(2,1)} %after.11.refs_5_.refs_7_), channel_id=1, source_target_pairs={{16,24},{12,4},{17,25},{13,5},{18,26},{14,6},{19,27},{15,7}} | collective-permute-start | bytes 2359304 | tf_op jit(solution)/shard_map/ppermute | solution.py:401
  38.9 1.8 %collective-permute-done.3.refs_0_ = bf16[2,256,768]{2,1,0:T(8,128)(2,1)S(1)} collective-permute-done((bf16[2,256,768]{2,1,0:T(8,128)(2,1)}, bf16[2,256,768]{2,1,0:T(8,128)(2,1)S(1)}, u32[]{:S(2)}, u32[]{:S(2)}) %collective-permute-start.3) | collective-permute-done | bytes 786464 | tf_op jit(solution)/shard_map/ppermute | solution.py:401
  41.5 1.7 %collective-permute-start.9 = (bf16[2,256,768]{2,1,0:T(8,128)(2,1)}, bf16[2,256,768]{2,1,0:T(8,128)(2,1)}, u32[]{:S(2)}, u32[]{:S(2)}) collective-permute-start(bf16[2,256,768]{2,1,0:T(8,128)(2,1)} %after.10.refs_4_.refs_6_), channel_id=1, source_target_pairs={{16,24},{12,4},{17,25},{13,5},{18,26},{14,6},{19,27},{15,7}} | collective-permute-start | bytes 2359304 | tf_op jit(solution)/shard_map/ppermute | solution.py:401
  43.2 10.1 %all-to-all-start.1 = ((bf16[8,64,1152]{2,1,0:T(8,128)(2,1)}), bf16[8,64,1152]{2,1,0:T(8,128)(2,1)S(1)}, u32[]{:S(2)}, u32[]{:S(2)}) async-start(bf16[8,64,1152]{2,1,0:T(8,128)(2,1)} %pack_heads.3.refs_1_), calls=%async_computation.1 | async-start | bytes 2359296 | tf_op jit(solution)/shard_map/all_to_all | solution.py:370
  54.4 5.9 %collective-permute-start.10 = (bf16[2,256,768]{2,1,0:T(8,128)(2,1)}, bf16[2,256,768]{2,1,0:T(8,128)(2,1)}, u32[]{:S(2)}, u32[]{:S(2)}) collective-permute-start(bf16[2,256,768]{2,1,0:T(8,128)(2,1)} %collective-permute-done.9.refs_10_), channel_id=1, source_target_pairs={{0,4},{4,0},{8,12},{12,8},{16,20},{20,16},{24,28},{28,24},{1,5},{5... | collective-permute-start | bytes 2359304 | tf_op jit(solution)/shard_map/ppermute | solution.py:375
  61.5 1.1 copy-done.12
  62.7 1.1 copy-done.15
  63.8 1.1 copy-done.19
  64.9 7.6 %attend_text.1.refs_0_ = bf16[8,64,384]{2,1,0:T(8,128)(2,1)S(1)} custom-call(s32[5]{0:T(128)S(1)} %stack.39.info, bf16[8,64,1152]{2,1,0:T(8,128)(2,1)S(1)} %all-to-all-done.refs_3_.txt, bf16[2,256,768]{2,1,0:T(8,128)(2,1)S(1)} %copy-done.19, bf16[2,256,768]{2,1,0:T(8,128)(2,1)} %collective-permute-done.2.refs_1_, bf16[2,256,768]{2,1,0:T(8,128)(2,1)S(1)} %copy-done.5, ...), custom_call_target="tpu_custom_call" | custom-call | flops 2013265920 | bytes 3932160 | tf_op jit(solution)/shard_map/attend_text/pallas_call | solution.py:261
  74.4 4.0 %all-to-all-start.3 = ((bf16[8,64,384]{2,1,0:T(8,128)(2,1)}), bf16[8,64,384]{2,1,0:T(8,128)(2,1)}, u32[]{:S(2)}, u32[]{:S(2)}) async-start(bf16[8,64,384]{2,1,0:T(8,128)(2,1)} %after.12.refs_1_), calls=%async_computation.3 | async-start | bytes 786432 | tf_op jit(solution)/shard_map/all_to_all | solution.py:370
  79.8 1.3 %copy-done.2 = bf16[8,64,1152]{2,1,0:T(8,128)(2,1)S(1)} copy-done((bf16[8,64,1152]{2,1,0:T(8,128)(2,1)S(1)}, bf16[8,64,1152]{2,1,0:T(8,128)(2,1)}, u32[]{:S(2)}) %copy-start.2) | copy-done | bytes 1179672
  81.1 1.1 copy-done.16
  82.2 1.1 copy-done.20
  83.3 8.9 %attend_image.1.refs_1_ = bf16[8,64,384]{2,1,0:T(8,128)(2,1)S(1)} custom-call(s32[5]{0:T(128)S(1)} %stack.39.info, bf16[8,64,1152]{2,1,0:T(8,128)(2,1)S(1)} %copy-done.2, bf16[8,64,1152]{2,1,0:T(8,128)(2,1)S(1)} %all-to-all-done.refs_3_.txt, bf16[2,256,768]{2,1,0:T(8,128)(2,1)S(1)} %copy-done.20, bf16[2,256,768]{2,1,0:T(8,128)(2,1)} %collective-permute-done.2.refs_1_, ...), custom_call_target="tpu_custom_call" | custom-call | flops 2013265920 | bytes 3932160 | tf_op jit(solution)/shard_map/attend_image/pallas_call | solution.py:261
  93.0 4.1 %all-to-all-start.2 = ((bf16[8,64,384]{2,1,0:T(8,128)(2,1)}), bf16[8,64,384]{2,1,0:T(8,128)(2,1)S(1)}, u32[]{:S(2)}, u32[]{:S(2)}) async-start(bf16[8,64,384]{2,1,0:T(8,128)(2,1)} %copy-done.18), calls=%async_computation.2 | async-start | bytes 786432 | tf_op jit(solution)/shard_map/all_to_all | solution.py:370
  98.2 1.3 %collective-permute-start.13 = (bf16[64,3072]{1,0:T(8,128)(2,1)S(1)}, bf16[64,3072]{1,0:T(8,128)(2,1)S(1)}, u32[]{:S(2)}, u32[]{:S(2)}) collective-permute-start(bf16[64,3072]{1,0:T(8,128)(2,1)S(1)} %unpack_text.1), channel_id=1, source_target_pairs={{8,0},{12,4},{16,24},{20,28},{9,1},{13,5},{17,25},{21,29},{10,2},{... | collective-permute-start | bytes 1179656 | tf_op jit(solution)/shard_map/ppermute | solution.py:443
  99.5 5.2 %all-to-all-done.2.x_ref = bf16[8,64,384]{2,1,0:T(8,128)(2,1)S(1)} async-done(((bf16[8,64,384]{2,1,0:T(8,128)(2,1)}), bf16[8,64,384]{2,1,0:T(8,128)(2,1)S(1)}, u32[]{:S(2)}, u32[]{:S(2)}) %all-to-all-start.2) | async-done | bytes 393248 | tf_op jit(solution)/shard_map/all_to_all | solution.py:370
  104.8 7.8 %project.1.refs_1_ = bf16[64,3072]{1,0:T(8,128)(2,1)} custom-call(bf16[8,64,384]{2,1,0:T(8,128)(2,1)S(1)} %all-to-all-done.2.x_ref, bf16[8,384,3072]{2,1,0:T(8,128)(2,1)} %bitcast.8, bf16[64,3072]{1,0:T(8,128)(2,1)S(1)} %copy-done.21, f32[1,3072]{1,0:T(1,128)S(1)} %bitcast.7), custom_call_target="tpu_custom_call" | custom-call | flops 1207959552 | bytes 18874368 | tf_op jit(solution)/shard_map/project/pallas_call | solution.py:299
  113.7 1.5 %collective-permute-done.14 = bf16[64,3072]{1,0:T(8,128)(2,1)S(1)} collective-permute-done((bf16[64,3072]{1,0:T(8,128)(2,1)S(1)}, bf16[64,3072]{1,0:T(8,128)(2,1)S(1)}, u32[]{:S(2)}, u32[]{:S(2)}) %collective-permute-start.14) | collective-permute-done | bytes 393248 | tf_op jit(solution)/shard_map/ppermute | solution.py:375
  (72 shorter events, 12.9 us)
Async XLA Ops:
  0.6 19.2 %collective-permute-start.1 = (bf16[2,256,768]{2,1,0:T(8,128)(2,1)}, bf16[2,256,768]{2,1,0:T(8,128)(2,1)S(1)}, u32[]{:S(2)}, u32[]{:S(2)}) collective-permute-start(bf16[2,256,768]{2,1,0:T(8,128)(2,1)} %refs_0_.7), channel_id=1, source_target_pairs={{4,8},{12,16},{20,24},{8,4},{16,12},{24,20},{5,9},{13,17},{21,25},... | collective-permute-start | bytes 2359304 | tf_op jit(solution)/shard_map/ppermute | solution.py:401
  4.4 18.6 %collective-permute-start = (bf16[2,256,768]{2,1,0:T(8,128)(2,1)}, bf16[2,256,768]{2,1,0:T(8,128)(2,1)S(1)}, u32[]{:S(2)}, u32[]{:S(2)}) collective-permute-start(bf16[2,256,768]{2,1,0:T(8,128)(2,1)} %refs_0_.7), channel_id=1, source_target_pairs={{0,8},{8,16},{16,24},{12,4},{20,12},{28,20},{1,9},{9,17},{17,25},{... | collective-permute-start | bytes 2359304 | tf_op jit(solution)/shard_map/ppermute | solution.py:401
  6.5 1.7 %copy-start = (bf16[128,9216]{1,0:T(8,128)(2,1)S(1)}, bf16[128,9216]{1,0:T(8,128)(2,1)}, u32[]{:S(2)}) copy-start(bf16[128,9216]{1,0:T(8,128)(2,1)} %refs_2_.2) | copy-start | bytes 7077892
  11.1 20.0 %all-to-all-start = ((bf16[8,64,1152]{2,1,0:T(8,128)(2,1)}), bf16[8,64,1152]{2,1,0:T(8,128)(2,1)S(1)}, u32[]{:S(2)}, u32[]{:S(2)}) async-start(bf16[8,64,1152]{2,1,0:T(8,128)(2,1)} %pack_heads.2.refs_1_), calls=%async_computation | async-start | bytes 2359296 | tf_op jit(solution)/shard_map/all_to_all | solution.py:370
  20.8 10.3 %copy-start.7 = (bf16[2,256,768]{2,1,0:T(8,128)(2,1)S(1)}, bf16[2,256,768]{2,1,0:T(8,128)(2,1)}, u32[]{:S(2)}) copy-start(bf16[2,256,768]{2,1,0:T(8,128)(2,1)} %after.9.refs_5_.refs_3_) | copy-start | bytes 2359300
  20.8 15.7 %collective-permute-start.4 = (bf16[2,256,768]{2,1,0:T(8,128)(2,1)}, bf16[2,256,768]{2,1,0:T(8,128)(2,1)S(1)}, u32[]{:S(2)}, u32[]{:S(2)}) collective-permute-start(bf16[2,256,768]{2,1,0:T(8,128)(2,1)} %after.9.refs_5_.refs_3_), channel_id=1, source_target_pairs={{8,16},{16,24},{12,4},{20,12},{9,17},{17,25},{13,5},{21,13},{10,18... | collective-permute-start | bytes 2359304 | tf_op jit(solution)/shard_map/ppermute | solution.py:401
  23.9 16.7 %collective-permute-start.3 = (bf16[2,256,768]{2,1,0:T(8,128)(2,1)}, bf16[2,256,768]{2,1,0:T(8,128)(2,1)S(1)}, u32[]{:S(2)}, u32[]{:S(2)}) collective-permute-start(bf16[2,256,768]{2,1,0:T(8,128)(2,1)} %after.8.refs_4_.refs_2_), channel_id=1, source_target_pairs={{8,16},{16,24},{12,4},{20,12},{9,17},{17,25},{13,5},{21,13},{10,18... | collective-permute-start | bytes 2359304 | tf_op jit(solution)/shard_map/ppermute | solution.py:401
  26.0 27.4 %collective-permute-start.2 = (bf16[2,256,768]{2,1,0:T(8,128)(2,1)}, bf16[2,256,768]{2,1,0:T(8,128)(2,1)}, u32[]{:S(2)}, u32[]{:S(2)}) collective-permute-start(bf16[2,256,768]{2,1,0:T(8,128)(2,1)} %refs_0_.7), channel_id=1, source_target_pairs={{0,4},{4,0},{8,12},{12,8},{16,20},{20,16},{24,28},{28,24},{1,5},{5... | collective-permute-start | bytes 2359304 | tf_op jit(solution)/shard_map/ppermute | solution.py:375
  28.1 25.8 %collective-permute-start.7 = (bf16[2,256,768]{2,1,0:T(8,128)(2,1)}, bf16[2,256,768]{2,1,0:T(8,128)(2,1)}, u32[]{:S(2)}, u32[]{:S(2)}) collective-permute-start(bf16[2,256,768]{2,1,0:T(8,128)(2,1)} %after.8.refs_4_.refs_2_), channel_id=1, source_target_pairs={{0,4},{4,0},{8,12},{12,8},{16,20},{20,16},{24,28},{28,24},{1,5},{5... | collective-permute-start | bytes 2359304 | tf_op jit(solution)/shard_map/ppermute | solution.py:375
  31.1 1.1 copy-start.4
  32.3 1.3 %copy-start.10 = (bf16[64,9216]{1,0:T(8,128)(2,1)S(1)}, bf16[64,9216]{1,0:T(8,128)(2,1)}, u32[]{:S(2)}) copy-start(bf16[64,9216]{1,0:T(8,128)(2,1)} %refs_2_.3) | copy-start | bytes 3538948
  37.3 16.6 %collective-permute-start.11 = (bf16[2,256,768]{2,1,0:T(8,128)(2,1)}, bf16[2,256,768]{2,1,0:T(8,128)(2,1)}, u32[]{:S(2)}, u32[]{:S(2)}) collective-permute-start(bf16[2,256,768]{2,1,0:T(8,128)(2,1)} %after.11.refs_5_.refs_7_), channel_id=1, source_target_pairs={{16,24},{12,4},{17,25},{13,5},{18,26},{14,6},{19,27},{15,7}} | collective-permute-start | bytes 2359304 | tf_op jit(solution)/shard_map/ppermute | solution.py:401
  41.5 18.9 %copy-start.5 = (bf16[2,256,768]{2,1,0:T(8,128)(2,1)S(1)}, bf16[2,256,768]{2,1,0:T(8,128)(2,1)}, u32[]{:S(2)}) copy-start(bf16[2,256,768]{2,1,0:T(8,128)(2,1)} %after.8.refs_4_.refs_2_) | copy-start | bytes 2359300
  41.5 12.9 %collective-permute-start.9 = (bf16[2,256,768]{2,1,0:T(8,128)(2,1)}, bf16[2,256,768]{2,1,0:T(8,128)(2,1)}, u32[]{:S(2)}, u32[]{:S(2)}) collective-permute-start(bf16[2,256,768]{2,1,0:T(8,128)(2,1)} %after.10.refs_4_.refs_6_), channel_id=1, source_target_pairs={{16,24},{12,4},{17,25},{13,5},{18,26},{14,6},{19,27},{15,7}} | collective-permute-start | bytes 2359304 | tf_op jit(solution)/shard_map/ppermute | solution.py:401
  43.2 30.1 %all-to-all-start.1 = ((bf16[8,64,1152]{2,1,0:T(8,128)(2,1)}), bf16[8,64,1152]{2,1,0:T(8,128)(2,1)S(1)}, u32[]{:S(2)}, u32[]{:S(2)}) async-start(bf16[8,64,1152]{2,1,0:T(8,128)(2,1)} %pack_heads.3.refs_1_), calls=%async_computation.1 | async-start | bytes 2359296 | tf_op jit(solution)/shard_map/all_to_all | solution.py:370
  53.3 7.0 %collective-permute-start.8 = (bf16[2,256,768]{2,1,0:T(8,128)(2,1)}, bf16[2,256,768]{2,1,0:T(8,128)(2,1)}, u32[]{:S(2)}, u32[]{:S(2)}) collective-permute-start(bf16[2,256,768]{2,1,0:T(8,128)(2,1)} %after.9.refs_5_.refs_3_), channel_id=1, source_target_pairs={{0,4},{4,0},{8,12},{12,8},{16,20},{20,16},{24,28},{28,24},{1,5},{5... | collective-permute-start | bytes 2359304 | tf_op jit(solution)/shard_map/ppermute | solution.py:375
  53.4 7.0 %collective-permute-start.6 = (bf16[2,256,768]{2,1,0:T(8,128)(2,1)}, bf16[2,256,768]{2,1,0:T(8,128)(2,1)}, u32[]{:S(2)}, u32[]{:S(2)}) collective-permute-start(bf16[2,256,768]{2,1,0:T(8,128)(2,1)} %after.11.refs_5_.refs_7_), channel_id=1, source_target_pairs={{0,4},{4,0},{8,12},{12,8},{16,20},{20,16},{24,28},{28,24},{1,5},{5... | collective-permute-start | bytes 2359304 | tf_op jit(solution)/shard_map/ppermute | solution.py:375
  53.9 6.5 %collective-permute-start.5 = (bf16[2,256,768]{2,1,0:T(8,128)(2,1)}, bf16[2,256,768]{2,1,0:T(8,128)(2,1)}, u32[]{:S(2)}, u32[]{:S(2)}) collective-permute-start(bf16[2,256,768]{2,1,0:T(8,128)(2,1)} %after.10.refs_4_.refs_6_), channel_id=1, source_target_pairs={{0,4},{4,0},{8,12},{12,8},{16,20},{20,16},{24,28},{28,24},{1,5},{5... | collective-permute-start | bytes 2359304 | tf_op jit(solution)/shard_map/ppermute | solution.py:375
  53.9 24.5 %collective-permute-start.12 = (bf16[2,256,768]{2,1,0:T(8,128)(2,1)}, bf16[2,256,768]{2,1,0:T(8,128)(2,1)}, u32[]{:S(2)}, u32[]{:S(2)}) collective-permute-start(bf16[2,256,768]{2,1,0:T(8,128)(2,1)} %collective-permute-done.11.refs_11_), channel_id=1, source_target_pairs={{0,4},{4,0},{8,12},{12,8},{16,20},{20,16},{24,28},{28,24},{1,5},{5... | collective-permute-start | bytes 2359304 | tf_op jit(solution)/shard_map/ppermute | solution.py:375
  54.4 24.1 %collective-permute-start.10 = (bf16[2,256,768]{2,1,0:T(8,128)(2,1)}, bf16[2,256,768]{2,1,0:T(8,128)(2,1)}, u32[]{:S(2)}, u32[]{:S(2)}) collective-permute-start(bf16[2,256,768]{2,1,0:T(8,128)(2,1)} %collective-permute-done.9.refs_10_), channel_id=1, source_target_pairs={{0,4},{4,0},{8,12},{12,8},{16,20},{20,16},{24,28},{28,24},{1,5},{5... | collective-permute-start | bytes 2359304 | tf_op jit(solution)/shard_map/ppermute | solution.py:375
  60.4 1.1 copy-start.8
  61.5 1.1 copy-start.12
  62.7 1.1 copy-start.15
  74.4 18.6 %all-to-all-start.3 = ((bf16[8,64,384]{2,1,0:T(8,128)(2,1)}), bf16[8,64,384]{2,1,0:T(8,128)(2,1)}, u32[]{:S(2)}, u32[]{:S(2)}) async-start(bf16[8,64,384]{2,1,0:T(8,128)(2,1)} %after.12.refs_1_), calls=%async_computation.3 | async-start | bytes 786432 | tf_op jit(solution)/shard_map/all_to_all | solution.py:370
  78.4 1.1 copy-start.9
  78.4 1.4 %copy-start.13 = (bf16[2,256,768]{2,1,0:T(8,128)(2,1)S(1)}, bf16[2,256,768]{2,1,0:T(8,128)(2,1)}, u32[]{:S(2)}) copy-start(bf16[2,256,768]{2,1,0:T(8,128)(2,1)} %after.11.refs_5_.refs_7_) | copy-start | bytes 2359300
  79.8 1.3 %copy-start.2 = (bf16[8,64,1152]{2,1,0:T(8,128)(2,1)S(1)}, bf16[8,64,1152]{2,1,0:T(8,128)(2,1)}, u32[]{:S(2)}) copy-start(bf16[8,64,1152]{2,1,0:T(8,128)(2,1)} %after.13.img) | copy-start | bytes 3538948
  93.0 11.8 %all-to-all-start.2 = ((bf16[8,64,384]{2,1,0:T(8,128)(2,1)}), bf16[8,64,384]{2,1,0:T(8,128)(2,1)S(1)}, u32[]{:S(2)}, u32[]{:S(2)}) async-start(bf16[8,64,384]{2,1,0:T(8,128)(2,1)} %copy-done.18), calls=%async_computation.2 | async-start | bytes 786432 | tf_op jit(solution)/shard_map/all_to_all | solution.py:370
  97.1 7.7 %copy-start.21 = (bf16[64,3072]{1,0:T(8,128)(2,1)S(1)}, bf16[64,3072]{1,0:T(8,128)(2,1)}, u32[]{:S(2)}) copy-start(bf16[64,3072]{1,0:T(8,128)(2,1)} %residual.1) | copy-start | bytes 1179652
  97.1 7.7 %copy-start.22 = (f32[3072]{0:T(1024)S(1)}, f32[3072]{0:T(1024)}, u32[]{:S(2)}) copy-start(f32[3072]{0:T(1024)} %param.10) | copy-start | bytes 36868
  98.2 14.4 %collective-permute-start.13 = (bf16[64,3072]{1,0:T(8,128)(2,1)S(1)}, bf16[64,3072]{1,0:T(8,128)(2,1)S(1)}, u32[]{:S(2)}, u32[]{:S(2)}) collective-permute-start(bf16[64,3072]{1,0:T(8,128)(2,1)S(1)} %unpack_text.1), channel_id=1, source_target_pairs={{8,0},{12,4},{16,24},{20,28},{9,1},{13,5},{17,25},{21,29},{10,2},{... | collective-permute-start | bytes 1179656 | tf_op jit(solution)/shard_map/ppermute | solution.py:443
  113.4 1.8 %collective-permute-start.14 = (bf16[64,3072]{1,0:T(8,128)(2,1)S(1)}, bf16[64,3072]{1,0:T(8,128)(2,1)S(1)}, u32[]{:S(2)}, u32[]{:S(2)}) collective-permute-start(bf16[64,3072]{1,0:T(8,128)(2,1)S(1)} %broadcast_select_fusion), channel_id=1, source_target_pairs={{0,4},{4,0},{8,12},{12,8},{16,20},{20,16},{24,28},{28,24},{1,5},{5... | collective-permute-start | bytes 1179656 | tf_op jit(solution)/shard_map/ppermute | solution.py:375
  (11 other events, 10.2 us)

commit v11 on v10

--- a/solution.py
+++ b/solution.py
@@ -13,6 +13,7 @@
 VMEM_LIMIT = 12 * 1024 * 1024
 WIDE_LIMIT = 48 * 1024 * 1024
 TILE = 256
+TEXT_TILE = 128
 FIRST_KEYS = 256
 LARGE = 2.0**60
 
@@ -75,8 +76,8 @@
     return dot(weights, values, (1, 0))
 
 
-def tiles_of(rows):
-    tile = min(TILE, rows)
+def tiles_of(rows, most):
+    tile = min(most, rows)
     return [slice(first, min(first + tile, rows)) for first in range(0, rows, tile)]
 
 
@@ -91,30 +92,46 @@
             flag[0] = jnp.where(jnp.max(total[:, :, HD:]) > LARGE, 1, 0).astype(jnp.int32)
 
 
-def copy_columns(target, at, block, core, width):
-    columns = pl.ds(pl.multiple_of(core * width, width), width)
-    target[:, at : at + block.shape[1], :] = block[:, :, columns]
-
-
-def settle(info, refs, entries, chosen):
-    width = chosen.shape[3]
+class Fetch:
+    def __init__(self, info, width, sems):
+        self.columns = pl.ds(pl.multiple_of(info[0] * width, width), width)
+        self.info, self.sems, self.waits = info, sems, []
+
+    def start(self, candidates, flags, target, at):
+        rows = candidates[0].shape[1]
+        sem = self.sems.at[len(self.waits)]
+        copies = [
+            pltpu.make_async_copy(
+                block.at[:, :, self.columns], target.at[:, pl.ds(at, rows), :], sem
+            )
+            for block in candidates
+        ]
+        if len(copies) == 1:
+            copies[0].start()
+        else:
+            for copy, flag in zip(copies, flags):
+                pl.when(flag)(copy.start)
+        self.waits.append(copies[0])
+
+    def wait(self):
+        for copy in self.waits:
+            copy.wait()
+
+
+def settle(fetch, refs, entries, chosen):
     for index, candidates in enumerate(entries):
-        for place, count in enumerate(candidates):
-            blocks, refs = refs[:count], refs[count:]
-
-            def copy():
-                at = 0
-                for block in blocks:
-                    copy_columns(chosen.at[index], at, block, info[0], width)
-                    at += block.shape[1]
-
-            if len(candidates) == 1:
-                copy()
-            else:
-                pl.when(info[1 + index] == 1 - place)(copy)
-
-
-def accumulate(flag, total, aug, heads, queries_of, first_keys_of, own, chosen):
+        sides = []
+        for count in candidates:
+            sides.append(refs[:count])
+            refs = refs[count:]
+        first = fetch.info[1 + index]
+        at = 0
+        for blocks in zip(*sides):
+            fetch.start(blocks, [first == 1, first == 0], chosen.at[index], at)
+            at += blocks[0].shape[1]
+
+
+def accumulate(flag, total, aug, heads, queries_of, first_keys_of, own, chosen, tile_rows):
     def columns(head):
         return slice(head * HD, (head + 1) * HD)
 
@@ -128,7 +145,7 @@
         for head in range(heads):
             queries = queries_of(head)
             for span, some in own:
-                for tile in tiles_of(span.stop - span.start):
+                for tile in tiles_of(span.stop - span.start, tile_rows):
                     tile = slice(span.start + tile.start, span.start + tile.stop)
                     yield head, tile, queries[tile, :], some
 
@@ -173,18 +190,20 @@
 
 
 def text_body(pair, entries, info, txt, *refs, wanted):
-    stale, came = refs[:pair], refs[pair:-6]
-    out, chosen, beside, aug, total, flag = refs[-6:]
+    stale, came = refs[:pair], refs[pair:-7]
+    out, chosen, beside, aug, total, flag, sems = refs[-7:]
     width = chosen.shape[3]
     heads = width // HD
 
     @pl.when(info[wanted] == 1)
     def _():
-        settle(info, came, entries, chosen)
+        fetch = Fetch(info, width, sems)
         at = 0
         for block in stale:
-            copy_columns(beside.at[0], at, block, info[0], width)
+            fetch.start([block], [], beside.at[0], at)
             at += block.shape[1]
+        settle(fetch, came, entries, chosen)
+        fetch.wait()
 
         def own(head):
             columns = slice(head * HD, (head + 1) * HD)
@@ -197,31 +216,31 @@
             flag, total, aug, heads,
             lambda head: part_of(txt, 0, head, width),
             lambda head: part_of(txt, 1, head, width)[: min(FIRST_KEYS, total.shape[1]), :],
-            [(slice(0, total.shape[1]), own)], chosen,
+            [(slice(0, total.shape[1]), own)], chosen, TEXT_TILE,
         )
         finish(out, total)
 
 
 def image_body(pair, entries, info, img, txt, *refs):
-    stale, came = refs[:pair], refs[pair:-6]
-    out, chosen, beside, aug, total, flag = refs[-6:]
+    stale, came = refs[:pair], refs[pair:-7]
+    out, chosen, beside, aug, total, flag, sems = refs[-7:]
     width = chosen.shape[3]
     heads = width // HD
     rows = total.shape[1]
     group_rows, sources = rows // pair, img.shape[0] // pair
-    settle(info, came, entries, chosen)
+    fetch = Fetch(info, width, sems)
+    if pair == 2:
+        for group in range(pair):
+            flags = [info[0] != group, info[0] == group]
+            fetch.start(stale, flags, beside.at[group], group_rows)
+    settle(fetch, came, entries, chosen)
     for group in range(pair):
         for part in range(2):
             fresh = img[
                 group * sources : (group + 1) * sources, :, (1 + part) * width : (2 + part) * width
             ]
             beside[group, part, :group_rows, :] = fresh.reshape(group_rows, width)
-        if pair == 2:
-            for place, block in enumerate(stale):
-
-                @pl.when((info[0] == group) == (place == 1))
-                def _():
-                    copy_columns(beside.at[group], group_rows, block, info[0], width)
+    fetch.wait()
 
     def own(group):
         def some(head):
@@ -238,7 +257,7 @@
         flag, total, aug, heads,
         lambda head: part_of(img, 0, head, width),
         lambda head: part_of(txt, 1, head, width)[: min(FIRST_KEYS, text_keys), :],
-        [own(group) for group in range(pair)], chosen,
+        [own(group) for group in range(pair)], chosen, TILE,
     )
     finish(out, total)
 
@@ -261,10 +280,15 @@
     return pl.pallas_call(
         functools.partial(body, len(stale), counts),
         in_specs=[pl.BlockSpec(memory_space=pltpu.SMEM)]
-        + [vmem] * (len(fresh) + len(stale) + len(came)),
+        + [vmem] * len(fresh)
+        + [pl.BlockSpec(memory_space=pl.ANY)] * (len(stale) + len(came)),
         out_specs=vmem,
         out_shape=jax.ShapeDtypeStruct(first.shape[:2] + (width,), first.dtype),
-        scratch_shapes=[pltpu.VMEM(*one) for one in scratch] + [pltpu.SMEM((1,), jnp.int32)],
+        scratch_shapes=[pltpu.VMEM(*one) for one in scratch]
+        + [
+            pltpu.SMEM((1,), jnp.int32),
+            pltpu.SemaphoreType.DMA((len(stale) * (1 + len(entries)),)),
+        ],
         compiler_params=pltpu.CompilerParams(vmem_limit_bytes=VMEM_LIMIT + needed),
         cost_estimate=pl.CostEstimate(
             flops=4 * rows * keys * (2 + len(entries)) * width,
@@ -314,18 +338,18 @@
     )(x, weight.reshape(destinations, width, model), residual, gate.reshape(1, model))
 
 
-def after_body(*refs):
-    del refs
+def after_body(x, other, out):
+    del other
+    out[...] = x[...]
 
 
 def after(x, other):
-    anywhere = pl.BlockSpec(memory_space=pl.ANY)
+    held = pl.BlockSpec(memory_space=pltpu.VMEM)
     return pl.pallas_call(
         after_body,
-        in_specs=[anywhere, anywhere],
-        out_specs=anywhere,
+        in_specs=[held, pl.BlockSpec(memory_space=pl.ANY)],
+        out_specs=held,
         out_shape=jax.ShapeDtypeStruct(x.shape, x.dtype),
-        input_output_aliases={0: 0},
         name="after",
     )(x, other)
 

time: 117 us -> 123 us (1.051)
  Pallas kernels: 31.2 us -> 48.8 us
  local copies, waits for them, and re-layouts: 20.4 us -> 12.8 us
  waiting for transfers between devices: 16.3 us -> 13.6 us
  starting transfers between devices: 46.4 us -> 44.9 us
    pallas_call x8, Pallas kernels: 0.01 us -> 16.1 us  [after(): pl.pallas_call(after_body, in_specs=[held, pl.BlockSpec(memory_space=pl.A...]
    unnamed x48 -> x36, local copies, waits for them, and re-layouts: 20.3 us -> 12.7 us
    all_to_all x4, waiting for transfers between devices: 8.18 us -> 3.47 us  [exchange(): lax.all_to_all(x, ('patch', 'head'), split_axis=0, concat_axis=0, axis_in...]
    ppermute x8, starting transfers between devices: 9.4 us -> 6.6 us  [swap(): return lax.ppermute(x, 'patch', swap_pairs)]
    pallas_call x2, Pallas kernels: 16.5 us -> 19 us  [attend(): pl.pallas_call(functools.partial(body, len(stale), counts), in_specs=[pl....]
    ppermute x6, waiting for transfers between devices: 6.61 us -> 8.58 us  [per_device(): lax.ppermute(block, 'patch', way)]
  transfers between devices with their start and end apart: 19 -> 19, of which waited for: 5 -> 4; matrix products, arithmetic and copies ran while one was open for 0% -> 0% of each run, Pallas kernels for 27% -> 39%
where the time goes in v11:
time: 123 us; the launch traced here: 122 us
  Pallas kernels  48.8 us (40%)
  starting transfers between devices  44.9 us (37%)
  waiting for transfers between devices  13.6 us (11%)
  local copies, waits for them, and re-layouts  12.8 us (10%)
    all_to_all x4, starting transfers between devices, exchange(): lax.all_to_all(x, ('patch', 'head'), split_axis=0, concat_axis=0, axis_in...  22.6 us
    pallas_call x2, Pallas kernels, attend(): pl.pallas_call(functools.partial(body, len(stale), counts), in_specs=[pl....  19 us
    pallas_call x8, Pallas kernels, after(): pl.pallas_call(after_body, in_specs=[held, pl.BlockSpec(memory_space=pl.A...  16.1 us
    ppermute x6, starting transfers between devices, per_device(): lax.ppermute(block, 'patch', way)  14.4 us
    unnamed x36, local copies, waits for them, and re-layouts  12.7 us
    ppermute x6, waiting for transfers between devices, per_device(): lax.ppermute(block, 'patch', way)  8.58 us
    pallas_call x1, Pallas kernels, project(): pl.pallas_call(functools.partial(project_body, order), in_specs=[vmem, pl...  7.81 us
    ppermute x8, starting transfers between devices, swap(): return lax.ppermute(x, 'patch', swap_pairs)  6.6 us
  transfers between devices with their start and end apart: 19, of which 4 were waited for; matrix products, arithmetic and copies ran while one was open for 0% of the time, Pallas kernels for 39%

profile of v11, /device:TPU:17, one launch (start us, length us, event | category | flops | bytes accessed | tf_op | source)
XLA Modules:
  0.0 121.9 jit_solution(6452087460559038349)
XLA Ops:
  0.6 3.8 %collective-permute-start.1 = (bf16[2,256,768]{2,1,0:T(8,128)(2,1)}, bf16[2,256,768]{2,1,0:T(8,128)(2,1)S(1)}, u32[]{:S(2)}, u32[]{:S(2)}) collective-permute-start(bf16[2,256,768]{2,1,0:T(8,128)(2,1)} %refs_0_.7), channel_id=1, source_target_pairs={{4,8},{12,16},{20,24},{8,4},{16,12},{24,20},{5,9},{13,17},{21,25},... | collective-permute-start | bytes 2359304 | tf_op jit(solution)/shard_map/ppermute | solution.py:425
  4.4 2.1 %collective-permute-start = (bf16[2,256,768]{2,1,0:T(8,128)(2,1)}, bf16[2,256,768]{2,1,0:T(8,128)(2,1)}, u32[]{:S(2)}, u32[]{:S(2)}) collective-permute-start(bf16[2,256,768]{2,1,0:T(8,128)(2,1)} %refs_0_.7), channel_id=1, source_target_pairs={{0,8},{8,16},{16,24},{12,4},{20,12},{28,20},{1,9},{9,17},{17,25},{... | collective-permute-start | bytes 2359304 | tf_op jit(solution)/shard_map/ppermute | solution.py:425
  6.5 1.7 %copy-done = bf16[128,9216]{1,0:T(8,128)(2,1)S(1)} copy-done((bf16[128,9216]{1,0:T(8,128)(2,1)S(1)}, bf16[128,9216]{1,0:T(8,128)(2,1)}, u32[]{:S(2)}) %copy-start) | copy-done | bytes 2359320
  8.2 2.9 %pack_heads.2.other = bf16[8,64,1152]{2,1,0:T(8,128)(2,1)} custom-call(s32[1]{0:T(128)} %bitcast._, bf16[128,9216]{1,0:T(8,128)(2,1)S(1)} %copy-done, bf16[128,9216]{1,0:T(8,128)(2,1)S(1)} %copy-done, bf16[128,9216]{1,0:T(8,128)(2,1)S(1)} %copy-done), custom_call_target="tpu_custom_call" | custom-call | tf_op jit(solution)/shard_map/pack_heads/pallas_call | solution.py:44
  11.1 4.0 %all-to-all-start = ((bf16[8,64,1152]{2,1,0:T(8,128)(2,1)}), bf16[8,64,1152]{2,1,0:T(8,128)(2,1)S(1)}, u32[]{:S(2)}, u32[]{:S(2)}) async-start(bf16[8,64,1152]{2,1,0:T(8,128)(2,1)} %pack_heads.2.other), calls=%async_computation | async-start | bytes 2359296 | tf_op jit(solution)/shard_map/all_to_all | solution.py:394
  15.0 4.9 %collective-permute-done.1.x = bf16[2,256,768]{2,1,0:T(8,128)(2,1)S(1)} collective-permute-done((bf16[2,256,768]{2,1,0:T(8,128)(2,1)}, bf16[2,256,768]{2,1,0:T(8,128)(2,1)S(1)}, u32[]{:S(2)}, u32[]{:S(2)}) %collective-permute-start.1) | collective-permute-done | bytes 786464 | tf_op jit(solution)/shard_map/ppermute | solution.py:425
  20.8 2.1 %after.9.refs_5_.refs_3_ = bf16[2,256,768]{2,1,0:T(8,128)(2,1)} custom-call(bf16[2,256,768]{2,1,0:T(8,128)(2,1)} %copy-done.16, bf16[8,64,1152]{2,1,0:T(8,128)(2,1)} %pack_heads.2.other), custom_call_target="tpu_custom_call" | custom-call | tf_op jit(solution)/shard_map/after/pallas_call | solution.py:348
  22.9 3.1 %collective-permute-start.4 = (bf16[2,256,768]{2,1,0:T(8,128)(2,1)}, bf16[2,256,768]{2,1,0:T(8,128)(2,1)}, u32[]{:S(2)}, u32[]{:S(2)}) collective-permute-start(bf16[2,256,768]{2,1,0:T(8,128)(2,1)} %after.9.refs_5_.refs_3_), channel_id=1, source_target_pairs={{8,16},{16,24},{12,4},{20,12},{9,17},{17,25},{13,5},{21,13},{10,18... | collective-permute-start | bytes 2359304 | tf_op jit(solution)/shard_map/ppermute | solution.py:425
  26.0 2.1 %after.8.refs_4_.refs_2_ = bf16[2,256,768]{2,1,0:T(8,128)(2,1)} custom-call(bf16[2,256,768]{2,1,0:T(8,128)(2,1)} %collective-permute-done.x, bf16[8,64,1152]{2,1,0:T(8,128)(2,1)} %pack_heads.2.other), custom_call_target="tpu_custom_call" | custom-call | tf_op jit(solution)/shard_map/after/pallas_call | solution.py:348
  28.1 2.2 %collective-permute-start.3 = (bf16[2,256,768]{2,1,0:T(8,128)(2,1)}, bf16[2,256,768]{2,1,0:T(8,128)(2,1)}, u32[]{:S(2)}, u32[]{:S(2)}) collective-permute-start(bf16[2,256,768]{2,1,0:T(8,128)(2,1)} %after.8.refs_4_.refs_2_), channel_id=1, source_target_pairs={{8,16},{16,24},{12,4},{20,12},{9,17},{17,25},{13,5},{21,13},{10,18... | collective-permute-start | bytes 2359304 | tf_op jit(solution)/shard_map/ppermute | solution.py:425
  32.6 2.9 %pack_heads.3.other = bf16[8,64,1152]{2,1,0:T(8,128)(2,1)} custom-call(s32[1]{0:T(128)} %constant.35.clone.1._, bf16[64,9216]{1,0:T(8,128)(2,1)S(1)} %copy-done.4, bf16[64,9216]{1,0:T(8,128)(2,1)S(1)} %copy-done.4, bf16[64,9216]{1,0:T(8,128)(2,1)S(1)} %copy-done.4, bf16[8,64,1152]{2,1,0:T(8,128)(2,1)S(1)} %all-to-all-done.refs_3_.txt, ...), custom_call_target="tpu_custom_call" | custom-call | tf_op jit(solution)/shard_map/pack_heads/pallas_call | solution.py:44
  35.5 2.1 %after.11.refs_5_.refs_7_ = bf16[2,256,768]{2,1,0:T(8,128)(2,1)} custom-call(bf16[2,256,768]{2,1,0:T(8,128)(2,1)} %collective-permute-done.4.x, bf16[8,64,1152]{2,1,0:T(8,128)(2,1)} %pack_heads.3.other), custom_call_target="tpu_custom_call" | custom-call | tf_op jit(solution)/shard_map/after/pallas_call | solution.py:348
  37.6 1.5 %collective-permute-start.11 = (bf16[2,256,768]{2,1,0:T(8,128)(2,1)}, bf16[2,256,768]{2,1,0:T(8,128)(2,1)}, u32[]{:S(2)}, u32[]{:S(2)}) collective-permute-start(bf16[2,256,768]{2,1,0:T(8,128)(2,1)} %after.11.refs_5_.refs_7_), channel_id=1, source_target_pairs={{16,24},{12,4},{17,25},{13,5},{18,26},{14,6},{19,27},{15,7}} | collective-permute-start | bytes 2359304 | tf_op jit(solution)/shard_map/ppermute | solution.py:425
  39.1 3.7 %collective-permute-done.3.x = bf16[2,256,768]{2,1,0:T(8,128)(2,1)} collective-permute-done((bf16[2,256,768]{2,1,0:T(8,128)(2,1)}, bf16[2,256,768]{2,1,0:T(8,128)(2,1)}, u32[]{:S(2)}, u32[]{:S(2)}) %collective-permute-start.3) | collective-permute-done | bytes 786464 | tf_op jit(solution)/shard_map/ppermute | solution.py:425
  42.8 2.1 %after.10.refs_4_.refs_6_ = bf16[2,256,768]{2,1,0:T(8,128)(2,1)} custom-call(bf16[2,256,768]{2,1,0:T(8,128)(2,1)} %collective-permute-done.3.x, bf16[8,64,1152]{2,1,0:T(8,128)(2,1)} %pack_heads.3.other), custom_call_target="tpu_custom_call" | custom-call | tf_op jit(solution)/shard_map/after/pallas_call | solution.py:348
  44.9 1.7 %collective-permute-start.9 = (bf16[2,256,768]{2,1,0:T(8,128)(2,1)}, bf16[2,256,768]{2,1,0:T(8,128)(2,1)}, u32[]{:S(2)}, u32[]{:S(2)}) collective-permute-start(bf16[2,256,768]{2,1,0:T(8,128)(2,1)} %after.10.refs_4_.refs_6_), channel_id=1, source_target_pairs={{16,24},{12,4},{17,25},{13,5},{18,26},{14,6},{19,27},{15,7}} | collective-permute-start | bytes 2359304 | tf_op jit(solution)/shard_map/ppermute | solution.py:425
  46.6 10.6 %all-to-all-start.1 = ((bf16[8,64,1152]{2,1,0:T(8,128)(2,1)}), bf16[8,64,1152]{2,1,0:T(8,128)(2,1)}, u32[]{:S(2)}, u32[]{:S(2)}) async-start(bf16[8,64,1152]{2,1,0:T(8,128)(2,1)} %pack_heads.3.other), calls=%async_computation.1 | async-start | bytes 2359296 | tf_op jit(solution)/shard_map/all_to_all | solution.py:394
  58.2 4.1 %collective-permute-start.10 = (bf16[2,256,768]{2,1,0:T(8,128)(2,1)}, bf16[2,256,768]{2,1,0:T(8,128)(2,1)}, u32[]{:S(2)}, u32[]{:S(2)}) collective-permute-start(bf16[2,256,768]{2,1,0:T(8,128)(2,1)} %collective-permute-done.9.refs_10_), channel_id=1, source_target_pairs={{0,4},{4,0},{8,12},{12,8},{16,20},{20,16},{24,28},{28,24},{1,5},{5... | collective-permute-start | bytes 2359304 | tf_op jit(solution)/shard_map/ppermute | solution.py:399
  63.6 1.1 copy-done.10
  64.7 11.5 %attend_text.1.x = bf16[8,64,384]{2,1,0:T(8,128)(2,1)S(1)} custom-call(s32[5]{0:T(128)S(1)} %stack.39.info, bf16[8,64,1152]{2,1,0:T(8,128)(2,1)S(1)} %all-to-all-done.refs_3_.txt, bf16[2,256,768]{2,1,0:T(8,128)(2,1)S(1)} %copy-done.10, bf16[2,256,768]{2,1,0:T(8,128)(2,1)} %collective-permute-done.2.refs_1_, bf16[2,256,768]{2,1,0:T(8,128)(2,1)S(1)} %copy-done.3, ...), custom_call_target="tpu_custom_call" | custom-call | flops 2013265920 | bytes 3932160 | tf_op jit(solution)/shard_map/attend_text/pallas_call | solution.py:280
  77.0 1.8 %after.12.other = bf16[8,64,384]{2,1,0:T(8,128)(2,1)} custom-call(bf16[8,64,384]{2,1,0:T(8,128)(2,1)} %copy-done.12, bf16[8,64,1152]{2,1,0:T(8,128)(2,1)} %all-to-all-done.1.other.x), custom_call_target="tpu_custom_call" | custom-call | tf_op jit(solution)/shard_map/after/pallas_call | solution.py:348
  78.8 4.2 %all-to-all-start.3 = ((bf16[8,64,384]{2,1,0:T(8,128)(2,1)}), bf16[8,64,384]{2,1,0:T(8,128)(2,1)}, u32[]{:S(2)}, u32[]{:S(2)}) async-start(bf16[8,64,384]{2,1,0:T(8,128)(2,1)} %after.12.other), calls=%async_computation.3 | async-start | bytes 786432 | tf_op jit(solution)/shard_map/all_to_all | solution.py:394
  83.0 2.4 %after.13.img = bf16[8,64,1152]{2,1,0:T(8,128)(2,1)} custom-call(bf16[8,64,1152]{2,1,0:T(8,128)(2,1)} %all-to-all-done.1.other.x, bf16[8,64,384]{2,1,0:T(8,128)(2,1)} %after.12.other), custom_call_target="tpu_custom_call" | custom-call | tf_op jit(solution)/shard_map/after/pallas_call | solution.py:348
  86.6 1.3 %copy-done.8 = bf16[8,64,1152]{2,1,0:T(8,128)(2,1)S(1)} copy-done((bf16[8,64,1152]{2,1,0:T(8,128)(2,1)S(1)}, bf16[8,64,1152]{2,1,0:T(8,128)(2,1)}, u32[]{:S(2)}) %copy-start.8) | copy-done | bytes 1179672
  89.0 7.4 %attend_image.1.other = bf16[8,64,384]{2,1,0:T(8,128)(2,1)S(1)} custom-call(s32[5]{0:T(128)S(1)} %stack.39.info, bf16[8,64,1152]{2,1,0:T(8,128)(2,1)S(1)} %copy-done.8, bf16[8,64,1152]{2,1,0:T(8,128)(2,1)S(1)} %all-to-all-done.refs_3_.txt, bf16[2,256,768]{2,1,0:T(8,128)(2,1)S(1)} %copy-done.11, bf16[2,256,768]{2,1,0:T(8,128)(2,1)} %collective-permute-done.2.refs_1_, ...), custom_call_target="tpu_custom_call" | custom-call | flops 2013265920 | bytes 3932160 | tf_op jit(solution)/shard_map/attend_image/pallas_call | solution.py:280
  97.2 3.9 %all-to-all-start.2 = ((bf16[8,64,384]{2,1,0:T(8,128)(2,1)}), bf16[8,64,384]{2,1,0:T(8,128)(2,1)S(1)}, u32[]{:S(2)}, u32[]{:S(2)}) async-start(bf16[8,64,384]{2,1,0:T(8,128)(2,1)} %copy-done.9), calls=%async_computation.2 | async-start | bytes 786432 | tf_op jit(solution)/shard_map/all_to_all | solution.py:394
  101.1 1.8 %after.14.x_ref = bf16[8,64,384]{2,1,0:T(8,128)(2,1)} custom-call(bf16[8,64,384]{2,1,0:T(8,128)(2,1)} %all-to-all-done.3.x, bf16[8,64,384]{2,1,0:T(8,128)(2,1)} %copy-done.9), custom_call_target="tpu_custom_call" | custom-call | tf_op jit(solution)/shard_map/after/pallas_call | solution.py:348
  103.9 1.3 %collective-permute-start.13 = (bf16[64,3072]{1,0:T(8,128)(2,1)S(1)}, bf16[64,3072]{1,0:T(8,128)(2,1)S(1)}, u32[]{:S(2)}, u32[]{:S(2)}) collective-permute-start(bf16[64,3072]{1,0:T(8,128)(2,1)S(1)} %unpack_text.1), channel_id=1, source_target_pairs={{8,0},{12,4},{16,24},{20,28},{9,1},{13,5},{17,25},{21,29},{10,2},{... | collective-permute-start | bytes 1179656 | tf_op jit(solution)/shard_map/ppermute | solution.py:467
  105.2 3.5 %all-to-all-done.2.x_ref = bf16[8,64,384]{2,1,0:T(8,128)(2,1)S(1)} async-done(((bf16[8,64,384]{2,1,0:T(8,128)(2,1)}), bf16[8,64,384]{2,1,0:T(8,128)(2,1)S(1)}, u32[]{:S(2)}, u32[]{:S(2)}) %all-to-all-start.2) | async-done | bytes 393248 | tf_op jit(solution)/shard_map/all_to_all | solution.py:394
  108.7 7.8 %project.1.other = bf16[64,3072]{1,0:T(8,128)(2,1)} custom-call(bf16[8,64,384]{2,1,0:T(8,128)(2,1)S(1)} %all-to-all-done.2.x_ref, bf16[8,384,3072]{2,1,0:T(8,128)(2,1)} %bitcast.8, bf16[64,3072]{1,0:T(8,128)(2,1)S(1)} %copy-done.14, f32[1,3072]{1,0:T(1,128)S(1)} %bitcast.7), custom_call_target="tpu_custom_call" | custom-call | flops 1207959552 | bytes 18874368 | tf_op jit(solution)/shard_map/project/pallas_call | solution.py:323
  117.3 1.8 %after.15 = bf16[64,3072]{1,0:T(8,128)(2,1)} custom-call(bf16[64,3072]{1,0:T(8,128)(2,1)} %copy-done.17, bf16[64,3072]{1,0:T(8,128)(2,1)} %project.1.other), custom_call_target="tpu_custom_call" | custom-call | tf_op jit(solution)/shard_map/after/pallas_call | solution.py:348
  119.4 1.5 %collective-permute-done.14 = bf16[64,3072]{1,0:T(8,128)(2,1)S(1)} collective-permute-done((bf16[64,3072]{1,0:T(8,128)(2,1)S(1)}, bf16[64,3072]{1,0:T(8,128)(2,1)S(1)}, u32[]{:S(2)}, u32[]{:S(2)}) %collective-permute-start.14) | collective-permute-done | bytes 393248 | tf_op jit(solution)/shard_map/ppermute | solution.py:399
  (60 shorter events, 12.3 us)
Async XLA Ops:
  0.6 19.3 %collective-permute-start.1 = (bf16[2,256,768]{2,1,0:T(8,128)(2,1)}, bf16[2,256,768]{2,1,0:T(8,128)(2,1)S(1)}, u32[]{:S(2)}, u32[]{:S(2)}) collective-permute-start(bf16[2,256,768]{2,1,0:T(8,128)(2,1)} %refs_0_.7), channel_id=1, source_target_pairs={{4,8},{12,16},{20,24},{8,4},{16,12},{24,20},{5,9},{13,17},{21,25},... | collective-permute-start | bytes 2359304 | tf_op jit(solution)/shard_map/ppermute | solution.py:425
  4.4 21.6 %collective-permute-start = (bf16[2,256,768]{2,1,0:T(8,128)(2,1)}, bf16[2,256,768]{2,1,0:T(8,128)(2,1)}, u32[]{:S(2)}, u32[]{:S(2)}) collective-permute-start(bf16[2,256,768]{2,1,0:T(8,128)(2,1)} %refs_0_.7), channel_id=1, source_target_pairs={{0,8},{8,16},{16,24},{12,4},{20,12},{28,20},{1,9},{9,17},{17,25},{... | collective-permute-start | bytes 2359304 | tf_op jit(solution)/shard_map/ppermute | solution.py:425
  6.5 1.7 %copy-start = (bf16[128,9216]{1,0:T(8,128)(2,1)S(1)}, bf16[128,9216]{1,0:T(8,128)(2,1)}, u32[]{:S(2)}) copy-start(bf16[128,9216]{1,0:T(8,128)(2,1)} %refs_2_.2) | copy-start | bytes 7077892
  11.1 20.3 %all-to-all-start = ((bf16[8,64,1152]{2,1,0:T(8,128)(2,1)}), bf16[8,64,1152]{2,1,0:T(8,128)(2,1)S(1)}, u32[]{:S(2)}, u32[]{:S(2)}) async-start(bf16[8,64,1152]{2,1,0:T(8,128)(2,1)} %pack_heads.2.other), calls=%async_computation | async-start | bytes 2359296 | tf_op jit(solution)/shard_map/all_to_all | solution.py:394
  22.9 8.5 %copy-start.1 = (bf16[2,256,768]{2,1,0:T(8,128)(2,1)S(1)}, bf16[2,256,768]{2,1,0:T(8,128)(2,1)}, u32[]{:S(2)}) copy-start(bf16[2,256,768]{2,1,0:T(8,128)(2,1)} %after.9.refs_5_.refs_3_) | copy-start | bytes 2359300
  22.9 8.5 %copy-start.4 = (bf16[64,9216]{1,0:T(8,128)(2,1)S(1)}, bf16[64,9216]{1,0:T(8,128)(2,1)}, u32[]{:S(2)}) copy-start(bf16[64,9216]{1,0:T(8,128)(2,1)} %refs_2_.3) | copy-start | bytes 3538948
  22.9 12.5 %collective-permute-start.4 = (bf16[2,256,768]{2,1,0:T(8,128)(2,1)}, bf16[2,256,768]{2,1,0:T(8,128)(2,1)}, u32[]{:S(2)}, u32[]{:S(2)}) collective-permute-start(bf16[2,256,768]{2,1,0:T(8,128)(2,1)} %after.9.refs_5_.refs_3_), channel_id=1, source_target_pairs={{8,16},{16,24},{12,4},{20,12},{9,17},{17,25},{13,5},{21,13},{10,18... | collective-permute-start | bytes 2359304 | tf_op jit(solution)/shard_map/ppermute | solution.py:425
  28.1 14.7 %collective-permute-start.3 = (bf16[2,256,768]{2,1,0:T(8,128)(2,1)}, bf16[2,256,768]{2,1,0:T(8,128)(2,1)}, u32[]{:S(2)}, u32[]{:S(2)}) collective-permute-start(bf16[2,256,768]{2,1,0:T(8,128)(2,1)} %after.8.refs_4_.refs_2_), channel_id=1, source_target_pairs={{8,16},{16,24},{12,4},{20,12},{9,17},{17,25},{13,5},{21,13},{10,18... | collective-permute-start | bytes 2359304 | tf_op jit(solution)/shard_map/ppermute | solution.py:425
  30.3 27.1 %collective-permute-start.2 = (bf16[2,256,768]{2,1,0:T(8,128)(2,1)}, bf16[2,256,768]{2,1,0:T(8,128)(2,1)}, u32[]{:S(2)}, u32[]{:S(2)}) collective-permute-start(bf16[2,256,768]{2,1,0:T(8,128)(2,1)} %refs_0_.7), channel_id=1, source_target_pairs={{0,4},{4,0},{8,12},{12,8},{16,20},{20,16},{24,28},{28,24},{1,5},{5... | collective-permute-start | bytes 2359304 | tf_op jit(solution)/shard_map/ppermute | solution.py:399
  31.3 26.4 %collective-permute-start.7 = (bf16[2,256,768]{2,1,0:T(8,128)(2,1)}, bf16[2,256,768]{2,1,0:T(8,128)(2,1)}, u32[]{:S(2)}, u32[]{:S(2)}) collective-permute-start(bf16[2,256,768]{2,1,0:T(8,128)(2,1)} %after.8.refs_4_.refs_2_), channel_id=1, source_target_pairs={{0,4},{4,0},{8,12},{12,8},{16,20},{20,16},{24,28},{28,24},{1,5},{5... | collective-permute-start | bytes 2359304 | tf_op jit(solution)/shard_map/ppermute | solution.py:399
  31.4 1.1 copy-start.2
  37.6 20.3 %collective-permute-start.11 = (bf16[2,256,768]{2,1,0:T(8,128)(2,1)}, bf16[2,256,768]{2,1,0:T(8,128)(2,1)}, u32[]{:S(2)}, u32[]{:S(2)}) collective-permute-start(bf16[2,256,768]{2,1,0:T(8,128)(2,1)} %after.11.refs_5_.refs_7_), channel_id=1, source_target_pairs={{16,24},{12,4},{17,25},{13,5},{18,26},{14,6},{19,27},{15,7}} | collective-permute-start | bytes 2359304 | tf_op jit(solution)/shard_map/ppermute | solution.py:425
  44.9 12.5 %copy-start.5 = (bf16[2,256,768]{2,1,0:T(8,128)(2,1)S(1)}, bf16[2,256,768]{2,1,0:T(8,128)(2,1)}, u32[]{:S(2)}) copy-start(bf16[2,256,768]{2,1,0:T(8,128)(2,1)} %after.11.refs_5_.refs_7_) | copy-start | bytes 2359300
  44.9 17.6 %copy-start.3 = (bf16[2,256,768]{2,1,0:T(8,128)(2,1)S(1)}, bf16[2,256,768]{2,1,0:T(8,128)(2,1)}, u32[]{:S(2)}) copy-start(bf16[2,256,768]{2,1,0:T(8,128)(2,1)} %after.8.refs_4_.refs_2_) | copy-start | bytes 2359300
  44.9 13.3 %collective-permute-start.9 = (bf16[2,256,768]{2,1,0:T(8,128)(2,1)}, bf16[2,256,768]{2,1,0:T(8,128)(2,1)}, u32[]{:S(2)}, u32[]{:S(2)}) collective-permute-start(bf16[2,256,768]{2,1,0:T(8,128)(2,1)} %after.10.refs_4_.refs_6_), channel_id=1, source_target_pairs={{16,24},{12,4},{17,25},{13,5},{18,26},{14,6},{19,27},{15,7}} | collective-permute-start | bytes 2359304 | tf_op jit(solution)/shard_map/ppermute | solution.py:425
  46.6 30.5 %all-to-all-start.1 = ((bf16[8,64,1152]{2,1,0:T(8,128)(2,1)}), bf16[8,64,1152]{2,1,0:T(8,128)(2,1)}, u32[]{:S(2)}, u32[]{:S(2)}) async-start(bf16[8,64,1152]{2,1,0:T(8,128)(2,1)} %pack_heads.3.other), calls=%async_computation.1 | async-start | bytes 2359296 | tf_op jit(solution)/shard_map/all_to_all | solution.py:394
  57.2 5.3 %collective-permute-start.8 = (bf16[2,256,768]{2,1,0:T(8,128)(2,1)S(1)}, bf16[2,256,768]{2,1,0:T(8,128)(2,1)}, u32[]{:S(2)}, u32[]{:S(2)}) collective-permute-start(bf16[2,256,768]{2,1,0:T(8,128)(2,1)S(1)} %copy-done.1), channel_id=1, source_target_pairs={{0,4},{4,0},{8,12},{12,8},{16,20},{20,16},{24,28},{28,24},{1,5},{5... | collective-permute-start | bytes 2359304 | tf_op jit(solution)/shard_map/ppermute | solution.py:399
  57.4 5.1 %collective-permute-start.6 = (bf16[2,256,768]{2,1,0:T(8,128)(2,1)S(1)}, bf16[2,256,768]{2,1,0:T(8,128)(2,1)}, u32[]{:S(2)}, u32[]{:S(2)}) collective-permute-start(bf16[2,256,768]{2,1,0:T(8,128)(2,1)S(1)} %copy-done.5), channel_id=1, source_target_pairs={{0,4},{4,0},{8,12},{12,8},{16,20},{20,16},{24,28},{28,24},{1,5},{5... | collective-permute-start | bytes 2359304 | tf_op jit(solution)/shard_map/ppermute | solution.py:399
  57.7 4.8 %collective-permute-start.5 = (bf16[2,256,768]{2,1,0:T(8,128)(2,1)}, bf16[2,256,768]{2,1,0:T(8,128)(2,1)}, u32[]{:S(2)}, u32[]{:S(2)}) collective-permute-start(bf16[2,256,768]{2,1,0:T(8,128)(2,1)} %after.10.refs_4_.refs_6_), channel_id=1, source_target_pairs={{0,4},{4,0},{8,12},{12,8},{16,20},{20,16},{24,28},{28,24},{1,5},{5... | collective-permute-start | bytes 2359304 | tf_op jit(solution)/shard_map/ppermute | solution.py:399
  57.9 27.6 %collective-permute-start.12 = (bf16[2,256,768]{2,1,0:T(8,128)(2,1)}, bf16[2,256,768]{2,1,0:T(8,128)(2,1)}, u32[]{:S(2)}, u32[]{:S(2)}) collective-permute-start(bf16[2,256,768]{2,1,0:T(8,128)(2,1)} %collective-permute-done.11.refs_11_), channel_id=1, source_target_pairs={{0,4},{4,0},{8,12},{12,8},{16,20},{20,16},{24,28},{28,24},{1,5},{5... | collective-permute-start | bytes 2359304 | tf_op jit(solution)/shard_map/ppermute | solution.py:399
  58.2 27.2 %collective-permute-start.10 = (bf16[2,256,768]{2,1,0:T(8,128)(2,1)}, bf16[2,256,768]{2,1,0:T(8,128)(2,1)}, u32[]{:S(2)}, u32[]{:S(2)}) collective-permute-start(bf16[2,256,768]{2,1,0:T(8,128)(2,1)} %collective-permute-done.9.refs_10_), channel_id=1, source_target_pairs={{0,4},{4,0},{8,12},{12,8},{16,20},{20,16},{24,28},{28,24},{1,5},{5... | collective-permute-start | bytes 2359304 | tf_op jit(solution)/shard_map/ppermute | solution.py:399
  62.5 1.1 copy-start.6
  63.6 1.1 copy-start.10
  78.8 18.4 %all-to-all-start.3 = ((bf16[8,64,384]{2,1,0:T(8,128)(2,1)}), bf16[8,64,384]{2,1,0:T(8,128)(2,1)}, u32[]{:S(2)}, u32[]{:S(2)}) async-start(bf16[8,64,384]{2,1,0:T(8,128)(2,1)} %after.12.other), calls=%async_computation.3 | async-start | bytes 786432 | tf_op jit(solution)/shard_map/all_to_all | solution.py:394
  85.4 1.1 copy-start.7
  86.6 1.3 %copy-start.8 = (bf16[8,64,1152]{2,1,0:T(8,128)(2,1)S(1)}, bf16[8,64,1152]{2,1,0:T(8,128)(2,1)}, u32[]{:S(2)}) copy-start(bf16[8,64,1152]{2,1,0:T(8,128)(2,1)} %after.13.img) | copy-start | bytes 3538948
  87.9 1.1 copy-start.11
  97.2 11.5 %all-to-all-start.2 = ((bf16[8,64,384]{2,1,0:T(8,128)(2,1)}), bf16[8,64,384]{2,1,0:T(8,128)(2,1)S(1)}, u32[]{:S(2)}, u32[]{:S(2)}) async-start(bf16[8,64,384]{2,1,0:T(8,128)(2,1)} %copy-done.9), calls=%async_computation.2 | async-start | bytes 786432 | tf_op jit(solution)/shard_map/all_to_all | solution.py:394
  101.1 7.7 %copy-start.14 = (bf16[64,3072]{1,0:T(8,128)(2,1)S(1)}, bf16[64,3072]{1,0:T(8,128)(2,1)}, u32[]{:S(2)}) copy-start(bf16[64,3072]{1,0:T(8,128)(2,1)} %residual.1) | copy-start | bytes 1179652
  101.1 7.7 %copy-start.15 = (f32[3072]{0:T(1024)S(1)}, f32[3072]{0:T(1024)}, u32[]{:S(2)}) copy-start(f32[3072]{0:T(1024)} %param.10) | copy-start | bytes 36868
  103.9 12.6 %collective-permute-start.13 = (bf16[64,3072]{1,0:T(8,128)(2,1)S(1)}, bf16[64,3072]{1,0:T(8,128)(2,1)S(1)}, u32[]{:S(2)}, u32[]{:S(2)}) collective-permute-start(bf16[64,3072]{1,0:T(8,128)(2,1)S(1)} %unpack_text.1), channel_id=1, source_target_pairs={{8,0},{12,4},{16,24},{20,28},{9,1},{13,5},{17,25},{21,29},{10,2},{... | collective-permute-start | bytes 1179656 | tf_op jit(solution)/shard_map/ppermute | solution.py:467
  119.1 1.8 %collective-permute-start.14 = (bf16[64,3072]{1,0:T(8,128)(2,1)S(1)}, bf16[64,3072]{1,0:T(8,128)(2,1)S(1)}, u32[]{:S(2)}, u32[]{:S(2)}) collective-permute-start(bf16[64,3072]{1,0:T(8,128)(2,1)S(1)} %broadcast_select_fusion), channel_id=1, source_target_pairs={{0,4},{4,0},{8,12},{12,8},{16,20},{20,16},{24,28},{28,24},{1,5},{5... | collective-permute-start | bytes 1179656 | tf_op jit(solution)/shard_map/ppermute | solution.py:399
  (5 other events, 4.1 us)

commit v12 on v11

--- a/solution.py
+++ b/solution.py
@@ -11,9 +11,9 @@
 HD = 128
 SCALE = math.log2(math.e) / math.sqrt(HD)
 VMEM_LIMIT = 12 * 1024 * 1024
+ATTEND_LIMIT = 24 * 1024 * 1024
 WIDE_LIMIT = 48 * 1024 * 1024
-TILE = 256
-TEXT_TILE = 128
+TILE = 512
 FIRST_KEYS = 256
 LARGE = 2.0**60
 
@@ -31,7 +31,7 @@
         packed[0, :, part * width : (part + 1) * width] = source[...]
 
 
-def pack(first_block, array, rows, head_owners, pair, width, after=()):
+def pack(first_block, array, rows, head_owners, pair, width, after=(), weight=1):
     blocks = array.shape[1] // 3 // width
     destinations = head_owners * pair
 
@@ -52,6 +52,9 @@
         ),
         out_shape=jax.ShapeDtypeStruct((destinations, rows, 3 * width), array.dtype),
         compiler_params=params(),
+        cost_estimate=pl.CostEstimate(
+            flops=0, bytes_accessed=weight * 12 * destinations * rows * width, transcendentals=0
+        ),
         name="pack_heads",
     )(first_block, array, array, array, *after)
 
@@ -131,49 +134,56 @@
             at += blocks[0].shape[1]
 
 
-def accumulate(flag, total, aug, heads, queries_of, first_keys_of, own, chosen, tile_rows):
+def accumulate(flag, total, aug, heads, queries_of, first_of, shared_of, own, chosen):
+    rows = total.shape[1]
+
     def columns(head):
         return slice(head * HD, (head + 1) * HD)
 
-    def pieces(head, some):
-        return some(head) + [
+    def shared(head):
+        return shared_of(head) + [
             (chosen[index, 0, :, columns(head)], chosen[index, 1, :, columns(head)])
             for index in range(chosen.shape[0])
         ]
 
-    def tiles():
-        for head in range(heads):
-            queries = queries_of(head)
-            for span, some in own:
-                for tile in tiles_of(span.stop - span.start, tile_rows):
-                    tile = slice(span.start + tile.start, span.start + tile.stop)
-                    yield head, tile, queries[tile, :], some
-
-    def largest(queries, key_rows):
-        return jnp.max(dot(queries, key_rows, (1, 1)), axis=1, keepdims=True)
+    def largest(queries, some):
+        row_max = None
+        for key_rows, _ in some:
+            piece_max = jnp.max(dot(queries, key_rows, (1, 1)), axis=1, keepdims=True)
+            row_max = piece_max if row_max is None else jnp.maximum(row_max, piece_max)
+        return row_max
 
     def attempt(turn):
         @pl.when(turn == 0)
         def _():
-            for head, tile, queries, _ in tiles():
-                aug[head, tile, :] = reference_columns(largest(queries, first_keys_of(head)))
+            for head in range(heads):
+                queries = queries_of(head)
+                for tile in tiles_of(rows, TILE):
+                    aug[head, tile, :] = reference_columns(
+                        largest(queries[tile, :], [(first_of(head), None)])
+                    )
 
         @pl.when(turn == 1)
         def _():
-            for head, tile, queries, some in tiles():
-                row_max = None
-                for key_rows, _ in pieces(head, some):
-                    piece_max = largest(queries, key_rows)
-                    row_max = piece_max if row_max is None else jnp.maximum(row_max, piece_max)
-                aug[head, tile, :] = reference_columns(row_max)
-
-        for head, tile, queries, some in tiles():
-            both = jnp.concatenate([queries, aug[head, tile, :]], axis=1)
-            summed = None
-            for key_rows, values in pieces(head, some):
-                part = weighted(both, with_ones(key_rows), with_ones(values))
-                summed = part if summed is None else summed + part
-            total[head, tile, :] = summed
+            for head in range(heads):
+                queries = queries_of(head)
+                for span, some in own:
+                    row_max = largest(queries[span, :], shared(head) + some(head))
+                    aug[head, span, :] = reference_columns(row_max)
+
+        for head in range(heads):
+            both = jnp.concatenate([queries_of(head), aug[head]], axis=1)
+            for tile in tiles_of(rows, TILE):
+                summed = None
+                for key_rows, values in shared(head):
+                    part = weighted(both[tile, :], with_ones(key_rows), with_ones(values))
+                    summed = part if summed is None else summed + part
+                total[head, tile, :] = summed
+            for span, some in own:
+                for key_rows, values in some(head):
+                    total[head, span, :] += weighted(
+                        both[span, :], with_ones(key_rows), with_ones(values)
+                    )
 
     until_small(flag, total, attempt)
 
@@ -190,53 +200,67 @@
 
 
 def text_body(pair, entries, info, txt, *refs, wanted):
-    stale, came = refs[:pair], refs[pair:-7]
-    out, chosen, beside, aug, total, flag, sems = refs[-7:]
+    stale, came = refs[:pair], refs[pair:-10]
+    result, held_txt, out, chosen, beside, aug, total, flag, sems, plain = refs[-10:]
     width = chosen.shape[3]
     heads = width // HD
 
     @pl.when(info[wanted] == 1)
     def _():
         fetch = Fetch(info, width, sems)
+        whole = pltpu.make_async_copy(txt, held_txt, plain.at[0])
+        whole.start()
         at = 0
         for block in stale:
             fetch.start([block], [], beside.at[0], at)
             at += block.shape[1]
         settle(fetch, came, entries, chosen)
+        whole.wait()
         fetch.wait()
 
-        def own(head):
+        def shared(head):
             columns = slice(head * HD, (head + 1) * HD)
             return [
-                (part_of(txt, 1, head, width), part_of(txt, 2, head, width)),
+                (part_of(held_txt, 1, head, width), part_of(held_txt, 2, head, width)),
                 (beside[0, 0, :, columns], beside[0, 1, :, columns]),
             ]
 
         accumulate(
             flag, total, aug, heads,
-            lambda head: part_of(txt, 0, head, width),
-            lambda head: part_of(txt, 1, head, width)[: min(FIRST_KEYS, total.shape[1]), :],
-            [(slice(0, total.shape[1]), own)], chosen, TEXT_TILE,
+            lambda head: part_of(held_txt, 0, head, width),
+            lambda head: part_of(held_txt, 1, head, width)[: min(FIRST_KEYS, total.shape[1]), :],
+            shared, [(slice(0, total.shape[1]), lambda head: [])], chosen,
         )
         finish(out, total)
+        back = pltpu.make_async_copy(out, result, plain.at[0])
+        back.start()
+        back.wait()
 
 
 def image_body(pair, entries, info, img, txt, *refs):
-    stale, came = refs[:pair], refs[pair:-7]
-    out, chosen, beside, aug, total, flag, sems = refs[-7:]
+    stale, came = refs[:pair], refs[pair:-12]
+    (result, held_img, held_txt, out, chosen, beside, aug, total, flag, sems, plain) = refs[-11:]
     width = chosen.shape[3]
     heads = width // HD
     rows = total.shape[1]
     group_rows, sources = rows // pair, img.shape[0] // pair
     fetch = Fetch(info, width, sems)
+    wholes = [
+        pltpu.make_async_copy(source, target, plain.at[index])
+        for index, (source, target) in enumerate(((txt, held_txt), (img, held_img)))
+    ]
+    for whole in wholes:
+        whole.start()
     if pair == 2:
         for group in range(pair):
             flags = [info[0] != group, info[0] == group]
             fetch.start(stale, flags, beside.at[group], group_rows)
     settle(fetch, came, entries, chosen)
+    for whole in wholes:
+        whole.wait()
     for group in range(pair):
         for part in range(2):
-            fresh = img[
+            fresh = held_img[
                 group * sources : (group + 1) * sources, :, (1 + part) * width : (2 + part) * width
             ]
             beside[group, part, :group_rows, :] = fresh.reshape(group_rows, width)
@@ -245,58 +269,60 @@
     def own(group):
         def some(head):
             columns = slice(head * HD, (head + 1) * HD)
-            return [
-                (part_of(txt, 1, head, width), part_of(txt, 2, head, width)),
-                (beside[group, 0, :, columns], beside[group, 1, :, columns]),
-            ]
+            return [(beside[group, 0, :, columns], beside[group, 1, :, columns])]
 
         return (slice(group * group_rows, (group + 1) * group_rows), some)
 
     text_keys = txt.shape[0] * txt.shape[1]
     accumulate(
         flag, total, aug, heads,
-        lambda head: part_of(img, 0, head, width),
-        lambda head: part_of(txt, 1, head, width)[: min(FIRST_KEYS, text_keys), :],
-        [own(group) for group in range(pair)], chosen, TILE,
+        lambda head: part_of(held_img, 0, head, width),
+        lambda head: part_of(held_txt, 1, head, width)[: min(FIRST_KEYS, text_keys), :],
+        lambda head: [(part_of(held_txt, 1, head, width), part_of(held_txt, 2, head, width))],
+        [own(group) for group in range(pair)], chosen,
     )
     finish(out, total)
-
-
-def attend(name, body, info, fresh, stale, entries, groups):
+    back = pltpu.make_async_copy(out, result, plain.at[0])
+    back.start()
+    back.wait()
+
+
+def attend(name, body, info, fresh, stale, entries, groups, earlier=()):
     first = fresh[0]
     width = first.shape[2] // 3
     heads, rows = width // HD, first.shape[0] * first.shape[1]
     keys = sum(block.shape[1] for block in stale)
     came = [b for candidates in entries for blocks in candidates for b in blocks]
     counts = [[len(blocks) for blocks in candidates] for candidates in entries]
-    vmem = pl.BlockSpec(memory_space=pltpu.VMEM)
-    scratch = [
+    anywhere = pl.BlockSpec(memory_space=pl.ANY)
+    result = jax.ShapeDtypeStruct(first.shape[:2] + (width,), first.dtype)
+    scratch = [(array.shape, array.dtype) for array in fresh] + [
+        (result.shape, result.dtype),
         ((len(entries), 2, keys, width), first.dtype),
         ((groups, 2, keys, width), first.dtype),
         ((heads, rows, HD), jnp.bfloat16),
         ((heads, rows, 2 * HD), jnp.float32),
     ]
-    needed = sum(math.prod(shape) * jnp.dtype(kind).itemsize for shape, kind in scratch)
+    operands = [*fresh, *stale, *came, *earlier]
     return pl.pallas_call(
         functools.partial(body, len(stale), counts),
-        in_specs=[pl.BlockSpec(memory_space=pltpu.SMEM)]
-        + [vmem] * len(fresh)
-        + [pl.BlockSpec(memory_space=pl.ANY)] * (len(stale) + len(came)),
-        out_specs=vmem,
-        out_shape=jax.ShapeDtypeStruct(first.shape[:2] + (width,), first.dtype),
+        in_specs=[pl.BlockSpec(memory_space=pltpu.SMEM)] + [anywhere] * len(operands),
+        out_specs=anywhere,
+        out_shape=result,
         scratch_shapes=[pltpu.VMEM(*one) for one in scratch]
         + [
             pltpu.SMEM((1,), jnp.int32),
             pltpu.SemaphoreType.DMA((len(stale) * (1 + len(entries)),)),
+            pltpu.SemaphoreType.DMA((2,)),
         ],
-        compiler_params=pltpu.CompilerParams(vmem_limit_bytes=VMEM_LIMIT + needed),
+        compiler_params=pltpu.CompilerParams(vmem_limit_bytes=ATTEND_LIMIT),
         cost_estimate=pl.CostEstimate(
             flops=4 * rows * keys * (2 + len(entries)) * width,
             bytes_accessed=4 * keys * (2 + len(entries)) * width,
             transcendentals=rows * keys * (2 + len(entries)) * heads,
         ),
         name=name,
-    )(info, *fresh, *stale, *came)
+    )(info, *operands)
 
 
 def project_body(order, x_ref, weight, residual, gate, out, held, total, sems):
@@ -338,39 +364,47 @@
     )(x, weight.reshape(destinations, width, model), residual, gate.reshape(1, model))
 
 
-def after_body(x, other, out):
-    del other
-    out[...] = x[...]
-
-
-def after(x, other):
-    held = pl.BlockSpec(memory_space=pltpu.VMEM)
-    return pl.pallas_call(
-        after_body,
-        in_specs=[held, pl.BlockSpec(memory_space=pl.ANY)],
-        out_specs=held,
-        out_shape=jax.ShapeDtypeStruct(x.shape, x.dtype),
-        name="after",
-    )(x, other)
-
-
-def unpack_body(order, x_ref, out):
+def unpack_body(order, x_ref, earlier, out):
+    del earlier
     width = x_ref.shape[2]
     for source, place in enumerate(order):
         out[:, place * width : (place + 1) * width] = x_ref[source]
 
 
-def unpack(x, order):
+def unpack(x, order, earlier):
     rows, model = x.shape[1], x.shape[0] * x.shape[2]
+    vmem = pl.BlockSpec(memory_space=pltpu.VMEM)
     return pl.pallas_call(
         functools.partial(unpack_body, order),
-        grid=(1,),
-        in_specs=[pl.BlockSpec(x.shape, lambda n: (0, 0, 0))],
-        out_specs=pl.BlockSpec((rows, model), lambda n: (0, 0)),
+        in_specs=[vmem, pl.BlockSpec(memory_space=pl.ANY)],
+        out_specs=vmem,
         out_shape=jax.ShapeDtypeStruct((rows, model), x.dtype),
-        compiler_params=params(),
         name="unpack_text",
-    )(x)
+    )(x, earlier)
+
+
+def choose_body(flag, first, second, earlier, out):
+    del earlier
+
+    @pl.when(flag[0] == 1)
+    def _():
+        out[...] = first[...]
+
+    @pl.when(flag[0] == 0)
+    def _():
+        out[...] = second[...]
+
+
+def choose(flag, first, second, earlier):
+    vmem = pl.BlockSpec(memory_space=pltpu.VMEM)
+    return pl.pallas_call(
+        choose_body,
+        in_specs=[pl.BlockSpec(memory_space=pltpu.SMEM), vmem, vmem]
+        + [pl.BlockSpec(memory_space=pl.ANY)],
+        out_specs=vmem,
+        out_shape=jax.ShapeDtypeStruct(first.shape, first.dtype),
+        name="choose_text",
+    )(flag, first, second, earlier)
 
 
 def per_device(img_qkv, txt_qkv, stale_kv, residual, gate_scale, proj_weight):
@@ -404,13 +438,8 @@
     def down_pairs(step):
         return [(z + 1, z) for z in range(0, planes - step)]
 
-    def pack_img(earlier):
-        first = jnp.zeros((1,), jnp.int32)
-        return pack(first, img_qkv, img_rows, head_owners, pair, width, earlier)
-
     core_only = core.astype(jnp.int32).reshape(1)
-    packed = pack(core_only, txt_qkv, text_rows, head_owners, pair, width)
-    txt = exchange(packed)
+    txt = exchange(pack(core_only, txt_qkv, text_rows, head_owners, pair, width))
 
     along, against = [], []
     if pair == 2:
@@ -423,11 +452,6 @@
                 for turn in ((0, 1) if step == 1 else (0, 0))
             ]
             held = [lax.ppermute(block, "patch", way) for block, way in zip(held, pairs)]
-            if step == 1:
-                held = [after(block, packed) for block in held]
-            elif step == 2:
-                packed = pack_img([txt] + along[0])
-                held = [after(block, packed) for block in held]
             along.append(held)
             against.append([swap(block) for block in held])
         ahead = jnp.where(core == 0, plane, planes - 1 - plane)
@@ -442,9 +466,10 @@
         ahead = plane
     entries = [[along[i - 1], against[planes - i - 1]] for i in range(1, planes)]
     first_holds = [ahead >= i for i in range(1, planes)]
-    if pair == 1 or planes < 3:
-        packed = pack_img([txt] + along[0])
-    img = exchange(packed)
+    zero_only = jnp.zeros((1,), jnp.int32)
+    img = exchange(
+        pack(zero_only, img_qkv, img_rows, head_owners, pair, width, [txt] + along[0], 64)
+    )
 
     early = planes > 2
     inner = (plane > 0) & (plane < planes - 1)
@@ -455,17 +480,16 @@
     text_attn = attend(
         "attend_text", functools.partial(text_body, wanted=planes), info, [txt], stale, known, 1
     )
-    text_attn = after(text_attn, img)
-    img = after(img, text_attn)
-    image_attn = attend("attend_image", image_body, info, [img, txt], stale, entries, pair)
-    image_back = exchange(image_attn)
-    text_out = unpack(after(exchange(text_attn), image_attn), order)
-    image_out = project(image_back, order, proj_weight, residual, gate_scale)
+    image_attn = attend(
+        "attend_image", image_body, info, [img, txt], stale, entries, pair, [text_attn]
+    )
+    text_out = unpack(exchange(text_attn), order, image_attn)
+    image_out = project(exchange(image_attn), order, proj_weight, residual, gate_scale)
     if early:
         ends = [(1, 0), (planes - 2, planes - 1)]
         ends = [(a * pair + c, b * pair + c) for a, b in ends for c in range(pair)]
-        hopped = after(lax.ppermute(text_out, "patch", ends), image_out)
-        text_out = jnp.where(inner, text_out, hopped)
+        hopped = lax.ppermute(text_out, "patch", ends)
+        text_out = choose(inner.astype(jnp.int32).reshape(1), text_out, hopped, image_out)
     if pair == 2:
         other = swap(text_out)
         lower = core == 0

time: 123 us -> 117 us (0.951)
  the two profiles are of different devices: /device:TPU:17 before, /device:TPU:9 now
where the time goes in v12:
time: 117 us; the launch traced here: 116 us
  starting transfers between devices  40.6 us (35%)
  waiting for transfers between devices  35.3 us (30%)
  Pallas kernels  30.6 us (26%)
  local copies, waits for them, and re-layouts  6.81 us (6%)
  other arithmetic  1.98 us (2%)
    all_to_all x4, starting transfers between devices, exchange(): lax.all_to_all(x, ('patch', 'head'), split_axis=0, concat_axis=0, axis_in...  21.8 us
    pallas_call x2, Pallas kernels, attend(): pl.pallas_call(functools.partial(body, len(stale), counts), in_specs=[pl....  17.8 us
    all_to_all x4, waiting for transfers between devices, exchange(): lax.all_to_all(x, ('patch', 'head'), split_axis=0, concat_axis=0, axis_in...  17.1 us
    ppermute x6, starting transfers between devices, per_device(): lax.ppermute(block, 'patch', way)  15.6 us
    ppermute x6, waiting for transfers between devices, per_device(): lax.ppermute(block, 'patch', way)  12.8 us
    pallas_call x1, Pallas kernels, project(): pl.pallas_call(functools.partial(project_body, order), in_specs=[vmem, pl...  7.81 us
    unnamed x20, local copies, waits for them, and re-layouts  6.73 us
    ppermute x8, waiting for transfers between devices, swap(): return lax.ppermute(x, 'patch', swap_pairs)  5.34 us
  transfers between devices with their start and end apart: 19, of which 9 were waited for; matrix products, arithmetic and copies ran while one was open for 0% of the time, Pallas kernels for 25%

profile of v12, /device:TPU:9, one launch (start us, length us, event | category | flops | bytes accessed | tf_op | source)
XLA Modules:
  0.0 116.1 jit_solution(10948560479777378858)
XLA Ops:
  0.6 1.9 %collective-permute-start = (bf16[2,256,768]{2,1,0:T(8,128)(2,1)}, bf16[2,256,768]{2,1,0:T(8,128)(2,1)S(1)}, u32[]{:S(2)}, u32[]{:S(2)}) collective-permute-start(bf16[2,256,768]{2,1,0:T(8,128)(2,1)} %refs_0_.7), channel_id=1, source_target_pairs={{0,8},{8,16},{16,24},{12,4},{20,12},{28,20},{1,9},{9,17},{17,25},{... | collective-permute-start | bytes 2359304 | tf_op jit(solution)/shard_map/ppermute | solution.py:454
  2.6 5.3 %collective-permute-start.1 = (bf16[2,256,768]{2,1,0:T(8,128)(2,1)}, bf16[2,256,768]{2,1,0:T(8,128)(2,1)}, u32[]{:S(2)}, u32[]{:S(2)}) collective-permute-start(bf16[2,256,768]{2,1,0:T(8,128)(2,1)} %refs_0_.7), channel_id=1, source_target_pairs={{4,8},{12,16},{20,24},{8,4},{16,12},{24,20},{5,9},{13,17},{21,25},... | collective-permute-start | bytes 2359304 | tf_op jit(solution)/shard_map/ppermute | solution.py:454
  7.9 10.2 %collective-permute-done.refs_4_.refs_2_ = bf16[2,256,768]{2,1,0:T(8,128)(2,1)S(1)} collective-permute-done((bf16[2,256,768]{2,1,0:T(8,128)(2,1)}, bf16[2,256,768]{2,1,0:T(8,128)(2,1)S(1)}, u32[]{:S(2)}, u32[]{:S(2)}) %collective-permute-start) | collective-permute-done | bytes 786464 | tf_op jit(solution)/shard_map/ppermute | solution.py:454
  18.1 1.9 %collective-permute-start.3 = (bf16[2,256,768]{2,1,0:T(8,128)(2,1)S(1)}, bf16[2,256,768]{2,1,0:T(8,128)(2,1)}, u32[]{:S(2)}, u32[]{:S(2)}) collective-permute-start(bf16[2,256,768]{2,1,0:T(8,128)(2,1)S(1)} %collective-permute-done.refs_4_.refs_2_), channel_id=1, source_target_pairs={{8,16},{16,24},{12,4},{20,12},{9,17},{17,25},{13,5},{21,13},{10,18... | collective-permute-start | bytes 2359304 | tf_op jit(solution)/shard_map/ppermute | solution.py:454
  20.1 2.6 %collective-permute-done.1.refs_5_.refs_3_ = bf16[2,256,768]{2,1,0:T(8,128)(2,1)} collective-permute-done((bf16[2,256,768]{2,1,0:T(8,128)(2,1)}, bf16[2,256,768]{2,1,0:T(8,128)(2,1)}, u32[]{:S(2)}, u32[]{:S(2)}) %collective-permute-start.1) | collective-permute-done | bytes 786464 | tf_op jit(solution)/shard_map/ppermute | solution.py:454
  22.6 2.1 %collective-permute-start.6 = (bf16[2,256,768]{2,1,0:T(8,128)(2,1)}, bf16[2,256,768]{2,1,0:T(8,128)(2,1)}, u32[]{:S(2)}, u32[]{:S(2)}) collective-permute-start(bf16[2,256,768]{2,1,0:T(8,128)(2,1)} %collective-permute-done.1.refs_5_.refs_3_), channel_id=1, source_target_pairs={{8,16},{16,24},{12,4},{20,12},{9,17},{17,25},{13,5},{21,13},{10,18... | collective-permute-start | bytes 2359304 | tf_op jit(solution)/shard_map/ppermute | solution.py:454
  24.7 1.7 %copy-done = bf16[128,9216]{1,0:T(8,128)(2,1)S(1)} copy-done((bf16[128,9216]{1,0:T(8,128)(2,1)S(1)}, bf16[128,9216]{1,0:T(8,128)(2,1)}, u32[]{:S(2)}) %copy-start) | copy-done | bytes 2359320
  27.1 1.0 copy-done.2
  28.1 10.1 %all-to-all-start = ((bf16[8,64,1152]{2,1,0:T(8,128)(2,1)}), bf16[8,64,1152]{2,1,0:T(8,128)(2,1)S(1)}, u32[]{:S(2)}, u32[]{:S(2)}) async-start(bf16[8,64,1152]{2,1,0:T(8,128)(2,1)} %copy-done.2), calls=%async_computation | async-start | bytes 2359296 | tf_op jit(solution)/shard_map/all_to_all | solution.py:428
  38.7 2.2 %collective-permute-start.4 = (bf16[2,256,768]{2,1,0:T(8,128)(2,1)}, bf16[2,256,768]{2,1,0:T(8,128)(2,1)}, u32[]{:S(2)}, u32[]{:S(2)}) collective-permute-start(bf16[2,256,768]{2,1,0:T(8,128)(2,1)} %collective-permute-done.3.refs_4_.refs_6_), channel_id=1, source_target_pairs={{16,24},{12,4},{17,25},{13,5},{18,26},{14,6},{19,27},{15,7}} | collective-permute-start | bytes 2359304 | tf_op jit(solution)/shard_map/ppermute | solution.py:454
  41.0 2.2 %collective-permute-start.7 = (bf16[2,256,768]{2,1,0:T(8,128)(2,1)}, bf16[2,256,768]{2,1,0:T(8,128)(2,1)}, u32[]{:S(2)}, u32[]{:S(2)}) collective-permute-start(bf16[2,256,768]{2,1,0:T(8,128)(2,1)} %collective-permute-done.6.refs_5_.refs_7_), channel_id=1, source_target_pairs={{16,24},{12,4},{17,25},{13,5},{18,26},{14,6},{19,27},{15,7}} | collective-permute-start | bytes 2359304 | tf_op jit(solution)/shard_map/ppermute | solution.py:454
  43.1 11.2 %all-to-all-done.refs_3_.txt = bf16[8,64,1152]{2,1,0:T(8,128)(2,1)S(1)} async-done(((bf16[8,64,1152]{2,1,0:T(8,128)(2,1)}), bf16[8,64,1152]{2,1,0:T(8,128)(2,1)S(1)}, u32[]{:S(2)}, u32[]{:S(2)}) %all-to-all-start) | async-done | bytes 1179680 | tf_op jit(solution)/shard_map/all_to_all | solution.py:428
  55.0 1.0 copy-done.3
  56.0 3.7 %all-to-all-start.1 = ((bf16[8,64,1152]{2,1,0:T(8,128)(2,1)}), bf16[8,64,1152]{2,1,0:T(8,128)(2,1)S(1)}, u32[]{:S(2)}, u32[]{:S(2)}) async-start(bf16[8,64,1152]{2,1,0:T(8,128)(2,1)} %copy-done.3), calls=%async_computation.1 | async-start | bytes 2359296 | tf_op jit(solution)/shard_map/all_to_all | solution.py:428
  61.0 1.4 %collective-permute-done.12.refs_9_.refs_13_ = bf16[2,256,768]{2,1,0:T(8,128)(2,1)} collective-permute-done((bf16[2,256,768]{2,1,0:T(8,128)(2,1)}, bf16[2,256,768]{2,1,0:T(8,128)(2,1)}, u32[]{:S(2)}, u32[]{:S(2)}) %collective-permute-start.12) | collective-permute-done | bytes 786464 | tf_op jit(solution)/shard_map/ppermute | solution.py:433
  62.3 1.1 collective-permute-done.10.refs_7_.refs_9_
  63.5 1.1 collective-permute-done.9.refs_6_.refs_8_
  64.6 1.1 copy-done.4
  65.7 8.7 %attend_text.1.refs_14_ = bf16[8,64,384]{2,1,0:T(8,128)(2,1)} custom-call(s32[5]{0:T(128)S(1)} %stack.38.info, bf16[8,64,1152]{2,1,0:T(8,128)(2,1)S(1)} %all-to-all-done.refs_3_.txt, bf16[2,256,768]{2,1,0:T(8,128)(2,1)S(1)} %copy-done.4, bf16[2,256,768]{2,1,0:T(8,128)(2,1)} %collective-permute-done.2.refs_1_, ...), custom_call_target="tpu_custom_call" | custom-call | flops 2013265920 | bytes 3932160 | tf_op jit(solution)/shard_map/attend_text/pallas_call | solution.py:307
  74.4 1.4 %all-to-all-done.1.img = bf16[8,64,1152]{2,1,0:T(8,128)(2,1)S(1)} async-done(((bf16[8,64,1152]{2,1,0:T(8,128)(2,1)}), bf16[8,64,1152]{2,1,0:T(8,128)(2,1)S(1)}, u32[]{:S(2)}, u32[]{:S(2)}) %all-to-all-start.1) | async-done | bytes 1179680 | tf_op jit(solution)/shard_map/all_to_all | solution.py:428
  75.8 3.6 %all-to-all-start.3 = ((bf16[8,64,384]{2,1,0:T(8,128)(2,1)}), bf16[8,64,384]{2,1,0:T(8,128)(2,1)S(1)}, u32[]{:S(2)}, u32[]{:S(2)}) async-start(bf16[8,64,384]{2,1,0:T(8,128)(2,1)} %attend_text.1.refs_14_), calls=%async_computation.3 | async-start | bytes 786432 | tf_op jit(solution)/shard_map/all_to_all | solution.py:428
  79.4 1.1 copy-done.5
  80.5 9.1 %attend_image.1.earlier = bf16[8,64,384]{2,1,0:T(8,128)(2,1)} custom-call(s32[5]{0:T(128)S(1)} %stack.38.info, bf16[8,64,1152]{2,1,0:T(8,128)(2,1)S(1)} %all-to-all-done.1.img, bf16[8,64,1152]{2,1,0:T(8,128)(2,1)S(1)} %all-to-all-done.refs_3_.txt, bf16[2,256,768]{2,1,0:T(8,128)(2,1)S(1)} %copy-done.5, bf16[2,256,768]{2,1,0:T(8,128)(2,1)} %collective-permute-done.2.refs_1_, ...), custom_call_target="tpu_custom_call" | custom-call | flops 2013265920 | bytes 3932160 | tf_op jit(solution)/shard_map/attend_image/pallas_call | solution.py:307
  89.7 4.3 %all-to-all-start.2 = ((bf16[8,64,384]{2,1,0:T(8,128)(2,1)}), bf16[8,64,384]{2,1,0:T(8,128)(2,1)S(1)}, u32[]{:S(2)}, u32[]{:S(2)}) async-start(bf16[8,64,384]{2,1,0:T(8,128)(2,1)} %attend_image.1.earlier), calls=%async_computation.2 | async-start | bytes 786432 | tf_op jit(solution)/shard_map/all_to_all | solution.py:428
  94.0 1.8 %unpack_text.1.first = bf16[64,3072]{1,0:T(8,128)(2,1)} custom-call(bf16[8,64,384]{2,1,0:T(8,128)(2,1)} %copy-done.8, bf16[8,64,384]{2,1,0:T(8,128)(2,1)} %attend_image.1.earlier), custom_call_target="tpu_custom_call" | custom-call | tf_op jit(solution)/shard_map/unpack_text/pallas_call | solution.py:377
  95.8 1.3 %collective-permute-start.13 = (bf16[64,3072]{1,0:T(8,128)(2,1)}, bf16[64,3072]{1,0:T(8,128)(2,1)S(1)}, u32[]{:S(2)}, u32[]{:S(2)}) collective-permute-start(bf16[64,3072]{1,0:T(8,128)(2,1)} %unpack_text.1.first), channel_id=1, source_target_pairs={{8,0},{12,4},{16,24},{20,28},{9,1},{13,5},{17,25},{21,29},{10,2},{... | collective-permute-start | bytes 1179656 | tf_op jit(solution)/shard_map/ppermute | solution.py:491
  97.1 4.6 %all-to-all-done.2.x_ref = bf16[8,64,384]{2,1,0:T(8,128)(2,1)S(1)} async-done(((bf16[8,64,384]{2,1,0:T(8,128)(2,1)}), bf16[8,64,384]{2,1,0:T(8,128)(2,1)S(1)}, u32[]{:S(2)}, u32[]{:S(2)}) %all-to-all-start.2) | async-done | bytes 393248 | tf_op jit(solution)/shard_map/all_to_all | solution.py:428
  101.7 7.8 %project.1.earlier = bf16[64,3072]{1,0:T(8,128)(2,1)} custom-call(bf16[8,64,384]{2,1,0:T(8,128)(2,1)S(1)} %all-to-all-done.2.x_ref, bf16[8,384,3072]{2,1,0:T(8,128)(2,1)} %bitcast.8, bf16[64,3072]{1,0:T(8,128)(2,1)S(1)} %copy-done.6, f32[1,3072]{1,0:T(1,128)S(1)} %bitcast.7), custom_call_target="tpu_custom_call" | custom-call | flops 1207959552 | bytes 18874368 | tf_op jit(solution)/shard_map/project/pallas_call | solution.py:349
  110.3 1.9 %choose_text.1 = bf16[64,3072]{1,0:T(8,128)(2,1)} custom-call(s32[1]{0:T(128)} %bitcast.4.flag, bf16[64,3072]{1,0:T(8,128)(2,1)} %unpack_text.1.first, bf16[64,3072]{1,0:T(8,128)(2,1)} %copy-done.9, bf16[64,3072]{1,0:T(8,128)(2,1)} %project.1.earlier), custom_call_target="tpu_custom_call" | custom-call | tf_op jit(solution)/shard_map/choose_text/pallas_call | solution.py:400
  112.4 1.7 %collective-permute-done.14 = bf16[64,3072]{1,0:T(8,128)(2,1)S(1)} collective-permute-done((bf16[64,3072]{1,0:T(8,128)(2,1)}, bf16[64,3072]{1,0:T(8,128)(2,1)S(1)}, u32[]{:S(2)}, u32[]{:S(2)}) %collective-permute-start.14) | collective-permute-done | bytes 393248 | tf_op jit(solution)/shard_map/ppermute | solution.py:433
  114.1 1.1 broadcast_select_fusion.1
  115.2 0.9 pad_maximum_fusion
  (36 shorter events, 4.1 us)
Async XLA Ops:
  0.6 17.5 %collective-permute-start = (bf16[2,256,768]{2,1,0:T(8,128)(2,1)}, bf16[2,256,768]{2,1,0:T(8,128)(2,1)S(1)}, u32[]{:S(2)}, u32[]{:S(2)}) collective-permute-start(bf16[2,256,768]{2,1,0:T(8,128)(2,1)} %refs_0_.7), channel_id=1, source_target_pairs={{0,8},{8,16},{16,24},{12,4},{20,12},{28,20},{1,9},{9,17},{17,25},{... | collective-permute-start | bytes 2359304 | tf_op jit(solution)/shard_map/ppermute | solution.py:454
  2.6 20.1 %collective-permute-start.1 = (bf16[2,256,768]{2,1,0:T(8,128)(2,1)}, bf16[2,256,768]{2,1,0:T(8,128)(2,1)}, u32[]{:S(2)}, u32[]{:S(2)}) collective-permute-start(bf16[2,256,768]{2,1,0:T(8,128)(2,1)} %refs_0_.7), channel_id=1, source_target_pairs={{4,8},{12,16},{20,24},{8,4},{16,12},{24,20},{5,9},{13,17},{21,25},... | collective-permute-start | bytes 2359304 | tf_op jit(solution)/shard_map/ppermute | solution.py:454
  18.1 20.6 %collective-permute-start.3 = (bf16[2,256,768]{2,1,0:T(8,128)(2,1)S(1)}, bf16[2,256,768]{2,1,0:T(8,128)(2,1)}, u32[]{:S(2)}, u32[]{:S(2)}) collective-permute-start(bf16[2,256,768]{2,1,0:T(8,128)(2,1)S(1)} %collective-permute-done.refs_4_.refs_2_), channel_id=1, source_target_pairs={{8,16},{16,24},{12,4},{20,12},{9,17},{17,25},{13,5},{21,13},{10,18... | collective-permute-start | bytes 2359304 | tf_op jit(solution)/shard_map/ppermute | solution.py:454
  22.6 18.3 %collective-permute-start.6 = (bf16[2,256,768]{2,1,0:T(8,128)(2,1)}, bf16[2,256,768]{2,1,0:T(8,128)(2,1)}, u32[]{:S(2)}, u32[]{:S(2)}) collective-permute-start(bf16[2,256,768]{2,1,0:T(8,128)(2,1)} %collective-permute-done.1.refs_5_.refs_3_), channel_id=1, source_target_pairs={{8,16},{16,24},{12,4},{20,12},{9,17},{17,25},{13,5},{21,13},{10,18... | collective-permute-start | bytes 2359304 | tf_op jit(solution)/shard_map/ppermute | solution.py:454
  24.7 1.7 %copy-start = (bf16[128,9216]{1,0:T(8,128)(2,1)S(1)}, bf16[128,9216]{1,0:T(8,128)(2,1)}, u32[]{:S(2)}) copy-start(bf16[128,9216]{1,0:T(8,128)(2,1)} %refs_2_.2) | copy-start | bytes 7077892
  27.1 1.0 copy-start.2
  28.1 26.2 %copy-start.1 = (bf16[64,9216]{1,0:T(8,128)(2,1)S(1)}, bf16[64,9216]{1,0:T(8,128)(2,1)}, u32[]{:S(2)}) copy-start(bf16[64,9216]{1,0:T(8,128)(2,1)} %refs_2_.3) | copy-start | bytes 3538948
  28.1 26.2 %all-to-all-start = ((bf16[8,64,1152]{2,1,0:T(8,128)(2,1)}), bf16[8,64,1152]{2,1,0:T(8,128)(2,1)S(1)}, u32[]{:S(2)}, u32[]{:S(2)}) async-start(bf16[8,64,1152]{2,1,0:T(8,128)(2,1)} %copy-done.2), calls=%async_computation | async-start | bytes 2359296 | tf_op jit(solution)/shard_map/all_to_all | solution.py:428
  38.2 21.6 %collective-permute-start.2 = (bf16[2,256,768]{2,1,0:T(8,128)(2,1)}, bf16[2,256,768]{2,1,0:T(8,128)(2,1)}, u32[]{:S(2)}, u32[]{:S(2)}) collective-permute-start(bf16[2,256,768]{2,1,0:T(8,128)(2,1)} %refs_0_.7), channel_id=1, source_target_pairs={{0,4},{4,0},{8,12},{12,8},{16,20},{20,16},{24,28},{28,24},{1,5},{5... | collective-permute-start | bytes 2359304 | tf_op jit(solution)/shard_map/ppermute | solution.py:433
  38.2 22.0 %collective-permute-start.11 = (bf16[2,256,768]{2,1,0:T(8,128)(2,1)S(1)}, bf16[2,256,768]{2,1,0:T(8,128)(2,1)}, u32[]{:S(2)}, u32[]{:S(2)}) collective-permute-start(bf16[2,256,768]{2,1,0:T(8,128)(2,1)S(1)} %collective-permute-done.refs_4_.refs_2_), channel_id=1, source_target_pairs={{0,4},{4,0},{8,12},{12,8},{16,20},{20,16},{24,28},{28,24},{1,5},{5... | collective-permute-start | bytes 2359304 | tf_op jit(solution)/shard_map/ppermute | solution.py:433
  38.7 21.6 %collective-permute-start.4 = (bf16[2,256,768]{2,1,0:T(8,128)(2,1)}, bf16[2,256,768]{2,1,0:T(8,128)(2,1)}, u32[]{:S(2)}, u32[]{:S(2)}) collective-permute-start(bf16[2,256,768]{2,1,0:T(8,128)(2,1)} %collective-permute-done.3.refs_4_.refs_6_), channel_id=1, source_target_pairs={{16,24},{12,4},{17,25},{13,5},{18,26},{14,6},{19,27},{15,7}} | collective-permute-start | bytes 2359304 | tf_op jit(solution)/shard_map/ppermute | solution.py:454
  41.0 19.8 %collective-permute-start.7 = (bf16[2,256,768]{2,1,0:T(8,128)(2,1)}, bf16[2,256,768]{2,1,0:T(8,128)(2,1)}, u32[]{:S(2)}, u32[]{:S(2)}) collective-permute-start(bf16[2,256,768]{2,1,0:T(8,128)(2,1)} %collective-permute-done.6.refs_5_.refs_7_), channel_id=1, source_target_pairs={{16,24},{12,4},{17,25},{13,5},{18,26},{14,6},{19,27},{15,7}} | collective-permute-start | bytes 2359304 | tf_op jit(solution)/shard_map/ppermute | solution.py:454
  55.0 1.0 copy-start.3
  56.0 19.8 %all-to-all-start.1 = ((bf16[8,64,1152]{2,1,0:T(8,128)(2,1)}), bf16[8,64,1152]{2,1,0:T(8,128)(2,1)S(1)}, u32[]{:S(2)}, u32[]{:S(2)}) async-start(bf16[8,64,1152]{2,1,0:T(8,128)(2,1)} %copy-done.3), calls=%async_computation.1 | async-start | bytes 2359296 | tf_op jit(solution)/shard_map/all_to_all | solution.py:428
  59.7 2.6 %collective-permute-start.12 = (bf16[2,256,768]{2,1,0:T(8,128)(2,1)}, bf16[2,256,768]{2,1,0:T(8,128)(2,1)}, u32[]{:S(2)}, u32[]{:S(2)}) collective-permute-start(bf16[2,256,768]{2,1,0:T(8,128)(2,1)} %collective-permute-done.1.refs_5_.refs_3_), channel_id=1, source_target_pairs={{0,4},{4,0},{8,12},{12,8},{16,20},{20,16},{24,28},{28,24},{1,5},{5... | collective-permute-start | bytes 2359304 | tf_op jit(solution)/shard_map/ppermute | solution.py:433
  59.9 3.6 %collective-permute-start.10 = (bf16[2,256,768]{2,1,0:T(8,128)(2,1)}, bf16[2,256,768]{2,1,0:T(8,128)(2,1)}, u32[]{:S(2)}, u32[]{:S(2)}) collective-permute-start(bf16[2,256,768]{2,1,0:T(8,128)(2,1)} %collective-permute-done.6.refs_5_.refs_7_), channel_id=1, source_target_pairs={{0,4},{4,0},{8,12},{12,8},{16,20},{20,16},{24,28},{28,24},{1,5},{5... | collective-permute-start | bytes 2359304 | tf_op jit(solution)/shard_map/ppermute | solution.py:433
  60.2 4.4 %collective-permute-start.9 = (bf16[2,256,768]{2,1,0:T(8,128)(2,1)}, bf16[2,256,768]{2,1,0:T(8,128)(2,1)}, u32[]{:S(2)}, u32[]{:S(2)}) collective-permute-start(bf16[2,256,768]{2,1,0:T(8,128)(2,1)} %collective-permute-done.3.refs_4_.refs_6_), channel_id=1, source_target_pairs={{0,4},{4,0},{8,12},{12,8},{16,20},{20,16},{24,28},{28,24},{1,5},{5... | collective-permute-start | bytes 2359304 | tf_op jit(solution)/shard_map/ppermute | solution.py:433
  60.4 19.0 %collective-permute-start.5 = (bf16[2,256,768]{2,1,0:T(8,128)(2,1)}, bf16[2,256,768]{2,1,0:T(8,128)(2,1)}, u32[]{:S(2)}, u32[]{:S(2)}) collective-permute-start(bf16[2,256,768]{2,1,0:T(8,128)(2,1)} %collective-permute-done.4.refs_10_), channel_id=1, source_target_pairs={{0,4},{4,0},{8,12},{12,8},{16,20},{20,16},{24,28},{28,24},{1,5},{5... | collective-permute-start | bytes 2359304 | tf_op jit(solution)/shard_map/ppermute | solution.py:433
  60.7 18.6 %collective-permute-start.8 = (bf16[2,256,768]{2,1,0:T(8,128)(2,1)}, bf16[2,256,768]{2,1,0:T(8,128)(2,1)}, u32[]{:S(2)}, u32[]{:S(2)}) collective-permute-start(bf16[2,256,768]{2,1,0:T(8,128)(2,1)} %collective-permute-done.7.refs_11_), channel_id=1, source_target_pairs={{0,4},{4,0},{8,12},{12,8},{16,20},{20,16},{24,28},{28,24},{1,5},{5... | collective-permute-start | bytes 2359304 | tf_op jit(solution)/shard_map/ppermute | solution.py:433
  64.6 1.1 copy-start.4
  75.8 13.9 %all-to-all-start.3 = ((bf16[8,64,384]{2,1,0:T(8,128)(2,1)}), bf16[8,64,384]{2,1,0:T(8,128)(2,1)S(1)}, u32[]{:S(2)}, u32[]{:S(2)}) async-start(bf16[8,64,384]{2,1,0:T(8,128)(2,1)} %attend_text.1.refs_14_), calls=%async_computation.3 | async-start | bytes 786432 | tf_op jit(solution)/shard_map/all_to_all | solution.py:428
  79.4 1.1 copy-start.5
  89.7 12.0 %copy-start.6 = (bf16[64,3072]{1,0:T(8,128)(2,1)S(1)}, bf16[64,3072]{1,0:T(8,128)(2,1)}, u32[]{:S(2)}) copy-start(bf16[64,3072]{1,0:T(8,128)(2,1)} %residual.1) | copy-start | bytes 1179652
  89.7 12.0 %copy-start.7 = (f32[3072]{0:T(1024)S(1)}, f32[3072]{0:T(1024)}, u32[]{:S(2)}) copy-start(f32[3072]{0:T(1024)} %param.10) | copy-start | bytes 36868
  89.7 4.3 %copy-start.8 = (bf16[8,64,384]{2,1,0:T(8,128)(2,1)}, bf16[8,64,384]{2,1,0:T(8,128)(2,1)S(1)}, u32[]{:S(2)}) copy-start(bf16[8,64,384]{2,1,0:T(8,128)(2,1)S(1)} %all-to-all-done.3.x_ref) | copy-start | bytes 1179652
  89.7 12.0 %all-to-all-start.2 = ((bf16[8,64,384]{2,1,0:T(8,128)(2,1)}), bf16[8,64,384]{2,1,0:T(8,128)(2,1)S(1)}, u32[]{:S(2)}, u32[]{:S(2)}) async-start(bf16[8,64,384]{2,1,0:T(8,128)(2,1)} %attend_image.1.earlier), calls=%async_computation.2 | async-start | bytes 786432 | tf_op jit(solution)/shard_map/all_to_all | solution.py:428
  95.8 13.7 %collective-permute-start.13 = (bf16[64,3072]{1,0:T(8,128)(2,1)}, bf16[64,3072]{1,0:T(8,128)(2,1)S(1)}, u32[]{:S(2)}, u32[]{:S(2)}) collective-permute-start(bf16[64,3072]{1,0:T(8,128)(2,1)} %unpack_text.1.first), channel_id=1, source_target_pairs={{8,0},{12,4},{16,24},{20,28},{9,1},{13,5},{17,25},{21,29},{10,2},{... | collective-permute-start | bytes 1179656 | tf_op jit(solution)/shard_map/ppermute | solution.py:491
  109.5 0.7 copy-start.9
  112.2 1.9 %collective-permute-start.14 = (bf16[64,3072]{1,0:T(8,128)(2,1)}, bf16[64,3072]{1,0:T(8,128)(2,1)S(1)}, u32[]{:S(2)}, u32[]{:S(2)}) collective-permute-start(bf16[64,3072]{1,0:T(8,128)(2,1)} %choose_text.1), channel_id=1, source_target_pairs={{0,4},{4,0},{8,12},{12,8},{16,20},{20,16},{24,28},{28,24},{1,5},{5... | collective-permute-start | bytes 1179656 | tf_op jit(solution)/shard_map/ppermute | solution.py:433

commit v13 on v12

--- a/solution.py
+++ b/solution.py
@@ -13,7 +13,7 @@
 VMEM_LIMIT = 12 * 1024 * 1024
 ATTEND_LIMIT = 24 * 1024 * 1024
 WIDE_LIMIT = 48 * 1024 * 1024
-TILE = 512
+TILE = 256
 FIRST_KEYS = 256
 LARGE = 2.0**60
 
@@ -134,56 +134,49 @@
             at += blocks[0].shape[1]
 
 
-def accumulate(flag, total, aug, heads, queries_of, first_of, shared_of, own, chosen):
-    rows = total.shape[1]
-
+def accumulate(flag, total, aug, heads, queries_of, first_keys_of, own, chosen):
     def columns(head):
         return slice(head * HD, (head + 1) * HD)
 
-    def shared(head):
-        return shared_of(head) + [
+    def pieces(head, some):
+        return some(head) + [
             (chosen[index, 0, :, columns(head)], chosen[index, 1, :, columns(head)])
             for index in range(chosen.shape[0])
         ]
 
-    def largest(queries, some):
-        row_max = None
-        for key_rows, _ in some:
-            piece_max = jnp.max(dot(queries, key_rows, (1, 1)), axis=1, keepdims=True)
-            row_max = piece_max if row_max is None else jnp.maximum(row_max, piece_max)
-        return row_max
+    def tiles():
+        for head in range(heads):
+            queries = queries_of(head)
+            for span, some in own:
+                for tile in tiles_of(span.stop - span.start, TILE):
+                    tile = slice(span.start + tile.start, span.start + tile.stop)
+                    yield head, tile, queries[tile, :], some
+
+    def largest(queries, key_rows):
+        return jnp.max(dot(queries, key_rows, (1, 1)), axis=1, keepdims=True)
 
     def attempt(turn):
         @pl.when(turn == 0)
         def _():
-            for head in range(heads):
-                queries = queries_of(head)
-                for tile in tiles_of(rows, TILE):
-                    aug[head, tile, :] = reference_columns(
-                        largest(queries[tile, :], [(first_of(head), None)])
-                    )
+            for head, tile, queries, _ in tiles():
+                aug[head, tile, :] = reference_columns(largest(queries, first_keys_of(head)))
 
         @pl.when(turn == 1)
         def _():
-            for head in range(heads):
-                queries = queries_of(head)
-                for span, some in own:
-                    row_max = largest(queries[span, :], shared(head) + some(head))
-                    aug[head, span, :] = reference_columns(row_max)
-
-        for head in range(heads):
-            both = jnp.concatenate([queries_of(head), aug[head]], axis=1)
-            for tile in tiles_of(rows, TILE):
-                summed = None
-                for key_rows, values in shared(head):
-                    part = weighted(both[tile, :], with_ones(key_rows), with_ones(values))
-                    summed = part if summed is None else summed + part
-                total[head, tile, :] = summed
-            for span, some in own:
-                for key_rows, values in some(head):
-                    total[head, span, :] += weighted(
-                        both[span, :], with_ones(key_rows), with_ones(values)
-                    )
+            for head, tile, queries, some in tiles():
+                row_max = None
+                for key_rows, _ in pieces(head, some):
+                    piece_max = largest(queries, key_rows)
+                    row_max = piece_max if row_max is None else jnp.maximum(row_max, piece_max)
+                aug[head, tile, :] = reference_columns(row_max)
+
+        for head, tile, queries, some in tiles():
+            both = jnp.concatenate([queries, aug[head, tile, :]], axis=1)
+            summed = None
+            for key_rows, values in pieces(head, some):
+                part = weighted(both, with_ones(key_rows), with_ones(values))
+                summed = part if summed is None else summed + part
+            total[head, tile, :] = summed
 
     until_small(flag, total, attempt)
 
@@ -218,7 +211,7 @@
         whole.wait()
         fetch.wait()
 
-        def shared(head):
+        def own(head):
             columns = slice(head * HD, (head + 1) * HD)
             return [
                 (part_of(held_txt, 1, head, width), part_of(held_txt, 2, head, width)),
@@ -229,7 +222,7 @@
             flag, total, aug, heads,
             lambda head: part_of(held_txt, 0, head, width),
             lambda head: part_of(held_txt, 1, head, width)[: min(FIRST_KEYS, total.shape[1]), :],
-            shared, [(slice(0, total.shape[1]), lambda head: [])], chosen,
+            [(slice(0, total.shape[1]), own)], chosen,
         )
         finish(out, total)
         back = pltpu.make_async_copy(out, result, plain.at[0])
@@ -269,7 +262,10 @@
     def own(group):
         def some(head):
             columns = slice(head * HD, (head + 1) * HD)
-            return [(beside[group, 0, :, columns], beside[group, 1, :, columns])]
+            return [
+                (part_of(held_txt, 1, head, width), part_of(held_txt, 2, head, width)),
+                (beside[group, 0, :, columns], beside[group, 1, :, columns]),
+            ]
 
         return (slice(group * group_rows, (group + 1) * group_rows), some)
 
@@ -278,7 +274,6 @@
         flag, total, aug, heads,
         lambda head: part_of(held_img, 0, head, width),
         lambda head: part_of(held_txt, 1, head, width)[: min(FIRST_KEYS, text_keys), :],
-        lambda head: [(part_of(held_txt, 1, head, width), part_of(held_txt, 2, head, width))],
         [own(group) for group in range(pair)], chosen,
     )
     finish(out, total)
@@ -383,28 +378,61 @@
     )(x, earlier)
 
 
-def choose_body(flag, first, second, earlier, out):
+def after_body(*refs):
+    del refs
+
+
+def after(x, other):
+    anywhere = pl.BlockSpec(memory_space=pl.ANY)
+    return pl.pallas_call(
+        after_body,
+        in_specs=[anywhere, anywhere],
+        out_specs=anywhere,
+        out_shape=jax.ShapeDtypeStruct(x.shape, x.dtype),
+        input_output_aliases={0: 0},
+        name="after",
+    )(x, other)
+
+
+def flag_body(flag, earlier, out):
     del earlier
-
-    @pl.when(flag[0] == 1)
+    out[0] = flag[0]
+
+
+def flag_after(flag, earlier):
+    smem = pl.BlockSpec(memory_space=pltpu.SMEM)
+    return pl.pallas_call(
+        flag_body,
+        in_specs=[smem, pl.BlockSpec(memory_space=pl.ANY)],
+        out_specs=smem,
+        out_shape=jax.ShapeDtypeStruct(flag.shape, flag.dtype),
+        name="flag_after",
+    )(flag, earlier)
+
+
+def stack_body(core, mine, other, out):
+    rows = mine.shape[0]
+
+    @pl.when(core[0] == 0)
     def _():
-        out[...] = first[...]
-
-    @pl.when(flag[0] == 0)
+        out[:rows, :] = mine[...]
+        out[rows:, :] = other[...]
+
+    @pl.when(core[0] == 1)
     def _():
-        out[...] = second[...]
-
-
-def choose(flag, first, second, earlier):
+        out[:rows, :] = other[...]
+        out[rows:, :] = mine[...]
+
+
+def stack_text(core, mine, other):
     vmem = pl.BlockSpec(memory_space=pltpu.VMEM)
     return pl.pallas_call(
-        choose_body,
-        in_specs=[pl.BlockSpec(memory_space=pltpu.SMEM), vmem, vmem]
-        + [pl.BlockSpec(memory_space=pl.ANY)],
+        stack_body,
+        in_specs=[pl.BlockSpec(memory_space=pltpu.SMEM), vmem, vmem],
         out_specs=vmem,
-        out_shape=jax.ShapeDtypeStruct(first.shape, first.dtype),
-        name="choose_text",
-    )(flag, first, second, earlier)
+        out_shape=jax.ShapeDtypeStruct((2 * mine.shape[0], mine.shape[1]), mine.dtype),
+        name="stack_text",
+    )(core, mine, other)
 
 
 def per_device(img_qkv, txt_qkv, stale_kv, residual, gate_scale, proj_weight):
@@ -439,7 +467,8 @@
         return [(z + 1, z) for z in range(0, planes - step)]
 
     core_only = core.astype(jnp.int32).reshape(1)
-    txt = exchange(pack(core_only, txt_qkv, text_rows, head_owners, pair, width))
+    packed_txt = pack(core_only, txt_qkv, text_rows, head_owners, pair, width)
+    txt = exchange(packed_txt)
 
     along, against = [], []
     if pair == 2:
@@ -452,6 +481,8 @@
                 for turn in ((0, 1) if step == 1 else (0, 0))
             ]
             held = [lax.ppermute(block, "patch", way) for block, way in zip(held, pairs)]
+            if step == 1:
+                held = [after(block, packed_txt) for block in held]
             along.append(held)
             against.append([swap(block) for block in held])
         ahead = jnp.where(core == 0, plane, planes - 1 - plane)
@@ -468,7 +499,7 @@
     first_holds = [ahead >= i for i in range(1, planes)]
     zero_only = jnp.zeros((1,), jnp.int32)
     img = exchange(
-        pack(zero_only, img_qkv, img_rows, head_owners, pair, width, [txt] + along[0], 64)
+        pack(zero_only, img_qkv, img_rows, head_owners, pair, width, [txt])
     )
 
     early = planes > 2
@@ -489,14 +520,10 @@
         ends = [(1, 0), (planes - 2, planes - 1)]
         ends = [(a * pair + c, b * pair + c) for a, b in ends for c in range(pair)]
         hopped = lax.ppermute(text_out, "patch", ends)
-        text_out = choose(inner.astype(jnp.int32).reshape(1), text_out, hopped, image_out)
+        keep = flag_after(inner.astype(jnp.int32).reshape(1), image_out)
+        text_out = jnp.where(keep[0] == 1, text_out, hopped)
     if pair == 2:
-        other = swap(text_out)
-        lower = core == 0
-        text_out = jnp.concatenate(
-            [jnp.where(lower, text_out, other), jnp.where(lower, other, text_out)], 0
-        )
-
+        text_out = stack_text(core_only, text_out, swap(text_out))
     return (image_out, text_out)
 
 

time: 117 us -> 115 us (0.983)
  waiting for transfers between devices: 35.3 us -> 31.1 us
  Pallas kernels: 30.6 us -> 33 us
  starting transfers between devices: 40.6 us -> 43 us
  other arithmetic: 1.98 us -> 0.04 us
  local copies, waits for them, and re-layouts: 6.81 us -> 5.35 us
    ppermute x6, waiting for transfers between devices: 12.8 us -> 9.28 us  [per_device(): lax.ppermute(block, 'patch', way)]
    pallas_call x2, Pallas kernels: 1.33 us -> 3.57 us  [pack(): pl.pallas_call(pack_body, grid_spec=pltpu.PrefetchScalarGridSpec(num_scal...]
    all_to_all x4, starting transfers between devices: 21.8 us -> 24 us  [exchange(): lax.all_to_all(x, ('patch', 'head'), split_axis=0, concat_axis=0, axis_in...]
    unnamed x20 -> x26, local copies, waits for them, and re-layouts: 6.73 us -> 5.27 us
    pallas_call x1 -> x4, Pallas kernels: 1.91 us -> 2.57 us  [the longest x1 2.04 us: stack_text(): pl.pallas_call(stack_body, in_specs=[pl.BlockSpec(memory_space=pltpu.SMEM...]
  transfers between devices with their start and end apart: 19 -> 19, of which waited for: 9 -> 10; matrix products, arithmetic and copies ran while one was open for 0% -> 0% of each run, Pallas kernels for 25% -> 27%
where the time goes in v13:
time: 115 us; the launch traced here: 114 us
  starting transfers between devices  43 us (37%)
  Pallas kernels  33 us (29%)
  waiting for transfers between devices  31.1 us (27%)
  local copies, waits for them, and re-layouts  5.35 us (5%)
  between operations  1.48 us (1%)
    all_to_all x4, starting transfers between devices, exchange(): lax.all_to_all(x, ('patch', 'head'), split_axis=0, concat_axis=0, axis_in...  24 us
    pallas_call x2, Pallas kernels, attend(): pl.pallas_call(functools.partial(body, len(stale), counts), in_specs=[pl....  17.3 us
    all_to_all x4, waiting for transfers between devices, exchange(): lax.all_to_all(x, ('patch', 'head'), split_axis=0, concat_axis=0, axis_in...  16.7 us
    ppermute x6, starting transfers between devices, per_device(): lax.ppermute(block, 'patch', way)  15.7 us
    ppermute x6, waiting for transfers between devices, per_device(): lax.ppermute(block, 'patch', way)  9.28 us
    pallas_call x1, Pallas kernels, project(): pl.pallas_call(functools.partial(project_body, order), in_specs=[vmem, pl...  7.85 us
    unnamed x26, local copies, waits for them, and re-layouts  5.27 us
    ppermute x8, waiting for transfers between devices, swap(): return lax.ppermute(x, 'patch', swap_pairs)  5.09 us
  transfers between devices with their start and end apart: 19, of which 10 were waited for; matrix products, arithmetic and copies ran while one was open for 0% of the time, Pallas kernels for 27%

profile of v13, /device:TPU:9, one launch (start us, length us, event | category | flops | bytes accessed | tf_op | source)
XLA Modules:
  0.0 114.0 jit_solution(9252315655829182700)
XLA Ops:
  0.6 1.9 %collective-permute-start.1 = (bf16[2,256,768]{2,1,0:T(8,128)(2,1)}, bf16[2,256,768]{2,1,0:T(8,128)(2,1)S(1)}, u32[]{:S(2)}, u32[]{:S(2)}) collective-permute-start(bf16[2,256,768]{2,1,0:T(8,128)(2,1)} %refs_0_.7), channel_id=1, source_target_pairs={{0,8},{8,16},{16,24},{12,4},{20,12},{28,20},{1,9},{9,17},{17,25},{... | collective-permute-start | bytes 2359304 | tf_op jit(solution)/shard_map/ppermute | solution.py:483
  2.6 5.3 %collective-permute-start.2 = (bf16[2,256,768]{2,1,0:T(8,128)(2,1)}, bf16[2,256,768]{2,1,0:T(8,128)(2,1)S(1)}, u32[]{:S(2)}, u32[]{:S(2)}) collective-permute-start(bf16[2,256,768]{2,1,0:T(8,128)(2,1)} %refs_0_.7), channel_id=1, source_target_pairs={{4,8},{12,16},{20,24},{8,4},{16,12},{24,20},{5,9},{13,17},{21,25},... | collective-permute-start | bytes 2359304 | tf_op jit(solution)/shard_map/ppermute | solution.py:483
  7.9 1.7 %copy-done = bf16[128,9216]{1,0:T(8,128)(2,1)S(1)} copy-done((bf16[128,9216]{1,0:T(8,128)(2,1)S(1)}, bf16[128,9216]{1,0:T(8,128)(2,1)}, u32[]{:S(2)}) %copy-start) | copy-done | bytes 2359320
  9.6 2.9 %pack_heads.2.refs_1_ = bf16[8,64,1152]{2,1,0:T(8,128)(2,1)} custom-call(s32[1]{0:T(128)} %bitcast._.core, bf16[128,9216]{1,0:T(8,128)(2,1)S(1)} %copy-done, bf16[128,9216]{1,0:T(8,128)(2,1)S(1)} %copy-done, bf16[128,9216]{1,0:T(8,128)(2,1)S(1)} %copy-done), custom_call_target="tpu_custom_call" | custom-call | bytes 2359296 | tf_op jit(solution)/shard_map/pack_heads/pallas_call | solution.py:44
  12.5 5.6 %collective-permute-done.1.refs_0_ = bf16[2,256,768]{2,1,0:T(8,128)(2,1)S(1)} collective-permute-done((bf16[2,256,768]{2,1,0:T(8,128)(2,1)}, bf16[2,256,768]{2,1,0:T(8,128)(2,1)S(1)}, u32[]{:S(2)}, u32[]{:S(2)}) %collective-permute-start.1) | collective-permute-done | bytes 786464 | tf_op jit(solution)/shard_map/ppermute | solution.py:483
  18.0 0.9 copy-done.4
  18.9 1.9 %collective-permute-start.3 = (bf16[2,256,768]{2,1,0:T(8,128)(2,1)}, bf16[2,256,768]{2,1,0:T(8,128)(2,1)}, u32[]{:S(2)}, u32[]{:S(2)}) collective-permute-start(bf16[2,256,768]{2,1,0:T(8,128)(2,1)} %after.2.refs_2_), channel_id=1, source_target_pairs={{8,16},{16,24},{12,4},{20,12},{9,17},{17,25},{13,5},{21,13},{10,18... | collective-permute-start | bytes 2359304 | tf_op jit(solution)/shard_map/ppermute | solution.py:483
  20.8 1.8 %collective-permute-done.2.refs_0_ = bf16[2,256,768]{2,1,0:T(8,128)(2,1)S(1)} collective-permute-done((bf16[2,256,768]{2,1,0:T(8,128)(2,1)}, bf16[2,256,768]{2,1,0:T(8,128)(2,1)S(1)}, u32[]{:S(2)}, u32[]{:S(2)}) %collective-permute-start.2) | collective-permute-done | bytes 786464 | tf_op jit(solution)/shard_map/ppermute | solution.py:483
  22.6 0.9 copy-done.2
  23.6 2.2 %collective-permute-start.6 = (bf16[2,256,768]{2,1,0:T(8,128)(2,1)}, bf16[2,256,768]{2,1,0:T(8,128)(2,1)}, u32[]{:S(2)}, u32[]{:S(2)}) collective-permute-start(bf16[2,256,768]{2,1,0:T(8,128)(2,1)} %after.3.refs_3_), channel_id=1, source_target_pairs={{8,16},{16,24},{12,4},{20,12},{9,17},{17,25},{13,5},{21,13},{10,18... | collective-permute-start | bytes 2359304 | tf_op jit(solution)/shard_map/ppermute | solution.py:483
  25.8 10.9 %all-to-all-start = ((bf16[8,64,1152]{2,1,0:T(8,128)(2,1)}), bf16[8,64,1152]{2,1,0:T(8,128)(2,1)S(1)}, u32[]{:S(2)}, u32[]{:S(2)}) async-start(bf16[8,64,1152]{2,1,0:T(8,128)(2,1)} %pack_heads.2.refs_1_), calls=%async_computation | async-start | bytes 2359296 | tf_op jit(solution)/shard_map/all_to_all | solution.py:456
  37.2 2.2 %collective-permute-start.4 = (bf16[2,256,768]{2,1,0:T(8,128)(2,1)}, bf16[2,256,768]{2,1,0:T(8,128)(2,1)}, u32[]{:S(2)}, u32[]{:S(2)}) collective-permute-start(bf16[2,256,768]{2,1,0:T(8,128)(2,1)} %collective-permute-done.3.refs_4_.refs_6_), channel_id=1, source_target_pairs={{16,24},{12,4},{17,25},{13,5},{18,26},{14,6},{19,27},{15,7}} | collective-permute-start | bytes 2359304 | tf_op jit(solution)/shard_map/ppermute | solution.py:483
  39.4 1.9 %collective-permute-done.6.refs_5_.refs_7_ = bf16[2,256,768]{2,1,0:T(8,128)(2,1)} collective-permute-done((bf16[2,256,768]{2,1,0:T(8,128)(2,1)}, bf16[2,256,768]{2,1,0:T(8,128)(2,1)}, u32[]{:S(2)}, u32[]{:S(2)}) %collective-permute-start.6) | collective-permute-done | bytes 786464 | tf_op jit(solution)/shard_map/ppermute | solution.py:483
  41.3 2.2 %collective-permute-start.7 = (bf16[2,256,768]{2,1,0:T(8,128)(2,1)}, bf16[2,256,768]{2,1,0:T(8,128)(2,1)}, u32[]{:S(2)}, u32[]{:S(2)}) collective-permute-start(bf16[2,256,768]{2,1,0:T(8,128)(2,1)} %collective-permute-done.6.refs_5_.refs_7_), channel_id=1, source_target_pairs={{16,24},{12,4},{17,25},{13,5},{18,26},{14,6},{19,27},{15,7}} | collective-permute-start | bytes 2359304 | tf_op jit(solution)/shard_map/ppermute | solution.py:483
  43.5 9.3 %all-to-all-done.refs_3_.txt = bf16[8,64,1152]{2,1,0:T(8,128)(2,1)S(1)} async-done(((bf16[8,64,1152]{2,1,0:T(8,128)(2,1)}), bf16[8,64,1152]{2,1,0:T(8,128)(2,1)S(1)}, u32[]{:S(2)}, u32[]{:S(2)}) %all-to-all-start) | async-done | bytes 1179680 | tf_op jit(solution)/shard_map/all_to_all | solution.py:456
  53.5 1.0 copy-done.6
  54.5 4.5 %all-to-all-start.1 = ((bf16[8,64,1152]{2,1,0:T(8,128)(2,1)}), bf16[8,64,1152]{2,1,0:T(8,128)(2,1)}, u32[]{:S(2)}, u32[]{:S(2)}) async-start(bf16[8,64,1152]{2,1,0:T(8,128)(2,1)} %copy-done.6), calls=%async_computation.1 | async-start | bytes 2359296 | tf_op jit(solution)/shard_map/all_to_all | solution.py:456
  60.3 1.1 collective-permute-done.12.refs_9_.refs_13_
  61.4 1.3 %collective-permute-done.9.refs_6_.refs_8_ = bf16[2,256,768]{2,1,0:T(8,128)(2,1)} collective-permute-done((bf16[2,256,768]{2,1,0:T(8,128)(2,1)}, bf16[2,256,768]{2,1,0:T(8,128)(2,1)}, u32[]{:S(2)}, u32[]{:S(2)}) %collective-permute-start.9) | collective-permute-done | bytes 786464 | tf_op jit(solution)/shard_map/ppermute | solution.py:461
  62.7 1.1 collective-permute-done.10.refs_7_.refs_9_
  63.9 8.4 %attend_text.1.refs_14_ = bf16[8,64,384]{2,1,0:T(8,128)(2,1)} custom-call(s32[5]{0:T(128)S(1)} %stack.38.info, bf16[8,64,1152]{2,1,0:T(8,128)(2,1)S(1)} %all-to-all-done.refs_3_.txt, bf16[2,256,768]{2,1,0:T(8,128)(2,1)S(1)} %copy-done.7, bf16[2,256,768]{2,1,0:T(8,128)(2,1)} %collective-permute-done.refs_1_, bf16[2,256,768]{2,1,0:T(8,128)(2,1)S(1)} %copy-done.5, ...), custom_call_target="tpu_custom_call" | custom-call | flops 2013265920 | bytes 3932160 | tf_op jit(solution)/shard_map/attend_text/pallas_call | solution.py:302
  72.3 2.9 %all-to-all-done.1.img = bf16[8,64,1152]{2,1,0:T(8,128)(2,1)} async-done(((bf16[8,64,1152]{2,1,0:T(8,128)(2,1)}), bf16[8,64,1152]{2,1,0:T(8,128)(2,1)}, u32[]{:S(2)}, u32[]{:S(2)}) %all-to-all-start.1) | async-done | bytes 1179680 | tf_op jit(solution)/shard_map/all_to_all | solution.py:456
  75.2 4.2 %all-to-all-start.3 = ((bf16[8,64,384]{2,1,0:T(8,128)(2,1)}), bf16[8,64,384]{2,1,0:T(8,128)(2,1)}, u32[]{:S(2)}, u32[]{:S(2)}) async-start(bf16[8,64,384]{2,1,0:T(8,128)(2,1)} %attend_text.1.refs_14_), calls=%async_computation.3 | async-start | bytes 786432 | tf_op jit(solution)/shard_map/all_to_all | solution.py:456
  79.4 8.8 %attend_image.1.earlier = bf16[8,64,384]{2,1,0:T(8,128)(2,1)} custom-call(s32[5]{0:T(128)S(1)} %stack.38.info, bf16[8,64,1152]{2,1,0:T(8,128)(2,1)} %all-to-all-done.1.img, bf16[8,64,1152]{2,1,0:T(8,128)(2,1)S(1)} %all-to-all-done.refs_3_.txt, bf16[2,256,768]{2,1,0:T(8,128)(2,1)S(1)} %copy-done.7, bf16[2,256,768]{2,1,0:T(8,128)(2,1)} %collective-permute-done.refs_1_, ...), custom_call_target="tpu_custom_call" | custom-call | flops 2013265920 | bytes 3932160 | tf_op jit(solution)/shard_map/attend_image/pallas_call | solution.py:302
  88.3 4.3 %all-to-all-start.2 = ((bf16[8,64,384]{2,1,0:T(8,128)(2,1)}), bf16[8,64,384]{2,1,0:T(8,128)(2,1)S(1)}, u32[]{:S(2)}, u32[]{:S(2)}) async-start(bf16[8,64,384]{2,1,0:T(8,128)(2,1)} %attend_image.1.earlier), calls=%async_computation.2 | async-start | bytes 786432 | tf_op jit(solution)/shard_map/all_to_all | solution.py:456
  92.6 1.8 %unpack_text.1 = bf16[64,3072]{1,0:T(8,128)(2,1)} custom-call(bf16[8,64,384]{2,1,0:T(8,128)(2,1)} %all-to-all-done.3.x_ref, bf16[8,64,384]{2,1,0:T(8,128)(2,1)} %attend_image.1.earlier), custom_call_target="tpu_custom_call" | custom-call | tf_op jit(solution)/shard_map/unpack_text/pallas_call | solution.py:372
  94.4 1.3 %collective-permute-start.13 = (bf16[64,3072]{1,0:T(8,128)(2,1)}, bf16[64,3072]{1,0:T(8,128)(2,1)S(1)}, u32[]{:S(2)}, u32[]{:S(2)}) collective-permute-start(bf16[64,3072]{1,0:T(8,128)(2,1)} %unpack_text.1), channel_id=1, source_target_pairs={{8,0},{12,4},{16,24},{20,28},{9,1},{13,5},{17,25},{21,29},{10,2},{... | collective-permute-start | bytes 1179656 | tf_op jit(solution)/shard_map/ppermute | solution.py:522
  95.7 4.6 %all-to-all-done.2.x_ref = bf16[8,64,384]{2,1,0:T(8,128)(2,1)S(1)} async-done(((bf16[8,64,384]{2,1,0:T(8,128)(2,1)}), bf16[8,64,384]{2,1,0:T(8,128)(2,1)S(1)}, u32[]{:S(2)}, u32[]{:S(2)}) %all-to-all-start.2) | async-done | bytes 393248 | tf_op jit(solution)/shard_map/all_to_all | solution.py:456
  100.3 7.8 %project.1.earlier = bf16[64,3072]{1,0:T(8,128)(2,1)} custom-call(bf16[8,64,384]{2,1,0:T(8,128)(2,1)S(1)} %all-to-all-done.2.x_ref, bf16[8,384,3072]{2,1,0:T(8,128)(2,1)} %bitcast.9, bf16[64,3072]{1,0:T(8,128)(2,1)S(1)} %copy-done.8, f32[1,3072]{1,0:T(1,128)S(1)} %bitcast.8), custom_call_target="tpu_custom_call" | custom-call | flops 1207959552 | bytes 18874368 | tf_op jit(solution)/shard_map/project/pallas_call | solution.py:344
  109.7 1.5 %collective-permute-done.14.other = bf16[64,3072]{1,0:T(8,128)(2,1)S(1)} collective-permute-done((bf16[64,3072]{1,0:T(8,128)(2,1)S(1)}, bf16[64,3072]{1,0:T(8,128)(2,1)S(1)}, u32[]{:S(2)}, u32[]{:S(2)}) %collective-permute-start.14) | collective-permute-done | bytes 393248 | tf_op jit(solution)/shard_map/ppermute | solution.py:461
  111.2 0.8 copy-done.12
  111.9 2.0 %stack_text.1 = bf16[128,3072]{1,0:T(8,128)(2,1)} custom-call(s32[1]{0:T(128)} %bitcast._.core, bf16[64,3072]{1,0:T(8,128)(2,1)} %copy-done.11, bf16[64,3072]{1,0:T(8,128)(2,1)} %copy-done.12), custom_call_target="tpu_custom_call" | custom-call | tf_op jit(solution)/shard_map/stack_text/pallas_call | solution.py:429
  (44 shorter events, 3.4 us)
Async XLA Ops:
  0.6 17.4 %collective-permute-start.1 = (bf16[2,256,768]{2,1,0:T(8,128)(2,1)}, bf16[2,256,768]{2,1,0:T(8,128)(2,1)S(1)}, u32[]{:S(2)}, u32[]{:S(2)}) collective-permute-start(bf16[2,256,768]{2,1,0:T(8,128)(2,1)} %refs_0_.7), channel_id=1, source_target_pairs={{0,8},{8,16},{16,24},{12,4},{20,12},{28,20},{1,9},{9,17},{17,25},{... | collective-permute-start | bytes 2359304 | tf_op jit(solution)/shard_map/ppermute | solution.py:483
  2.6 20.1 %collective-permute-start.2 = (bf16[2,256,768]{2,1,0:T(8,128)(2,1)}, bf16[2,256,768]{2,1,0:T(8,128)(2,1)S(1)}, u32[]{:S(2)}, u32[]{:S(2)}) collective-permute-start(bf16[2,256,768]{2,1,0:T(8,128)(2,1)} %refs_0_.7), channel_id=1, source_target_pairs={{4,8},{12,16},{20,24},{8,4},{16,12},{24,20},{5,9},{13,17},{21,25},... | collective-permute-start | bytes 2359304 | tf_op jit(solution)/shard_map/ppermute | solution.py:483
  7.9 1.7 %copy-start = (bf16[128,9216]{1,0:T(8,128)(2,1)S(1)}, bf16[128,9216]{1,0:T(8,128)(2,1)}, u32[]{:S(2)}) copy-start(bf16[128,9216]{1,0:T(8,128)(2,1)} %refs_2_.2) | copy-start | bytes 7077892
  18.0 0.9 copy-start.4
  18.9 18.3 %collective-permute-start.3 = (bf16[2,256,768]{2,1,0:T(8,128)(2,1)}, bf16[2,256,768]{2,1,0:T(8,128)(2,1)}, u32[]{:S(2)}, u32[]{:S(2)}) collective-permute-start(bf16[2,256,768]{2,1,0:T(8,128)(2,1)} %after.2.refs_2_), channel_id=1, source_target_pairs={{8,16},{16,24},{12,4},{20,12},{9,17},{17,25},{13,5},{21,13},{10,18... | collective-permute-start | bytes 2359304 | tf_op jit(solution)/shard_map/ppermute | solution.py:483
  22.6 0.9 copy-start.2
  23.6 13.1 %copy-start.5 = (bf16[2,256,768]{2,1,0:T(8,128)(2,1)S(1)}, bf16[2,256,768]{2,1,0:T(8,128)(2,1)}, u32[]{:S(2)}) copy-start(bf16[2,256,768]{2,1,0:T(8,128)(2,1)} %after.2.refs_2_) | copy-start | bytes 2359300
  23.6 29.2 %copy-start.1 = (bf16[64,9216]{1,0:T(8,128)(2,1)S(1)}, bf16[64,9216]{1,0:T(8,128)(2,1)}, u32[]{:S(2)}) copy-start(bf16[64,9216]{1,0:T(8,128)(2,1)} %refs_2_.3) | copy-start | bytes 3538948
  23.6 17.8 %collective-permute-start.6 = (bf16[2,256,768]{2,1,0:T(8,128)(2,1)}, bf16[2,256,768]{2,1,0:T(8,128)(2,1)}, u32[]{:S(2)}, u32[]{:S(2)}) collective-permute-start(bf16[2,256,768]{2,1,0:T(8,128)(2,1)} %after.3.refs_3_), channel_id=1, source_target_pairs={{8,16},{16,24},{12,4},{20,12},{9,17},{17,25},{13,5},{21,13},{10,18... | collective-permute-start | bytes 2359304 | tf_op jit(solution)/shard_map/ppermute | solution.py:483
  25.8 27.0 %all-to-all-start = ((bf16[8,64,1152]{2,1,0:T(8,128)(2,1)}), bf16[8,64,1152]{2,1,0:T(8,128)(2,1)S(1)}, u32[]{:S(2)}, u32[]{:S(2)}) async-start(bf16[8,64,1152]{2,1,0:T(8,128)(2,1)} %pack_heads.2.refs_1_), calls=%async_computation | async-start | bytes 2359296 | tf_op jit(solution)/shard_map/all_to_all | solution.py:456
  36.7 22.5 %collective-permute-start = (bf16[2,256,768]{2,1,0:T(8,128)(2,1)}, bf16[2,256,768]{2,1,0:T(8,128)(2,1)}, u32[]{:S(2)}, u32[]{:S(2)}) collective-permute-start(bf16[2,256,768]{2,1,0:T(8,128)(2,1)} %refs_0_.7), channel_id=1, source_target_pairs={{0,4},{4,0},{8,12},{12,8},{16,20},{20,16},{24,28},{28,24},{1,5},{5... | collective-permute-start | bytes 2359304 | tf_op jit(solution)/shard_map/ppermute | solution.py:461
  36.7 22.8 %collective-permute-start.11 = (bf16[2,256,768]{2,1,0:T(8,128)(2,1)S(1)}, bf16[2,256,768]{2,1,0:T(8,128)(2,1)}, u32[]{:S(2)}, u32[]{:S(2)}) collective-permute-start(bf16[2,256,768]{2,1,0:T(8,128)(2,1)S(1)} %copy-done.5), channel_id=1, source_target_pairs={{0,4},{4,0},{8,12},{12,8},{16,20},{20,16},{24,28},{28,24},{1,5},{5... | collective-permute-start | bytes 2359304 | tf_op jit(solution)/shard_map/ppermute | solution.py:461
  37.2 22.5 %collective-permute-start.4 = (bf16[2,256,768]{2,1,0:T(8,128)(2,1)}, bf16[2,256,768]{2,1,0:T(8,128)(2,1)}, u32[]{:S(2)}, u32[]{:S(2)}) collective-permute-start(bf16[2,256,768]{2,1,0:T(8,128)(2,1)} %collective-permute-done.3.refs_4_.refs_6_), channel_id=1, source_target_pairs={{16,24},{12,4},{17,25},{13,5},{18,26},{14,6},{19,27},{15,7}} | collective-permute-start | bytes 2359304 | tf_op jit(solution)/shard_map/ppermute | solution.py:483
  41.3 18.7 %collective-permute-start.7 = (bf16[2,256,768]{2,1,0:T(8,128)(2,1)}, bf16[2,256,768]{2,1,0:T(8,128)(2,1)}, u32[]{:S(2)}, u32[]{:S(2)}) collective-permute-start(bf16[2,256,768]{2,1,0:T(8,128)(2,1)} %collective-permute-done.6.refs_5_.refs_7_), channel_id=1, source_target_pairs={{16,24},{12,4},{17,25},{13,5},{18,26},{14,6},{19,27},{15,7}} | collective-permute-start | bytes 2359304 | tf_op jit(solution)/shard_map/ppermute | solution.py:483
  53.5 1.0 copy-start.6
  54.5 4.5 %copy-start.3 = (bf16[2,256,768]{2,1,0:T(8,128)(2,1)S(1)}, bf16[2,256,768]{2,1,0:T(8,128)(2,1)}, u32[]{:S(2)}) copy-start(bf16[2,256,768]{2,1,0:T(8,128)(2,1)} %after.3.refs_3_) | copy-start | bytes 2359300
  54.5 9.4 %copy-start.7 = (bf16[2,256,768]{2,1,0:T(8,128)(2,1)S(1)}, bf16[2,256,768]{2,1,0:T(8,128)(2,1)}, u32[]{:S(2)}) copy-start(bf16[2,256,768]{2,1,0:T(8,128)(2,1)} %refs_0_.7) | copy-start | bytes 2359300
  54.5 20.7 %all-to-all-start.1 = ((bf16[8,64,1152]{2,1,0:T(8,128)(2,1)}), bf16[8,64,1152]{2,1,0:T(8,128)(2,1)}, u32[]{:S(2)}, u32[]{:S(2)}) async-start(bf16[8,64,1152]{2,1,0:T(8,128)(2,1)} %copy-done.6), calls=%async_computation.1 | async-start | bytes 2359296 | tf_op jit(solution)/shard_map/all_to_all | solution.py:456
  59.0 2.4 %collective-permute-start.12 = (bf16[2,256,768]{2,1,0:T(8,128)(2,1)S(1)}, bf16[2,256,768]{2,1,0:T(8,128)(2,1)}, u32[]{:S(2)}, u32[]{:S(2)}) collective-permute-start(bf16[2,256,768]{2,1,0:T(8,128)(2,1)S(1)} %copy-done.3), channel_id=1, source_target_pairs={{0,4},{4,0},{8,12},{12,8},{16,20},{20,16},{24,28},{28,24},{1,5},{5... | collective-permute-start | bytes 2359304 | tf_op jit(solution)/shard_map/ppermute | solution.py:461
  59.2 3.6 %collective-permute-start.9 = (bf16[2,256,768]{2,1,0:T(8,128)(2,1)}, bf16[2,256,768]{2,1,0:T(8,128)(2,1)}, u32[]{:S(2)}, u32[]{:S(2)}) collective-permute-start(bf16[2,256,768]{2,1,0:T(8,128)(2,1)} %collective-permute-done.3.refs_4_.refs_6_), channel_id=1, source_target_pairs={{0,4},{4,0},{8,12},{12,8},{16,20},{20,16},{24,28},{28,24},{1,5},{5... | collective-permute-start | bytes 2359304 | tf_op jit(solution)/shard_map/ppermute | solution.py:461
  59.5 4.4 %collective-permute-start.10 = (bf16[2,256,768]{2,1,0:T(8,128)(2,1)}, bf16[2,256,768]{2,1,0:T(8,128)(2,1)}, u32[]{:S(2)}, u32[]{:S(2)}) collective-permute-start(bf16[2,256,768]{2,1,0:T(8,128)(2,1)} %collective-permute-done.6.refs_5_.refs_7_), channel_id=1, source_target_pairs={{0,4},{4,0},{8,12},{12,8},{16,20},{20,16},{24,28},{28,24},{1,5},{5... | collective-permute-start | bytes 2359304 | tf_op jit(solution)/shard_map/ppermute | solution.py:461
  59.7 19.7 %collective-permute-start.5 = (bf16[2,256,768]{2,1,0:T(8,128)(2,1)}, bf16[2,256,768]{2,1,0:T(8,128)(2,1)}, u32[]{:S(2)}, u32[]{:S(2)}) collective-permute-start(bf16[2,256,768]{2,1,0:T(8,128)(2,1)} %collective-permute-done.4.refs_10_), channel_id=1, source_target_pairs={{0,4},{4,0},{8,12},{12,8},{16,20},{20,16},{24,28},{28,24},{1,5},{5... | collective-permute-start | bytes 2359304 | tf_op jit(solution)/shard_map/ppermute | solution.py:461
  60.0 19.4 %collective-permute-start.8 = (bf16[2,256,768]{2,1,0:T(8,128)(2,1)}, bf16[2,256,768]{2,1,0:T(8,128)(2,1)}, u32[]{:S(2)}, u32[]{:S(2)}) collective-permute-start(bf16[2,256,768]{2,1,0:T(8,128)(2,1)} %collective-permute-done.7.refs_11_), channel_id=1, source_target_pairs={{0,4},{4,0},{8,12},{12,8},{16,20},{20,16},{24,28},{28,24},{1,5},{5... | collective-permute-start | bytes 2359304 | tf_op jit(solution)/shard_map/ppermute | solution.py:461
  75.2 13.1 %all-to-all-start.3 = ((bf16[8,64,384]{2,1,0:T(8,128)(2,1)}), bf16[8,64,384]{2,1,0:T(8,128)(2,1)}, u32[]{:S(2)}, u32[]{:S(2)}) async-start(bf16[8,64,384]{2,1,0:T(8,128)(2,1)} %attend_text.1.refs_14_), calls=%async_computation.3 | async-start | bytes 786432 | tf_op jit(solution)/shard_map/all_to_all | solution.py:456
  88.2 12.0 %copy-start.8 = (bf16[64,3072]{1,0:T(8,128)(2,1)S(1)}, bf16[64,3072]{1,0:T(8,128)(2,1)}, u32[]{:S(2)}) copy-start(bf16[64,3072]{1,0:T(8,128)(2,1)} %residual.1) | copy-start | bytes 1179652
  88.2 12.0 %copy-start.9 = (f32[3072]{0:T(1024)S(1)}, f32[3072]{0:T(1024)}, u32[]{:S(2)}) copy-start(f32[3072]{0:T(1024)} %param.10) | copy-start | bytes 36868
  88.3 12.0 %all-to-all-start.2 = ((bf16[8,64,384]{2,1,0:T(8,128)(2,1)}), bf16[8,64,384]{2,1,0:T(8,128)(2,1)S(1)}, u32[]{:S(2)}, u32[]{:S(2)}) async-start(bf16[8,64,384]{2,1,0:T(8,128)(2,1)} %attend_image.1.earlier), calls=%async_computation.2 | async-start | bytes 786432 | tf_op jit(solution)/shard_map/all_to_all | solution.py:456
  94.4 14.9 %collective-permute-start.13 = (bf16[64,3072]{1,0:T(8,128)(2,1)}, bf16[64,3072]{1,0:T(8,128)(2,1)S(1)}, u32[]{:S(2)}, u32[]{:S(2)}) collective-permute-start(bf16[64,3072]{1,0:T(8,128)(2,1)} %unpack_text.1), channel_id=1, source_target_pairs={{8,0},{12,4},{16,24},{20,28},{9,1},{13,5},{17,25},{21,29},{10,2},{... | collective-permute-start | bytes 1179656 | tf_op jit(solution)/shard_map/ppermute | solution.py:522
  100.3 9.0 %copy-start.10 = (bf16[64,3072]{1,0:T(8,128)(2,1)S(1)}, bf16[64,3072]{1,0:T(8,128)(2,1)}, u32[]{:S(2)}) copy-start(bf16[64,3072]{1,0:T(8,128)(2,1)} %unpack_text.1) | copy-start | bytes 1179652
  109.4 1.8 %copy-start.11 = (bf16[64,3072]{1,0:T(8,128)(2,1)}, bf16[64,3072]{1,0:T(8,128)(2,1)S(1)}, u32[]{:S(2)}) copy-start(bf16[64,3072]{1,0:T(8,128)(2,1)S(1)} %broadcast_select_fusion.mine) | copy-start | bytes 1179652
  109.4 1.8 %collective-permute-start.14 = (bf16[64,3072]{1,0:T(8,128)(2,1)S(1)}, bf16[64,3072]{1,0:T(8,128)(2,1)S(1)}, u32[]{:S(2)}, u32[]{:S(2)}) collective-permute-start(bf16[64,3072]{1,0:T(8,128)(2,1)S(1)} %broadcast_select_fusion.mine), channel_id=1, source_target_pairs={{0,4},{4,0},{8,12},{12,8},{16,20},{20,16},{24,28},{28,24},{1,5},{5... | collective-permute-start | bytes 1179656 | tf_op jit(solution)/shard_map/ppermute | solution.py:461
  111.2 0.8 copy-start.12

commit v14 on v13

--- a/solution.py
+++ b/solution.py
@@ -134,7 +134,7 @@
             at += blocks[0].shape[1]
 
 
-def accumulate(flag, total, aug, heads, queries_of, first_keys_of, own, chosen):
+def accumulate(flag, total, aug, heads, queries_of, first_keys_of, own, chosen, ready):
     def columns(head):
         return slice(head * HD, (head + 1) * HD)
 
@@ -160,6 +160,7 @@
         def _():
             for head, tile, queries, _ in tiles():
                 aug[head, tile, :] = reference_columns(largest(queries, first_keys_of(head)))
+            ready()
 
         @pl.when(turn == 1)
         def _():
@@ -209,7 +210,6 @@
             at += block.shape[1]
         settle(fetch, came, entries, chosen)
         whole.wait()
-        fetch.wait()
 
         def own(head):
             columns = slice(head * HD, (head + 1) * HD)
@@ -222,7 +222,7 @@
             flag, total, aug, heads,
             lambda head: part_of(held_txt, 0, head, width),
             lambda head: part_of(held_txt, 1, head, width)[: min(FIRST_KEYS, total.shape[1]), :],
-            [(slice(0, total.shape[1]), own)], chosen,
+            [(slice(0, total.shape[1]), own)], chosen, fetch.wait,
         )
         finish(out, total)
         back = pltpu.make_async_copy(out, result, plain.at[0])
@@ -257,7 +257,6 @@
                 group * sources : (group + 1) * sources, :, (1 + part) * width : (2 + part) * width
             ]
             beside[group, part, :group_rows, :] = fresh.reshape(group_rows, width)
-    fetch.wait()
 
     def own(group):
         def some(head):
@@ -274,7 +273,7 @@
         flag, total, aug, heads,
         lambda head: part_of(held_img, 0, head, width),
         lambda head: part_of(held_txt, 1, head, width)[: min(FIRST_KEYS, text_keys), :],
-        [own(group) for group in range(pair)], chosen,
+        [own(group) for group in range(pair)], chosen, fetch.wait,
     )
     finish(out, total)
     back = pltpu.make_async_copy(out, result, plain.at[0])
@@ -410,31 +409,6 @@
     )(flag, earlier)
 
 
-def stack_body(core, mine, other, out):
-    rows = mine.shape[0]
-
-    @pl.when(core[0] == 0)
-    def _():
-        out[:rows, :] = mine[...]
-        out[rows:, :] = other[...]
-
-    @pl.when(core[0] == 1)
-    def _():
-        out[:rows, :] = other[...]
-        out[rows:, :] = mine[...]
-
-
-def stack_text(core, mine, other):
-    vmem = pl.BlockSpec(memory_space=pltpu.VMEM)
-    return pl.pallas_call(
-        stack_body,
-        in_specs=[pl.BlockSpec(memory_space=pltpu.SMEM), vmem, vmem],
-        out_specs=vmem,
-        out_shape=jax.ShapeDtypeStruct((2 * mine.shape[0], mine.shape[1]), mine.dtype),
-        name="stack_text",
-    )(core, mine, other)
-
-
 def per_device(img_qkv, txt_qkv, stale_kv, residual, gate_scale, proj_weight):
     patches, head_owners = lax.axis_size("patch"), lax.axis_size("head")
     patch = lax.axis_index("patch")
@@ -467,8 +441,7 @@
         return [(z + 1, z) for z in range(0, planes - step)]
 
     core_only = core.astype(jnp.int32).reshape(1)
-    packed_txt = pack(core_only, txt_qkv, text_rows, head_owners, pair, width)
-    txt = exchange(packed_txt)
+    txt = exchange(pack(core_only, txt_qkv, text_rows, head_owners, pair, width))
 
     along, against = [], []
     if pair == 2:
@@ -482,7 +455,7 @@
             ]
             held = [lax.ppermute(block, "patch", way) for block, way in zip(held, pairs)]
             if step == 1:
-                held = [after(block, packed_txt) for block in held]
+                held = [held[0], after(held[1], txt)]
             along.append(held)
             against.append([swap(block) for block in held])
         ahead = jnp.where(core == 0, plane, planes - 1 - plane)
@@ -523,7 +496,11 @@
         keep = flag_after(inner.astype(jnp.int32).reshape(1), image_out)
         text_out = jnp.where(keep[0] == 1, text_out, hopped)
     if pair == 2:
-        text_out = stack_text(core_only, text_out, swap(text_out))
+        other = swap(text_out)
+        lower = core == 0
+        text_out = jnp.concatenate(
+            [jnp.where(lower, text_out, other), jnp.where(lower, other, text_out)], 0
+        )
     return (image_out, text_out)
 
 

time: 115 us -> 119 us (1.035)
  the two profiles are of different devices: /device:TPU:9 before, /device:TPU:17 now
where the time goes in v14:
time: 119 us; the launch traced here: 118 us
  starting transfers between devices  47.6 us (40%)
  waiting for transfers between devices  31.6 us (27%)
  Pallas kernels  30.4 us (26%)
  local copies, waits for them, and re-layouts  5.97 us (5%)
  between operations  1.46 us (1%)
    all_to_all x4, starting transfers between devices, exchange(): lax.all_to_all(x, ('patch', 'head'), split_axis=0, concat_axis=0, axis_in...  26 us
    ppermute x6, waiting for transfers between devices, per_device(): lax.ppermute(block, 'patch', way)  22.1 us
    pallas_call x2, Pallas kernels, attend(): pl.pallas_call(functools.partial(body, len(stale), counts), in_specs=[pl....  16.7 us
    ppermute x6, starting transfers between devices, per_device(): lax.ppermute(block, 'patch', way)  12.8 us
    pallas_call x1, Pallas kernels, project(): pl.pallas_call(functools.partial(project_body, order), in_specs=[vmem, pl...  7.85 us
    all_to_all x4, waiting for transfers between devices, exchange(): lax.all_to_all(x, ('patch', 'head'), split_axis=0, concat_axis=0, axis_in...  7.58 us
    ppermute x8, starting transfers between devices, swap(): return lax.ppermute(x, 'patch', swap_pairs)  7.45 us
    unnamed x24, local copies, waits for them, and re-layouts  5.89 us
  transfers between devices with their start and end apart: 19, of which 8 were waited for; matrix products, arithmetic and copies ran while one was open for 0% of the time, Pallas kernels for 23%

profile of v14, /device:TPU:17, one launch (start us, length us, event | category | flops | bytes accessed | tf_op | source)
XLA Modules:
  0.0 118.1 jit_solution(8349332020337263508)
XLA Ops:
  0.7 1.7 %copy-done.3 = bf16[128,9216]{1,0:T(8,128)(2,1)S(1)} copy-done((bf16[128,9216]{1,0:T(8,128)(2,1)S(1)}, bf16[128,9216]{1,0:T(8,128)(2,1)}, u32[]{:S(2)}) %copy-start.3) | copy-done | bytes 2359320
  2.3 2.9 %pack_heads.2 = bf16[8,64,1152]{2,1,0:T(8,128)(2,1)} custom-call(s32[1]{0:T(128)} %bitcast._, bf16[128,9216]{1,0:T(8,128)(2,1)S(1)} %copy-done.3, bf16[128,9216]{1,0:T(8,128)(2,1)S(1)} %copy-done.3, bf16[128,9216]{1,0:T(8,128)(2,1)S(1)} %copy-done.3), custom_call_target="tpu_custom_call" | custom-call | bytes 2359296 | tf_op jit(solution)/shard_map/pack_heads/pallas_call | solution.py:44
  5.2 4.4 %all-to-all-start = ((bf16[8,64,1152]{2,1,0:T(8,128)(2,1)}), bf16[8,64,1152]{2,1,0:T(8,128)(2,1)S(1)}, u32[]{:S(2)}, u32[]{:S(2)}) async-start(bf16[8,64,1152]{2,1,0:T(8,128)(2,1)} %pack_heads.2), calls=%async_computation | async-start | bytes 2359296 | tf_op jit(solution)/shard_map/all_to_all | solution.py:430
  9.6 2.2 %collective-permute-start.1 = (bf16[2,256,768]{2,1,0:T(8,128)(2,1)}, bf16[2,256,768]{2,1,0:T(8,128)(2,1)}, u32[]{:S(2)}, u32[]{:S(2)}) collective-permute-start(bf16[2,256,768]{2,1,0:T(8,128)(2,1)} %refs_0_.7), channel_id=1, source_target_pairs={{0,8},{8,16},{16,24},{12,4},{20,12},{28,20},{1,9},{9,17},{17,25},{... | collective-permute-start | bytes 2359304 | tf_op jit(solution)/shard_map/ppermute | solution.py:456
  11.8 2.3 %collective-permute-start.2 = (bf16[2,256,768]{2,1,0:T(8,128)(2,1)}, bf16[2,256,768]{2,1,0:T(8,128)(2,1)S(1)}, u32[]{:S(2)}, u32[]{:S(2)}) collective-permute-start(bf16[2,256,768]{2,1,0:T(8,128)(2,1)} %refs_0_.7), channel_id=1, source_target_pairs={{4,8},{12,16},{20,24},{8,4},{16,12},{24,20},{5,9},{13,17},{21,25},... | collective-permute-start | bytes 2359304 | tf_op jit(solution)/shard_map/ppermute | solution.py:456
  14.1 14.6 %collective-permute-done.1.refs_2_ = bf16[2,256,768]{2,1,0:T(8,128)(2,1)} collective-permute-done((bf16[2,256,768]{2,1,0:T(8,128)(2,1)}, bf16[2,256,768]{2,1,0:T(8,128)(2,1)}, u32[]{:S(2)}, u32[]{:S(2)}) %collective-permute-start.1) | collective-permute-done | bytes 786464 | tf_op jit(solution)/shard_map/ppermute | solution.py:456
  28.8 2.2 %collective-permute-start.3 = (bf16[2,256,768]{2,1,0:T(8,128)(2,1)}, bf16[2,256,768]{2,1,0:T(8,128)(2,1)}, u32[]{:S(2)}, u32[]{:S(2)}) collective-permute-start(bf16[2,256,768]{2,1,0:T(8,128)(2,1)} %collective-permute-done.1.refs_2_), channel_id=1, source_target_pairs={{8,16},{16,24},{12,4},{20,12},{9,17},{17,25},{13,5},{21,13},{10,18... | collective-permute-start | bytes 2359304 | tf_op jit(solution)/shard_map/ppermute | solution.py:456
  31.4 0.9 copy-done.5
  32.3 1.0 copy-done
  33.3 3.0 %collective-permute-start.6 = (bf16[2,256,768]{2,1,0:T(8,128)(2,1)}, bf16[2,256,768]{2,1,0:T(8,128)(2,1)}, u32[]{:S(2)}, u32[]{:S(2)}) collective-permute-start(bf16[2,256,768]{2,1,0:T(8,128)(2,1)} %after.1.refs_3_), channel_id=1, source_target_pairs={{8,16},{16,24},{12,4},{20,12},{9,17},{17,25},{13,5},{21,13},{10,18... | collective-permute-start | bytes 2359304 | tf_op jit(solution)/shard_map/ppermute | solution.py:456
  36.3 2.8 %collective-permute-start = (bf16[2,256,768]{2,1,0:T(8,128)(2,1)}, bf16[2,256,768]{2,1,0:T(8,128)(2,1)}, u32[]{:S(2)}, u32[]{:S(2)}) collective-permute-start(bf16[2,256,768]{2,1,0:T(8,128)(2,1)} %refs_0_.7), channel_id=1, source_target_pairs={{0,4},{4,0},{8,12},{12,8},{16,20},{20,16},{24,28},{28,24},{1,5},{5... | collective-permute-start | bytes 2359304 | tf_op jit(solution)/shard_map/ppermute | solution.py:435
  39.3 1.6 %collective-permute-start.4 = (bf16[2,256,768]{2,1,0:T(8,128)(2,1)}, bf16[2,256,768]{2,1,0:T(8,128)(2,1)}, u32[]{:S(2)}, u32[]{:S(2)}) collective-permute-start(bf16[2,256,768]{2,1,0:T(8,128)(2,1)} %collective-permute-done.3.refs_4_.refs_6_), channel_id=1, source_target_pairs={{16,24},{12,4},{17,25},{13,5},{18,26},{14,6},{19,27},{15,7}} | collective-permute-start | bytes 2359304 | tf_op jit(solution)/shard_map/ppermute | solution.py:456
  40.9 6.8 %collective-permute-done.6.refs_5_.refs_7_ = bf16[2,256,768]{2,1,0:T(8,128)(2,1)} collective-permute-done((bf16[2,256,768]{2,1,0:T(8,128)(2,1)}, bf16[2,256,768]{2,1,0:T(8,128)(2,1)}, u32[]{:S(2)}, u32[]{:S(2)}) %collective-permute-start.6) | collective-permute-done | bytes 786464 | tf_op jit(solution)/shard_map/ppermute | solution.py:456
  47.7 1.5 %collective-permute-start.7 = (bf16[2,256,768]{2,1,0:T(8,128)(2,1)}, bf16[2,256,768]{2,1,0:T(8,128)(2,1)}, u32[]{:S(2)}, u32[]{:S(2)}) collective-permute-start(bf16[2,256,768]{2,1,0:T(8,128)(2,1)} %collective-permute-done.6.refs_5_.refs_7_), channel_id=1, source_target_pairs={{16,24},{12,4},{17,25},{13,5},{18,26},{14,6},{19,27},{15,7}} | collective-permute-start | bytes 2359304 | tf_op jit(solution)/shard_map/ppermute | solution.py:456
  49.3 1.3 %copy-done.1 = bf16[8,64,1152]{2,1,0:T(8,128)(2,1)S(1)} copy-done((bf16[8,64,1152]{2,1,0:T(8,128)(2,1)S(1)}, bf16[8,64,1152]{2,1,0:T(8,128)(2,1)}, u32[]{:S(2)}) %copy-start.1) | copy-done | bytes 1179672
  50.5 0.7 pack_heads.3
  51.2 1.0 copy-done.7
  52.2 13.7 %all-to-all-start.1 = ((bf16[8,64,1152]{2,1,0:T(8,128)(2,1)}), bf16[8,64,1152]{2,1,0:T(8,128)(2,1)S(1)}, u32[]{:S(2)}, u32[]{:S(2)}) async-start(bf16[8,64,1152]{2,1,0:T(8,128)(2,1)} %copy-done.7), calls=%async_computation.1 | async-start | bytes 2359296 | tf_op jit(solution)/shard_map/all_to_all | solution.py:430
  67.0 3.3 %collective-permute-start.8 = (bf16[2,256,768]{2,1,0:T(8,128)(2,1)}, bf16[2,256,768]{2,1,0:T(8,128)(2,1)}, u32[]{:S(2)}, u32[]{:S(2)}) collective-permute-start(bf16[2,256,768]{2,1,0:T(8,128)(2,1)} %collective-permute-done.7.refs_11_), channel_id=1, source_target_pairs={{0,4},{4,0},{8,12},{12,8},{16,20},{20,16},{24,28},{28,24},{1,5},{5... | collective-permute-start | bytes 2359304 | tf_op jit(solution)/shard_map/ppermute | solution.py:435
  70.3 0.5 collective-permute-done.10.refs_7_.refs_9_
  70.8 8.2 %attend_text.1.refs_14_ = bf16[8,64,384]{2,1,0:T(8,128)(2,1)} custom-call(s32[5]{0:T(128)S(1)} %stack.38.info, bf16[8,64,1152]{2,1,0:T(8,128)(2,1)S(1)} %copy-done.2, bf16[2,256,768]{2,1,0:T(8,128)(2,1)} %refs_0_.7, bf16[2,256,768]{2,1,0:T(8,128)(2,1)} %collective-permute-done.refs_1_, bf16[2,256,768]{2,1,0:T(8,128)(2,1)} %collective-permute-done.1.refs_2_, ...), custom_call_target="tpu_custom_call" | custom-call | flops 2013265920 | bytes 3932160 | tf_op jit(solution)/shard_map/attend_text/pallas_call | solution.py:301
  79.0 3.0 %all-to-all-done.1.img = bf16[8,64,1152]{2,1,0:T(8,128)(2,1)S(1)} async-done(((bf16[8,64,1152]{2,1,0:T(8,128)(2,1)}), bf16[8,64,1152]{2,1,0:T(8,128)(2,1)S(1)}, u32[]{:S(2)}, u32[]{:S(2)}) %all-to-all-start.1) | async-done | bytes 1179680 | tf_op jit(solution)/shard_map/all_to_all | solution.py:430
  82.0 3.6 %all-to-all-start.3 = ((bf16[8,64,384]{2,1,0:T(8,128)(2,1)}), bf16[8,64,384]{2,1,0:T(8,128)(2,1)S(1)}, u32[]{:S(2)}, u32[]{:S(2)}) async-start(bf16[8,64,384]{2,1,0:T(8,128)(2,1)} %attend_text.1.refs_14_), calls=%async_computation.3 | async-start | bytes 786432 | tf_op jit(solution)/shard_map/all_to_all | solution.py:430
  85.6 8.5 %attend_image.1.earlier = bf16[8,64,384]{2,1,0:T(8,128)(2,1)} custom-call(s32[5]{0:T(128)S(1)} %stack.38.info, bf16[8,64,1152]{2,1,0:T(8,128)(2,1)S(1)} %all-to-all-done.1.img, bf16[8,64,1152]{2,1,0:T(8,128)(2,1)S(1)} %copy-done.2, bf16[2,256,768]{2,1,0:T(8,128)(2,1)} %refs_0_.7, bf16[2,256,768]{2,1,0:T(8,128)(2,1)} %collective-permute-done.refs_1_, ...), custom_call_target="tpu_custom_call" | custom-call | flops 2013265920 | bytes 3932160 | tf_op jit(solution)/shard_map/attend_image/pallas_call | solution.py:301
  94.2 4.3 %all-to-all-start.2 = ((bf16[8,64,384]{2,1,0:T(8,128)(2,1)}), bf16[8,64,384]{2,1,0:T(8,128)(2,1)S(1)}, u32[]{:S(2)}, u32[]{:S(2)}) async-start(bf16[8,64,384]{2,1,0:T(8,128)(2,1)} %attend_image.1.earlier), calls=%async_computation.2 | async-start | bytes 786432 | tf_op jit(solution)/shard_map/all_to_all | solution.py:430
  98.6 1.8 %unpack_text.1 = bf16[64,3072]{1,0:T(8,128)(2,1)} custom-call(bf16[8,64,384]{2,1,0:T(8,128)(2,1)} %copy-done.10, bf16[8,64,384]{2,1,0:T(8,128)(2,1)} %attend_image.1.earlier), custom_call_target="tpu_custom_call" | custom-call | tf_op jit(solution)/shard_map/unpack_text/pallas_call | solution.py:371
  100.3 1.3 %collective-permute-start.13 = (bf16[64,3072]{1,0:T(8,128)(2,1)}, bf16[64,3072]{1,0:T(8,128)(2,1)S(1)}, u32[]{:S(2)}, u32[]{:S(2)}) collective-permute-start(bf16[64,3072]{1,0:T(8,128)(2,1)} %unpack_text.1), channel_id=1, source_target_pairs={{8,0},{12,4},{16,24},{20,28},{9,1},{13,5},{17,25},{21,29},{10,2},{... | collective-permute-start | bytes 1179656 | tf_op jit(solution)/shard_map/ppermute | solution.py:495
  101.6 4.6 %all-to-all-done.2.x_ref = bf16[8,64,384]{2,1,0:T(8,128)(2,1)S(1)} async-done(((bf16[8,64,384]{2,1,0:T(8,128)(2,1)}), bf16[8,64,384]{2,1,0:T(8,128)(2,1)S(1)}, u32[]{:S(2)}, u32[]{:S(2)}) %all-to-all-start.2) | async-done | bytes 393248 | tf_op jit(solution)/shard_map/all_to_all | solution.py:430
  106.2 7.9 %project.1.earlier = bf16[64,3072]{1,0:T(8,128)(2,1)} custom-call(bf16[8,64,384]{2,1,0:T(8,128)(2,1)S(1)} %all-to-all-done.2.x_ref, bf16[8,384,3072]{2,1,0:T(8,128)(2,1)} %bitcast.9, bf16[64,3072]{1,0:T(8,128)(2,1)S(1)} %copy-done.8, f32[1,3072]{1,0:T(1,128)S(1)} %bitcast.8), custom_call_target="tpu_custom_call" | custom-call | flops 1207959552 | bytes 18874368 | tf_op jit(solution)/shard_map/project/pallas_call | solution.py:343
  114.1 0.5 flag_after.1
  115.6 1.5 %collective-permute-done.14 = bf16[64,3072]{1,0:T(8,128)(2,1)S(1)} collective-permute-done((bf16[64,3072]{1,0:T(8,128)(2,1)S(1)}, bf16[64,3072]{1,0:T(8,128)(2,1)S(1)}, u32[]{:S(2)}, u32[]{:S(2)}) %collective-permute-start.14) | collective-permute-done | bytes 393248 | tf_op jit(solution)/shard_map/ppermute | solution.py:435
  117.2 0.9 pad_maximum_fusion
  (42 shorter events, 2.2 us)
Async XLA Ops:
  0.6 1.7 %copy-start.3 = (bf16[128,9216]{1,0:T(8,128)(2,1)S(1)}, bf16[128,9216]{1,0:T(8,128)(2,1)}, u32[]{:S(2)}) copy-start(bf16[128,9216]{1,0:T(8,128)(2,1)} %refs_2_.2) | copy-start | bytes 7077892
  5.2 26.2 %all-to-all-start = ((bf16[8,64,1152]{2,1,0:T(8,128)(2,1)}), bf16[8,64,1152]{2,1,0:T(8,128)(2,1)S(1)}, u32[]{:S(2)}, u32[]{:S(2)}) async-start(bf16[8,64,1152]{2,1,0:T(8,128)(2,1)} %pack_heads.2), calls=%async_computation | async-start | bytes 2359296 | tf_op jit(solution)/shard_map/all_to_all | solution.py:430
  9.6 39.6 %copy-start.4 = (bf16[64,9216]{1,0:T(8,128)(2,1)S(1)}, bf16[64,9216]{1,0:T(8,128)(2,1)}, u32[]{:S(2)}) copy-start(bf16[64,9216]{1,0:T(8,128)(2,1)} %refs_2_.3) | copy-start | bytes 3538948
  9.6 19.2 %collective-permute-start.1 = (bf16[2,256,768]{2,1,0:T(8,128)(2,1)}, bf16[2,256,768]{2,1,0:T(8,128)(2,1)}, u32[]{:S(2)}, u32[]{:S(2)}) collective-permute-start(bf16[2,256,768]{2,1,0:T(8,128)(2,1)} %refs_0_.7), channel_id=1, source_target_pairs={{0,8},{8,16},{16,24},{12,4},{20,12},{28,20},{1,9},{9,17},{17,25},{... | collective-permute-start | bytes 2359304 | tf_op jit(solution)/shard_map/ppermute | solution.py:456
  11.8 19.6 %collective-permute-start.2 = (bf16[2,256,768]{2,1,0:T(8,128)(2,1)}, bf16[2,256,768]{2,1,0:T(8,128)(2,1)S(1)}, u32[]{:S(2)}, u32[]{:S(2)}) collective-permute-start(bf16[2,256,768]{2,1,0:T(8,128)(2,1)} %refs_0_.7), channel_id=1, source_target_pairs={{4,8},{12,16},{20,24},{8,4},{16,12},{24,20},{5,9},{13,17},{21,25},... | collective-permute-start | bytes 2359304 | tf_op jit(solution)/shard_map/ppermute | solution.py:456
  28.8 10.5 %collective-permute-start.3 = (bf16[2,256,768]{2,1,0:T(8,128)(2,1)}, bf16[2,256,768]{2,1,0:T(8,128)(2,1)}, u32[]{:S(2)}, u32[]{:S(2)}) collective-permute-start(bf16[2,256,768]{2,1,0:T(8,128)(2,1)} %collective-permute-done.1.refs_2_), channel_id=1, source_target_pairs={{8,16},{16,24},{12,4},{20,12},{9,17},{17,25},{13,5},{21,13},{10,18... | collective-permute-start | bytes 2359304 | tf_op jit(solution)/shard_map/ppermute | solution.py:456
  31.4 0.9 copy-start.5
  32.3 1.0 copy-start
  33.3 14.4 %collective-permute-start.6 = (bf16[2,256,768]{2,1,0:T(8,128)(2,1)}, bf16[2,256,768]{2,1,0:T(8,128)(2,1)}, u32[]{:S(2)}, u32[]{:S(2)}) collective-permute-start(bf16[2,256,768]{2,1,0:T(8,128)(2,1)} %after.1.refs_3_), channel_id=1, source_target_pairs={{8,16},{16,24},{12,4},{20,12},{9,17},{17,25},{13,5},{21,13},{10,18... | collective-permute-start | bytes 2359304 | tf_op jit(solution)/shard_map/ppermute | solution.py:456
  36.3 29.7 %collective-permute-start = (bf16[2,256,768]{2,1,0:T(8,128)(2,1)}, bf16[2,256,768]{2,1,0:T(8,128)(2,1)}, u32[]{:S(2)}, u32[]{:S(2)}) collective-permute-start(bf16[2,256,768]{2,1,0:T(8,128)(2,1)} %refs_0_.7), channel_id=1, source_target_pairs={{0,4},{4,0},{8,12},{12,8},{16,20},{20,16},{24,28},{28,24},{1,5},{5... | collective-permute-start | bytes 2359304 | tf_op jit(solution)/shard_map/ppermute | solution.py:435
  39.1 27.4 %collective-permute-start.11 = (bf16[2,256,768]{2,1,0:T(8,128)(2,1)}, bf16[2,256,768]{2,1,0:T(8,128)(2,1)}, u32[]{:S(2)}, u32[]{:S(2)}) collective-permute-start(bf16[2,256,768]{2,1,0:T(8,128)(2,1)} %collective-permute-done.1.refs_2_), channel_id=1, source_target_pairs={{0,4},{4,0},{8,12},{12,8},{16,20},{20,16},{24,28},{28,24},{1,5},{5... | collective-permute-start | bytes 2359304 | tf_op jit(solution)/shard_map/ppermute | solution.py:435
  39.3 27.3 %collective-permute-start.4 = (bf16[2,256,768]{2,1,0:T(8,128)(2,1)}, bf16[2,256,768]{2,1,0:T(8,128)(2,1)}, u32[]{:S(2)}, u32[]{:S(2)}) collective-permute-start(bf16[2,256,768]{2,1,0:T(8,128)(2,1)} %collective-permute-done.3.refs_4_.refs_6_), channel_id=1, source_target_pairs={{16,24},{12,4},{17,25},{13,5},{18,26},{14,6},{19,27},{15,7}} | collective-permute-start | bytes 2359304 | tf_op jit(solution)/shard_map/ppermute | solution.py:456
  47.7 19.3 %collective-permute-start.7 = (bf16[2,256,768]{2,1,0:T(8,128)(2,1)}, bf16[2,256,768]{2,1,0:T(8,128)(2,1)}, u32[]{:S(2)}, u32[]{:S(2)}) collective-permute-start(bf16[2,256,768]{2,1,0:T(8,128)(2,1)} %collective-permute-done.6.refs_5_.refs_7_), channel_id=1, source_target_pairs={{16,24},{12,4},{17,25},{13,5},{18,26},{14,6},{19,27},{15,7}} | collective-permute-start | bytes 2359304 | tf_op jit(solution)/shard_map/ppermute | solution.py:456
  49.3 1.3 %copy-start.1 = (bf16[8,64,1152]{2,1,0:T(8,128)(2,1)S(1)}, bf16[8,64,1152]{2,1,0:T(8,128)(2,1)}, u32[]{:S(2)}) copy-start(bf16[8,64,1152]{2,1,0:T(8,128)(2,1)} %copy-done) | copy-start | bytes 3538948
  51.2 1.0 copy-start.7
  52.2 13.7 %copy-start.6 = (bf16[2,256,768]{2,1,0:T(8,128)(2,1)S(1)}, bf16[2,256,768]{2,1,0:T(8,128)(2,1)}, u32[]{:S(2)}) copy-start(bf16[2,256,768]{2,1,0:T(8,128)(2,1)} %after.1.refs_3_) | copy-start | bytes 2359300
  52.2 18.6 %copy-start.2 = (bf16[8,64,1152]{2,1,0:T(8,128)(2,1)S(1)}, bf16[8,64,1152]{2,1,0:T(8,128)(2,1)}, u32[]{:S(2)}) copy-start(bf16[8,64,1152]{2,1,0:T(8,128)(2,1)} %copy-done) | copy-start | bytes 3538948
  52.2 29.8 %all-to-all-start.1 = ((bf16[8,64,1152]{2,1,0:T(8,128)(2,1)}), bf16[8,64,1152]{2,1,0:T(8,128)(2,1)S(1)}, u32[]{:S(2)}, u32[]{:S(2)}) async-start(bf16[8,64,1152]{2,1,0:T(8,128)(2,1)} %copy-done.7), calls=%async_computation.1 | async-start | bytes 2359296 | tf_op jit(solution)/shard_map/all_to_all | solution.py:430
  65.9 4.4 %collective-permute-start.12 = (bf16[2,256,768]{2,1,0:T(8,128)(2,1)S(1)}, bf16[2,256,768]{2,1,0:T(8,128)(2,1)}, u32[]{:S(2)}, u32[]{:S(2)}) collective-permute-start(bf16[2,256,768]{2,1,0:T(8,128)(2,1)S(1)} %copy-done.6), channel_id=1, source_target_pairs={{0,4},{4,0},{8,12},{12,8},{16,20},{20,16},{24,28},{28,24},{1,5},{5... | collective-permute-start | bytes 2359304 | tf_op jit(solution)/shard_map/ppermute | solution.py:435
  66.0 4.3 %collective-permute-start.9 = (bf16[2,256,768]{2,1,0:T(8,128)(2,1)}, bf16[2,256,768]{2,1,0:T(8,128)(2,1)}, u32[]{:S(2)}, u32[]{:S(2)}) collective-permute-start(bf16[2,256,768]{2,1,0:T(8,128)(2,1)} %collective-permute-done.3.refs_4_.refs_6_), channel_id=1, source_target_pairs={{0,4},{4,0},{8,12},{12,8},{16,20},{20,16},{24,28},{28,24},{1,5},{5... | collective-permute-start | bytes 2359304 | tf_op jit(solution)/shard_map/ppermute | solution.py:435
  66.5 4.4 %collective-permute-start.10 = (bf16[2,256,768]{2,1,0:T(8,128)(2,1)}, bf16[2,256,768]{2,1,0:T(8,128)(2,1)}, u32[]{:S(2)}, u32[]{:S(2)}) collective-permute-start(bf16[2,256,768]{2,1,0:T(8,128)(2,1)} %collective-permute-done.6.refs_5_.refs_7_), channel_id=1, source_target_pairs={{0,4},{4,0},{8,12},{12,8},{16,20},{20,16},{24,28},{28,24},{1,5},{5... | collective-permute-start | bytes 2359304 | tf_op jit(solution)/shard_map/ppermute | solution.py:435
  66.5 19.1 %collective-permute-start.5 = (bf16[2,256,768]{2,1,0:T(8,128)(2,1)}, bf16[2,256,768]{2,1,0:T(8,128)(2,1)}, u32[]{:S(2)}, u32[]{:S(2)}) collective-permute-start(bf16[2,256,768]{2,1,0:T(8,128)(2,1)} %collective-permute-done.4.refs_10_), channel_id=1, source_target_pairs={{0,4},{4,0},{8,12},{12,8},{16,20},{20,16},{24,28},{28,24},{1,5},{5... | collective-permute-start | bytes 2359304 | tf_op jit(solution)/shard_map/ppermute | solution.py:435
  67.0 18.6 %collective-permute-start.8 = (bf16[2,256,768]{2,1,0:T(8,128)(2,1)}, bf16[2,256,768]{2,1,0:T(8,128)(2,1)}, u32[]{:S(2)}, u32[]{:S(2)}) collective-permute-start(bf16[2,256,768]{2,1,0:T(8,128)(2,1)} %collective-permute-done.7.refs_11_), channel_id=1, source_target_pairs={{0,4},{4,0},{8,12},{12,8},{16,20},{20,16},{24,28},{28,24},{1,5},{5... | collective-permute-start | bytes 2359304 | tf_op jit(solution)/shard_map/ppermute | solution.py:435
  82.0 12.2 %all-to-all-start.3 = ((bf16[8,64,384]{2,1,0:T(8,128)(2,1)}), bf16[8,64,384]{2,1,0:T(8,128)(2,1)S(1)}, u32[]{:S(2)}, u32[]{:S(2)}) async-start(bf16[8,64,384]{2,1,0:T(8,128)(2,1)} %attend_text.1.refs_14_), calls=%async_computation.3 | async-start | bytes 786432 | tf_op jit(solution)/shard_map/all_to_all | solution.py:430
  94.2 12.0 %copy-start.8 = (bf16[64,3072]{1,0:T(8,128)(2,1)S(1)}, bf16[64,3072]{1,0:T(8,128)(2,1)}, u32[]{:S(2)}) copy-start(bf16[64,3072]{1,0:T(8,128)(2,1)} %residual.1) | copy-start | bytes 1179652
  94.2 12.0 %copy-start.9 = (f32[3072]{0:T(1024)S(1)}, f32[3072]{0:T(1024)}, u32[]{:S(2)}) copy-start(f32[3072]{0:T(1024)} %param.10) | copy-start | bytes 36868
  94.2 4.4 %copy-start.10 = (bf16[8,64,384]{2,1,0:T(8,128)(2,1)}, bf16[8,64,384]{2,1,0:T(8,128)(2,1)S(1)}, u32[]{:S(2)}) copy-start(bf16[8,64,384]{2,1,0:T(8,128)(2,1)S(1)} %all-to-all-done.3.x_ref) | copy-start | bytes 1179652
  94.2 12.0 %all-to-all-start.2 = ((bf16[8,64,384]{2,1,0:T(8,128)(2,1)}), bf16[8,64,384]{2,1,0:T(8,128)(2,1)S(1)}, u32[]{:S(2)}, u32[]{:S(2)}) async-start(bf16[8,64,384]{2,1,0:T(8,128)(2,1)} %attend_image.1.earlier), calls=%async_computation.2 | async-start | bytes 786432 | tf_op jit(solution)/shard_map/all_to_all | solution.py:430
  100.3 14.9 %collective-permute-start.13 = (bf16[64,3072]{1,0:T(8,128)(2,1)}, bf16[64,3072]{1,0:T(8,128)(2,1)S(1)}, u32[]{:S(2)}, u32[]{:S(2)}) collective-permute-start(bf16[64,3072]{1,0:T(8,128)(2,1)} %unpack_text.1), channel_id=1, source_target_pairs={{8,0},{12,4},{16,24},{20,28},{9,1},{13,5},{17,25},{21,29},{10,2},{... | collective-permute-start | bytes 1179656 | tf_op jit(solution)/shard_map/ppermute | solution.py:495
  106.2 9.1 %copy-start.11 = (bf16[64,3072]{1,0:T(8,128)(2,1)S(1)}, bf16[64,3072]{1,0:T(8,128)(2,1)}, u32[]{:S(2)}) copy-start(bf16[64,3072]{1,0:T(8,128)(2,1)} %unpack_text.1) | copy-start | bytes 1179652
  115.3 1.8 %collective-permute-start.14 = (bf16[64,3072]{1,0:T(8,128)(2,1)S(1)}, bf16[64,3072]{1,0:T(8,128)(2,1)S(1)}, u32[]{:S(2)}, u32[]{:S(2)}) collective-permute-start(bf16[64,3072]{1,0:T(8,128)(2,1)S(1)} %broadcast_select_fusion), channel_id=1, source_target_pairs={{0,4},{4,0},{8,12},{12,8},{16,20},{20,16},{24,28},{28,24},{1,5},{5... | collective-permute-start | bytes 1179656 | tf_op jit(solution)/shard_map/ppermute | solution.py:435

commit v15 on v14

--- a/solution.py
+++ b/solution.py
@@ -281,7 +281,7 @@
     back.wait()
 
 
-def attend(name, body, info, fresh, stale, entries, groups, earlier=()):
+def attend(name, body, info, fresh, stale, entries, groups, earlier=(), weight=1):
     first = fresh[0]
     width = first.shape[2] // 3
     heads, rows = width // HD, first.shape[0] * first.shape[1]
@@ -311,8 +311,8 @@
         ],
         compiler_params=pltpu.CompilerParams(vmem_limit_bytes=ATTEND_LIMIT),
         cost_estimate=pl.CostEstimate(
-            flops=4 * rows * keys * (2 + len(entries)) * width,
-            bytes_accessed=4 * keys * (2 + len(entries)) * width,
+            flops=weight * 4 * rows * keys * (2 + len(entries)) * width,
+            bytes_accessed=weight * 4 * keys * (2 + len(entries)) * width,
             transcendentals=rows * keys * (2 + len(entries)) * heads,
         ),
         name=name,
@@ -482,7 +482,8 @@
     if early:
         known = [[along[0]]] + entries[1:-1] + [[against[0]]]
     text_attn = attend(
-        "attend_text", functools.partial(text_body, wanted=planes), info, [txt], stale, known, 1
+        "attend_text", functools.partial(text_body, wanted=planes), info, [txt], stale, known, 1,
+        [img], 16,
     )
     image_attn = attend(
         "attend_image", image_body, info, [img, txt], stale, entries, pair, [text_attn]

time: 119 us -> 116 us (0.975)
  waiting for transfers between devices: 31.6 us -> 21.2 us
  starting transfers between devices: 47.6 us -> 53.9 us
  Pallas kernels: 30.4 us -> 32.7 us
    ppermute x8, starting transfers between devices: 7.45 us -> 22.1 us  [swap(): return lax.ppermute(x, 'patch', swap_pairs)]
    all_to_all x4, starting transfers between devices: 26 us -> 17.8 us  [exchange(): lax.all_to_all(x, ('patch', 'head'), split_axis=0, concat_axis=0, axis_in...]
    ppermute x6, waiting for transfers between devices: 22.1 us -> 15.1 us  [per_device(): lax.ppermute(block, 'patch', way)]
    all_to_all x4, waiting for transfers between devices: 7.58 us -> 4.58 us  [exchange(): lax.all_to_all(x, ('patch', 'head'), split_axis=0, concat_axis=0, axis_in...]
    pallas_call x2, Pallas kernels: 3.56 us -> 5.82 us  [pack(): pl.pallas_call(pack_body, grid_spec=pltpu.PrefetchScalarGridSpec(num_scal...]
    unnamed x24 -> x22, local copies, waits for them, and re-layouts: 5.89 us -> 4.87 us
  transfers between devices with their start and end apart: 19 -> 19, of which waited for: 8 -> 4; matrix products, arithmetic and copies ran while one was open for 0% -> 0% of each run, Pallas kernels for 23% -> 26%
where the time goes in v15:
time: 116 us; the launch traced here: 115 us
  starting transfers between devices  53.9 us (46%)
  Pallas kernels  32.7 us (28%)
  waiting for transfers between devices  21.2 us (18%)
  local copies, waits for them, and re-layouts  4.96 us (4%)
  between operations  1.46 us (1%)
    ppermute x8, starting transfers between devices, swap(): return lax.ppermute(x, 'patch', swap_pairs)  22.1 us
    all_to_all x4, starting transfers between devices, exchange(): lax.all_to_all(x, ('patch', 'head'), split_axis=0, concat_axis=0, axis_in...  17.8 us
    pallas_call x2, Pallas kernels, attend(): pl.pallas_call(functools.partial(body, len(stale), counts), in_specs=[pl....  16.7 us
    ppermute x6, waiting for transfers between devices, per_device(): lax.ppermute(block, 'patch', way)  15.1 us
    ppermute x6, starting transfers between devices, per_device(): lax.ppermute(block, 'patch', way)  12.8 us
    pallas_call x1, Pallas kernels, project(): pl.pallas_call(functools.partial(project_body, order), in_specs=[vmem, pl...  7.85 us
    pallas_call x2, Pallas kernels, pack(): pl.pallas_call(pack_body, grid_spec=pltpu.PrefetchScalarGridSpec(num_scal...  5.82 us
    unnamed x22, local copies, waits for them, and re-layouts  4.87 us
  transfers between devices with their start and end apart: 19, of which 4 were waited for; matrix products, arithmetic and copies ran while one was open for 0% of the time, Pallas kernels for 26%

profile of v15, /device:TPU:17, one launch (start us, length us, event | category | flops | bytes accessed | tf_op | source)
XLA Modules:
  0.0 115.3 jit_solution(10042498190675755782)
XLA Ops:
  0.7 1.7 %copy-done = bf16[128,9216]{1,0:T(8,128)(2,1)S(1)} copy-done((bf16[128,9216]{1,0:T(8,128)(2,1)S(1)}, bf16[128,9216]{1,0:T(8,128)(2,1)}, u32[]{:S(2)}) %copy-start) | copy-done | bytes 2359320
  2.3 2.9 %pack_heads.2 = bf16[8,64,1152]{2,1,0:T(8,128)(2,1)} custom-call(s32[1]{0:T(128)} %bitcast._, bf16[128,9216]{1,0:T(8,128)(2,1)S(1)} %copy-done, bf16[128,9216]{1,0:T(8,128)(2,1)S(1)} %copy-done, bf16[128,9216]{1,0:T(8,128)(2,1)S(1)} %copy-done), custom_call_target="tpu_custom_call" | custom-call | bytes 2359296 | tf_op jit(solution)/shard_map/pack_heads/pallas_call | solution.py:44
  5.2 4.4 %all-to-all-start = ((bf16[8,64,1152]{2,1,0:T(8,128)(2,1)}), bf16[8,64,1152]{2,1,0:T(8,128)(2,1)S(1)}, u32[]{:S(2)}, u32[]{:S(2)}) async-start(bf16[8,64,1152]{2,1,0:T(8,128)(2,1)} %pack_heads.2), calls=%async_computation | async-start | bytes 2359296 | tf_op jit(solution)/shard_map/all_to_all | solution.py:430
  9.6 2.2 %collective-permute-start.1 = (bf16[2,256,768]{2,1,0:T(8,128)(2,1)}, bf16[2,256,768]{2,1,0:T(8,128)(2,1)}, u32[]{:S(2)}, u32[]{:S(2)}) collective-permute-start(bf16[2,256,768]{2,1,0:T(8,128)(2,1)} %refs_0_.7), channel_id=1, source_target_pairs={{0,8},{8,16},{16,24},{12,4},{20,12},{28,20},{1,9},{9,17},{17,25},{... | collective-permute-start | bytes 2359304 | tf_op jit(solution)/shard_map/ppermute | solution.py:456
  11.8 2.3 %collective-permute-start.2 = (bf16[2,256,768]{2,1,0:T(8,128)(2,1)}, bf16[2,256,768]{2,1,0:T(8,128)(2,1)S(1)}, u32[]{:S(2)}, u32[]{:S(2)}) collective-permute-start(bf16[2,256,768]{2,1,0:T(8,128)(2,1)} %refs_0_.7), channel_id=1, source_target_pairs={{4,8},{12,16},{20,24},{8,4},{16,12},{24,20},{5,9},{13,17},{21,25},... | collective-permute-start | bytes 2359304 | tf_op jit(solution)/shard_map/ppermute | solution.py:456
  14.1 14.6 %collective-permute-done.1.refs_2_ = bf16[2,256,768]{2,1,0:T(8,128)(2,1)} collective-permute-done((bf16[2,256,768]{2,1,0:T(8,128)(2,1)}, bf16[2,256,768]{2,1,0:T(8,128)(2,1)}, u32[]{:S(2)}, u32[]{:S(2)}) %collective-permute-start.1) | collective-permute-done | bytes 786464 | tf_op jit(solution)/shard_map/ppermute | solution.py:456
  28.8 2.2 %collective-permute-start.3 = (bf16[2,256,768]{2,1,0:T(8,128)(2,1)}, bf16[2,256,768]{2,1,0:T(8,128)(2,1)}, u32[]{:S(2)}, u32[]{:S(2)}) collective-permute-start(bf16[2,256,768]{2,1,0:T(8,128)(2,1)} %collective-permute-done.1.refs_2_), channel_id=1, source_target_pairs={{8,16},{16,24},{12,4},{20,12},{9,17},{17,25},{13,5},{21,13},{10,18... | collective-permute-start | bytes 2359304 | tf_op jit(solution)/shard_map/ppermute | solution.py:456
  30.9 0.5 collective-permute-done.2.refs_0_
  31.4 0.9 copy-done.5
  32.3 1.0 copy-done.1
  33.3 3.0 %collective-permute-start.6 = (bf16[2,256,768]{2,1,0:T(8,128)(2,1)}, bf16[2,256,768]{2,1,0:T(8,128)(2,1)}, u32[]{:S(2)}, u32[]{:S(2)}) collective-permute-start(bf16[2,256,768]{2,1,0:T(8,128)(2,1)} %after.1.refs_3_), channel_id=1, source_target_pairs={{8,16},{16,24},{12,4},{20,12},{9,17},{17,25},{13,5},{21,13},{10,18... | collective-permute-start | bytes 2359304 | tf_op jit(solution)/shard_map/ppermute | solution.py:456
  36.3 2.8 %collective-permute-start = (bf16[2,256,768]{2,1,0:T(8,128)(2,1)}, bf16[2,256,768]{2,1,0:T(8,128)(2,1)}, u32[]{:S(2)}, u32[]{:S(2)}) collective-permute-start(bf16[2,256,768]{2,1,0:T(8,128)(2,1)} %refs_0_.7), channel_id=1, source_target_pairs={{0,4},{4,0},{8,12},{12,8},{16,20},{20,16},{24,28},{28,24},{1,5},{5... | collective-permute-start | bytes 2359304 | tf_op jit(solution)/shard_map/ppermute | solution.py:435
  39.2 1.3 %copy-done.2 = bf16[8,64,1152]{2,1,0:T(8,128)(2,1)S(1)} copy-done((bf16[8,64,1152]{2,1,0:T(8,128)(2,1)S(1)}, bf16[8,64,1152]{2,1,0:T(8,128)(2,1)}, u32[]{:S(2)}) %copy-start.2) | copy-done | bytes 1179672
  40.4 2.9 %pack_heads.3 = bf16[8,64,1152]{2,1,0:T(8,128)(2,1)} custom-call(s32[1]{0:T(128)} %constant.36.clone.1._, bf16[64,9216]{1,0:T(8,128)(2,1)S(1)} %copy-done.4, bf16[64,9216]{1,0:T(8,128)(2,1)S(1)} %copy-done.4, bf16[64,9216]{1,0:T(8,128)(2,1)S(1)} %copy-done.4, bf16[8,64,1152]{2,1,0:T(8,128)(2,1)S(1)} %copy-done.2), custom_call_target="tpu_custom_call" | custom-call | bytes 2359296 | tf_op jit(solution)/shard_map/pack_heads/pallas_call | solution.py:44
  43.4 4.7 %all-to-all-start.1 = ((bf16[8,64,1152]{2,1,0:T(8,128)(2,1)}), bf16[8,64,1152]{2,1,0:T(8,128)(2,1)S(1)}, u32[]{:S(2)}, u32[]{:S(2)}) async-start(bf16[8,64,1152]{2,1,0:T(8,128)(2,1)} %pack_heads.3), calls=%async_computation.1 | async-start | bytes 2359296 | tf_op jit(solution)/shard_map/all_to_all | solution.py:430
  48.1 1.5 %collective-permute-start.4 = (bf16[2,256,768]{2,1,0:T(8,128)(2,1)}, bf16[2,256,768]{2,1,0:T(8,128)(2,1)}, u32[]{:S(2)}, u32[]{:S(2)}) collective-permute-start(bf16[2,256,768]{2,1,0:T(8,128)(2,1)} %collective-permute-done.3.refs_4_.refs_6_), channel_id=1, source_target_pairs={{16,24},{12,4},{17,25},{13,5},{18,26},{14,6},{19,27},{15,7}} | collective-permute-start | bytes 2359304 | tf_op jit(solution)/shard_map/ppermute | solution.py:456
  49.7 1.6 %collective-permute-start.7 = (bf16[2,256,768]{2,1,0:T(8,128)(2,1)}, bf16[2,256,768]{2,1,0:T(8,128)(2,1)}, u32[]{:S(2)}, u32[]{:S(2)}) collective-permute-start(bf16[2,256,768]{2,1,0:T(8,128)(2,1)} %collective-permute-done.6.refs_5_.refs_7_), channel_id=1, source_target_pairs={{16,24},{12,4},{17,25},{13,5},{18,26},{14,6},{19,27},{15,7}} | collective-permute-start | bytes 2359304 | tf_op jit(solution)/shard_map/ppermute | solution.py:456
  51.2 7.5 %collective-permute-start.12 = (bf16[2,256,768]{2,1,0:T(8,128)(2,1)S(1)}, bf16[2,256,768]{2,1,0:T(8,128)(2,1)}, u32[]{:S(2)}, u32[]{:S(2)}) collective-permute-start(bf16[2,256,768]{2,1,0:T(8,128)(2,1)S(1)} %copy-done.6), channel_id=1, source_target_pairs={{0,4},{4,0},{8,12},{12,8},{16,20},{20,16},{24,28},{28,24},{1,5},{5... | collective-permute-start | bytes 2359304 | tf_op jit(solution)/shard_map/ppermute | solution.py:435
  58.8 0.4 collective-permute-start.10
  59.3 2.5 %collective-permute-start.5 = (bf16[2,256,768]{2,1,0:T(8,128)(2,1)}, bf16[2,256,768]{2,1,0:T(8,128)(2,1)}, u32[]{:S(2)}, u32[]{:S(2)}) collective-permute-start(bf16[2,256,768]{2,1,0:T(8,128)(2,1)} %collective-permute-done.4.refs_10_), channel_id=1, source_target_pairs={{0,4},{4,0},{8,12},{12,8},{16,20},{20,16},{24,28},{28,24},{1,5},{5... | collective-permute-start | bytes 2359304 | tf_op jit(solution)/shard_map/ppermute | solution.py:435
  61.8 8.4 %collective-permute-start.8 = (bf16[2,256,768]{2,1,0:T(8,128)(2,1)}, bf16[2,256,768]{2,1,0:T(8,128)(2,1)}, u32[]{:S(2)}, u32[]{:S(2)}) collective-permute-start(bf16[2,256,768]{2,1,0:T(8,128)(2,1)} %collective-permute-done.7.refs_11_), channel_id=1, source_target_pairs={{0,4},{4,0},{8,12},{12,8},{16,20},{20,16},{24,28},{28,24},{1,5},{5... | collective-permute-start | bytes 2359304 | tf_op jit(solution)/shard_map/ppermute | solution.py:435
  70.3 8.2 %attend_text.1.refs_14_ = bf16[8,64,384]{2,1,0:T(8,128)(2,1)} custom-call(s32[5]{0:T(128)S(1)} %stack.38.info, bf16[8,64,1152]{2,1,0:T(8,128)(2,1)S(1)} %copy-done.3, bf16[2,256,768]{2,1,0:T(8,128)(2,1)} %refs_0_.7, bf16[2,256,768]{2,1,0:T(8,128)(2,1)} %collective-permute-done.refs_1_, bf16[2,256,768]{2,1,0:T(8,128)(2,1)} %collective-permute-done.1.refs_2_, ...), custom_call_target="tpu_custom_call" | custom-call | flops 32212254720 | bytes 62914560 | tf_op jit(solution)/shard_map/attend_text/pallas_call | solution.py:301
  78.5 4.3 %all-to-all-start.3 = ((bf16[8,64,384]{2,1,0:T(8,128)(2,1)}), bf16[8,64,384]{2,1,0:T(8,128)(2,1)S(1)}, u32[]{:S(2)}, u32[]{:S(2)}) async-start(bf16[8,64,384]{2,1,0:T(8,128)(2,1)} %attend_text.1.refs_14_), calls=%async_computation.3 | async-start | bytes 786432 | tf_op jit(solution)/shard_map/all_to_all | solution.py:430
  82.8 8.5 %attend_image.1.earlier = bf16[8,64,384]{2,1,0:T(8,128)(2,1)} custom-call(s32[5]{0:T(128)S(1)} %stack.38.info, bf16[8,64,1152]{2,1,0:T(8,128)(2,1)S(1)} %all-to-all-done.1.refs_10_.img, bf16[8,64,1152]{2,1,0:T(8,128)(2,1)S(1)} %copy-done.3, bf16[2,256,768]{2,1,0:T(8,128)(2,1)} %refs_0_.7, bf16[2,256,768]{2,1,0:T(8,128)(2,1)} %collective-permute-done.refs_1_, ...), custom_call_target="tpu_custom_call" | custom-call | flops 2013265920 | bytes 3932160 | tf_op jit(solution)/shard_map/attend_image/pallas_call | solution.py:301
  91.4 4.3 %all-to-all-start.2 = ((bf16[8,64,384]{2,1,0:T(8,128)(2,1)}), bf16[8,64,384]{2,1,0:T(8,128)(2,1)S(1)}, u32[]{:S(2)}, u32[]{:S(2)}) async-start(bf16[8,64,384]{2,1,0:T(8,128)(2,1)} %attend_image.1.earlier), calls=%async_computation.2 | async-start | bytes 786432 | tf_op jit(solution)/shard_map/all_to_all | solution.py:430
  95.7 1.8 %unpack_text.1 = bf16[64,3072]{1,0:T(8,128)(2,1)} custom-call(bf16[8,64,384]{2,1,0:T(8,128)(2,1)} %copy-done.9, bf16[8,64,384]{2,1,0:T(8,128)(2,1)} %attend_image.1.earlier), custom_call_target="tpu_custom_call" | custom-call | tf_op jit(solution)/shard_map/unpack_text/pallas_call | solution.py:371
  97.5 1.3 %collective-permute-start.13 = (bf16[64,3072]{1,0:T(8,128)(2,1)}, bf16[64,3072]{1,0:T(8,128)(2,1)S(1)}, u32[]{:S(2)}, u32[]{:S(2)}) collective-permute-start(bf16[64,3072]{1,0:T(8,128)(2,1)} %unpack_text.1), channel_id=1, source_target_pairs={{8,0},{12,4},{16,24},{20,28},{9,1},{13,5},{17,25},{21,29},{10,2},{... | collective-permute-start | bytes 1179656 | tf_op jit(solution)/shard_map/ppermute | solution.py:496
  98.8 4.6 %all-to-all-done.2.x_ref = bf16[8,64,384]{2,1,0:T(8,128)(2,1)S(1)} async-done(((bf16[8,64,384]{2,1,0:T(8,128)(2,1)}), bf16[8,64,384]{2,1,0:T(8,128)(2,1)S(1)}, u32[]{:S(2)}, u32[]{:S(2)}) %all-to-all-start.2) | async-done | bytes 393248 | tf_op jit(solution)/shard_map/all_to_all | solution.py:430
  103.4 7.9 %project.1.earlier = bf16[64,3072]{1,0:T(8,128)(2,1)} custom-call(bf16[8,64,384]{2,1,0:T(8,128)(2,1)S(1)} %all-to-all-done.2.x_ref, bf16[8,384,3072]{2,1,0:T(8,128)(2,1)} %bitcast.9, bf16[64,3072]{1,0:T(8,128)(2,1)S(1)} %copy-done.7, f32[1,3072]{1,0:T(1,128)S(1)} %bitcast.8), custom_call_target="tpu_custom_call" | custom-call | flops 1207959552 | bytes 18874368 | tf_op jit(solution)/shard_map/project/pallas_call | solution.py:343
  111.2 0.5 flag_after.1
  112.8 1.5 %collective-permute-done.14 = bf16[64,3072]{1,0:T(8,128)(2,1)S(1)} collective-permute-done((bf16[64,3072]{1,0:T(8,128)(2,1)S(1)}, bf16[64,3072]{1,0:T(8,128)(2,1)S(1)}, u32[]{:S(2)}, u32[]{:S(2)}) %collective-permute-start.14) | collective-permute-done | bytes 393248 | tf_op jit(solution)/shard_map/ppermute | solution.py:435
  114.3 0.9 pad_maximum_fusion
  (40 shorter events, 0.7 us)
Async XLA Ops:
  0.6 1.7 %copy-start = (bf16[128,9216]{1,0:T(8,128)(2,1)S(1)}, bf16[128,9216]{1,0:T(8,128)(2,1)}, u32[]{:S(2)}) copy-start(bf16[128,9216]{1,0:T(8,128)(2,1)} %refs_2_.2) | copy-start | bytes 7077892
  5.2 26.2 %all-to-all-start = ((bf16[8,64,1152]{2,1,0:T(8,128)(2,1)}), bf16[8,64,1152]{2,1,0:T(8,128)(2,1)S(1)}, u32[]{:S(2)}, u32[]{:S(2)}) async-start(bf16[8,64,1152]{2,1,0:T(8,128)(2,1)} %pack_heads.2), calls=%async_computation | async-start | bytes 2359296 | tf_op jit(solution)/shard_map/all_to_all | solution.py:430
  9.6 29.6 %copy-start.4 = (bf16[64,9216]{1,0:T(8,128)(2,1)S(1)}, bf16[64,9216]{1,0:T(8,128)(2,1)}, u32[]{:S(2)}) copy-start(bf16[64,9216]{1,0:T(8,128)(2,1)} %refs_2_.3) | copy-start | bytes 3538948
  9.6 19.2 %collective-permute-start.1 = (bf16[2,256,768]{2,1,0:T(8,128)(2,1)}, bf16[2,256,768]{2,1,0:T(8,128)(2,1)}, u32[]{:S(2)}, u32[]{:S(2)}) collective-permute-start(bf16[2,256,768]{2,1,0:T(8,128)(2,1)} %refs_0_.7), channel_id=1, source_target_pairs={{0,8},{8,16},{16,24},{12,4},{20,12},{28,20},{1,9},{9,17},{17,25},{... | collective-permute-start | bytes 2359304 | tf_op jit(solution)/shard_map/ppermute | solution.py:456
  11.8 19.6 %collective-permute-start.2 = (bf16[2,256,768]{2,1,0:T(8,128)(2,1)}, bf16[2,256,768]{2,1,0:T(8,128)(2,1)S(1)}, u32[]{:S(2)}, u32[]{:S(2)}) collective-permute-start(bf16[2,256,768]{2,1,0:T(8,128)(2,1)} %refs_0_.7), channel_id=1, source_target_pairs={{4,8},{12,16},{20,24},{8,4},{16,12},{24,20},{5,9},{13,17},{21,25},... | collective-permute-start | bytes 2359304 | tf_op jit(solution)/shard_map/ppermute | solution.py:456
  28.8 19.3 %collective-permute-start.3 = (bf16[2,256,768]{2,1,0:T(8,128)(2,1)}, bf16[2,256,768]{2,1,0:T(8,128)(2,1)}, u32[]{:S(2)}, u32[]{:S(2)}) collective-permute-start(bf16[2,256,768]{2,1,0:T(8,128)(2,1)} %collective-permute-done.1.refs_2_), channel_id=1, source_target_pairs={{8,16},{16,24},{12,4},{20,12},{9,17},{17,25},{13,5},{21,13},{10,18... | collective-permute-start | bytes 2359304 | tf_op jit(solution)/shard_map/ppermute | solution.py:456
  31.4 0.9 copy-start.5
  32.3 1.0 copy-start.1
  33.3 16.3 %collective-permute-start.6 = (bf16[2,256,768]{2,1,0:T(8,128)(2,1)}, bf16[2,256,768]{2,1,0:T(8,128)(2,1)}, u32[]{:S(2)}, u32[]{:S(2)}) collective-permute-start(bf16[2,256,768]{2,1,0:T(8,128)(2,1)} %after.1.refs_3_), channel_id=1, source_target_pairs={{8,16},{16,24},{12,4},{20,12},{9,17},{17,25},{13,5},{21,13},{10,18... | collective-permute-start | bytes 2359304 | tf_op jit(solution)/shard_map/ppermute | solution.py:456
  36.3 22.4 %collective-permute-start = (bf16[2,256,768]{2,1,0:T(8,128)(2,1)}, bf16[2,256,768]{2,1,0:T(8,128)(2,1)}, u32[]{:S(2)}, u32[]{:S(2)}) collective-permute-start(bf16[2,256,768]{2,1,0:T(8,128)(2,1)} %refs_0_.7), channel_id=1, source_target_pairs={{0,4},{4,0},{8,12},{12,8},{16,20},{20,16},{24,28},{28,24},{1,5},{5... | collective-permute-start | bytes 2359304 | tf_op jit(solution)/shard_map/ppermute | solution.py:435
  39.1 19.7 %collective-permute-start.11 = (bf16[2,256,768]{2,1,0:T(8,128)(2,1)}, bf16[2,256,768]{2,1,0:T(8,128)(2,1)}, u32[]{:S(2)}, u32[]{:S(2)}) collective-permute-start(bf16[2,256,768]{2,1,0:T(8,128)(2,1)} %collective-permute-done.1.refs_2_), channel_id=1, source_target_pairs={{0,4},{4,0},{8,12},{12,8},{16,20},{20,16},{24,28},{28,24},{1,5},{5... | collective-permute-start | bytes 2359304 | tf_op jit(solution)/shard_map/ppermute | solution.py:435
  39.2 1.3 %copy-start.2 = (bf16[8,64,1152]{2,1,0:T(8,128)(2,1)S(1)}, bf16[8,64,1152]{2,1,0:T(8,128)(2,1)}, u32[]{:S(2)}) copy-start(bf16[8,64,1152]{2,1,0:T(8,128)(2,1)} %copy-done.1) | copy-start | bytes 3538948
  43.4 7.9 %copy-start.6 = (bf16[2,256,768]{2,1,0:T(8,128)(2,1)S(1)}, bf16[2,256,768]{2,1,0:T(8,128)(2,1)}, u32[]{:S(2)}) copy-start(bf16[2,256,768]{2,1,0:T(8,128)(2,1)} %after.1.refs_3_) | copy-start | bytes 2359300
  43.4 26.9 %copy-start.3 = (bf16[8,64,1152]{2,1,0:T(8,128)(2,1)S(1)}, bf16[8,64,1152]{2,1,0:T(8,128)(2,1)}, u32[]{:S(2)}) copy-start(bf16[8,64,1152]{2,1,0:T(8,128)(2,1)} %copy-done.1) | copy-start | bytes 3538948
  43.4 26.9 %all-to-all-start.1 = ((bf16[8,64,1152]{2,1,0:T(8,128)(2,1)}), bf16[8,64,1152]{2,1,0:T(8,128)(2,1)S(1)}, u32[]{:S(2)}, u32[]{:S(2)}) async-start(bf16[8,64,1152]{2,1,0:T(8,128)(2,1)} %pack_heads.3), calls=%async_computation.1 | async-start | bytes 2359296 | tf_op jit(solution)/shard_map/all_to_all | solution.py:430
  48.1 11.2 %collective-permute-start.4 = (bf16[2,256,768]{2,1,0:T(8,128)(2,1)}, bf16[2,256,768]{2,1,0:T(8,128)(2,1)}, u32[]{:S(2)}, u32[]{:S(2)}) collective-permute-start(bf16[2,256,768]{2,1,0:T(8,128)(2,1)} %collective-permute-done.3.refs_4_.refs_6_), channel_id=1, source_target_pairs={{16,24},{12,4},{17,25},{13,5},{18,26},{14,6},{19,27},{15,7}} | collective-permute-start | bytes 2359304 | tf_op jit(solution)/shard_map/ppermute | solution.py:456
  49.7 12.2 %collective-permute-start.7 = (bf16[2,256,768]{2,1,0:T(8,128)(2,1)}, bf16[2,256,768]{2,1,0:T(8,128)(2,1)}, u32[]{:S(2)}, u32[]{:S(2)}) collective-permute-start(bf16[2,256,768]{2,1,0:T(8,128)(2,1)} %collective-permute-done.6.refs_5_.refs_7_), channel_id=1, source_target_pairs={{16,24},{12,4},{17,25},{13,5},{18,26},{14,6},{19,27},{15,7}} | collective-permute-start | bytes 2359304 | tf_op jit(solution)/shard_map/ppermute | solution.py:456
  51.2 19.0 %collective-permute-start.12 = (bf16[2,256,768]{2,1,0:T(8,128)(2,1)S(1)}, bf16[2,256,768]{2,1,0:T(8,128)(2,1)}, u32[]{:S(2)}, u32[]{:S(2)}) collective-permute-start(bf16[2,256,768]{2,1,0:T(8,128)(2,1)S(1)} %copy-done.6), channel_id=1, source_target_pairs={{0,4},{4,0},{8,12},{12,8},{16,20},{20,16},{24,28},{28,24},{1,5},{5... | collective-permute-start | bytes 2359304 | tf_op jit(solution)/shard_map/ppermute | solution.py:435
  58.7 11.6 %collective-permute-start.9 = (bf16[2,256,768]{2,1,0:T(8,128)(2,1)}, bf16[2,256,768]{2,1,0:T(8,128)(2,1)}, u32[]{:S(2)}, u32[]{:S(2)}) collective-permute-start(bf16[2,256,768]{2,1,0:T(8,128)(2,1)} %collective-permute-done.3.refs_4_.refs_6_), channel_id=1, source_target_pairs={{0,4},{4,0},{8,12},{12,8},{16,20},{20,16},{24,28},{28,24},{1,5},{5... | collective-permute-start | bytes 2359304 | tf_op jit(solution)/shard_map/ppermute | solution.py:435
  58.8 11.5 %collective-permute-start.10 = (bf16[2,256,768]{2,1,0:T(8,128)(2,1)}, bf16[2,256,768]{2,1,0:T(8,128)(2,1)}, u32[]{:S(2)}, u32[]{:S(2)}) collective-permute-start(bf16[2,256,768]{2,1,0:T(8,128)(2,1)} %collective-permute-done.6.refs_5_.refs_7_), channel_id=1, source_target_pairs={{0,4},{4,0},{8,12},{12,8},{16,20},{20,16},{24,28},{28,24},{1,5},{5... | collective-permute-start | bytes 2359304 | tf_op jit(solution)/shard_map/ppermute | solution.py:435
  59.3 23.5 %collective-permute-start.5 = (bf16[2,256,768]{2,1,0:T(8,128)(2,1)}, bf16[2,256,768]{2,1,0:T(8,128)(2,1)}, u32[]{:S(2)}, u32[]{:S(2)}) collective-permute-start(bf16[2,256,768]{2,1,0:T(8,128)(2,1)} %collective-permute-done.4.refs_10_), channel_id=1, source_target_pairs={{0,4},{4,0},{8,12},{12,8},{16,20},{20,16},{24,28},{28,24},{1,5},{5... | collective-permute-start | bytes 2359304 | tf_op jit(solution)/shard_map/ppermute | solution.py:435
  61.8 21.0 %collective-permute-start.8 = (bf16[2,256,768]{2,1,0:T(8,128)(2,1)}, bf16[2,256,768]{2,1,0:T(8,128)(2,1)}, u32[]{:S(2)}, u32[]{:S(2)}) collective-permute-start(bf16[2,256,768]{2,1,0:T(8,128)(2,1)} %collective-permute-done.7.refs_11_), channel_id=1, source_target_pairs={{0,4},{4,0},{8,12},{12,8},{16,20},{20,16},{24,28},{28,24},{1,5},{5... | collective-permute-start | bytes 2359304 | tf_op jit(solution)/shard_map/ppermute | solution.py:435
  78.5 12.9 %all-to-all-start.3 = ((bf16[8,64,384]{2,1,0:T(8,128)(2,1)}), bf16[8,64,384]{2,1,0:T(8,128)(2,1)S(1)}, u32[]{:S(2)}, u32[]{:S(2)}) async-start(bf16[8,64,384]{2,1,0:T(8,128)(2,1)} %attend_text.1.refs_14_), calls=%async_computation.3 | async-start | bytes 786432 | tf_op jit(solution)/shard_map/all_to_all | solution.py:430
  91.3 12.0 %copy-start.7 = (bf16[64,3072]{1,0:T(8,128)(2,1)S(1)}, bf16[64,3072]{1,0:T(8,128)(2,1)}, u32[]{:S(2)}) copy-start(bf16[64,3072]{1,0:T(8,128)(2,1)} %residual.1) | copy-start | bytes 1179652
  91.3 12.0 %copy-start.8 = (f32[3072]{0:T(1024)S(1)}, f32[3072]{0:T(1024)}, u32[]{:S(2)}) copy-start(f32[3072]{0:T(1024)} %param.10) | copy-start | bytes 36868
  91.4 4.4 %copy-start.9 = (bf16[8,64,384]{2,1,0:T(8,128)(2,1)}, bf16[8,64,384]{2,1,0:T(8,128)(2,1)S(1)}, u32[]{:S(2)}) copy-start(bf16[8,64,384]{2,1,0:T(8,128)(2,1)S(1)} %all-to-all-done.3.x_ref) | copy-start | bytes 1179652
  91.4 12.0 %all-to-all-start.2 = ((bf16[8,64,384]{2,1,0:T(8,128)(2,1)}), bf16[8,64,384]{2,1,0:T(8,128)(2,1)S(1)}, u32[]{:S(2)}, u32[]{:S(2)}) async-start(bf16[8,64,384]{2,1,0:T(8,128)(2,1)} %attend_image.1.earlier), calls=%async_computation.2 | async-start | bytes 786432 | tf_op jit(solution)/shard_map/all_to_all | solution.py:430
  97.5 14.9 %collective-permute-start.13 = (bf16[64,3072]{1,0:T(8,128)(2,1)}, bf16[64,3072]{1,0:T(8,128)(2,1)S(1)}, u32[]{:S(2)}, u32[]{:S(2)}) collective-permute-start(bf16[64,3072]{1,0:T(8,128)(2,1)} %unpack_text.1), channel_id=1, source_target_pairs={{8,0},{12,4},{16,24},{20,28},{9,1},{13,5},{17,25},{21,29},{10,2},{... | collective-permute-start | bytes 1179656 | tf_op jit(solution)/shard_map/ppermute | solution.py:496
  103.4 9.1 %copy-start.10 = (bf16[64,3072]{1,0:T(8,128)(2,1)S(1)}, bf16[64,3072]{1,0:T(8,128)(2,1)}, u32[]{:S(2)}) copy-start(bf16[64,3072]{1,0:T(8,128)(2,1)} %unpack_text.1) | copy-start | bytes 1179652
  112.5 1.8 %collective-permute-start.14 = (bf16[64,3072]{1,0:T(8,128)(2,1)S(1)}, bf16[64,3072]{1,0:T(8,128)(2,1)S(1)}, u32[]{:S(2)}, u32[]{:S(2)}) collective-permute-start(bf16[64,3072]{1,0:T(8,128)(2,1)S(1)} %broadcast_select_fusion), channel_id=1, source_target_pairs={{0,4},{4,0},{8,12},{12,8},{16,20},{20,16},{24,28},{28,24},{1,5},{5... | collective-permute-start | bytes 1179656 | tf_op jit(solution)/shard_map/ppermute | solution.py:435

commit v16 on v15

--- a/solution.py
+++ b/solution.py
@@ -443,7 +443,27 @@
     core_only = core.astype(jnp.int32).reshape(1)
     txt = exchange(pack(core_only, txt_qkv, text_rows, head_owners, pair, width))
 
+    zero_only = jnp.zeros((1,), jnp.int32)
+    img = exchange(
+        pack(zero_only, img_qkv, img_rows, head_owners, pair, width, [txt])
+    )
+
+    early = planes > 2
+    inner = (plane > 0) & (plane < planes - 1)
+    ahead = jnp.where(core == 0, plane, planes - 1 - plane) if pair == 2 else plane
+    first_holds = [ahead >= i for i in range(1, planes)]
+    info = jnp.stack([core] + first_holds + [inner if early else core >= 0]).astype(jnp.int32)
+
+    def attend_text(known):
+        if early:
+            known = [[along[0]]] + known[1:-1] + [[against[0]]]
+        return attend(
+            "attend_text", functools.partial(text_body, wanted=planes), info, [txt], stale,
+            known, 1, [img], 16,
+        )
+
     along, against = [], []
+    ordered = early and pair == 2
     if pair == 2:
         stale = [stale_kv, swap(stale_kv)]
         held = [stale_kv, stale_kv]
@@ -456,9 +476,12 @@
             held = [lax.ppermute(block, "patch", way) for block, way in zip(held, pairs)]
             if step == 1:
                 held = [held[0], after(held[1], txt)]
+            if ordered and step == planes - 1:
+                known = [[along[i - 1], against[planes - i - 1]] for i in range(2, planes - 1)]
+                text_attn = attend_text([[]] + known + [[]])
+                held = [after(block, text_attn) for block in held]
             along.append(held)
             against.append([swap(block) for block in held])
-        ahead = jnp.where(core == 0, plane, planes - 1 - plane)
     else:
         stale = [stale_kv]
         from_below = from_above = stale_kv
@@ -467,24 +490,9 @@
             from_above = lax.ppermute(from_above, "patch", down_pairs(step))
             along.append([from_below])
             against.append([from_above])
-        ahead = plane
     entries = [[along[i - 1], against[planes - i - 1]] for i in range(1, planes)]
-    first_holds = [ahead >= i for i in range(1, planes)]
-    zero_only = jnp.zeros((1,), jnp.int32)
-    img = exchange(
-        pack(zero_only, img_qkv, img_rows, head_owners, pair, width, [txt])
-    )
-
-    early = planes > 2
-    inner = (plane > 0) & (plane < planes - 1)
-    info = jnp.stack([core] + first_holds + [inner if early else core >= 0]).astype(jnp.int32)
-    known = entries
-    if early:
-        known = [[along[0]]] + entries[1:-1] + [[against[0]]]
-    text_attn = attend(
-        "attend_text", functools.partial(text_body, wanted=planes), info, [txt], stale, known, 1,
-        [img], 16,
-    )
+    if not ordered:
+        text_attn = attend_text(entries)
     image_attn = attend(
         "attend_image", image_body, info, [img, txt], stale, entries, pair, [text_attn]
     )

time: 116 us -> 118 us (1.017)
  starting transfers between devices: 53.9 us -> 47.4 us
  waiting for transfers between devices: 21.2 us -> 25.4 us
  local copies, waits for them, and re-layouts: 4.96 us -> 8.35 us
    ppermute x8, starting transfers between devices: 22.1 us -> 11 us  [swap(): return lax.ppermute(x, 'patch', swap_pairs)]
    all_to_all x4, waiting for transfers between devices: 4.58 us -> 8.82 us  [exchange(): lax.all_to_all(x, ('patch', 'head'), split_axis=0, concat_axis=0, axis_in...]
    unnamed x22 -> x28, local copies, waits for them, and re-layouts: 4.87 us -> 8.27 us
    ppermute x1, starting transfers between devices: 1.3 us -> 4 us  [per_device(): hopped = lax.ppermute(text_out, 'patch', ends)]
    all_to_all x4, starting transfers between devices: 17.8 us -> 20.5 us  [exchange(): lax.all_to_all(x, ('patch', 'head'), split_axis=0, concat_axis=0, axis_in...]
  transfers between devices with their start and end apart: 19 -> 19, of which waited for: 4 -> 5; matrix products, arithmetic and copies ran while one was open for 0% -> 0% of each run, Pallas kernels for 26% -> 26%
where the time goes in v16:
time: 118 us; the launch traced here: 116 us
  starting transfers between devices  47.4 us (40%)
  Pallas kernels  32.8 us (28%)
  waiting for transfers between devices  25.4 us (22%)
  local copies, waits for them, and re-layouts  8.35 us (7%)
  between operations  1.5 us (1%)
    all_to_all x4, starting transfers between devices, exchange(): lax.all_to_all(x, ('patch', 'head'), split_axis=0, concat_axis=0, axis_in...  20.5 us
    pallas_call x2, Pallas kernels, attend(): pl.pallas_call(functools.partial(body, len(stale), counts), in_specs=[pl....  16.8 us
    ppermute x6, waiting for transfers between devices, per_device(): lax.ppermute(block, 'patch', way)  15 us
    ppermute x6, starting transfers between devices, per_device(): lax.ppermute(block, 'patch', way)  11.9 us
    ppermute x8, starting transfers between devices, swap(): return lax.ppermute(x, 'patch', swap_pairs)  11 us
    all_to_all x4, waiting for transfers between devices, exchange(): lax.all_to_all(x, ('patch', 'head'), split_axis=0, concat_axis=0, axis_in...  8.82 us
    unnamed x28, local copies, waits for them, and re-layouts  8.27 us
    pallas_call x1, Pallas kernels, project(): pl.pallas_call(functools.partial(project_body, order), in_specs=[vmem, pl...  7.85 us
  transfers between devices with their start and end apart: 19, of which 5 were waited for; matrix products, arithmetic and copies ran while one was open for 0% of the time, Pallas kernels for 26%

profile of v16, /device:TPU:17, one launch (start us, length us, event | category | flops | bytes accessed | tf_op | source)
XLA Modules:
  0.0 116.4 jit_solution(4279379028437706580)
XLA Ops:
  0.7 1.7 %copy-done = bf16[128,9216]{1,0:T(8,128)(2,1)S(1)} copy-done((bf16[128,9216]{1,0:T(8,128)(2,1)S(1)}, bf16[128,9216]{1,0:T(8,128)(2,1)}, u32[]{:S(2)}) %copy-start) | copy-done | bytes 2359320
  2.3 2.9 %pack_heads.2 = bf16[8,64,1152]{2,1,0:T(8,128)(2,1)} custom-call(s32[1]{0:T(128)} %bitcast._, bf16[128,9216]{1,0:T(8,128)(2,1)S(1)} %copy-done, bf16[128,9216]{1,0:T(8,128)(2,1)S(1)} %copy-done, bf16[128,9216]{1,0:T(8,128)(2,1)S(1)} %copy-done), custom_call_target="tpu_custom_call" | custom-call | bytes 2359296 | tf_op jit(solution)/shard_map/pack_heads/pallas_call | solution.py:44
  5.2 4.5 %all-to-all-start = ((bf16[8,64,1152]{2,1,0:T(8,128)(2,1)}), bf16[8,64,1152]{2,1,0:T(8,128)(2,1)S(1)}, u32[]{:S(2)}, u32[]{:S(2)}) async-start(bf16[8,64,1152]{2,1,0:T(8,128)(2,1)} %pack_heads.2), calls=%async_computation | async-start | bytes 2359296 | tf_op jit(solution)/shard_map/all_to_all | solution.py:430
  9.8 2.2 %collective-permute-start.1 = (bf16[2,256,768]{2,1,0:T(8,128)(2,1)S(1)}, bf16[2,256,768]{2,1,0:T(8,128)(2,1)}, u32[]{:S(2)}, u32[]{:S(2)}) collective-permute-start(bf16[2,256,768]{2,1,0:T(8,128)(2,1)S(1)} %copy-done.7), channel_id=1, source_target_pairs={{0,8},{8,16},{16,24},{12,4},{20,12},{28,20},{1,9},{9,17},{17,25},{... | collective-permute-start | bytes 2359304 | tf_op jit(solution)/shard_map/ppermute | solution.py:476
  12.0 2.3 %collective-permute-start.2 = (bf16[2,256,768]{2,1,0:T(8,128)(2,1)S(1)}, bf16[2,256,768]{2,1,0:T(8,128)(2,1)}, u32[]{:S(2)}, u32[]{:S(2)}) collective-permute-start(bf16[2,256,768]{2,1,0:T(8,128)(2,1)S(1)} %copy-done.7), channel_id=1, source_target_pairs={{4,8},{12,16},{20,24},{8,4},{16,12},{24,20},{5,9},{13,17},{21,25},... | collective-permute-start | bytes 2359304 | tf_op jit(solution)/shard_map/ppermute | solution.py:476
  14.3 14.4 %collective-permute-done.1.refs_2_ = bf16[2,256,768]{2,1,0:T(8,128)(2,1)} collective-permute-done((bf16[2,256,768]{2,1,0:T(8,128)(2,1)S(1)}, bf16[2,256,768]{2,1,0:T(8,128)(2,1)}, u32[]{:S(2)}, u32[]{:S(2)}) %collective-permute-start.1) | collective-permute-done | bytes 786464 | tf_op jit(solution)/shard_map/ppermute | solution.py:476
  28.7 2.2 %collective-permute-start.3 = (bf16[2,256,768]{2,1,0:T(8,128)(2,1)}, bf16[2,256,768]{2,1,0:T(8,128)(2,1)}, u32[]{:S(2)}, u32[]{:S(2)}) collective-permute-start(bf16[2,256,768]{2,1,0:T(8,128)(2,1)} %collective-permute-done.1.refs_2_), channel_id=1, source_target_pairs={{8,16},{16,24},{12,4},{20,12},{9,17},{17,25},{13,5},{21,13},{10,18... | collective-permute-start | bytes 2359304 | tf_op jit(solution)/shard_map/ppermute | solution.py:476
  30.9 0.6 collective-permute-done.2.refs_0_
  31.4 1.0 copy-done.1
  32.5 3.0 %collective-permute-start.5 = (bf16[2,256,768]{2,1,0:T(8,128)(2,1)}, bf16[2,256,768]{2,1,0:T(8,128)(2,1)}, u32[]{:S(2)}, u32[]{:S(2)}) collective-permute-start(bf16[2,256,768]{2,1,0:T(8,128)(2,1)} %after.3.refs_3_), channel_id=1, source_target_pairs={{8,16},{16,24},{12,4},{20,12},{9,17},{17,25},{13,5},{21,13},{10,18... | collective-permute-start | bytes 2359304 | tf_op jit(solution)/shard_map/ppermute | solution.py:476
  35.4 1.3 %copy-done.2 = bf16[8,64,1152]{2,1,0:T(8,128)(2,1)S(1)} copy-done((bf16[8,64,1152]{2,1,0:T(8,128)(2,1)S(1)}, bf16[8,64,1152]{2,1,0:T(8,128)(2,1)}, u32[]{:S(2)}) %copy-start.2) | copy-done | bytes 1179672
  36.7 2.9 %pack_heads.3 = bf16[8,64,1152]{2,1,0:T(8,128)(2,1)} custom-call(s32[1]{0:T(128)} %constant.36.clone.1._, bf16[64,9216]{1,0:T(8,128)(2,1)S(1)} %copy-done.4, bf16[64,9216]{1,0:T(8,128)(2,1)S(1)} %copy-done.4, bf16[64,9216]{1,0:T(8,128)(2,1)S(1)} %copy-done.4, bf16[8,64,1152]{2,1,0:T(8,128)(2,1)S(1)} %copy-done.2), custom_call_target="tpu_custom_call" | custom-call | bytes 2359296 | tf_op jit(solution)/shard_map/pack_heads/pallas_call | solution.py:44
  39.6 7.0 %all-to-all-start.1 = ((bf16[8,64,1152]{2,1,0:T(8,128)(2,1)}), bf16[8,64,1152]{2,1,0:T(8,128)(2,1)S(1)}, u32[]{:S(2)}, u32[]{:S(2)}) async-start(bf16[8,64,1152]{2,1,0:T(8,128)(2,1)} %pack_heads.3), calls=%async_computation.1 | async-start | bytes 2359296 | tf_op jit(solution)/shard_map/all_to_all | solution.py:430
  47.7 5.7 %collective-permute-start.7 = (bf16[2,256,768]{2,1,0:T(8,128)(2,1)}, bf16[2,256,768]{2,1,0:T(8,128)(2,1)}, u32[]{:S(2)}, u32[]{:S(2)}) collective-permute-start(bf16[2,256,768]{2,1,0:T(8,128)(2,1)} %collective-permute-done.5.refs_5_.refs_7_), channel_id=1, source_target_pairs={{0,4},{4,0},{8,12},{12,8},{16,20},{20,16},{24,28},{28,24},{1,5},{5... | collective-permute-start | bytes 2359304 | tf_op jit(solution)/shard_map/ppermute | solution.py:435
  53.4 0.7 collective-permute-start.4
  54.1 1.6 %collective-permute-start.11 = (bf16[2,256,768]{2,1,0:T(8,128)(2,1)}, bf16[2,256,768]{2,1,0:T(8,128)(2,1)}, u32[]{:S(2)}, u32[]{:S(2)}) collective-permute-start(bf16[2,256,768]{2,1,0:T(8,128)(2,1)} %collective-permute-done.5.refs_5_.refs_7_), channel_id=1, source_target_pairs={{16,24},{12,4},{17,25},{13,5},{18,26},{14,6},{19,27},{15,7}} | collective-permute-start | bytes 2359304 | tf_op jit(solution)/shard_map/ppermute | solution.py:476
  55.7 7.0 %all-to-all-done.1.refs_10_.img = bf16[8,64,1152]{2,1,0:T(8,128)(2,1)S(1)} async-done(((bf16[8,64,1152]{2,1,0:T(8,128)(2,1)}), bf16[8,64,1152]{2,1,0:T(8,128)(2,1)S(1)}, u32[]{:S(2)}, u32[]{:S(2)}) %all-to-all-start.1) | async-done | bytes 1179680 | tf_op jit(solution)/shard_map/all_to_all | solution.py:430
  62.7 1.1 copy-done.8
  63.8 8.2 %attend_text.1.refs_1_.refs_14_ = bf16[8,64,384]{2,1,0:T(8,128)(2,1)} custom-call(s32[5]{0:T(128)S(1)} %stack.38.info, bf16[8,64,1152]{2,1,0:T(8,128)(2,1)S(1)} %copy-done.3, bf16[2,256,768]{2,1,0:T(8,128)(2,1)S(1)} %copy-done.8, bf16[2,256,768]{2,1,0:T(8,128)(2,1)} %collective-permute-done.refs_1_, bf16[2,256,768]{2,1,0:T(8,128)(2,1)} %collective-permute-done.1.refs_2_, ...), custom_call_target="tpu_custom_call" | custom-call | flops 32212254720 | bytes 62914560 | tf_op jit(solution)/shard_map/attend_text/pallas_call | solution.py:301
  72.0 4.0 %collective-permute-start.12 = (bf16[2,256,768]{2,1,0:T(8,128)(2,1)}, bf16[2,256,768]{2,1,0:T(8,128)(2,1)}, u32[]{:S(2)}, u32[]{:S(2)}) collective-permute-start(bf16[2,256,768]{2,1,0:T(8,128)(2,1)} %after.5.refs_11_), channel_id=1, source_target_pairs={{0,4},{4,0},{8,12},{12,8},{16,20},{20,16},{24,28},{28,24},{1,5},{5... | collective-permute-start | bytes 2359304 | tf_op jit(solution)/shard_map/ppermute | solution.py:435
  76.0 0.9 copy-done.5
  76.9 4.7 %all-to-all-start.3 = ((bf16[8,64,384]{2,1,0:T(8,128)(2,1)}), bf16[8,64,384]{2,1,0:T(8,128)(2,1)S(1)}, u32[]{:S(2)}, u32[]{:S(2)}) async-start(bf16[8,64,384]{2,1,0:T(8,128)(2,1)} %attend_text.1.refs_1_.refs_14_), calls=%async_computation.3 | async-start | bytes 786432 | tf_op jit(solution)/shard_map/all_to_all | solution.py:430
  81.6 1.1 copy-done.6
  82.8 1.1 copy-done.9
  83.9 8.6 %attend_image.1.earlier = bf16[8,64,384]{2,1,0:T(8,128)(2,1)} custom-call(s32[5]{0:T(128)S(1)} %stack.38.info, bf16[8,64,1152]{2,1,0:T(8,128)(2,1)S(1)} %all-to-all-done.1.refs_10_.img, bf16[8,64,1152]{2,1,0:T(8,128)(2,1)S(1)} %copy-done.3, bf16[2,256,768]{2,1,0:T(8,128)(2,1)S(1)} %copy-done.9, bf16[2,256,768]{2,1,0:T(8,128)(2,1)} %collective-permute-done.refs_1_, ...), custom_call_target="tpu_custom_call" | custom-call | flops 2013265920 | bytes 3932160 | tf_op jit(solution)/shard_map/attend_image/pallas_call | solution.py:301
  92.5 4.3 %all-to-all-start.2 = ((bf16[8,64,384]{2,1,0:T(8,128)(2,1)}), bf16[8,64,384]{2,1,0:T(8,128)(2,1)S(1)}, u32[]{:S(2)}, u32[]{:S(2)}) async-start(bf16[8,64,384]{2,1,0:T(8,128)(2,1)} %attend_image.1.earlier), calls=%async_computation.2 | async-start | bytes 786432 | tf_op jit(solution)/shard_map/all_to_all | solution.py:430
  96.8 1.8 %unpack_text.1 = bf16[64,3072]{1,0:T(8,128)(2,1)} custom-call(bf16[8,64,384]{2,1,0:T(8,128)(2,1)} %copy-done.12, bf16[8,64,384]{2,1,0:T(8,128)(2,1)} %attend_image.1.earlier), custom_call_target="tpu_custom_call" | custom-call | tf_op jit(solution)/shard_map/unpack_text/pallas_call | solution.py:371
  98.6 4.0 %collective-permute-start.13 = (bf16[64,3072]{1,0:T(8,128)(2,1)}, bf16[64,3072]{1,0:T(8,128)(2,1)S(1)}, u32[]{:S(2)}, u32[]{:S(2)}) collective-permute-start(bf16[64,3072]{1,0:T(8,128)(2,1)} %unpack_text.1), channel_id=1, source_target_pairs={{8,0},{12,4},{16,24},{20,28},{9,1},{13,5},{17,25},{21,29},{10,2},{... | collective-permute-start | bytes 1179656 | tf_op jit(solution)/shard_map/ppermute | solution.py:504
  102.6 1.9 %all-to-all-done.2.x_ref = bf16[8,64,384]{2,1,0:T(8,128)(2,1)S(1)} async-done(((bf16[8,64,384]{2,1,0:T(8,128)(2,1)}), bf16[8,64,384]{2,1,0:T(8,128)(2,1)S(1)}, u32[]{:S(2)}, u32[]{:S(2)}) %all-to-all-start.2) | async-done | bytes 393248 | tf_op jit(solution)/shard_map/all_to_all | solution.py:430
  104.5 7.9 %project.1.earlier = bf16[64,3072]{1,0:T(8,128)(2,1)} custom-call(bf16[8,64,384]{2,1,0:T(8,128)(2,1)S(1)} %all-to-all-done.2.x_ref, bf16[8,384,3072]{2,1,0:T(8,128)(2,1)} %bitcast.9, bf16[64,3072]{1,0:T(8,128)(2,1)S(1)} %copy-done.10, f32[1,3072]{1,0:T(1,128)S(1)} %bitcast.8), custom_call_target="tpu_custom_call" | custom-call | flops 1207959552 | bytes 18874368 | tf_op jit(solution)/shard_map/project/pallas_call | solution.py:343
  113.9 1.5 %collective-permute-done.14 = bf16[64,3072]{1,0:T(8,128)(2,1)S(1)} collective-permute-done((bf16[64,3072]{1,0:T(8,128)(2,1)S(1)}, bf16[64,3072]{1,0:T(8,128)(2,1)S(1)}, u32[]{:S(2)}, u32[]{:S(2)}) %collective-permute-start.14) | collective-permute-done | bytes 393248 | tf_op jit(solution)/shard_map/ppermute | solution.py:435
  115.4 0.9 pad_maximum_fusion
  (48 shorter events, 2.1 us)
Async XLA Ops:
  0.6 1.7 %copy-start = (bf16[128,9216]{1,0:T(8,128)(2,1)S(1)}, bf16[128,9216]{1,0:T(8,128)(2,1)}, u32[]{:S(2)}) copy-start(bf16[128,9216]{1,0:T(8,128)(2,1)} %refs_2_.2) | copy-start | bytes 7077892
  5.2 4.5 %copy-start.7 = (bf16[2,256,768]{2,1,0:T(8,128)(2,1)S(1)}, bf16[2,256,768]{2,1,0:T(8,128)(2,1)}, u32[]{:S(2)}) copy-start(bf16[2,256,768]{2,1,0:T(8,128)(2,1)} %refs_0_.7) | copy-start | bytes 2359300
  5.2 26.2 %all-to-all-start = ((bf16[8,64,1152]{2,1,0:T(8,128)(2,1)}), bf16[8,64,1152]{2,1,0:T(8,128)(2,1)S(1)}, u32[]{:S(2)}, u32[]{:S(2)}) async-start(bf16[8,64,1152]{2,1,0:T(8,128)(2,1)} %pack_heads.2), calls=%async_computation | async-start | bytes 2359296 | tf_op jit(solution)/shard_map/all_to_all | solution.py:430
  9.7 25.7 %copy-start.4 = (bf16[64,9216]{1,0:T(8,128)(2,1)S(1)}, bf16[64,9216]{1,0:T(8,128)(2,1)}, u32[]{:S(2)}) copy-start(bf16[64,9216]{1,0:T(8,128)(2,1)} %refs_2_.3) | copy-start | bytes 3538948
  9.8 19.0 %collective-permute-start.1 = (bf16[2,256,768]{2,1,0:T(8,128)(2,1)S(1)}, bf16[2,256,768]{2,1,0:T(8,128)(2,1)}, u32[]{:S(2)}, u32[]{:S(2)}) collective-permute-start(bf16[2,256,768]{2,1,0:T(8,128)(2,1)S(1)} %copy-done.7), channel_id=1, source_target_pairs={{0,8},{8,16},{16,24},{12,4},{20,12},{28,20},{1,9},{9,17},{17,25},{... | collective-permute-start | bytes 2359304 | tf_op jit(solution)/shard_map/ppermute | solution.py:476
  12.0 19.5 %collective-permute-start.2 = (bf16[2,256,768]{2,1,0:T(8,128)(2,1)S(1)}, bf16[2,256,768]{2,1,0:T(8,128)(2,1)}, u32[]{:S(2)}, u32[]{:S(2)}) collective-permute-start(bf16[2,256,768]{2,1,0:T(8,128)(2,1)S(1)} %copy-done.7), channel_id=1, source_target_pairs={{4,8},{12,16},{20,24},{8,4},{16,12},{24,20},{5,9},{13,17},{21,25},... | collective-permute-start | bytes 2359304 | tf_op jit(solution)/shard_map/ppermute | solution.py:476
  28.7 18.4 %collective-permute-start.3 = (bf16[2,256,768]{2,1,0:T(8,128)(2,1)}, bf16[2,256,768]{2,1,0:T(8,128)(2,1)}, u32[]{:S(2)}, u32[]{:S(2)}) collective-permute-start(bf16[2,256,768]{2,1,0:T(8,128)(2,1)} %collective-permute-done.1.refs_2_), channel_id=1, source_target_pairs={{8,16},{16,24},{12,4},{20,12},{9,17},{17,25},{13,5},{21,13},{10,18... | collective-permute-start | bytes 2359304 | tf_op jit(solution)/shard_map/ppermute | solution.py:476
  31.4 1.0 copy-start.1
  32.5 15.2 %collective-permute-start.5 = (bf16[2,256,768]{2,1,0:T(8,128)(2,1)}, bf16[2,256,768]{2,1,0:T(8,128)(2,1)}, u32[]{:S(2)}, u32[]{:S(2)}) collective-permute-start(bf16[2,256,768]{2,1,0:T(8,128)(2,1)} %after.3.refs_3_), channel_id=1, source_target_pairs={{8,16},{16,24},{12,4},{20,12},{9,17},{17,25},{13,5},{21,13},{10,18... | collective-permute-start | bytes 2359304 | tf_op jit(solution)/shard_map/ppermute | solution.py:476
  35.4 1.3 %copy-start.2 = (bf16[8,64,1152]{2,1,0:T(8,128)(2,1)S(1)}, bf16[8,64,1152]{2,1,0:T(8,128)(2,1)}, u32[]{:S(2)}) copy-start(bf16[8,64,1152]{2,1,0:T(8,128)(2,1)} %copy-done.1) | copy-start | bytes 3538948
  39.6 23.0 %copy-start.3 = (bf16[8,64,1152]{2,1,0:T(8,128)(2,1)S(1)}, bf16[8,64,1152]{2,1,0:T(8,128)(2,1)}, u32[]{:S(2)}) copy-start(bf16[8,64,1152]{2,1,0:T(8,128)(2,1)} %copy-done.1) | copy-start | bytes 3538948
  39.6 23.0 %all-to-all-start.1 = ((bf16[8,64,1152]{2,1,0:T(8,128)(2,1)}), bf16[8,64,1152]{2,1,0:T(8,128)(2,1)S(1)}, u32[]{:S(2)}, u32[]{:S(2)}) async-start(bf16[8,64,1152]{2,1,0:T(8,128)(2,1)} %pack_heads.3), calls=%async_computation.1 | async-start | bytes 2359296 | tf_op jit(solution)/shard_map/all_to_all | solution.py:430
  46.6 6.8 %collective-permute-start = (bf16[2,256,768]{2,1,0:T(8,128)(2,1)S(1)}, bf16[2,256,768]{2,1,0:T(8,128)(2,1)}, u32[]{:S(2)}, u32[]{:S(2)}) collective-permute-start(bf16[2,256,768]{2,1,0:T(8,128)(2,1)S(1)} %copy-done.7), channel_id=1, source_target_pairs={{0,4},{4,0},{8,12},{12,8},{16,20},{20,16},{24,28},{28,24},{1,5},{5... | collective-permute-start | bytes 2359304 | tf_op jit(solution)/shard_map/ppermute | solution.py:435
  46.6 7.5 %collective-permute-start.8 = (bf16[2,256,768]{2,1,0:T(8,128)(2,1)}, bf16[2,256,768]{2,1,0:T(8,128)(2,1)}, u32[]{:S(2)}, u32[]{:S(2)}) collective-permute-start(bf16[2,256,768]{2,1,0:T(8,128)(2,1)} %collective-permute-done.1.refs_2_), channel_id=1, source_target_pairs={{0,4},{4,0},{8,12},{12,8},{16,20},{20,16},{24,28},{28,24},{1,5},{5... | collective-permute-start | bytes 2359304 | tf_op jit(solution)/shard_map/ppermute | solution.py:435
  47.1 8.6 %collective-permute-start.9 = (bf16[2,256,768]{2,1,0:T(8,128)(2,1)}, bf16[2,256,768]{2,1,0:T(8,128)(2,1)}, u32[]{:S(2)}, u32[]{:S(2)}) collective-permute-start(bf16[2,256,768]{2,1,0:T(8,128)(2,1)} %after.3.refs_3_), channel_id=1, source_target_pairs={{0,4},{4,0},{8,12},{12,8},{16,20},{20,16},{24,28},{28,24},{1,5},{5... | collective-permute-start | bytes 2359304 | tf_op jit(solution)/shard_map/ppermute | solution.py:435
  47.1 15.6 %collective-permute-start.6 = (bf16[2,256,768]{2,1,0:T(8,128)(2,1)}, bf16[2,256,768]{2,1,0:T(8,128)(2,1)}, u32[]{:S(2)}, u32[]{:S(2)}) collective-permute-start(bf16[2,256,768]{2,1,0:T(8,128)(2,1)} %collective-permute-done.3.refs_4_.refs_6_), channel_id=1, source_target_pairs={{0,4},{4,0},{8,12},{12,8},{16,20},{20,16},{24,28},{28,24},{1,5},{5... | collective-permute-start | bytes 2359304 | tf_op jit(solution)/shard_map/ppermute | solution.py:435
  47.7 15.0 %collective-permute-start.7 = (bf16[2,256,768]{2,1,0:T(8,128)(2,1)}, bf16[2,256,768]{2,1,0:T(8,128)(2,1)}, u32[]{:S(2)}, u32[]{:S(2)}) collective-permute-start(bf16[2,256,768]{2,1,0:T(8,128)(2,1)} %collective-permute-done.5.refs_5_.refs_7_), channel_id=1, source_target_pairs={{0,4},{4,0},{8,12},{12,8},{16,20},{20,16},{24,28},{28,24},{1,5},{5... | collective-permute-start | bytes 2359304 | tf_op jit(solution)/shard_map/ppermute | solution.py:435
  53.4 22.6 %collective-permute-start.4 = (bf16[2,256,768]{2,1,0:T(8,128)(2,1)}, bf16[2,256,768]{2,1,0:T(8,128)(2,1)S(1)}, u32[]{:S(2)}, u32[]{:S(2)}) collective-permute-start(bf16[2,256,768]{2,1,0:T(8,128)(2,1)} %collective-permute-done.3.refs_4_.refs_6_), channel_id=1, source_target_pairs={{16,24},{12,4},{17,25},{13,5},{18,26},{14,6},{19,27},{15,7}} | collective-permute-start | bytes 2359304 | tf_op jit(solution)/shard_map/ppermute | solution.py:476
  54.1 17.9 %collective-permute-start.11 = (bf16[2,256,768]{2,1,0:T(8,128)(2,1)}, bf16[2,256,768]{2,1,0:T(8,128)(2,1)}, u32[]{:S(2)}, u32[]{:S(2)}) collective-permute-start(bf16[2,256,768]{2,1,0:T(8,128)(2,1)} %collective-permute-done.5.refs_5_.refs_7_), channel_id=1, source_target_pairs={{16,24},{12,4},{17,25},{13,5},{18,26},{14,6},{19,27},{15,7}} | collective-permute-start | bytes 2359304 | tf_op jit(solution)/shard_map/ppermute | solution.py:476
  62.7 1.1 copy-start.8
  72.0 9.6 %collective-permute-start.12 = (bf16[2,256,768]{2,1,0:T(8,128)(2,1)}, bf16[2,256,768]{2,1,0:T(8,128)(2,1)}, u32[]{:S(2)}, u32[]{:S(2)}) collective-permute-start(bf16[2,256,768]{2,1,0:T(8,128)(2,1)} %after.5.refs_11_), channel_id=1, source_target_pairs={{0,4},{4,0},{8,12},{12,8},{16,20},{20,16},{24,28},{28,24},{1,5},{5... | collective-permute-start | bytes 2359304 | tf_op jit(solution)/shard_map/ppermute | solution.py:435
  76.9 4.7 %collective-permute-start.10 = (bf16[2,256,768]{2,1,0:T(8,128)(2,1)}, bf16[2,256,768]{2,1,0:T(8,128)(2,1)S(1)}, u32[]{:S(2)}, u32[]{:S(2)}) collective-permute-start(bf16[2,256,768]{2,1,0:T(8,128)(2,1)} %after.4.refs_10_), channel_id=1, source_target_pairs={{0,4},{4,0},{8,12},{12,8},{16,20},{20,16},{24,28},{28,24},{1,5},{5... | collective-permute-start | bytes 2359304 | tf_op jit(solution)/shard_map/ppermute | solution.py:435
  76.9 15.6 %all-to-all-start.3 = ((bf16[8,64,384]{2,1,0:T(8,128)(2,1)}), bf16[8,64,384]{2,1,0:T(8,128)(2,1)S(1)}, u32[]{:S(2)}, u32[]{:S(2)}) async-start(bf16[8,64,384]{2,1,0:T(8,128)(2,1)} %attend_text.1.refs_1_.refs_14_), calls=%async_computation.3 | async-start | bytes 786432 | tf_op jit(solution)/shard_map/all_to_all | solution.py:430
  81.6 1.1 copy-start.6
  82.8 1.1 copy-start.9
  92.5 12.0 %copy-start.10 = (bf16[64,3072]{1,0:T(8,128)(2,1)S(1)}, bf16[64,3072]{1,0:T(8,128)(2,1)}, u32[]{:S(2)}) copy-start(bf16[64,3072]{1,0:T(8,128)(2,1)} %residual.1) | copy-start | bytes 1179652
  92.5 12.0 %copy-start.11 = (f32[3072]{0:T(1024)S(1)}, f32[3072]{0:T(1024)}, u32[]{:S(2)}) copy-start(f32[3072]{0:T(1024)} %param.10) | copy-start | bytes 36868
  92.5 4.3 %copy-start.12 = (bf16[8,64,384]{2,1,0:T(8,128)(2,1)}, bf16[8,64,384]{2,1,0:T(8,128)(2,1)S(1)}, u32[]{:S(2)}) copy-start(bf16[8,64,384]{2,1,0:T(8,128)(2,1)S(1)} %all-to-all-done.3.x_ref) | copy-start | bytes 1179652
  92.5 11.9 %all-to-all-start.2 = ((bf16[8,64,384]{2,1,0:T(8,128)(2,1)}), bf16[8,64,384]{2,1,0:T(8,128)(2,1)S(1)}, u32[]{:S(2)}, u32[]{:S(2)}) async-start(bf16[8,64,384]{2,1,0:T(8,128)(2,1)} %attend_image.1.earlier), calls=%async_computation.2 | async-start | bytes 786432 | tf_op jit(solution)/shard_map/all_to_all | solution.py:430
  98.6 14.9 %collective-permute-start.13 = (bf16[64,3072]{1,0:T(8,128)(2,1)}, bf16[64,3072]{1,0:T(8,128)(2,1)S(1)}, u32[]{:S(2)}, u32[]{:S(2)}) collective-permute-start(bf16[64,3072]{1,0:T(8,128)(2,1)} %unpack_text.1), channel_id=1, source_target_pairs={{8,0},{12,4},{16,24},{20,28},{9,1},{13,5},{17,25},{21,29},{10,2},{... | collective-permute-start | bytes 1179656 | tf_op jit(solution)/shard_map/ppermute | solution.py:504
  104.5 9.1 %copy-start.13 = (bf16[64,3072]{1,0:T(8,128)(2,1)S(1)}, bf16[64,3072]{1,0:T(8,128)(2,1)}, u32[]{:S(2)}) copy-start(bf16[64,3072]{1,0:T(8,128)(2,1)} %unpack_text.1) | copy-start | bytes 1179652
  113.6 1.8 %collective-permute-start.14 = (bf16[64,3072]{1,0:T(8,128)(2,1)S(1)}, bf16[64,3072]{1,0:T(8,128)(2,1)S(1)}, u32[]{:S(2)}, u32[]{:S(2)}) collective-permute-start(bf16[64,3072]{1,0:T(8,128)(2,1)S(1)} %broadcast_select_fusion), channel_id=1, source_target_pairs={{0,4},{4,0},{8,12},{12,8},{16,20},{20,16},{24,28},{28,24},{1,5},{5... | collective-permute-start | bytes 1179656 | tf_op jit(solution)/shard_map/ppermute | solution.py:435
  (1 other events, 0.9 us)

commit v17 on v2

--- a/solution.py
+++ b/solution.py
@@ -11,6 +11,7 @@
 HD = 128
 SCALE = math.log2(math.e) / math.sqrt(HD)
 VMEM_LIMIT = 24 * 1024 * 1024
+WIDE_LIMIT = 48 * 1024 * 1024
 TILE = 256
 LARGE = 2.0**60
 
@@ -330,38 +331,44 @@
     )(info, qkv, *state, *blocks)
 
 
-def project_body(order, x_ref, weight, residual, gate, out, flat):
-    @pl.when(pl.program_id(0) == 0)
-    def _():
-        rows, width = flat.shape[0], x_ref.shape[2]
-        for source, place in enumerate(order):
-            flat[:, place * width : (place + 1) * width] = x_ref[source, :rows, :]
-
-    projected = jnp.dot(flat[...], weight[...], preferred_element_type=jnp.float32)
-    out[...] = (residual[...].astype(jnp.float32) + gate[...] * projected).astype(out.dtype)
+def project_body(order, x_ref, weight, residual, gate, out, held, total, sems):
+    rows = out.shape[0]
+    copies = [
+        pltpu.make_async_copy(weight.at[place], held.at[place], sems.at[place])
+        for place in order
+    ]
+    for copy in copies:
+        copy.start()
+    for source, (place, copy) in enumerate(zip(order, copies)):
+        copy.wait()
+        part = jnp.dot(x_ref[source, :rows, :], held[place], preferred_element_type=jnp.float32)
+        if source == 0:
+            total[...] = part
+        else:
+            total[...] += part
+    out[...] = (residual[...].astype(jnp.float32) + gate[...] * total[...]).astype(out.dtype)
 
 
 def project(x, order, weight, residual, gate):
     rows, model = residual.shape
-    columns = 512 if model % 512 == 0 else HD
+    destinations, _, width = x.shape
+    vmem = pl.BlockSpec(memory_space=pltpu.VMEM)
     return pl.pallas_call(
         functools.partial(project_body, order),
-        grid=(model // columns,),
-        in_specs=[
-            pl.BlockSpec(x.shape, lambda n: (0, 0, 0)),
-            pl.BlockSpec((weight.shape[0], columns), lambda n: (0, n)),
-            pl.BlockSpec((rows, columns), lambda n: (0, n)),
-            pl.BlockSpec((1, columns), lambda n: (0, n)),
+        in_specs=[vmem, pl.BlockSpec(memory_space=pl.ANY), vmem, vmem],
+        out_specs=vmem,
+        out_shape=jax.ShapeDtypeStruct((rows, model), residual.dtype),
+        scratch_shapes=[
+            pltpu.VMEM((destinations, width, model), weight.dtype),
+            pltpu.VMEM((rows, model), jnp.float32),
+            pltpu.SemaphoreType.DMA((destinations,)),
         ],
-        out_specs=pl.BlockSpec((rows, columns), lambda n: (0, n)),
-        out_shape=jax.ShapeDtypeStruct((rows, model), residual.dtype),
-        scratch_shapes=[pltpu.VMEM((rows, weight.shape[0]), x.dtype)],
-        compiler_params=params(),
+        compiler_params=pltpu.CompilerParams(vmem_limit_bytes=WIDE_LIMIT),
         cost_estimate=pl.CostEstimate(
             flops=2 * rows * model * model, bytes_accessed=2 * model * model, transcendentals=0
         ),
         name="project",
-    )(x, weight, residual, gate.reshape(1, model))
+    )(x, weight.reshape(destinations, width, model), residual, gate.reshape(1, model))
 
 
 def unpack_body(order, first, x_ref, out):

time: 114 us -> 109 us (0.956)
  local copies, waits for them, and re-layouts: 16.1 us -> 9.68 us
  Pallas kernels: 27.3 us -> 29.1 us
    unnamed x24 -> x22, local copies, waits for them, and re-layouts: 14.7 us -> 8.31 us
    pallas_call x1, Pallas kernels: 5.98 us -> 7.82 us  [project(): pl.pallas_call(functools.partial(project_body, order), in_specs=[vmem, pl...]
  transfers between devices with their start and end apart: 15 -> 15, of which waited for: 4 -> 4; matrix products, arithmetic and copies ran while one was open for 0% -> 0% of each run, Pallas kernels for 20% -> 22%
where the time goes in v17:
time: 109 us; the launch traced here: 108 us
  starting transfers between devices  37.2 us (34%)
  Pallas kernels  29.1 us (27%)
  blocking collectives  18.1 us (17%)
  waiting for transfers between devices  12.3 us (11%)
  local copies, waits for them, and re-layouts  9.68 us (9%)
    all_to_all x1, blocking collectives, exchange(): lax.all_to_all(x, ('patch', 'head'), split_axis=0, concat_axis=0, axis_in...  18.1 us
    ppermute x6, starting transfers between devices, per_device(): lax.ppermute(block, 'patch', right_pairs)  17.4 us
    pallas_call x1, Pallas kernels, attend_most(): pl.pallas_call(functools.partial(most_body, len(stale), img_rows, len(arr...  16.4 us
    ppermute x6, starting transfers between devices, per_device(): lax.ppermute(block, 'patch', left_pairs)  14.6 us
    ppermute x6, waiting for transfers between devices, per_device(): lax.ppermute(block, 'patch', right_pairs)  8.91 us
    unnamed x22, local copies, waits for them, and re-layouts  8.31 us
    pallas_call x1, Pallas kernels, project(): pl.pallas_call(functools.partial(project_body, order), in_specs=[vmem, pl...  7.82 us
    all_to_all x1, starting transfers between devices, exchange(): lax.all_to_all(x, ('patch', 'head'), split_axis=0, concat_axis=0, axis_in...  4.09 us
  transfers between devices with their start and end apart: 15, of which 4 were waited for; matrix products, arithmetic and copies ran while one was open for 0% of the time, Pallas kernels for 22%

profile of v17, /device:TPU:17, one launch (start us, length us, event | category | flops | bytes accessed | tf_op | source)
XLA Modules:
  0.0 108.4 jit_solution(1362349529425893079)
XLA Ops:
  0.7 1.3 %constant_dynamic-slice_fusion = (bf16[2,256,384]{2,1,0:T(8,128)(2,1)S(1)}, bf16[2,256,384]{2,1,0:T(8,128)(2,1)S(1)}) fusion(bf16[2,256,768]{2,1,0:T(8,128)(2,1)} %param.8, s32[]{:T(128)S(6)} %select_n.32, s32[]{:T(128)S(6)} %select_n.31), kind=kLoop, calls=%fused_computation.4 | loop fusion | bytes 1572872 | tf_op jit(solution)/shard_map/dynamic_slice | solution.py:417
  2.0 0.7 collective-permute-start
  2.7 1.3 %collective-permute-done.refs_6_.refs_4_ = bf16[2,256,384]{2,1,0:T(8,128)(2,1)S(1)} collective-permute-done((bf16[2,256,384]{2,1,0:T(8,128)(2,1)S(1)}, bf16[2,256,384]{2,1,0:T(8,128)(2,1)S(1)}, u32[]{:S(2)}, u32[]{:S(2)}) %collective-permute-start) | collective-permute-done | bytes 393248 | tf_op jit(solution)/shard_map/ppermute | solution.py:420
  4.1 1.7 %copy-done = bf16[128,9216]{1,0:T(8,128)(2,1)S(1)} copy-done((bf16[128,9216]{1,0:T(8,128)(2,1)S(1)}, bf16[128,9216]{1,0:T(8,128)(2,1)}, u32[]{:S(2)}) %copy-start) | copy-done | bytes 2359320
  5.7 1.0 pack_heads.1
  6.8 1.4 %copy-done.2 = bf16[8,128,1152]{2,1,0:T(8,128)(2,1)} copy-done((bf16[8,128,1152]{2,1,0:T(8,128)(2,1)}, bf16[8,128,1152]{2,1,0:T(8,128)(2,1)S(1)}, u32[]{:S(2)}) %copy-start.2) | copy-done | bytes 2359320
  8.2 4.1 %all-to-all-start = ((bf16[8,128,1152]{2,1,0:T(8,128)(2,1)}), bf16[8,128,1152]{2,1,0:T(8,128)(2,1)S(1)}, u32[]{:S(2)}, u32[]{:S(2)}) async-start(bf16[8,128,1152]{2,1,0:T(8,128)(2,1)} %copy-done.2), calls=%async_computation | async-start | bytes 4718592 | tf_op jit(solution)/shard_map/all_to_all | solution.py:412
  12.3 2.1 %collective-permute-start.3 = (bf16[2,256,384]{2,1,0:T(8,128)(2,1)S(1)}, bf16[2,256,384]{2,1,0:T(8,128)(2,1)S(1)}, u32[]{:S(2)}, u32[]{:S(2)}) collective-permute-start(bf16[2,256,384]{2,1,0:T(8,128)(2,1)S(1)} %get-tuple-element.8.refs_3_), channel_id=1, source_target_pairs={{8,0},{12,4},{16,8},{20,12},{24,16},{28,20},{9,1},{13,5},{17,9},{2... | collective-permute-start | bytes 1179656 | tf_op jit(solution)/shard_map/ppermute | solution.py:433
  14.3 3.2 %collective-permute-start.1 = (bf16[2,256,384]{2,1,0:T(8,128)(2,1)S(1)}, bf16[2,256,384]{2,1,0:T(8,128)(2,1)S(1)}, u32[]{:S(2)}, u32[]{:S(2)}) collective-permute-start(bf16[2,256,384]{2,1,0:T(8,128)(2,1)S(1)} %get-tuple-element.8.refs_3_), channel_id=1, source_target_pairs={{0,8},{4,12},{8,16},{12,20},{16,24},{20,28},{1,9},{5,13},{9,17},{1... | collective-permute-start | bytes 1179656 | tf_op jit(solution)/shard_map/ppermute | solution.py:432
  17.6 1.9 %collective-permute-start.2 = (bf16[2,256,384]{2,1,0:T(8,128)(2,1)S(1)}, bf16[2,256,384]{2,1,0:T(8,128)(2,1)S(1)}, u32[]{:S(2)}, u32[]{:S(2)}) collective-permute-start(bf16[2,256,384]{2,1,0:T(8,128)(2,1)S(1)} %collective-permute-done.refs_6_.refs_4_), channel_id=1, source_target_pairs={{0,8},{4,12},{8,16},{12,20},{16,24},{20,28},{1,9},{5,13},{9,17},{1... | collective-permute-start | bytes 1179656 | tf_op jit(solution)/shard_map/ppermute | solution.py:432
  19.5 3.4 %collective-permute-start.4 = (bf16[2,256,384]{2,1,0:T(8,128)(2,1)S(1)}, bf16[2,256,384]{2,1,0:T(8,128)(2,1)S(1)}, u32[]{:S(2)}, u32[]{:S(2)}) collective-permute-start(bf16[2,256,384]{2,1,0:T(8,128)(2,1)S(1)} %collective-permute-done.refs_6_.refs_4_), channel_id=1, source_target_pairs={{8,0},{12,4},{16,8},{20,12},{24,16},{28,20},{9,1},{13,5},{17,9},{2... | collective-permute-start | bytes 1179656 | tf_op jit(solution)/shard_map/ppermute | solution.py:433
  22.9 2.0 %collective-permute-done.3.refs_7_ = bf16[2,256,384]{2,1,0:T(8,128)(2,1)S(1)} collective-permute-done((bf16[2,256,384]{2,1,0:T(8,128)(2,1)S(1)}, bf16[2,256,384]{2,1,0:T(8,128)(2,1)S(1)}, u32[]{:S(2)}, u32[]{:S(2)}) %collective-permute-start.3) | collective-permute-done | bytes 393248 | tf_op jit(solution)/shard_map/ppermute | solution.py:433
  24.9 2.8 %collective-permute-start.7 = (bf16[2,256,384]{2,1,0:T(8,128)(2,1)S(1)}, bf16[2,256,384]{2,1,0:T(8,128)(2,1)}, u32[]{:S(2)}, u32[]{:S(2)}) collective-permute-start(bf16[2,256,384]{2,1,0:T(8,128)(2,1)S(1)} %collective-permute-done.3.refs_7_), channel_id=1, source_target_pairs={{8,0},{12,4},{16,8},{20,12},{9,1},{13,5},{17,9},{21,13},{10,2},{14... | collective-permute-start | bytes 1179656 | tf_op jit(solution)/shard_map/ppermute | solution.py:433
  27.7 2.2 %collective-permute-start.5 = (bf16[2,256,384]{2,1,0:T(8,128)(2,1)S(1)}, bf16[2,256,384]{2,1,0:T(8,128)(2,1)}, u32[]{:S(2)}, u32[]{:S(2)}) collective-permute-start(bf16[2,256,384]{2,1,0:T(8,128)(2,1)S(1)} %collective-permute-done.1.refs_5_), channel_id=1, source_target_pairs={{8,16},{12,20},{16,24},{20,28},{9,17},{13,21},{17,25},{21,29},{10,... | collective-permute-start | bytes 1179656 | tf_op jit(solution)/shard_map/ppermute | solution.py:432
  29.9 0.7 copy-done.3
  30.6 4.5 %collective-permute-done.2.refs_6_ = bf16[2,256,384]{2,1,0:T(8,128)(2,1)S(1)} collective-permute-done((bf16[2,256,384]{2,1,0:T(8,128)(2,1)S(1)}, bf16[2,256,384]{2,1,0:T(8,128)(2,1)S(1)}, u32[]{:S(2)}, u32[]{:S(2)}) %collective-permute-start.2) | collective-permute-done | bytes 393248 | tf_op jit(solution)/shard_map/ppermute | solution.py:432
  35.1 3.2 %collective-permute-start.6 = (bf16[2,256,384]{2,1,0:T(8,128)(2,1)S(1)}, bf16[2,256,384]{2,1,0:T(8,128)(2,1)}, u32[]{:S(2)}, u32[]{:S(2)}) collective-permute-start(bf16[2,256,384]{2,1,0:T(8,128)(2,1)S(1)} %collective-permute-done.2.refs_6_), channel_id=1, source_target_pairs={{8,16},{12,20},{16,24},{20,28},{9,17},{13,21},{17,25},{21,29},{10,... | collective-permute-start | bytes 1179656 | tf_op jit(solution)/shard_map/ppermute | solution.py:432
  38.3 0.7 copy-done.5
  39.1 3.5 %collective-permute-start.8 = (bf16[2,256,384]{2,1,0:T(8,128)(2,1)S(1)}, bf16[2,256,384]{2,1,0:T(8,128)(2,1)}, u32[]{:S(2)}, u32[]{:S(2)}) collective-permute-start(bf16[2,256,384]{2,1,0:T(8,128)(2,1)S(1)} %collective-permute-done.4.refs_8_), channel_id=1, source_target_pairs={{8,0},{12,4},{16,8},{20,12},{9,1},{13,5},{17,9},{21,13},{10,2},{14... | collective-permute-start | bytes 1179656 | tf_op jit(solution)/shard_map/ppermute | solution.py:433
  43.3 1.4 %collective-permute-start.11 = (bf16[2,256,384]{2,1,0:T(8,128)(2,1)}, bf16[2,256,384]{2,1,0:T(8,128)(2,1)}, u32[]{:S(2)}, u32[]{:S(2)}) collective-permute-start(bf16[2,256,384]{2,1,0:T(8,128)(2,1)} %collective-permute-done.7.refs_11_), channel_id=1, source_target_pairs={{8,0},{12,4},{9,1},{13,5},{10,2},{14,6},{11,3},{15,7}} | collective-permute-start | bytes 1179656 | tf_op jit(solution)/shard_map/ppermute | solution.py:433
  44.7 2.9 %collective-permute-start.9 = (bf16[2,256,384]{2,1,0:T(8,128)(2,1)}, bf16[2,256,384]{2,1,0:T(8,128)(2,1)}, u32[]{:S(2)}, u32[]{:S(2)}) collective-permute-start(bf16[2,256,384]{2,1,0:T(8,128)(2,1)} %collective-permute-done.5.refs_9_), channel_id=1, source_target_pairs={{16,24},{20,28},{17,25},{21,29},{18,26},{22,30},{19,27},{23,31}} | collective-permute-start | bytes 1179656 | tf_op jit(solution)/shard_map/ppermute | solution.py:432
  47.6 4.4 %collective-permute-done.6.refs_10_ = bf16[2,256,384]{2,1,0:T(8,128)(2,1)} collective-permute-done((bf16[2,256,384]{2,1,0:T(8,128)(2,1)S(1)}, bf16[2,256,384]{2,1,0:T(8,128)(2,1)}, u32[]{:S(2)}, u32[]{:S(2)}) %collective-permute-start.6) | collective-permute-done | bytes 393248 | tf_op jit(solution)/shard_map/ppermute | solution.py:432
  52.0 4.0 %collective-permute-start.10 = (bf16[2,256,384]{2,1,0:T(8,128)(2,1)}, bf16[2,256,384]{2,1,0:T(8,128)(2,1)}, u32[]{:S(2)}, u32[]{:S(2)}) collective-permute-start(bf16[2,256,384]{2,1,0:T(8,128)(2,1)} %collective-permute-done.6.refs_10_), channel_id=1, source_target_pairs={{16,24},{20,28},{17,25},{21,29},{18,26},{22,30},{19,27},{23,31}} | collective-permute-start | bytes 1179656 | tf_op jit(solution)/shard_map/ppermute | solution.py:432
  56.0 1.4 %collective-permute-start.12 = (bf16[2,256,384]{2,1,0:T(8,128)(2,1)}, bf16[2,256,384]{2,1,0:T(8,128)(2,1)}, u32[]{:S(2)}, u32[]{:S(2)}) collective-permute-start(bf16[2,256,384]{2,1,0:T(8,128)(2,1)} %collective-permute-done.8.refs_12_), channel_id=1, source_target_pairs={{8,0},{12,4},{9,1},{13,5},{10,2},{14,6},{11,3},{15,7}} | collective-permute-start | bytes 1179656 | tf_op jit(solution)/shard_map/ppermute | solution.py:433
  57.6 1.0 copy-done.4
  58.6 1.0 copy-done.6
  59.6 1.0 copy-done.8
  60.6 16.4 %attend_most.1 = (bf16[3,1024,128]{2,1,0:T(8,128)(2,1)S(1)}, f32[3,1024,256]{2,1,0:T(8,128)S(1)}) custom-call(s32[5]{0:T(128)S(1)} %stack.60.info, bf16[8,128,1152]{2,1,0:T(8,128)(2,1)S(1)} %all-to-all-done.refs_0_.refs_1_.refs_2_, bf16[8,128,1152]{2,1,0:T(8,128)(2,1)S(1)} %all-to-all-done.refs_0_.refs_1_.refs_2_, ...), custom_call_target="tpu_custom_call" | custom-call | flops 2818572288 | bytes 4325376 | tf_op jit(solution)/shard_map/attend_most/pallas_call | solution.py:232
  77.1 3.9 %attend_last.1 = bf16[8,128,384]{2,1,0:T(8,128)(2,1)S(1)} custom-call(s32[3]{0:T(128)S(1)} %pad_add_fusion.info, bf16[8,128,1152]{2,1,0:T(8,128)(2,1)S(1)} %all-to-all-done.refs_0_.refs_1_.refs_2_, bf16[3,1024,128]{2,1,0:T(8,128)(2,1)S(1)} %get-tuple-element.4.refs_1_, f32[3,1024,256]{2,1,0:T(8,128)S(1)} %get-tuple-element.5.refs_2_, ...), custom_call_target="tpu_custom_call" | custom-call | flops 805306368 | bytes 2359296 | tf_op jit(solution)/shard_map/attend_last/pallas_call | solution.py:312
  81.0 18.1 %all_to_all.10.x_ref = bf16[8,128,384]{2,1,0:T(8,128)(2,1)S(1)} all-to-all(bf16[8,128,384]{2,1,0:T(8,128)(2,1)S(1)} %attend_last.1), channel_id=1, replica_groups={{0,1,2,3,4,5,6,7},{8,9,10,11,12,13,14,15},{16,17,18,19,20,21,22,23},{24..., dimensions={0} | all-to-all | bytes 1572864 | tf_op jit(solution)/shard_map/all_to_all | solution.py:412
  99.5 7.8 %project.1 = bf16[64,3072]{1,0:T(8,128)(2,1)} custom-call(bf16[8,128,384]{2,1,0:T(8,128)(2,1)S(1)} %all_to_all.10.x_ref, bf16[8,384,3072]{2,1,0:T(8,128)(2,1)} %bitcast.10, bf16[64,3072]{1,0:T(8,128)(2,1)S(1)} %copy-done.9, f32[1,3072]{1,0:T(1,128)S(1)} %bitcast.9), custom_call_target="tpu_custom_call" | custom-call | flops 1207959552 | bytes 18874368 | tf_op jit(solution)/shard_map/project/pallas_call | solution.py:356
  107.4 0.9 pad_maximum_fusion
  (31 shorter events, 1.5 us)
Async XLA Ops:
  0.6 3.4 %copy-start.1 = (bf16[64,9216]{1,0:T(8,128)(2,1)S(1)}, bf16[64,9216]{1,0:T(8,128)(2,1)}, u32[]{:S(2)}) copy-start(bf16[64,9216]{1,0:T(8,128)(2,1)} %refs_2_.1) | copy-start | bytes 3538948
  2.0 2.1 %collective-permute-start = (bf16[2,256,384]{2,1,0:T(8,128)(2,1)S(1)}, bf16[2,256,384]{2,1,0:T(8,128)(2,1)S(1)}, u32[]{:S(2)}, u32[]{:S(2)}) collective-permute-start(bf16[2,256,384]{2,1,0:T(8,128)(2,1)S(1)} %get-tuple-element.9), channel_id=1, source_target_pairs={{0,4},{4,0},{8,12},{12,8},{16,20},{20,16},{24,28},{28,24},{1,5},{5... | collective-permute-start | bytes 1179656 | tf_op jit(solution)/shard_map/ppermute | solution.py:420
  4.0 1.7 %copy-start = (bf16[128,9216]{1,0:T(8,128)(2,1)S(1)}, bf16[128,9216]{1,0:T(8,128)(2,1)}, u32[]{:S(2)}) copy-start(bf16[128,9216]{1,0:T(8,128)(2,1)} %refs_5_.1) | copy-start | bytes 7077892
  6.7 1.4 %copy-start.2 = (bf16[8,128,1152]{2,1,0:T(8,128)(2,1)}, bf16[8,128,1152]{2,1,0:T(8,128)(2,1)S(1)}, u32[]{:S(2)}) copy-start(bf16[8,128,1152]{2,1,0:T(8,128)(2,1)S(1)} %pack_heads.1) | copy-start | bytes 7077892
  8.2 49.4 %all-to-all-start = ((bf16[8,128,1152]{2,1,0:T(8,128)(2,1)}), bf16[8,128,1152]{2,1,0:T(8,128)(2,1)S(1)}, u32[]{:S(2)}, u32[]{:S(2)}) async-start(bf16[8,128,1152]{2,1,0:T(8,128)(2,1)} %copy-done.2), calls=%async_computation | async-start | bytes 4718592 | tf_op jit(solution)/shard_map/all_to_all | solution.py:412
  12.3 12.6 %collective-permute-start.3 = (bf16[2,256,384]{2,1,0:T(8,128)(2,1)S(1)}, bf16[2,256,384]{2,1,0:T(8,128)(2,1)S(1)}, u32[]{:S(2)}, u32[]{:S(2)}) collective-permute-start(bf16[2,256,384]{2,1,0:T(8,128)(2,1)S(1)} %get-tuple-element.8.refs_3_), channel_id=1, source_target_pairs={{8,0},{12,4},{16,8},{20,12},{24,16},{28,20},{9,1},{13,5},{17,9},{2... | collective-permute-start | bytes 1179656 | tf_op jit(solution)/shard_map/ppermute | solution.py:433
  14.3 13.4 %collective-permute-start.1 = (bf16[2,256,384]{2,1,0:T(8,128)(2,1)S(1)}, bf16[2,256,384]{2,1,0:T(8,128)(2,1)S(1)}, u32[]{:S(2)}, u32[]{:S(2)}) collective-permute-start(bf16[2,256,384]{2,1,0:T(8,128)(2,1)S(1)} %get-tuple-element.8.refs_3_), channel_id=1, source_target_pairs={{0,8},{4,12},{8,16},{12,20},{16,24},{20,28},{1,9},{5,13},{9,17},{1... | collective-permute-start | bytes 1179656 | tf_op jit(solution)/shard_map/ppermute | solution.py:432
  17.6 17.5 %collective-permute-start.2 = (bf16[2,256,384]{2,1,0:T(8,128)(2,1)S(1)}, bf16[2,256,384]{2,1,0:T(8,128)(2,1)S(1)}, u32[]{:S(2)}, u32[]{:S(2)}) collective-permute-start(bf16[2,256,384]{2,1,0:T(8,128)(2,1)S(1)} %collective-permute-done.refs_6_.refs_4_), channel_id=1, source_target_pairs={{0,8},{4,12},{8,16},{12,20},{16,24},{20,28},{1,9},{5,13},{9,17},{1... | collective-permute-start | bytes 1179656 | tf_op jit(solution)/shard_map/ppermute | solution.py:432
  19.5 19.6 %collective-permute-start.4 = (bf16[2,256,384]{2,1,0:T(8,128)(2,1)S(1)}, bf16[2,256,384]{2,1,0:T(8,128)(2,1)S(1)}, u32[]{:S(2)}, u32[]{:S(2)}) collective-permute-start(bf16[2,256,384]{2,1,0:T(8,128)(2,1)S(1)} %collective-permute-done.refs_6_.refs_4_), channel_id=1, source_target_pairs={{8,0},{12,4},{16,8},{20,12},{24,16},{28,20},{9,1},{13,5},{17,9},{2... | collective-permute-start | bytes 1179656 | tf_op jit(solution)/shard_map/ppermute | solution.py:433
  24.9 18.4 %collective-permute-start.7 = (bf16[2,256,384]{2,1,0:T(8,128)(2,1)S(1)}, bf16[2,256,384]{2,1,0:T(8,128)(2,1)}, u32[]{:S(2)}, u32[]{:S(2)}) collective-permute-start(bf16[2,256,384]{2,1,0:T(8,128)(2,1)S(1)} %collective-permute-done.3.refs_7_), channel_id=1, source_target_pairs={{8,0},{12,4},{16,8},{20,12},{9,1},{13,5},{17,9},{21,13},{10,2},{14... | collective-permute-start | bytes 1179656 | tf_op jit(solution)/shard_map/ppermute | solution.py:433
  27.7 17.0 %collective-permute-start.5 = (bf16[2,256,384]{2,1,0:T(8,128)(2,1)S(1)}, bf16[2,256,384]{2,1,0:T(8,128)(2,1)}, u32[]{:S(2)}, u32[]{:S(2)}) collective-permute-start(bf16[2,256,384]{2,1,0:T(8,128)(2,1)S(1)} %collective-permute-done.1.refs_5_), channel_id=1, source_target_pairs={{8,16},{12,20},{16,24},{20,28},{9,17},{13,21},{17,25},{21,29},{10,... | collective-permute-start | bytes 1179656 | tf_op jit(solution)/shard_map/ppermute | solution.py:432
  29.9 0.7 copy-start.3
  35.1 17.0 %collective-permute-start.6 = (bf16[2,256,384]{2,1,0:T(8,128)(2,1)S(1)}, bf16[2,256,384]{2,1,0:T(8,128)(2,1)}, u32[]{:S(2)}, u32[]{:S(2)}) collective-permute-start(bf16[2,256,384]{2,1,0:T(8,128)(2,1)S(1)} %collective-permute-done.2.refs_6_), channel_id=1, source_target_pairs={{8,16},{12,20},{16,24},{20,28},{9,17},{13,21},{17,25},{21,29},{10,... | collective-permute-start | bytes 1179656 | tf_op jit(solution)/shard_map/ppermute | solution.py:432
  38.3 0.7 copy-start.5
  39.1 17.0 %collective-permute-start.8 = (bf16[2,256,384]{2,1,0:T(8,128)(2,1)S(1)}, bf16[2,256,384]{2,1,0:T(8,128)(2,1)}, u32[]{:S(2)}, u32[]{:S(2)}) collective-permute-start(bf16[2,256,384]{2,1,0:T(8,128)(2,1)S(1)} %collective-permute-done.4.refs_8_), channel_id=1, source_target_pairs={{8,0},{12,4},{16,8},{20,12},{9,1},{13,5},{17,9},{21,13},{10,2},{14... | collective-permute-start | bytes 1179656 | tf_op jit(solution)/shard_map/ppermute | solution.py:433
  42.6 0.7 copy-start.7
  43.3 33.7 %collective-permute-start.11 = (bf16[2,256,384]{2,1,0:T(8,128)(2,1)}, bf16[2,256,384]{2,1,0:T(8,128)(2,1)}, u32[]{:S(2)}, u32[]{:S(2)}) collective-permute-start(bf16[2,256,384]{2,1,0:T(8,128)(2,1)} %collective-permute-done.7.refs_11_), channel_id=1, source_target_pairs={{8,0},{12,4},{9,1},{13,5},{10,2},{14,6},{11,3},{15,7}} | collective-permute-start | bytes 1179656 | tf_op jit(solution)/shard_map/ppermute | solution.py:433
  44.7 32.3 %collective-permute-start.9 = (bf16[2,256,384]{2,1,0:T(8,128)(2,1)}, bf16[2,256,384]{2,1,0:T(8,128)(2,1)}, u32[]{:S(2)}, u32[]{:S(2)}) collective-permute-start(bf16[2,256,384]{2,1,0:T(8,128)(2,1)} %collective-permute-done.5.refs_9_), channel_id=1, source_target_pairs={{16,24},{20,28},{17,25},{21,29},{18,26},{22,30},{19,27},{23,31}} | collective-permute-start | bytes 1179656 | tf_op jit(solution)/shard_map/ppermute | solution.py:432
  52.0 25.0 %collective-permute-start.10 = (bf16[2,256,384]{2,1,0:T(8,128)(2,1)}, bf16[2,256,384]{2,1,0:T(8,128)(2,1)}, u32[]{:S(2)}, u32[]{:S(2)}) collective-permute-start(bf16[2,256,384]{2,1,0:T(8,128)(2,1)} %collective-permute-done.6.refs_10_), channel_id=1, source_target_pairs={{16,24},{20,28},{17,25},{21,29},{18,26},{22,30},{19,27},{23,31}} | collective-permute-start | bytes 1179656 | tf_op jit(solution)/shard_map/ppermute | solution.py:432
  56.0 21.0 %collective-permute-start.12 = (bf16[2,256,384]{2,1,0:T(8,128)(2,1)}, bf16[2,256,384]{2,1,0:T(8,128)(2,1)}, u32[]{:S(2)}, u32[]{:S(2)}) collective-permute-start(bf16[2,256,384]{2,1,0:T(8,128)(2,1)} %collective-permute-done.8.refs_12_), channel_id=1, source_target_pairs={{8,0},{12,4},{9,1},{13,5},{10,2},{14,6},{11,3},{15,7}} | collective-permute-start | bytes 1179656 | tf_op jit(solution)/shard_map/ppermute | solution.py:433
  57.6 1.0 copy-start.4
  58.6 1.0 copy-start.6
  59.6 1.0 copy-start.8
  80.9 18.6 %copy-start.9 = (bf16[64,3072]{1,0:T(8,128)(2,1)S(1)}, bf16[64,3072]{1,0:T(8,128)(2,1)}, u32[]{:S(2)}) copy-start(bf16[64,3072]{1,0:T(8,128)(2,1)} %residual.1) | copy-start | bytes 1179652
  80.9 18.6 %copy-start.10 = (f32[3072]{0:T(1024)S(1)}, f32[3072]{0:T(1024)}, u32[]{:S(2)}) copy-start(f32[3072]{0:T(1024)} %param.10) | copy-start | bytes 36868
  99.1 8.2 %collective-permute-start.13 = (bf16[64,3072]{1,0:T(8,128)(2,1)S(1)}, bf16[64,3072]{1,0:T(8,128)(2,1)S(1)}, u32[]{:S(2)}, u32[]{:S(2)}) collective-permute-start(bf16[64,3072]{1,0:T(8,128)(2,1)S(1)} %unpack_text.1), channel_id=1, source_target_pairs={{0,4},{4,0},{8,12},{12,8},{16,20},{20,16},{24,28},{28,24},{1,5},{5... | collective-permute-start | bytes 1179656 | tf_op jit(solution)/shard_map/ppermute | solution.py:445

commit v18 on v17

--- a/solution.py
+++ b/solution.py
@@ -105,7 +105,19 @@
             flag[0] = jnp.where(jnp.max(total[0, :, HD:]) > LARGE, 1, 0).astype(jnp.int32)
 
 
-def most_body(pair, img_rows, sides, info, *refs):
+def whereabouts(pair, first_step, sides):
+    patch, planes = lax.axis_index("patch"), lax.axis_size("patch") // pair
+    plane = patch // pair
+    flags = []
+    for side in range(sides):
+        step = first_step + side // 2
+        there = plane >= step if side % 2 == 0 else plane + step < planes
+        flags.append(there.astype(jnp.int32))
+    return [patch % pair] + flags
+
+
+def most_body(pair, img_rows, sides, _, *refs):
+    info = whereabouts(pair, 1, sides)
     q_ref, k_ref, v_ref = refs[:3]
     stale = refs[3 : 3 + pair]
     arrived = refs[3 + pair : 3 + pair + sides * pair]
@@ -246,7 +258,8 @@
     )(info, qkv, qkv, qkv, *blocks)
 
 
-def last_body(pair, img_rows, sides, info, *refs):
+def last_body(pair, img_rows, sides, _, *refs):
+    info = whereabouts(pair, lax.axis_size("patch") // pair - 1, sides)
     q_ref, aug_ref, total_ref = refs[:3]
     arrived = refs[3 : 3 + sides * pair]
     out, total, shift, flag = refs[3 + sides * pair :]
@@ -424,7 +437,7 @@
         pack(core_only, img_qkv, txt_qkv, text_rows, destinations, column_block, width, stale[1:])
     )
 
-    arrived, valid = [], []
+    arrived = []
     from_left, from_right = stale, stale
     for step in range(1, planes):
         right_pairs = [(p, p + pair) for p in range((step - 1) * pair, patches - pair)]
@@ -432,12 +445,9 @@
         from_left = [lax.ppermute(block, "patch", right_pairs) for block in from_left]
         from_right = [lax.ppermute(block, "patch", left_pairs) for block in from_right]
         arrived += [from_left, from_right]
-        valid += [plane >= step, plane + step < planes]
     early = max(0, len(arrived) - 2)
-    info = jnp.stack([core] + valid[:early]).astype(jnp.int32)
-    last_info = jnp.stack([core] + valid[early:]).astype(jnp.int32)
-    state = attend_most(info, qkv, img_rows, stale, arrived[:early])
-    attended = attend_last(last_info, qkv, img_rows, state, arrived[early:])
+    state = attend_most(core_only, qkv, img_rows, stale, arrived[:early])
+    attended = attend_last(core_only, qkv, img_rows, state, arrived[early:])
 
     back = exchange(attended)
     text_out = unpack_text(back, order, img_rows)

time: 109 us -> 108 us (level)
  Pallas kernels: 29.1 us -> 28 us
where the time goes in v18:
time: 108 us; the launch traced here: 107 us
  starting transfers between devices  37.2 us (34%)
  Pallas kernels  28 us (26%)
  blocking collectives  18.1 us (17%)
  waiting for transfers between devices  12.3 us (11%)
  local copies, waits for them, and re-layouts  9.6 us (9%)
    all_to_all x1, blocking collectives, exchange(): lax.all_to_all(x, ('patch', 'head'), split_axis=0, concat_axis=0, axis_in...  18.1 us
    ppermute x6, starting transfers between devices, per_device(): lax.ppermute(block, 'patch', right_pairs)  17.4 us
    pallas_call x1, Pallas kernels, attend_most(): pl.pallas_call(functools.partial(most_body, len(stale), img_rows, len(arr...  15.8 us
    ppermute x6, starting transfers between devices, per_device(): lax.ppermute(block, 'patch', left_pairs)  14.6 us
    ppermute x6, waiting for transfers between devices, per_device(): lax.ppermute(block, 'patch', right_pairs)  8.91 us
    unnamed x22, local copies, waits for them, and re-layouts  8.31 us
    pallas_call x1, Pallas kernels, project(): pl.pallas_call(functools.partial(project_body, order), in_specs=[vmem, pl...  7.81 us
    all_to_all x1, starting transfers between devices, exchange(): lax.all_to_all(x, ('patch', 'head'), split_axis=0, concat_axis=0, axis_in...  4.09 us
  transfers between devices with their start and end apart: 15, of which 4 were waited for; matrix products, arithmetic and copies ran while one was open for 0% of the time, Pallas kernels for 22%

profile of v18, /device:TPU:17, one launch (start us, length us, event | category | flops | bytes accessed | tf_op | source)
XLA Modules:
  0.0 107.1 jit_solution(11507303516230965191)
XLA Ops:
  0.7 1.3 %constant_dynamic-slice_fusion = (bf16[2,256,384]{2,1,0:T(8,128)(2,1)S(1)}, bf16[2,256,384]{2,1,0:T(8,128)(2,1)S(1)}) fusion(bf16[2,256,768]{2,1,0:T(8,128)(2,1)} %param.8, s32[]{:T(128)S(6)} %select_n.27, s32[]{:T(128)S(6)} %select_n.26), kind=kLoop, calls=%fused_computation.3 | loop fusion | bytes 1572872 | tf_op jit(solution)/shard_map/dynamic_slice | solution.py:430
  2.0 0.7 collective-permute-start
  2.7 1.3 %collective-permute-done.refs_6_.refs_4_ = bf16[2,256,384]{2,1,0:T(8,128)(2,1)S(1)} collective-permute-done((bf16[2,256,384]{2,1,0:T(8,128)(2,1)S(1)}, bf16[2,256,384]{2,1,0:T(8,128)(2,1)S(1)}, u32[]{:S(2)}, u32[]{:S(2)}) %collective-permute-start) | collective-permute-done | bytes 393248 | tf_op jit(solution)/shard_map/ppermute | solution.py:433
  4.0 1.7 %copy-done = bf16[128,9216]{1,0:T(8,128)(2,1)S(1)} copy-done((bf16[128,9216]{1,0:T(8,128)(2,1)S(1)}, bf16[128,9216]{1,0:T(8,128)(2,1)}, u32[]{:S(2)}) %copy-start) | copy-done | bytes 2359320
  5.7 1.0 pack_heads.1
  6.7 1.4 %copy-done.2 = bf16[8,128,1152]{2,1,0:T(8,128)(2,1)} copy-done((bf16[8,128,1152]{2,1,0:T(8,128)(2,1)}, bf16[8,128,1152]{2,1,0:T(8,128)(2,1)S(1)}, u32[]{:S(2)}) %copy-start.2) | copy-done | bytes 2359320
  8.2 4.1 %all-to-all-start = ((bf16[8,128,1152]{2,1,0:T(8,128)(2,1)}), bf16[8,128,1152]{2,1,0:T(8,128)(2,1)S(1)}, u32[]{:S(2)}, u32[]{:S(2)}) async-start(bf16[8,128,1152]{2,1,0:T(8,128)(2,1)} %copy-done.2), calls=%async_computation | async-start | bytes 4718592 | tf_op jit(solution)/shard_map/all_to_all | solution.py:425
  12.3 2.1 %collective-permute-start.3 = (bf16[2,256,384]{2,1,0:T(8,128)(2,1)S(1)}, bf16[2,256,384]{2,1,0:T(8,128)(2,1)S(1)}, u32[]{:S(2)}, u32[]{:S(2)}) collective-permute-start(bf16[2,256,384]{2,1,0:T(8,128)(2,1)S(1)} %get-tuple-element.8.refs_3_), channel_id=1, source_target_pairs={{8,0},{12,4},{16,8},{20,12},{24,16},{28,20},{9,1},{13,5},{17,9},{2... | collective-permute-start | bytes 1179656 | tf_op jit(solution)/shard_map/ppermute | solution.py:446
  14.3 3.2 %collective-permute-start.1 = (bf16[2,256,384]{2,1,0:T(8,128)(2,1)S(1)}, bf16[2,256,384]{2,1,0:T(8,128)(2,1)S(1)}, u32[]{:S(2)}, u32[]{:S(2)}) collective-permute-start(bf16[2,256,384]{2,1,0:T(8,128)(2,1)S(1)} %get-tuple-element.8.refs_3_), channel_id=1, source_target_pairs={{0,8},{4,12},{8,16},{12,20},{16,24},{20,28},{1,9},{5,13},{9,17},{1... | collective-permute-start | bytes 1179656 | tf_op jit(solution)/shard_map/ppermute | solution.py:445
  17.6 1.9 %collective-permute-start.2 = (bf16[2,256,384]{2,1,0:T(8,128)(2,1)S(1)}, bf16[2,256,384]{2,1,0:T(8,128)(2,1)S(1)}, u32[]{:S(2)}, u32[]{:S(2)}) collective-permute-start(bf16[2,256,384]{2,1,0:T(8,128)(2,1)S(1)} %collective-permute-done.refs_6_.refs_4_), channel_id=1, source_target_pairs={{0,8},{4,12},{8,16},{12,20},{16,24},{20,28},{1,9},{5,13},{9,17},{1... | collective-permute-start | bytes 1179656 | tf_op jit(solution)/shard_map/ppermute | solution.py:445
  19.5 3.4 %collective-permute-start.4 = (bf16[2,256,384]{2,1,0:T(8,128)(2,1)S(1)}, bf16[2,256,384]{2,1,0:T(8,128)(2,1)S(1)}, u32[]{:S(2)}, u32[]{:S(2)}) collective-permute-start(bf16[2,256,384]{2,1,0:T(8,128)(2,1)S(1)} %collective-permute-done.refs_6_.refs_4_), channel_id=1, source_target_pairs={{8,0},{12,4},{16,8},{20,12},{24,16},{28,20},{9,1},{13,5},{17,9},{2... | collective-permute-start | bytes 1179656 | tf_op jit(solution)/shard_map/ppermute | solution.py:446
  22.9 2.0 %collective-permute-done.3.refs_7_ = bf16[2,256,384]{2,1,0:T(8,128)(2,1)S(1)} collective-permute-done((bf16[2,256,384]{2,1,0:T(8,128)(2,1)S(1)}, bf16[2,256,384]{2,1,0:T(8,128)(2,1)S(1)}, u32[]{:S(2)}, u32[]{:S(2)}) %collective-permute-start.3) | collective-permute-done | bytes 393248 | tf_op jit(solution)/shard_map/ppermute | solution.py:446
  24.9 2.8 %collective-permute-start.7 = (bf16[2,256,384]{2,1,0:T(8,128)(2,1)S(1)}, bf16[2,256,384]{2,1,0:T(8,128)(2,1)}, u32[]{:S(2)}, u32[]{:S(2)}) collective-permute-start(bf16[2,256,384]{2,1,0:T(8,128)(2,1)S(1)} %collective-permute-done.3.refs_7_), channel_id=1, source_target_pairs={{8,0},{12,4},{16,8},{20,12},{9,1},{13,5},{17,9},{21,13},{10,2},{14... | collective-permute-start | bytes 1179656 | tf_op jit(solution)/shard_map/ppermute | solution.py:446
  27.7 2.2 %collective-permute-start.5 = (bf16[2,256,384]{2,1,0:T(8,128)(2,1)S(1)}, bf16[2,256,384]{2,1,0:T(8,128)(2,1)}, u32[]{:S(2)}, u32[]{:S(2)}) collective-permute-start(bf16[2,256,384]{2,1,0:T(8,128)(2,1)S(1)} %collective-permute-done.1.refs_5_), channel_id=1, source_target_pairs={{8,16},{12,20},{16,24},{20,28},{9,17},{13,21},{17,25},{21,29},{10,... | collective-permute-start | bytes 1179656 | tf_op jit(solution)/shard_map/ppermute | solution.py:445
  29.9 0.7 copy-done.3
  30.6 4.5 %collective-permute-done.2.refs_6_ = bf16[2,256,384]{2,1,0:T(8,128)(2,1)S(1)} collective-permute-done((bf16[2,256,384]{2,1,0:T(8,128)(2,1)S(1)}, bf16[2,256,384]{2,1,0:T(8,128)(2,1)S(1)}, u32[]{:S(2)}, u32[]{:S(2)}) %collective-permute-start.2) | collective-permute-done | bytes 393248 | tf_op jit(solution)/shard_map/ppermute | solution.py:445
  35.1 3.2 %collective-permute-start.6 = (bf16[2,256,384]{2,1,0:T(8,128)(2,1)S(1)}, bf16[2,256,384]{2,1,0:T(8,128)(2,1)}, u32[]{:S(2)}, u32[]{:S(2)}) collective-permute-start(bf16[2,256,384]{2,1,0:T(8,128)(2,1)S(1)} %collective-permute-done.2.refs_6_), channel_id=1, source_target_pairs={{8,16},{12,20},{16,24},{20,28},{9,17},{13,21},{17,25},{21,29},{10,... | collective-permute-start | bytes 1179656 | tf_op jit(solution)/shard_map/ppermute | solution.py:445
  38.3 0.7 copy-done.5
  39.1 3.5 %collective-permute-start.8 = (bf16[2,256,384]{2,1,0:T(8,128)(2,1)S(1)}, bf16[2,256,384]{2,1,0:T(8,128)(2,1)}, u32[]{:S(2)}, u32[]{:S(2)}) collective-permute-start(bf16[2,256,384]{2,1,0:T(8,128)(2,1)S(1)} %collective-permute-done.4.refs_8_), channel_id=1, source_target_pairs={{8,0},{12,4},{16,8},{20,12},{9,1},{13,5},{17,9},{21,13},{10,2},{14... | collective-permute-start | bytes 1179656 | tf_op jit(solution)/shard_map/ppermute | solution.py:446
  43.3 1.4 %collective-permute-start.11 = (bf16[2,256,384]{2,1,0:T(8,128)(2,1)}, bf16[2,256,384]{2,1,0:T(8,128)(2,1)}, u32[]{:S(2)}, u32[]{:S(2)}) collective-permute-start(bf16[2,256,384]{2,1,0:T(8,128)(2,1)} %collective-permute-done.7.refs_11_), channel_id=1, source_target_pairs={{8,0},{12,4},{9,1},{13,5},{10,2},{14,6},{11,3},{15,7}} | collective-permute-start | bytes 1179656 | tf_op jit(solution)/shard_map/ppermute | solution.py:446
  44.7 2.9 %collective-permute-start.9 = (bf16[2,256,384]{2,1,0:T(8,128)(2,1)}, bf16[2,256,384]{2,1,0:T(8,128)(2,1)}, u32[]{:S(2)}, u32[]{:S(2)}) collective-permute-start(bf16[2,256,384]{2,1,0:T(8,128)(2,1)} %collective-permute-done.5.refs_9_), channel_id=1, source_target_pairs={{16,24},{20,28},{17,25},{21,29},{18,26},{22,30},{19,27},{23,31}} | collective-permute-start | bytes 1179656 | tf_op jit(solution)/shard_map/ppermute | solution.py:445
  47.6 4.4 %collective-permute-done.6.refs_10_ = bf16[2,256,384]{2,1,0:T(8,128)(2,1)} collective-permute-done((bf16[2,256,384]{2,1,0:T(8,128)(2,1)S(1)}, bf16[2,256,384]{2,1,0:T(8,128)(2,1)}, u32[]{:S(2)}, u32[]{:S(2)}) %collective-permute-start.6) | collective-permute-done | bytes 393248 | tf_op jit(solution)/shard_map/ppermute | solution.py:445
  52.0 4.0 %collective-permute-start.10 = (bf16[2,256,384]{2,1,0:T(8,128)(2,1)}, bf16[2,256,384]{2,1,0:T(8,128)(2,1)}, u32[]{:S(2)}, u32[]{:S(2)}) collective-permute-start(bf16[2,256,384]{2,1,0:T(8,128)(2,1)} %collective-permute-done.6.refs_10_), channel_id=1, source_target_pairs={{16,24},{20,28},{17,25},{21,29},{18,26},{22,30},{19,27},{23,31}} | collective-permute-start | bytes 1179656 | tf_op jit(solution)/shard_map/ppermute | solution.py:445
  56.0 1.4 %collective-permute-start.12 = (bf16[2,256,384]{2,1,0:T(8,128)(2,1)}, bf16[2,256,384]{2,1,0:T(8,128)(2,1)}, u32[]{:S(2)}, u32[]{:S(2)}) collective-permute-start(bf16[2,256,384]{2,1,0:T(8,128)(2,1)} %collective-permute-done.8.refs_12_), channel_id=1, source_target_pairs={{8,0},{12,4},{9,1},{13,5},{10,2},{14,6},{11,3},{15,7}} | collective-permute-start | bytes 1179656 | tf_op jit(solution)/shard_map/ppermute | solution.py:446
  57.5 1.0 copy-done.4
  58.5 1.0 copy-done.6
  59.5 1.0 copy-done.8
  60.4 15.8 %attend_most.1 = (bf16[3,1024,128]{2,1,0:T(8,128)(2,1)S(1)}, f32[3,1024,256]{2,1,0:T(8,128)S(1)}) custom-call(s32[1]{0:T(128)} %bitcast.info._, bf16[8,128,1152]{2,1,0:T(8,128)(2,1)S(1)} %all-to-all-done.refs_0_.refs_1_.refs_2_, bf16[8,128,1152]{2,1,0:T(8,128)(2,1)S(1)} %all-to-all-done.refs_0_.refs_1_.refs_2_, ...), custom_call_target="tpu_custom_call" | custom-call | flops 2818572288 | bytes 4325376 | tf_op jit(solution)/shard_map/attend_most/pallas_call | solution.py:244
  76.3 3.3 %attend_last.1 = bf16[8,128,384]{2,1,0:T(8,128)(2,1)S(1)} custom-call(s32[1]{0:T(128)} %bitcast.info._, bf16[8,128,1152]{2,1,0:T(8,128)(2,1)S(1)} %all-to-all-done.refs_0_.refs_1_.refs_2_, bf16[3,1024,128]{2,1,0:T(8,128)(2,1)S(1)} %get-tuple-element.4.refs_1_, f32[3,1024,256]{2,1,0:T(8,128)S(1)} %get-tuple-element.5.refs_2_, ...), custom_call_target="tpu_custom_call" | custom-call | flops 805306368 | bytes 2359296 | tf_op jit(solution)/shard_map/attend_last/pallas_call | solution.py:325
  79.7 18.1 %all_to_all.10.x_ref = bf16[8,128,384]{2,1,0:T(8,128)(2,1)S(1)} all-to-all(bf16[8,128,384]{2,1,0:T(8,128)(2,1)S(1)} %attend_last.1), channel_id=1, replica_groups={{0,1,2,3,4,5,6,7},{8,9,10,11,12,13,14,15},{16,17,18,19,20,21,22,23},{24..., dimensions={0} | all-to-all | bytes 1572864 | tf_op jit(solution)/shard_map/all_to_all | solution.py:425
  98.3 7.8 %project.1 = bf16[64,3072]{1,0:T(8,128)(2,1)} custom-call(bf16[8,128,384]{2,1,0:T(8,128)(2,1)S(1)} %all_to_all.10.x_ref, bf16[8,384,3072]{2,1,0:T(8,128)(2,1)} %bitcast.4, bf16[64,3072]{1,0:T(8,128)(2,1)S(1)} %copy-done.9, f32[1,3072]{1,0:T(1,128)S(1)} %bitcast.3), custom_call_target="tpu_custom_call" | custom-call | flops 1207959552 | bytes 18874368 | tf_op jit(solution)/shard_map/project/pallas_call | solution.py:369
  106.1 0.9 pad_maximum_fusion
  (29 shorter events, 1.3 us)
Async XLA Ops:
  0.6 3.4 %copy-start.1 = (bf16[64,9216]{1,0:T(8,128)(2,1)S(1)}, bf16[64,9216]{1,0:T(8,128)(2,1)}, u32[]{:S(2)}) copy-start(bf16[64,9216]{1,0:T(8,128)(2,1)} %refs_2_.1) | copy-start | bytes 3538948
  2.0 2.1 %collective-permute-start = (bf16[2,256,384]{2,1,0:T(8,128)(2,1)S(1)}, bf16[2,256,384]{2,1,0:T(8,128)(2,1)S(1)}, u32[]{:S(2)}, u32[]{:S(2)}) collective-permute-start(bf16[2,256,384]{2,1,0:T(8,128)(2,1)S(1)} %get-tuple-element.9), channel_id=1, source_target_pairs={{0,4},{4,0},{8,12},{12,8},{16,20},{20,16},{24,28},{28,24},{1,5},{5... | collective-permute-start | bytes 1179656 | tf_op jit(solution)/shard_map/ppermute | solution.py:433
  4.0 1.7 %copy-start = (bf16[128,9216]{1,0:T(8,128)(2,1)S(1)}, bf16[128,9216]{1,0:T(8,128)(2,1)}, u32[]{:S(2)}) copy-start(bf16[128,9216]{1,0:T(8,128)(2,1)} %refs_5_.1) | copy-start | bytes 7077892
  6.7 1.4 %copy-start.2 = (bf16[8,128,1152]{2,1,0:T(8,128)(2,1)}, bf16[8,128,1152]{2,1,0:T(8,128)(2,1)S(1)}, u32[]{:S(2)}) copy-start(bf16[8,128,1152]{2,1,0:T(8,128)(2,1)S(1)} %pack_heads.1) | copy-start | bytes 7077892
  8.2 49.3 %all-to-all-start = ((bf16[8,128,1152]{2,1,0:T(8,128)(2,1)}), bf16[8,128,1152]{2,1,0:T(8,128)(2,1)S(1)}, u32[]{:S(2)}, u32[]{:S(2)}) async-start(bf16[8,128,1152]{2,1,0:T(8,128)(2,1)} %copy-done.2), calls=%async_computation | async-start | bytes 4718592 | tf_op jit(solution)/shard_map/all_to_all | solution.py:425
  12.3 12.6 %collective-permute-start.3 = (bf16[2,256,384]{2,1,0:T(8,128)(2,1)S(1)}, bf16[2,256,384]{2,1,0:T(8,128)(2,1)S(1)}, u32[]{:S(2)}, u32[]{:S(2)}) collective-permute-start(bf16[2,256,384]{2,1,0:T(8,128)(2,1)S(1)} %get-tuple-element.8.refs_3_), channel_id=1, source_target_pairs={{8,0},{12,4},{16,8},{20,12},{24,16},{28,20},{9,1},{13,5},{17,9},{2... | collective-permute-start | bytes 1179656 | tf_op jit(solution)/shard_map/ppermute | solution.py:446
  14.3 13.4 %collective-permute-start.1 = (bf16[2,256,384]{2,1,0:T(8,128)(2,1)S(1)}, bf16[2,256,384]{2,1,0:T(8,128)(2,1)S(1)}, u32[]{:S(2)}, u32[]{:S(2)}) collective-permute-start(bf16[2,256,384]{2,1,0:T(8,128)(2,1)S(1)} %get-tuple-element.8.refs_3_), channel_id=1, source_target_pairs={{0,8},{4,12},{8,16},{12,20},{16,24},{20,28},{1,9},{5,13},{9,17},{1... | collective-permute-start | bytes 1179656 | tf_op jit(solution)/shard_map/ppermute | solution.py:445
  17.6 17.5 %collective-permute-start.2 = (bf16[2,256,384]{2,1,0:T(8,128)(2,1)S(1)}, bf16[2,256,384]{2,1,0:T(8,128)(2,1)S(1)}, u32[]{:S(2)}, u32[]{:S(2)}) collective-permute-start(bf16[2,256,384]{2,1,0:T(8,128)(2,1)S(1)} %collective-permute-done.refs_6_.refs_4_), channel_id=1, source_target_pairs={{0,8},{4,12},{8,16},{12,20},{16,24},{20,28},{1,9},{5,13},{9,17},{1... | collective-permute-start | bytes 1179656 | tf_op jit(solution)/shard_map/ppermute | solution.py:445
  19.5 19.6 %collective-permute-start.4 = (bf16[2,256,384]{2,1,0:T(8,128)(2,1)S(1)}, bf16[2,256,384]{2,1,0:T(8,128)(2,1)S(1)}, u32[]{:S(2)}, u32[]{:S(2)}) collective-permute-start(bf16[2,256,384]{2,1,0:T(8,128)(2,1)S(1)} %collective-permute-done.refs_6_.refs_4_), channel_id=1, source_target_pairs={{8,0},{12,4},{16,8},{20,12},{24,16},{28,20},{9,1},{13,5},{17,9},{2... | collective-permute-start | bytes 1179656 | tf_op jit(solution)/shard_map/ppermute | solution.py:446
  24.9 18.4 %collective-permute-start.7 = (bf16[2,256,384]{2,1,0:T(8,128)(2,1)S(1)}, bf16[2,256,384]{2,1,0:T(8,128)(2,1)}, u32[]{:S(2)}, u32[]{:S(2)}) collective-permute-start(bf16[2,256,384]{2,1,0:T(8,128)(2,1)S(1)} %collective-permute-done.3.refs_7_), channel_id=1, source_target_pairs={{8,0},{12,4},{16,8},{20,12},{9,1},{13,5},{17,9},{21,13},{10,2},{14... | collective-permute-start | bytes 1179656 | tf_op jit(solution)/shard_map/ppermute | solution.py:446
  27.7 17.0 %collective-permute-start.5 = (bf16[2,256,384]{2,1,0:T(8,128)(2,1)S(1)}, bf16[2,256,384]{2,1,0:T(8,128)(2,1)}, u32[]{:S(2)}, u32[]{:S(2)}) collective-permute-start(bf16[2,256,384]{2,1,0:T(8,128)(2,1)S(1)} %collective-permute-done.1.refs_5_), channel_id=1, source_target_pairs={{8,16},{12,20},{16,24},{20,28},{9,17},{13,21},{17,25},{21,29},{10,... | collective-permute-start | bytes 1179656 | tf_op jit(solution)/shard_map/ppermute | solution.py:445
  29.9 0.7 copy-start.3
  35.1 17.0 %collective-permute-start.6 = (bf16[2,256,384]{2,1,0:T(8,128)(2,1)S(1)}, bf16[2,256,384]{2,1,0:T(8,128)(2,1)}, u32[]{:S(2)}, u32[]{:S(2)}) collective-permute-start(bf16[2,256,384]{2,1,0:T(8,128)(2,1)S(1)} %collective-permute-done.2.refs_6_), channel_id=1, source_target_pairs={{8,16},{12,20},{16,24},{20,28},{9,17},{13,21},{17,25},{21,29},{10,... | collective-permute-start | bytes 1179656 | tf_op jit(solution)/shard_map/ppermute | solution.py:445
  38.3 0.7 copy-start.5
  39.1 17.0 %collective-permute-start.8 = (bf16[2,256,384]{2,1,0:T(8,128)(2,1)S(1)}, bf16[2,256,384]{2,1,0:T(8,128)(2,1)}, u32[]{:S(2)}, u32[]{:S(2)}) collective-permute-start(bf16[2,256,384]{2,1,0:T(8,128)(2,1)S(1)} %collective-permute-done.4.refs_8_), channel_id=1, source_target_pairs={{8,0},{12,4},{16,8},{20,12},{9,1},{13,5},{17,9},{21,13},{10,2},{14... | collective-permute-start | bytes 1179656 | tf_op jit(solution)/shard_map/ppermute | solution.py:446
  42.6 0.7 copy-start.7
  43.3 33.0 %collective-permute-start.11 = (bf16[2,256,384]{2,1,0:T(8,128)(2,1)}, bf16[2,256,384]{2,1,0:T(8,128)(2,1)}, u32[]{:S(2)}, u32[]{:S(2)}) collective-permute-start(bf16[2,256,384]{2,1,0:T(8,128)(2,1)} %collective-permute-done.7.refs_11_), channel_id=1, source_target_pairs={{8,0},{12,4},{9,1},{13,5},{10,2},{14,6},{11,3},{15,7}} | collective-permute-start | bytes 1179656 | tf_op jit(solution)/shard_map/ppermute | solution.py:446
  44.7 31.6 %collective-permute-start.9 = (bf16[2,256,384]{2,1,0:T(8,128)(2,1)}, bf16[2,256,384]{2,1,0:T(8,128)(2,1)}, u32[]{:S(2)}, u32[]{:S(2)}) collective-permute-start(bf16[2,256,384]{2,1,0:T(8,128)(2,1)} %collective-permute-done.5.refs_9_), channel_id=1, source_target_pairs={{16,24},{20,28},{17,25},{21,29},{18,26},{22,30},{19,27},{23,31}} | collective-permute-start | bytes 1179656 | tf_op jit(solution)/shard_map/ppermute | solution.py:445
  52.0 24.3 %collective-permute-start.10 = (bf16[2,256,384]{2,1,0:T(8,128)(2,1)}, bf16[2,256,384]{2,1,0:T(8,128)(2,1)}, u32[]{:S(2)}, u32[]{:S(2)}) collective-permute-start(bf16[2,256,384]{2,1,0:T(8,128)(2,1)} %collective-permute-done.6.refs_10_), channel_id=1, source_target_pairs={{16,24},{20,28},{17,25},{21,29},{18,26},{22,30},{19,27},{23,31}} | collective-permute-start | bytes 1179656 | tf_op jit(solution)/shard_map/ppermute | solution.py:445
  56.0 20.3 %collective-permute-start.12 = (bf16[2,256,384]{2,1,0:T(8,128)(2,1)}, bf16[2,256,384]{2,1,0:T(8,128)(2,1)}, u32[]{:S(2)}, u32[]{:S(2)}) collective-permute-start(bf16[2,256,384]{2,1,0:T(8,128)(2,1)} %collective-permute-done.8.refs_12_), channel_id=1, source_target_pairs={{8,0},{12,4},{9,1},{13,5},{10,2},{14,6},{11,3},{15,7}} | collective-permute-start | bytes 1179656 | tf_op jit(solution)/shard_map/ppermute | solution.py:446
  57.5 1.0 copy-start.4
  58.5 1.0 copy-start.6
  59.5 1.0 copy-start.8
  79.7 18.6 %copy-start.9 = (bf16[64,3072]{1,0:T(8,128)(2,1)S(1)}, bf16[64,3072]{1,0:T(8,128)(2,1)}, u32[]{:S(2)}) copy-start(bf16[64,3072]{1,0:T(8,128)(2,1)} %residual.1) | copy-start | bytes 1179652
  79.7 18.6 %copy-start.10 = (f32[3072]{0:T(1024)S(1)}, f32[3072]{0:T(1024)}, u32[]{:S(2)}) copy-start(f32[3072]{0:T(1024)} %param.10) | copy-start | bytes 36868
  97.8 8.2 %collective-permute-start.13 = (bf16[64,3072]{1,0:T(8,128)(2,1)S(1)}, bf16[64,3072]{1,0:T(8,128)(2,1)S(1)}, u32[]{:S(2)}, u32[]{:S(2)}) collective-permute-start(bf16[64,3072]{1,0:T(8,128)(2,1)S(1)} %unpack_text.1), channel_id=1, source_target_pairs={{0,4},{4,0},{8,12},{12,8},{16,20},{20,16},{24,28},{28,24},{1,5},{5... | collective-permute-start | bytes 1179656 | tf_op jit(solution)/shard_map/ppermute | solution.py:455

commit v19 on v18

--- a/solution.py
+++ b/solution.py
@@ -434,7 +434,7 @@
 
     core_only = core.astype(jnp.int32).reshape(1)
     qkv = exchange(
-        pack(core_only, img_qkv, txt_qkv, text_rows, destinations, column_block, width, stale[1:])
+        pack(core_only, img_qkv, txt_qkv, text_rows, destinations, column_block, width, ())
     )
 
     arrived = []

time: 108 us -> 106 us (0.981)
  waiting for transfers between devices: 12.3 us -> 10.4 us
    ppermute x1, waiting for transfers between devices: 1.35 us -> 0.01 us  [per_device(): stale.append(lax.ppermute(theirs, 'patch', swap_pairs))]
    unnamed x22 -> x24, local copies, waits for them, and re-layouts: 8.31 us -> 9.58 us
    dynamic_slice x1, local copies, waits for them, and re-layouts: 1.29 us -> 0.09 us  [per_device(): theirs = lax.dynamic_slice_in_dim(stale_kv, (1 - core) * width, width, 2)]
  transfers between devices with their start and end apart: 15 -> 15, of which waited for: 4 -> 3; matrix products, arithmetic and copies ran while one was open for 0% -> 0% of each run, Pallas kernels for 22% -> 22%
where the time goes in v19:
time: 106 us
  starting transfers between devices  37 us (35%)
  Pallas kernels  28 us (26%)
  blocking collectives  18.8 us (18%)
  waiting for transfers between devices  10.4 us (10%)
  local copies, waits for them, and re-layouts  9.67 us (9%)
    all_to_all x1, blocking collectives, exchange(): lax.all_to_all(x, ('patch', 'head'), split_axis=0, concat_axis=0, axis_in...  18.8 us
    ppermute x6, starting transfers between devices, per_device(): lax.ppermute(block, 'patch', right_pairs)  17.4 us
    pallas_call x1, Pallas kernels, attend_most(): pl.pallas_call(functools.partial(most_body, len(stale), img_rows, len(arr...  15.8 us
    ppermute x6, starting transfers between devices, per_device(): lax.ppermute(block, 'patch', left_pairs)  14.6 us
    unnamed x24, local copies, waits for them, and re-layouts  9.58 us
    ppermute x6, waiting for transfers between devices, per_device(): lax.ppermute(block, 'patch', right_pairs)  8.91 us
    pallas_call x1, Pallas kernels, project(): pl.pallas_call(functools.partial(project_body, order), in_specs=[vmem, pl...  7.82 us
    all_to_all x1, starting transfers between devices, exchange(): lax.all_to_all(x, ('patch', 'head'), split_axis=0, concat_axis=0, axis_in...  4.53 us
  transfers between devices with their start and end apart: 15, of which 3 were waited for; matrix products, arithmetic and copies ran while one was open for 0% of the time, Pallas kernels for 22%

profile of v19, /device:TPU:17, one launch (start us, length us, event | category | flops | bytes accessed | tf_op | source)
XLA Modules:
  0.0 105.7 jit_solution(4303225751691683857)
XLA Ops:
  0.7 1.7 %copy-done = bf16[128,9216]{1,0:T(8,128)(2,1)S(1)} copy-done((bf16[128,9216]{1,0:T(8,128)(2,1)S(1)}, bf16[128,9216]{1,0:T(8,128)(2,1)}, u32[]{:S(2)}) %copy-start) | copy-done | bytes 2359320
  2.3 1.3 %copy-done.1 = bf16[64,9216]{1,0:T(8,128)(2,1)S(1)} copy-done((bf16[64,9216]{1,0:T(8,128)(2,1)S(1)}, bf16[64,9216]{1,0:T(8,128)(2,1)}, u32[]{:S(2)}) %copy-start.1) | copy-done | bytes 1179672
  3.6 1.0 pack_heads.1
  4.6 1.4 %copy-done.2 = bf16[8,128,1152]{2,1,0:T(8,128)(2,1)} copy-done((bf16[8,128,1152]{2,1,0:T(8,128)(2,1)}, bf16[8,128,1152]{2,1,0:T(8,128)(2,1)S(1)}, u32[]{:S(2)}) %copy-start.2) | copy-done | bytes 2359320
  6.0 4.5 %all-to-all-start = ((bf16[8,128,1152]{2,1,0:T(8,128)(2,1)}), bf16[8,128,1152]{2,1,0:T(8,128)(2,1)S(1)}, u32[]{:S(2)}, u32[]{:S(2)}) async-start(bf16[8,128,1152]{2,1,0:T(8,128)(2,1)} %copy-done.2), calls=%async_computation | async-start | bytes 4718592 | tf_op jit(solution)/shard_map/all_to_all | solution.py:425
  10.7 2.1 %collective-permute-start.3 = (bf16[2,256,384]{2,1,0:T(8,128)(2,1)S(1)}, bf16[2,256,384]{2,1,0:T(8,128)(2,1)S(1)}, u32[]{:S(2)}, u32[]{:S(2)}) collective-permute-start(bf16[2,256,384]{2,1,0:T(8,128)(2,1)S(1)} %get-tuple-element.9.refs_3_), channel_id=1, source_target_pairs={{8,0},{12,4},{16,8},{20,12},{24,16},{28,20},{9,1},{13,5},{17,9},{2... | collective-permute-start | bytes 1179656 | tf_op jit(solution)/shard_map/ppermute | solution.py:446
  12.8 3.2 %collective-permute-start.1 = (bf16[2,256,384]{2,1,0:T(8,128)(2,1)S(1)}, bf16[2,256,384]{2,1,0:T(8,128)(2,1)S(1)}, u32[]{:S(2)}, u32[]{:S(2)}) collective-permute-start(bf16[2,256,384]{2,1,0:T(8,128)(2,1)S(1)} %get-tuple-element.9.refs_3_), channel_id=1, source_target_pairs={{0,8},{4,12},{8,16},{12,20},{16,24},{20,28},{1,9},{5,13},{9,17},{1... | collective-permute-start | bytes 1179656 | tf_op jit(solution)/shard_map/ppermute | solution.py:445
  16.1 1.9 %collective-permute-start.2 = (bf16[2,256,384]{2,1,0:T(8,128)(2,1)S(1)}, bf16[2,256,384]{2,1,0:T(8,128)(2,1)S(1)}, u32[]{:S(2)}, u32[]{:S(2)}) collective-permute-start(bf16[2,256,384]{2,1,0:T(8,128)(2,1)S(1)} %collective-permute-done.refs_4_), channel_id=1, source_target_pairs={{0,8},{4,12},{8,16},{12,20},{16,24},{20,28},{1,9},{5,13},{9,17},{1... | collective-permute-start | bytes 1179656 | tf_op jit(solution)/shard_map/ppermute | solution.py:445
  18.0 3.4 %collective-permute-start.4 = (bf16[2,256,384]{2,1,0:T(8,128)(2,1)S(1)}, bf16[2,256,384]{2,1,0:T(8,128)(2,1)S(1)}, u32[]{:S(2)}, u32[]{:S(2)}) collective-permute-start(bf16[2,256,384]{2,1,0:T(8,128)(2,1)S(1)} %collective-permute-done.refs_4_), channel_id=1, source_target_pairs={{8,0},{12,4},{16,8},{20,12},{24,16},{28,20},{9,1},{13,5},{17,9},{2... | collective-permute-start | bytes 1179656 | tf_op jit(solution)/shard_map/ppermute | solution.py:446
  21.4 1.5 %collective-permute-done.3.refs_7_ = bf16[2,256,384]{2,1,0:T(8,128)(2,1)S(1)} collective-permute-done((bf16[2,256,384]{2,1,0:T(8,128)(2,1)S(1)}, bf16[2,256,384]{2,1,0:T(8,128)(2,1)S(1)}, u32[]{:S(2)}, u32[]{:S(2)}) %collective-permute-start.3) | collective-permute-done | bytes 393248 | tf_op jit(solution)/shard_map/ppermute | solution.py:446
  22.8 2.8 %collective-permute-start.7 = (bf16[2,256,384]{2,1,0:T(8,128)(2,1)S(1)}, bf16[2,256,384]{2,1,0:T(8,128)(2,1)}, u32[]{:S(2)}, u32[]{:S(2)}) collective-permute-start(bf16[2,256,384]{2,1,0:T(8,128)(2,1)S(1)} %collective-permute-done.3.refs_7_), channel_id=1, source_target_pairs={{8,0},{12,4},{16,8},{20,12},{9,1},{13,5},{17,9},{21,13},{10,2},{14... | collective-permute-start | bytes 1179656 | tf_op jit(solution)/shard_map/ppermute | solution.py:446
  25.7 2.1 %collective-permute-start.5 = (bf16[2,256,384]{2,1,0:T(8,128)(2,1)S(1)}, bf16[2,256,384]{2,1,0:T(8,128)(2,1)}, u32[]{:S(2)}, u32[]{:S(2)}) collective-permute-start(bf16[2,256,384]{2,1,0:T(8,128)(2,1)S(1)} %collective-permute-done.1.refs_5_), channel_id=1, source_target_pairs={{8,16},{12,20},{16,24},{20,28},{9,17},{13,21},{17,25},{21,29},{10,... | collective-permute-start | bytes 1179656 | tf_op jit(solution)/shard_map/ppermute | solution.py:445
  27.8 0.7 copy-done.3
  28.6 4.5 %collective-permute-done.2.refs_6_ = bf16[2,256,384]{2,1,0:T(8,128)(2,1)S(1)} collective-permute-done((bf16[2,256,384]{2,1,0:T(8,128)(2,1)S(1)}, bf16[2,256,384]{2,1,0:T(8,128)(2,1)S(1)}, u32[]{:S(2)}, u32[]{:S(2)}) %collective-permute-start.2) | collective-permute-done | bytes 393248 | tf_op jit(solution)/shard_map/ppermute | solution.py:445
  33.0 3.2 %collective-permute-start.6 = (bf16[2,256,384]{2,1,0:T(8,128)(2,1)S(1)}, bf16[2,256,384]{2,1,0:T(8,128)(2,1)}, u32[]{:S(2)}, u32[]{:S(2)}) collective-permute-start(bf16[2,256,384]{2,1,0:T(8,128)(2,1)S(1)} %collective-permute-done.2.refs_6_), channel_id=1, source_target_pairs={{8,16},{12,20},{16,24},{20,28},{9,17},{13,21},{17,25},{21,29},{10,... | collective-permute-start | bytes 1179656 | tf_op jit(solution)/shard_map/ppermute | solution.py:445
  36.3 0.7 copy-done.5
  37.0 3.5 %collective-permute-start.8 = (bf16[2,256,384]{2,1,0:T(8,128)(2,1)S(1)}, bf16[2,256,384]{2,1,0:T(8,128)(2,1)}, u32[]{:S(2)}, u32[]{:S(2)}) collective-permute-start(bf16[2,256,384]{2,1,0:T(8,128)(2,1)S(1)} %collective-permute-done.4.refs_8_), channel_id=1, source_target_pairs={{8,0},{12,4},{16,8},{20,12},{9,1},{13,5},{17,9},{21,13},{10,2},{14... | collective-permute-start | bytes 1179656 | tf_op jit(solution)/shard_map/ppermute | solution.py:446
  40.5 0.7 copy-done.7
  41.3 1.4 %collective-permute-start.11 = (bf16[2,256,384]{2,1,0:T(8,128)(2,1)}, bf16[2,256,384]{2,1,0:T(8,128)(2,1)}, u32[]{:S(2)}, u32[]{:S(2)}) collective-permute-start(bf16[2,256,384]{2,1,0:T(8,128)(2,1)} %collective-permute-done.7.refs_11_), channel_id=1, source_target_pairs={{8,0},{12,4},{9,1},{13,5},{10,2},{14,6},{11,3},{15,7}} | collective-permute-start | bytes 1179656 | tf_op jit(solution)/shard_map/ppermute | solution.py:446
  42.7 2.9 %collective-permute-start.9 = (bf16[2,256,384]{2,1,0:T(8,128)(2,1)}, bf16[2,256,384]{2,1,0:T(8,128)(2,1)}, u32[]{:S(2)}, u32[]{:S(2)}) collective-permute-start(bf16[2,256,384]{2,1,0:T(8,128)(2,1)} %collective-permute-done.5.refs_9_), channel_id=1, source_target_pairs={{16,24},{20,28},{17,25},{21,29},{18,26},{22,30},{19,27},{23,31}} | collective-permute-start | bytes 1179656 | tf_op jit(solution)/shard_map/ppermute | solution.py:445
  45.5 4.4 %collective-permute-done.6.refs_10_ = bf16[2,256,384]{2,1,0:T(8,128)(2,1)} collective-permute-done((bf16[2,256,384]{2,1,0:T(8,128)(2,1)S(1)}, bf16[2,256,384]{2,1,0:T(8,128)(2,1)}, u32[]{:S(2)}, u32[]{:S(2)}) %collective-permute-start.6) | collective-permute-done | bytes 393248 | tf_op jit(solution)/shard_map/ppermute | solution.py:445
  50.0 4.0 %collective-permute-start.10 = (bf16[2,256,384]{2,1,0:T(8,128)(2,1)}, bf16[2,256,384]{2,1,0:T(8,128)(2,1)}, u32[]{:S(2)}, u32[]{:S(2)}) collective-permute-start(bf16[2,256,384]{2,1,0:T(8,128)(2,1)} %collective-permute-done.6.refs_10_), channel_id=1, source_target_pairs={{16,24},{20,28},{17,25},{21,29},{18,26},{22,30},{19,27},{23,31}} | collective-permute-start | bytes 1179656 | tf_op jit(solution)/shard_map/ppermute | solution.py:445
  54.0 1.4 %collective-permute-start.12 = (bf16[2,256,384]{2,1,0:T(8,128)(2,1)}, bf16[2,256,384]{2,1,0:T(8,128)(2,1)}, u32[]{:S(2)}, u32[]{:S(2)}) collective-permute-start(bf16[2,256,384]{2,1,0:T(8,128)(2,1)} %collective-permute-done.8.refs_12_), channel_id=1, source_target_pairs={{8,0},{12,4},{9,1},{13,5},{10,2},{14,6},{11,3},{15,7}} | collective-permute-start | bytes 1179656 | tf_op jit(solution)/shard_map/ppermute | solution.py:446
  55.4 1.0 copy-done.4
  56.4 1.0 copy-done.6
  57.4 1.0 copy-done.8
  58.4 15.8 %attend_most.1 = (bf16[3,1024,128]{2,1,0:T(8,128)(2,1)S(1)}, f32[3,1024,256]{2,1,0:T(8,128)S(1)}) custom-call(s32[1]{0:T(128)} %bitcast.info._, bf16[8,128,1152]{2,1,0:T(8,128)(2,1)S(1)} %all-to-all-done.refs_0_.refs_1_.refs_2_, bf16[8,128,1152]{2,1,0:T(8,128)(2,1)S(1)} %all-to-all-done.refs_0_.refs_1_.refs_2_, ...), custom_call_target="tpu_custom_call" | custom-call | flops 2818572288 | bytes 4325376 | tf_op jit(solution)/shard_map/attend_most/pallas_call | solution.py:244
  74.3 3.3 %attend_last.1 = bf16[8,128,384]{2,1,0:T(8,128)(2,1)S(1)} custom-call(s32[1]{0:T(128)} %bitcast.info._, bf16[8,128,1152]{2,1,0:T(8,128)(2,1)S(1)} %all-to-all-done.refs_0_.refs_1_.refs_2_, bf16[3,1024,128]{2,1,0:T(8,128)(2,1)S(1)} %get-tuple-element.4.refs_1_, f32[3,1024,256]{2,1,0:T(8,128)S(1)} %get-tuple-element.5.refs_2_, ...), custom_call_target="tpu_custom_call" | custom-call | flops 805306368 | bytes 2359296 | tf_op jit(solution)/shard_map/attend_last/pallas_call | solution.py:325
  77.6 18.8 %all_to_all.10.x_ref = bf16[8,128,384]{2,1,0:T(8,128)(2,1)S(1)} all-to-all(bf16[8,128,384]{2,1,0:T(8,128)(2,1)S(1)} %attend_last.1), channel_id=1, replica_groups={{0,1,2,3,4,5,6,7},{8,9,10,11,12,13,14,15},{16,17,18,19,20,21,22,23},{24..., dimensions={0} | all-to-all | bytes 1572864 | tf_op jit(solution)/shard_map/all_to_all | solution.py:425
  96.5 0.4 collective-permute-start.13
  96.9 7.8 %project.1 = bf16[64,3072]{1,0:T(8,128)(2,1)} custom-call(bf16[8,128,384]{2,1,0:T(8,128)(2,1)S(1)} %all_to_all.10.x_ref, bf16[8,384,3072]{2,1,0:T(8,128)(2,1)} %bitcast.4, bf16[64,3072]{1,0:T(8,128)(2,1)S(1)} %copy-done.9, f32[1,3072]{1,0:T(1,128)S(1)} %bitcast.3), custom_call_target="tpu_custom_call" | custom-call | flops 1207959552 | bytes 18874368 | tf_op jit(solution)/shard_map/project/pallas_call | solution.py:369
  104.8 0.9 pad_maximum_fusion
  (31 shorter events, 0.3 us)
Async XLA Ops:
  0.6 1.7 %copy-start = (bf16[128,9216]{1,0:T(8,128)(2,1)S(1)}, bf16[128,9216]{1,0:T(8,128)(2,1)}, u32[]{:S(2)}) copy-start(bf16[128,9216]{1,0:T(8,128)(2,1)} %refs_5_.1) | copy-start | bytes 7077892
  2.3 1.3 %copy-start.1 = (bf16[64,9216]{1,0:T(8,128)(2,1)S(1)}, bf16[64,9216]{1,0:T(8,128)(2,1)}, u32[]{:S(2)}) copy-start(bf16[64,9216]{1,0:T(8,128)(2,1)} %refs_2_.1) | copy-start | bytes 3538948
  4.6 1.4 %copy-start.2 = (bf16[8,128,1152]{2,1,0:T(8,128)(2,1)}, bf16[8,128,1152]{2,1,0:T(8,128)(2,1)S(1)}, u32[]{:S(2)}) copy-start(bf16[8,128,1152]{2,1,0:T(8,128)(2,1)S(1)} %pack_heads.1) | copy-start | bytes 7077892
  6.0 4.5 %copy-start.11 = (bf16[2,256,768]{2,1,0:T(8,128)(2,1)S(1)}, bf16[2,256,768]{2,1,0:T(8,128)(2,1)}, u32[]{:S(2)}) copy-start(bf16[2,256,768]{2,1,0:T(8,128)(2,1)} %param.8) | copy-start | bytes 2359300
  6.0 49.4 %all-to-all-start = ((bf16[8,128,1152]{2,1,0:T(8,128)(2,1)}), bf16[8,128,1152]{2,1,0:T(8,128)(2,1)S(1)}, u32[]{:S(2)}, u32[]{:S(2)}) async-start(bf16[8,128,1152]{2,1,0:T(8,128)(2,1)} %copy-done.2), calls=%async_computation | async-start | bytes 4718592 | tf_op jit(solution)/shard_map/all_to_all | solution.py:425
  10.7 5.4 %collective-permute-start = (bf16[2,256,384]{2,1,0:T(8,128)(2,1)S(1)}, bf16[2,256,384]{2,1,0:T(8,128)(2,1)S(1)}, u32[]{:S(2)}, u32[]{:S(2)}) collective-permute-start(bf16[2,256,384]{2,1,0:T(8,128)(2,1)S(1)} %get-tuple-element.8), channel_id=1, source_target_pairs={{0,4},{4,0},{8,12},{12,8},{16,20},{20,16},{24,28},{28,24},{1,5},{5... | collective-permute-start | bytes 1179656 | tf_op jit(solution)/shard_map/ppermute | solution.py:433
  10.7 12.1 %collective-permute-start.3 = (bf16[2,256,384]{2,1,0:T(8,128)(2,1)S(1)}, bf16[2,256,384]{2,1,0:T(8,128)(2,1)S(1)}, u32[]{:S(2)}, u32[]{:S(2)}) collective-permute-start(bf16[2,256,384]{2,1,0:T(8,128)(2,1)S(1)} %get-tuple-element.9.refs_3_), channel_id=1, source_target_pairs={{8,0},{12,4},{16,8},{20,12},{24,16},{28,20},{9,1},{13,5},{17,9},{2... | collective-permute-start | bytes 1179656 | tf_op jit(solution)/shard_map/ppermute | solution.py:446
  12.8 12.8 %collective-permute-start.1 = (bf16[2,256,384]{2,1,0:T(8,128)(2,1)S(1)}, bf16[2,256,384]{2,1,0:T(8,128)(2,1)S(1)}, u32[]{:S(2)}, u32[]{:S(2)}) collective-permute-start(bf16[2,256,384]{2,1,0:T(8,128)(2,1)S(1)} %get-tuple-element.9.refs_3_), channel_id=1, source_target_pairs={{0,8},{4,12},{8,16},{12,20},{16,24},{20,28},{1,9},{5,13},{9,17},{1... | collective-permute-start | bytes 1179656 | tf_op jit(solution)/shard_map/ppermute | solution.py:445
  16.1 17.0 %collective-permute-start.2 = (bf16[2,256,384]{2,1,0:T(8,128)(2,1)S(1)}, bf16[2,256,384]{2,1,0:T(8,128)(2,1)S(1)}, u32[]{:S(2)}, u32[]{:S(2)}) collective-permute-start(bf16[2,256,384]{2,1,0:T(8,128)(2,1)S(1)} %collective-permute-done.refs_4_), channel_id=1, source_target_pairs={{0,8},{4,12},{8,16},{12,20},{16,24},{20,28},{1,9},{5,13},{9,17},{1... | collective-permute-start | bytes 1179656 | tf_op jit(solution)/shard_map/ppermute | solution.py:445
  18.0 19.0 %collective-permute-start.4 = (bf16[2,256,384]{2,1,0:T(8,128)(2,1)S(1)}, bf16[2,256,384]{2,1,0:T(8,128)(2,1)S(1)}, u32[]{:S(2)}, u32[]{:S(2)}) collective-permute-start(bf16[2,256,384]{2,1,0:T(8,128)(2,1)S(1)} %collective-permute-done.refs_4_), channel_id=1, source_target_pairs={{8,0},{12,4},{16,8},{20,12},{24,16},{28,20},{9,1},{13,5},{17,9},{2... | collective-permute-start | bytes 1179656 | tf_op jit(solution)/shard_map/ppermute | solution.py:446
  22.8 18.4 %collective-permute-start.7 = (bf16[2,256,384]{2,1,0:T(8,128)(2,1)S(1)}, bf16[2,256,384]{2,1,0:T(8,128)(2,1)}, u32[]{:S(2)}, u32[]{:S(2)}) collective-permute-start(bf16[2,256,384]{2,1,0:T(8,128)(2,1)S(1)} %collective-permute-done.3.refs_7_), channel_id=1, source_target_pairs={{8,0},{12,4},{16,8},{20,12},{9,1},{13,5},{17,9},{21,13},{10,2},{14... | collective-permute-start | bytes 1179656 | tf_op jit(solution)/shard_map/ppermute | solution.py:446
  25.7 17.0 %collective-permute-start.5 = (bf16[2,256,384]{2,1,0:T(8,128)(2,1)S(1)}, bf16[2,256,384]{2,1,0:T(8,128)(2,1)}, u32[]{:S(2)}, u32[]{:S(2)}) collective-permute-start(bf16[2,256,384]{2,1,0:T(8,128)(2,1)S(1)} %collective-permute-done.1.refs_5_), channel_id=1, source_target_pairs={{8,16},{12,20},{16,24},{20,28},{9,17},{13,21},{17,25},{21,29},{10,... | collective-permute-start | bytes 1179656 | tf_op jit(solution)/shard_map/ppermute | solution.py:445
  27.8 0.7 copy-start.3
  33.0 17.0 %collective-permute-start.6 = (bf16[2,256,384]{2,1,0:T(8,128)(2,1)S(1)}, bf16[2,256,384]{2,1,0:T(8,128)(2,1)}, u32[]{:S(2)}, u32[]{:S(2)}) collective-permute-start(bf16[2,256,384]{2,1,0:T(8,128)(2,1)S(1)} %collective-permute-done.2.refs_6_), channel_id=1, source_target_pairs={{8,16},{12,20},{16,24},{20,28},{9,17},{13,21},{17,25},{21,29},{10,... | collective-permute-start | bytes 1179656 | tf_op jit(solution)/shard_map/ppermute | solution.py:445
  36.2 0.7 copy-start.5
  37.0 17.0 %collective-permute-start.8 = (bf16[2,256,384]{2,1,0:T(8,128)(2,1)S(1)}, bf16[2,256,384]{2,1,0:T(8,128)(2,1)}, u32[]{:S(2)}, u32[]{:S(2)}) collective-permute-start(bf16[2,256,384]{2,1,0:T(8,128)(2,1)S(1)} %collective-permute-done.4.refs_8_), channel_id=1, source_target_pairs={{8,0},{12,4},{16,8},{20,12},{9,1},{13,5},{17,9},{21,13},{10,2},{14... | collective-permute-start | bytes 1179656 | tf_op jit(solution)/shard_map/ppermute | solution.py:446
  40.5 0.7 copy-start.7
  41.3 33.0 %collective-permute-start.11 = (bf16[2,256,384]{2,1,0:T(8,128)(2,1)}, bf16[2,256,384]{2,1,0:T(8,128)(2,1)}, u32[]{:S(2)}, u32[]{:S(2)}) collective-permute-start(bf16[2,256,384]{2,1,0:T(8,128)(2,1)} %collective-permute-done.7.refs_11_), channel_id=1, source_target_pairs={{8,0},{12,4},{9,1},{13,5},{10,2},{14,6},{11,3},{15,7}} | collective-permute-start | bytes 1179656 | tf_op jit(solution)/shard_map/ppermute | solution.py:446
  42.7 31.6 %collective-permute-start.9 = (bf16[2,256,384]{2,1,0:T(8,128)(2,1)}, bf16[2,256,384]{2,1,0:T(8,128)(2,1)}, u32[]{:S(2)}, u32[]{:S(2)}) collective-permute-start(bf16[2,256,384]{2,1,0:T(8,128)(2,1)} %collective-permute-done.5.refs_9_), channel_id=1, source_target_pairs={{16,24},{20,28},{17,25},{21,29},{18,26},{22,30},{19,27},{23,31}} | collective-permute-start | bytes 1179656 | tf_op jit(solution)/shard_map/ppermute | solution.py:445
  50.0 24.3 %collective-permute-start.10 = (bf16[2,256,384]{2,1,0:T(8,128)(2,1)}, bf16[2,256,384]{2,1,0:T(8,128)(2,1)}, u32[]{:S(2)}, u32[]{:S(2)}) collective-permute-start(bf16[2,256,384]{2,1,0:T(8,128)(2,1)} %collective-permute-done.6.refs_10_), channel_id=1, source_target_pairs={{16,24},{20,28},{17,25},{21,29},{18,26},{22,30},{19,27},{23,31}} | collective-permute-start | bytes 1179656 | tf_op jit(solution)/shard_map/ppermute | solution.py:445
  54.0 20.3 %collective-permute-start.12 = (bf16[2,256,384]{2,1,0:T(8,128)(2,1)}, bf16[2,256,384]{2,1,0:T(8,128)(2,1)}, u32[]{:S(2)}, u32[]{:S(2)}) collective-permute-start(bf16[2,256,384]{2,1,0:T(8,128)(2,1)} %collective-permute-done.8.refs_12_), channel_id=1, source_target_pairs={{8,0},{12,4},{9,1},{13,5},{10,2},{14,6},{11,3},{15,7}} | collective-permute-start | bytes 1179656 | tf_op jit(solution)/shard_map/ppermute | solution.py:446
  55.4 1.0 copy-start.4
  56.4 1.0 copy-start.6
  57.4 1.0 copy-start.8
  77.6 19.2 %copy-start.9 = (bf16[64,3072]{1,0:T(8,128)(2,1)S(1)}, bf16[64,3072]{1,0:T(8,128)(2,1)}, u32[]{:S(2)}) copy-start(bf16[64,3072]{1,0:T(8,128)(2,1)} %residual.1) | copy-start | bytes 1179652
  77.6 19.2 %copy-start.10 = (f32[3072]{0:T(1024)S(1)}, f32[3072]{0:T(1024)}, u32[]{:S(2)}) copy-start(f32[3072]{0:T(1024)} %param.10) | copy-start | bytes 36868
  96.5 8.2 %collective-permute-start.13 = (bf16[64,3072]{1,0:T(8,128)(2,1)S(1)}, bf16[64,3072]{1,0:T(8,128)(2,1)S(1)}, u32[]{:S(2)}, u32[]{:S(2)}) collective-permute-start(bf16[64,3072]{1,0:T(8,128)(2,1)S(1)} %unpack_text.1), channel_id=1, source_target_pairs={{0,4},{4,0},{8,12},{12,8},{16,20},{20,16},{24,28},{28,24},{1,5},{5... | collective-permute-start | bytes 1179656 | tf_op jit(solution)/shard_map/ppermute | solution.py:455
